TPU v7x, 32 devices: a whole 2x2x4 slice. The times are simulated.
32 devices in a mesh: groups: 2 (over y), latent: 4 (over z), dp: 4 (over x, core).
Axes of the slice: x: 2, y: 2, z: 4, core: 2. Of those that a mesh axis runs over, the one named last changes fastest.
Arguments:
- activations: bfloat16 [3072, 2048], P(('groups', 'dp'), 'latent'), parts along dimension 0, may hold values from -40 to 40
- encoder: float32 [4096, 2048], P(('groups', 'dp'), 'latent'), parts along dimension 0, may hold values from -0.12 to 0.12
- enc_bias: float32 [4096], P(('groups', 'latent', 'dp')), parts along dimension 0, may hold values from -3 to 3
- decoder: float32 [4096, 2048], P(('groups', 'dp'), 'latent'), parts along dimension 0, may hold values from -1.2 to 1.2
- enc_moment: float32 [4096, 2048], P(('groups', 'dp'), 'latent'), parts along dimension 0, may hold values from -1.2 to 1.2
- enc_square: float32 [4096, 2048], P(('groups', 'dp'), 'latent'), parts along dimension 0, may hold values from 0.001 to 1
- bias_moment: float32 [4096], P(('groups', 'latent', 'dp')), parts along dimension 0, may hold values from -1.2 to 1.2
- bias_square: float32 [4096], P(('groups', 'latent', 'dp')), parts along dimension 0, may hold values from 0.001 to 1
- dec_moment: float32 [4096, 2048], P(('groups', 'dp'), 'latent'), parts along dimension 0, may hold values from -1.2 to 1.2
- dec_square: float32 [4096, 2048], P(('groups', 'dp'), 'latent'), parts along dimension 0, may hold values from 0.001 to 1
Outputs:
- error: bfloat16 [3072, 2048], P(('groups', 'dp'), 'latent'), parts along dimension 0
- new_encoder: float32 [4096, 2048], P(('groups', 'dp'), 'latent'), parts along dimension 0
- new_enc_bias: float32 [4096], P(('groups', 'latent', 'dp')), parts along dimension 0
- new_decoder: float32 [4096, 2048], P(('groups', 'dp'), 'latent'), parts along dimension 0
- new_enc_moment: float32 [4096, 2048], P(('groups', 'dp'), 'latent'), parts along dimension 0
- new_enc_square: float32 [4096, 2048], P(('groups', 'dp'), 'latent'), parts along dimension 0
- new_bias_moment: float32 [4096], P(('groups', 'latent', 'dp')), parts along dimension 0
- new_bias_square: float32 [4096], P(('groups', 'latent', 'dp')), parts along dimension 0
- new_dec_moment: float32 [4096, 2048], P(('groups', 'dp'), 'latent'), parts along dimension 0
- new_dec_square: float32 [4096, 2048], P(('groups', 'dp'), 'latent'), parts along dimension 0
There are 2 independent parts, one for each index of `groups`. A program takes and returns all parts, laid end to end along the dimension named above; each array names one. Nothing has to cross between parts.
All inputs are finite; a program needn't handle non-finite values.
Results may differ from a plain program's by a relative error of at most 0.00055.
The roundings to bfloat16 on the way count: a program that leaves them out, or rounds other values in their place, can miss the bound.
Values may be sent and summed in bfloat16 or wider, within the bound.
No kernel may reach another device: no remote copies, remote signals or barrier semaphores. Data moves between devices by JAX's collectives and lax.ppermute only.
A program may use at most 64 MiB of HBM per device.

v0:
```python
import jax
import jax.numpy as jnp
from jax import lax
from jax.sharding import PartitionSpec as P

ADAM_STEP = 1000


first_decay = 0.9
second_decay = 0.999
learn_rate = 0.001
epsilon = 1e-08


def adam_update(param, grad, moment, square):
    moment_new = first_decay * moment + (1.0 - first_decay) * grad
    square_new = second_decay * square + (1.0 - second_decay) * grad * grad
    first_fix = 1.0 - first_decay**ADAM_STEP
    second_fix = 1.0 - second_decay**ADAM_STEP
    param_new = param - learn_rate * (moment_new / first_fix) / (
        jnp.sqrt(square_new / second_fix) + epsilon
    )
    return (param_new, moment_new, square_new)


def shards(
    activations,
    encoder,
    enc_bias,
    decoder,
    enc_moment,
    enc_square,
    bias_moment,
    bias_square,
    dec_moment,
    dec_square,
):
    row_count = activations.shape[0] * lax.axis_size("dp")
    loss_scale = 2.0 / row_count
    inputs = lax.all_gather(activations, "latent", axis=1, tiled=True)
    enc_low, dec_low = (
        lax.all_gather(encoder.astype(jnp.bfloat16), "dp", axis=0, tiled=True),
        lax.all_gather(decoder.astype(jnp.bfloat16), "dp", axis=0, tiled=True),
    )
    bias_full = lax.all_gather(enc_bias, "dp", axis=0, tiled=True)
    square_sums = lax.psum(jnp.sum(decoder * decoder, axis=0), "dp")
    column_norms = jnp.sqrt(square_sums + 1e-06)
    preact = jnp.dot(inputs, enc_low, preferred_element_type=jnp.float32) + bias_full
    latent_codes = jnp.maximum(preact, 0.0).astype(jnp.bfloat16)
    partial_sums = lax.dot_general(
        latent_codes, dec_low, (((1,), (1,)), ((), ())), preferred_element_type=jnp.float32
    )
    rebuilt = lax.psum_scatter(partial_sums, "latent", scatter_dimension=1, tiled=True)
    error = (activations.astype(jnp.float32) - rebuilt).astype(jnp.bfloat16)
    full_error = lax.all_gather(error, "latent", axis=1, tiled=True)
    active_sum = lax.psum(jnp.sum(latent_codes.astype(jnp.float32), axis=0), "dp")
    grad_dec_rows = -loss_scale * lax.dot_general(
        full_error, latent_codes, (((0,), (0,)), ((), ())), preferred_element_type=jnp.float32
    )
    code_grad = (
        -loss_scale * jnp.dot(full_error, dec_low, preferred_element_type=jnp.float32)
        + column_norms / row_count
    )
    grad_preact = jnp.where(preact > 0.0, code_grad, 0.0)
    grad_encoder = lax.dot_general(
        inputs,
        grad_preact.astype(jnp.bfloat16),
        (((0,), (0,)), ((), ())),
        preferred_element_type=jnp.float32,
    )
    grad_bias = jnp.sum(grad_preact, axis=0)
    grad_encoder, grad_dec_rows, grad_bias = (
        lax.psum_scatter(grad_encoder, "dp", scatter_dimension=0, tiled=True),
        lax.psum_scatter(grad_dec_rows, "dp", scatter_dimension=0, tiled=True),
        lax.psum_scatter(grad_bias, "dp", scatter_dimension=0, tiled=True),
    )
    grad_decoder = grad_dec_rows + decoder * (active_sum / column_norms) / row_count
    new_encoder, new_enc_moment, new_enc_square = adam_update(
        encoder, grad_encoder, enc_moment, enc_square
    )
    new_enc_bias, new_bias_moment, new_bias_square = adam_update(
        enc_bias, grad_bias, bias_moment, bias_square
    )
    new_decoder, new_dec_moment, new_dec_square = adam_update(
        decoder, grad_decoder, dec_moment, dec_square
    )
    return (
        error,
        new_encoder,
        new_enc_bias,
        new_decoder,
        new_enc_moment,
        new_enc_square,
        new_bias_moment,
        new_bias_square,
        new_dec_moment,
        new_dec_square,
    )


def solution(mesh):
    in_specs = (
        P(("groups", "dp"), "latent"),
        P(("groups", "dp"), "latent"),
        P(("groups", "latent", "dp")),
        P(("groups", "dp"), "latent"),
        P(("groups", "dp"), "latent"),
        P(("groups", "dp"), "latent"),
        P(("groups", "latent", "dp")),
        P(("groups", "latent", "dp")),
        P(("groups", "dp"), "latent"),
        P(("groups", "dp"), "latent"),
    )
    out_specs = (
        P(("groups", "dp"), "latent"),
        P(("groups", "dp"), "latent"),
        P(("groups", "latent", "dp")),
        P(("groups", "dp"), "latent"),
        P(("groups", "dp"), "latent"),
        P(("groups", "dp"), "latent"),
        P(("groups", "latent", "dp")),
        P(("groups", "latent", "dp")),
        P(("groups", "dp"), "latent"),
        P(("groups", "dp"), "latent"),
    )
    return jax.shard_map(shards, mesh=mesh, in_specs=in_specs, out_specs=out_specs, check_vma=False)
```

profile of v0, /device:TPU:0, one launch (start us, length us, event | category | flops | bytes accessed | tf_op | source)
XLA Modules:
  0.0 312.8 jit_solution(15528149386761069267)
XLA Ops:
  7.2 0.0 all-gather.6.cloned.1.call-start
  7.2 0.7 all-gather.6.cloned.1.call-update
  7.9 0.0 all-gather.8.cloned.1.call-start
  8.0 2.1 convert_element_type.22
  10.1 0.0 all-gather.10.cloned.1.call-start
  10.1 0.9 multiply_reduce_fusion
  11.1 0.0 reduce-scatter.4.cloned.1.call-start
  11.1 6.0 %all-gather = f32[4,1,128]{2,1,0:T(1,128)S(1)} all-gather(f32[1,1,128]{2,1,0:T(1,128)S(1)} %bitcast.14), channel_id=1, replica_groups=mesh['groups'=2,'latent'=4,'dp'=4] {'dp'}, dimensions={0}, use_global_device_ids=true | all-gather | bytes 2560 | tf_op jit(solution)/shard_map/all_gather | solution.py:45
  17.1 32.3 %all-gather.6.cloned.1.call-done = bf16[384,2048]{1,0:T(8,128)(2,1)} async-done(((bf16[384,512]{1,0:T(8,128)(2,1)}), bf16[384,2048]{1,0:T(8,128)(2,1)}) %all-gather.6.cloned.1.call-update) | async-done | bytes 1572880 | tf_op jit(solution)/shard_map/all_gather | solution.py:40
  49.4 23.6 %all-gather.8.cloned.1.call-done = bf16[2048,512]{1,0:T(8,128)(2,1)} async-done(((bf16[512,512]{1,0:T(8,128)(2,1)}), bf16[2048,512]{1,0:T(8,128)(2,1)}) %all-gather.8.cloned.1.call-update) | async-done | bytes 2097168 | tf_op jit(solution)/shard_map/all_gather | solution.py:42
  73.0 3.1 convert_reduce_fusion
  76.1 21.7 %all-gather.10.cloned.1.call-done = bf16[2048,512]{1,0:T(8,128)(2,1)} async-done(((bf16[512,512]{1,0:T(8,128)(2,1)}), bf16[2048,512]{1,0:T(8,128)(2,1)}) %all-gather.10.cloned.1.call-update) | async-done | bytes 2097168 | tf_op jit(solution)/shard_map/all_gather | solution.py:43
  97.8 4.3 %fusion.8 = f32[384,2048]{1,0:T(8,128)} fusion(bf16[2048,512]{1,0:T(8,128)(2,1)} %all-gather.10.cloned.1.call-done, f32[384,512]{1,0:T(8,128)S(1)} %get-tuple-element.46), kind=kOutput, calls=%fused_computation.27 | convolution fusion | flops 805699584 | bytes 6029312 | tf_op jit(solution)/shard_map/dot_general | solution.py:50
  102.1 0.0 reduce-scatter.4.cloned.1.call-update
  102.1 0.0 all-gather.12.cloned.1.call-start
  102.1 60.4 %reduce-scatter.4.cloned.1.call-done = f32[384,512]{1,0:T(8,128)} async-done(((f32[384,2048]{1,0:T(8,128)}), f32[384,512]{1,0:T(8,128)}) %reduce-scatter.4.cloned.1.call-update) | async-done | bytes 786448 | tf_op jit(solution)/shard_map/reduce_scatter | solution.py:53
  162.5 2.0 subtract_convert_fusion
  164.5 0.0 all-gather.12.cloned.1.call-update
  164.5 0.0 reduce-scatter.8.cloned.1.call-start
  164.6 37.2 %all-gather.12.cloned.1.call-done = bf16[384,2048]{1,0:T(8,128)(2,1)} async-done(((bf16[384,512]{1,0:T(8,128)(2,1)}), bf16[384,2048]{1,0:T(8,128)(2,1)}) %all-gather.12.cloned.1.call-update) | async-done | bytes 1572880 | tf_op jit(solution)/shard_map/all_gather | solution.py:55
  201.8 4.7 %convolution_multiply_fusion = f32[2048,512]{0,1:T(8,128)} fusion(bf16[384,2048]{1,0:T(8,128)(2,1)} %all-gather.12.cloned.1.call-done, f32[384,512]{1,0:T(8,128)S(1)} %get-tuple-element.46), kind=kOutput, calls=%fused_computation | convolution fusion | flops 806748160 | bytes 6553600 | tf_op jit(solution)/shard_map/dot_general | solution.py:57
  206.5 0.0 reduce-scatter.8.cloned.1.call-update
  206.5 0.0 reduce-scatter.6.cloned.1.call-start
  206.5 6.5 %psum.14 = f32[512]{0:T(512)S(1)} all-reduce(f32[512]{0:T(512)S(1)} %get-tuple-element.41), channel_id=1, replica_groups=mesh['groups'=2,'latent'=4,'dp'=4] {'dp'}, use_global_device_ids=true, to_apply=%region_2.0 | all-reduce | flops 512 | bytes 4096 | tf_op jit(solution)/shard_map/psum | solution.py:46
  213.1 3.4 %fusion.12 = (f32[512]{0:T(512)S(1)}, bf16[384,512]{1,0:T(8,128)(2,1)S(1)}) fusion(f32[512]{0:T(512)S(1)} %fusion.6, bf16[384,2048]{1,0:T(8,128)(2,1)S(1)} %copy-done.4, bf16[2048,512]{1,0:T(8,128)(2,1)} %all-gather.10.cloned.1.call-done, f32[384,512]{1,0:T(8,128)S(1)} %get-tuple-element.46), kind=kOutput, calls=%fused_computation.28 | convolution fusion | flops 806485504 | bytes 4853760 | tf_op jit(solution)/shard_map/dot_general | solution.py:61
  216.5 3.3 %convolution_bitcast_fusion = f32[2048,512]{0,1:T(8,128)} fusion(bf16[384,2048]{1,0:T(8,128)(2,1)S(1)} %copy-done.6, bf16[384,512]{1,0:T(8,128)(2,1)S(1)} %get-tuple-element.44), kind=kOutput, calls=%fused_computation.1 | convolution fusion | flops 805306368 | bytes 6160384 | tf_op jit(solution)/shard_map/dot_general | solution.py:65
  219.7 0.0 reduce-scatter.6.cloned.1.call-update
  219.8 1.3 copy.41
  221.1 0.3 copy.36
  221.4 0.3 copy-done.7
  221.7 1.3 copy.37
  223.0 1.3 copy.40
  224.3 0.2 copy-done.9
  224.6 0.3 copy.34
  224.9 1.6 copy.35
  226.5 0.6 dynamic-slice
  227.7 6.2 %all-reduce.1 = (f32[512]{0:T(512)S(1)}, f32[512]{0:T(512)S(1)}) all-reduce(f32[512]{0:T(512)S(1)} %get-tuple-element.43, f32[512]{0:T(512)S(1)} %get-tuple-element.45), channel_id=4, replica_groups=mesh['groups'=2,'latent'=4,'dp'=4] {'dp'}, use_global_device_ids=true, to_apply=%region_5.6.clone | all-reduce | flops 1024 | bytes 8192
  233.9 0.6 divide_subtract_fusion.2
  234.5 15.6 %reduce-scatter.8.cloned.1.call-done = f32[512,512]{0,1:T(8,128)} async-done(((f32[2048,512]{0,1:T(8,128)}), f32[512,512]{0,1:T(8,128)}) %reduce-scatter.8.cloned.1.call-update) | async-done | bytes 1048592 | tf_op jit(solution)/shard_map/reduce_scatter | solution.py:74
  250.1 4.7 %divide_subtract_fusion = (f32[512,512]{0,1:T(8,128)}, f32[512,512]{0,1:T(8,128)}, f32[512,512]{0,1:T(8,128)}) fusion(f32[512,512]{0,1:T(8,128)} %copy.41, f32[512,512]{0,1:T(8,128)} %reduce-scatter.8.cloned.1.call-done, f32[512]{0:T(512)S(1)} %fusion.5, f32[512,512]{0,1:T(8,128)} %copy.37, f32[512,512]{0,1:T(8,128)} %copy.40), kind=kLoop, calls=%fused_computation.10 | loop fusion | flops 3932160 | bytes 7342080 | tf_op jit(solution)/shard_map/sub | solution.py:20
  254.8 2.5 copy.43
  257.3 2.8 copy.46
  260.2 2.8 copy.47
  262.9 34.4 %reduce-scatter.6.cloned.1.call-done = f32[512,512]{0,1:T(8,128)} async-done(((f32[2048,512]{0,1:T(8,128)}), f32[512,512]{0,1:T(8,128)}) %reduce-scatter.6.cloned.1.call-update) | async-done | bytes 1048592 | tf_op jit(solution)/shard_map/reduce_scatter | solution.py:73
  297.3 3.3 %divide_subtract_fusion.1 = (f32[512,512]{0,1:T(8,128)}, f32[512,512]{0,1:T(8,128)}, f32[512,512]{0,1:T(8,128)}) fusion(f32[512,512]{0,1:T(8,128)S(1)} %copy.36, f32[512,512]{0,1:T(8,128)} %reduce-scatter.6.cloned.1.call-done, f32[512,512]{0,1:T(8,128)S(1)} %copy.34, f32[512,512]{0,1:T(8,128)S(1)} %copy.35), kind=kLoop, calls=%fused_computation.13 | loop fusion | flops 3145728 | bytes 7340032 | tf_op jit(solution)/shard_map/sub | solution.py:20
  300.7 2.7 copy.42
  303.4 1.3 copy.44
  304.7 1.3 copy.45
  (30 shorter events, 0.1 us)
Async XLA Ops:
  7.2 3.0 copy-start.2
  7.2 42.2 %all-gather.6.cloned.1.call-start = ((), (), s32[]{:S(2)}) async-start(), calls=%async_computation.3 | async-start | bytes 1966080 | tf_op jit(solution)/shard_map/all_gather | solution.py:40
  7.9 3.2 %copy-start.10 = (f32[128]{0:T(128)S(1)}, f32[128]{0:T(128)}, u32[]{:S(2)}) copy-start(f32[128]{0:T(128)} %param.12) | copy-start | bytes 1540
  7.9 65.1 %all-gather.8.cloned.1.call-start = ((), (), s32[]{:S(2)}) async-start(), calls=%async_computation.4 | async-start | bytes 2621440 | tf_op jit(solution)/shard_map/all_gather | solution.py:42
  10.1 87.7 %all-gather.10.cloned.1.call-start = ((), (), s32[]{:S(2)}) async-start(), calls=%async_computation.5 | async-start | bytes 2621440 | tf_op jit(solution)/shard_map/all_gather | solution.py:43
  11.1 151.4 %reduce-scatter.4.cloned.1.call-start = ((), (), s32[]{:S(2)}) async-start(), calls=%async_computation.6 | async-start | bytes 3932160 | tf_op jit(solution)/shard_map/reduce_scatter | solution.py:53
  102.0 60.4 %copy-start.5 = (bf16[384,512]{1,0:T(8,128)(2,1)S(1)}, bf16[384,512]{1,0:T(8,128)(2,1)}, u32[]{:S(2)}) copy-start(bf16[384,512]{1,0:T(8,128)(2,1)} %param.10) | copy-start | bytes 1179652
  102.1 99.7 %all-gather.12.cloned.1.call-start = ((), (), s32[]{:S(2)}) async-start(), calls=%async_computation.7 | async-start | bytes 1966080 | tf_op jit(solution)/shard_map/all_gather | solution.py:55
  164.5 85.6 %reduce-scatter.8.cloned.1.call-start = ((), (), s32[]{:S(2)}) async-start(), calls=%async_computation.9 | async-start | bytes 5242880 | tf_op jit(solution)/shard_map/reduce_scatter | solution.py:74
  206.5 6.6 %copy-start.4 = (bf16[384,2048]{1,0:T(8,128)(2,1)S(1)}, bf16[384,2048]{1,0:T(8,128)(2,1)}, u32[]{:S(2)}) copy-start(bf16[384,2048]{1,0:T(8,128)(2,1)} %all-gather.12.cloned.1.call-done) | copy-start | bytes 4718596
  206.5 90.9 %reduce-scatter.6.cloned.1.call-start = ((), (), s32[]{:S(2)}) async-start(), calls=%async_computation.8 | async-start | bytes 5242880 | tf_op jit(solution)/shard_map/reduce_scatter | solution.py:73
  213.1 3.4 %copy-start.6 = (bf16[384,2048]{1,0:T(8,128)(2,1)S(1)}, bf16[384,2048]{1,0:T(8,128)(2,1)}, u32[]{:S(2)}) copy-start(bf16[384,2048]{1,0:T(8,128)(2,1)} %all-gather.6.cloned.1.call-done) | copy-start | bytes 4718596
  219.8 1.3 copy-start.3
  219.8 1.9 copy-start.7
  221.7 1.3 copy-start.8
  223.0 1.6 copy-start.9
  224.6 1.9 copy-start.13
  224.6 9.3 %copy-start.11 = (f32[128]{0:T(128)S(1)}, f32[128]{0:T(128)}, u32[]{:S(2)}) copy-start(f32[128]{0:T(128)} %param.16) | copy-start | bytes 1540
  224.6 9.3 %copy-start.12 = (f32[128]{0:T(128)S(1)}, f32[128]{0:T(128)}, u32[]{:S(2)}) copy-start(f32[128]{0:T(128)} %param.17) | copy-start | bytes 1540
  300.7 2.7 copy-start.1
  300.7 4.0 %copy-start = (f32[512,512]{0,1:T(8,128)S(1)}, f32[512,512]{0,1:T(8,128)}, u32[]{:S(2)}) copy-start(f32[512,512]{0,1:T(8,128)} %get-tuple-element.40) | copy-start | bytes 3145732
Sparse Core Ops, SparseCore 0:
  9.6 39.7 all-gather.5
  51.5 21.4 all-gather.7
  75.2 22.5 all-gather.9
  102.2 60.2 reduce-scatter.3
  164.6 37.1 all-gather.11
  206.6 43.4 reduce-scatter.7
  252.8 44.5 reduce-scatter.5
where the time goes:
time: 313 us
  waiting for transfers between devices  226 us (72%)
  local copies, waits for them, and re-layouts  20.7 us (7%)
  blocking collectives  18.7 us (6%)
  matrix products  18.6 us (6%)
  between operations  14.9 us (5%)
  other arithmetic  13.6 us (4%)
    reduce_scatter x1, waiting for transfers between devices, shards(): lax.psum_scatter(partial_sums, 'latent', scatter_dimension=1, tiled=True)  60.4 us
    all_gather x1, waiting for transfers between devices, shards(): full_error = lax.all_gather(error, 'latent', axis=1, tiled=True)  37.2 us
    reduce_scatter x1, waiting for transfers between devices, shards(): lax.psum_scatter(grad_encoder, 'dp', scatter_dimension=0, tiled=True)  34.4 us
    all_gather x1, waiting for transfers between devices, shards(): inputs = lax.all_gather(activations, 'latent', axis=1, tiled=True)  32.3 us
    all_gather x1, waiting for transfers between devices, shards(): lax.all_gather(encoder.astype(jnp.bfloat16), 'dp', axis=0, tiled=True)  23.6 us
    all_gather x1, waiting for transfers between devices, shards(): lax.all_gather(decoder.astype(jnp.bfloat16), 'dp', axis=0, tiled=True)  21.7 us
    unnamed x41, local copies, waits for them, and re-layouts  20.7 us
    reduce_scatter x1, waiting for transfers between devices, shards(): lax.psum_scatter(grad_dec_rows, 'dp', scatter_dimension=0, tiled=True)  15.6 us
  transfers between devices with their start and end apart: 7, of which 7 were waited for; matrix products, arithmetic and copies ran while one was open for 10% of the time, Pallas kernels for 0%

commit v1 on v0

--- a/solution.py
+++ b/solution.py
@@ -1,6 +1,10 @@
+import functools
+
 import jax
 import jax.numpy as jnp
 from jax import lax
+from jax.experimental import pallas as pl
+from jax.experimental.pallas import tpu as pltpu
 from jax.sharding import PartitionSpec as P
 
 ADAM_STEP = 1000
@@ -10,6 +14,10 @@
 second_decay = 0.999
 learn_rate = 0.001
 epsilon = 1e-08
+
+F32 = jnp.float32
+BF16 = jnp.bfloat16
+CHUNKS = 2
 
 
 def adam_update(param, grad, moment, square):
@@ -98,6 +106,330 @@
     )
 
 
+VMEM = pl.BlockSpec(memory_space=pltpu.VMEM)
+SMEM = pl.BlockSpec(memory_space=pltpu.SMEM)
+
+
+def local_kernel(body, outs, place, *args, flops):
+    moved = sum(a.size * a.dtype.itemsize for a in args)
+    moved += sum(o.size * jnp.dtype(o.dtype).itemsize for o in outs)
+    return pl.pallas_call(
+        body,
+        out_shape=outs,
+        in_specs=[SMEM] + [VMEM] * len(args),
+        out_specs=[VMEM] * len(outs),
+        compiler_params=pltpu.CompilerParams(vmem_limit_bytes=48 * 1024 * 1024),
+        cost_estimate=pl.CostEstimate(flops=flops, bytes_accessed=moved, transcendentals=0),
+    )(place, *args)
+
+
+def shape(dims, dtype):
+    return jax.ShapeDtypeStruct(dims, dtype)
+
+
+def columns(start, width):
+    return pl.ds(pl.multiple_of(start, width), width)
+
+
+def codes_body(place, own, low, high, across, relay, enc, bias, codes, mask, full, active):
+    z, i = place[0], place[1]
+    width = own.shape[1]
+    full[:, columns(z * width, width)] = own[...]
+    full[:, columns(((z + 2) % 4) * width, width)] = across[...]
+
+    @pl.when(z < 3)
+    def _():
+        full[:, columns((z + 1) * width, width)] = high[...]
+
+    @pl.when(z == 3)
+    def _():
+        full[:, :width] = relay[...]
+
+    @pl.when(z > 0)
+    def _():
+        full[:, columns((z - 1) * width, width)] = low[...]
+
+    @pl.when(z == 0)
+    def _():
+        full[:, 3 * width :] = relay[...]
+
+    total = jnp.zeros(codes.shape, F32)
+    pieces = []
+    for b in range(4):
+        slot = b ^ i
+        total += jnp.dot(
+            full[:, b * width : (b + 1) * width],
+            enc[columns(slot * width, width), :],
+            preferred_element_type=F32,
+        )
+        pieces.append(bias[pl.ds(slot, 1), :])
+    preact = total + jnp.concatenate(pieces, axis=1)
+    low_codes = jnp.maximum(preact, 0.0).astype(BF16)
+    codes[...] = low_codes
+    mask[...] = (preact > 0.0).astype(F32).astype(BF16)
+    active[...] = jnp.sum(low_codes.astype(F32), axis=0, keepdims=True)
+
+
+def error_body(place, own, low, high, across, dec0, dec1, dec2, dec3, inputs, error):
+    z, i = place[0], place[1]
+    half = dec0.shape[0] // 4
+    shift = jnp.where(z >= 2, half, 0)
+    for t, dec in enumerate((dec0, dec1, dec2, dec3)):
+        total = jnp.zeros((own.shape[0], half), F32)
+        for m, codes in enumerate((own, low, high, across)):
+            total += lax.dot_general(
+                codes[...],
+                dec[m * half : (m + 1) * half, :],
+                (((1,), (1,)), ((), ())),
+                preferred_element_type=F32,
+            )
+        q = i ^ t
+        given = inputs[:, columns(q * 2 * half + shift, half)].astype(F32)
+        error[:, columns(q * half, half)] = (given - total).astype(BF16)
+
+
+def grad_code_body(
+    rows, place, mine, swapped, passed, relayed, mask, dec, norms, grad_low, bias_sum, full, home
+):
+    z, i = place[0], place[1]
+    half = mine.shape[1] // 4
+    width = 2 * half
+    for q in range(4):
+        piece = slice(q * half, (q + 1) * half)
+        first = slice(q * width, q * width + half)
+        second = slice(q * width + half, (q + 1) * width)
+
+        @pl.when(z == 0)
+        def _():
+            full[:, first] = passed[:, piece]
+            full[:, second] = relayed[:, piece]
+
+        @pl.when(z == 1)
+        def _():
+            full[:, first] = mine[:, piece]
+            full[:, second] = swapped[:, piece]
+
+        @pl.when(z == 2)
+        def _():
+            full[:, first] = swapped[:, piece]
+            full[:, second] = mine[:, piece]
+
+        @pl.when(z == 3)
+        def _():
+            full[:, first] = relayed[:, piece]
+            full[:, second] = passed[:, piece]
+
+    total = jnp.zeros(grad_low.shape, F32)
+    for b in range(4):
+        total += jnp.dot(
+            full[:, b * width : (b + 1) * width],
+            dec[columns((b ^ i) * width, width), :],
+            preferred_element_type=F32,
+        )
+    code_grad = (-2.0 / rows) * total + norms[...] / rows
+    grad = jnp.where(mask[...] > 0, code_grad, 0.0)
+    grad_low[...] = grad.astype(BF16)
+    bias_sum[...] = jnp.sum(grad, axis=0, keepdims=True)
+    home[...] = full[:, columns(z * width, width)]
+
+
+def grad_body(scale, slots, place, *refs):
+    i = place[1]
+    lefts, rights = refs[:CHUNKS], refs[CHUNKS : 2 * CHUNKS]
+    outs = refs[2 * CHUNKS :]
+    width = outs[0].shape[0]
+    for slot, out in zip(slots, outs):
+        total = jnp.zeros(out.shape, F32)
+        for left, right in zip(lefts, rights):
+            total += lax.dot_general(
+                left[:, columns((i ^ slot) * width, width)],
+                right[...],
+                (((0,), (0,)), ((), ())),
+                preferred_element_type=F32,
+            )
+        out[...] = scale * total
+
+
+def line_shards(
+    activations,
+    encoder,
+    enc_bias,
+    decoder,
+    enc_moment,
+    enc_square,
+    bias_moment,
+    bias_square,
+    dec_moment,
+    dec_square,
+):
+    rows = activations.shape[0] * 4
+    chunk = activations.shape[0] // CHUNKS
+    width = activations.shape[1]
+    latents = encoder.shape[1]
+    half = width // 2
+    features = 4 * width
+    z, i = lax.axis_index("latent"), lax.axis_index("dp")
+    place = jnp.stack([z, i]).astype(jnp.int32)
+
+    def along(value, pairs):
+        return lax.ppermute(value, "latent", pairs)
+
+    def flip(value, bits):
+        return lax.ppermute(value, "dp", [(k, k ^ bits) for k in range(4)])
+
+    def sum_dp(value):
+        return (value + flip(value, 1)) + (flip(value, 2) + flip(value, 3))
+
+    def by_slot(value):
+        core, chip = flip(value, 1), flip(value, 2)
+        return [value, core, chip, flip(chip, 1)]
+
+    up = [(0, 1), (1, 2), (2, 3)]
+    down = [(1, 0), (2, 1), (3, 2)]
+    two = [(0, 2), (1, 3), (2, 0), (3, 1)]
+
+    parts = [activations[c * chunk : (c + 1) * chunk] for c in range(CHUNKS)]
+    gathered = []
+    for part in parts:
+        low, high, across = along(part, up), along(part, down), along(part, two)
+        relay = along(across, [(2, 3), (1, 0)])
+        gathered.append((part, low, high, across, relay))
+
+    enc_all = jnp.concatenate(by_slot(encoder.astype(BF16)), axis=0)
+    bias_all = jnp.stack(by_slot(enc_bias), axis=0)
+    dec_low = decoder.astype(BF16)
+    dec_all = jnp.concatenate(by_slot(dec_low), axis=0)
+    norms = jnp.sqrt(sum_dp(jnp.sum(decoder * decoder, axis=0, keepdims=True)) + 1e-06)
+
+    first, second = dec_low[:half], dec_low[half:]
+    mine = jnp.where(z >= 2, second, first)
+    dec_rows = jnp.concatenate(
+        [
+            mine,
+            along(jnp.where(z >= 1, second, first), [(0, 1), (1, 2)]),
+            along(jnp.where(z >= 3, second, first), [(2, 1), (3, 2)]),
+            along(jnp.where(z >= 2, first, second), [(0, 2), (3, 1)]),
+        ],
+        axis=0,
+    )
+    dec_rows = by_slot(dec_rows)
+
+    flops = 2 * chunk * features * latents
+    inputs, codes, masks, actives, errors = [], [], [], [], []
+    for part in gathered:
+        low_codes, mask, full, active = local_kernel(
+            codes_body,
+            [
+                shape((chunk, latents), BF16),
+                shape((chunk, latents), BF16),
+                shape((chunk, features), BF16),
+                shape((1, latents), F32),
+            ],
+            place,
+            *part,
+            enc_all,
+            bias_all,
+            flops=flops,
+        )
+        inputs.append(full)
+        codes.append(low_codes)
+        masks.append(mask)
+        actives.append(active)
+        low = along(low_codes, [(0, 1), (1, 2)])
+        high = along(low_codes, [(2, 1), (3, 2)])
+        across = along(low_codes, [(0, 2), (3, 1)])
+        (own_error,) = local_kernel(
+            error_body,
+            [shape((chunk, features // 2), BF16)],
+            place,
+            low_codes,
+            low,
+            high,
+            across,
+            *dec_rows,
+            full,
+            flops=2 * flops,
+        )
+        passed = along(own_error, [(1, 0), (2, 3)])
+        swapped = along(own_error, [(1, 2), (2, 1)])
+        relayed = along(swapped, [(1, 0), (2, 3)])
+        errors.append((own_error, swapped, passed, relayed))
+
+    active_sum = sum_dp(functools.reduce(jnp.add, actives))
+
+    grads, bias_sums, fulls, homes = [], [], [], []
+    for error, mask in zip(errors, masks):
+        grad_low, bias_sum, full, home = local_kernel(
+            functools.partial(grad_code_body, rows),
+            [
+                shape((chunk, latents), BF16),
+                shape((1, latents), F32),
+                shape((chunk, features), BF16),
+                shape((chunk, width), BF16),
+            ],
+            place,
+            *error,
+            mask,
+            dec_all,
+            norms,
+            flops=flops,
+        )
+        grads.append(grad_low)
+        bias_sums.append(bias_sum)
+        fulls.append(full)
+        homes.append(home)
+    error = jnp.concatenate(homes, axis=0)
+
+    def reduced(scale, lefts, rights):
+        def slots(*which):
+            return local_kernel(
+                functools.partial(grad_body, scale, which),
+                [shape((width, latents), F32)] * 2,
+                place,
+                *lefts,
+                *rights,
+                flops=CHUNKS * flops // 2,
+            )
+
+        send_far, send_near = slots(3, 1)
+        keep_far, keep_near = slots(2, 0)
+        far = keep_far + flip(send_far, 1)
+        largest = jnp.maximum(jnp.max(jnp.abs(far), axis=0, keepdims=True), 1e-30)
+        sent = (far * (16384.0 / largest)).astype(jnp.float16)
+        near = keep_near + flip(send_near, 1)
+        return near + flip(sent, 2).astype(F32) * (flip(largest, 2) / 16384.0)
+
+    grad_dec_rows = reduced(-2.0 / rows, fulls, codes)
+    grad_encoder = reduced(1.0, inputs, grads)
+    grad_bias = sum_dp(functools.reduce(jnp.add, bias_sums))
+    grad_bias = lax.dynamic_slice(
+        grad_bias.reshape(latents), (i * enc_bias.shape[0],), (enc_bias.shape[0],)
+    )
+    grad_decoder = grad_dec_rows + decoder * (active_sum / norms) / rows
+
+    new_decoder, new_dec_moment, new_dec_square = adam_update(
+        decoder, grad_decoder, dec_moment, dec_square
+    )
+    new_enc_bias, new_bias_moment, new_bias_square = adam_update(
+        enc_bias, grad_bias, bias_moment, bias_square
+    )
+    new_encoder, new_enc_moment, new_enc_square = adam_update(
+        encoder, grad_encoder, enc_moment, enc_square
+    )
+    return (
+        error,
+        new_encoder,
+        new_enc_bias,
+        new_decoder,
+        new_enc_moment,
+        new_enc_square,
+        new_bias_moment,
+        new_bias_square,
+        new_dec_moment,
+        new_dec_square,
+    )
+
+
 def solution(mesh):
     in_specs = (
         P(("groups", "dp"), "latent"),
@@ -123,4 +455,6 @@
         P(("groups", "dp"), "latent"),
         P(("groups", "dp"), "latent"),
     )
-    return jax.shard_map(shards, mesh=mesh, in_specs=in_specs, out_specs=out_specs, check_vma=False)
+    line = mesh.shape["latent"] == 4 and mesh.shape["dp"] == 4
+    plan = line_shards if line else shards
+    return jax.shard_map(plan, mesh=mesh, in_specs=in_specs, out_specs=out_specs, check_vma=False)

time: 313 us -> 219 us (0.70)
  waiting for transfers between devices: 226 us -> 114 us
  starting transfers between devices: 0.29 us -> 68.1 us
  blocking collectives: 18.7 us -> 0 us
  matrix products: 18.6 us -> 0 us
  Pallas kernels: 0 us -> 18 us
  local copies, waits for them, and re-layouts: 20.7 us -> 2.7 us
  between operations: 14.9 us -> 1.35 us
    all_gather x4 -> x0, waiting for transfers between devices: 115 us -> none  [the longest x1 37.2 us: shards(): full_error = lax.all_gather(error, 'latent', axis=1, tiled=True)]
    ppermute x0 -> x52, waiting for transfers between devices: none -> 114 us  [the longest x23 59.3 us: along(): return lax.ppermute(value, 'latent', pairs)]
    reduce_scatter x3 -> x0, waiting for transfers between devices: 110 us -> none  [the longest x1 60.4 us: shards(): lax.psum_scatter(partial_sums, 'latent', scatter_dimension=1, tiled=True)]
    ppermute x0 -> x52, starting transfers between devices: none -> 68.1 us  [the longest x23 51.4 us: along(): return lax.ppermute(value, 'latent', pairs)]
    dot_general x5 -> x0, matrix products: 18.6 us -> none  [the longest x1 4.67 us: shards(): lax.dot_general(full_error, latent_codes, (((0,), (0,)), ((), ())), prefe...]
    unnamed x41 -> x48, local copies, waits for them, and re-layouts: 20.7 us -> 2.67 us
    pallas_call x0 -> x10, Pallas kernels: none -> 18 us  [local_kernel(): pl.pallas_call(body, out_shape=outs, in_specs=[SMEM] + [VMEM] * len(args)...]
    psum x1 -> x0, blocking collectives: 6.54 us -> none  [shards(): square_sums = lax.psum(jnp.sum(decoder * decoder, axis=0), 'dp')]
  transfers between devices with their start and end apart: 7 -> 52, of which waited for: 7 -> 19; matrix products, arithmetic and copies ran while one was open for 10% -> 4% of each run, Pallas kernels for 0% -> 7%
where the time goes in v1:
time: 219 us; the launch traced here: 218 us
  waiting for transfers between devices  114 us (52%)
  starting transfers between devices  68.1 us (31%)
  Pallas kernels  18 us (8%)
  other arithmetic  14.4 us (7%)
  local copies, waits for them, and re-layouts  2.7 us (1%)
    ppermute x23, waiting for transfers between devices, along(): return lax.ppermute(value, 'latent', pairs)  59.3 us
    ppermute x29, waiting for transfers between devices, flip(): return lax.ppermute(value, 'dp', [(k, k ^ bits) for k in range(4)])  54.4 us
    ppermute x23, starting transfers between devices, along(): return lax.ppermute(value, 'latent', pairs)  51.4 us
    pallas_call x10, Pallas kernels, local_kernel(): pl.pallas_call(body, out_shape=outs, in_specs=[SMEM] + [VMEM] * len(args)...  18 us
    ppermute x29, starting transfers between devices, flip(): return lax.ppermute(value, 'dp', [(k, k ^ bits) for k in range(4)])  16.7 us
    sub x3, other arithmetic, adam_update(): param - learn_rate * (moment_new / first_fix) / (jnp.sqrt(square_new / se...  5.26 us
  transfers between devices with their start and end apart: 52, of which 19 were waited for; matrix products, arithmetic and copies ran while one was open for 4% of the time, Pallas kernels for 7%

profile of v1, /device:TPU:0, one launch (start us, length us, event | category | flops | bytes accessed | tf_op | source)
XLA Modules:
  0.0 218.2 jit_solution(6477399411133515885)
XLA Ops:
  0.7 2.5 %multiply_reduce_fusion = (f32[512]{0:T(512)S(1)}, bf16[512,512]{1,0:T(8,128)(2,1)}) fusion(f32[512,512]{1,0:T(8,128)} %param.13), kind=kLoop, calls=%fused_computation.17 | loop fusion | flops 785920 | bytes 1574912 | tf_op jit(solution)/shard_map/reduce_sum | solution.py:302
  5.1 5.6 %collective-permute-start.13 = (bf16[256,512]{1,0:T(8,128)(2,1)S(1)}, bf16[256,512]{1,0:T(8,128)(2,1)S(1)}, u32[]{:S(2)}, u32[]{:S(2)}) collective-permute-start(bf16[256,512]{1,0:T(8,128)(2,1)S(1)} %get-tuple-element.77), channel_id=1, source_target_pairs={{0,4},{4,8},{1,5},{5,9},{2,6},{6,10},{3,7},{7,11},{16,20},{20,24},... | collective-permute-start | bytes 786440 | tf_op jit(solution)/shard_map/ppermute | solution.py:275
  10.7 3.4 %collective-permute-start.15 = (bf16[256,512]{1,0:T(8,128)(2,1)S(1)}, bf16[256,512]{1,0:T(8,128)(2,1)S(1)}, u32[]{:S(2)}, u32[]{:S(2)}) collective-permute-start(bf16[256,512]{1,0:T(8,128)(2,1)S(1)} %get-tuple-element.78), channel_id=1, source_target_pairs={{0,8},{12,4},{1,9},{13,5},{2,10},{14,6},{3,11},{15,7},{16,24},{28,... | collective-permute-start | bytes 786440 | tf_op jit(solution)/shard_map/ppermute | solution.py:275
  14.1 3.3 %collective-permute-done.13 = bf16[256,512]{1,0:T(8,128)(2,1)S(1)} collective-permute-done((bf16[256,512]{1,0:T(8,128)(2,1)S(1)}, bf16[256,512]{1,0:T(8,128)(2,1)S(1)}, u32[]{:S(2)}, u32[]{:S(2)}) %collective-permute-start.13) | collective-permute-done | bytes 262176 | tf_op jit(solution)/shard_map/ppermute | solution.py:275
  17.4 4.5 %collective-permute-done.15 = bf16[256,512]{1,0:T(8,128)(2,1)S(1)} collective-permute-done((bf16[256,512]{1,0:T(8,128)(2,1)S(1)}, bf16[256,512]{1,0:T(8,128)(2,1)S(1)}, u32[]{:S(2)}, u32[]{:S(2)}) %collective-permute-start.15) | collective-permute-done | bytes 262176 | tf_op jit(solution)/shard_map/ppermute | solution.py:275
  22.0 1.6 collective-permute-start.17
  24.2 4.3 %collective-permute-start.2 = (bf16[192,512]{1,0:T(8,128)(2,1)S(1)}, bf16[192,512]{1,0:T(8,128)(2,1)S(1)}, u32[]{:S(2)}, u32[]{:S(2)}) collective-permute-start(bf16[192,512]{1,0:T(8,128)(2,1)S(1)} %get-tuple-element.79.own), channel_id=1, source_target_pairs={{0,8},{4,12},{8,0},{12,4},{1,9},{5,13},{9,1},{13,5},{2,10},{6,14},... | collective-permute-start | bytes 589832 | tf_op jit(solution)/shard_map/ppermute | solution.py:275
  31.0 1.5 collective-permute-start.8
  32.5 24.9 %collective-permute-done.8 = f32[128]{0:T(128)S(1)} collective-permute-done((f32[128]{0:T(128)S(1)}, f32[128]{0:T(128)S(1)}, u32[]{:S(2)}, u32[]{:S(2)}) %collective-permute-start.8) | collective-permute-done | bytes 544 | tf_op jit(solution)/shard_map/ppermute | solution.py:278
  58.5 3.9 %collective-permute-start = (bf16[192,512]{1,0:T(8,128)(2,1)S(1)}, bf16[192,512]{1,0:T(8,128)(2,1)S(1)}, u32[]{:S(2)}, u32[]{:S(2)}) collective-permute-start(bf16[192,512]{1,0:T(8,128)(2,1)S(1)} %get-tuple-element.79.own), channel_id=1, source_target_pairs={{0,4},{4,8},{8,12},{1,5},{5,9},{9,13},{2,6},{6,10},{10,14},{3,7},{... | collective-permute-start | bytes 589832 | tf_op jit(solution)/shard_map/ppermute | solution.py:275
  62.4 1.5 collective-permute-start.30
  63.9 1.3 collective-permute-start.29
  65.2 2.4 %collective-permute-done.low = bf16[192,512]{1,0:T(8,128)(2,1)S(1)} collective-permute-done((bf16[192,512]{1,0:T(8,128)(2,1)S(1)}, bf16[192,512]{1,0:T(8,128)(2,1)S(1)}, u32[]{:S(2)}, u32[]{:S(2)}) %collective-permute-start) | collective-permute-done | bytes 196640 | tf_op jit(solution)/shard_map/ppermute | solution.py:275
  68.2 7.2 %collective-permute-done.30.across = bf16[192,512]{1,0:T(8,128)(2,1)S(1)} collective-permute-done((bf16[192,512]{1,0:T(8,128)(2,1)S(1)}, bf16[192,512]{1,0:T(8,128)(2,1)S(1)}, u32[]{:S(2)}, u32[]{:S(2)}) %collective-permute-start.30) | collective-permute-done | bytes 196640 | tf_op jit(solution)/shard_map/ppermute | solution.py:275
  75.4 1.3 collective-permute-start.3
  77.3 5.8 %collective-permute-done.3.relay = bf16[192,512]{1,0:T(8,128)(2,1)S(1)} collective-permute-done((bf16[192,512]{1,0:T(8,128)(2,1)S(1)}, bf16[192,512]{1,0:T(8,128)(2,1)S(1)}, u32[]{:S(2)}, u32[]{:S(2)}) %collective-permute-start.3) | collective-permute-done | bytes 196640 | tf_op jit(solution)/shard_map/ppermute | solution.py:275
  83.0 1.5 collective-permute-start.23
  84.6 1.5 collective-permute-start.28
  86.1 1.3 collective-permute-start.31
  87.4 1.5 pad_maximum_fusion.enc
  90.2 8.6 %collective-permute-start.12 = (bf16[192,512]{1,0:T(8,128)(2,1)S(1)}, bf16[192,512]{1,0:T(8,128)(2,1)S(1)}, u32[]{:S(2)}, u32[]{:S(2)}) collective-permute-start(bf16[192,512]{1,0:T(8,128)(2,1)S(1)} %get-tuple-element.34.own.refs_2_), channel_id=1, source_target_pairs={{0,8},{12,4},{1,9},{13,5},{2,10},{14,6},{3,11},{15,7},{16,24},{28,... | collective-permute-start | bytes 589832 | tf_op jit(solution)/shard_map/ppermute | solution.py:275
  99.5 1.3 collective-permute-start.10
  102.7 5.3 %collective-permute-start.34 = (bf16[192,512]{1,0:T(8,128)(2,1)S(1)}, bf16[192,512]{1,0:T(8,128)(2,1)S(1)}, u32[]{:S(2)}, u32[]{:S(2)}) collective-permute-start(bf16[192,512]{1,0:T(8,128)(2,1)S(1)} %get-tuple-element.38.own.refs_3_), channel_id=1, source_target_pairs={{0,8},{12,4},{1,9},{13,5},{2,10},{14,6},{3,11},{15,7},{16,24},{28,... | collective-permute-start | bytes 589832 | tf_op jit(solution)/shard_map/ppermute | solution.py:275
  108.7 2.3 %collective-permute-start.32 = (bf16[192,512]{1,0:T(8,128)(2,1)S(1)}, bf16[192,512]{1,0:T(8,128)(2,1)S(1)}, u32[]{:S(2)}, u32[]{:S(2)}) collective-permute-start(bf16[192,512]{1,0:T(8,128)(2,1)S(1)} %get-tuple-element.38.own.refs_3_), channel_id=1, source_target_pairs={{0,4},{4,8},{1,5},{5,9},{2,6},{6,10},{3,7},{7,11},{16,20},{20,24},... | collective-permute-start | bytes 589832 | tf_op jit(solution)/shard_map/ppermute | solution.py:275
  111.7 3.4 %shard_map.178.mine = bf16[192,1024]{1,0:T(8,128)(2,1)S(1)} custom-call(s32[2]{0:T(128)S(1)} %pad_add_fusion.place, bf16[192,512]{1,0:T(8,128)(2,1)S(1)} %get-tuple-element.34.own.refs_2_, bf16[192,512]{1,0:T(8,128)(2,1)S(1)} %collective-permute-done.10.low, bf16[192,512]{1,0:T(8,128)(2,1)S(1)} %collective-permute-done.11.high, ...), custom_call_target="tpu_custom_call" | custom-call | flops 805306368 | bytes 6160384 | tf_op jit(solution)/shard_map/pallas_call | solution.py:116
  115.8 3.4 %shard_map.181.mine = bf16[192,1024]{1,0:T(8,128)(2,1)S(1)} custom-call(s32[2]{0:T(128)S(1)} %pad_add_fusion.place, bf16[192,512]{1,0:T(8,128)(2,1)S(1)} %get-tuple-element.38.own.refs_3_, bf16[192,512]{1,0:T(8,128)(2,1)S(1)} %collective-permute-done.32.low, bf16[192,512]{1,0:T(8,128)(2,1)S(1)} %collective-permute-done.33.high, ...), custom_call_target="tpu_custom_call" | custom-call | flops 805306368 | bytes 6160384 | tf_op jit(solution)/shard_map/pallas_call | solution.py:116
  120.2 2.8 %collective-permute-done.27 = f32[1,512]{1,0:T(1,128)S(1)} collective-permute-done((f32[1,512]{1,0:T(1,128)S(1)}, f32[1,512]{1,0:T(1,128)S(1)}, u32[]{:S(2)}, u32[]{:S(2)}) %collective-permute-start.27) | collective-permute-done | bytes 2080 | tf_op jit(solution)/shard_map/ppermute | solution.py:278
  123.5 3.1 %collective-permute-done.26 = f32[1,512]{1,0:T(1,128)S(1)} collective-permute-done((f32[1,512]{1,0:T(1,128)S(1)}, f32[1,512]{1,0:T(1,128)S(1)}, u32[]{:S(2)}, u32[]{:S(2)}) %collective-permute-start.26) | collective-permute-done | bytes 2080 | tf_op jit(solution)/shard_map/ppermute | solution.py:278
  128.0 1.5 collective-permute-start.50
  132.0 1.3 collective-permute-start.36
  133.3 1.3 collective-permute-start.21
  134.6 1.3 collective-permute-start.37
  137.1 11.7 %collective-permute-done.20.passed = bf16[192,1024]{1,0:T(8,128)(2,1)S(1)} collective-permute-done((bf16[192,1024]{1,0:T(8,128)(2,1)S(1)}, bf16[192,1024]{1,0:T(8,128)(2,1)S(1)}, u32[]{:S(2)}, u32[]{:S(2)}) %collective-permute-start.20) | collective-permute-done | bytes 393248 | tf_op jit(solution)/shard_map/ppermute | solution.py:275
  148.9 16.9 %collective-permute-done.21.relayed = bf16[192,1024]{1,0:T(8,128)(2,1)S(1)} collective-permute-done((bf16[192,1024]{1,0:T(8,128)(2,1)S(1)}, bf16[192,1024]{1,0:T(8,128)(2,1)S(1)}, u32[]{:S(2)}, u32[]{:S(2)}) %collective-permute-start.21) | collective-permute-done | bytes 393248 | tf_op jit(solution)/shard_map/ppermute | solution.py:275
  165.7 1.3 shard_map.179
  167.1 6.9 %collective-permute-done.37.relayed = bf16[192,1024]{1,0:T(8,128)(2,1)S(1)} collective-permute-done((bf16[192,1024]{1,0:T(8,128)(2,1)S(1)}, bf16[192,1024]{1,0:T(8,128)(2,1)S(1)}, u32[]{:S(2)}, u32[]{:S(2)}) %collective-permute-start.37) | collective-permute-done | bytes 393248 | tf_op jit(solution)/shard_map/ppermute | solution.py:275
  173.9 1.5 shard_map.182
  176.1 2.0 shard_map.184
  179.8 1.5 collective-permute-start.43
  182.2 1.3 shard_map.186
  184.1 1.3 shard_map.183
  186.2 1.3 shard_map.185
  188.7 1.3 abs_reduce_fusion.1
  190.8 1.5 collective-permute-start.40
  194.8 10.9 %collective-permute-done.48 = f32[1,512]{1,0:T(1,128)S(1)} collective-permute-done((f32[1,512]{1,0:T(1,128)S(1)}, f32[1,512]{1,0:T(1,128)S(1)}, u32[]{:S(2)}, u32[]{:S(2)}) %collective-permute-start.48) | collective-permute-done | bytes 2080 | tf_op jit(solution)/shard_map/ppermute | solution.py:278
  205.8 2.3 %divide_subtract_fusion.1 = (f32[512,512]{1,0:T(8,128)}, f32[512,512]{1,0:T(8,128)}, f32[512,512]{1,0:T(8,128)}) fusion(f32[512,512]{1,0:T(8,128)S(1)} %copy-done.13, f32[512]{0:T(512)S(1)} %bitcast.23, f16[512,512]{1,0:T(8,128)(2,1)S(1)} %collective-permute-done.40, f32[512,512]{1,0:T(8,128)S(1)} %get-tuple-element.44, ...), kind=kLoop, calls=%fused_computation.12 | loop fusion | flops 4194304 | bytes 8914944 | tf_op jit(solution)/shard_map/sub | solution.py:28
  208.1 7.7 %collective-permute-done.47 = f16[512,512]{1,0:T(8,128)(2,1)S(1)} collective-permute-done((f16[512,512]{1,0:T(8,128)(2,1)S(1)}, f16[512,512]{1,0:T(8,128)(2,1)S(1)}, u32[]{:S(2)}, u32[]{:S(2)}) %collective-permute-start.47) | collective-permute-done | bytes 524320 | tf_op jit(solution)/shard_map/ppermute | solution.py:278
  215.8 2.4 %divide_subtract_fusion = (f32[512,512]{1,0:T(8,128)}, f32[512,512]{1,0:T(8,128)}, f32[512,512]{1,0:T(8,128)}) fusion(f32[512,512]{1,0:T(8,128)S(1)} %copy-done.14, f32[512,512]{1,0:T(8,128)S(1)} %copy-done.17, f32[512,512]{1,0:T(8,128)S(1)} %copy-done.18, f32[512]{0:T(512)S(1)} %bitcast.24, f32[512]{0:T(512)S(1)} %bitcast.25, ...), kind=kLoop, calls=%fused_computation.7 | loop fusion | flops 4980736 | bytes 8916992 | tf_op jit(solution)/shard_map/sub | solution.py:28
  (138 shorter events, 28.9 us)
Async XLA Ops:
  4.3 9.8 %collective-permute-start.14 = (bf16[256,512]{1,0:T(8,128)(2,1)S(1)}, bf16[256,512]{1,0:T(8,128)(2,1)S(1)}, u32[]{:S(2)}, u32[]{:S(2)}) collective-permute-start(bf16[256,512]{1,0:T(8,128)(2,1)S(1)} %get-tuple-element.76), channel_id=1, source_target_pairs={{8,4},{12,8},{9,5},{13,9},{10,6},{14,10},{11,7},{15,11},{24,20},{2... | collective-permute-start | bytes 786440 | tf_op jit(solution)/shard_map/ppermute | solution.py:275
  5.1 12.2 %collective-permute-start.13 = (bf16[256,512]{1,0:T(8,128)(2,1)S(1)}, bf16[256,512]{1,0:T(8,128)(2,1)S(1)}, u32[]{:S(2)}, u32[]{:S(2)}) collective-permute-start(bf16[256,512]{1,0:T(8,128)(2,1)S(1)} %get-tuple-element.77), channel_id=1, source_target_pairs={{0,4},{4,8},{1,5},{5,9},{2,6},{6,10},{3,7},{7,11},{16,20},{20,24},... | collective-permute-start | bytes 786440 | tf_op jit(solution)/shard_map/ppermute | solution.py:275
  10.7 11.2 %collective-permute-start.15 = (bf16[256,512]{1,0:T(8,128)(2,1)S(1)}, bf16[256,512]{1,0:T(8,128)(2,1)S(1)}, u32[]{:S(2)}, u32[]{:S(2)}) collective-permute-start(bf16[256,512]{1,0:T(8,128)(2,1)S(1)} %get-tuple-element.78), channel_id=1, source_target_pairs={{0,8},{12,4},{1,9},{13,5},{2,10},{14,6},{3,11},{15,7},{16,24},{28,... | collective-permute-start | bytes 786440 | tf_op jit(solution)/shard_map/ppermute | solution.py:275
  22.0 54.8 %collective-permute-start.17 = (bf16[1024,512]{1,0:T(8,128)(2,1)S(1)}, bf16[1024,512]{1,0:T(8,128)(2,1)}, u32[]{:S(2)}, u32[]{:S(2)}) collective-permute-start(bf16[1024,512]{1,0:T(8,128)(2,1)S(1)} %pad_maximum_fusion.2.dec0), channel_id=1, source_target_pairs={{0,2},{1,3},{2,0},{3,1},{4,6},{5,7},{6,4},{7,5},{8,10},{9,11},{10,... | collective-permute-start | bytes 3145736 | tf_op jit(solution)/shard_map/ppermute | solution.py:278
  23.6 44.0 %collective-permute-start.5 = (bf16[512,512]{1,0:T(8,128)(2,1)S(1)}, bf16[512,512]{1,0:T(8,128)(2,1)}, u32[]{:S(2)}, u32[]{:S(2)}) collective-permute-start(bf16[512,512]{1,0:T(8,128)(2,1)S(1)} %convert_element_type.18), channel_id=1, source_target_pairs={{0,2},{1,3},{2,0},{3,1},{4,6},{5,7},{6,4},{7,5},{8,10},{9,11},{10,... | collective-permute-start | bytes 1572872 | tf_op jit(solution)/shard_map/ppermute | solution.py:278
  24.2 38.2 %collective-permute-start.2 = (bf16[192,512]{1,0:T(8,128)(2,1)S(1)}, bf16[192,512]{1,0:T(8,128)(2,1)S(1)}, u32[]{:S(2)}, u32[]{:S(2)}) collective-permute-start(bf16[192,512]{1,0:T(8,128)(2,1)S(1)} %get-tuple-element.79.own), channel_id=1, source_target_pairs={{0,8},{4,12},{8,0},{12,4},{1,9},{5,13},{9,1},{13,5},{2,10},{6,14},... | collective-permute-start | bytes 589832 | tf_op jit(solution)/shard_map/ppermute | solution.py:275
  28.5 35.4 %collective-permute-start.1 = (bf16[192,512]{1,0:T(8,128)(2,1)S(1)}, bf16[192,512]{1,0:T(8,128)(2,1)S(1)}, u32[]{:S(2)}, u32[]{:S(2)}) collective-permute-start(bf16[192,512]{1,0:T(8,128)(2,1)S(1)} %get-tuple-element.79.own), channel_id=1, source_target_pairs={{4,0},{8,4},{12,8},{5,1},{9,5},{13,9},{6,2},{10,6},{14,10},{7,3},{... | collective-permute-start | bytes 589832 | tf_op jit(solution)/shard_map/ppermute | solution.py:275
  31.0 26.4 %collective-permute-start.8 = (f32[128]{0:T(128)S(1)}, f32[128]{0:T(128)S(1)}, u32[]{:S(2)}, u32[]{:S(2)}) collective-permute-start(f32[128]{0:T(128)S(1)} %copy-done.20), channel_id=1, source_target_pairs={{0,2},{1,3},{2,0},{3,1},{4,6},{5,7},{6,4},{7,5},{8,10},{9,11},{10,... | collective-permute-start | bytes 1544 | tf_op jit(solution)/shard_map/ppermute | solution.py:278
  58.5 9.1 %collective-permute-start = (bf16[192,512]{1,0:T(8,128)(2,1)S(1)}, bf16[192,512]{1,0:T(8,128)(2,1)S(1)}, u32[]{:S(2)}, u32[]{:S(2)}) collective-permute-start(bf16[192,512]{1,0:T(8,128)(2,1)S(1)} %get-tuple-element.79.own), channel_id=1, source_target_pairs={{0,4},{4,8},{8,12},{1,5},{5,9},{9,13},{2,6},{6,10},{10,14},{3,7},{... | collective-permute-start | bytes 589832 | tf_op jit(solution)/shard_map/ppermute | solution.py:275
  62.4 13.0 %collective-permute-start.30 = (bf16[192,512]{1,0:T(8,128)(2,1)S(1)}, bf16[192,512]{1,0:T(8,128)(2,1)S(1)}, u32[]{:S(2)}, u32[]{:S(2)}) collective-permute-start(bf16[192,512]{1,0:T(8,128)(2,1)S(1)} %get-tuple-element.80.own), channel_id=1, source_target_pairs={{0,8},{4,12},{8,0},{12,4},{1,9},{5,13},{9,1},{13,5},{2,10},{6,14},... | collective-permute-start | bytes 589832 | tf_op jit(solution)/shard_map/ppermute | solution.py:275
  63.9 12.8 %collective-permute-start.29 = (bf16[192,512]{1,0:T(8,128)(2,1)S(1)}, bf16[192,512]{1,0:T(8,128)(2,1)S(1)}, u32[]{:S(2)}, u32[]{:S(2)}) collective-permute-start(bf16[192,512]{1,0:T(8,128)(2,1)S(1)} %get-tuple-element.80.own), channel_id=1, source_target_pairs={{4,0},{8,4},{12,8},{5,1},{9,5},{13,9},{6,2},{10,6},{14,10},{7,3},{... | collective-permute-start | bytes 589832 | tf_op jit(solution)/shard_map/ppermute | solution.py:275
  67.6 17.0 %collective-permute-start.4 = (bf16[512,512]{1,0:T(8,128)(2,1)S(1)}, bf16[512,512]{1,0:T(8,128)(2,1)}, u32[]{:S(2)}, u32[]{:S(2)}) collective-permute-start(bf16[512,512]{1,0:T(8,128)(2,1)S(1)} %convert_element_type.18), channel_id=1, source_target_pairs={{0,1},{1,0},{2,3},{3,2},{4,5},{5,4},{6,7},{7,6},{8,9},{9,8},{10,11... | collective-permute-start | bytes 1572872 | tf_op jit(solution)/shard_map/ppermute | solution.py:278
  67.7 18.4 %collective-permute-start.6 = (bf16[512,512]{1,0:T(8,128)(2,1)}, bf16[512,512]{1,0:T(8,128)(2,1)}, u32[]{:S(2)}, u32[]{:S(2)}) collective-permute-start(bf16[512,512]{1,0:T(8,128)(2,1)} %collective-permute-done.5), channel_id=1, source_target_pairs={{0,1},{1,0},{2,3},{3,2},{4,5},{5,4},{6,7},{7,6},{8,9},{9,8},{10,11... | collective-permute-start | bytes 1572872 | tf_op jit(solution)/shard_map/ppermute | solution.py:278
  75.4 7.6 %collective-permute-start.3 = (bf16[192,512]{1,0:T(8,128)(2,1)S(1)}, bf16[192,512]{1,0:T(8,128)(2,1)S(1)}, u32[]{:S(2)}, u32[]{:S(2)}) collective-permute-start(bf16[192,512]{1,0:T(8,128)(2,1)S(1)} %collective-permute-done.2.across), channel_id=1, source_target_pairs={{8,12},{4,0},{9,13},{5,1},{10,14},{6,2},{11,15},{7,3},{24,28},{20,... | collective-permute-start | bytes 589832 | tf_op jit(solution)/shard_map/ppermute | solution.py:275
  76.7 34.4 %collective-permute-start.16 = (bf16[1024,512]{1,0:T(8,128)(2,1)S(1)}, bf16[1024,512]{1,0:T(8,128)(2,1)}, u32[]{:S(2)}, u32[]{:S(2)}) collective-permute-start(bf16[1024,512]{1,0:T(8,128)(2,1)S(1)} %pad_maximum_fusion.2.dec0), channel_id=1, source_target_pairs={{0,1},{1,0},{2,3},{3,2},{4,5},{5,4},{6,7},{7,6},{8,9},{9,8},{10,11... | collective-permute-start | bytes 3145736 | tf_op jit(solution)/shard_map/ppermute | solution.py:278
  76.8 34.4 %collective-permute-start.18 = (bf16[1024,512]{1,0:T(8,128)(2,1)}, bf16[1024,512]{1,0:T(8,128)(2,1)}, u32[]{:S(2)}, u32[]{:S(2)}) collective-permute-start(bf16[1024,512]{1,0:T(8,128)(2,1)} %collective-permute-done.17.dec2), channel_id=1, source_target_pairs={{0,1},{1,0},{2,3},{3,2},{4,5},{5,4},{6,7},{7,6},{8,9},{9,8},{10,11... | collective-permute-start | bytes 3145736 | tf_op jit(solution)/shard_map/ppermute | solution.py:278
  83.0 16.4 %collective-permute-start.23 = (bf16[512,512]{1,0:T(8,128)(2,1)}, bf16[512,512]{1,0:T(8,128)(2,1)S(1)}, u32[]{:S(2)}, u32[]{:S(2)}) collective-permute-start(bf16[512,512]{1,0:T(8,128)(2,1)} %get-tuple-element.74), channel_id=1, source_target_pairs={{0,2},{1,3},{2,0},{3,1},{4,6},{5,7},{6,4},{7,5},{8,10},{9,11},{10,... | collective-permute-start | bytes 1572872 | tf_op jit(solution)/shard_map/ppermute | solution.py:278
  84.6 5.6 %collective-permute-start.28 = (bf16[192,512]{1,0:T(8,128)(2,1)S(1)}, bf16[192,512]{1,0:T(8,128)(2,1)S(1)}, u32[]{:S(2)}, u32[]{:S(2)}) collective-permute-start(bf16[192,512]{1,0:T(8,128)(2,1)S(1)} %get-tuple-element.80.own), channel_id=1, source_target_pairs={{0,4},{4,8},{8,12},{1,5},{5,9},{9,13},{2,6},{6,10},{10,14},{3,7},{... | collective-permute-start | bytes 589832 | tf_op jit(solution)/shard_map/ppermute | solution.py:275
  86.1 12.7 %collective-permute-start.31 = (bf16[192,512]{1,0:T(8,128)(2,1)S(1)}, bf16[192,512]{1,0:T(8,128)(2,1)S(1)}, u32[]{:S(2)}, u32[]{:S(2)}) collective-permute-start(bf16[192,512]{1,0:T(8,128)(2,1)S(1)} %collective-permute-done.30.across), channel_id=1, source_target_pairs={{8,12},{4,0},{9,13},{5,1},{10,14},{6,2},{11,15},{7,3},{24,28},{20,... | collective-permute-start | bytes 589832 | tf_op jit(solution)/shard_map/ppermute | solution.py:275
  90.2 12.5 %collective-permute-start.12 = (bf16[192,512]{1,0:T(8,128)(2,1)S(1)}, bf16[192,512]{1,0:T(8,128)(2,1)S(1)}, u32[]{:S(2)}, u32[]{:S(2)}) collective-permute-start(bf16[192,512]{1,0:T(8,128)(2,1)S(1)} %get-tuple-element.34.own.refs_2_), channel_id=1, source_target_pairs={{0,8},{12,4},{1,9},{13,5},{2,10},{14,6},{3,11},{15,7},{16,24},{28,... | collective-permute-start | bytes 589832 | tf_op jit(solution)/shard_map/ppermute | solution.py:275
  98.8 9.2 %collective-permute-start.11 = (bf16[192,512]{1,0:T(8,128)(2,1)S(1)}, bf16[192,512]{1,0:T(8,128)(2,1)S(1)}, u32[]{:S(2)}, u32[]{:S(2)}) collective-permute-start(bf16[192,512]{1,0:T(8,128)(2,1)S(1)} %get-tuple-element.34.own.refs_2_), channel_id=1, source_target_pairs={{8,4},{12,8},{9,5},{13,9},{10,6},{14,10},{11,7},{15,11},{24,20},{2... | collective-permute-start | bytes 589832 | tf_op jit(solution)/shard_map/ppermute | solution.py:275
  99.5 9.2 %collective-permute-start.10 = (bf16[192,512]{1,0:T(8,128)(2,1)S(1)}, bf16[192,512]{1,0:T(8,128)(2,1)S(1)}, u32[]{:S(2)}, u32[]{:S(2)}) collective-permute-start(bf16[192,512]{1,0:T(8,128)(2,1)S(1)} %get-tuple-element.34.own.refs_2_), channel_id=1, source_target_pairs={{0,4},{4,8},{1,5},{5,9},{2,6},{6,10},{3,7},{7,11},{16,20},{20,24},... | collective-permute-start | bytes 589832 | tf_op jit(solution)/shard_map/ppermute | solution.py:275
  102.7 12.4 %collective-permute-start.34 = (bf16[192,512]{1,0:T(8,128)(2,1)S(1)}, bf16[192,512]{1,0:T(8,128)(2,1)S(1)}, u32[]{:S(2)}, u32[]{:S(2)}) collective-permute-start(bf16[192,512]{1,0:T(8,128)(2,1)S(1)} %get-tuple-element.38.own.refs_3_), channel_id=1, source_target_pairs={{0,8},{12,4},{1,9},{13,5},{2,10},{14,6},{3,11},{15,7},{16,24},{28,... | collective-permute-start | bytes 589832 | tf_op jit(solution)/shard_map/ppermute | solution.py:275
  108.0 7.7 %collective-permute-start.33 = (bf16[192,512]{1,0:T(8,128)(2,1)S(1)}, bf16[192,512]{1,0:T(8,128)(2,1)S(1)}, u32[]{:S(2)}, u32[]{:S(2)}) collective-permute-start(bf16[192,512]{1,0:T(8,128)(2,1)S(1)} %get-tuple-element.38.own.refs_3_), channel_id=1, source_target_pairs={{8,4},{12,8},{9,5},{13,9},{10,6},{14,10},{11,7},{15,11},{24,20},{2... | collective-permute-start | bytes 589832 | tf_op jit(solution)/shard_map/ppermute | solution.py:275
  108.7 7.1 %collective-permute-start.32 = (bf16[192,512]{1,0:T(8,128)(2,1)S(1)}, bf16[192,512]{1,0:T(8,128)(2,1)S(1)}, u32[]{:S(2)}, u32[]{:S(2)}) collective-permute-start(bf16[192,512]{1,0:T(8,128)(2,1)S(1)} %get-tuple-element.38.own.refs_3_), channel_id=1, source_target_pairs={{0,4},{4,8},{1,5},{5,9},{2,6},{6,10},{3,7},{7,11},{16,20},{20,24},... | collective-permute-start | bytes 589832 | tf_op jit(solution)/shard_map/ppermute | solution.py:275
  111.1 16.9 %collective-permute-start.22 = (bf16[512,512]{1,0:T(8,128)(2,1)}, bf16[512,512]{1,0:T(8,128)(2,1)S(1)}, u32[]{:S(2)}, u32[]{:S(2)}) collective-permute-start(bf16[512,512]{1,0:T(8,128)(2,1)} %get-tuple-element.74), channel_id=1, source_target_pairs={{0,1},{1,0},{2,3},{3,2},{4,5},{5,4},{6,7},{7,6},{8,9},{9,8},{10,11... | collective-permute-start | bytes 1572872 | tf_op jit(solution)/shard_map/ppermute | solution.py:278
  111.2 18.3 %collective-permute-start.24 = (bf16[512,512]{1,0:T(8,128)(2,1)S(1)}, bf16[512,512]{1,0:T(8,128)(2,1)S(1)}, u32[]{:S(2)}, u32[]{:S(2)}) collective-permute-start(bf16[512,512]{1,0:T(8,128)(2,1)S(1)} %collective-permute-done.23), channel_id=1, source_target_pairs={{0,1},{1,0},{2,3},{3,2},{4,5},{5,4},{6,7},{7,6},{8,9},{9,8},{10,11... | collective-permute-start | bytes 1572872 | tf_op jit(solution)/shard_map/ppermute | solution.py:278
  115.1 18.2 %collective-permute-start.19 = (bf16[192,1024]{1,0:T(8,128)(2,1)S(1)}, bf16[192,1024]{1,0:T(8,128)(2,1)S(1)}, u32[]{:S(2)}, u32[]{:S(2)}) collective-permute-start(bf16[192,1024]{1,0:T(8,128)(2,1)S(1)} %shard_map.178.mine), channel_id=1, source_target_pairs={{4,8},{8,4},{5,9},{9,5},{6,10},{10,6},{7,11},{11,7},{20,24},{24,20... | collective-permute-start | bytes 1179656 | tf_op jit(solution)/shard_map/ppermute | solution.py:275
  119.2 15.4 %collective-permute-start.35 = (bf16[192,1024]{1,0:T(8,128)(2,1)S(1)}, bf16[192,1024]{1,0:T(8,128)(2,1)S(1)}, u32[]{:S(2)}, u32[]{:S(2)}) collective-permute-start(bf16[192,1024]{1,0:T(8,128)(2,1)S(1)} %shard_map.181.mine), channel_id=1, source_target_pairs={{4,8},{8,4},{5,9},{9,5},{6,10},{10,6},{7,11},{11,7},{20,24},{24,20... | collective-permute-start | bytes 1179656 | tf_op jit(solution)/shard_map/ppermute | solution.py:275
  119.9 3.1 %collective-permute-start.27 = (f32[1,512]{1,0:T(1,128)S(1)}, f32[1,512]{1,0:T(1,128)S(1)}, u32[]{:S(2)}, u32[]{:S(2)}) collective-permute-start(f32[1,512]{1,0:T(1,128)S(1)} %bitcast.19), channel_id=1, source_target_pairs={{0,3},{1,2},{2,1},{3,0},{4,7},{5,6},{6,5},{7,4},{8,11},{9,10},{10,... | collective-permute-start | bytes 6152 | tf_op jit(solution)/shard_map/ppermute | solution.py:278
  122.9 3.6 %collective-permute-start.26 = (f32[1,512]{1,0:T(1,128)S(1)}, f32[1,512]{1,0:T(1,128)S(1)}, u32[]{:S(2)}, u32[]{:S(2)}) collective-permute-start(f32[1,512]{1,0:T(1,128)S(1)} %bitcast.20), channel_id=1, source_target_pairs={{0,2},{1,3},{2,0},{3,1},{4,6},{5,7},{6,4},{7,5},{8,10},{9,11},{10,... | collective-permute-start | bytes 6152 | tf_op jit(solution)/shard_map/ppermute | solution.py:278
  128.0 4.0 %collective-permute-start.50 = (f32[1,512]{1,0:T(1,128)S(1)}, f32[1,512]{1,0:T(1,128)S(1)}, u32[]{:S(2)}, u32[]{:S(2)}) collective-permute-start(f32[1,512]{1,0:T(1,128)S(1)} %add.116), channel_id=1, source_target_pairs={{0,2},{1,3},{2,0},{3,1},{4,6},{5,7},{6,4},{7,5},{8,10},{9,11},{10,... | collective-permute-start | bytes 6152 | tf_op jit(solution)/shard_map/ppermute | solution.py:278
  129.5 7.6 %collective-permute-start.49 = (f32[1,512]{1,0:T(1,128)S(1)}, f32[1,512]{1,0:T(1,128)S(1)}, u32[]{:S(2)}, u32[]{:S(2)}) collective-permute-start(f32[1,512]{1,0:T(1,128)S(1)} %add.116), channel_id=1, source_target_pairs={{0,1},{1,0},{2,3},{3,2},{4,5},{5,4},{6,7},{7,6},{8,9},{9,8},{10,11... | collective-permute-start | bytes 6152 | tf_op jit(solution)/shard_map/ppermute | solution.py:278
  130.7 18.2 %collective-permute-start.20 = (bf16[192,1024]{1,0:T(8,128)(2,1)S(1)}, bf16[192,1024]{1,0:T(8,128)(2,1)S(1)}, u32[]{:S(2)}, u32[]{:S(2)}) collective-permute-start(bf16[192,1024]{1,0:T(8,128)(2,1)S(1)} %shard_map.178.mine), channel_id=1, source_target_pairs={{4,0},{8,12},{5,1},{9,13},{6,2},{10,14},{7,3},{11,15},{20,16},{24,... | collective-permute-start | bytes 1179656 | tf_op jit(solution)/shard_map/ppermute | solution.py:275
  132.0 35.1 %collective-permute-start.36 = (bf16[192,1024]{1,0:T(8,128)(2,1)S(1)}, bf16[192,1024]{1,0:T(8,128)(2,1)S(1)}, u32[]{:S(2)}, u32[]{:S(2)}) collective-permute-start(bf16[192,1024]{1,0:T(8,128)(2,1)S(1)} %shard_map.181.mine), channel_id=1, source_target_pairs={{4,0},{8,12},{5,1},{9,13},{6,2},{10,14},{7,3},{11,15},{20,16},{24,... | collective-permute-start | bytes 1179656 | tf_op jit(solution)/shard_map/ppermute | solution.py:275
  133.3 32.4 %collective-permute-start.21 = (bf16[192,1024]{1,0:T(8,128)(2,1)S(1)}, bf16[192,1024]{1,0:T(8,128)(2,1)S(1)}, u32[]{:S(2)}, u32[]{:S(2)}) collective-permute-start(bf16[192,1024]{1,0:T(8,128)(2,1)S(1)} %collective-permute-done.19.swapped), channel_id=1, source_target_pairs={{4,0},{8,12},{5,1},{9,13},{6,2},{10,14},{7,3},{11,15},{20,16},{24,... | collective-permute-start | bytes 1179656 | tf_op jit(solution)/shard_map/ppermute | solution.py:275
  134.6 39.3 %collective-permute-start.37 = (bf16[192,1024]{1,0:T(8,128)(2,1)S(1)}, bf16[192,1024]{1,0:T(8,128)(2,1)S(1)}, u32[]{:S(2)}, u32[]{:S(2)}) collective-permute-start(bf16[192,1024]{1,0:T(8,128)(2,1)S(1)} %collective-permute-done.35.swapped), channel_id=1, source_target_pairs={{4,0},{8,12},{5,1},{9,13},{6,2},{10,14},{7,3},{11,15},{20,16},{24,... | collective-permute-start | bytes 1179656 | tf_op jit(solution)/shard_map/ppermute | solution.py:275
  179.1 9.6 %collective-permute-start.39 = (f32[512,512]{1,0:T(8,128)}, f32[512,512]{1,0:T(8,128)}, u32[]{:S(2)}, u32[]{:S(2)}) collective-permute-start(f32[512,512]{1,0:T(8,128)} %get-tuple-element.47), channel_id=1, source_target_pairs={{0,1},{1,0},{2,3},{3,2},{4,5},{5,4},{6,7},{7,6},{8,9},{9,8},{10,11... | collective-permute-start | bytes 3145736 | tf_op jit(solution)/shard_map/ppermute | solution.py:278
  179.1 8.4 %collective-permute-start.44 = (f32[1,512]{1,0:T(1,128)S(1)}, f32[1,512]{1,0:T(1,128)S(1)}, u32[]{:S(2)}, u32[]{:S(2)}) collective-permute-start(f32[1,512]{1,0:T(1,128)S(1)} %add.104), channel_id=1, source_target_pairs={{0,3},{1,2},{2,1},{3,0},{4,7},{5,6},{6,5},{7,4},{8,11},{9,10},{10,... | collective-permute-start | bytes 6152 | tf_op jit(solution)/shard_map/ppermute | solution.py:278
  179.8 7.9 %collective-permute-start.43 = (f32[1,512]{1,0:T(1,128)S(1)}, f32[1,512]{1,0:T(1,128)S(1)}, u32[]{:S(2)}, u32[]{:S(2)}) collective-permute-start(f32[1,512]{1,0:T(1,128)S(1)} %add.104), channel_id=1, source_target_pairs={{0,2},{1,3},{2,0},{3,1},{4,6},{5,7},{6,4},{7,5},{8,10},{9,11},{10,... | collective-permute-start | bytes 6152 | tf_op jit(solution)/shard_map/ppermute | solution.py:278
  181.3 6.9 %collective-permute-start.42 = (f32[1,512]{1,0:T(1,128)S(1)}, f32[1,512]{1,0:T(1,128)S(1)}, u32[]{:S(2)}, u32[]{:S(2)}) collective-permute-start(f32[1,512]{1,0:T(1,128)S(1)} %add.104), channel_id=1, source_target_pairs={{0,1},{1,0},{2,3},{3,2},{4,5},{5,4},{6,7},{7,6},{8,9},{9,8},{10,11... | collective-permute-start | bytes 6152 | tf_op jit(solution)/shard_map/ppermute | solution.py:278
  183.6 8.8 %collective-permute-start.46 = (f32[512,512]{1,0:T(8,128)S(1)}, f32[512,512]{1,0:T(8,128)S(1)}, u32[]{:S(2)}, u32[]{:S(2)}) collective-permute-start(f32[512,512]{1,0:T(8,128)S(1)} %get-tuple-element.55), channel_id=1, source_target_pairs={{0,1},{1,0},{2,3},{3,2},{4,5},{5,4},{6,7},{7,6},{8,9},{9,8},{10,11... | collective-permute-start | bytes 3145736 | tf_op jit(solution)/shard_map/ppermute | solution.py:278
  187.5 18.2 %collective-permute-start.38 = (f32[512,512]{1,0:T(8,128)S(1)}, f32[512,512]{1,0:T(8,128)S(1)}, u32[]{:S(2)}, u32[]{:S(2)}) collective-permute-start(f32[512,512]{1,0:T(8,128)S(1)} %copy-done.11), channel_id=1, source_target_pairs={{0,1},{1,0},{2,3},{3,2},{4,5},{5,4},{6,7},{7,6},{8,9},{9,8},{10,11... | collective-permute-start | bytes 3145736 | tf_op jit(solution)/shard_map/ppermute | solution.py:278
  187.6 20.5 %collective-permute-start.45 = (f32[512,512]{1,0:T(8,128)S(1)}, f32[512,512]{1,0:T(8,128)S(1)}, u32[]{:S(2)}, u32[]{:S(2)}) collective-permute-start(f32[512,512]{1,0:T(8,128)S(1)} %get-tuple-element.53), channel_id=1, source_target_pairs={{0,1},{1,0},{2,3},{3,2},{4,5},{5,4},{6,7},{7,6},{8,9},{9,8},{10,11... | collective-permute-start | bytes 3145736 | tf_op jit(solution)/shard_map/ppermute | solution.py:278
  190.0 3.7 %collective-permute-start.41 = (f32[1,512]{1,0:T(1,128)S(1)}, f32[1,512]{1,0:T(1,128)S(1)}, u32[]{:S(2)}, u32[]{:S(2)}) collective-permute-start(f32[1,512]{1,0:T(1,128)S(1)} %bitcast.26), channel_id=1, source_target_pairs={{0,2},{1,3},{2,0},{3,1},{4,6},{5,7},{6,4},{7,5},{8,10},{9,11},{10,... | collective-permute-start | bytes 6152 | tf_op jit(solution)/shard_map/ppermute | solution.py:278
  190.8 14.9 %collective-permute-start.40 = (f16[512,512]{1,0:T(8,128)(2,1)S(1)}, f16[512,512]{1,0:T(8,128)(2,1)S(1)}, u32[]{:S(2)}, u32[]{:S(2)}) collective-permute-start(f16[512,512]{1,0:T(8,128)(2,1)S(1)} %multiply_convert_fusion.1), channel_id=1, source_target_pairs={{0,2},{1,3},{2,0},{3,1},{4,6},{5,7},{6,4},{7,5},{8,10},{9,11},{10,... | collective-permute-start | bytes 1572872 | tf_op jit(solution)/shard_map/ppermute | solution.py:278
  192.5 13.2 %collective-permute-start.48 = (f32[1,512]{1,0:T(1,128)S(1)}, f32[1,512]{1,0:T(1,128)S(1)}, u32[]{:S(2)}, u32[]{:S(2)}) collective-permute-start(f32[1,512]{1,0:T(1,128)S(1)} %bitcast.27), channel_id=1, source_target_pairs={{0,2},{1,3},{2,0},{3,1},{4,6},{5,7},{6,4},{7,5},{8,10},{9,11},{10,... | collective-permute-start | bytes 6152 | tf_op jit(solution)/shard_map/ppermute | solution.py:278
  193.7 22.1 %collective-permute-start.47 = (f16[512,512]{1,0:T(8,128)(2,1)S(1)}, f16[512,512]{1,0:T(8,128)(2,1)S(1)}, u32[]{:S(2)}, u32[]{:S(2)}) collective-permute-start(f16[512,512]{1,0:T(8,128)(2,1)S(1)} %multiply_convert_fusion), channel_id=1, source_target_pairs={{0,2},{1,3},{2,0},{3,1},{4,6},{5,7},{6,4},{7,5},{8,10},{9,11},{10,... | collective-permute-start | bytes 1572872 | tf_op jit(solution)/shard_map/ppermute | solution.py:278
  (28 other events, 212.5 us)

commit v2 on v1

--- a/solution.py
+++ b/solution.py
@@ -108,19 +108,26 @@
 
 VMEM = pl.BlockSpec(memory_space=pltpu.VMEM)
 SMEM = pl.BlockSpec(memory_space=pltpu.SMEM)
-
-
-def local_kernel(body, outs, place, *args, flops):
+ANY = pl.BlockSpec(memory_space=pl.ANY)
+EXTRA = 16
+
+
+def local_kernel(body, outs, place, *args, flops=0, after=(), scratch=()):
     moved = sum(a.size * a.dtype.itemsize for a in args)
     moved += sum(o.size * jnp.dtype(o.dtype).itemsize for o in outs)
+
+    def run(place, *refs):
+        body(place, *refs[: len(args)], *refs[len(args) + len(after) :])
+
     return pl.pallas_call(
-        body,
+        run,
         out_shape=outs,
-        in_specs=[SMEM] + [VMEM] * len(args),
+        in_specs=[SMEM] + [VMEM] * len(args) + [ANY] * len(after),
         out_specs=[VMEM] * len(outs),
+        scratch_shapes=scratch,
         compiler_params=pltpu.CompilerParams(vmem_limit_bytes=48 * 1024 * 1024),
         cost_estimate=pl.CostEstimate(flops=flops, bytes_accessed=moved, transcendentals=0),
-    )(place, *args)
+    )(place, *args, *after)
 
 
 def shape(dims, dtype):
@@ -131,7 +138,39 @@
     return pl.ds(pl.multiple_of(start, width), width)
 
 
-def codes_body(place, own, low, high, across, relay, enc, bias, codes, mask, full, active):
+def three_rows(row):
+    high = row.astype(BF16).astype(F32)
+    middle = (row - high).astype(BF16).astype(F32)
+    low = row - high - middle
+    at = lax.broadcasted_iota(jnp.int32, (EXTRA, row.shape[1]), 0)
+    rows = jnp.where(at == 0, high, jnp.where(at == 1, middle, jnp.where(at == 2, low, 0.0)))
+    return rows.astype(BF16)
+
+
+def behind(value, *others):
+    return lax.optimization_barrier((value, *others))[0]
+
+
+def one_row(rows):
+    return jnp.sum(rows.astype(F32), axis=0, keepdims=True)
+
+
+def encoder_body(place, encoder, bias, out):
+    depth = encoder.shape[0]
+    out[:depth] = encoder[...].astype(BF16)
+    out[depth:] = three_rows(jnp.concatenate([bias[...]] * 4, axis=1))
+
+
+def decoder_body(place, decoder, out):
+    depth = decoder.shape[0]
+    value = decoder[...]
+    out[:depth] = value.astype(BF16)
+    out[depth:] = three_rows(jnp.sum(value * value, axis=0, keepdims=True))
+
+
+def codes_body(
+    place, own, low, high, across, relay, enc0, enc1, enc2, enc3, codes, mask, full, active, bias
+):
     z, i = place[0], place[1]
     width = own.shape[1]
     full[:, columns(z * width, width)] = own[...]
@@ -154,34 +193,34 @@
         full[:, 3 * width :] = relay[...]
 
     total = jnp.zeros(codes.shape, F32)
-    pieces = []
-    for b in range(4):
-        slot = b ^ i
+    piece = codes.shape[1] // 4
+    for t, enc in enumerate((enc0, enc1, enc2, enc3)):
+        b = i ^ t
         total += jnp.dot(
-            full[:, b * width : (b + 1) * width],
-            enc[columns(slot * width, width), :],
-            preferred_element_type=F32,
+            full[:, columns(b * width, width)], enc[:width, :], preferred_element_type=F32
         )
-        pieces.append(bias[pl.ds(slot, 1), :])
-    preact = total + jnp.concatenate(pieces, axis=1)
+        bias[:, columns(b * piece, piece)] = one_row(enc[width:, :piece])
+    preact = total + bias[...]
     low_codes = jnp.maximum(preact, 0.0).astype(BF16)
     codes[...] = low_codes
     mask[...] = (preact > 0.0).astype(F32).astype(BF16)
     active[...] = jnp.sum(low_codes.astype(F32), axis=0, keepdims=True)
 
 
-def error_body(place, own, low, high, across, dec0, dec1, dec2, dec3, inputs, error):
+def error_body(
+    place, own, low, high, across, dec0, dec1, dec2, dec3, row0, row1, row2, row3, inputs, error
+):
     z, i = place[0], place[1]
-    half = dec0.shape[0] // 4
-    shift = jnp.where(z >= 2, half, 0)
-    for t, dec in enumerate((dec0, dec1, dec2, dec3)):
+    half = row0.shape[0] // 3
+    shift = pl.multiple_of(jnp.where(z >= 2, half, 0), half)
+    for t in range(4):
+        dec, row = (dec0, dec1, dec2, dec3)[t], (row0, row1, row2, row3)[t]
+        lefts = (own, low, high, across)
+        rights = [dec[pl.ds(shift, half), :]] + [row[m * half : (m + 1) * half, :] for m in range(3)]
         total = jnp.zeros((own.shape[0], half), F32)
-        for m, codes in enumerate((own, low, high, across)):
+        for left, right in zip(lefts, rights):
             total += lax.dot_general(
-                codes[...],
-                dec[m * half : (m + 1) * half, :],
-                (((1,), (1,)), ((), ())),
-                preferred_element_type=F32,
+                left[...], right, (((1,), (1,)), ((), ())), preferred_element_type=F32
             )
         q = i ^ t
         given = inputs[:, columns(q * 2 * half + shift, half)].astype(F32)
@@ -189,44 +228,46 @@
 
 
 def grad_code_body(
-    rows, place, mine, swapped, passed, relayed, mask, dec, norms, grad_low, bias_sum, full, home
+    rows,
+    place,
+    mine,
+    swapped,
+    passed,
+    relayed,
+    mask,
+    dec0,
+    dec1,
+    dec2,
+    dec3,
+    grad_low,
+    bias_sum,
+    norms,
+    full,
+    home,
 ):
     z, i = place[0], place[1]
     half = mine.shape[1] // 4
     width = 2 * half
-    for q in range(4):
-        piece = slice(q * half, (q + 1) * half)
-        first = slice(q * width, q * width + half)
-        second = slice(q * width + half, (q + 1) * width)
-
-        @pl.when(z == 0)
-        def _():
-            full[:, first] = passed[:, piece]
-            full[:, second] = relayed[:, piece]
-
-        @pl.when(z == 1)
-        def _():
-            full[:, first] = mine[:, piece]
-            full[:, second] = swapped[:, piece]
-
-        @pl.when(z == 2)
-        def _():
-            full[:, first] = swapped[:, piece]
-            full[:, second] = mine[:, piece]
-
-        @pl.when(z == 3)
-        def _():
-            full[:, first] = relayed[:, piece]
-            full[:, second] = passed[:, piece]
+    for at, (near, far) in enumerate(
+        ((passed, relayed), (mine, swapped), (swapped, mine), (relayed, passed))
+    ):
+
+        @pl.when(z == at)
+        def _(near=near, far=far):
+            for q in range(4):
+                full[:, q * width : q * width + half] = near[:, q * half : (q + 1) * half]
+                full[:, q * width + half : (q + 1) * width] = far[:, q * half : (q + 1) * half]
 
     total = jnp.zeros(grad_low.shape, F32)
-    for b in range(4):
+    squares = jnp.zeros(bias_sum.shape, F32)
+    for t, dec in enumerate((dec0, dec1, dec2, dec3)):
         total += jnp.dot(
-            full[:, b * width : (b + 1) * width],
-            dec[columns((b ^ i) * width, width), :],
-            preferred_element_type=F32,
+            full[:, columns((i ^ t) * width, width)], dec[:width, :], preferred_element_type=F32
         )
-    code_grad = (-2.0 / rows) * total + norms[...] / rows
+        squares += one_row(dec[width:, :])
+    column_norms = jnp.sqrt(squares + 1e-06)
+    norms[...] = column_norms
+    code_grad = (-2.0 / rows) * total + column_norms / rows
     grad = jnp.where(mask[...] > 0, code_grad, 0.0)
     grad_low[...] = grad.astype(BF16)
     bias_sum[...] = jnp.sum(grad, axis=0, keepdims=True)
@@ -235,11 +276,11 @@
 
 def grad_body(scale, slots, place, *refs):
     i = place[1]
-    lefts, rights = refs[:CHUNKS], refs[CHUNKS : 2 * CHUNKS]
-    outs = refs[2 * CHUNKS :]
-    width = outs[0].shape[0]
+    lefts, rights, sums = refs[:CHUNKS], refs[CHUNKS : 2 * CHUNKS], refs[2 * CHUNKS : 3 * CHUNKS]
+    outs = refs[3 * CHUNKS :]
+    width = lefts[0].shape[1] // 4
     for slot, out in zip(slots, outs):
-        total = jnp.zeros(out.shape, F32)
+        total = jnp.zeros((width, out.shape[1]), F32)
         for left, right in zip(lefts, rights):
             total += lax.dot_general(
                 left[:, columns((i ^ slot) * width, width)],
@@ -247,7 +288,9 @@
                 (((0,), (0,)), ((), ())),
                 preferred_element_type=F32,
             )
-        out[...] = scale * total
+        out[:width] = scale * total
+    row = functools.reduce(jnp.add, [value[...] for value in sums])
+    outs[0][width:] = jnp.broadcast_to(row, (outs[0].shape[0] - width, row.shape[1]))
 
 
 def line_shards(
@@ -274,49 +317,51 @@
     def along(value, pairs):
         return lax.ppermute(value, "latent", pairs)
 
-    def flip(value, bits):
-        return lax.ppermute(value, "dp", [(k, k ^ bits) for k in range(4)])
-
-    def sum_dp(value):
-        return (value + flip(value, 1)) + (flip(value, 2) + flip(value, 3))
-
-    def by_slot(value):
-        core, chip = flip(value, 1), flip(value, 2)
-        return [value, core, chip, flip(chip, 1)]
+    def flip(value, bits, planes=(0, 1, 2, 3)):
+        pairs = [(4 * p + k, 4 * p + (k ^ bits)) for p in planes for k in range(4)]
+        return lax.ppermute(value, ("latent", "dp"), pairs)
 
     up = [(0, 1), (1, 2), (2, 3)]
     down = [(1, 0), (2, 1), (3, 2)]
     two = [(0, 2), (1, 3), (2, 0), (3, 1)]
 
+    (enc_own,) = local_kernel(
+        encoder_body,
+        [shape((width + EXTRA, latents), BF16)],
+        place,
+        encoder,
+        enc_bias.reshape(1, -1),
+    )
+
     parts = [activations[c * chunk : (c + 1) * chunk] for c in range(CHUNKS)]
     gathered = []
     for part in parts:
+        part = behind(part, *(gathered[-1][1:4] if gathered else (enc_own,)))
         low, high, across = along(part, up), along(part, down), along(part, two)
         relay = along(across, [(2, 3), (1, 0)])
         gathered.append((part, low, high, across, relay))
 
-    enc_all = jnp.concatenate(by_slot(encoder.astype(BF16)), axis=0)
-    bias_all = jnp.stack(by_slot(enc_bias), axis=0)
-    dec_low = decoder.astype(BF16)
-    dec_all = jnp.concatenate(by_slot(dec_low), axis=0)
-    norms = jnp.sqrt(sum_dp(jnp.sum(decoder * decoder, axis=0, keepdims=True)) + 1e-06)
-
-    first, second = dec_low[:half], dec_low[half:]
-    mine = jnp.where(z >= 2, second, first)
-    dec_rows = jnp.concatenate(
-        [
-            mine,
-            along(jnp.where(z >= 1, second, first), [(0, 1), (1, 2)]),
-            along(jnp.where(z >= 3, second, first), [(2, 1), (3, 2)]),
-            along(jnp.where(z >= 2, first, second), [(0, 2), (3, 1)]),
-        ],
-        axis=0,
-    )
-    dec_rows = by_slot(dec_rows)
+    enc_chip, enc_core = flip(enc_own, 2), flip(enc_own, 1)
+    enc = [enc_own, enc_core, enc_chip, flip(enc_chip, 1)]
+    (dec_own,) = local_kernel(
+        decoder_body,
+        [shape((width + EXTRA, latents), BF16)],
+        place,
+        decoder,
+        after=(enc_core, enc_chip, *gathered[0][1:4]),
+    )
+    dec_core, dec_chip = flip(dec_own, 1), flip(dec_own, 2)
+
+    first, second = dec_own[:half], dec_own[half:width]
+    dec_pieces = [
+        along(jnp.where(z >= 1, second, first), [(0, 1), (1, 2)]),
+        along(jnp.where(z >= 3, second, first), [(2, 1), (3, 2)]),
+        along(jnp.where(z >= 2, first, second), [(0, 2), (3, 1)]),
+    ]
 
     flops = 2 * chunk * features * latents
-    inputs, codes, masks, actives, errors = [], [], [], [], []
-    for part in gathered:
+    inputs, codes, masks, actives = [], [], [], []
+    for step, part in enumerate(gathered):
         low_codes, mask, full, active = local_kernel(
             codes_body,
             [
@@ -327,42 +372,55 @@
             ],
             place,
             *part,
-            enc_all,
-            bias_all,
+            *enc,
             flops=flops,
+            scratch=[pltpu.VMEM((1, latents), F32)],
         )
+        if step == 0:
+            dec = [dec_own, dec_core, dec_chip, flip(behind(dec_chip, low_codes), 1)]
+            first_codes = low_codes
         inputs.append(full)
         codes.append(low_codes)
         masks.append(mask)
         actives.append(active)
+    nearby = []
+    for low_codes in codes:
         low = along(low_codes, [(0, 1), (1, 2)])
         high = along(low_codes, [(2, 1), (3, 2)])
         across = along(low_codes, [(0, 2), (3, 1)])
+        nearby.append((low_codes, low, high, across))
+    dec_pieces = [
+        behind(piece, dec_chip, first_codes, *gathered[-1][1:3]) for piece in dec_pieces
+    ]
+    rows_own = jnp.concatenate(dec_pieces, axis=0)
+    rows_chip, rows_core = flip(rows_own, 2, (1, 2)), flip(rows_own, 1, (1, 2))
+    rows_both = flip(behind(rows_chip, *gathered[-1][3:], *nearby[0][1:]), 1, (1, 2))
+    dec_rows = [rows_own, rows_core, rows_chip, rows_both]
+    errors = []
+    for step in range(CHUNKS):
         (own_error,) = local_kernel(
             error_body,
             [shape((chunk, features // 2), BF16)],
             place,
-            low_codes,
-            low,
-            high,
-            across,
+            *nearby[step],
+            *dec,
             *dec_rows,
-            full,
+            inputs[step],
             flops=2 * flops,
+            after=errors[-1][1:3] if errors else (),
         )
         passed = along(own_error, [(1, 0), (2, 3)])
         swapped = along(own_error, [(1, 2), (2, 1)])
         relayed = along(swapped, [(1, 0), (2, 3)])
         errors.append((own_error, swapped, passed, relayed))
 
-    active_sum = sum_dp(functools.reduce(jnp.add, actives))
-
     grads, bias_sums, fulls, homes = [], [], [], []
     for error, mask in zip(errors, masks):
-        grad_low, bias_sum, full, home = local_kernel(
+        grad_low, bias_sum, norms, full, home = local_kernel(
             functools.partial(grad_code_body, rows),
             [
                 shape((chunk, latents), BF16),
+                shape((1, latents), F32),
                 shape((1, latents), F32),
                 shape((chunk, features), BF16),
                 shape((chunk, width), BF16),
@@ -370,8 +428,7 @@
             place,
             *error,
             mask,
-            dec_all,
-            norms,
+            *dec,
             flops=flops,
         )
         grads.append(grad_low)
@@ -380,28 +437,32 @@
         homes.append(home)
     error = jnp.concatenate(homes, axis=0)
 
-    def reduced(scale, lefts, rights):
+    def reduced(scale, lefts, rights, sums):
         def slots(*which):
             return local_kernel(
                 functools.partial(grad_body, scale, which),
-                [shape((width, latents), F32)] * 2,
+                [shape((width + 8, latents), F32), shape((width, latents), F32)],
                 place,
                 *lefts,
                 *rights,
+                *sums,
                 flops=CHUNKS * flops // 2,
             )
 
         send_far, send_near = slots(3, 1)
         keep_far, keep_near = slots(2, 0)
         far = keep_far + flip(send_far, 1)
+        row = far[width : width + 1]
+        far = far[:width]
         largest = jnp.maximum(jnp.max(jnp.abs(far), axis=0, keepdims=True), 1e-30)
         sent = (far * (16384.0 / largest)).astype(jnp.float16)
         near = keep_near + flip(send_near, 1)
-        return near + flip(sent, 2).astype(F32) * (flip(largest, 2) / 16384.0)
-
-    grad_dec_rows = reduced(-2.0 / rows, fulls, codes)
-    grad_encoder = reduced(1.0, inputs, grads)
-    grad_bias = sum_dp(functools.reduce(jnp.add, bias_sums))
+        small = flip(jnp.concatenate([largest, row], axis=0), 2)
+        block = near + flip(sent, 2).astype(F32) * (small[:1] / 16384.0)
+        return block, row + small[1:]
+
+    grad_dec_rows, active_sum = reduced(-2.0 / rows, fulls, codes, actives)
+    grad_encoder, grad_bias = reduced(1.0, inputs, grads, bias_sums)
     grad_bias = lax.dynamic_slice(
         grad_bias.reshape(latents), (i * enc_bias.shape[0],), (enc_bias.shape[0],)
     )

time: 219 us -> 194 us (0.89)
  waiting for transfers between devices: 114 us -> 80 us
  local copies, waits for them, and re-layouts: 2.7 us -> 9.67 us
  other arithmetic: 14.4 us -> 9.48 us
  starting transfers between devices: 68.1 us -> 72.4 us
    ppermute x29 -> x17, waiting for transfers between devices: 54.4 us -> 24.8 us  [flip(): return lax.ppermute(value, ('latent', 'dp'), pairs)]
    ppermute x23, starting transfers between devices: 51.4 us -> 62.4 us  [along(): return lax.ppermute(value, 'latent', pairs)]
    unnamed x48 -> x88, local copies, waits for them, and re-layouts: 2.67 us -> 9.61 us
    ppermute x29 -> x17, starting transfers between devices: 16.7 us -> 10 us  [flip(): return lax.ppermute(value, ('latent', 'dp'), pairs)]
    ppermute x23, waiting for transfers between devices: 59.3 us -> 55.2 us  [along(): return lax.ppermute(value, 'latent', pairs)]
    add x2, other arithmetic: 0.01 us -> 2.89 us  [reduced(): far = keep_far + flip(send_far, 1)]
    concatenate x3 -> x2, other arithmetic: 2.74 us -> 0.02 us  [reduced(): small = flip(jnp.concatenate([largest, row], axis=0), 2)]
    reduce_sum x1 -> x0, other arithmetic: 2.46 us -> none  [line_shards(): jnp.sum(decoder * decoder, axis=0, keepdims=True)]
  transfers between devices with their start and end apart: 52 -> 40, of which waited for: 19 -> 18; matrix products, arithmetic and copies ran while one was open for 4% -> 4% of each run, Pallas kernels for 7% -> 5%
where the time goes in v2:
time: 194 us; the launch traced here: 193 us
  waiting for transfers between devices  80 us (41%)
  starting transfers between devices  72.4 us (37%)
  Pallas kernels  19.9 us (10%)
  local copies, waits for them, and re-layouts  9.67 us (5%)
  other arithmetic  9.48 us (5%)
    ppermute x23, starting transfers between devices, along(): return lax.ppermute(value, 'latent', pairs)  62.4 us
    ppermute x23, waiting for transfers between devices, along(): return lax.ppermute(value, 'latent', pairs)  55.2 us
    ppermute x17, waiting for transfers between devices, flip(): return lax.ppermute(value, ('latent', 'dp'), pairs)  24.8 us
    pallas_call x12, Pallas kernels, local_kernel(): pl.pallas_call(run, out_shape=outs, in_specs=[SMEM] + [VMEM] * len(args)...  19.9 us
    ppermute x17, starting transfers between devices, flip(): return lax.ppermute(value, ('latent', 'dp'), pairs)  10 us
    unnamed x88, local copies, waits for them, and re-layouts  9.61 us
    sub x3, other arithmetic, adam_update(): param - learn_rate * (moment_new / first_fix) / (jnp.sqrt(square_new / se...  5.26 us
  transfers between devices with their start and end apart: 40, of which 18 were waited for; matrix products, arithmetic and copies ran while one was open for 4% of the time, Pallas kernels for 5%

profile of v2, /device:TPU:0, one launch (start us, length us, event | category | flops | bytes accessed | tf_op | source)
XLA Modules:
  0.0 192.9 jit_solution(18001214004149067978)
XLA Ops:
  0.7 1.2 copy-done.4
  3.2 3.0 %collective-permute-start.5 = (bf16[528,512]{1,0:T(8,128)(2,1)S(1)}, bf16[528,512]{1,0:T(8,128)(2,1)S(1)}, u32[]{:S(2)}, u32[]{:S(2)}) collective-permute-start(bf16[528,512]{1,0:T(8,128)(2,1)S(1)} %shard_map.177.refs_5_), channel_id=1, source_target_pairs={{0,2},{1,3},{2,0},{3,1},{4,6},{5,7},{6,4},{7,5},{8,10},{9,11},{10,... | collective-permute-start | bytes 1622024 | tf_op jit(solution)/shard_map/ppermute | solution.py:322
  6.3 2.7 %collective-permute-start.2 = (bf16[192,512]{1,0:T(8,128)(2,1)S(1)}, bf16[192,512]{1,0:T(8,128)(2,1)S(1)}, u32[]{:S(2)}, u32[]{:S(2)}) collective-permute-start(bf16[192,512]{1,0:T(8,128)(2,1)S(1)} %get-tuple-element.42.refs_0_), channel_id=1, source_target_pairs={{0,8},{4,12},{8,0},{12,4},{1,9},{5,13},{9,1},{13,5},{2,10},{6,14},... | collective-permute-start | bytes 589832 | tf_op jit(solution)/shard_map/ppermute | solution.py:318
  8.9 1.3 collective-permute-start.1
  10.2 4.6 %collective-permute-start = (bf16[192,512]{1,0:T(8,128)(2,1)S(1)}, bf16[192,512]{1,0:T(8,128)(2,1)S(1)}, u32[]{:S(2)}, u32[]{:S(2)}) collective-permute-start(bf16[192,512]{1,0:T(8,128)(2,1)S(1)} %get-tuple-element.42.refs_0_), channel_id=1, source_target_pairs={{0,4},{4,8},{8,12},{1,5},{5,9},{9,13},{2,6},{6,10},{10,14},{3,7},{... | collective-permute-start | bytes 589832 | tf_op jit(solution)/shard_map/ppermute | solution.py:318
  15.4 3.0 %collective-permute-done.5.refs_7_.refs_2_ = bf16[528,512]{1,0:T(8,128)(2,1)S(1)} collective-permute-done((bf16[528,512]{1,0:T(8,128)(2,1)S(1)}, bf16[528,512]{1,0:T(8,128)(2,1)S(1)}, u32[]{:S(2)}, u32[]{:S(2)}) %collective-permute-start.5) | collective-permute-done | bytes 540704 | tf_op jit(solution)/shard_map/ppermute | solution.py:322
  19.2 1.7 collective-permute-done.1.refs_2_.refs_4_
  22.8 1.4 collective-permute-start.15
  24.2 1.3 collective-permute-start.3
  25.6 9.9 %collective-permute-start.17 = (bf16[256,512]{1,0:T(8,128)(2,1)S(1)}, bf16[256,512]{1,0:T(8,128)(2,1)S(1)}, u32[]{:S(2)}, u32[]{:S(2)}) collective-permute-start(bf16[256,512]{1,0:T(8,128)(2,1)S(1)} %get-tuple-element.83), channel_id=1, source_target_pairs={{0,8},{12,4},{1,9},{13,5},{2,10},{14,6},{3,11},{15,7},{16,24},{28,... | collective-permute-start | bytes 786440 | tf_op jit(solution)/shard_map/ppermute | solution.py:318
  36.7 1.6 collective-permute-start.13
  39.0 4.4 %collective-permute-start.14 = (bf16[192,512]{1,0:T(8,128)(2,1)S(1)}, bf16[192,512]{1,0:T(8,128)(2,1)S(1)}, u32[]{:S(2)}, u32[]{:S(2)}) collective-permute-start(bf16[192,512]{1,0:T(8,128)(2,1)S(1)} %get-tuple-element.45.refs_0_), channel_id=1, source_target_pairs={{0,4},{4,8},{8,12},{1,5},{5,9},{9,13},{2,6},{6,10},{10,14},{3,7},{... | collective-permute-start | bytes 589832 | tf_op jit(solution)/shard_map/ppermute | solution.py:318
  43.4 1.2 shard_map.178
  44.7 5.6 %collective-permute-done.14.refs_1_ = bf16[192,512]{1,0:T(8,128)(2,1)S(1)} collective-permute-done((bf16[192,512]{1,0:T(8,128)(2,1)S(1)}, bf16[192,512]{1,0:T(8,128)(2,1)S(1)}, u32[]{:S(2)}, u32[]{:S(2)}) %collective-permute-start.14) | collective-permute-done | bytes 196640 | tf_op jit(solution)/shard_map/ppermute | solution.py:318
  51.1 6.1 %collective-permute-start.20 = (bf16[192,512]{1,0:T(8,128)(2,1)S(1)}, bf16[192,512]{1,0:T(8,128)(2,1)S(1)}, u32[]{:S(2)}, u32[]{:S(2)}) collective-permute-start(bf16[192,512]{1,0:T(8,128)(2,1)S(1)} %get-tuple-element.45.refs_0_), channel_id=1, source_target_pairs={{0,8},{4,12},{8,0},{12,4},{1,9},{5,13},{9,1},{13,5},{2,10},{6,14},... | collective-permute-start | bytes 589832 | tf_op jit(solution)/shard_map/ppermute | solution.py:318
  57.2 8.5 %collective-permute-done.20.refs_3_ = bf16[192,512]{1,0:T(8,128)(2,1)S(1)} collective-permute-done((bf16[192,512]{1,0:T(8,128)(2,1)S(1)}, bf16[192,512]{1,0:T(8,128)(2,1)S(1)}, u32[]{:S(2)}, u32[]{:S(2)}) %collective-permute-start.20) | collective-permute-done | bytes 196640 | tf_op jit(solution)/shard_map/ppermute | solution.py:318
  65.7 1.3 collective-permute-start.21
  67.0 3.9 %collective-permute-start.9 = (bf16[192,512]{1,0:T(8,128)(2,1)S(1)}, bf16[192,512]{1,0:T(8,128)(2,1)S(1)}, u32[]{:S(2)}, u32[]{:S(2)}) collective-permute-start(bf16[192,512]{1,0:T(8,128)(2,1)S(1)} %get-tuple-element.43.refs_0_.refs_2_), channel_id=1, source_target_pairs={{0,8},{12,4},{1,9},{13,5},{2,10},{14,6},{3,11},{15,7},{16,24},{28,... | collective-permute-start | bytes 589832 | tf_op jit(solution)/shard_map/ppermute | solution.py:318
  71.6 2.6 %collective-permute-start.7 = (bf16[192,512]{1,0:T(8,128)(2,1)S(1)}, bf16[192,512]{1,0:T(8,128)(2,1)S(1)}, u32[]{:S(2)}, u32[]{:S(2)}) collective-permute-start(bf16[192,512]{1,0:T(8,128)(2,1)S(1)} %get-tuple-element.43.refs_0_.refs_2_), channel_id=1, source_target_pairs={{0,4},{4,8},{1,5},{5,9},{2,6},{6,10},{3,7},{7,11},{16,20},{20,24},... | collective-permute-start | bytes 589832 | tf_op jit(solution)/shard_map/ppermute | solution.py:318
  75.0 3.3 %collective-permute-done.7.refs_1_ = bf16[192,512]{1,0:T(8,128)(2,1)S(1)} collective-permute-done((bf16[192,512]{1,0:T(8,128)(2,1)S(1)}, bf16[192,512]{1,0:T(8,128)(2,1)S(1)}, u32[]{:S(2)}, u32[]{:S(2)}) %collective-permute-start.7) | collective-permute-done | bytes 196640 | tf_op jit(solution)/shard_map/ppermute | solution.py:318
  79.6 1.4 collective-permute-done.10.refs_5_.refs_6_
  82.7 2.9 %shard_map.180.refs_0_ = bf16[192,1024]{1,0:T(8,128)(2,1)S(1)} custom-call(s32[2]{0:T(128)S(1)} %pad_add_fusion.place, bf16[192,512]{1,0:T(8,128)(2,1)S(1)} %get-tuple-element.43.refs_0_.refs_2_, bf16[192,512]{1,0:T(8,128)(2,1)S(1)} %collective-permute-done.7.refs_1_, bf16[192,512]{1,0:T(8,128)(2,1)S(1)} %collective-permute-done.8.refs_2_, ...), custom_call_target="tpu_custom_call" | custom-call | flops 805306368 | bytes 7274496 | tf_op jit(solution)/shard_map/pallas_call | solution.py:122
  85.6 1.3 collective-permute-start.24
  87.6 1.2 shard_map.182
  89.7 11.6 %collective-permute-start.28 = (bf16[192,512]{1,0:T(8,128)(2,1)S(1)}, bf16[192,512]{1,0:T(8,128)(2,1)S(1)}, u32[]{:S(2)}, u32[]{:S(2)}) collective-permute-start(bf16[192,512]{1,0:T(8,128)(2,1)S(1)} %get-tuple-element.53.refs_0_.refs_3_), channel_id=1, source_target_pairs={{0,8},{12,4},{1,9},{13,5},{2,10},{14,6},{3,11},{15,7},{16,24},{28,... | collective-permute-start | bytes 589832 | tf_op jit(solution)/shard_map/ppermute | solution.py:318
  102.0 1.3 collective-permute-start.26
  103.3 3.3 %collective-permute-done.28.refs_3_ = bf16[192,512]{1,0:T(8,128)(2,1)S(1)} collective-permute-done((bf16[192,512]{1,0:T(8,128)(2,1)S(1)}, bf16[192,512]{1,0:T(8,128)(2,1)S(1)}, u32[]{:S(2)}, u32[]{:S(2)}) %collective-permute-start.28) | collective-permute-done | bytes 196640 | tf_op jit(solution)/shard_map/ppermute | solution.py:318
  106.6 3.1 %collective-permute-done.26.refs_1_ = bf16[192,512]{1,0:T(8,128)(2,1)S(1)} collective-permute-done((bf16[192,512]{1,0:T(8,128)(2,1)S(1)}, bf16[192,512]{1,0:T(8,128)(2,1)S(1)}, u32[]{:S(2)}, u32[]{:S(2)}) %collective-permute-start.26) | collective-permute-done | bytes 196640 | tf_op jit(solution)/shard_map/ppermute | solution.py:318
  109.8 3.1 %shard_map.183.refs_0_ = bf16[192,1024]{1,0:T(8,128)(2,1)S(1)} custom-call(s32[2]{0:T(128)S(1)} %pad_add_fusion.place, bf16[192,512]{1,0:T(8,128)(2,1)S(1)} %get-tuple-element.53.refs_0_.refs_3_, bf16[192,512]{1,0:T(8,128)(2,1)S(1)} %collective-permute-done.26.refs_1_, bf16[192,512]{1,0:T(8,128)(2,1)S(1)} %collective-permute-done.27.refs_2_, ...), custom_call_target="tpu_custom_call" | custom-call | flops 805306368 | bytes 7274496 | tf_op jit(solution)/shard_map/pallas_call | solution.py:122
  113.6 1.3 collective-permute-start.25
  114.9 1.3 collective-permute-start.30
  116.2 1.3 collective-permute-start.31
  117.5 14.9 %collective-permute-done.25.refs_3_ = bf16[192,1024]{1,0:T(8,128)(2,1)S(1)} collective-permute-done((bf16[192,1024]{1,0:T(8,128)(2,1)S(1)}, bf16[192,1024]{1,0:T(8,128)(2,1)S(1)}, u32[]{:S(2)}, u32[]{:S(2)}) %collective-permute-start.25) | collective-permute-done | bytes 393248 | tf_op jit(solution)/shard_map/ppermute | solution.py:318
  132.4 1.7 shard_map.181
  134.8 6.0 %collective-permute-done.30.refs_2_ = bf16[192,1024]{1,0:T(8,128)(2,1)S(1)} collective-permute-done((bf16[192,1024]{1,0:T(8,128)(2,1)S(1)}, bf16[192,1024]{1,0:T(8,128)(2,1)S(1)}, u32[]{:S(2)}, u32[]{:S(2)}) %collective-permute-start.30) | collective-permute-done | bytes 393248 | tf_op jit(solution)/shard_map/ppermute | solution.py:318
  140.8 6.7 %collective-permute-done.31.refs_3_ = bf16[192,1024]{1,0:T(8,128)(2,1)S(1)} collective-permute-done((bf16[192,1024]{1,0:T(8,128)(2,1)S(1)}, bf16[192,1024]{1,0:T(8,128)(2,1)S(1)}, u32[]{:S(2)}, u32[]{:S(2)}) %collective-permute-start.31) | collective-permute-done | bytes 393248 | tf_op jit(solution)/shard_map/ppermute | solution.py:318
  147.5 1.4 shard_map.184
  149.0 2.2 %shard_map.186 = (f32[520,512]{1,0:T(8,128)}, f32[512,512]{1,0:T(8,128)S(1)}) custom-call(s32[2]{0:T(128)S(1)} %pad_add_fusion.place, bf16[192,2048]{1,0:T(8,128)(2,1)S(1)} %copy-done.1, bf16[192,2048]{1,0:T(8,128)(2,1)S(1)} %copy-done.3, bf16[192,512]{1,0:T(8,128)(2,1)S(1)} %get-tuple-element.57.refs_2_, bf16[192,512]{1,0:T(8,128)(2,1)S(1)} %get-tuple-element.58.refs_3_, ...), custom_call_target="tpu_custom_call" | custom-call | flops 402653184 | bytes 4083712 | tf_op jit(solution)/shard_map/pallas_call | solution.py:122
  152.2 2.2 %shard_map.188 = (f32[520,512]{1,0:T(8,128)}, f32[512,512]{1,0:T(8,128)S(1)}) custom-call(s32[2]{0:T(128)S(1)} %pad_add_fusion.place, bf16[192,2048]{1,0:T(8,128)(2,1)S(1)} %get-tuple-element.65.refs_0_, bf16[192,2048]{1,0:T(8,128)(2,1)S(1)} %get-tuple-element.66.refs_1_, bf16[192,512]{1,0:T(8,128)(2,1)S(1)} %get-tuple-element.43.refs_0_.refs_2_, ...), custom_call_target="tpu_custom_call" | custom-call | flops 402653184 | bytes 4083712 | tf_op jit(solution)/shard_map/pallas_call | solution.py:122
  157.7 1.3 shard_map.185
  159.1 1.3 shard_map.187
  161.2 1.4 add.61
  162.7 1.4 add.73
  165.1 1.5 collective-permute-start.34
  168.9 11.0 %collective-permute-done.39 = f32[2,512]{1,0:T(2,128)S(1)} collective-permute-done((f32[2,512]{1,0:T(2,128)S(1)}, f32[2,512]{1,0:T(2,128)S(1)}, u32[]{:S(2)}, u32[]{:S(2)}) %collective-permute-start.39) | collective-permute-done | bytes 4128 | tf_op jit(solution)/shard_map/ppermute | solution.py:322
  180.6 2.3 %divide_subtract_fusion.1 = (f32[512,512]{1,0:T(8,128)}, f32[512,512]{1,0:T(8,128)}, f32[512,512]{1,0:T(8,128)}) fusion(f32[512,512]{1,0:T(8,128)S(1)} %copy-done.5, f32[512]{0:T(512)S(1)} %bitcast.17, f16[512,512]{1,0:T(8,128)(2,1)S(1)} %collective-permute-done.34, f32[512,512]{1,0:T(8,128)S(1)} %get-tuple-element.61, ...), kind=kLoop, calls=%fused_computation.9 | loop fusion | flops 4194304 | bytes 8914944 | tf_op jit(solution)/shard_map/sub | solution.py:28
  182.9 7.6 %collective-permute-done.38 = f16[512,512]{1,0:T(8,128)(2,1)S(1)} collective-permute-done((f16[512,512]{1,0:T(8,128)(2,1)S(1)}, f16[512,512]{1,0:T(8,128)(2,1)S(1)}, u32[]{:S(2)}, u32[]{:S(2)}) %collective-permute-start.38) | collective-permute-done | bytes 524320 | tf_op jit(solution)/shard_map/ppermute | solution.py:322
  190.5 2.4 %divide_subtract_fusion = (f32[512,512]{1,0:T(8,128)}, f32[512,512]{1,0:T(8,128)}, f32[512,512]{1,0:T(8,128)}) fusion(f32[512,512]{1,0:T(8,128)S(1)} %copy-done.7, f32[512,512]{1,0:T(8,128)S(1)} %copy-done.38, f32[512,512]{1,0:T(8,128)S(1)} %copy-done.39, f32[512]{0:T(512)S(1)} %bitcast.21, f32[512]{0:T(512)S(1)} %bitcast.20, ...), kind=kLoop, calls=%fused_computation.4 | loop fusion | flops 4980736 | bytes 8916992 | tf_op jit(solution)/shard_map/sub | solution.py:28
  (154 shorter events, 24.2 us)
Async XLA Ops:
  2.6 18.3 %copy-start.6 = (f32[512,512]{1,0:T(8,128)S(1)}, f32[512,512]{1,0:T(8,128)}, u32[]{:S(2)}) copy-start(f32[512,512]{1,0:T(8,128)} %refs_0_.3) | copy-start | bytes 3145732
  3.2 15.3 %collective-permute-start.5 = (bf16[528,512]{1,0:T(8,128)(2,1)S(1)}, bf16[528,512]{1,0:T(8,128)(2,1)S(1)}, u32[]{:S(2)}, u32[]{:S(2)}) collective-permute-start(bf16[528,512]{1,0:T(8,128)(2,1)S(1)} %shard_map.177.refs_5_), channel_id=1, source_target_pairs={{0,2},{1,3},{2,0},{3,1},{4,6},{5,7},{6,4},{7,5},{8,10},{9,11},{10,... | collective-permute-start | bytes 1622024 | tf_op jit(solution)/shard_map/ppermute | solution.py:322
  6.2 14.7 %collective-permute-start.4 = (bf16[528,512]{1,0:T(8,128)(2,1)S(1)}, bf16[528,512]{1,0:T(8,128)(2,1)S(1)}, u32[]{:S(2)}, u32[]{:S(2)}) collective-permute-start(bf16[528,512]{1,0:T(8,128)(2,1)S(1)} %shard_map.177.refs_5_), channel_id=1, source_target_pairs={{0,1},{1,0},{2,3},{3,2},{4,5},{5,4},{6,7},{7,6},{8,9},{9,8},{10,11... | collective-permute-start | bytes 1622024 | tf_op jit(solution)/shard_map/ppermute | solution.py:322
  6.3 12.9 %collective-permute-start.2 = (bf16[192,512]{1,0:T(8,128)(2,1)S(1)}, bf16[192,512]{1,0:T(8,128)(2,1)S(1)}, u32[]{:S(2)}, u32[]{:S(2)}) collective-permute-start(bf16[192,512]{1,0:T(8,128)(2,1)S(1)} %get-tuple-element.42.refs_0_), channel_id=1, source_target_pairs={{0,8},{4,12},{8,0},{12,4},{1,9},{5,13},{9,1},{13,5},{2,10},{6,14},... | collective-permute-start | bytes 589832 | tf_op jit(solution)/shard_map/ppermute | solution.py:318
  8.9 12.0 %collective-permute-start.1 = (bf16[192,512]{1,0:T(8,128)(2,1)S(1)}, bf16[192,512]{1,0:T(8,128)(2,1)S(1)}, u32[]{:S(2)}, u32[]{:S(2)}) collective-permute-start(bf16[192,512]{1,0:T(8,128)(2,1)S(1)} %get-tuple-element.42.refs_0_), channel_id=1, source_target_pairs={{4,0},{8,4},{12,8},{5,1},{9,5},{13,9},{6,2},{10,6},{14,10},{7,3},{... | collective-permute-start | bytes 589832 | tf_op jit(solution)/shard_map/ppermute | solution.py:318
  10.2 10.7 %collective-permute-start = (bf16[192,512]{1,0:T(8,128)(2,1)S(1)}, bf16[192,512]{1,0:T(8,128)(2,1)S(1)}, u32[]{:S(2)}, u32[]{:S(2)}) collective-permute-start(bf16[192,512]{1,0:T(8,128)(2,1)S(1)} %get-tuple-element.42.refs_0_), channel_id=1, source_target_pairs={{0,4},{4,8},{8,12},{1,5},{5,9},{9,13},{2,6},{6,10},{10,14},{3,7},{... | collective-permute-start | bytes 589832 | tf_op jit(solution)/shard_map/ppermute | solution.py:318
  18.5 20.5 %collective-permute-start.6 = (bf16[528,512]{1,0:T(8,128)(2,1)S(1)}, bf16[528,512]{1,0:T(8,128)(2,1)S(1)}, u32[]{:S(2)}, u32[]{:S(2)}) collective-permute-start(bf16[528,512]{1,0:T(8,128)(2,1)S(1)} %collective-permute-done.5.refs_7_.refs_2_), channel_id=1, source_target_pairs={{0,1},{1,0},{2,3},{3,2},{4,5},{5,4},{6,7},{7,6},{8,9},{9,8},{10,11... | collective-permute-start | bytes 1622024 | tf_op jit(solution)/shard_map/ppermute | solution.py:322
  22.3 28.0 %collective-permute-start.11 = (bf16[528,512]{1,0:T(8,128)(2,1)S(1)}, bf16[528,512]{1,0:T(8,128)(2,1)S(1)}, u32[]{:S(2)}, u32[]{:S(2)}) collective-permute-start(bf16[528,512]{1,0:T(8,128)(2,1)S(1)} %shard_map.179.refs_4_.refs_5_), channel_id=1, source_target_pairs={{0,2},{1,3},{2,0},{3,1},{4,6},{5,7},{6,4},{7,5},{8,10},{9,11},{10,... | collective-permute-start | bytes 1622024 | tf_op jit(solution)/shard_map/ppermute | solution.py:322
  22.8 20.6 %copy-start.20 = (bf16[192,512]{1,0:T(8,128)(2,1)S(1)}, bf16[192,512]{1,0:T(8,128)(2,1)}, u32[]{:S(2)}) copy-start(bf16[192,512]{1,0:T(8,128)(2,1)} %copy-done.19) | copy-start | bytes 589828
  22.8 20.6 %copy-start.22 = (bf16[192,512]{1,0:T(8,128)(2,1)S(1)}, bf16[192,512]{1,0:T(8,128)(2,1)}, u32[]{:S(2)}) copy-start(bf16[192,512]{1,0:T(8,128)(2,1)} %copy-done.21) | copy-start | bytes 589828
  22.8 20.6 %copy-start.24 = (bf16[192,512]{1,0:T(8,128)(2,1)S(1)}, bf16[192,512]{1,0:T(8,128)(2,1)}, u32[]{:S(2)}) copy-start(bf16[192,512]{1,0:T(8,128)(2,1)} %copy-done.23) | copy-start | bytes 589828
  22.8 20.6 %copy-start.26 = (bf16[192,512]{1,0:T(8,128)(2,1)S(1)}, bf16[192,512]{1,0:T(8,128)(2,1)}, u32[]{:S(2)}) copy-start(bf16[192,512]{1,0:T(8,128)(2,1)} %copy-done.25) | copy-start | bytes 589828
  22.8 15.5 %collective-permute-start.15 = (bf16[192,512]{1,0:T(8,128)(2,1)S(1)}, bf16[192,512]{1,0:T(8,128)(2,1)S(1)}, u32[]{:S(2)}, u32[]{:S(2)}) collective-permute-start(bf16[192,512]{1,0:T(8,128)(2,1)S(1)} %get-tuple-element.45.refs_0_), channel_id=1, source_target_pairs={{4,0},{8,4},{12,8},{5,1},{9,5},{13,9},{6,2},{10,6},{14,10},{7,3},{... | collective-permute-start | bytes 589832 | tf_op jit(solution)/shard_map/ppermute | solution.py:318
  24.2 12.5 %collective-permute-start.3 = (bf16[192,512]{1,0:T(8,128)(2,1)}, bf16[192,512]{1,0:T(8,128)(2,1)S(1)}, u32[]{:S(2)}, u32[]{:S(2)}) collective-permute-start(bf16[192,512]{1,0:T(8,128)(2,1)} %copy-done.21), channel_id=1, source_target_pairs={{8,12},{4,0},{9,13},{5,1},{10,14},{6,2},{11,15},{7,3},{24,28},{20,... | collective-permute-start | bytes 589832 | tf_op jit(solution)/shard_map/ppermute | solution.py:318
  25.6 24.7 %collective-permute-start.17 = (bf16[256,512]{1,0:T(8,128)(2,1)S(1)}, bf16[256,512]{1,0:T(8,128)(2,1)S(1)}, u32[]{:S(2)}, u32[]{:S(2)}) collective-permute-start(bf16[256,512]{1,0:T(8,128)(2,1)S(1)} %get-tuple-element.83), channel_id=1, source_target_pairs={{0,8},{12,4},{1,9},{13,5},{2,10},{14,6},{3,11},{15,7},{16,24},{28,... | collective-permute-start | bytes 786440 | tf_op jit(solution)/shard_map/ppermute | solution.py:318
  36.7 13.6 %collective-permute-start.13 = (bf16[256,512]{1,0:T(8,128)(2,1)S(1)}, bf16[256,512]{1,0:T(8,128)(2,1)S(1)}, u32[]{:S(2)}, u32[]{:S(2)}) collective-permute-start(bf16[256,512]{1,0:T(8,128)(2,1)S(1)} %get-tuple-element.84), channel_id=1, source_target_pairs={{0,4},{4,8},{1,5},{5,9},{2,6},{6,10},{3,7},{7,11},{16,20},{20,24},... | collective-permute-start | bytes 786440 | tf_op jit(solution)/shard_map/ppermute | solution.py:318
  38.3 12.0 %collective-permute-start.16 = (bf16[256,512]{1,0:T(8,128)(2,1)S(1)}, bf16[256,512]{1,0:T(8,128)(2,1)S(1)}, u32[]{:S(2)}, u32[]{:S(2)}) collective-permute-start(bf16[256,512]{1,0:T(8,128)(2,1)S(1)} %get-tuple-element.85), channel_id=1, source_target_pairs={{8,4},{12,8},{9,5},{13,9},{10,6},{14,10},{11,7},{15,11},{24,20},{2... | collective-permute-start | bytes 786440 | tf_op jit(solution)/shard_map/ppermute | solution.py:318
  39.0 11.3 %collective-permute-start.14 = (bf16[192,512]{1,0:T(8,128)(2,1)S(1)}, bf16[192,512]{1,0:T(8,128)(2,1)S(1)}, u32[]{:S(2)}, u32[]{:S(2)}) collective-permute-start(bf16[192,512]{1,0:T(8,128)(2,1)S(1)} %get-tuple-element.45.refs_0_), channel_id=1, source_target_pairs={{0,4},{4,8},{8,12},{1,5},{5,9},{9,13},{2,6},{6,10},{10,14},{3,7},{... | collective-permute-start | bytes 589832 | tf_op jit(solution)/shard_map/ppermute | solution.py:318
  44.6 37.2 %copy-start = (bf16[192,2048]{1,0:T(8,128)(2,1)}, bf16[192,2048]{1,0:T(8,128)(2,1)S(1)}, u32[]{:S(2)}) copy-start(bf16[192,2048]{1,0:T(8,128)(2,1)S(1)} %get-tuple-element.50.refs_12_.refs_0_) | copy-start | bytes 2359300
  44.6 107.5 %copy-start.11 = (bf16[192,512]{1,0:T(8,128)(2,1)}, bf16[192,512]{1,0:T(8,128)(2,1)S(1)}, u32[]{:S(2)}) copy-start(bf16[192,512]{1,0:T(8,128)(2,1)S(1)} %get-tuple-element.43.refs_0_.refs_2_) | copy-start | bytes 589828
  50.4 28.0 %collective-permute-start.19 = (bf16[768,512]{1,0:T(8,128)(2,1)S(1)}, bf16[768,512]{1,0:T(8,128)(2,1)S(1)}, u32[]{:S(2)}, u32[]{:S(2)}) collective-permute-start(bf16[768,512]{1,0:T(8,128)(2,1)S(1)} %constant_dynamic-update-slice_fusion.refs_8_), channel_id=1, source_target_pairs={{4,6},{5,7},{6,4},{7,5},{8,10},{9,11},{10,8},{11,9},{20,22},{21,23... | collective-permute-start | bytes 2359304 | tf_op jit(solution)/shard_map/ppermute | solution.py:322
  51.1 14.6 %collective-permute-start.20 = (bf16[192,512]{1,0:T(8,128)(2,1)S(1)}, bf16[192,512]{1,0:T(8,128)(2,1)S(1)}, u32[]{:S(2)}, u32[]{:S(2)}) collective-permute-start(bf16[192,512]{1,0:T(8,128)(2,1)S(1)} %get-tuple-element.45.refs_0_), channel_id=1, source_target_pairs={{0,8},{4,12},{8,0},{12,4},{1,9},{5,13},{9,1},{13,5},{2,10},{6,14},... | collective-permute-start | bytes 589832 | tf_op jit(solution)/shard_map/ppermute | solution.py:318
  65.7 8.5 %collective-permute-start.21 = (bf16[192,512]{1,0:T(8,128)(2,1)S(1)}, bf16[192,512]{1,0:T(8,128)(2,1)S(1)}, u32[]{:S(2)}, u32[]{:S(2)}) collective-permute-start(bf16[192,512]{1,0:T(8,128)(2,1)S(1)} %collective-permute-done.20.refs_3_), channel_id=1, source_target_pairs={{8,12},{4,0},{9,13},{5,1},{10,14},{6,2},{11,15},{7,3},{24,28},{20,... | collective-permute-start | bytes 589832 | tf_op jit(solution)/shard_map/ppermute | solution.py:318
  67.0 8.0 %collective-permute-start.9 = (bf16[192,512]{1,0:T(8,128)(2,1)S(1)}, bf16[192,512]{1,0:T(8,128)(2,1)S(1)}, u32[]{:S(2)}, u32[]{:S(2)}) collective-permute-start(bf16[192,512]{1,0:T(8,128)(2,1)S(1)} %get-tuple-element.43.refs_0_.refs_2_), channel_id=1, source_target_pairs={{0,8},{12,4},{1,9},{13,5},{2,10},{14,6},{3,11},{15,7},{16,24},{28,... | collective-permute-start | bytes 589832 | tf_op jit(solution)/shard_map/ppermute | solution.py:318
  70.9 4.1 %collective-permute-start.8 = (bf16[192,512]{1,0:T(8,128)(2,1)S(1)}, bf16[192,512]{1,0:T(8,128)(2,1)S(1)}, u32[]{:S(2)}, u32[]{:S(2)}) collective-permute-start(bf16[192,512]{1,0:T(8,128)(2,1)S(1)} %get-tuple-element.43.refs_0_.refs_2_), channel_id=1, source_target_pairs={{8,4},{12,8},{9,5},{13,9},{10,6},{14,10},{11,7},{15,11},{24,20},{2... | collective-permute-start | bytes 589832 | tf_op jit(solution)/shard_map/ppermute | solution.py:318
  71.6 6.7 %collective-permute-start.7 = (bf16[192,512]{1,0:T(8,128)(2,1)S(1)}, bf16[192,512]{1,0:T(8,128)(2,1)S(1)}, u32[]{:S(2)}, u32[]{:S(2)}) collective-permute-start(bf16[192,512]{1,0:T(8,128)(2,1)S(1)} %get-tuple-element.43.refs_0_.refs_2_), channel_id=1, source_target_pairs={{0,4},{4,8},{1,5},{5,9},{2,6},{6,10},{3,7},{7,11},{16,20},{20,24},... | collective-permute-start | bytes 589832 | tf_op jit(solution)/shard_map/ppermute | solution.py:318
  74.3 7.5 %collective-permute-start.18 = (bf16[768,512]{1,0:T(8,128)(2,1)S(1)}, bf16[768,512]{1,0:T(8,128)(2,1)S(1)}, u32[]{:S(2)}, u32[]{:S(2)}) collective-permute-start(bf16[768,512]{1,0:T(8,128)(2,1)S(1)} %constant_dynamic-update-slice_fusion.refs_8_), channel_id=1, source_target_pairs={{4,5},{5,4},{6,7},{7,6},{8,9},{9,8},{10,11},{11,10},{20,21},{21,20... | collective-permute-start | bytes 2359304 | tf_op jit(solution)/shard_map/ppermute | solution.py:322
  78.3 3.5 %collective-permute-start.22 = (bf16[768,512]{1,0:T(8,128)(2,1)S(1)}, bf16[768,512]{1,0:T(8,128)(2,1)S(1)}, u32[]{:S(2)}, u32[]{:S(2)}) collective-permute-start(bf16[768,512]{1,0:T(8,128)(2,1)S(1)} %collective-permute-done.19.refs_10_), channel_id=1, source_target_pairs={{4,5},{5,4},{6,7},{7,6},{8,9},{9,8},{10,11},{11,10},{20,21},{21,20... | collective-permute-start | bytes 2359304 | tf_op jit(solution)/shard_map/ppermute | solution.py:322
  79.0 2.0 %collective-permute-start.10 = (bf16[528,512]{1,0:T(8,128)(2,1)S(1)}, bf16[528,512]{1,0:T(8,128)(2,1)S(1)}, u32[]{:S(2)}, u32[]{:S(2)}) collective-permute-start(bf16[528,512]{1,0:T(8,128)(2,1)S(1)} %shard_map.179.refs_4_.refs_5_), channel_id=1, source_target_pairs={{0,1},{1,0},{2,3},{3,2},{4,5},{5,4},{6,7},{7,6},{8,9},{9,8},{10,11... | collective-permute-start | bytes 1622024 | tf_op jit(solution)/shard_map/ppermute | solution.py:322
  79.1 2.7 %collective-permute-start.12 = (bf16[528,512]{1,0:T(8,128)(2,1)S(1)}, bf16[528,512]{1,0:T(8,128)(2,1)S(1)}, u32[]{:S(2)}, u32[]{:S(2)}) collective-permute-start(bf16[528,512]{1,0:T(8,128)(2,1)S(1)} %collective-permute-done.11.refs_6_.refs_7_), channel_id=1, source_target_pairs={{0,1},{1,0},{2,3},{3,2},{4,5},{5,4},{6,7},{7,6},{8,9},{9,8},{10,11... | collective-permute-start | bytes 1622024 | tf_op jit(solution)/shard_map/ppermute | solution.py:322
  85.6 24.2 %collective-permute-start.24 = (bf16[192,1024]{1,0:T(8,128)(2,1)S(1)}, bf16[192,1024]{1,0:T(8,128)(2,1)S(1)}, u32[]{:S(2)}, u32[]{:S(2)}) collective-permute-start(bf16[192,1024]{1,0:T(8,128)(2,1)S(1)} %shard_map.180.refs_0_), channel_id=1, source_target_pairs={{4,0},{8,12},{5,1},{9,13},{6,2},{10,14},{7,3},{11,15},{20,16},{24,... | collective-permute-start | bytes 1179656 | tf_op jit(solution)/shard_map/ppermute | solution.py:318
  86.9 22.9 %collective-permute-start.23 = (bf16[192,1024]{1,0:T(8,128)(2,1)S(1)}, bf16[192,1024]{1,0:T(8,128)(2,1)S(1)}, u32[]{:S(2)}, u32[]{:S(2)}) collective-permute-start(bf16[192,1024]{1,0:T(8,128)(2,1)S(1)} %shard_map.180.refs_0_), channel_id=1, source_target_pairs={{4,8},{8,4},{5,9},{9,5},{6,10},{10,6},{7,11},{11,7},{20,24},{24,20... | collective-permute-start | bytes 1179656 | tf_op jit(solution)/shard_map/ppermute | solution.py:318
  89.7 62.5 %copy-start.13 = (bf16[192,512]{1,0:T(8,128)(2,1)}, bf16[192,512]{1,0:T(8,128)(2,1)S(1)}, u32[]{:S(2)}) copy-start(bf16[192,512]{1,0:T(8,128)(2,1)S(1)} %get-tuple-element.53.refs_0_.refs_3_) | copy-start | bytes 589828
  89.7 16.9 %collective-permute-start.28 = (bf16[192,512]{1,0:T(8,128)(2,1)S(1)}, bf16[192,512]{1,0:T(8,128)(2,1)S(1)}, u32[]{:S(2)}, u32[]{:S(2)}) collective-permute-start(bf16[192,512]{1,0:T(8,128)(2,1)S(1)} %get-tuple-element.53.refs_0_.refs_3_), channel_id=1, source_target_pairs={{0,8},{12,4},{1,9},{13,5},{2,10},{14,6},{3,11},{15,7},{16,24},{28,... | collective-permute-start | bytes 589832 | tf_op jit(solution)/shard_map/ppermute | solution.py:318
  101.3 5.3 %collective-permute-start.27 = (bf16[192,512]{1,0:T(8,128)(2,1)S(1)}, bf16[192,512]{1,0:T(8,128)(2,1)S(1)}, u32[]{:S(2)}, u32[]{:S(2)}) collective-permute-start(bf16[192,512]{1,0:T(8,128)(2,1)S(1)} %get-tuple-element.53.refs_0_.refs_3_), channel_id=1, source_target_pairs={{8,4},{12,8},{9,5},{13,9},{10,6},{14,10},{11,7},{15,11},{24,20},{2... | collective-permute-start | bytes 589832 | tf_op jit(solution)/shard_map/ppermute | solution.py:318
  102.0 7.7 %collective-permute-start.26 = (bf16[192,512]{1,0:T(8,128)(2,1)S(1)}, bf16[192,512]{1,0:T(8,128)(2,1)S(1)}, u32[]{:S(2)}, u32[]{:S(2)}) collective-permute-start(bf16[192,512]{1,0:T(8,128)(2,1)S(1)} %get-tuple-element.53.refs_0_.refs_3_), channel_id=1, source_target_pairs={{0,4},{4,8},{1,5},{5,9},{2,6},{6,10},{3,7},{7,11},{16,20},{20,24},... | collective-permute-start | bytes 589832 | tf_op jit(solution)/shard_map/ppermute | solution.py:318
  112.9 3.3 %collective-permute-start.29 = (bf16[192,1024]{1,0:T(8,128)(2,1)S(1)}, bf16[192,1024]{1,0:T(8,128)(2,1)S(1)}, u32[]{:S(2)}, u32[]{:S(2)}) collective-permute-start(bf16[192,1024]{1,0:T(8,128)(2,1)S(1)} %shard_map.183.refs_0_), channel_id=1, source_target_pairs={{4,8},{8,4},{5,9},{9,5},{6,10},{10,6},{7,11},{11,7},{20,24},{24,20... | collective-permute-start | bytes 1179656 | tf_op jit(solution)/shard_map/ppermute | solution.py:318
  113.6 18.8 %collective-permute-start.25 = (bf16[192,1024]{1,0:T(8,128)(2,1)S(1)}, bf16[192,1024]{1,0:T(8,128)(2,1)S(1)}, u32[]{:S(2)}, u32[]{:S(2)}) collective-permute-start(bf16[192,1024]{1,0:T(8,128)(2,1)S(1)} %collective-permute-done.23.refs_1_.refs_13_), channel_id=1, source_target_pairs={{4,0},{8,12},{5,1},{9,13},{6,2},{10,14},{7,3},{11,15},{20,16},{24,... | collective-permute-start | bytes 1179656 | tf_op jit(solution)/shard_map/ppermute | solution.py:318
  114.9 25.9 %collective-permute-start.30 = (bf16[192,1024]{1,0:T(8,128)(2,1)S(1)}, bf16[192,1024]{1,0:T(8,128)(2,1)S(1)}, u32[]{:S(2)}, u32[]{:S(2)}) collective-permute-start(bf16[192,1024]{1,0:T(8,128)(2,1)S(1)} %shard_map.183.refs_0_), channel_id=1, source_target_pairs={{4,0},{8,12},{5,1},{9,13},{6,2},{10,14},{7,3},{11,15},{20,16},{24,... | collective-permute-start | bytes 1179656 | tf_op jit(solution)/shard_map/ppermute | solution.py:318
  116.2 31.3 %collective-permute-start.31 = (bf16[192,1024]{1,0:T(8,128)(2,1)S(1)}, bf16[192,1024]{1,0:T(8,128)(2,1)S(1)}, u32[]{:S(2)}, u32[]{:S(2)}) collective-permute-start(bf16[192,1024]{1,0:T(8,128)(2,1)S(1)} %collective-permute-done.29.refs_1_), channel_id=1, source_target_pairs={{4,0},{8,12},{5,1},{9,13},{6,2},{10,14},{7,3},{11,15},{20,16},{24,... | collective-permute-start | bytes 1179656 | tf_op jit(solution)/shard_map/ppermute | solution.py:318
  151.2 10.0 %collective-permute-start.33 = (f32[520,512]{1,0:T(8,128)}, f32[520,512]{1,0:T(8,128)}, u32[]{:S(2)}, u32[]{:S(2)}) collective-permute-start(f32[520,512]{1,0:T(8,128)} %get-tuple-element.64), channel_id=1, source_target_pairs={{0,1},{1,0},{2,3},{3,2},{4,5},{5,4},{6,7},{7,6},{8,9},{9,8},{10,11... | collective-permute-start | bytes 3194888 | tf_op jit(solution)/shard_map/ppermute | solution.py:322
  155.4 7.4 %collective-permute-start.37 = (f32[520,512]{1,0:T(8,128)}, f32[520,512]{1,0:T(8,128)}, u32[]{:S(2)}, u32[]{:S(2)}) collective-permute-start(f32[520,512]{1,0:T(8,128)} %get-tuple-element.72), channel_id=1, source_target_pairs={{0,1},{1,0},{2,3},{3,2},{4,5},{5,4},{6,7},{7,6},{8,9},{9,8},{10,11... | collective-permute-start | bytes 3194888 | tf_op jit(solution)/shard_map/ppermute | solution.py:322
  155.4 25.1 %collective-permute-start.32 = (f32[512,512]{1,0:T(8,128)}, f32[512,512]{1,0:T(8,128)S(1)}, u32[]{:S(2)}, u32[]{:S(2)}) collective-permute-start(f32[512,512]{1,0:T(8,128)} %copy-done.34), channel_id=1, source_target_pairs={{0,1},{1,0},{2,3},{3,2},{4,5},{5,4},{6,7},{7,6},{8,9},{9,8},{10,11... | collective-permute-start | bytes 3145736 | tf_op jit(solution)/shard_map/ppermute | solution.py:322
  155.9 27.0 %collective-permute-start.36 = (f32[512,512]{1,0:T(8,128)}, f32[512,512]{1,0:T(8,128)S(1)}, u32[]{:S(2)}, u32[]{:S(2)}) collective-permute-start(f32[512,512]{1,0:T(8,128)} %copy-done.33), channel_id=1, source_target_pairs={{0,1},{1,0},{2,3},{3,2},{4,5},{5,4},{6,7},{7,6},{8,9},{9,8},{10,11... | collective-permute-start | bytes 3145736 | tf_op jit(solution)/shard_map/ppermute | solution.py:322
  164.5 3.7 %collective-permute-start.35 = (f32[2,512]{1,0:T(2,128)S(1)}, f32[2,512]{1,0:T(2,128)S(1)}, u32[]{:S(2)}, u32[]{:S(2)}) collective-permute-start(f32[2,512]{1,0:T(2,128)S(1)} %pad_maximum_fusion.1), channel_id=1, source_target_pairs={{0,2},{1,3},{2,0},{3,1},{4,6},{5,7},{6,4},{7,5},{8,10},{9,11},{10,... | collective-permute-start | bytes 12296 | tf_op jit(solution)/shard_map/ppermute | solution.py:322
  165.1 15.4 %collective-permute-start.34 = (f16[512,512]{1,0:T(8,128)(2,1)S(1)}, f16[512,512]{1,0:T(8,128)(2,1)S(1)}, u32[]{:S(2)}, u32[]{:S(2)}) collective-permute-start(f16[512,512]{1,0:T(8,128)(2,1)S(1)} %multiply_convert_fusion.1), channel_id=1, source_target_pairs={{0,2},{1,3},{2,0},{3,1},{4,6},{5,7},{6,4},{7,5},{8,10},{9,11},{10,... | collective-permute-start | bytes 1572872 | tf_op jit(solution)/shard_map/ppermute | solution.py:322
  166.6 13.3 %collective-permute-start.39 = (f32[2,512]{1,0:T(2,128)S(1)}, f32[2,512]{1,0:T(2,128)S(1)}, u32[]{:S(2)}, u32[]{:S(2)}) collective-permute-start(f32[2,512]{1,0:T(2,128)S(1)} %pad_maximum_fusion.2), channel_id=1, source_target_pairs={{0,2},{1,3},{2,0},{3,1},{4,6},{5,7},{6,4},{7,5},{8,10},{9,11},{10,... | collective-permute-start | bytes 12296 | tf_op jit(solution)/shard_map/ppermute | solution.py:322
  168.2 22.3 %collective-permute-start.38 = (f16[512,512]{1,0:T(8,128)(2,1)S(1)}, f16[512,512]{1,0:T(8,128)(2,1)S(1)}, u32[]{:S(2)}, u32[]{:S(2)}) collective-permute-start(f16[512,512]{1,0:T(8,128)(2,1)S(1)} %multiply_convert_fusion), channel_id=1, source_target_pairs={{0,2},{1,3},{2,0},{3,1},{4,6},{5,7},{6,4},{7,5},{8,10},{9,11},{10,... | collective-permute-start | bytes 1572872 | tf_op jit(solution)/shard_map/ppermute | solution.py:322
  (35 other events, 196.4 us)

commit v3 on v2

--- a/solution.py
+++ b/solution.py
@@ -17,7 +17,6 @@
 
 F32 = jnp.float32
 BF16 = jnp.bfloat16
-CHUNKS = 2
 
 
 def adam_update(param, grad, moment, square):
@@ -169,28 +168,38 @@
 
 
 def codes_body(
-    place, own, low, high, across, relay, enc0, enc1, enc2, enc3, codes, mask, full, active, bias
+    place,
+    own,
+    low,
+    high,
+    across,
+    relay1,
+    relay2,
+    enc0,
+    enc1,
+    enc2,
+    enc3,
+    codes,
+    mask,
+    full,
+    active,
+    bias,
 ):
     z, i = place[0], place[1]
     width = own.shape[1]
-    full[:, columns(z * width, width)] = own[...]
-    full[:, columns(((z + 2) % 4) * width, width)] = across[...]
-
-    @pl.when(z < 3)
-    def _():
-        full[:, columns((z + 1) * width, width)] = high[...]
-
-    @pl.when(z == 3)
-    def _():
-        full[:, :width] = relay[...]
-
-    @pl.when(z > 0)
-    def _():
-        full[:, columns((z - 1) * width, width)] = low[...]
-
-    @pl.when(z == 0)
-    def _():
-        full[:, 3 * width :] = relay[...]
+    for at, blocks in enumerate(
+        (
+            (own, high, relay1, relay2),
+            (low, own, high, across),
+            (across, low, own, high),
+            (relay2, relay1, low, own),
+        )
+    ):
+
+        @pl.when(z == at)
+        def _(blocks=blocks):
+            for b, block in enumerate(blocks):
+                full[:, b * width : (b + 1) * width] = block[...]
 
     total = jnp.zeros(codes.shape, F32)
     piece = codes.shape[1] // 4
@@ -274,23 +283,27 @@
     home[...] = full[:, columns(z * width, width)]
 
 
-def grad_body(scale, slots, place, *refs):
+def grad_body(scale, slots, place, left, right, row, *outs):
     i = place[1]
-    lefts, rights, sums = refs[:CHUNKS], refs[CHUNKS : 2 * CHUNKS], refs[2 * CHUNKS : 3 * CHUNKS]
-    outs = refs[3 * CHUNKS :]
-    width = lefts[0].shape[1] // 4
+    width = left.shape[1] // 4
     for slot, out in zip(slots, outs):
-        total = jnp.zeros((width, out.shape[1]), F32)
-        for left, right in zip(lefts, rights):
-            total += lax.dot_general(
-                left[:, columns((i ^ slot) * width, width)],
-                right[...],
-                (((0,), (0,)), ((), ())),
-                preferred_element_type=F32,
-            )
-        out[:width] = scale * total
-    row = functools.reduce(jnp.add, [value[...] for value in sums])
-    outs[0][width:] = jnp.broadcast_to(row, (outs[0].shape[0] - width, row.shape[1]))
+        out[:width] = scale * lax.dot_general(
+            left[:, columns((i ^ slot) * width, width)],
+            right[...],
+            (((0,), (0,)), ((), ())),
+            preferred_element_type=F32,
+        )
+    outs[0][width:] = jnp.broadcast_to(row[...], (outs[0].shape[0] - width, row.shape[1]))
+
+
+def far_body(place, kept, received, scaled, small):
+    width = scaled.shape[0]
+    total = kept[:width] + received[:width]
+    largest = jnp.maximum(jnp.max(jnp.abs(total), axis=0, keepdims=True), 1e-30)
+    scaled[...] = total * (16384.0 / largest)
+    row = kept[width:] + received[width:]
+    at = lax.broadcasted_iota(jnp.int32, row.shape, 0)
+    small[...] = jnp.where(at == 0, largest * (1.0 / 16384.0), row)
 
 
 def line_shards(
@@ -306,8 +319,7 @@
     dec_square,
 ):
     rows = activations.shape[0] * 4
-    chunk = activations.shape[0] // CHUNKS
-    width = activations.shape[1]
+    count, width = activations.shape
     latents = encoder.shape[1]
     half = width // 2
     features = 4 * width
@@ -321,9 +333,9 @@
         pairs = [(4 * p + k, 4 * p + (k ^ bits)) for p in planes for k in range(4)]
         return lax.ppermute(value, ("latent", "dp"), pairs)
 
-    up = [(0, 1), (1, 2), (2, 3)]
-    down = [(1, 0), (2, 1), (3, 2)]
-    two = [(0, 2), (1, 3), (2, 0), (3, 1)]
+    low = along(activations, [(0, 1), (1, 2), (2, 3)])
+    high = along(activations, [(1, 0), (2, 1), (3, 2)])
+    across = along(activations, [(0, 2), (3, 1)])
 
     (enc_own,) = local_kernel(
         encoder_body,
@@ -332,140 +344,132 @@
         encoder,
         enc_bias.reshape(1, -1),
     )
-
-    parts = [activations[c * chunk : (c + 1) * chunk] for c in range(CHUNKS)]
-    gathered = []
-    for part in parts:
-        part = behind(part, *(gathered[-1][1:4] if gathered else (enc_own,)))
-        low, high, across = along(part, up), along(part, down), along(part, two)
-        relay = along(across, [(2, 3), (1, 0)])
-        gathered.append((part, low, high, across, relay))
-
     enc_chip, enc_core = flip(enc_own, 2), flip(enc_own, 1)
-    enc = [enc_own, enc_core, enc_chip, flip(enc_chip, 1)]
     (dec_own,) = local_kernel(
         decoder_body,
         [shape((width + EXTRA, latents), BF16)],
         place,
         decoder,
-        after=(enc_core, enc_chip, *gathered[0][1:4]),
-    )
-    dec_core, dec_chip = flip(dec_own, 1), flip(dec_own, 2)
-
-    first, second = dec_own[:half], dec_own[half:width]
+        after=(enc_core, enc_chip),
+    )
+    dec_chip, dec_core = flip(dec_own, 2), flip(dec_own, 1)
+    relay1 = along(behind(jnp.where(z == 1, high, low), enc_core), [(1, 0), (2, 3)])
+    relay2 = along(behind(across, relay1), [(1, 0), (2, 3)])
+    enc = [enc_own, enc_core, enc_chip, flip(enc_chip, 1)]
+
+    dec_late = behind(dec_own, across)
+    first, second = dec_late[:half], dec_late[half:width]
     dec_pieces = [
         along(jnp.where(z >= 1, second, first), [(0, 1), (1, 2)]),
         along(jnp.where(z >= 3, second, first), [(2, 1), (3, 2)]),
         along(jnp.where(z >= 2, first, second), [(0, 2), (3, 1)]),
     ]
-
-    flops = 2 * chunk * features * latents
-    inputs, codes, masks, actives = [], [], [], []
-    for step, part in enumerate(gathered):
-        low_codes, mask, full, active = local_kernel(
-            codes_body,
-            [
-                shape((chunk, latents), BF16),
-                shape((chunk, latents), BF16),
-                shape((chunk, features), BF16),
-                shape((1, latents), F32),
-            ],
-            place,
-            *part,
-            *enc,
-            flops=flops,
-            scratch=[pltpu.VMEM((1, latents), F32)],
-        )
-        if step == 0:
-            dec = [dec_own, dec_core, dec_chip, flip(behind(dec_chip, low_codes), 1)]
-            first_codes = low_codes
-        inputs.append(full)
-        codes.append(low_codes)
-        masks.append(mask)
-        actives.append(active)
-    nearby = []
-    for low_codes in codes:
-        low = along(low_codes, [(0, 1), (1, 2)])
-        high = along(low_codes, [(2, 1), (3, 2)])
-        across = along(low_codes, [(0, 2), (3, 1)])
-        nearby.append((low_codes, low, high, across))
-    dec_pieces = [
-        behind(piece, dec_chip, first_codes, *gathered[-1][1:3]) for piece in dec_pieces
-    ]
+    dec_pieces = [behind(piece, dec_chip, relay2) for piece in dec_pieces]
     rows_own = jnp.concatenate(dec_pieces, axis=0)
+    dec = [dec_own, dec_core, dec_chip, flip(dec_chip, 1)]
     rows_chip, rows_core = flip(rows_own, 2, (1, 2)), flip(rows_own, 1, (1, 2))
-    rows_both = flip(behind(rows_chip, *gathered[-1][3:], *nearby[0][1:]), 1, (1, 2))
-    dec_rows = [rows_own, rows_core, rows_chip, rows_both]
-    errors = []
-    for step in range(CHUNKS):
-        (own_error,) = local_kernel(
-            error_body,
-            [shape((chunk, features // 2), BF16)],
-            place,
-            *nearby[step],
-            *dec,
-            *dec_rows,
-            inputs[step],
-            flops=2 * flops,
-            after=errors[-1][1:3] if errors else (),
-        )
-        passed = along(own_error, [(1, 0), (2, 3)])
-        swapped = along(own_error, [(1, 2), (2, 1)])
-        relayed = along(swapped, [(1, 0), (2, 3)])
-        errors.append((own_error, swapped, passed, relayed))
-
-    grads, bias_sums, fulls, homes = [], [], [], []
-    for error, mask in zip(errors, masks):
-        grad_low, bias_sum, norms, full, home = local_kernel(
-            functools.partial(grad_code_body, rows),
-            [
-                shape((chunk, latents), BF16),
-                shape((1, latents), F32),
-                shape((1, latents), F32),
-                shape((chunk, features), BF16),
-                shape((chunk, width), BF16),
-            ],
-            place,
-            *error,
-            mask,
-            *dec,
-            flops=flops,
-        )
-        grads.append(grad_low)
-        bias_sums.append(bias_sum)
-        fulls.append(full)
-        homes.append(home)
-    error = jnp.concatenate(homes, axis=0)
-
-    def reduced(scale, lefts, rights, sums):
+
+    flops = 2 * count * features * latents
+    codes, mask, inputs, active = local_kernel(
+        codes_body,
+        [
+            shape((count, latents), BF16),
+            shape((count, latents), BF16),
+            shape((count, features), BF16),
+            shape((1, latents), F32),
+        ],
+        place,
+        activations,
+        low,
+        high,
+        across,
+        relay1,
+        relay2,
+        *enc,
+        flops=flops,
+        after=(rows_core, dec[1], dec[3]),
+        scratch=[pltpu.VMEM((1, latents), F32)],
+    )
+    codes_low = along(codes, [(0, 1), (1, 2)])
+    codes_high = along(codes, [(2, 1), (3, 2)])
+    codes_across = along(codes, [(0, 2), (3, 1)])
+    rows_both = flip(behind(rows_chip, codes_low, codes_high, codes_across), 1, (1, 2))
+
+    (own_error,) = local_kernel(
+        error_body,
+        [shape((count, features // 2), BF16)],
+        place,
+        codes,
+        codes_low,
+        codes_high,
+        codes_across,
+        *dec,
+        rows_own,
+        rows_core,
+        rows_chip,
+        rows_both,
+        inputs,
+        flops=2 * flops,
+    )
+    swapped = along(own_error, [(1, 2), (2, 1)])
+    passed = along(own_error, [(1, 0), (2, 3)])
+    relayed = along(swapped, [(1, 0), (2, 3)])
+
+    grad_low, bias_sum, norms, full_error, error = local_kernel(
+        functools.partial(grad_code_body, rows),
+        [
+            shape((count, latents), BF16),
+            shape((1, latents), F32),
+            shape((1, latents), F32),
+            shape((count, features), BF16),
+            shape((count, width), BF16),
+        ],
+        place,
+        own_error,
+        swapped,
+        passed,
+        relayed,
+        mask,
+        *dec,
+        flops=flops,
+    )
+
+    def reduced(scale, left, right, row):
         def slots(*which):
             return local_kernel(
                 functools.partial(grad_body, scale, which),
                 [shape((width + 8, latents), F32), shape((width, latents), F32)],
                 place,
-                *lefts,
-                *rights,
-                *sums,
-                flops=CHUNKS * flops // 2,
+                left,
+                right,
+                row,
+                flops=flops // 2,
             )
 
         send_far, send_near = slots(3, 1)
         keep_far, keep_near = slots(2, 0)
-        far = keep_far + flip(send_far, 1)
-        row = far[width : width + 1]
-        far = far[:width]
-        largest = jnp.maximum(jnp.max(jnp.abs(far), axis=0, keepdims=True), 1e-30)
-        sent = (far * (16384.0 / largest)).astype(jnp.float16)
+        scaled, small = local_kernel(
+            far_body,
+            [shape((width, latents), F32), shape((8, latents), F32)],
+            place,
+            keep_far,
+            flip(send_far, 1),
+        )
+        sent = scaled.astype(jnp.float16)
+        received, small_received = flip(sent, 2), flip(small, 2)
         near = keep_near + flip(send_near, 1)
-        small = flip(jnp.concatenate([largest, row], axis=0), 2)
-        block = near + flip(sent, 2).astype(F32) * (small[:1] / 16384.0)
-        return block, row + small[1:]
-
-    grad_dec_rows, active_sum = reduced(-2.0 / rows, fulls, codes, actives)
-    grad_encoder, grad_bias = reduced(1.0, inputs, grads, bias_sums)
-    grad_bias = lax.dynamic_slice(
-        grad_bias.reshape(latents), (i * enc_bias.shape[0],), (enc_bias.shape[0],)
-    )
+        block = near + received.astype(F32) * small_received[:1]
+        return block, small[1] + small_received[1], sent
+
+    grad_dec_rows, active_sum, dec_sent = reduced(-2.0 / rows, full_error, codes, active)
+    grad_encoder, grad_bias, enc_sent = reduced(1.0, inputs, grad_low, bias_sum)
+    grad_bias = lax.dynamic_slice(grad_bias, (i * enc_bias.shape[0],), (enc_bias.shape[0],))
+    decoder, dec_moment, dec_square = lax.optimization_barrier(
+        (decoder, dec_moment, dec_square, dec_sent)
+    )[:3]
+    encoder, enc_moment, enc_square = lax.optimization_barrier(
+        (encoder, enc_moment, enc_square, enc_sent)
+    )[:3]
     grad_decoder = grad_dec_rows + decoder * (active_sum / norms) / rows
 
     new_decoder, new_dec_moment, new_dec_square = adam_update(

time: 194 us -> 191 us (0.985)
  starting transfers between devices: 72.4 us -> 52.8 us
  waiting for transfers between devices: 80 us -> 95.9 us
    ppermute x23 -> x14, starting transfers between devices: 62.4 us -> 41.8 us  [along(): return lax.ppermute(value, 'latent', pairs)]
    ppermute x23 -> x14, waiting for transfers between devices: 55.2 us -> 67.5 us  [along(): return lax.ppermute(value, 'latent', pairs)]
    ppermute x17, waiting for transfers between devices: 24.8 us -> 28.3 us  [flip(): return lax.ppermute(value, ('latent', 'dp'), pairs)]
    add x2 -> x0, other arithmetic: 2.89 us -> none  [reduced(): far = keep_far + flip(send_far, 1)]
    pallas_call x12 -> x11, Pallas kernels: 19.9 us -> 21.8 us  [local_kernel(): pl.pallas_call(run, out_shape=outs, in_specs=[SMEM] + [VMEM] * len(args)...]
    unnamed x88 -> x70, local copies, waits for them, and re-layouts: 9.61 us -> 10.8 us
  transfers between devices with their start and end apart: 40 -> 31, of which waited for: 18 -> 14; matrix products, arithmetic and copies ran while one was open for 4% -> 3% of each run, Pallas kernels for 5% -> 7%
where the time goes in v3:
time: 191 us; the launch traced here: 190 us
  waiting for transfers between devices  95.9 us (50%)
  starting transfers between devices  52.8 us (28%)
  Pallas kernels  21.8 us (11%)
  local copies, waits for them, and re-layouts  10.8 us (6%)
  other arithmetic  7.87 us (4%)
    ppermute x14, waiting for transfers between devices, along(): return lax.ppermute(value, 'latent', pairs)  67.5 us
    ppermute x14, starting transfers between devices, along(): return lax.ppermute(value, 'latent', pairs)  41.8 us
    ppermute x17, waiting for transfers between devices, flip(): return lax.ppermute(value, ('latent', 'dp'), pairs)  28.3 us
    pallas_call x11, Pallas kernels, local_kernel(): pl.pallas_call(run, out_shape=outs, in_specs=[SMEM] + [VMEM] * len(args)...  21.8 us
    ppermute x17, starting transfers between devices, flip(): return lax.ppermute(value, ('latent', 'dp'), pairs)  11 us
    unnamed x70, local copies, waits for them, and re-layouts  10.8 us
    sub x3, other arithmetic, adam_update(): param - learn_rate * (moment_new / first_fix) / (jnp.sqrt(square_new / se...  6.73 us
  transfers between devices with their start and end apart: 31, of which 14 were waited for; matrix products, arithmetic and copies ran while one was open for 3% of the time, Pallas kernels for 7%

profile of v3, /device:TPU:0, one launch (start us, length us, event | category | flops | bytes accessed | tf_op | source)
XLA Modules:
  0.0 190.4 jit_solution(15936020430733831176)
XLA Ops:
  0.6 5.0 %collective-permute-start = (bf16[384,512]{1,0:T(8,128)(2,1)}, bf16[384,512]{1,0:T(8,128)(2,1)S(1)}, u32[]{:S(2)}, u32[]{:S(2)}) collective-permute-start(bf16[384,512]{1,0:T(8,128)(2,1)} %refs_0_.5), channel_id=1, source_target_pairs={{0,4},{4,8},{8,12},{1,5},{5,9},{9,13},{2,6},{6,10},{10,14},{3,7},{... | collective-permute-start | bytes 1179656 | tf_op jit(solution)/shard_map/ppermute | solution.py:330
  5.6 1.3 collective-permute-start.1
  7.0 1.2 copy-done.4
  9.6 1.6 collective-permute-start.6
  11.1 6.3 %collective-permute-start.2 = (bf16[384,512]{1,0:T(8,128)(2,1)}, bf16[384,512]{1,0:T(8,128)(2,1)}, u32[]{:S(2)}, u32[]{:S(2)}) collective-permute-start(bf16[384,512]{1,0:T(8,128)(2,1)} %refs_0_.5), channel_id=1, source_target_pairs={{0,8},{12,4},{1,9},{13,5},{2,10},{14,6},{3,11},{15,7},{16,24},{28,... | collective-permute-start | bytes 1179656 | tf_op jit(solution)/shard_map/ppermute | solution.py:330
  17.4 1.0 collective-permute-done.1.refs_2_
  19.2 1.3 collective-permute-start.4
  20.5 3.8 %collective-permute-done.6.refs_2_.refs_8_ = bf16[528,512]{1,0:T(8,128)(2,1)S(1)} collective-permute-done((bf16[528,512]{1,0:T(8,128)(2,1)S(1)}, bf16[528,512]{1,0:T(8,128)(2,1)S(1)}, u32[]{:S(2)}, u32[]{:S(2)}) %collective-permute-start.6) | collective-permute-done | bytes 540704 | tf_op jit(solution)/shard_map/ppermute | solution.py:334
  24.9 1.6 collective-permute-start.9
  26.5 4.9 %collective-permute-done.4.refs_4_ = bf16[384,512]{1,0:T(8,128)(2,1)} collective-permute-done((bf16[384,512]{1,0:T(8,128)(2,1)}, bf16[384,512]{1,0:T(8,128)(2,1)}, u32[]{:S(2)}, u32[]{:S(2)}) %collective-permute-start.4) | collective-permute-done | bytes 393248 | tf_op jit(solution)/shard_map/ppermute | solution.py:330
  31.4 1.3 collective-permute-start.5
  32.8 0.8 collective-permute-start.10
  33.6 5.2 %collective-permute-start.8 = (bf16[256,512]{1,0:T(8,128)(2,1)S(1)}, bf16[256,512]{1,0:T(8,128)(2,1)S(1)}, u32[]{:S(2)}, u32[]{:S(2)}) collective-permute-start(bf16[256,512]{1,0:T(8,128)(2,1)S(1)} %get-tuple-element.88), channel_id=1, source_target_pairs={{0,4},{4,8},{1,5},{5,9},{2,6},{6,10},{3,7},{7,11},{16,20},{20,24},... | collective-permute-start | bytes 786440 | tf_op jit(solution)/shard_map/ppermute | solution.py:330
  38.8 3.4 %collective-permute-start.11 = (bf16[256,512]{1,0:T(8,128)(2,1)S(1)}, bf16[256,512]{1,0:T(8,128)(2,1)S(1)}, u32[]{:S(2)}, u32[]{:S(2)}) collective-permute-start(bf16[256,512]{1,0:T(8,128)(2,1)S(1)} %get-tuple-element.87), channel_id=1, source_target_pairs={{0,8},{12,4},{1,9},{13,5},{2,10},{14,6},{3,11},{15,7},{16,24},{28,... | collective-permute-start | bytes 786440 | tf_op jit(solution)/shard_map/ppermute | solution.py:330
  42.5 2.8 %collective-permute-done.8 = bf16[256,512]{1,0:T(8,128)(2,1)S(1)} collective-permute-done((bf16[256,512]{1,0:T(8,128)(2,1)S(1)}, bf16[256,512]{1,0:T(8,128)(2,1)S(1)}, u32[]{:S(2)}, u32[]{:S(2)}) %collective-permute-start.8) | collective-permute-done | bytes 262176 | tf_op jit(solution)/shard_map/ppermute | solution.py:330
  45.3 2.8 %collective-permute-done.11 = bf16[256,512]{1,0:T(8,128)(2,1)S(1)} collective-permute-done((bf16[256,512]{1,0:T(8,128)(2,1)S(1)}, bf16[256,512]{1,0:T(8,128)(2,1)S(1)}, u32[]{:S(2)}, u32[]{:S(2)}) %collective-permute-start.11) | collective-permute-done | bytes 262176 | tf_op jit(solution)/shard_map/ppermute | solution.py:330
  53.2 0.9 copy-done.8
  54.1 1.0 copy-done.17
  55.2 3.5 %shard_map.179 = (bf16[384,512]{1,0:T(8,128)(2,1)S(1)}, bf16[384,512]{1,0:T(8,128)(2,1)S(1)}, bf16[384,2048]{1,0:T(8,128)(2,1)}, f32[1,512]{1,0:T(1,128)S(1)}) custom-call(s32[2]{0:T(128)S(1)} %pad_add_fusion.place, bf16[384,512]{1,0:T(8,128)(2,1)} %refs_0_.5, bf16[384,512]{1,0:T(8,128)(2,1)S(1)} %copy-done.21, ...), custom_call_target="tpu_custom_call" | custom-call | flops 805306368 | bytes 6883328 | tf_op jit(solution)/shard_map/pallas_call | solution.py:121
  58.6 6.6 %collective-permute-start.15 = (bf16[384,512]{1,0:T(8,128)(2,1)S(1)}, bf16[384,512]{1,0:T(8,128)(2,1)S(1)}, u32[]{:S(2)}, u32[]{:S(2)}) collective-permute-start(bf16[384,512]{1,0:T(8,128)(2,1)S(1)} %get-tuple-element.50.refs_0_.refs_1_), channel_id=1, source_target_pairs={{0,4},{4,8},{1,5},{5,9},{2,6},{6,10},{3,7},{7,11},{16,20},{20,24},... | collective-permute-start | bytes 1179656 | tf_op jit(solution)/shard_map/ppermute | solution.py:330
  66.0 6.7 %collective-permute-start.17 = (bf16[384,512]{1,0:T(8,128)(2,1)S(1)}, bf16[384,512]{1,0:T(8,128)(2,1)S(1)}, u32[]{:S(2)}, u32[]{:S(2)}) collective-permute-start(bf16[384,512]{1,0:T(8,128)(2,1)S(1)} %get-tuple-element.50.refs_0_.refs_1_), channel_id=1, source_target_pairs={{0,8},{12,4},{1,9},{13,5},{2,10},{14,6},{3,11},{15,7},{16,24},{28,... | collective-permute-start | bytes 1179656 | tf_op jit(solution)/shard_map/ppermute | solution.py:330
  72.7 2.0 %collective-permute-done.15.refs_1_ = bf16[384,512]{1,0:T(8,128)(2,1)S(1)} collective-permute-done((bf16[384,512]{1,0:T(8,128)(2,1)S(1)}, bf16[384,512]{1,0:T(8,128)(2,1)S(1)}, u32[]{:S(2)}, u32[]{:S(2)}) %collective-permute-start.15) | collective-permute-done | bytes 393248 | tf_op jit(solution)/shard_map/ppermute | solution.py:330
  74.7 7.7 %collective-permute-done.17.refs_3_ = bf16[384,512]{1,0:T(8,128)(2,1)S(1)} collective-permute-done((bf16[384,512]{1,0:T(8,128)(2,1)S(1)}, bf16[384,512]{1,0:T(8,128)(2,1)S(1)}, u32[]{:S(2)}, u32[]{:S(2)}) %collective-permute-start.17) | collective-permute-done | bytes 393248 | tf_op jit(solution)/shard_map/ppermute | solution.py:330
  83.1 0.8 copy-done.31
  84.0 1.0 copy-done.3
  85.0 1.1 copy-done.9
  86.2 3.8 %shard_map.180.refs_0_ = bf16[384,1024]{1,0:T(8,128)(2,1)S(1)} custom-call(s32[2]{0:T(128)S(1)} %pad_add_fusion.place, bf16[384,512]{1,0:T(8,128)(2,1)S(1)} %get-tuple-element.50.refs_0_.refs_1_, bf16[384,512]{1,0:T(8,128)(2,1)S(1)} %collective-permute-done.15.refs_1_, bf16[384,512]{1,0:T(8,128)(2,1)S(1)} %collective-permute-done.16.refs_2_, ...), custom_call_target="tpu_custom_call" | custom-call | flops 1610612736 | bytes 9240576 | tf_op jit(solution)/shard_map/pallas_call | solution.py:121
  90.7 1.3 collective-permute-start.21
  92.0 1.3 collective-permute-start.22
  93.3 27.4 %collective-permute-done.21.refs_2_ = bf16[384,1024]{1,0:T(8,128)(2,1)S(1)} collective-permute-done((bf16[384,1024]{1,0:T(8,128)(2,1)S(1)}, bf16[384,1024]{1,0:T(8,128)(2,1)S(1)}, u32[]{:S(2)}, u32[]{:S(2)}) %collective-permute-start.21) | collective-permute-done | bytes 786464 | tf_op jit(solution)/shard_map/ppermute | solution.py:330
  120.6 18.7 %collective-permute-done.22.refs_3_ = bf16[384,1024]{1,0:T(8,128)(2,1)S(1)} collective-permute-done((bf16[384,1024]{1,0:T(8,128)(2,1)S(1)}, bf16[384,1024]{1,0:T(8,128)(2,1)S(1)}, u32[]{:S(2)}, u32[]{:S(2)}) %collective-permute-start.22) | collective-permute-done | bytes 786464 | tf_op jit(solution)/shard_map/ppermute | solution.py:330
  139.4 1.0 copy-done.11
  140.4 2.9 %shard_map.181 = (bf16[384,512]{1,0:T(8,128)(2,1)S(1)}, f32[1,512]{1,0:T(1,128)S(1)}, f32[1,512]{1,0:T(1,128)S(1)}, bf16[384,2048]{1,0:T(8,128)(2,1)}, bf16[384,512]{1,0:T(8,128)(2,1)}) custom-call(s32[2]{0:T(128)S(1)} %pad_add_fusion.place, bf16[384,1024]{1,0:T(8,128)(2,1)S(1)} %shard_map.180.refs_0_, ...), custom_call_target="tpu_custom_call" | custom-call | flops 805306368 | bytes 8065024 | tf_op jit(solution)/shard_map/pallas_call | solution.py:121
  143.3 2.5 %shard_map.183 = (f32[520,512]{1,0:T(8,128)}, f32[512,512]{1,0:T(8,128)}) custom-call(s32[2]{0:T(128)S(1)} %pad_add_fusion.place, bf16[384,2048]{1,0:T(8,128)(2,1)S(1)} %copy-done, bf16[384,512]{1,0:T(8,128)(2,1)S(1)} %get-tuple-element.55.refs_1_, f32[1,512]{1,0:T(1,128)S(1)} %get-tuple-element.56.refs_2_), custom_call_target="tpu_custom_call" | custom-call | flops 402653184 | bytes 4081664 | tf_op jit(solution)/shard_map/pallas_call | solution.py:121
  145.9 2.2 %shard_map.186 = (f32[520,512]{1,0:T(8,128)}, f32[512,512]{1,0:T(8,128)S(1)}) custom-call(s32[2]{0:T(128)S(1)} %pad_add_fusion.place, bf16[384,2048]{1,0:T(8,128)(2,1)S(1)} %copy-done.1, bf16[384,512]{1,0:T(8,128)(2,1)S(1)} %get-tuple-element.50.refs_0_.refs_1_, f32[1,512]{1,0:T(1,128)S(1)} %get-tuple-element.67.refs_2_), custom_call_target="tpu_custom_call" | custom-call | flops 402653184 | bytes 4081664 | tf_op jit(solution)/shard_map/pallas_call | solution.py:121
  148.1 1.0 copy-done.24
  149.6 1.0 copy-done.19
  150.6 1.3 shard_map.182
  151.9 1.5 shard_map.184
  153.4 1.0 collective-permute-start.26
  154.4 1.3 shard_map.185
  156.0 1.5 shard_map.187
  157.7 1.2 collective-permute-start.29
  159.0 1.0 collective-permute-start.25
  160.0 1.1 collective-permute-start.30
  161.1 22.4 %collective-permute-done.30 = f32[8,512]{1,0:T(8,128)S(1)} collective-permute-done((f32[8,512]{1,0:T(8,128)S(1)}, f32[8,512]{1,0:T(8,128)S(1)}, u32[]{:S(2)}, u32[]{:S(2)}) %collective-permute-start.30) | collective-permute-done | bytes 16416 | tf_op jit(solution)/shard_map/ppermute | solution.py:334
  184.1 3.7 %divide_subtract_fusion.1 = (f32[512,512]{1,0:T(8,128)}, f32[512,512]{1,0:T(8,128)}, f32[512,512]{1,0:T(8,128)}) fusion(f32[512,512]{1,0:T(8,128)S(1)} %copy-done.5, f32[512]{0:T(512)S(1)} %bitcast.15, f16[512,512]{1,0:T(8,128)(2,1)S(1)} %collective-permute-done.25, f32[512,512]{1,0:T(8,128)S(1)} %get-tuple-element.62, ...), kind=kLoop, calls=%fused_computation.7 | loop fusion | flops 4194304 | bytes 8914944 | tf_op jit(solution)/shard_map/sub | solution.py:27
  187.9 2.5 %divide_subtract_fusion = (f32[512,512]{1,0:T(8,128)}, f32[512,512]{1,0:T(8,128)}, f32[512,512]{1,0:T(8,128)}) fusion(f32[512,512]{1,0:T(8,128)S(1)} %copy-done.7, f32[512,512]{1,0:T(8,128)S(1)} %copy-done.28, f32[512,512]{1,0:T(8,128)S(1)} %copy-done.29, f32[512]{0:T(512)S(1)} %bitcast.17, f32[512]{0:T(512)S(1)} %bitcast.16, ...), kind=kLoop, calls=%fused_computation.4 | loop fusion | flops 4980736 | bytes 8916992 | tf_op jit(solution)/shard_map/sub | solution.py:27
  (107 shorter events, 12.1 us)
Async XLA Ops:
  0.6 16.8 %collective-permute-start = (bf16[384,512]{1,0:T(8,128)(2,1)}, bf16[384,512]{1,0:T(8,128)(2,1)S(1)}, u32[]{:S(2)}, u32[]{:S(2)}) collective-permute-start(bf16[384,512]{1,0:T(8,128)(2,1)} %refs_0_.5), channel_id=1, source_target_pairs={{0,4},{4,8},{8,12},{1,5},{5,9},{9,13},{2,6},{6,10},{10,14},{3,7},{... | collective-permute-start | bytes 1179656 | tf_op jit(solution)/shard_map/ppermute | solution.py:330
  5.6 12.8 %collective-permute-start.1 = (bf16[384,512]{1,0:T(8,128)(2,1)}, bf16[384,512]{1,0:T(8,128)(2,1)}, u32[]{:S(2)}, u32[]{:S(2)}) collective-permute-start(bf16[384,512]{1,0:T(8,128)(2,1)} %refs_0_.5), channel_id=1, source_target_pairs={{4,0},{8,4},{12,8},{5,1},{9,5},{13,9},{6,2},{10,6},{14,10},{7,3},{... | collective-permute-start | bytes 1179656 | tf_op jit(solution)/shard_map/ppermute | solution.py:330
  8.9 15.4 %copy-start.6 = (f32[512,512]{1,0:T(8,128)S(1)}, f32[512,512]{1,0:T(8,128)}, u32[]{:S(2)}) copy-start(f32[512,512]{1,0:T(8,128)} %refs_0_.4) | copy-start | bytes 3145732
  9.5 11.0 %copy-start.12 = (bf16[528,512]{1,0:T(8,128)(2,1)}, bf16[528,512]{1,0:T(8,128)(2,1)S(1)}, u32[]{:S(2)}) copy-start(bf16[528,512]{1,0:T(8,128)(2,1)S(1)} %shard_map.177.refs_6_) | copy-start | bytes 1622020
  9.5 9.7 %collective-permute-start.3 = (bf16[528,512]{1,0:T(8,128)(2,1)S(1)}, bf16[528,512]{1,0:T(8,128)(2,1)S(1)}, u32[]{:S(2)}, u32[]{:S(2)}) collective-permute-start(bf16[528,512]{1,0:T(8,128)(2,1)S(1)} %shard_map.177.refs_6_), channel_id=1, source_target_pairs={{0,1},{1,0},{2,3},{3,2},{4,5},{5,4},{6,7},{7,6},{8,9},{9,8},{10,11... | collective-permute-start | bytes 1622024 | tf_op jit(solution)/shard_map/ppermute | solution.py:334
  9.6 14.7 %collective-permute-start.6 = (bf16[528,512]{1,0:T(8,128)(2,1)S(1)}, bf16[528,512]{1,0:T(8,128)(2,1)S(1)}, u32[]{:S(2)}, u32[]{:S(2)}) collective-permute-start(bf16[528,512]{1,0:T(8,128)(2,1)S(1)} %shard_map.177.refs_6_), channel_id=1, source_target_pairs={{0,2},{1,3},{2,0},{3,1},{4,6},{5,7},{6,4},{7,5},{8,10},{9,11},{10,... | collective-permute-start | bytes 1622024 | tf_op jit(solution)/shard_map/ppermute | solution.py:334
  11.1 15.4 %collective-permute-start.2 = (bf16[384,512]{1,0:T(8,128)(2,1)}, bf16[384,512]{1,0:T(8,128)(2,1)}, u32[]{:S(2)}, u32[]{:S(2)}) collective-permute-start(bf16[384,512]{1,0:T(8,128)(2,1)} %refs_0_.5), channel_id=1, source_target_pairs={{0,8},{12,4},{1,9},{13,5},{2,10},{14,6},{3,11},{15,7},{16,24},{28,... | collective-permute-start | bytes 1179656 | tf_op jit(solution)/shard_map/ppermute | solution.py:330
  19.2 5.7 %copy-start.14 = (bf16[528,512]{1,0:T(8,128)(2,1)}, bf16[528,512]{1,0:T(8,128)(2,1)S(1)}, u32[]{:S(2)}) copy-start(bf16[528,512]{1,0:T(8,128)(2,1)S(1)} %collective-permute-done.3.refs_1_.refs_7_) | copy-start | bytes 1622020
  19.2 12.2 %collective-permute-start.4 = (bf16[384,512]{1,0:T(8,128)(2,1)}, bf16[384,512]{1,0:T(8,128)(2,1)}, u32[]{:S(2)}, u32[]{:S(2)}) collective-permute-start(bf16[384,512]{1,0:T(8,128)(2,1)} %broadcast_select_fusion), channel_id=1, source_target_pairs={{4,0},{8,12},{5,1},{9,13},{6,2},{10,14},{7,3},{11,15},{20,16},{24,... | collective-permute-start | bytes 1179656 | tf_op jit(solution)/shard_map/ppermute | solution.py:330
  24.3 24.7 %copy-start.16 = (bf16[528,512]{1,0:T(8,128)(2,1)}, bf16[528,512]{1,0:T(8,128)(2,1)S(1)}, u32[]{:S(2)}) copy-start(bf16[528,512]{1,0:T(8,128)(2,1)S(1)} %collective-permute-done.6.refs_2_.refs_8_) | copy-start | bytes 1622020
  24.9 17.3 %collective-permute-start.9 = (bf16[528,512]{1,0:T(8,128)(2,1)S(1)}, bf16[528,512]{1,0:T(8,128)(2,1)S(1)}, u32[]{:S(2)}, u32[]{:S(2)}) collective-permute-start(bf16[528,512]{1,0:T(8,128)(2,1)S(1)} %shard_map.178.refs_4_.refs_5_), channel_id=1, source_target_pairs={{0,2},{1,3},{2,0},{3,1},{4,6},{5,7},{6,4},{7,5},{8,10},{9,11},{10,... | collective-permute-start | bytes 1622024 | tf_op jit(solution)/shard_map/ppermute | solution.py:334
  31.4 11.1 %collective-permute-start.5 = (bf16[384,512]{1,0:T(8,128)(2,1)}, bf16[384,512]{1,0:T(8,128)(2,1)S(1)}, u32[]{:S(2)}, u32[]{:S(2)}) collective-permute-start(bf16[384,512]{1,0:T(8,128)(2,1)} %collective-permute-done.2.refs_3_), channel_id=1, source_target_pairs={{4,0},{8,12},{5,1},{9,13},{6,2},{10,14},{7,3},{11,15},{20,16},{24,... | collective-permute-start | bytes 1179656 | tf_op jit(solution)/shard_map/ppermute | solution.py:330
  32.8 21.4 %copy-start.13 = (bf16[528,512]{1,0:T(8,128)(2,1)S(1)}, bf16[528,512]{1,0:T(8,128)(2,1)}, u32[]{:S(2)}) copy-start(bf16[528,512]{1,0:T(8,128)(2,1)} %copy-done.12) | copy-start | bytes 1622020
  32.8 21.4 %copy-start.15 = (bf16[528,512]{1,0:T(8,128)(2,1)S(1)}, bf16[528,512]{1,0:T(8,128)(2,1)}, u32[]{:S(2)}) copy-start(bf16[528,512]{1,0:T(8,128)(2,1)} %copy-done.14) | copy-start | bytes 1622020
  32.8 21.3 %copy-start.21 = (bf16[384,512]{1,0:T(8,128)(2,1)S(1)}, bf16[384,512]{1,0:T(8,128)(2,1)}, u32[]{:S(2)}) copy-start(bf16[384,512]{1,0:T(8,128)(2,1)} %copy-done.20) | copy-start | bytes 1179652
  32.8 9.4 %collective-permute-start.10 = (bf16[256,512]{1,0:T(8,128)(2,1)S(1)}, bf16[256,512]{1,0:T(8,128)(2,1)S(1)}, u32[]{:S(2)}, u32[]{:S(2)}) collective-permute-start(bf16[256,512]{1,0:T(8,128)(2,1)S(1)} %get-tuple-element.89), channel_id=1, source_target_pairs={{8,4},{12,8},{9,5},{13,9},{10,6},{14,10},{11,7},{15,11},{24,20},{2... | collective-permute-start | bytes 786440 | tf_op jit(solution)/shard_map/ppermute | solution.py:330
  33.6 11.7 %collective-permute-start.8 = (bf16[256,512]{1,0:T(8,128)(2,1)S(1)}, bf16[256,512]{1,0:T(8,128)(2,1)S(1)}, u32[]{:S(2)}, u32[]{:S(2)}) collective-permute-start(bf16[256,512]{1,0:T(8,128)(2,1)S(1)} %get-tuple-element.88), channel_id=1, source_target_pairs={{0,4},{4,8},{1,5},{5,9},{2,6},{6,10},{3,7},{7,11},{16,20},{20,24},... | collective-permute-start | bytes 786440 | tf_op jit(solution)/shard_map/ppermute | solution.py:330
  38.8 9.3 %collective-permute-start.11 = (bf16[256,512]{1,0:T(8,128)(2,1)S(1)}, bf16[256,512]{1,0:T(8,128)(2,1)S(1)}, u32[]{:S(2)}, u32[]{:S(2)}) collective-permute-start(bf16[256,512]{1,0:T(8,128)(2,1)S(1)} %get-tuple-element.87), channel_id=1, source_target_pairs={{0,8},{12,4},{1,9},{13,5},{2,10},{14,6},{3,11},{15,7},{16,24},{28,... | collective-permute-start | bytes 786440 | tf_op jit(solution)/shard_map/ppermute | solution.py:330
  42.2 40.9 %copy-start.10 = (bf16[528,512]{1,0:T(8,128)(2,1)}, bf16[528,512]{1,0:T(8,128)(2,1)S(1)}, u32[]{:S(2)}) copy-start(bf16[528,512]{1,0:T(8,128)(2,1)S(1)} %collective-permute-done.9.refs_6_.refs_7_) | copy-start | bytes 1622020
  48.2 4.3 %collective-permute-start.12 = (bf16[768,512]{1,0:T(8,128)(2,1)S(1)}, bf16[768,512]{1,0:T(8,128)(2,1)S(1)}, u32[]{:S(2)}, u32[]{:S(2)}) collective-permute-start(bf16[768,512]{1,0:T(8,128)(2,1)S(1)} %constant_dynamic-update-slice_fusion.refs_8_), channel_id=1, source_target_pairs={{4,5},{5,4},{6,7},{7,6},{8,9},{9,8},{10,11},{11,10},{20,21},{21,20... | collective-permute-start | bytes 2359304 | tf_op jit(solution)/shard_map/ppermute | solution.py:334
  48.9 2.0 %collective-permute-start.13 = (bf16[528,512]{1,0:T(8,128)(2,1)S(1)}, bf16[528,512]{1,0:T(8,128)(2,1)S(1)}, u32[]{:S(2)}, u32[]{:S(2)}) collective-permute-start(bf16[528,512]{1,0:T(8,128)(2,1)S(1)} %shard_map.178.refs_4_.refs_5_), channel_id=1, source_target_pairs={{0,1},{1,0},{2,3},{3,2},{4,5},{5,4},{6,7},{7,6},{8,9},{9,8},{10,11... | collective-permute-start | bytes 1622024 | tf_op jit(solution)/shard_map/ppermute | solution.py:334
  49.0 2.7 %collective-permute-start.7 = (bf16[528,512]{1,0:T(8,128)(2,1)S(1)}, bf16[528,512]{1,0:T(8,128)(2,1)S(1)}, u32[]{:S(2)}, u32[]{:S(2)}) collective-permute-start(bf16[528,512]{1,0:T(8,128)(2,1)S(1)} %collective-permute-done.6.refs_2_.refs_8_), channel_id=1, source_target_pairs={{0,1},{1,0},{2,3},{3,2},{4,5},{5,4},{6,7},{7,6},{8,9},{9,8},{10,11... | collective-permute-start | bytes 1622024 | tf_op jit(solution)/shard_map/ppermute | solution.py:334
  49.5 3.0 %collective-permute-start.14 = (bf16[528,512]{1,0:T(8,128)(2,1)S(1)}, bf16[528,512]{1,0:T(8,128)(2,1)S(1)}, u32[]{:S(2)}, u32[]{:S(2)}) collective-permute-start(bf16[528,512]{1,0:T(8,128)(2,1)S(1)} %collective-permute-done.9.refs_6_.refs_7_), channel_id=1, source_target_pairs={{0,1},{1,0},{2,3},{3,2},{4,5},{5,4},{6,7},{7,6},{8,9},{9,8},{10,11... | collective-permute-start | bytes 1622024 | tf_op jit(solution)/shard_map/ppermute | solution.py:334
  49.6 23.1 %collective-permute-start.18 = (bf16[768,512]{1,0:T(8,128)(2,1)S(1)}, bf16[768,512]{1,0:T(8,128)(2,1)S(1)}, u32[]{:S(2)}, u32[]{:S(2)}) collective-permute-start(bf16[768,512]{1,0:T(8,128)(2,1)S(1)} %constant_dynamic-update-slice_fusion.refs_8_), channel_id=1, source_target_pairs={{4,6},{5,7},{6,4},{7,5},{8,10},{9,11},{10,8},{11,9},{20,22},{21,23... | collective-permute-start | bytes 2359304 | tf_op jit(solution)/shard_map/ppermute | solution.py:334
  58.6 16.1 %collective-permute-start.15 = (bf16[384,512]{1,0:T(8,128)(2,1)S(1)}, bf16[384,512]{1,0:T(8,128)(2,1)S(1)}, u32[]{:S(2)}, u32[]{:S(2)}) collective-permute-start(bf16[384,512]{1,0:T(8,128)(2,1)S(1)} %get-tuple-element.50.refs_0_.refs_1_), channel_id=1, source_target_pairs={{0,4},{4,8},{1,5},{5,9},{2,6},{6,10},{3,7},{7,11},{16,20},{20,24},... | collective-permute-start | bytes 1179656 | tf_op jit(solution)/shard_map/ppermute | solution.py:330
  65.3 9.4 %collective-permute-start.16 = (bf16[384,512]{1,0:T(8,128)(2,1)S(1)}, bf16[384,512]{1,0:T(8,128)(2,1)S(1)}, u32[]{:S(2)}, u32[]{:S(2)}) collective-permute-start(bf16[384,512]{1,0:T(8,128)(2,1)S(1)} %get-tuple-element.50.refs_0_.refs_1_), channel_id=1, source_target_pairs={{8,4},{12,8},{9,5},{13,9},{10,6},{14,10},{11,7},{15,11},{24,20},{2... | collective-permute-start | bytes 1179656 | tf_op jit(solution)/shard_map/ppermute | solution.py:330
  66.0 16.4 %collective-permute-start.17 = (bf16[384,512]{1,0:T(8,128)(2,1)S(1)}, bf16[384,512]{1,0:T(8,128)(2,1)S(1)}, u32[]{:S(2)}, u32[]{:S(2)}) collective-permute-start(bf16[384,512]{1,0:T(8,128)(2,1)S(1)} %get-tuple-element.50.refs_0_.refs_1_), channel_id=1, source_target_pairs={{0,8},{12,4},{1,9},{13,5},{2,10},{14,6},{3,11},{15,7},{16,24},{28,... | collective-permute-start | bytes 1179656 | tf_op jit(solution)/shard_map/ppermute | solution.py:330
  72.7 10.4 %copy-start.30 = (bf16[768,512]{1,0:T(8,128)(2,1)}, bf16[768,512]{1,0:T(8,128)(2,1)S(1)}, u32[]{:S(2)}) copy-start(bf16[768,512]{1,0:T(8,128)(2,1)S(1)} %collective-permute-done.18.refs_10_) | copy-start | bytes 2359300
  82.4 0.7 collective-permute-start.19
  90.0 2.0 %collective-permute-start.20 = (bf16[384,1024]{1,0:T(8,128)(2,1)S(1)}, bf16[384,1024]{1,0:T(8,128)(2,1)S(1)}, u32[]{:S(2)}, u32[]{:S(2)}) collective-permute-start(bf16[384,1024]{1,0:T(8,128)(2,1)S(1)} %shard_map.180.refs_0_), channel_id=1, source_target_pairs={{4,8},{8,4},{5,9},{9,5},{6,10},{10,6},{7,11},{11,7},{20,24},{24,20... | collective-permute-start | bytes 2359304 | tf_op jit(solution)/shard_map/ppermute | solution.py:330
  90.7 30.0 %collective-permute-start.21 = (bf16[384,1024]{1,0:T(8,128)(2,1)S(1)}, bf16[384,1024]{1,0:T(8,128)(2,1)S(1)}, u32[]{:S(2)}, u32[]{:S(2)}) collective-permute-start(bf16[384,1024]{1,0:T(8,128)(2,1)S(1)} %shard_map.180.refs_0_), channel_id=1, source_target_pairs={{4,0},{8,12},{5,1},{9,13},{6,2},{10,14},{7,3},{11,15},{20,16},{24,... | collective-permute-start | bytes 2359304 | tf_op jit(solution)/shard_map/ppermute | solution.py:330
  92.0 47.4 %collective-permute-start.22 = (bf16[384,1024]{1,0:T(8,128)(2,1)S(1)}, bf16[384,1024]{1,0:T(8,128)(2,1)S(1)}, u32[]{:S(2)}, u32[]{:S(2)}) collective-permute-start(bf16[384,1024]{1,0:T(8,128)(2,1)S(1)} %collective-permute-done.20.refs_1_), channel_id=1, source_target_pairs={{4,0},{8,12},{5,1},{9,13},{6,2},{10,14},{7,3},{11,15},{20,16},{24,... | collective-permute-start | bytes 2359304 | tf_op jit(solution)/shard_map/ppermute | solution.py:330
  143.3 4.8 %copy-start.18 = (bf16[384,512]{1,0:T(8,128)(2,1)}, bf16[384,512]{1,0:T(8,128)(2,1)S(1)}, u32[]{:S(2)}) copy-start(bf16[384,512]{1,0:T(8,128)(2,1)S(1)} %get-tuple-element.55.refs_1_) | copy-start | bytes 1179652
  145.9 6.0 %collective-permute-start.23 = (f32[520,512]{1,0:T(8,128)}, f32[520,512]{1,0:T(8,128)}, u32[]{:S(2)}, u32[]{:S(2)}) collective-permute-start(f32[520,512]{1,0:T(8,128)} %get-tuple-element.58), channel_id=1, source_target_pairs={{0,1},{1,0},{2,3},{3,2},{4,5},{5,4},{6,7},{7,6},{8,9},{9,8},{10,11... | collective-permute-start | bytes 3194888 | tf_op jit(solution)/shard_map/ppermute | solution.py:334
  149.1 6.9 %collective-permute-start.27 = (f32[520,512]{1,0:T(8,128)}, f32[520,512]{1,0:T(8,128)}, u32[]{:S(2)}, u32[]{:S(2)}) collective-permute-start(f32[520,512]{1,0:T(8,128)} %get-tuple-element.69), channel_id=1, source_target_pairs={{0,1},{1,0},{2,3},{3,2},{4,5},{5,4},{6,7},{7,6},{8,9},{9,8},{10,11... | collective-permute-start | bytes 3194888 | tf_op jit(solution)/shard_map/ppermute | solution.py:334
  149.6 34.5 %collective-permute-start.24 = (f32[512,512]{1,0:T(8,128)}, f32[512,512]{1,0:T(8,128)}, u32[]{:S(2)}, u32[]{:S(2)}) collective-permute-start(f32[512,512]{1,0:T(8,128)} %get-tuple-element.63), channel_id=1, source_target_pairs={{0,1},{1,0},{2,3},{3,2},{4,5},{5,4},{6,7},{7,6},{8,9},{9,8},{10,11... | collective-permute-start | bytes 3145736 | tf_op jit(solution)/shard_map/ppermute | solution.py:334
  153.4 6.6 %collective-permute-start.26 = (f32[8,512]{1,0:T(8,128)S(1)}, f32[8,512]{1,0:T(8,128)S(1)}, u32[]{:S(2)}, u32[]{:S(2)}) collective-permute-start(f32[8,512]{1,0:T(8,128)S(1)} %get-tuple-element.64), channel_id=1, source_target_pairs={{0,2},{1,3},{2,0},{3,1},{4,6},{5,7},{6,4},{7,5},{8,10},{9,11},{10,... | collective-permute-start | bytes 49160 | tf_op jit(solution)/shard_map/ppermute | solution.py:334
  155.7 32.1 %collective-permute-start.28 = (f32[512,512]{1,0:T(8,128)S(1)}, f32[512,512]{1,0:T(8,128)S(1)}, u32[]{:S(2)}, u32[]{:S(2)}) collective-permute-start(f32[512,512]{1,0:T(8,128)S(1)} %copy-done.25), channel_id=1, source_target_pairs={{0,1},{1,0},{2,3},{3,2},{4,5},{5,4},{6,7},{7,6},{8,9},{9,8},{10,11... | collective-permute-start | bytes 3145736 | tf_op jit(solution)/shard_map/ppermute | solution.py:334
  157.5 26.5 %copy-start.26 = (f32[512,512]{1,0:T(8,128)S(1)}, f32[512,512]{1,0:T(8,128)}, u32[]{:S(2)}) copy-start(f32[512,512]{1,0:T(8,128)} %param.14) | copy-start | bytes 3145732
  157.6 26.5 %copy-start.27 = (f32[512,512]{1,0:T(8,128)S(1)}, f32[512,512]{1,0:T(8,128)}, u32[]{:S(2)}) copy-start(f32[512,512]{1,0:T(8,128)} %param.15) | copy-start | bytes 3145732
  157.7 25.8 %copy-start.23 = (f32[128]{0:T(128)S(1)}, f32[128]{0:T(128)}, u32[]{:S(2)}) copy-start(f32[128]{0:T(128)} %param.12) | copy-start | bytes 1540
  157.7 25.8 %copy-start.32 = (f32[128]{0:T(128)S(1)}, f32[128]{0:T(128)}, u32[]{:S(2)}) copy-start(f32[128]{0:T(128)} %param.16) | copy-start | bytes 1540
  157.7 25.8 %copy-start.33 = (f32[128]{0:T(128)S(1)}, f32[128]{0:T(128)}, u32[]{:S(2)}) copy-start(f32[128]{0:T(128)} %param.17) | copy-start | bytes 1540
  157.7 26.4 %copy-start.5 = (f32[512,512]{1,0:T(8,128)S(1)}, f32[512,512]{1,0:T(8,128)}, u32[]{:S(2)}) copy-start(f32[512,512]{1,0:T(8,128)} %refs_0_.3) | copy-start | bytes 3145732
  157.7 30.1 %collective-permute-start.29 = (f16[512,512]{1,0:T(8,128)(2,1)S(1)}, f16[512,512]{1,0:T(8,128)(2,1)S(1)}, u32[]{:S(2)}, u32[]{:S(2)}) collective-permute-start(f16[512,512]{1,0:T(8,128)(2,1)S(1)} %convert_element_type.14), channel_id=1, source_target_pairs={{0,2},{1,3},{2,0},{3,1},{4,6},{5,7},{6,4},{7,5},{8,10},{9,11},{10,... | collective-permute-start | bytes 1572872 | tf_op jit(solution)/shard_map/ppermute | solution.py:334
  159.0 25.1 %collective-permute-start.25 = (f16[512,512]{1,0:T(8,128)(2,1)S(1)}, f16[512,512]{1,0:T(8,128)(2,1)S(1)}, u32[]{:S(2)}, u32[]{:S(2)}) collective-permute-start(f16[512,512]{1,0:T(8,128)(2,1)S(1)} %convert_element_type.12), channel_id=1, source_target_pairs={{0,2},{1,3},{2,0},{3,1},{4,6},{5,7},{6,4},{7,5},{8,10},{9,11},{10,... | collective-permute-start | bytes 1572872 | tf_op jit(solution)/shard_map/ppermute | solution.py:334
  160.0 23.5 %collective-permute-start.30 = (f32[8,512]{1,0:T(8,128)S(1)}, f32[8,512]{1,0:T(8,128)S(1)}, u32[]{:S(2)}, u32[]{:S(2)}) collective-permute-start(f32[8,512]{1,0:T(8,128)S(1)} %get-tuple-element.75), channel_id=1, source_target_pairs={{0,2},{1,3},{2,0},{3,1},{4,6},{5,7},{6,4},{7,5},{8,10},{9,11},{10,... | collective-permute-start | bytes 49160 | tf_op jit(solution)/shard_map/ppermute | solution.py:334
  184.1 3.7 %copy-start.7 = (f32[512,512]{1,0:T(8,128)S(1)}, f32[512,512]{1,0:T(8,128)}, u32[]{:S(2)}) copy-start(f32[512,512]{1,0:T(8,128)} %refs_0_.4) | copy-start | bytes 3145732
  (17 other events, 29.0 us)

commit v4 on v3

--- a/solution.py
+++ b/solution.py
@@ -111,10 +111,7 @@
 EXTRA = 16
 
 
-def local_kernel(body, outs, place, *args, flops=0, after=(), scratch=()):
-    moved = sum(a.size * a.dtype.itemsize for a in args)
-    moved += sum(o.size * jnp.dtype(o.dtype).itemsize for o in outs)
-
+def local_kernel(body, outs, place, *args, after=(), scratch=()):
     def run(place, *refs):
         body(place, *refs[: len(args)], *refs[len(args) + len(after) :])
 
@@ -124,8 +121,8 @@
         in_specs=[SMEM] + [VMEM] * len(args) + [ANY] * len(after),
         out_specs=[VMEM] * len(outs),
         scratch_shapes=scratch,
-        compiler_params=pltpu.CompilerParams(vmem_limit_bytes=48 * 1024 * 1024),
-        cost_estimate=pl.CostEstimate(flops=flops, bytes_accessed=moved, transcendentals=0),
+        compiler_params=pltpu.CompilerParams(vmem_limit_bytes=24 * 1024 * 1024),
+        cost_estimate=pl.CostEstimate(flops=1, bytes_accessed=1, transcendentals=0),
     )(place, *args, *after)
 
 
@@ -168,39 +165,12 @@
 
 
 def codes_body(
-    place,
-    own,
-    low,
-    high,
-    across,
-    relay1,
-    relay2,
-    enc0,
-    enc1,
-    enc2,
-    enc3,
-    codes,
-    mask,
-    full,
-    active,
-    bias,
+    place, own, one, two, three, enc0, enc1, enc2, enc3, codes, mask, full, active, bias
 ):
     z, i = place[0], place[1]
     width = own.shape[1]
-    for at, blocks in enumerate(
-        (
-            (own, high, relay1, relay2),
-            (low, own, high, across),
-            (across, low, own, high),
-            (relay2, relay1, low, own),
-        )
-    ):
-
-        @pl.when(z == at)
-        def _(blocks=blocks):
-            for b, block in enumerate(blocks):
-                full[:, b * width : (b + 1) * width] = block[...]
-
+    for k, block in enumerate((own, one, two, three)):
+        full[:, columns((z ^ k) * width, width)] = block[...]
     total = jnp.zeros(codes.shape, F32)
     piece = codes.shape[1] // 4
     for t, enc in enumerate((enc0, enc1, enc2, enc3)):
@@ -214,6 +184,10 @@
     codes[...] = low_codes
     mask[...] = (preact > 0.0).astype(F32).astype(BF16)
     active[...] = jnp.sum(low_codes.astype(F32), axis=0, keepdims=True)
+
+
+def turn_body(place, full, turned):
+    turned[...] = full[...].T
 
 
 def error_body(
@@ -236,74 +210,101 @@
         error[:, columns(q * half, half)] = (given - total).astype(BF16)
 
 
-def grad_code_body(
-    rows,
-    place,
-    mine,
-    swapped,
-    passed,
-    relayed,
-    mask,
-    dec0,
-    dec1,
-    dec2,
-    dec3,
-    grad_low,
-    bias_sum,
-    norms,
-    full,
-    home,
+def pick(place, middle, end, out):
+    z = place[0]
+    is_middle = (z == 1) | (z == 2)
+
+    @pl.when(is_middle)
+    def _():
+        out[...] = middle[...]
+
+    @pl.when(jnp.logical_not(is_middle))
+    def _():
+        out[...] = end[...]
+
+
+def decoder_grads(scale, i, error, codes, row, send, keep):
+    half = error.shape[1] // 4
+    for out, slots in ((send, (3, 1)), (keep, (2, 0))):
+        for at, slot in enumerate(slots):
+            out[at * half : (at + 1) * half] = scale * lax.dot_general(
+                error[:, columns((i ^ slot) * half, half)],
+                codes[...],
+                (((0,), (0,)), ((), ())),
+                preferred_element_type=F32,
+            )
+    send[2 * half :] = jnp.broadcast_to(row[...], (send.shape[0] - 2 * half, row.shape[1]))
+
+
+def back_through(i, error, decs, shift):
+    half = error.shape[1] // 4
+    return functools.reduce(
+        jnp.add,
+        [
+            jnp.dot(
+                error[:, columns((i ^ t) * half, half)],
+                dec[pl.ds(pl.multiple_of(shift, half), half), :],
+                preferred_element_type=F32,
+            )
+            for t, dec in enumerate(decs)
+        ],
+    )
+
+
+def near_body(
+    rows, place, mine, passed, codes, active, dec0, dec1, dec2, dec3, part, send, keep, near
 ):
     z, i = place[0], place[1]
     half = mine.shape[1] // 4
+    pick(place, mine, passed, near)
+    decoder_grads(-2.0 / rows, i, near, codes, active, send, keep)
+    part[...] = back_through(i, near, (dec0, dec1, dec2, dec3), jnp.where(z >= 2, half, 0))
+
+
+def far_error_body(rows, place, swapped, direct, codes, active, send, keep, far):
+    pick(place, swapped, direct, far)
+    decoder_grads(-2.0 / rows, place[1], far, codes, active, send, keep)
+
+
+def far_code_body(
+    rows, place, near, far, part, mask, dec0, dec1, dec2, dec3, grad_low, bias_sum, norms, home
+):
+    z, i = place[0], place[1]
+    half = far.shape[1] // 4
     width = 2 * half
-    for at, (near, far) in enumerate(
-        ((passed, relayed), (mine, swapped), (swapped, mine), (relayed, passed))
-    ):
-
-        @pl.when(z == at)
-        def _(near=near, far=far):
-            for q in range(4):
-                full[:, q * width : q * width + half] = near[:, q * half : (q + 1) * half]
-                full[:, q * width + half : (q + 1) * width] = far[:, q * half : (q + 1) * half]
-
-    total = jnp.zeros(grad_low.shape, F32)
-    squares = jnp.zeros(bias_sum.shape, F32)
-    for t, dec in enumerate((dec0, dec1, dec2, dec3)):
-        total += jnp.dot(
-            full[:, columns((i ^ t) * width, width)], dec[:width, :], preferred_element_type=F32
-        )
-        squares += one_row(dec[width:, :])
+    decs = (dec0, dec1, dec2, dec3)
+    shift = jnp.where(z >= 2, 0, half)
+    total = part[...] + back_through(i, far, decs, shift)
+    squares = functools.reduce(jnp.add, [one_row(dec[width:, :]) for dec in decs])
     column_norms = jnp.sqrt(squares + 1e-06)
     norms[...] = column_norms
     code_grad = (-2.0 / rows) * total + column_norms / rows
     grad = jnp.where(mask[...] > 0, code_grad, 0.0)
     grad_low[...] = grad.astype(BF16)
     bias_sum[...] = jnp.sum(grad, axis=0, keepdims=True)
-    home[...] = full[:, columns(z * width, width)]
-
-
-def grad_body(scale, slots, place, left, right, row, *outs):
+    home[:, columns(half - shift, half)] = near[:, columns(z * half, half)]
+    home[:, columns(shift, half)] = far[:, columns(z * half, half)]
+
+
+def encoder_grad_body(place, turned, grad_low, row, send_far, send_near, keep_far, keep_near):
     i = place[1]
-    width = left.shape[1] // 4
-    for slot, out in zip(slots, outs):
-        out[:width] = scale * lax.dot_general(
-            left[:, columns((i ^ slot) * width, width)],
-            right[...],
-            (((0,), (0,)), ((), ())),
-            preferred_element_type=F32,
-        )
-    outs[0][width:] = jnp.broadcast_to(row[...], (outs[0].shape[0] - width, row.shape[1]))
-
-
-def far_body(place, kept, received, scaled, small):
+    width = turned.shape[0] // 4
+    for slot, out in ((3, send_far), (1, send_near), (2, keep_far), (0, keep_near)):
+        at = pl.ds(pl.multiple_of((i ^ slot) * width, width), width)
+        out[:width] = jnp.dot(turned[at, :], grad_low[...], preferred_element_type=F32)
+    send_far[width:] = jnp.broadcast_to(row[...], (send_far.shape[0] - width, row.shape[1]))
+
+
+def far_body(place, kept, received, row, scaled, small, *near):
     width = scaled.shape[0]
     total = kept[:width] + received[:width]
     largest = jnp.maximum(jnp.max(jnp.abs(total), axis=0, keepdims=True), 1e-30)
     scaled[...] = total * (16384.0 / largest)
-    row = kept[width:] + received[width:]
-    at = lax.broadcasted_iota(jnp.int32, row.shape, 0)
-    small[...] = jnp.where(at == 0, largest * (1.0 / 16384.0), row)
+    rows = received[received.shape[0] - small.shape[0] :] + row[...]
+    at = lax.broadcasted_iota(jnp.int32, rows.shape, 0)
+    small[...] = jnp.where(at == 0, largest * (1.0 / 16384.0), rows)
+    for out in near:
+        out[...] = kept[width:] + received[width : kept.shape[0]]
 
 
 def line_shards(
@@ -333,9 +334,7 @@
         pairs = [(4 * p + k, 4 * p + (k ^ bits)) for p in planes for k in range(4)]
         return lax.ppermute(value, ("latent", "dp"), pairs)
 
-    low = along(activations, [(0, 1), (1, 2), (2, 3)])
-    high = along(activations, [(1, 0), (2, 1), (3, 2)])
-    across = along(activations, [(0, 2), (3, 1)])
+    one, two, three = [along(activations, [(k, k ^ d) for k in range(4)]) for d in (1, 2, 3)]
 
     (enc_own,) = local_kernel(
         encoder_body,
@@ -350,26 +349,20 @@
         [shape((width + EXTRA, latents), BF16)],
         place,
         decoder,
-        after=(enc_core, enc_chip),
-    )
-    dec_chip, dec_core = flip(dec_own, 2), flip(dec_own, 1)
-    relay1 = along(behind(jnp.where(z == 1, high, low), enc_core), [(1, 0), (2, 3)])
-    relay2 = along(behind(across, relay1), [(1, 0), (2, 3)])
-    enc = [enc_own, enc_core, enc_chip, flip(enc_chip, 1)]
-
-    dec_late = behind(dec_own, across)
+        after=(enc_core,),
+    )
+    dec_chip, dec_core = flip(behind(dec_own, enc_chip), 2), flip(dec_own, 1)
+    enc = [enc_own, enc_core, enc_chip, flip(behind(enc_chip, one, two), 1)]
+
+    dec_late = behind(dec_own, one, two)
     first, second = dec_late[:half], dec_late[half:width]
     dec_pieces = [
         along(jnp.where(z >= 1, second, first), [(0, 1), (1, 2)]),
         along(jnp.where(z >= 3, second, first), [(2, 1), (3, 2)]),
         along(jnp.where(z >= 2, first, second), [(0, 2), (3, 1)]),
     ]
-    dec_pieces = [behind(piece, dec_chip, relay2) for piece in dec_pieces]
-    rows_own = jnp.concatenate(dec_pieces, axis=0)
     dec = [dec_own, dec_core, dec_chip, flip(dec_chip, 1)]
-    rows_chip, rows_core = flip(rows_own, 2, (1, 2)), flip(rows_own, 1, (1, 2))
-
-    flops = 2 * count * features * latents
+
     codes, mask, inputs, active = local_kernel(
         codes_body,
         [
@@ -380,20 +373,23 @@
         ],
         place,
         activations,
-        low,
-        high,
-        across,
-        relay1,
-        relay2,
+        one,
+        two,
+        three,
         *enc,
-        flops=flops,
-        after=(rows_core, dec[1], dec[3]),
         scratch=[pltpu.VMEM((1, latents), F32)],
     )
     codes_low = along(codes, [(0, 1), (1, 2)])
     codes_high = along(codes, [(2, 1), (3, 2)])
     codes_across = along(codes, [(0, 2), (3, 1)])
-    rows_both = flip(behind(rows_chip, codes_low, codes_high, codes_across), 1, (1, 2))
+    dec_pieces = [behind(piece, codes, dec_chip) for piece in dec_pieces]
+    rows_own = jnp.concatenate(dec_pieces, axis=0)
+    (turned,) = local_kernel(turn_body, [shape((features, count), BF16)], place, inputs)
+    rows_chip = flip(rows_own, 2, (1, 2))
+    rows_core = flip(behind(rows_own, turned), 1, (1, 2))
+    rows_both = flip(
+        behind(rows_chip, codes_low, codes_high, codes_across, dec[1], dec[3]), 1, (1, 2)
+    )
 
     (own_error,) = local_kernel(
         error_body,
@@ -409,67 +405,102 @@
         rows_chip,
         rows_both,
         inputs,
-        flops=2 * flops,
     )
     swapped = along(own_error, [(1, 2), (2, 1)])
     passed = along(own_error, [(1, 0), (2, 3)])
-    relayed = along(swapped, [(1, 0), (2, 3)])
-
-    grad_low, bias_sum, norms, full_error, error = local_kernel(
-        functools.partial(grad_code_body, rows),
+    direct = along(own_error, [(2, 0), (1, 3)])
+
+    def across_chips(scaled, small):
+        sent = scaled.astype(jnp.float16)
+        received, small_received = flip(sent, 2), flip(small, 2)
+        block = received.astype(F32) * small_received[:1]
+        return received, block, small[1] + small_received[1]
+
+    def decoder_half(send, keep, row):
+        scaled, small, near = local_kernel(
+            far_body,
+            [shape((half, latents), F32), shape((8, latents), F32), shape((half, latents), F32)],
+            place,
+            keep,
+            flip(send, 1),
+            row,
+        )
+        received, block, row = across_chips(scaled, small)
+        return scaled, received, near + block, row
+
+    blocks = [shape((width + 8, latents), F32), shape((width, latents), F32)]
+    part, send, keep, near = local_kernel(
+        functools.partial(near_body, rows),
+        [shape((count, latents), F32), *blocks, shape((count, features // 2), BF16)],
+        place,
+        own_error,
+        passed,
+        codes,
+        active,
+        *dec,
+        after=(swapped,),
+    )
+    near_scaled, near_received, near_grad, active_sum = decoder_half(send, keep, active)
+    send, keep, far = local_kernel(
+        functools.partial(far_error_body, rows),
+        [*blocks, shape((count, features // 2), BF16)],
+        place,
+        swapped,
+        direct,
+        codes,
+        active,
+        after=(near_scaled,),
+    )
+    _, _, far_grad, _ = decoder_half(send, keep, active)
+    grad_low, bias_sum, norms, error = local_kernel(
+        functools.partial(far_code_body, rows),
         [
             shape((count, latents), BF16),
             shape((1, latents), F32),
             shape((1, latents), F32),
-            shape((count, features), BF16),
             shape((count, width), BF16),
         ],
         place,
-        own_error,
-        swapped,
-        passed,
-        relayed,
+        near,
+        far,
+        behind(part, near_received),
         mask,
         *dec,
-        flops=flops,
-    )
-
-    def reduced(scale, left, right, row):
-        def slots(*which):
-            return local_kernel(
-                functools.partial(grad_body, scale, which),
-                [shape((width + 8, latents), F32), shape((width, latents), F32)],
-                place,
-                left,
-                right,
-                row,
-                flops=flops // 2,
-            )
-
-        send_far, send_near = slots(3, 1)
-        keep_far, keep_near = slots(2, 0)
-        scaled, small = local_kernel(
-            far_body,
-            [shape((width, latents), F32), shape((8, latents), F32)],
-            place,
-            keep_far,
-            flip(send_far, 1),
-        )
-        sent = scaled.astype(jnp.float16)
-        received, small_received = flip(sent, 2), flip(small, 2)
-        near = keep_near + flip(send_near, 1)
-        block = near + received.astype(F32) * small_received[:1]
-        return block, small[1] + small_received[1], sent
-
-    grad_dec_rows, active_sum, dec_sent = reduced(-2.0 / rows, full_error, codes, active)
-    grad_encoder, grad_bias, enc_sent = reduced(1.0, inputs, grad_low, bias_sum)
+    )
+    send_far, send_near, keep_far, keep_near = local_kernel(
+        encoder_grad_body,
+        [shape((width + 8, latents), F32)] + [shape((width, latents), F32)] * 3,
+        place,
+        turned,
+        grad_low,
+        bias_sum,
+    )
+    scaled, small = local_kernel(
+        far_body,
+        [shape((width, latents), F32), shape((8, latents), F32)],
+        place,
+        keep_far,
+        flip(send_far, 1),
+        bias_sum,
+    )
+    _, block, grad_bias = across_chips(scaled, small)
+    grad_encoder = keep_near + flip(send_near, 1) + block
     grad_bias = lax.dynamic_slice(grad_bias, (i * enc_bias.shape[0],), (enc_bias.shape[0],))
+
     decoder, dec_moment, dec_square = lax.optimization_barrier(
-        (decoder, dec_moment, dec_square, dec_sent)
+        (decoder, dec_moment, dec_square, small)
     )[:3]
     encoder, enc_moment, enc_square = lax.optimization_barrier(
-        (encoder, enc_moment, enc_square, enc_sent)
+        (encoder, enc_moment, enc_square, small)
     )[:3]
+    low_first = z < 2
+    grad_dec_rows = jnp.concatenate(
+        [
+            jnp.where(low_first, near_grad, far_grad),
+            jnp.where(low_first, far_grad, near_grad),
+        ],
+        axis=0,
+    )
     grad_decoder = grad_dec_rows + decoder * (active_sum / norms) / rows
 
     new_decoder, new_dec_moment, new_dec_square = adam_update(

time: 191 us -> 177 us (0.927)
  starting transfers between devices: 52.8 us -> 47.3 us
  local copies, waits for them, and re-layouts: 10.8 us -> 6.19 us
  Pallas kernels: 21.8 us -> 17.6 us
    ppermute x14 -> x12, waiting for transfers between devices: 67.5 us -> 82.3 us  [along(): return lax.ppermute(value, 'latent', pairs)]
    ppermute x17 -> x19, waiting for transfers between devices: 28.3 us -> 14.9 us  [flip(): return lax.ppermute(value, ('latent', 'dp'), pairs)]
    ppermute x14 -> x12, starting transfers between devices: 41.8 us -> 35.4 us  [along(): return lax.ppermute(value, 'latent', pairs)]
    unnamed x70 -> x46, local copies, waits for them, and re-layouts: 10.8 us -> 6.16 us
    pallas_call x11 -> x12, Pallas kernels: 21.8 us -> 17.6 us  [local_kernel(): pl.pallas_call(run, out_shape=outs, in_specs=[SMEM] + [VMEM] * len(args)...]
    ppermute x17 -> x19, starting transfers between devices: 11 us -> 11.8 us  [flip(): return lax.ppermute(value, ('latent', 'dp'), pairs)]
  transfers between devices with their start and end apart: 31 -> 31, of which waited for: 14 -> 12; matrix products, arithmetic and copies ran while one was open for 3% -> 3% of each run, Pallas kernels for 7% -> 7%
where the time goes in v4:
time: 177 us
  waiting for transfers between devices  97.2 us (55%)
  starting transfers between devices  47.3 us (27%)
  Pallas kernels  17.6 us (10%)
  other arithmetic  7.49 us (4%)
  local copies, waits for them, and re-layouts  6.19 us (3%)
    ppermute x12, waiting for transfers between devices, along(): return lax.ppermute(value, 'latent', pairs)  82.3 us
    ppermute x12, starting transfers between devices, along(): return lax.ppermute(value, 'latent', pairs)  35.4 us
    pallas_call x12, Pallas kernels, local_kernel(): pl.pallas_call(run, out_shape=outs, in_specs=[SMEM] + [VMEM] * len(args)...  17.6 us
    ppermute x19, waiting for transfers between devices, flip(): return lax.ppermute(value, ('latent', 'dp'), pairs)  14.9 us
    ppermute x19, starting transfers between devices, flip(): return lax.ppermute(value, ('latent', 'dp'), pairs)  11.8 us
    unnamed x46, local copies, waits for them, and re-layouts  6.16 us
    sub x3, other arithmetic, adam_update(): param - learn_rate * (moment_new / first_fix) / (jnp.sqrt(square_new / se...  5.11 us
  transfers between devices with their start and end apart: 31, of which 12 were waited for; matrix products, arithmetic and copies ran while one was open for 3% of the time, Pallas kernels for 7%

profile of v4, /device:TPU:0, one launch (start us, length us, event | category | flops | bytes accessed | tf_op | source)
XLA Modules:
  0.0 176.9 jit_solution(14425507985884608220)
XLA Ops:
  0.7 1.2 copy-done
  3.2 3.0 %collective-permute-start.4 = (bf16[528,512]{1,0:T(8,128)(2,1)S(1)}, bf16[528,512]{1,0:T(8,128)(2,1)}, u32[]{:S(2)}, u32[]{:S(2)}) collective-permute-start(bf16[528,512]{1,0:T(8,128)(2,1)S(1)} %shard_map.177.refs_4_), channel_id=1, source_target_pairs={{0,2},{1,3},{2,0},{3,1},{4,6},{5,7},{6,4},{7,5},{8,10},{9,11},{10,... | collective-permute-start | bytes 1622024 | tf_op jit(solution)/shard_map/ppermute | solution.py:335
  6.2 1.6 collective-permute-start
  7.8 2.6 %collective-permute-start.1 = (bf16[384,512]{1,0:T(8,128)(2,1)}, bf16[384,512]{1,0:T(8,128)(2,1)S(1)}, u32[]{:S(2)}, u32[]{:S(2)}) collective-permute-start(bf16[384,512]{1,0:T(8,128)(2,1)} %refs_0_.4), channel_id=1, source_target_pairs={{0,8},{4,12},{8,0},{12,4},{1,9},{5,13},{9,1},{13,5},{2,10},{6,14},... | collective-permute-start | bytes 1179656 | tf_op jit(solution)/shard_map/ppermute | solution.py:331
  10.4 15.9 %collective-permute-done.refs_1_ = bf16[384,512]{1,0:T(8,128)(2,1)S(1)} collective-permute-done((bf16[384,512]{1,0:T(8,128)(2,1)}, bf16[384,512]{1,0:T(8,128)(2,1)S(1)}, u32[]{:S(2)}, u32[]{:S(2)}) %collective-permute-start) | collective-permute-done | bytes 393248 | tf_op jit(solution)/shard_map/ppermute | solution.py:331
  26.3 0.7 copy-done.9
  27.0 1.6 collective-permute-done.1.refs_2_
  28.6 0.7 copy-done.11
  30.7 2.5 %collective-permute-start.2 = (bf16[384,512]{1,0:T(8,128)(2,1)}, bf16[384,512]{1,0:T(8,128)(2,1)}, u32[]{:S(2)}, u32[]{:S(2)}) collective-permute-start(bf16[384,512]{1,0:T(8,128)(2,1)} %refs_0_.4), channel_id=1, source_target_pairs={{0,12},{4,8},{8,4},{12,0},{1,13},{5,9},{9,5},{13,1},{2,14},{6,10},... | collective-permute-start | bytes 1179656 | tf_op jit(solution)/shard_map/ppermute | solution.py:331
  33.2 0.8 collective-permute-start.13
  34.0 1.3 collective-permute-start.12
  35.3 9.5 %collective-permute-done.2.refs_3_ = bf16[384,512]{1,0:T(8,128)(2,1)} collective-permute-done((bf16[384,512]{1,0:T(8,128)(2,1)}, bf16[384,512]{1,0:T(8,128)(2,1)}, u32[]{:S(2)}, u32[]{:S(2)}) %collective-permute-start.2) | collective-permute-done | bytes 393248 | tf_op jit(solution)/shard_map/ppermute | solution.py:331
  44.8 8.8 %collective-permute-start.14 = (bf16[256,512]{1,0:T(8,128)(2,1)S(1)}, bf16[256,512]{1,0:T(8,128)(2,1)S(1)}, u32[]{:S(2)}, u32[]{:S(2)}) collective-permute-start(bf16[256,512]{1,0:T(8,128)(2,1)S(1)} %get-tuple-element.105), channel_id=1, source_target_pairs={{0,8},{12,4},{1,9},{13,5},{2,10},{14,6},{3,11},{15,7},{16,24},{28,... | collective-permute-start | bytes 786440 | tf_op jit(solution)/shard_map/ppermute | solution.py:331
  53.7 2.7 %shard_map.178 = (bf16[384,512]{1,0:T(8,128)(2,1)S(1)}, bf16[384,512]{1,0:T(8,128)(2,1)S(1)}, bf16[384,2048]{1,0:T(8,128)(2,1)S(1)}, f32[1,512]{1,0:T(1,128)S(1)}) custom-call(s32[2]{0:T(128)S(1)} %pad_add_fusion.place, bf16[384,512]{1,0:T(8,128)(2,1)} %refs_0_.4, bf16[384,512]{1,0:T(8,128)(2,1)S(1)} %copy-done.10, bf16[384,512]{1,0:T(8,128)(2,1)S(1)} %copy-done.12, ...), custom_call_target="tpu_custom_call" | custom-call | flops 1 | bytes 1 | tf_op jit(solution)/shard_map/pallas_call | solution.py:118
  56.4 1.6 collective-permute-done.14
  58.0 0.7 collective-permute-start.16
  58.8 8.9 %collective-permute-start.6 = (bf16[384,512]{1,0:T(8,128)(2,1)S(1)}, bf16[384,512]{1,0:T(8,128)(2,1)S(1)}, u32[]{:S(2)}, u32[]{:S(2)}) collective-permute-start(bf16[384,512]{1,0:T(8,128)(2,1)S(1)} %get-tuple-element.53.refs_0_.refs_2_), channel_id=1, source_target_pairs={{0,4},{4,8},{1,5},{5,9},{2,6},{6,10},{3,7},{7,11},{16,20},{20,24},... | collective-permute-start | bytes 1179656 | tf_op jit(solution)/shard_map/ppermute | solution.py:331
  67.7 0.7 collective-permute-start.7
  68.4 5.0 %collective-permute-start.8 = (bf16[384,512]{1,0:T(8,128)(2,1)S(1)}, bf16[384,512]{1,0:T(8,128)(2,1)S(1)}, u32[]{:S(2)}, u32[]{:S(2)}) collective-permute-start(bf16[384,512]{1,0:T(8,128)(2,1)S(1)} %get-tuple-element.53.refs_0_.refs_2_), channel_id=1, source_target_pairs={{0,8},{12,4},{1,9},{13,5},{2,10},{14,6},{3,11},{15,7},{16,24},{28,... | collective-permute-start | bytes 1179656 | tf_op jit(solution)/shard_map/ppermute | solution.py:331
  73.5 1.0 shard_map.180.refs_0_
  74.5 2.6 %collective-permute-done.6.refs_1_ = bf16[384,512]{1,0:T(8,128)(2,1)S(1)} collective-permute-done((bf16[384,512]{1,0:T(8,128)(2,1)S(1)}, bf16[384,512]{1,0:T(8,128)(2,1)S(1)}, u32[]{:S(2)}, u32[]{:S(2)}) %collective-permute-start.6) | collective-permute-done | bytes 393248 | tf_op jit(solution)/shard_map/ppermute | solution.py:331
  77.1 0.7 collective-permute-start.15
  77.8 7.3 %collective-permute-done.8.refs_3_ = bf16[384,512]{1,0:T(8,128)(2,1)S(1)} collective-permute-done((bf16[384,512]{1,0:T(8,128)(2,1)S(1)}, bf16[384,512]{1,0:T(8,128)(2,1)S(1)}, u32[]{:S(2)}, u32[]{:S(2)}) %collective-permute-start.8) | collective-permute-done | bytes 393248 | tf_op jit(solution)/shard_map/ppermute | solution.py:331
  85.1 0.7 collective-permute-start.17
  85.9 2.4 %shard_map.181.refs_0_ = bf16[384,1024]{1,0:T(8,128)(2,1)S(1)} custom-call(s32[2]{0:T(128)S(1)} %pad_add_fusion.place, bf16[384,512]{1,0:T(8,128)(2,1)S(1)} %get-tuple-element.53.refs_0_.refs_2_, bf16[384,512]{1,0:T(8,128)(2,1)S(1)} %collective-permute-done.6.refs_1_, bf16[384,512]{1,0:T(8,128)(2,1)S(1)} %collective-permute-done.7.refs_2_, ...), custom_call_target="tpu_custom_call" | custom-call | flops 1 | bytes 1 | tf_op jit(solution)/shard_map/pallas_call | solution.py:118
  88.3 1.3 collective-permute-start.18
  89.6 0.7 collective-permute-start.19
  90.3 25.1 %collective-permute-done.18.refs_1_ = bf16[384,1024]{1,0:T(8,128)(2,1)S(1)} collective-permute-done((bf16[384,1024]{1,0:T(8,128)(2,1)S(1)}, bf16[384,1024]{1,0:T(8,128)(2,1)S(1)}, u32[]{:S(2)}, u32[]{:S(2)}) %collective-permute-start.18) | collective-permute-done | bytes 786464 | tf_op jit(solution)/shard_map/ppermute | solution.py:331
  115.4 1.8 shard_map.182
  117.3 1.3 collective-permute-start.20
  118.6 1.4 collective-permute-done.21.refs_1_
  119.9 0.7 shard_map.183
  121.4 18.7 %collective-permute-done.20.refs_1_ = bf16[384,1024]{1,0:T(8,128)(2,1)S(1)} collective-permute-done((bf16[384,1024]{1,0:T(8,128)(2,1)S(1)}, bf16[384,1024]{1,0:T(8,128)(2,1)S(1)}, u32[]{:S(2)}, u32[]{:S(2)}) %collective-permute-start.20) | collective-permute-done | bytes 786464 | tf_op jit(solution)/shard_map/ppermute | solution.py:331
  140.2 1.5 shard_map.184
  141.8 2.0 %shard_map.185 = (bf16[384,512]{1,0:T(8,128)(2,1)S(1)}, f32[1,512]{1,0:T(1,128)S(1)}, f32[1,512]{1,0:T(1,128)S(1)}, bf16[384,512]{1,0:T(8,128)(2,1)}) custom-call(s32[2]{0:T(128)S(1)} %pad_add_fusion.place, bf16[384,1024]{1,0:T(8,128)(2,1)S(1)} %get-tuple-element.63.refs_0_, bf16[384,1024]{1,0:T(8,128)(2,1)S(1)} %get-tuple-element.67.refs_1_, ...), custom_call_target="tpu_custom_call" | custom-call | flops 1 | bytes 1 | tf_op jit(solution)/shard_map/pallas_call | solution.py:118
  143.8 2.7 %shard_map.186 = (f32[520,512]{1,0:T(8,128)}, f32[512,512]{1,0:T(8,128)S(1)}, f32[512,512]{1,0:T(8,128)S(1)}, f32[512,512]{1,0:T(8,128)S(1)}) custom-call(s32[2]{0:T(128)S(1)} %pad_add_fusion.place, bf16[2048,384]{1,0:T(8,128)(2,1)S(1)} %shard_map.180.refs_0_, bf16[384,512]{1,0:T(8,128)(2,1)S(1)} %get-tuple-element.72.refs_1_, ...), custom_call_target="tpu_custom_call" | custom-call | flops 1 | bytes 1 | tf_op jit(solution)/shard_map/pallas_call | solution.py:118
  146.5 1.0 copy-done.3
  147.9 0.7 shard_map.188
  148.7 0.8 convert_element_type.22
  150.1 1.5 collective-permute-start.27
  152.1 6.4 %collective-permute-done.27 = f32[8,512]{1,0:T(8,128)S(1)} collective-permute-done((f32[8,512]{1,0:T(8,128)S(1)}, f32[8,512]{1,0:T(8,128)S(1)}, u32[]{:S(2)}, u32[]{:S(2)}) %collective-permute-start.27) | collective-permute-done | bytes 16416 | tf_op jit(solution)/shard_map/ppermute | solution.py:335
  158.7 1.2 copy-done.4
  159.9 0.8 shard_map.187
  161.5 1.5 collective-permute-start.25
  163.1 1.3 fusion.3
  164.7 2.3 %divide_subtract_fusion = (f32[512,512]{1,0:T(8,128)}, f32[512,512]{1,0:T(8,128)}, f32[512,512]{1,0:T(8,128)}) fusion(f32[512,512]{1,0:T(8,128)S(1)} %copy-done.2, f32[512]{0:T(512)S(1)} %bitcast.19, f32[256,512]{1,0:T(8,128)S(1)} %get-tuple-element.104, f32[256,512]{1,0:T(8,128)S(1)} %get-tuple-element.103, f32[512,512]{1,0:T(8,128)S(1)} %copy-done.18, ...), kind=kLoop, calls=%fused_computation.5 | loop fusion | flops 4194304 | bytes 7342080 | tf_op jit(solution)/shard_map/sub | solution.py:27
  167.6 7.0 %collective-permute-done.25 = f16[512,512]{1,0:T(8,128)(2,1)S(1)} collective-permute-done((f16[512,512]{1,0:T(8,128)(2,1)S(1)}, f16[512,512]{1,0:T(8,128)(2,1)S(1)}, u32[]{:S(2)}, u32[]{:S(2)}) %collective-permute-start.25) | collective-permute-done | bytes 524320 | tf_op jit(solution)/shard_map/ppermute | solution.py:335
  174.6 2.3 %divide_subtract_fusion.1 = (f32[512,512]{1,0:T(8,128)}, f32[512,512]{1,0:T(8,128)}, f32[512,512]{1,0:T(8,128)}) fusion(f32[512,512]{1,0:T(8,128)S(1)} %copy-done.1, f32[512]{0:T(512)S(1)} %bitcast.16, f16[512,512]{1,0:T(8,128)(2,1)S(1)} %collective-permute-done.25, f32[512,512]{1,0:T(8,128)S(1)} %get-tuple-element.79, ...), kind=kLoop, calls=%fused_computation.7 | loop fusion | flops 4194304 | bytes 8914944 | tf_op jit(solution)/shard_map/sub | solution.py:27
  (86 shorter events, 7.2 us)
Async XLA Ops:
  0.7 1.2 copy-start
  2.6 26.8 %copy-start.2 = (f32[512,512]{1,0:T(8,128)S(1)}, f32[512,512]{1,0:T(8,128)}, u32[]{:S(2)}) copy-start(f32[512,512]{1,0:T(8,128)} %refs_0_.5) | copy-start | bytes 3145732
  3.2 26.2 %collective-permute-start.4 = (bf16[528,512]{1,0:T(8,128)(2,1)S(1)}, bf16[528,512]{1,0:T(8,128)(2,1)}, u32[]{:S(2)}, u32[]{:S(2)}) collective-permute-start(bf16[528,512]{1,0:T(8,128)(2,1)S(1)} %shard_map.177.refs_4_), channel_id=1, source_target_pairs={{0,2},{1,3},{2,0},{3,1},{4,6},{5,7},{6,4},{7,5},{8,10},{9,11},{10,... | collective-permute-start | bytes 1622024 | tf_op jit(solution)/shard_map/ppermute | solution.py:335
  6.2 23.2 %collective-permute-start.3 = (bf16[528,512]{1,0:T(8,128)(2,1)S(1)}, bf16[528,512]{1,0:T(8,128)(2,1)S(1)}, u32[]{:S(2)}, u32[]{:S(2)}) collective-permute-start(bf16[528,512]{1,0:T(8,128)(2,1)S(1)} %shard_map.177.refs_4_), channel_id=1, source_target_pairs={{0,1},{1,0},{2,3},{3,2},{4,5},{5,4},{6,7},{7,6},{8,9},{9,8},{10,11... | collective-permute-start | bytes 1622024 | tf_op jit(solution)/shard_map/ppermute | solution.py:335
  6.2 20.0 %collective-permute-start = (bf16[384,512]{1,0:T(8,128)(2,1)}, bf16[384,512]{1,0:T(8,128)(2,1)S(1)}, u32[]{:S(2)}, u32[]{:S(2)}) collective-permute-start(bf16[384,512]{1,0:T(8,128)(2,1)} %refs_0_.4), channel_id=1, source_target_pairs={{0,4},{4,0},{8,12},{12,8},{1,5},{5,1},{9,13},{13,9},{2,6},{6,2},{1... | collective-permute-start | bytes 1179656 | tf_op jit(solution)/shard_map/ppermute | solution.py:331
  7.8 20.8 %collective-permute-start.1 = (bf16[384,512]{1,0:T(8,128)(2,1)}, bf16[384,512]{1,0:T(8,128)(2,1)S(1)}, u32[]{:S(2)}, u32[]{:S(2)}) collective-permute-start(bf16[384,512]{1,0:T(8,128)(2,1)} %refs_0_.4), channel_id=1, source_target_pairs={{0,8},{4,12},{8,0},{12,4},{1,9},{5,13},{9,1},{13,5},{2,10},{6,14},... | collective-permute-start | bytes 1179656 | tf_op jit(solution)/shard_map/ppermute | solution.py:331
  29.4 24.2 %collective-permute-start.5 = (bf16[528,512]{1,0:T(8,128)(2,1)}, bf16[528,512]{1,0:T(8,128)(2,1)}, u32[]{:S(2)}, u32[]{:S(2)}) collective-permute-start(bf16[528,512]{1,0:T(8,128)(2,1)} %collective-permute-done.4.refs_6_), channel_id=1, source_target_pairs={{0,1},{1,0},{2,3},{3,2},{4,5},{5,4},{6,7},{7,6},{8,9},{9,8},{10,11... | collective-permute-start | bytes 1622024 | tf_op jit(solution)/shard_map/ppermute | solution.py:335
  30.1 26.3 %collective-permute-start.10 = (bf16[528,512]{1,0:T(8,128)(2,1)S(1)}, bf16[528,512]{1,0:T(8,128)(2,1)S(1)}, u32[]{:S(2)}, u32[]{:S(2)}) collective-permute-start(bf16[528,512]{1,0:T(8,128)(2,1)S(1)} %shard_map.179.refs_4_), channel_id=1, source_target_pairs={{0,2},{1,3},{2,0},{3,1},{4,6},{5,7},{6,4},{7,5},{8,10},{9,11},{10,... | collective-permute-start | bytes 1622024 | tf_op jit(solution)/shard_map/ppermute | solution.py:335
  30.7 14.1 %collective-permute-start.2 = (bf16[384,512]{1,0:T(8,128)(2,1)}, bf16[384,512]{1,0:T(8,128)(2,1)}, u32[]{:S(2)}, u32[]{:S(2)}) collective-permute-start(bf16[384,512]{1,0:T(8,128)(2,1)} %refs_0_.4), channel_id=1, source_target_pairs={{0,12},{4,8},{8,4},{12,0},{1,13},{5,9},{9,5},{13,1},{2,14},{6,10},... | collective-permute-start | bytes 1179656 | tf_op jit(solution)/shard_map/ppermute | solution.py:331
  33.1 20.6 %copy-start.10 = (bf16[384,512]{1,0:T(8,128)(2,1)S(1)}, bf16[384,512]{1,0:T(8,128)(2,1)}, u32[]{:S(2)}) copy-start(bf16[384,512]{1,0:T(8,128)(2,1)} %copy-done.9) | copy-start | bytes 1179652
  33.1 20.6 %copy-start.12 = (bf16[384,512]{1,0:T(8,128)(2,1)S(1)}, bf16[384,512]{1,0:T(8,128)(2,1)}, u32[]{:S(2)}) copy-start(bf16[384,512]{1,0:T(8,128)(2,1)} %copy-done.11) | copy-start | bytes 1179652
  33.2 23.2 %collective-permute-start.13 = (bf16[256,512]{1,0:T(8,128)(2,1)S(1)}, bf16[256,512]{1,0:T(8,128)(2,1)S(1)}, u32[]{:S(2)}, u32[]{:S(2)}) collective-permute-start(bf16[256,512]{1,0:T(8,128)(2,1)S(1)} %get-tuple-element.107), channel_id=1, source_target_pairs={{8,4},{12,8},{9,5},{13,9},{10,6},{14,10},{11,7},{15,11},{24,20},{2... | collective-permute-start | bytes 786440 | tf_op jit(solution)/shard_map/ppermute | solution.py:331
  34.0 22.4 %collective-permute-start.12 = (bf16[256,512]{1,0:T(8,128)(2,1)S(1)}, bf16[256,512]{1,0:T(8,128)(2,1)S(1)}, u32[]{:S(2)}, u32[]{:S(2)}) collective-permute-start(bf16[256,512]{1,0:T(8,128)(2,1)S(1)} %get-tuple-element.106), channel_id=1, source_target_pairs={{0,4},{4,8},{1,5},{5,9},{2,6},{6,10},{3,7},{7,11},{16,20},{20,24},... | collective-permute-start | bytes 786440 | tf_op jit(solution)/shard_map/ppermute | solution.py:331
  44.8 13.2 %collective-permute-start.14 = (bf16[256,512]{1,0:T(8,128)(2,1)S(1)}, bf16[256,512]{1,0:T(8,128)(2,1)S(1)}, u32[]{:S(2)}, u32[]{:S(2)}) collective-permute-start(bf16[256,512]{1,0:T(8,128)(2,1)S(1)} %get-tuple-element.105), channel_id=1, source_target_pairs={{0,8},{12,4},{1,9},{13,5},{2,10},{14,6},{3,11},{15,7},{16,24},{28,... | collective-permute-start | bytes 786440 | tf_op jit(solution)/shard_map/ppermute | solution.py:331
  53.6 14.8 %collective-permute-start.9 = (bf16[528,512]{1,0:T(8,128)(2,1)S(1)}, bf16[528,512]{1,0:T(8,128)(2,1)S(1)}, u32[]{:S(2)}, u32[]{:S(2)}) collective-permute-start(bf16[528,512]{1,0:T(8,128)(2,1)S(1)} %shard_map.179.refs_4_), channel_id=1, source_target_pairs={{0,1},{1,0},{2,3},{3,2},{4,5},{5,4},{6,7},{7,6},{8,9},{9,8},{10,11... | collective-permute-start | bytes 1622024 | tf_op jit(solution)/shard_map/ppermute | solution.py:335
  58.0 27.1 %collective-permute-start.16 = (bf16[768,512]{1,0:T(8,128)(2,1)S(1)}, bf16[768,512]{1,0:T(8,128)(2,1)S(1)}, u32[]{:S(2)}, u32[]{:S(2)}) collective-permute-start(bf16[768,512]{1,0:T(8,128)(2,1)S(1)} %constant_dynamic-update-slice_fusion.refs_8_), channel_id=1, source_target_pairs={{4,6},{5,7},{6,4},{7,5},{8,10},{9,11},{10,8},{11,9},{20,22},{21,23... | collective-permute-start | bytes 2359304 | tf_op jit(solution)/shard_map/ppermute | solution.py:335
  58.8 26.4 %collective-permute-start.11 = (bf16[528,512]{1,0:T(8,128)(2,1)S(1)}, bf16[528,512]{1,0:T(8,128)(2,1)S(1)}, u32[]{:S(2)}, u32[]{:S(2)}) collective-permute-start(bf16[528,512]{1,0:T(8,128)(2,1)S(1)} %collective-permute-done.10.refs_6_), channel_id=1, source_target_pairs={{0,1},{1,0},{2,3},{3,2},{4,5},{5,4},{6,7},{7,6},{8,9},{9,8},{10,11... | collective-permute-start | bytes 1622024 | tf_op jit(solution)/shard_map/ppermute | solution.py:335
  58.8 18.3 %collective-permute-start.6 = (bf16[384,512]{1,0:T(8,128)(2,1)S(1)}, bf16[384,512]{1,0:T(8,128)(2,1)S(1)}, u32[]{:S(2)}, u32[]{:S(2)}) collective-permute-start(bf16[384,512]{1,0:T(8,128)(2,1)S(1)} %get-tuple-element.53.refs_0_.refs_2_), channel_id=1, source_target_pairs={{0,4},{4,8},{1,5},{5,9},{2,6},{6,10},{3,7},{7,11},{16,20},{20,24},... | collective-permute-start | bytes 1179656 | tf_op jit(solution)/shard_map/ppermute | solution.py:331
  67.7 10.1 %collective-permute-start.7 = (bf16[384,512]{1,0:T(8,128)(2,1)S(1)}, bf16[384,512]{1,0:T(8,128)(2,1)S(1)}, u32[]{:S(2)}, u32[]{:S(2)}) collective-permute-start(bf16[384,512]{1,0:T(8,128)(2,1)S(1)} %get-tuple-element.53.refs_0_.refs_2_), channel_id=1, source_target_pairs={{8,4},{12,8},{9,5},{13,9},{10,6},{14,10},{11,7},{15,11},{24,20},{2... | collective-permute-start | bytes 1179656 | tf_op jit(solution)/shard_map/ppermute | solution.py:331
  68.4 16.7 %collective-permute-start.8 = (bf16[384,512]{1,0:T(8,128)(2,1)S(1)}, bf16[384,512]{1,0:T(8,128)(2,1)S(1)}, u32[]{:S(2)}, u32[]{:S(2)}) collective-permute-start(bf16[384,512]{1,0:T(8,128)(2,1)S(1)} %get-tuple-element.53.refs_0_.refs_2_), channel_id=1, source_target_pairs={{0,8},{12,4},{1,9},{13,5},{2,10},{14,6},{3,11},{15,7},{16,24},{28,... | collective-permute-start | bytes 1179656 | tf_op jit(solution)/shard_map/ppermute | solution.py:331
  77.1 8.7 %collective-permute-start.15 = (bf16[768,512]{1,0:T(8,128)(2,1)S(1)}, bf16[768,512]{1,0:T(8,128)(2,1)S(1)}, u32[]{:S(2)}, u32[]{:S(2)}) collective-permute-start(bf16[768,512]{1,0:T(8,128)(2,1)S(1)} %constant_dynamic-update-slice_fusion.refs_8_), channel_id=1, source_target_pairs={{4,5},{5,4},{6,7},{7,6},{8,9},{9,8},{10,11},{11,10},{20,21},{21,20... | collective-permute-start | bytes 2359304 | tf_op jit(solution)/shard_map/ppermute | solution.py:335
  85.1 0.7 collective-permute-start.17
  88.3 27.1 %collective-permute-start.18 = (bf16[384,1024]{1,0:T(8,128)(2,1)S(1)}, bf16[384,1024]{1,0:T(8,128)(2,1)S(1)}, u32[]{:S(2)}, u32[]{:S(2)}) collective-permute-start(bf16[384,1024]{1,0:T(8,128)(2,1)S(1)} %shard_map.181.refs_0_), channel_id=1, source_target_pairs={{4,0},{8,12},{5,1},{9,13},{6,2},{10,14},{7,3},{11,15},{20,16},{24,... | collective-permute-start | bytes 2359304 | tf_op jit(solution)/shard_map/ppermute | solution.py:331
  89.6 25.8 %collective-permute-start.19 = (bf16[384,1024]{1,0:T(8,128)(2,1)S(1)}, bf16[384,1024]{1,0:T(8,128)(2,1)S(1)}, u32[]{:S(2)}, u32[]{:S(2)}) collective-permute-start(bf16[384,1024]{1,0:T(8,128)(2,1)S(1)} %shard_map.181.refs_0_), channel_id=1, source_target_pairs={{4,8},{8,4},{5,9},{9,5},{6,10},{10,6},{7,11},{11,7},{20,24},{24,20... | collective-permute-start | bytes 2359304 | tf_op jit(solution)/shard_map/ppermute | solution.py:331
  117.2 2.7 %collective-permute-start.21 = (f32[520,512]{1,0:T(8,128)S(1)}, f32[520,512]{1,0:T(8,128)S(1)}, u32[]{:S(2)}, u32[]{:S(2)}) collective-permute-start(f32[520,512]{1,0:T(8,128)S(1)} %get-tuple-element.65), channel_id=1, source_target_pairs={{0,1},{1,0},{2,3},{3,2},{4,5},{5,4},{6,7},{7,6},{8,9},{9,8},{10,11... | collective-permute-start | bytes 3194888 | tf_op jit(solution)/shard_map/ppermute | solution.py:335
  117.3 22.9 %collective-permute-start.20 = (bf16[384,1024]{1,0:T(8,128)(2,1)S(1)}, bf16[384,1024]{1,0:T(8,128)(2,1)S(1)}, u32[]{:S(2)}, u32[]{:S(2)}) collective-permute-start(bf16[384,1024]{1,0:T(8,128)(2,1)S(1)} %shard_map.181.refs_0_), channel_id=1, source_target_pairs={{8,0},{4,12},{9,1},{5,13},{10,2},{6,14},{11,3},{7,15},{24,16},{20,... | collective-permute-start | bytes 2359304 | tf_op jit(solution)/shard_map/ppermute | solution.py:331
  120.7 21.1 %collective-permute-start.22 = (f16[256,512]{1,0:T(8,128)(2,1)S(1)}, f16[256,512]{1,0:T(8,128)(2,1)S(1)}, u32[]{:S(2)}, u32[]{:S(2)}) collective-permute-start(f16[256,512]{1,0:T(8,128)(2,1)S(1)} %convert_element_type.18), channel_id=1, source_target_pairs={{0,2},{1,3},{2,0},{3,1},{4,6},{5,7},{6,4},{7,5},{8,10},{9,11},{10,... | collective-permute-start | bytes 786440 | tf_op jit(solution)/shard_map/ppermute | solution.py:335
  141.7 6.3 %collective-permute-start.28 = (f32[520,512]{1,0:T(8,128)S(1)}, f32[520,512]{1,0:T(8,128)S(1)}, u32[]{:S(2)}, u32[]{:S(2)}) collective-permute-start(f32[520,512]{1,0:T(8,128)S(1)} %get-tuple-element.88), channel_id=1, source_target_pairs={{0,1},{1,0},{2,3},{3,2},{4,5},{5,4},{6,7},{7,6},{8,9},{9,8},{10,11... | collective-permute-start | bytes 3194888 | tf_op jit(solution)/shard_map/ppermute | solution.py:335
  146.5 1.0 copy-start.3
  147.5 2.0 %copy-start.15 = (f32[512,512]{1,0:T(8,128)}, f32[512,512]{1,0:T(8,128)S(1)}, u32[]{:S(2)}) copy-start(f32[512,512]{1,0:T(8,128)S(1)} %get-tuple-element.80) | copy-start | bytes 3145732
  147.5 11.3 %collective-permute-start.23 = (f32[520,512]{1,0:T(8,128)}, f32[520,512]{1,0:T(8,128)S(1)}, u32[]{:S(2)}, u32[]{:S(2)}) collective-permute-start(f32[520,512]{1,0:T(8,128)} %get-tuple-element.75), channel_id=1, source_target_pairs={{0,1},{1,0},{2,3},{3,2},{4,5},{5,4},{6,7},{7,6},{8,9},{9,8},{10,11... | collective-permute-start | bytes 3194888 | tf_op jit(solution)/shard_map/ppermute | solution.py:335
  149.6 13.5 %collective-permute-start.29 = (f16[256,512]{1,0:T(8,128)(2,1)}, f16[256,512]{1,0:T(8,128)(2,1)}, u32[]{:S(2)}, u32[]{:S(2)}) collective-permute-start(f16[256,512]{1,0:T(8,128)(2,1)} %convert_element_type.22), channel_id=1, source_target_pairs={{0,2},{1,3},{2,0},{3,1},{4,6},{5,7},{6,4},{7,5},{8,10},{9,11},{10,... | collective-permute-start | bytes 786440 | tf_op jit(solution)/shard_map/ppermute | solution.py:335
  150.1 8.4 %collective-permute-start.27 = (f32[8,512]{1,0:T(8,128)S(1)}, f32[8,512]{1,0:T(8,128)S(1)}, u32[]{:S(2)}, u32[]{:S(2)}) collective-permute-start(f32[8,512]{1,0:T(8,128)S(1)} %get-tuple-element.86), channel_id=1, source_target_pairs={{0,2},{1,3},{2,0},{3,1},{4,6},{5,7},{6,4},{7,5},{8,10},{9,11},{10,... | collective-permute-start | bytes 49160 | tf_op jit(solution)/shard_map/ppermute | solution.py:335
  151.6 16.0 %collective-permute-start.24 = (f32[512,512]{1,0:T(8,128)}, f32[512,512]{1,0:T(8,128)S(1)}, u32[]{:S(2)}, u32[]{:S(2)}) collective-permute-start(f32[512,512]{1,0:T(8,128)} %copy-done.15), channel_id=1, source_target_pairs={{0,1},{1,0},{2,3},{3,2},{4,5},{5,4},{6,7},{7,6},{8,9},{9,8},{10,11... | collective-permute-start | bytes 3145736 | tf_op jit(solution)/shard_map/ppermute | solution.py:335
  151.6 7.1 %collective-permute-start.30 = (f32[8,512]{1,0:T(8,128)S(1)}, f32[8,512]{1,0:T(8,128)S(1)}, u32[]{:S(2)}, u32[]{:S(2)}) collective-permute-start(f32[8,512]{1,0:T(8,128)S(1)} %get-tuple-element.91), channel_id=1, source_target_pairs={{0,2},{1,3},{2,0},{3,1},{4,6},{5,7},{6,4},{7,5},{8,10},{9,11},{10,... | collective-permute-start | bytes 49160 | tf_op jit(solution)/shard_map/ppermute | solution.py:335
  158.7 1.2 copy-start.4
  160.8 2.3 %copy-start.6 = (f32[256,512]{1,0:T(8,128)S(1)}, f32[256,512]{1,0:T(8,128)}, u32[]{:S(2)}) copy-start(f32[256,512]{1,0:T(8,128)} %copy-done.5) | copy-start | bytes 1572868
  160.8 2.3 %copy-start.8 = (f32[256,512]{1,0:T(8,128)S(1)}, f32[256,512]{1,0:T(8,128)}, u32[]{:S(2)}) copy-start(f32[256,512]{1,0:T(8,128)} %copy-done.7) | copy-start | bytes 1572868
  160.8 6.2 %collective-permute-start.26 = (f32[8,512]{1,0:T(8,128)S(1)}, f32[8,512]{1,0:T(8,128)S(1)}, u32[]{:S(2)}, u32[]{:S(2)}) collective-permute-start(f32[8,512]{1,0:T(8,128)S(1)} %get-tuple-element.76), channel_id=1, source_target_pairs={{0,2},{1,3},{2,0},{3,1},{4,6},{5,7},{6,4},{7,5},{8,10},{9,11},{10,... | collective-permute-start | bytes 49160 | tf_op jit(solution)/shard_map/ppermute | solution.py:335
  161.5 13.1 %collective-permute-start.25 = (f16[512,512]{1,0:T(8,128)(2,1)S(1)}, f16[512,512]{1,0:T(8,128)(2,1)S(1)}, u32[]{:S(2)}, u32[]{:S(2)}) collective-permute-start(f16[512,512]{1,0:T(8,128)(2,1)S(1)} %convert_element_type.19), channel_id=1, source_target_pairs={{0,2},{1,3},{2,0},{3,1},{4,6},{5,7},{6,4},{7,5},{8,10},{9,11},{10,... | collective-permute-start | bytes 1572872 | tf_op jit(solution)/shard_map/ppermute | solution.py:335
  163.1 1.3 copy-start.18
  163.1 1.6 copy-start.19
  164.7 2.3 %copy-start.14 = (f32[128]{0:T(128)S(1)}, f32[128]{0:T(128)}, u32[]{:S(2)}) copy-start(f32[128]{0:T(128)} %param.12) | copy-start | bytes 1540
  164.7 2.3 %copy-start.20 = (f32[128]{0:T(128)S(1)}, f32[128]{0:T(128)}, u32[]{:S(2)}) copy-start(f32[128]{0:T(128)} %param.16) | copy-start | bytes 1540
  164.7 2.4 %copy-start.21 = (f32[128]{0:T(128)S(1)}, f32[128]{0:T(128)}, u32[]{:S(2)}) copy-start(f32[128]{0:T(128)} %param.17) | copy-start | bytes 1540
  164.7 9.9 %copy-start.1 = (f32[512,512]{1,0:T(8,128)S(1)}, f32[512,512]{1,0:T(8,128)}, u32[]{:S(2)}) copy-start(f32[512,512]{1,0:T(8,128)} %refs_0_.3) | copy-start | bytes 3145732
  164.7 9.9 %copy-start.16 = (f32[512,512]{1,0:T(8,128)S(1)}, f32[512,512]{1,0:T(8,128)}, u32[]{:S(2)}) copy-start(f32[512,512]{1,0:T(8,128)} %param.14) | copy-start | bytes 3145732
  164.7 9.9 %copy-start.17 = (f32[512,512]{1,0:T(8,128)S(1)}, f32[512,512]{1,0:T(8,128)}, u32[]{:S(2)}) copy-start(f32[512,512]{1,0:T(8,128)} %param.15) | copy-start | bytes 3145732
  (5 other events, 3.8 us)

commit v5 on v4

--- a/solution.py
+++ b/solution.py
@@ -165,12 +165,39 @@
 
 
 def codes_body(
-    place, own, one, two, three, enc0, enc1, enc2, enc3, codes, mask, full, active, bias
+    place,
+    own,
+    low,
+    high,
+    across,
+    relay1,
+    relay2,
+    enc0,
+    enc1,
+    enc2,
+    enc3,
+    codes,
+    mask,
+    full,
+    active,
+    bias,
 ):
     z, i = place[0], place[1]
     width = own.shape[1]
-    for k, block in enumerate((own, one, two, three)):
-        full[:, columns((z ^ k) * width, width)] = block[...]
+    for at, blocks in enumerate(
+        (
+            (own, high, relay1, relay2),
+            (low, own, high, across),
+            (across, low, own, high),
+            (relay2, relay1, low, own),
+        )
+    ):
+
+        @pl.when(z == at)
+        def _(blocks=blocks):
+            for b, block in enumerate(blocks):
+                full[:, b * width : (b + 1) * width] = block[...]
+
     total = jnp.zeros(codes.shape, F32)
     piece = codes.shape[1] // 4
     for t, enc in enumerate((enc0, enc1, enc2, enc3)):
@@ -184,6 +211,23 @@
     codes[...] = low_codes
     mask[...] = (preact > 0.0).astype(F32).astype(BF16)
     active[...] = jnp.sum(low_codes.astype(F32), axis=0, keepdims=True)
+
+
+def onward_body(place, low, high, out):
+    @pl.when(place[0] == 1)
+    def _():
+        out[...] = high[...]
+
+    @pl.when(place[0] != 1)
+    def _():
+        out[...] = low[...]
+
+
+def pieces_body(place, dec, up, down, across):
+    z = place[0]
+    half = up.shape[0]
+    for out, second in ((up, z >= 1), (down, z >= 3), (across, z < 2)):
+        out[...] = dec[pl.ds(pl.multiple_of(jnp.where(second, half, 0), half), half), :]
 
 
 def turn_body(place, full, turned):
@@ -223,17 +267,16 @@
         out[...] = end[...]
 
 
-def decoder_grads(scale, i, error, codes, row, send, keep):
+def decoder_grads(scale, i, error, codes, row, outs):
     half = error.shape[1] // 4
-    for out, slots in ((send, (3, 1)), (keep, (2, 0))):
-        for at, slot in enumerate(slots):
-            out[at * half : (at + 1) * half] = scale * lax.dot_general(
-                error[:, columns((i ^ slot) * half, half)],
-                codes[...],
-                (((0,), (0,)), ((), ())),
-                preferred_element_type=F32,
-            )
-    send[2 * half :] = jnp.broadcast_to(row[...], (send.shape[0] - 2 * half, row.shape[1]))
+    for out, slot in zip(outs, (3, 1, 2, 0)):
+        out[:half] = scale * lax.dot_general(
+            error[:, columns((i ^ slot) * half, half)],
+            codes[...],
+            (((0,), (0,)), ((), ())),
+            preferred_element_type=F32,
+        )
+    outs[0][half:] = jnp.broadcast_to(row[...], (outs[0].shape[0] - half, row.shape[1]))
 
 
 def back_through(i, error, decs, shift):
@@ -251,19 +294,17 @@
     )
 
 
-def near_body(
-    rows, place, mine, passed, codes, active, dec0, dec1, dec2, dec3, part, send, keep, near
-):
+def near_body(rows, place, mine, passed, codes, active, dec0, dec1, dec2, dec3, part, near, *outs):
     z, i = place[0], place[1]
     half = mine.shape[1] // 4
     pick(place, mine, passed, near)
-    decoder_grads(-2.0 / rows, i, near, codes, active, send, keep)
+    decoder_grads(-2.0 / rows, i, near, codes, active, outs)
     part[...] = back_through(i, near, (dec0, dec1, dec2, dec3), jnp.where(z >= 2, half, 0))
 
 
-def far_error_body(rows, place, swapped, direct, codes, active, send, keep, far):
+def far_error_body(rows, place, swapped, direct, codes, active, far, *outs):
     pick(place, swapped, direct, far)
-    decoder_grads(-2.0 / rows, place[1], far, codes, active, send, keep)
+    decoder_grads(-2.0 / rows, place[1], far, codes, active, outs)
 
 
 def far_code_body(
@@ -295,16 +336,28 @@
     send_far[width:] = jnp.broadcast_to(row[...], (send_far.shape[0] - width, row.shape[1]))
 
 
-def far_body(place, kept, received, row, scaled, small, *near):
+def far_body(place, kept, received, row, *refs):
+    scaled, small = refs[-2:]
     width = scaled.shape[0]
-    total = kept[:width] + received[:width]
+    total = kept[...] + received[:width]
     largest = jnp.maximum(jnp.max(jnp.abs(total), axis=0, keepdims=True), 1e-30)
     scaled[...] = total * (16384.0 / largest)
-    rows = received[received.shape[0] - small.shape[0] :] + row[...]
+    rows = received[width:] + row[...]
     at = lax.broadcasted_iota(jnp.int32, rows.shape, 0)
-    small[...] = jnp.where(at == 0, largest * (1.0 / 16384.0), rows)
-    for out in near:
-        out[...] = kept[width:] + received[width : kept.shape[0]]
+    small[:8] = jnp.where(at == 0, largest * (1.0 / 16384.0), rows)
+    for other in refs[:-2]:
+        small[8:] = other[...]
+
+
+def decoder_step_body(
+    rows, place, param, moment, square, near, far, active, norms, param_out, moment_out, square_out
+):
+    is_near = (pl.program_id(0) < pl.num_programs(0) // 2) == (place[0] < 2)
+    grad = jnp.where(is_near, near[...], far[...])
+    grad += param[...] * (active[...] / norms[...]) / rows
+    param_out[...], moment_out[...], square_out[...] = adam_update(
+        param[...], grad, moment[...], square[...]
+    )
 
 
 def line_shards(
@@ -334,7 +387,10 @@
         pairs = [(4 * p + k, 4 * p + (k ^ bits)) for p in planes for k in range(4)]
         return lax.ppermute(value, ("latent", "dp"), pairs)
 
-    one, two, three = [along(activations, [(k, k ^ d) for k in range(4)]) for d in (1, 2, 3)]
+    ends = [(1, 0), (2, 3)]
+    low = along(activations, [(0, 1), (1, 2), (2, 3)])
+    high = along(activations, [(1, 0), (2, 1), (3, 2)])
+    across = along(activations, [(0, 2), (3, 1)])
 
     (enc_own,) = local_kernel(
         encoder_body,
@@ -352,14 +408,20 @@
         after=(enc_core,),
     )
     dec_chip, dec_core = flip(behind(dec_own, enc_chip), 2), flip(dec_own, 1)
-    enc = [enc_own, enc_core, enc_chip, flip(behind(enc_chip, one, two), 1)]
-
-    dec_late = behind(dec_own, one, two)
-    first, second = dec_late[:half], dec_late[half:width]
+    (onward,) = local_kernel(
+        onward_body, [shape((count, width), BF16)], place, low, high, after=(dec_core,)
+    )
+    relay1 = along(onward, ends)
+    relay2 = along(across, ends)
+    enc = [enc_own, enc_core, enc_chip, flip(behind(enc_chip, onward), 1)]
+
+    up, down, beyond = local_kernel(
+        pieces_body, [shape((half, latents), BF16)] * 3, place, dec_own, after=(onward,)
+    )
     dec_pieces = [
-        along(jnp.where(z >= 1, second, first), [(0, 1), (1, 2)]),
-        along(jnp.where(z >= 3, second, first), [(2, 1), (3, 2)]),
-        along(jnp.where(z >= 2, first, second), [(0, 2), (3, 1)]),
+        along(up, [(0, 1), (1, 2)]),
+        along(down, [(2, 1), (3, 2)]),
+        along(beyond, [(0, 2), (3, 1)]),
     ]
     dec = [dec_own, dec_core, dec_chip, flip(dec_chip, 1)]
 
@@ -373,9 +435,11 @@
         ],
         place,
         activations,
-        one,
-        two,
-        three,
+        low,
+        high,
+        across,
+        relay1,
+        relay2,
         *enc,
         scratch=[pltpu.VMEM((1, latents), F32)],
     )
@@ -411,27 +475,23 @@
     direct = along(own_error, [(2, 0), (1, 3)])
 
     def across_chips(scaled, small):
-        sent = scaled.astype(jnp.float16)
-        received, small_received = flip(sent, 2), flip(small, 2)
-        block = received.astype(F32) * small_received[:1]
-        return received, block, small[1] + small_received[1]
-
-    def decoder_half(send, keep, row):
-        scaled, small, near = local_kernel(
+        return flip(scaled.astype(jnp.float16), 2), flip(small, 2)
+
+    def decoder_half(send_far, send_near, keep_far, keep_near):
+        scaled, small = local_kernel(
             far_body,
-            [shape((half, latents), F32), shape((8, latents), F32), shape((half, latents), F32)],
+            [shape((half, latents), F32), shape((8, latents), F32)],
             place,
-            keep,
-            flip(send, 1),
-            row,
+            keep_far,
+            flip(send_far, 1),
+            active,
         )
-        received, block, row = across_chips(scaled, small)
-        return scaled, received, near + block, row
-
-    blocks = [shape((width + 8, latents), F32), shape((width, latents), F32)]
-    part, send, keep, near = local_kernel(
+        return scaled, small, (keep_near, flip(send_near, 1))
+
+    blocks = [shape((half + 8, latents), F32)] + [shape((half, latents), F32)] * 3
+    part, near, *near_blocks = local_kernel(
         functools.partial(near_body, rows),
-        [shape((count, latents), F32), *blocks, shape((count, features // 2), BF16)],
+        [shape((count, latents), F32), shape((count, features // 2), BF16), *blocks],
         place,
         own_error,
         passed,
@@ -440,10 +500,10 @@
         *dec,
         after=(swapped,),
     )
-    near_scaled, near_received, near_grad, active_sum = decoder_half(send, keep, active)
-    send, keep, far = local_kernel(
+    near_scaled, near_small, near_kept = decoder_half(*near_blocks)
+    far, *far_blocks = local_kernel(
         functools.partial(far_error_body, rows),
-        [*blocks, shape((count, features // 2), BF16)],
+        [shape((count, features // 2), BF16), *blocks],
         place,
         swapped,
         direct,
@@ -451,7 +511,9 @@
         active,
         after=(near_scaled,),
     )
-    _, _, far_grad, _ = decoder_half(send, keep, active)
+    near_received = across_chips(near_scaled, behind(near_small, far))
+    far_scaled, far_small, far_kept = decoder_half(*far_blocks)
+    far_received = flip(far_scaled.astype(jnp.float16), 2)
     grad_low, bias_sum, norms, error = local_kernel(
         functools.partial(far_code_body, rows),
         [
@@ -463,7 +525,7 @@
         place,
         near,
         far,
-        behind(part, near_received),
+        behind(part, *near_received),
         mask,
         *dec,
     )
@@ -477,35 +539,41 @@
     )
     scaled, small = local_kernel(
         far_body,
-        [shape((width, latents), F32), shape((8, latents), F32)],
+        [shape((width, latents), F32), shape((16, latents), F32)],
         place,
         keep_far,
         flip(send_far, 1),
         bias_sum,
-    )
-    _, block, grad_bias = across_chips(scaled, small)
-    grad_encoder = keep_near + flip(send_near, 1) + block
+        far_small,
+    )
+    enc_received, enc_small = across_chips(scaled, small)
+
+    decoder, dec_moment, dec_square, encoder, enc_moment, enc_square = lax.optimization_barrier(
+        (decoder, dec_moment, dec_square, encoder, enc_moment, enc_square, small)
+    )[:6]
+
+    def added(kept, received):
+        return kept[0] + kept[1] + received[0].astype(F32) * received[1][:1]
+
+    near_grad = added(near_kept, near_received)
+    far_grad = added(far_kept, (far_received, enc_small[8:]))
+    active_sum = near_small[1] + near_received[1][1]
+    grad_encoder = added((keep_near, flip(send_near, 1)), (enc_received, enc_small))
+    grad_bias = small[1] + enc_small[1]
     grad_bias = lax.dynamic_slice(grad_bias, (i * enc_bias.shape[0],), (enc_bias.shape[0],))
-
-    decoder, dec_moment, dec_square = lax.optimization_barrier(
-        (decoder, dec_moment, dec_square, small)
-    )[:3]
-    encoder, enc_moment, enc_square = lax.optimization_barrier(
-        (encoder, enc_moment, enc_square, small)
-    )[:3]
-    low_first = z < 2
-    grad_dec_rows = jnp.concatenate(
-        [
-            jnp.where(low_first, near_grad, far_grad),
-            jnp.where(low_first, far_grad, near_grad),
-        ],
-        axis=0,
-    )
-    grad_decoder = grad_dec_rows + decoder * (active_sum / norms) / rows
-
-    new_decoder, new_dec_moment, new_dec_square = adam_update(
-        decoder, grad_decoder, dec_moment, dec_square
-    )
+    step = width // 4
+    block = pl.BlockSpec((step, latents), lambda r: (r, 0))
+    in_half = pl.BlockSpec((step, latents), lambda r: (r % 2, 0))
+    row = pl.BlockSpec((1, latents), lambda r: (0, 0))
+    new_decoder, new_dec_moment, new_dec_square = pl.pallas_call(
+        functools.partial(decoder_step_body, rows),
+        grid=(4,),
+        out_shape=[shape((width, latents), F32)] * 3,
+        in_specs=[SMEM, block, block, block, in_half, in_half, row, row],
+        out_specs=[block] * 3,
+        compiler_params=pltpu.CompilerParams(vmem_limit_bytes=24 * 1024 * 1024),
+        cost_estimate=pl.CostEstimate(flops=1, bytes_accessed=1, transcendentals=0),
+    )(place, decoder, dec_moment, dec_square, near_grad, far_grad, active_sum[None], norms)
     new_enc_bias, new_bias_moment, new_bias_square = adam_update(
         enc_bias, grad_bias, bias_moment, bias_square
     )

time: 177 us -> 171 us (0.966)
  waiting for transfers between devices: 97.2 us -> 92 us
  Pallas kernels: 17.6 us -> 22.4 us
  other arithmetic: 7.49 us -> 4.48 us
  starting transfers between devices: 47.3 us -> 44.5 us
    ppermute x12 -> x14, waiting for transfers between devices: 82.3 us -> 71.1 us  [along(): return lax.ppermute(value, 'latent', pairs)]
    ppermute x19 -> x20, waiting for transfers between devices: 14.9 us -> 20.9 us  [flip(): return lax.ppermute(value, ('latent', 'dp'), pairs)]
    ppermute x12 -> x14, starting transfers between devices: 35.4 us -> 31.7 us  [along(): return lax.ppermute(value, 'latent', pairs)]
    pallas_call x0 -> x1, Pallas kernels: none -> 2.88 us  [line_shards(): pl.pallas_call(functools.partial(decoder_step_body, rows), grid=(4,), out...]
    sub x3 -> x2, other arithmetic: 5.11 us -> 2.87 us  [adam_update(): param - learn_rate * (moment_new / first_fix) / (jnp.sqrt(square_new / se...]
    pallas_call x12 -> x14, Pallas kernels: 17.6 us -> 19.5 us  [local_kernel(): pl.pallas_call(run, out_shape=outs, in_specs=[SMEM] + [VMEM] * len(args)...]
    ppermute x19 -> x20, starting transfers between devices: 11.8 us -> 12.7 us  [flip(): return lax.ppermute(value, ('latent', 'dp'), pairs)]
  transfers between devices with their start and end apart: 31 -> 34, of which waited for: 12 -> 14; matrix products, arithmetic and copies ran while one was open for 3% -> 1% of each run, Pallas kernels for 7% -> 8%
where the time goes in v5:
time: 171 us; the launch traced here: 170 us
  waiting for transfers between devices  92 us (54%)
  starting transfers between devices  44.5 us (26%)
  Pallas kernels  22.4 us (13%)
  local copies, waits for them, and re-layouts  5.89 us (3%)
  other arithmetic  4.48 us (3%)
    ppermute x14, waiting for transfers between devices, along(): return lax.ppermute(value, 'latent', pairs)  71.1 us
    ppermute x14, starting transfers between devices, along(): return lax.ppermute(value, 'latent', pairs)  31.7 us
    ppermute x20, waiting for transfers between devices, flip(): return lax.ppermute(value, ('latent', 'dp'), pairs)  20.9 us
    pallas_call x14, Pallas kernels, local_kernel(): pl.pallas_call(run, out_shape=outs, in_specs=[SMEM] + [VMEM] * len(args)...  19.5 us
    ppermute x20, starting transfers between devices, flip(): return lax.ppermute(value, ('latent', 'dp'), pairs)  12.7 us
    unnamed x46, local copies, waits for them, and re-layouts  5.86 us
  transfers between devices with their start and end apart: 34, of which 14 were waited for; matrix products, arithmetic and copies ran while one was open for 1% of the time, Pallas kernels for 8%

profile of v5, /device:TPU:0, one launch (start us, length us, event | category | flops | bytes accessed | tf_op | source)
XLA Modules:
  0.0 170.4 jit_solution(3769239721084436200)
XLA Ops:
  0.7 1.3 copy-done.1
  3.8 1.6 collective-permute-done.3.refs_1_.refs_7_
  6.5 2.6 %collective-permute-start.7 = (bf16[528,512]{1,0:T(8,128)(2,1)S(1)}, bf16[528,512]{1,0:T(8,128)(2,1)S(1)}, u32[]{:S(2)}, u32[]{:S(2)}) collective-permute-start(bf16[528,512]{1,0:T(8,128)(2,1)S(1)} %shard_map.177.refs_6_), channel_id=1, source_target_pairs={{0,2},{1,3},{2,0},{3,1},{4,6},{5,7},{6,4},{7,5},{8,10},{9,11},{10,... | collective-permute-start | bytes 1622024 | tf_op jit(solution)/shard_map/ppermute | solution.py:388
  9.1 4.5 %collective-permute-start.2 = (bf16[384,512]{1,0:T(8,128)(2,1)S(1)}, bf16[384,512]{1,0:T(8,128)(2,1)S(1)}, u32[]{:S(2)}, u32[]{:S(2)}) collective-permute-start(bf16[384,512]{1,0:T(8,128)(2,1)S(1)} %copy-done.13), channel_id=1, source_target_pairs={{0,8},{12,4},{1,9},{13,5},{2,10},{14,6},{3,11},{15,7},{16,24},{28,... | collective-permute-start | bytes 1179656 | tf_op jit(solution)/shard_map/ppermute | solution.py:384
  13.6 1.3 collective-permute-start
  14.9 1.3 collective-permute-start.1
  16.2 6.9 %collective-permute-done.2.refs_3_ = bf16[384,512]{1,0:T(8,128)(2,1)S(1)} collective-permute-done((bf16[384,512]{1,0:T(8,128)(2,1)S(1)}, bf16[384,512]{1,0:T(8,128)(2,1)S(1)}, u32[]{:S(2)}, u32[]{:S(2)}) %collective-permute-start.2) | collective-permute-done | bytes 393248 | tf_op jit(solution)/shard_map/ppermute | solution.py:384
  23.1 1.3 collective-permute-start.6
  24.4 6.3 %collective-permute-done.refs_0_.refs_1_ = bf16[384,512]{1,0:T(8,128)(2,1)S(1)} collective-permute-done((bf16[384,512]{1,0:T(8,128)(2,1)S(1)}, bf16[384,512]{1,0:T(8,128)(2,1)S(1)}, u32[]{:S(2)}, u32[]{:S(2)}) %collective-permute-start) | collective-permute-done | bytes 393248 | tf_op jit(solution)/shard_map/ppermute | solution.py:384
  31.3 1.3 collective-permute-start.5
  33.9 5.3 %collective-permute-start.16 = (bf16[256,512]{1,0:T(8,128)(2,1)S(1)}, bf16[256,512]{1,0:T(8,128)(2,1)S(1)}, u32[]{:S(2)}, u32[]{:S(2)}) collective-permute-start(bf16[256,512]{1,0:T(8,128)(2,1)S(1)} %get-tuple-element.67), channel_id=1, source_target_pairs={{0,8},{12,4},{1,9},{13,5},{2,10},{14,6},{3,11},{15,7},{16,24},{28,... | collective-permute-start | bytes 786440 | tf_op jit(solution)/shard_map/ppermute | solution.py:384
  39.8 4.7 %collective-permute-done.5.refs_4_ = bf16[384,512]{1,0:T(8,128)(2,1)S(1)} collective-permute-done((bf16[384,512]{1,0:T(8,128)(2,1)S(1)}, bf16[384,512]{1,0:T(8,128)(2,1)S(1)}, u32[]{:S(2)}, u32[]{:S(2)}) %collective-permute-start.5) | collective-permute-done | bytes 393248 | tf_op jit(solution)/shard_map/ppermute | solution.py:384
  44.5 1.5 collective-permute-start.14
  46.0 1.7 %shard_map.180 = (bf16[384,512]{1,0:T(8,128)(2,1)S(1)}, bf16[384,512]{1,0:T(8,128)(2,1)S(1)}, bf16[384,2048]{1,0:T(8,128)(2,1)S(1)}, f32[1,512]{1,0:T(1,128)S(1)}) custom-call(s32[2]{0:T(128)S(1)} %pad_add_fusion.place, bf16[384,512]{1,0:T(8,128)(2,1)S(1)} %copy-done.13, bf16[384,512]{1,0:T(8,128)(2,1)S(1)} %collective-permute-done.refs_0_.refs_1_, ...), custom_call_target="tpu_custom_call" | custom-call | flops 1 | bytes 1 | tf_op jit(solution)/shard_map/pallas_call | solution.py:118
  47.8 3.5 %collective-permute-done.14 = bf16[256,512]{1,0:T(8,128)(2,1)S(1)} collective-permute-done((bf16[256,512]{1,0:T(8,128)(2,1)S(1)}, bf16[256,512]{1,0:T(8,128)(2,1)S(1)}, u32[]{:S(2)}, u32[]{:S(2)}) %collective-permute-start.14) | collective-permute-done | bytes 262176 | tf_op jit(solution)/shard_map/ppermute | solution.py:384
  52.8 9.3 %collective-permute-start.11 = (bf16[384,512]{1,0:T(8,128)(2,1)S(1)}, bf16[384,512]{1,0:T(8,128)(2,1)S(1)}, u32[]{:S(2)}, u32[]{:S(2)}) collective-permute-start(bf16[384,512]{1,0:T(8,128)(2,1)S(1)} %get-tuple-element.61.refs_0_.refs_2_), channel_id=1, source_target_pairs={{0,8},{12,4},{1,9},{13,5},{2,10},{14,6},{3,11},{15,7},{16,24},{28,... | collective-permute-start | bytes 1179656 | tf_op jit(solution)/shard_map/ppermute | solution.py:384
  62.2 1.3 collective-permute-start.9
  63.5 1.0 shard_map.182.refs_0_
  65.3 6.4 %collective-permute-done.11.refs_3_ = bf16[384,512]{1,0:T(8,128)(2,1)S(1)} collective-permute-done((bf16[384,512]{1,0:T(8,128)(2,1)S(1)}, bf16[384,512]{1,0:T(8,128)(2,1)S(1)}, u32[]{:S(2)}, u32[]{:S(2)}) %collective-permute-start.11) | collective-permute-done | bytes 393248 | tf_op jit(solution)/shard_map/ppermute | solution.py:384
  71.7 7.7 %collective-permute-done.9.refs_1_ = bf16[384,512]{1,0:T(8,128)(2,1)S(1)} collective-permute-done((bf16[384,512]{1,0:T(8,128)(2,1)S(1)}, bf16[384,512]{1,0:T(8,128)(2,1)S(1)}, u32[]{:S(2)}, u32[]{:S(2)}) %collective-permute-start.9) | collective-permute-done | bytes 393248 | tf_op jit(solution)/shard_map/ppermute | solution.py:384
  80.1 2.4 %shard_map.183.refs_0_ = bf16[384,1024]{1,0:T(8,128)(2,1)S(1)} custom-call(s32[2]{0:T(128)S(1)} %pad_add_fusion.place, bf16[384,512]{1,0:T(8,128)(2,1)S(1)} %get-tuple-element.61.refs_0_.refs_2_, bf16[384,512]{1,0:T(8,128)(2,1)S(1)} %collective-permute-done.9.refs_1_, bf16[384,512]{1,0:T(8,128)(2,1)S(1)} %collective-permute-done.10.refs_2_, ...), custom_call_target="tpu_custom_call" | custom-call | flops 1 | bytes 1 | tf_op jit(solution)/shard_map/pallas_call | solution.py:118
  82.5 1.3 collective-permute-start.20
  84.5 1.3 collective-permute-start.22
  85.8 21.7 %collective-permute-done.20.refs_1_ = bf16[384,1024]{1,0:T(8,128)(2,1)S(1)} collective-permute-done((bf16[384,1024]{1,0:T(8,128)(2,1)S(1)}, bf16[384,1024]{1,0:T(8,128)(2,1)S(1)}, u32[]{:S(2)}, u32[]{:S(2)}) %collective-permute-start.20) | collective-permute-done | bytes 786464 | tf_op jit(solution)/shard_map/ppermute | solution.py:384
  107.5 2.3 %shard_map.184 = (f32[384,512]{1,0:T(8,128)S(1)}, bf16[384,1024]{1,0:T(8,128)(2,1)S(1)}, f32[264,512]{1,0:T(8,128)S(1)}, f32[256,512]{1,0:T(8,128)}, f32[256,512]{1,0:T(8,128)S(1)}, /*index=5*/f32[256,512]{1,0:T(8,128)S(1)}) custom-call(s32[2]{0:T(128)S(1)} %pad_add_fusion.place, bf16[384,1024]{1,0:T(8,128)(2,1)S(1)} %shard_map.183.refs_0_, ...), custom_call_target="tpu_custom_call" | custom-call | flops 1 | bytes 1 | tf_op jit(solution)/shard_map/pallas_call | solution.py:118
  109.9 1.9 %collective-permute-done.23.refs_1_ = f32[264,512]{1,0:T(8,128)S(1)} collective-permute-done((f32[264,512]{1,0:T(8,128)S(1)}, f32[264,512]{1,0:T(8,128)S(1)}, u32[]{:S(2)}, u32[]{:S(2)}) %collective-permute-start.23) | collective-permute-done | bytes 540704 | tf_op jit(solution)/shard_map/ppermute | solution.py:388
  112.5 1.1 collective-permute-start.24
  113.6 14.0 %collective-permute-done.22.refs_1_ = bf16[384,1024]{1,0:T(8,128)(2,1)S(1)} collective-permute-done((bf16[384,1024]{1,0:T(8,128)(2,1)S(1)}, bf16[384,1024]{1,0:T(8,128)(2,1)S(1)}, u32[]{:S(2)}, u32[]{:S(2)}) %collective-permute-start.22) | collective-permute-done | bytes 786464 | tf_op jit(solution)/shard_map/ppermute | solution.py:384
  127.5 2.2 %shard_map.186 = (bf16[384,1024]{1,0:T(8,128)(2,1)S(1)}, f32[264,512]{1,0:T(8,128)}, f32[256,512]{1,0:T(8,128)S(1)}, f32[256,512]{1,0:T(8,128)S(1)}, f32[256,512]{1,0:T(8,128)S(1)}) custom-call(s32[2]{0:T(128)S(1)} %pad_add_fusion.place, bf16[384,1024]{1,0:T(8,128)(2,1)S(1)} %collective-permute-done.21.refs_8_.refs_0_, ...), custom_call_target="tpu_custom_call" | custom-call | flops 1 | bytes 1 | tf_op jit(solution)/shard_map/pallas_call | solution.py:118
  129.7 0.8 copy-done.9
  130.5 1.0 collective-permute-start.25
  131.5 2.8 %collective-permute-done.25 = f32[8,512]{1,0:T(8,128)S(1)} collective-permute-done((f32[8,512]{1,0:T(8,128)S(1)}, f32[8,512]{1,0:T(8,128)S(1)}, u32[]{:S(2)}, u32[]{:S(2)}) %collective-permute-start.25) | collective-permute-done | bytes 16416 | tf_op jit(solution)/shard_map/ppermute | solution.py:388
  134.3 2.0 %shard_map.187 = (bf16[384,512]{1,0:T(8,128)(2,1)S(1)}, f32[1,512]{1,0:T(1,128)S(1)}, f32[1,512]{1,0:T(1,128)S(1)}, bf16[384,512]{1,0:T(8,128)(2,1)}) custom-call(s32[2]{0:T(128)S(1)} %pad_add_fusion.place, bf16[384,1024]{1,0:T(8,128)(2,1)S(1)} %get-tuple-element.73.refs_0_, bf16[384,1024]{1,0:T(8,128)(2,1)S(1)} %get-tuple-element.77.refs_1_, ...), custom_call_target="tpu_custom_call" | custom-call | flops 1 | bytes 1 | tf_op jit(solution)/shard_map/pallas_call | solution.py:118
  136.3 2.7 %shard_map.188 = (f32[520,512]{1,0:T(8,128)}, f32[512,512]{1,0:T(8,128)S(1)}, f32[512,512]{1,0:T(8,128)S(1)}, f32[512,512]{1,0:T(8,128)S(1)}) custom-call(s32[2]{0:T(128)S(1)} %pad_add_fusion.place, bf16[2048,384]{1,0:T(8,128)(2,1)S(1)} %shard_map.182.refs_0_, bf16[384,512]{1,0:T(8,128)(2,1)S(1)} %get-tuple-element.84.refs_1_, ...), custom_call_target="tpu_custom_call" | custom-call | flops 1 | bytes 1 | tf_op jit(solution)/shard_map/pallas_call | solution.py:118
  139.0 1.0 copy-done.5
  140.0 1.0 copy-done.16
  142.0 3.2 %collective-permute-done.27.refs_1_ = f32[264,512]{1,0:T(8,128)} collective-permute-done((f32[264,512]{1,0:T(8,128)}, f32[264,512]{1,0:T(8,128)}, u32[]{:S(2)}, u32[]{:S(2)}) %collective-permute-start.27) | collective-permute-done | bytes 540704 | tf_op jit(solution)/shard_map/ppermute | solution.py:388
  145.2 1.0 copy-done.8
  146.2 1.2 shard_map.189
  147.5 1.1 collective-permute-start.33
  148.6 0.8 shard_map.190
  149.4 1.1 collective-permute-start.30
  150.5 1.2 multiply_add_fusion.3.near
  151.9 1.0 collective-permute-start.29
  152.9 4.5 %collective-permute-done.30 = f32[16,512]{1,0:T(8,128)S(1)} collective-permute-done((f32[16,512]{1,0:T(8,128)S(1)}, f32[16,512]{1,0:T(8,128)S(1)}, u32[]{:S(2)}, u32[]{:S(2)}) %collective-permute-start.30) | collective-permute-done | bytes 32800 | tf_op jit(solution)/shard_map/ppermute | solution.py:388
  157.7 2.9 %shard_map.191 = (f32[512,512]{1,0:T(8,128)}, f32[512,512]{1,0:T(8,128)}, f32[512,512]{1,0:T(8,128)}) custom-call(s32[2]{0:T(128)S(1)} %pad_add_fusion.place, f32[512,512]{1,0:T(8,128)S(1)} %copy-done, f32[512,512]{1,0:T(8,128)S(1)} %copy-done.3, f32[512,512]{1,0:T(8,128)S(1)} %copy-done.4, f32[256,512]{1,0:T(8,128)S(1)} %multiply_add_fusion.3.near, ...), custom_call_target="tpu_custom_call" | custom-call | flops 1 | bytes 1 | tf_op jit(solution)/shard_map/pallas_call | solution.py:568
  161.1 7.0 %collective-permute-done.29 = f16[512,512]{1,0:T(8,128)(2,1)S(1)} collective-permute-done((f16[512,512]{1,0:T(8,128)(2,1)S(1)}, f16[512,512]{1,0:T(8,128)(2,1)S(1)}, u32[]{:S(2)}, u32[]{:S(2)}) %collective-permute-start.29) | collective-permute-done | bytes 524320 | tf_op jit(solution)/shard_map/ppermute | solution.py:388
  168.1 2.3 %divide_subtract_fusion = (f32[512,512]{1,0:T(8,128)}, f32[512,512]{1,0:T(8,128)}, f32[512,512]{1,0:T(8,128)}) fusion(f32[512,512]{1,0:T(8,128)S(1)} %copy-done.2, f32[512]{0:T(512)S(1)} %bitcast.15, f16[512,512]{1,0:T(8,128)(2,1)S(1)} %collective-permute-done.29, f32[512,512]{1,0:T(8,128)S(1)} %get-tuple-element.94, ...), kind=kLoop, calls=%fused_computation.2 | loop fusion | flops 4194304 | bytes 8914944 | tf_op jit(solution)/shard_map/sub | solution.py:27
  (93 shorter events, 11.8 us)
Async XLA Ops:
  0.6 4.7 %copy-start = (f32[512,512]{1,0:T(8,128)S(1)}, f32[512,512]{1,0:T(8,128)}, u32[]{:S(2)}) copy-start(f32[512,512]{1,0:T(8,128)} %param.20) | copy-start | bytes 3145732
  2.7 6.4 %copy-start.13 = (bf16[384,512]{1,0:T(8,128)(2,1)S(1)}, bf16[384,512]{1,0:T(8,128)(2,1)}, u32[]{:S(2)}) copy-start(bf16[384,512]{1,0:T(8,128)(2,1)} %refs_0_.5) | copy-start | bytes 1179652
  3.3 2.1 %collective-permute-start.3 = (bf16[528,512]{1,0:T(8,128)(2,1)S(1)}, bf16[528,512]{1,0:T(8,128)(2,1)S(1)}, u32[]{:S(2)}, u32[]{:S(2)}) collective-permute-start(bf16[528,512]{1,0:T(8,128)(2,1)S(1)} %shard_map.177.refs_6_), channel_id=1, source_target_pairs={{0,1},{1,0},{2,3},{3,2},{4,5},{5,4},{6,7},{7,6},{8,9},{9,8},{10,11... | collective-permute-start | bytes 1622024 | tf_op jit(solution)/shard_map/ppermute | solution.py:388
  6.0 24.6 %collective-permute-start.4 = (bf16[528,512]{1,0:T(8,128)(2,1)S(1)}, bf16[528,512]{1,0:T(8,128)(2,1)S(1)}, u32[]{:S(2)}, u32[]{:S(2)}) collective-permute-start(bf16[528,512]{1,0:T(8,128)(2,1)S(1)} %shard_map.178.refs_0_.refs_4_), channel_id=1, source_target_pairs={{0,1},{1,0},{2,3},{3,2},{4,5},{5,4},{6,7},{7,6},{8,9},{9,8},{10,11... | collective-permute-start | bytes 1622024 | tf_op jit(solution)/shard_map/ppermute | solution.py:388
  6.5 26.1 %collective-permute-start.7 = (bf16[528,512]{1,0:T(8,128)(2,1)S(1)}, bf16[528,512]{1,0:T(8,128)(2,1)S(1)}, u32[]{:S(2)}, u32[]{:S(2)}) collective-permute-start(bf16[528,512]{1,0:T(8,128)(2,1)S(1)} %shard_map.177.refs_6_), channel_id=1, source_target_pairs={{0,2},{1,3},{2,0},{3,1},{4,6},{5,7},{6,4},{7,5},{8,10},{9,11},{10,... | collective-permute-start | bytes 1622024 | tf_op jit(solution)/shard_map/ppermute | solution.py:388
  9.1 14.0 %collective-permute-start.2 = (bf16[384,512]{1,0:T(8,128)(2,1)S(1)}, bf16[384,512]{1,0:T(8,128)(2,1)S(1)}, u32[]{:S(2)}, u32[]{:S(2)}) collective-permute-start(bf16[384,512]{1,0:T(8,128)(2,1)S(1)} %copy-done.13), channel_id=1, source_target_pairs={{0,8},{12,4},{1,9},{13,5},{2,10},{14,6},{3,11},{15,7},{16,24},{28,... | collective-permute-start | bytes 1179656 | tf_op jit(solution)/shard_map/ppermute | solution.py:384
  13.6 17.0 %collective-permute-start = (bf16[384,512]{1,0:T(8,128)(2,1)S(1)}, bf16[384,512]{1,0:T(8,128)(2,1)S(1)}, u32[]{:S(2)}, u32[]{:S(2)}) collective-permute-start(bf16[384,512]{1,0:T(8,128)(2,1)S(1)} %copy-done.13), channel_id=1, source_target_pairs={{0,4},{4,8},{8,12},{1,5},{5,9},{9,13},{2,6},{6,10},{10,14},{3,7},{... | collective-permute-start | bytes 1179656 | tf_op jit(solution)/shard_map/ppermute | solution.py:384
  14.9 15.7 %collective-permute-start.1 = (bf16[384,512]{1,0:T(8,128)(2,1)S(1)}, bf16[384,512]{1,0:T(8,128)(2,1)S(1)}, u32[]{:S(2)}, u32[]{:S(2)}) collective-permute-start(bf16[384,512]{1,0:T(8,128)(2,1)S(1)} %copy-done.13), channel_id=1, source_target_pairs={{4,0},{8,4},{12,8},{5,1},{9,5},{13,9},{6,2},{10,6},{14,10},{7,3},{... | collective-permute-start | bytes 1179656 | tf_op jit(solution)/shard_map/ppermute | solution.py:384
  23.1 16.0 %collective-permute-start.6 = (bf16[384,512]{1,0:T(8,128)(2,1)S(1)}, bf16[384,512]{1,0:T(8,128)(2,1)S(1)}, u32[]{:S(2)}, u32[]{:S(2)}) collective-permute-start(bf16[384,512]{1,0:T(8,128)(2,1)S(1)} %collective-permute-done.2.refs_3_), channel_id=1, source_target_pairs={{4,0},{8,12},{5,1},{9,13},{6,2},{10,14},{7,3},{11,15},{20,16},{24,... | collective-permute-start | bytes 1179656 | tf_op jit(solution)/shard_map/ppermute | solution.py:384
  31.3 13.2 %collective-permute-start.5 = (bf16[384,512]{1,0:T(8,128)(2,1)S(1)}, bf16[384,512]{1,0:T(8,128)(2,1)S(1)}, u32[]{:S(2)}, u32[]{:S(2)}) collective-permute-start(bf16[384,512]{1,0:T(8,128)(2,1)S(1)} %shard_map.179.refs_1_), channel_id=1, source_target_pairs={{4,0},{8,12},{5,1},{9,13},{6,2},{10,14},{7,3},{11,15},{20,16},{24,... | collective-permute-start | bytes 1179656 | tf_op jit(solution)/shard_map/ppermute | solution.py:384
  32.6 13.4 %collective-permute-start.8 = (bf16[528,512]{1,0:T(8,128)(2,1)S(1)}, bf16[528,512]{1,0:T(8,128)(2,1)S(1)}, u32[]{:S(2)}, u32[]{:S(2)}) collective-permute-start(bf16[528,512]{1,0:T(8,128)(2,1)S(1)} %collective-permute-done.7.refs_8_), channel_id=1, source_target_pairs={{0,1},{1,0},{2,3},{3,2},{4,5},{5,4},{6,7},{7,6},{8,9},{9,8},{10,11... | collective-permute-start | bytes 1622024 | tf_op jit(solution)/shard_map/ppermute | solution.py:388
  32.6 15.1 %collective-permute-start.12 = (bf16[528,512]{1,0:T(8,128)(2,1)S(1)}, bf16[528,512]{1,0:T(8,128)(2,1)S(1)}, u32[]{:S(2)}, u32[]{:S(2)}) collective-permute-start(bf16[528,512]{1,0:T(8,128)(2,1)S(1)} %shard_map.178.refs_0_.refs_4_), channel_id=1, source_target_pairs={{0,2},{1,3},{2,0},{3,1},{4,6},{5,7},{6,4},{7,5},{8,10},{9,11},{10,... | collective-permute-start | bytes 1622024 | tf_op jit(solution)/shard_map/ppermute | solution.py:388
  33.9 13.9 %collective-permute-start.16 = (bf16[256,512]{1,0:T(8,128)(2,1)S(1)}, bf16[256,512]{1,0:T(8,128)(2,1)S(1)}, u32[]{:S(2)}, u32[]{:S(2)}) collective-permute-start(bf16[256,512]{1,0:T(8,128)(2,1)S(1)} %get-tuple-element.67), channel_id=1, source_target_pairs={{0,8},{12,4},{1,9},{13,5},{2,10},{14,6},{3,11},{15,7},{16,24},{28,... | collective-permute-start | bytes 786440 | tf_op jit(solution)/shard_map/ppermute | solution.py:384
  39.1 8.6 %collective-permute-start.15 = (bf16[256,512]{1,0:T(8,128)(2,1)S(1)}, bf16[256,512]{1,0:T(8,128)(2,1)S(1)}, u32[]{:S(2)}, u32[]{:S(2)}) collective-permute-start(bf16[256,512]{1,0:T(8,128)(2,1)S(1)} %get-tuple-element.65), channel_id=1, source_target_pairs={{8,4},{12,8},{9,5},{13,9},{10,6},{14,10},{11,7},{15,11},{24,20},{2... | collective-permute-start | bytes 786440 | tf_op jit(solution)/shard_map/ppermute | solution.py:384
  44.5 6.8 %collective-permute-start.14 = (bf16[256,512]{1,0:T(8,128)(2,1)S(1)}, bf16[256,512]{1,0:T(8,128)(2,1)S(1)}, u32[]{:S(2)}, u32[]{:S(2)}) collective-permute-start(bf16[256,512]{1,0:T(8,128)(2,1)S(1)} %get-tuple-element.63), channel_id=1, source_target_pairs={{0,4},{4,8},{1,5},{5,9},{2,6},{6,10},{3,7},{7,11},{16,20},{20,24},... | collective-permute-start | bytes 786440 | tf_op jit(solution)/shard_map/ppermute | solution.py:384
  51.3 28.0 %collective-permute-start.18 = (bf16[768,512]{1,0:T(8,128)(2,1)S(1)}, bf16[768,512]{1,0:T(8,128)(2,1)S(1)}, u32[]{:S(2)}, u32[]{:S(2)}) collective-permute-start(bf16[768,512]{1,0:T(8,128)(2,1)S(1)} %constant_dynamic-update-slice_fusion.refs_8_), channel_id=1, source_target_pairs={{4,6},{5,7},{6,4},{7,5},{8,10},{9,11},{10,8},{11,9},{20,22},{21,23... | collective-permute-start | bytes 2359304 | tf_op jit(solution)/shard_map/ppermute | solution.py:388
  52.1 12.5 %collective-permute-start.13 = (bf16[528,512]{1,0:T(8,128)(2,1)S(1)}, bf16[528,512]{1,0:T(8,128)(2,1)S(1)}, u32[]{:S(2)}, u32[]{:S(2)}) collective-permute-start(bf16[528,512]{1,0:T(8,128)(2,1)S(1)} %collective-permute-done.12.refs_6_), channel_id=1, source_target_pairs={{0,1},{1,0},{2,3},{3,2},{4,5},{5,4},{6,7},{7,6},{8,9},{9,8},{10,11... | collective-permute-start | bytes 1622024 | tf_op jit(solution)/shard_map/ppermute | solution.py:388
  52.1 13.1 %collective-permute-start.10 = (bf16[384,512]{1,0:T(8,128)(2,1)S(1)}, bf16[384,512]{1,0:T(8,128)(2,1)S(1)}, u32[]{:S(2)}, u32[]{:S(2)}) collective-permute-start(bf16[384,512]{1,0:T(8,128)(2,1)S(1)} %get-tuple-element.61.refs_0_.refs_2_), channel_id=1, source_target_pairs={{8,4},{12,8},{9,5},{13,9},{10,6},{14,10},{11,7},{15,11},{24,20},{2... | collective-permute-start | bytes 1179656 | tf_op jit(solution)/shard_map/ppermute | solution.py:384
  52.8 18.8 %collective-permute-start.11 = (bf16[384,512]{1,0:T(8,128)(2,1)S(1)}, bf16[384,512]{1,0:T(8,128)(2,1)S(1)}, u32[]{:S(2)}, u32[]{:S(2)}) collective-permute-start(bf16[384,512]{1,0:T(8,128)(2,1)S(1)} %get-tuple-element.61.refs_0_.refs_2_), channel_id=1, source_target_pairs={{0,8},{12,4},{1,9},{13,5},{2,10},{14,6},{3,11},{15,7},{16,24},{28,... | collective-permute-start | bytes 1179656 | tf_op jit(solution)/shard_map/ppermute | solution.py:384
  62.2 17.2 %collective-permute-start.9 = (bf16[384,512]{1,0:T(8,128)(2,1)S(1)}, bf16[384,512]{1,0:T(8,128)(2,1)S(1)}, u32[]{:S(2)}, u32[]{:S(2)}) collective-permute-start(bf16[384,512]{1,0:T(8,128)(2,1)S(1)} %get-tuple-element.61.refs_0_.refs_2_), channel_id=1, source_target_pairs={{0,4},{4,8},{1,5},{5,9},{2,6},{6,10},{3,7},{7,11},{16,20},{20,24},... | collective-permute-start | bytes 1179656 | tf_op jit(solution)/shard_map/ppermute | solution.py:384
  64.5 15.5 %collective-permute-start.17 = (bf16[768,512]{1,0:T(8,128)(2,1)S(1)}, bf16[768,512]{1,0:T(8,128)(2,1)S(1)}, u32[]{:S(2)}, u32[]{:S(2)}) collective-permute-start(bf16[768,512]{1,0:T(8,128)(2,1)S(1)} %constant_dynamic-update-slice_fusion.refs_8_), channel_id=1, source_target_pairs={{4,5},{5,4},{6,7},{7,6},{8,9},{9,8},{10,11},{11,10},{20,21},{21,20... | collective-permute-start | bytes 2359304 | tf_op jit(solution)/shard_map/ppermute | solution.py:388
  79.4 0.7 collective-permute-start.19
  82.5 25.0 %collective-permute-start.20 = (bf16[384,1024]{1,0:T(8,128)(2,1)S(1)}, bf16[384,1024]{1,0:T(8,128)(2,1)S(1)}, u32[]{:S(2)}, u32[]{:S(2)}) collective-permute-start(bf16[384,1024]{1,0:T(8,128)(2,1)S(1)} %shard_map.183.refs_0_), channel_id=1, source_target_pairs={{4,0},{8,12},{5,1},{9,13},{6,2},{10,14},{7,3},{11,15},{20,16},{24,... | collective-permute-start | bytes 2359304 | tf_op jit(solution)/shard_map/ppermute | solution.py:384
  83.8 23.7 %collective-permute-start.21 = (bf16[384,1024]{1,0:T(8,128)(2,1)S(1)}, bf16[384,1024]{1,0:T(8,128)(2,1)S(1)}, u32[]{:S(2)}, u32[]{:S(2)}) collective-permute-start(bf16[384,1024]{1,0:T(8,128)(2,1)S(1)} %shard_map.183.refs_0_), channel_id=1, source_target_pairs={{4,8},{8,4},{5,9},{9,5},{6,10},{10,6},{7,11},{11,7},{20,24},{24,20... | collective-permute-start | bytes 2359304 | tf_op jit(solution)/shard_map/ppermute | solution.py:384
  84.5 43.0 %collective-permute-start.22 = (bf16[384,1024]{1,0:T(8,128)(2,1)S(1)}, bf16[384,1024]{1,0:T(8,128)(2,1)S(1)}, u32[]{:S(2)}, u32[]{:S(2)}) collective-permute-start(bf16[384,1024]{1,0:T(8,128)(2,1)S(1)} %shard_map.183.refs_0_), channel_id=1, source_target_pairs={{8,0},{4,12},{9,1},{5,13},{10,2},{6,14},{11,3},{7,15},{24,16},{20,... | collective-permute-start | bytes 2359304 | tf_op jit(solution)/shard_map/ppermute | solution.py:384
  109.9 19.9 %copy-start.11 = (f32[256,512]{1,0:T(8,128)}, f32[256,512]{1,0:T(8,128)S(1)}, u32[]{:S(2)}) copy-start(f32[256,512]{1,0:T(8,128)S(1)} %get-tuple-element.101) | copy-start | bytes 1572868
  109.9 1.9 %collective-permute-start.23 = (f32[264,512]{1,0:T(8,128)S(1)}, f32[264,512]{1,0:T(8,128)S(1)}, u32[]{:S(2)}, u32[]{:S(2)}) collective-permute-start(f32[264,512]{1,0:T(8,128)S(1)} %get-tuple-element.75), channel_id=1, source_target_pairs={{0,1},{1,0},{2,3},{3,2},{4,5},{5,4},{6,7},{7,6},{8,9},{9,8},{10,11... | collective-permute-start | bytes 1622024 | tf_op jit(solution)/shard_map/ppermute | solution.py:388
  112.5 21.8 %collective-permute-start.24 = (f16[256,512]{1,0:T(8,128)(2,1)S(1)}, f16[256,512]{1,0:T(8,128)(2,1)S(1)}, u32[]{:S(2)}, u32[]{:S(2)}) collective-permute-start(f16[256,512]{1,0:T(8,128)(2,1)S(1)} %convert_element_type.18), channel_id=1, source_target_pairs={{0,2},{1,3},{2,0},{3,1},{4,6},{5,7},{6,4},{7,5},{8,10},{9,11},{10,... | collective-permute-start | bytes 786440 | tf_op jit(solution)/shard_map/ppermute | solution.py:388
  130.5 5.7 %copy-start.7 = (f32[256,512]{1,0:T(8,128)}, f32[256,512]{1,0:T(8,128)S(1)}, u32[]{:S(2)}) copy-start(f32[256,512]{1,0:T(8,128)S(1)} %get-tuple-element.88.refs_0_) | copy-start | bytes 1572868
  130.5 5.7 %copy-start.17 = (f32[256,512]{1,0:T(8,128)}, f32[256,512]{1,0:T(8,128)S(1)}, u32[]{:S(2)}) copy-start(f32[256,512]{1,0:T(8,128)S(1)} %get-tuple-element.104) | copy-start | bytes 1572868
  130.5 3.7 %collective-permute-start.25 = (f32[8,512]{1,0:T(8,128)S(1)}, f32[8,512]{1,0:T(8,128)S(1)}, u32[]{:S(2)}, u32[]{:S(2)}) collective-permute-start(f32[8,512]{1,0:T(8,128)S(1)} %get-tuple-element.80), channel_id=1, source_target_pairs={{0,2},{1,3},{2,0},{3,1},{4,6},{5,7},{6,4},{7,5},{8,10},{9,11},{10,... | collective-permute-start | bytes 49160 | tf_op jit(solution)/shard_map/ppermute | solution.py:388
  141.0 7.6 %collective-permute-start.26 = (f32[520,512]{1,0:T(8,128)}, f32[520,512]{1,0:T(8,128)S(1)}, u32[]{:S(2)}, u32[]{:S(2)}) collective-permute-start(f32[520,512]{1,0:T(8,128)} %get-tuple-element.87), channel_id=1, source_target_pairs={{0,1},{1,0},{2,3},{3,2},{4,5},{5,4},{6,7},{7,6},{8,9},{9,8},{10,11... | collective-permute-start | bytes 3194888 | tf_op jit(solution)/shard_map/ppermute | solution.py:388
  141.0 4.2 %collective-permute-start.27 = (f32[264,512]{1,0:T(8,128)}, f32[264,512]{1,0:T(8,128)}, u32[]{:S(2)}, u32[]{:S(2)}) collective-permute-start(f32[264,512]{1,0:T(8,128)} %get-tuple-element.89), channel_id=1, source_target_pairs={{0,1},{1,0},{2,3},{3,2},{4,5},{5,4},{6,7},{7,6},{8,9},{9,8},{10,11... | collective-permute-start | bytes 1622024 | tf_op jit(solution)/shard_map/ppermute | solution.py:388
  141.5 9.0 %collective-permute-start.31 = (f32[256,512]{1,0:T(8,128)}, f32[256,512]{1,0:T(8,128)}, u32[]{:S(2)}, u32[]{:S(2)}) collective-permute-start(f32[256,512]{1,0:T(8,128)} %get-tuple-element.102), channel_id=1, source_target_pairs={{0,1},{1,0},{2,3},{3,2},{4,5},{5,4},{6,7},{7,6},{8,9},{9,8},{10,11... | collective-permute-start | bytes 1572872 | tf_op jit(solution)/shard_map/ppermute | solution.py:388
  141.5 7.1 %copy-start.6 = (f32[512,512]{1,0:T(8,128)S(1)}, f32[512,512]{1,0:T(8,128)}, u32[]{:S(2)}) copy-start(f32[512,512]{1,0:T(8,128)} %copy-done.5) | copy-start | bytes 3145732
  141.5 15.9 %collective-permute-start.32 = (f32[256,512]{1,0:T(8,128)}, f32[256,512]{1,0:T(8,128)S(1)}, u32[]{:S(2)}, u32[]{:S(2)}) collective-permute-start(f32[256,512]{1,0:T(8,128)} %copy-done.17), channel_id=1, source_target_pairs={{0,1},{1,0},{2,3},{3,2},{4,5},{5,4},{6,7},{7,6},{8,9},{9,8},{10,11... | collective-permute-start | bytes 1572872 | tf_op jit(solution)/shard_map/ppermute | solution.py:388
  142.0 19.1 %collective-permute-start.28 = (f32[512,512]{1,0:T(8,128)}, f32[512,512]{1,0:T(8,128)S(1)}, u32[]{:S(2)}, u32[]{:S(2)}) collective-permute-start(f32[512,512]{1,0:T(8,128)} %copy-done.16), channel_id=1, source_target_pairs={{0,1},{1,0},{2,3},{3,2},{4,5},{5,4},{6,7},{7,6},{8,9},{9,8},{10,11... | collective-permute-start | bytes 3145736 | tf_op jit(solution)/shard_map/ppermute | solution.py:388
  147.4 3.1 %copy-start.12 = (f32[256,512]{1,0:T(8,128)S(1)}, f32[256,512]{1,0:T(8,128)}, u32[]{:S(2)}) copy-start(f32[256,512]{1,0:T(8,128)} %copy-done.11) | copy-start | bytes 1572868
  147.5 9.9 %collective-permute-start.33 = (f16[256,512]{1,0:T(8,128)(2,1)S(1)}, f16[256,512]{1,0:T(8,128)(2,1)S(1)}, u32[]{:S(2)}, u32[]{:S(2)}) collective-permute-start(f16[256,512]{1,0:T(8,128)(2,1)S(1)} %convert_element_type.22), channel_id=1, source_target_pairs={{0,2},{1,3},{2,0},{3,1},{4,6},{5,7},{6,4},{7,5},{8,10},{9,11},{10,... | collective-permute-start | bytes 786440 | tf_op jit(solution)/shard_map/ppermute | solution.py:388
  149.4 8.0 %collective-permute-start.30 = (f32[16,512]{1,0:T(8,128)S(1)}, f32[16,512]{1,0:T(8,128)S(1)}, u32[]{:S(2)}, u32[]{:S(2)}) collective-permute-start(f32[16,512]{1,0:T(8,128)S(1)} %get-tuple-element.91), channel_id=1, source_target_pairs={{0,2},{1,3},{2,0},{3,1},{4,6},{5,7},{6,4},{7,5},{8,10},{9,11},{10,... | collective-permute-start | bytes 98312 | tf_op jit(solution)/shard_map/ppermute | solution.py:388
  150.5 6.9 %copy-start.10 = (f32[256,512]{1,0:T(8,128)S(1)}, f32[256,512]{1,0:T(8,128)}, u32[]{:S(2)}) copy-start(f32[256,512]{1,0:T(8,128)} %copy-done.9) | copy-start | bytes 1572868
  151.7 5.8 %copy-start.3 = (f32[512,512]{1,0:T(8,128)S(1)}, f32[512,512]{1,0:T(8,128)}, u32[]{:S(2)}) copy-start(f32[512,512]{1,0:T(8,128)} %moment) | copy-start | bytes 3145732
  151.8 5.8 %copy-start.4 = (f32[512,512]{1,0:T(8,128)S(1)}, f32[512,512]{1,0:T(8,128)}, u32[]{:S(2)}) copy-start(f32[512,512]{1,0:T(8,128)} %square) | copy-start | bytes 3145732
  151.9 16.2 %collective-permute-start.29 = (f16[512,512]{1,0:T(8,128)(2,1)S(1)}, f16[512,512]{1,0:T(8,128)(2,1)S(1)}, u32[]{:S(2)}, u32[]{:S(2)}) collective-permute-start(f16[512,512]{1,0:T(8,128)(2,1)S(1)} %convert_element_type.19), channel_id=1, source_target_pairs={{0,2},{1,3},{2,0},{3,1},{4,6},{5,7},{6,4},{7,5},{8,10},{9,11},{10,... | collective-permute-start | bytes 1572872 | tf_op jit(solution)/shard_map/ppermute | solution.py:388
  157.6 3.0 %copy-start.15 = (f32[128]{0:T(128)S(1)}, f32[128]{0:T(128)}, u32[]{:S(2)}) copy-start(f32[128]{0:T(128)} %param.12) | copy-start | bytes 1540
  157.6 10.5 %copy-start.2 = (f32[512,512]{1,0:T(8,128)S(1)}, f32[512,512]{1,0:T(8,128)}, u32[]{:S(2)}) copy-start(f32[512,512]{1,0:T(8,128)} %refs_0_.3) | copy-start | bytes 3145732
  157.6 10.4 %copy-start.18 = (f32[512,512]{1,0:T(8,128)S(1)}, f32[512,512]{1,0:T(8,128)}, u32[]{:S(2)}) copy-start(f32[512,512]{1,0:T(8,128)} %param.14) | copy-start | bytes 3145732
  157.6 10.4 %copy-start.19 = (f32[512,512]{1,0:T(8,128)S(1)}, f32[512,512]{1,0:T(8,128)}, u32[]{:S(2)}) copy-start(f32[512,512]{1,0:T(8,128)} %param.15) | copy-start | bytes 3145732
  (8 other events, 11.6 us)

commit v6 on v5

--- a/solution.py
+++ b/solution.py
@@ -115,13 +115,14 @@
     def run(place, *refs):
         body(place, *refs[: len(args)], *refs[len(args) + len(after) :])
 
+    held = sum(a.size * jnp.dtype(a.dtype).itemsize for a in (*args, *outs))
     return pl.pallas_call(
         run,
         out_shape=outs,
         in_specs=[SMEM] + [VMEM] * len(args) + [ANY] * len(after),
         out_specs=[VMEM] * len(outs),
         scratch_shapes=scratch,
-        compiler_params=pltpu.CompilerParams(vmem_limit_bytes=24 * 1024 * 1024),
+        compiler_params=pltpu.CompilerParams(vmem_limit_bytes=held + 6 * 1024 * 1024),
         cost_estimate=pl.CostEstimate(flops=1, bytes_accessed=1, transcendentals=0),
     )(place, *args, *after)
 
@@ -267,7 +268,7 @@
         out[...] = end[...]
 
 
-def decoder_grads(scale, i, error, codes, row, outs):
+def decoder_grads(scale, i, error, codes, outs):
     half = error.shape[1] // 4
     for out, slot in zip(outs, (3, 1, 2, 0)):
         out[:half] = scale * lax.dot_general(
@@ -276,7 +277,6 @@
             (((0,), (0,)), ((), ())),
             preferred_element_type=F32,
         )
-    outs[0][half:] = jnp.broadcast_to(row[...], (outs[0].shape[0] - half, row.shape[1]))
 
 
 def back_through(i, error, decs, shift):
@@ -298,42 +298,62 @@
     z, i = place[0], place[1]
     half = mine.shape[1] // 4
     pick(place, mine, passed, near)
-    decoder_grads(-2.0 / rows, i, near, codes, active, outs)
+    decoder_grads(-2.0 / rows, i, near, codes, outs)
+    outs[0][half:] = jnp.broadcast_to(active[...], (outs[0].shape[0] - half, active.shape[1]))
     part[...] = back_through(i, near, (dec0, dec1, dec2, dec3), jnp.where(z >= 2, half, 0))
 
 
-def far_error_body(rows, place, swapped, direct, codes, active, far, *outs):
-    pick(place, swapped, direct, far)
-    decoder_grads(-2.0 / rows, place[1], far, codes, active, outs)
-
-
-def far_code_body(
-    rows, place, near, far, part, mask, dec0, dec1, dec2, dec3, grad_low, bias_sum, norms, home
+def code_grad_body(
+    rows,
+    place,
+    swapped,
+    direct,
+    part,
+    mask,
+    dec0,
+    dec1,
+    dec2,
+    dec3,
+    turned,
+    far,
+    grad_low,
+    bias_sum,
+    norms,
+    send_far,
 ):
     z, i = place[0], place[1]
     half = far.shape[1] // 4
     width = 2 * half
     decs = (dec0, dec1, dec2, dec3)
-    shift = jnp.where(z >= 2, 0, half)
-    total = part[...] + back_through(i, far, decs, shift)
+    pick(place, swapped, direct, far)
+    total = part[...] + back_through(i, far, decs, jnp.where(z >= 2, 0, half))
     squares = functools.reduce(jnp.add, [one_row(dec[width:, :]) for dec in decs])
     column_norms = jnp.sqrt(squares + 1e-06)
     norms[...] = column_norms
     code_grad = (-2.0 / rows) * total + column_norms / rows
     grad = jnp.where(mask[...] > 0, code_grad, 0.0)
     grad_low[...] = grad.astype(BF16)
-    bias_sum[...] = jnp.sum(grad, axis=0, keepdims=True)
+    row = jnp.sum(grad, axis=0, keepdims=True)
+    bias_sum[...] = row
+    encoder_grads(i, turned, grad_low, (3,), (send_far,))
+    send_far[width:] = jnp.broadcast_to(row, (send_far.shape[0] - width, row.shape[1]))
+
+
+def encoder_grads(i, turned, grad_low, slots, outs):
+    width = turned.shape[0] // 4
+    for slot, out in zip(slots, outs):
+        at = pl.ds(pl.multiple_of((i ^ slot) * width, width), width)
+        out[:width] = jnp.dot(turned[at, :], grad_low[...], preferred_element_type=F32)
+
+
+def rest_body(rows, place, turned, grad_low, near, far, codes, home, send, kept_far, kept, *outs):
+    z, i = place[0], place[1]
+    half = far.shape[1] // 4
+    shift = jnp.where(z >= 2, 0, half)
+    encoder_grads(i, turned, grad_low, (2, 1, 0), (kept_far, send, kept))
+    decoder_grads(-2.0 / rows, i, far, codes, outs)
     home[:, columns(half - shift, half)] = near[:, columns(z * half, half)]
     home[:, columns(shift, half)] = far[:, columns(z * half, half)]
-
-
-def encoder_grad_body(place, turned, grad_low, row, send_far, send_near, keep_far, keep_near):
-    i = place[1]
-    width = turned.shape[0] // 4
-    for slot, out in ((3, send_far), (1, send_near), (2, keep_far), (0, keep_near)):
-        at = pl.ds(pl.multiple_of((i ^ slot) * width, width), width)
-        out[:width] = jnp.dot(turned[at, :], grad_low[...], preferred_element_type=F32)
-    send_far[width:] = jnp.broadcast_to(row[...], (send_far.shape[0] - width, row.shape[1]))
 
 
 def far_body(place, kept, received, row, *refs):
@@ -342,7 +362,9 @@
     total = kept[...] + received[:width]
     largest = jnp.maximum(jnp.max(jnp.abs(total), axis=0, keepdims=True), 1e-30)
     scaled[...] = total * (16384.0 / largest)
-    rows = received[width:] + row[...]
+    rows = jnp.broadcast_to(row[...], (8, row.shape[1]))
+    if received.shape[0] > width:
+        rows += received[width:]
     at = lax.broadcasted_iota(jnp.int32, rows.shape, 0)
     small[:8] = jnp.where(at == 0, largest * (1.0 / 16384.0), rows)
     for other in refs[:-2]:
@@ -407,16 +429,16 @@
         decoder,
         after=(enc_core,),
     )
-    dec_chip, dec_core = flip(behind(dec_own, enc_chip), 2), flip(dec_own, 1)
+    dec_chip, dec_core = flip(dec_own, 2), flip(dec_own, 1)
     (onward,) = local_kernel(
-        onward_body, [shape((count, width), BF16)], place, low, high, after=(dec_core,)
+        onward_body, [shape((count, width), BF16)], place, low, high
     )
     relay1 = along(onward, ends)
     relay2 = along(across, ends)
-    enc = [enc_own, enc_core, enc_chip, flip(behind(enc_chip, onward), 1)]
+    enc = [enc_own, enc_core, enc_chip, flip(behind(enc_chip, relay1), 1)]
 
     up, down, beyond = local_kernel(
-        pieces_body, [shape((half, latents), BF16)] * 3, place, dec_own, after=(onward,)
+        pieces_body, [shape((half, latents), BF16)] * 3, place, dec_own
     )
     dec_pieces = [
         along(up, [(0, 1), (1, 2)]),
@@ -425,6 +447,7 @@
     ]
     dec = [dec_own, dec_core, dec_chip, flip(dec_chip, 1)]
 
+    rows_own = jnp.concatenate([behind(piece, dec_chip) for piece in dec_pieces], axis=0)
     codes, mask, inputs, active = local_kernel(
         codes_body,
         [
@@ -441,13 +464,12 @@
         relay1,
         relay2,
         *enc,
+        after=(rows_own,),
         scratch=[pltpu.VMEM((1, latents), F32)],
     )
     codes_low = along(codes, [(0, 1), (1, 2)])
     codes_high = along(codes, [(2, 1), (3, 2)])
     codes_across = along(codes, [(0, 2), (3, 1)])
-    dec_pieces = [behind(piece, codes, dec_chip) for piece in dec_pieces]
-    rows_own = jnp.concatenate(dec_pieces, axis=0)
     (turned,) = local_kernel(turn_body, [shape((features, count), BF16)], place, inputs)
     rows_chip = flip(rows_own, 2, (1, 2))
     rows_core = flip(behind(rows_own, turned), 1, (1, 2))
@@ -474,17 +496,16 @@
     passed = along(own_error, [(1, 0), (2, 3)])
     direct = along(own_error, [(2, 0), (1, 3)])
 
-    def across_chips(scaled, small):
-        return flip(scaled.astype(jnp.float16), 2), flip(small, 2)
-
-    def decoder_half(send_far, send_near, keep_far, keep_near):
+    def decoder_half(send_far, send_near, keep_far, keep_near, *others, after=()):
         scaled, small = local_kernel(
             far_body,
-            [shape((half, latents), F32), shape((8, latents), F32)],
+            [shape((half, latents), F32), shape((8 + 8 * len(others), latents), F32)],
             place,
             keep_far,
             flip(send_far, 1),
             active,
+            *others,
+            after=after,
         )
         return scaled, small, (keep_near, flip(send_near, 1))
 
@@ -501,66 +522,75 @@
         after=(swapped,),
     )
     near_scaled, near_small, near_kept = decoder_half(*near_blocks)
-    far, *far_blocks = local_kernel(
-        functools.partial(far_error_body, rows),
-        [shape((count, features // 2), BF16), *blocks],
-        place,
-        swapped,
-        direct,
-        codes,
-        active,
-        after=(near_scaled,),
-    )
-    near_received = across_chips(near_scaled, behind(near_small, far))
-    far_scaled, far_small, far_kept = decoder_half(*far_blocks)
-    far_received = flip(far_scaled.astype(jnp.float16), 2)
-    grad_low, bias_sum, norms, error = local_kernel(
-        functools.partial(far_code_body, rows),
+    near_received = flip(near_scaled.astype(jnp.float16), 2)
+    far, grad_low, bias_sum, norms, send_far = local_kernel(
+        functools.partial(code_grad_body, rows),
         [
+            shape((count, features // 2), BF16),
             shape((count, latents), BF16),
             shape((1, latents), F32),
             shape((1, latents), F32),
-            shape((count, width), BF16),
+            shape((width + 8, latents), F32),
         ],
         place,
+        swapped,
+        direct,
+        behind(part, near_received),
+        mask,
+        *dec,
+        turned,
+    )
+    error, send_near, keep_far, keep_near, *far_blocks = local_kernel(
+        functools.partial(rest_body, rows),
+        [shape((count, width), BF16)]
+        + [shape((width, latents), F32)] * 3
+        + [shape((half, latents), F32)] * 4,
+        place,
+        turned,
+        grad_low,
         near,
         far,
-        behind(part, *near_received),
-        mask,
-        *dec,
-    )
-    send_far, send_near, keep_far, keep_near = local_kernel(
-        encoder_grad_body,
-        [shape((width + 8, latents), F32)] + [shape((width, latents), F32)] * 3,
-        place,
-        turned,
-        grad_low,
-        bias_sum,
-    )
+        codes,
+    )
+    near_small_received = flip(behind(near_small, far), 2)
     scaled, small = local_kernel(
         far_body,
-        [shape((width, latents), F32), shape((16, latents), F32)],
+        [shape((width, latents), F32), shape((8, latents), F32)],
         place,
         keep_far,
         flip(send_far, 1),
         bias_sum,
-        far_small,
-    )
-    enc_received, enc_small = across_chips(scaled, small)
+    )
+    enc_received = flip(scaled.astype(jnp.float16), 2)
+    far_scaled, small, far_kept = decoder_half(*far_blocks, small, after=(scaled,))
+    far_received = flip(far_scaled.astype(jnp.float16), 2)
+    small_received = behind(flip(small, 2), enc_received)
 
     decoder, dec_moment, dec_square, encoder, enc_moment, enc_square = lax.optimization_barrier(
         (decoder, dec_moment, dec_square, encoder, enc_moment, enc_square, small)
     )[:6]
 
-    def added(kept, received):
-        return kept[0] + kept[1] + received[0].astype(F32) * received[1][:1]
-
-    near_grad = added(near_kept, near_received)
-    far_grad = added(far_kept, (far_received, enc_small[8:]))
-    active_sum = near_small[1] + near_received[1][1]
-    grad_encoder = added((keep_near, flip(send_near, 1)), (enc_received, enc_small))
-    grad_bias = small[1] + enc_small[1]
+    def added(kept, received, scale):
+        return kept[0] + kept[1] + received.astype(F32) * scale
+
+    near_received, near_small_received = lax.optimization_barrier(
+        (near_received, near_small_received, enc_received)
+    )[:2]
+    near_grad = added(near_kept, near_received, near_small_received[:1])
+    active_sum = near_small[1] + near_small_received[1]
+    grad_encoder = added((keep_near, flip(send_near, 1)), enc_received, small_received[8:9])
+    grad_bias = small[9] + small_received[9]
     grad_bias = lax.dynamic_slice(grad_bias, (i * enc_bias.shape[0],), (enc_bias.shape[0],))
+    new_enc_bias, new_bias_moment, new_bias_square = adam_update(
+        enc_bias, grad_bias, bias_moment, bias_square
+    )
+    new_encoder, new_enc_moment, new_enc_square = adam_update(
+        encoder, grad_encoder, enc_moment, enc_square
+    )
+    far_received, new_encoder, near_grad = lax.optimization_barrier(
+        (far_received, new_encoder, near_grad)
+    )
+    far_grad = added(far_kept, far_received, small_received[:1])
     step = width // 4
     block = pl.BlockSpec((step, latents), lambda r: (r, 0))
     in_half = pl.BlockSpec((step, latents), lambda r: (r % 2, 0))
@@ -571,15 +601,9 @@
         out_shape=[shape((width, latents), F32)] * 3,
         in_specs=[SMEM, block, block, block, in_half, in_half, row, row],
         out_specs=[block] * 3,
-        compiler_params=pltpu.CompilerParams(vmem_limit_bytes=24 * 1024 * 1024),
+        compiler_params=pltpu.CompilerParams(vmem_limit_bytes=12 * 1024 * 1024),
         cost_estimate=pl.CostEstimate(flops=1, bytes_accessed=1, transcendentals=0),
     )(place, decoder, dec_moment, dec_square, near_grad, far_grad, active_sum[None], norms)
-    new_enc_bias, new_bias_moment, new_bias_square = adam_update(
-        enc_bias, grad_bias, bias_moment, bias_square
-    )
-    new_encoder, new_enc_moment, new_enc_square = adam_update(
-        encoder, grad_encoder, enc_moment, enc_square
-    )
     return (
         error,
         new_encoder,

time: 171 us -> 166 us (0.971)
  waiting for transfers between devices: 92 us -> 82.8 us
  starting transfers between devices: 44.5 us -> 50.2 us
  Pallas kernels: 22.4 us -> 19.5 us
  other arithmetic: 4.48 us -> 7.2 us
    ppermute x14, waiting for transfers between devices: 71.1 us -> 58.9 us  [along(): return lax.ppermute(value, 'latent', pairs)]
    ppermute x14, starting transfers between devices: 31.7 us -> 40.4 us  [along(): return lax.ppermute(value, 'latent', pairs)]
    ppermute x20, waiting for transfers between devices: 20.9 us -> 23.9 us  [flip(): return lax.ppermute(value, ('latent', 'dp'), pairs)]
    ppermute x20, starting transfers between devices: 12.7 us -> 9.77 us  [flip(): return lax.ppermute(value, ('latent', 'dp'), pairs)]
    pallas_call x14 -> x13, Pallas kernels: 19.5 us -> 16.6 us  [local_kernel(): pl.pallas_call(run, out_shape=outs, in_specs=[SMEM] + [VMEM] * len(args)...]
    sub x2, other arithmetic: 2.87 us -> 4.82 us  [adam_update(): param - learn_rate * (moment_new / first_fix) / (jnp.sqrt(square_new / se...]
    unnamed x46 -> x36, local copies, waits for them, and re-layouts: 5.86 us -> 4.43 us
  transfers between devices with their start and end apart: 34 -> 34, of which waited for: 14 -> 13; matrix products, arithmetic and copies ran while one was open for 1% -> 4% of each run, Pallas kernels for 8% -> 6%
where the time goes in v6:
time: 166 us; the launch traced here: 165 us
  waiting for transfers between devices  82.8 us (50%)
  starting transfers between devices  50.2 us (30%)
  Pallas kernels  19.5 us (12%)
  other arithmetic  7.2 us (4%)
  local copies, waits for them, and re-layouts  4.46 us (3%)
    ppermute x14, waiting for transfers between devices, along(): return lax.ppermute(value, 'latent', pairs)  58.9 us
    ppermute x14, starting transfers between devices, along(): return lax.ppermute(value, 'latent', pairs)  40.4 us
    ppermute x20, waiting for transfers between devices, flip(): return lax.ppermute(value, ('latent', 'dp'), pairs)  23.9 us
    pallas_call x13, Pallas kernels, local_kernel(): pl.pallas_call(run, out_shape=outs, in_specs=[SMEM] + [VMEM] * len(args)...  16.6 us
    ppermute x20, starting transfers between devices, flip(): return lax.ppermute(value, ('latent', 'dp'), pairs)  9.77 us
    sub x2, other arithmetic, adam_update(): param - learn_rate * (moment_new / first_fix) / (jnp.sqrt(square_new / se...  4.82 us
    unnamed x36, local copies, waits for them, and re-layouts  4.43 us
  transfers between devices with their start and end apart: 34, of which 13 were waited for; matrix products, arithmetic and copies ran while one was open for 4% of the time, Pallas kernels for 6%

profile of v6, /device:TPU:0, one launch (start us, length us, event | category | flops | bytes accessed | tf_op | source)
XLA Modules:
  0.0 165.3 jit_solution(14346970095348027672)
XLA Ops:
  0.7 1.3 copy-done.1
  3.8 4.8 %collective-permute-start = (bf16[384,512]{1,0:T(8,128)(2,1)S(1)}, bf16[384,512]{1,0:T(8,128)(2,1)S(1)}, u32[]{:S(2)}, u32[]{:S(2)}) collective-permute-start(bf16[384,512]{1,0:T(8,128)(2,1)S(1)} %copy-done.10), channel_id=1, source_target_pairs={{0,4},{4,8},{8,12},{1,5},{5,9},{9,13},{2,6},{6,10},{10,14},{3,7},{... | collective-permute-start | bytes 1179656 | tf_op jit(solution)/shard_map/ppermute | solution.py:406
  8.6 1.3 collective-permute-start.1
  9.9 5.6 %collective-permute-start.2 = (bf16[384,512]{1,0:T(8,128)(2,1)S(1)}, bf16[384,512]{1,0:T(8,128)(2,1)S(1)}, u32[]{:S(2)}, u32[]{:S(2)}) collective-permute-start(bf16[384,512]{1,0:T(8,128)(2,1)S(1)} %copy-done.10), channel_id=1, source_target_pairs={{0,8},{12,4},{1,9},{13,5},{2,10},{14,6},{3,11},{15,7},{16,24},{28,... | collective-permute-start | bytes 1179656 | tf_op jit(solution)/shard_map/ppermute | solution.py:406
  15.5 1.6 collective-permute-start.6
  18.3 3.1 %collective-permute-done.1.refs_1_.refs_2_ = bf16[384,512]{1,0:T(8,128)(2,1)S(1)} collective-permute-done((bf16[384,512]{1,0:T(8,128)(2,1)S(1)}, bf16[384,512]{1,0:T(8,128)(2,1)S(1)}, u32[]{:S(2)}, u32[]{:S(2)}) %collective-permute-start.1) | collective-permute-done | bytes 393248 | tf_op jit(solution)/shard_map/ppermute | solution.py:406
  22.0 1.3 collective-permute-start.3
  23.9 4.6 %collective-permute-start.8 = (bf16[256,512]{1,0:T(8,128)(2,1)S(1)}, bf16[256,512]{1,0:T(8,128)(2,1)S(1)}, u32[]{:S(2)}, u32[]{:S(2)}) collective-permute-start(bf16[256,512]{1,0:T(8,128)(2,1)S(1)} %get-tuple-element.66), channel_id=1, source_target_pairs={{0,4},{4,8},{1,5},{5,9},{2,6},{6,10},{3,7},{7,11},{16,20},{20,24},... | collective-permute-start | bytes 786440 | tf_op jit(solution)/shard_map/ppermute | solution.py:406
  28.5 0.7 collective-permute-start.10
  29.2 1.5 collective-permute-done.6.refs_8_
  30.8 8.8 %collective-permute-start.11 = (bf16[256,512]{1,0:T(8,128)(2,1)S(1)}, bf16[256,512]{1,0:T(8,128)(2,1)S(1)}, u32[]{:S(2)}, u32[]{:S(2)}) collective-permute-start(bf16[256,512]{1,0:T(8,128)(2,1)S(1)} %get-tuple-element.70), channel_id=1, source_target_pairs={{0,8},{12,4},{1,9},{13,5},{2,10},{14,6},{3,11},{15,7},{16,24},{28,... | collective-permute-start | bytes 786440 | tf_op jit(solution)/shard_map/ppermute | solution.py:406
  39.6 1.3 collective-permute-start.4
  41.5 1.9 %collective-permute-done.11 = bf16[256,512]{1,0:T(8,128)(2,1)S(1)} collective-permute-done((bf16[256,512]{1,0:T(8,128)(2,1)S(1)}, bf16[256,512]{1,0:T(8,128)(2,1)S(1)}, u32[]{:S(2)}, u32[]{:S(2)}) %collective-permute-start.11) | collective-permute-done | bytes 262176 | tf_op jit(solution)/shard_map/ppermute | solution.py:406
  43.4 0.7 collective-permute-start.18
  44.2 5.0 %collective-permute-done.4.refs_5_ = bf16[384,512]{1,0:T(8,128)(2,1)S(1)} collective-permute-done((bf16[384,512]{1,0:T(8,128)(2,1)S(1)}, bf16[384,512]{1,0:T(8,128)(2,1)S(1)}, u32[]{:S(2)}, u32[]{:S(2)}) %collective-permute-start.4) | collective-permute-done | bytes 393248 | tf_op jit(solution)/shard_map/ppermute | solution.py:406
  49.2 1.7 %shard_map.181 = (bf16[384,512]{1,0:T(8,128)(2,1)S(1)}, bf16[384,512]{1,0:T(8,128)(2,1)S(1)}, bf16[384,2048]{1,0:T(8,128)(2,1)S(1)}, f32[1,512]{1,0:T(1,128)S(1)}) custom-call(s32[2]{0:T(128)S(1)} %pad_add_fusion.place, bf16[384,512]{1,0:T(8,128)(2,1)S(1)} %copy-done.10, bf16[384,512]{1,0:T(8,128)(2,1)S(1)} %collective-permute-done.refs_0_.refs_1_, ...), custom_call_target="tpu_custom_call" | custom-call | flops 1 | bytes 1 | tf_op jit(solution)/shard_map/pallas_call | solution.py:119
  51.0 3.5 %collective-permute-start.12 = (bf16[384,512]{1,0:T(8,128)(2,1)S(1)}, bf16[384,512]{1,0:T(8,128)(2,1)S(1)}, u32[]{:S(2)}, u32[]{:S(2)}) collective-permute-start(bf16[384,512]{1,0:T(8,128)(2,1)S(1)} %get-tuple-element.73.refs_0_.refs_2_.refs_4_), channel_id=1, source_target_pairs={{0,4},{4,8},{1,5},{5,9},{2,6},{6,10},{3,7},{7,11},{16,20},{20,24},... | collective-permute-start | bytes 1179656 | tf_op jit(solution)/shard_map/ppermute | solution.py:406
  54.5 0.7 collective-permute-start.13
  55.2 4.7 %collective-permute-start.14 = (bf16[384,512]{1,0:T(8,128)(2,1)S(1)}, bf16[384,512]{1,0:T(8,128)(2,1)S(1)}, u32[]{:S(2)}, u32[]{:S(2)}) collective-permute-start(bf16[384,512]{1,0:T(8,128)(2,1)S(1)} %get-tuple-element.73.refs_0_.refs_2_.refs_4_), channel_id=1, source_target_pairs={{0,8},{12,4},{1,9},{13,5},{2,10},{14,6},{3,11},{15,7},{16,24},{28,... | collective-permute-start | bytes 1179656 | tf_op jit(solution)/shard_map/ppermute | solution.py:406
  59.9 1.0 shard_map.182.refs_8_.refs_0_
  60.9 0.7 collective-permute-start.17
  61.6 2.3 %collective-permute-done.12.refs_1_ = bf16[384,512]{1,0:T(8,128)(2,1)S(1)} collective-permute-done((bf16[384,512]{1,0:T(8,128)(2,1)S(1)}, bf16[384,512]{1,0:T(8,128)(2,1)S(1)}, u32[]{:S(2)}, u32[]{:S(2)}) %collective-permute-start.12) | collective-permute-done | bytes 393248 | tf_op jit(solution)/shard_map/ppermute | solution.py:406
  63.9 8.0 %collective-permute-done.14.refs_3_ = bf16[384,512]{1,0:T(8,128)(2,1)S(1)} collective-permute-done((bf16[384,512]{1,0:T(8,128)(2,1)S(1)}, bf16[384,512]{1,0:T(8,128)(2,1)S(1)}, u32[]{:S(2)}, u32[]{:S(2)}) %collective-permute-start.14) | collective-permute-done | bytes 393248 | tf_op jit(solution)/shard_map/ppermute | solution.py:406
  71.9 0.7 collective-permute-start.19
  72.6 2.4 %shard_map.183.refs_0_ = bf16[384,1024]{1,0:T(8,128)(2,1)S(1)} custom-call(s32[2]{0:T(128)S(1)} %pad_add_fusion.place, bf16[384,512]{1,0:T(8,128)(2,1)S(1)} %get-tuple-element.73.refs_0_.refs_2_.refs_4_, bf16[384,512]{1,0:T(8,128)(2,1)S(1)} %collective-permute-done.12.refs_1_, bf16[384,512]{1,0:T(8,128)(2,1)S(1)} %collective-permute-done.13.refs_2_, ...), custom_call_target="tpu_custom_call" | custom-call | flops 1 | bytes 1 | tf_op jit(solution)/shard_map/pallas_call | solution.py:119
  75.1 0.7 collective-permute-start.20
  75.8 1.3 collective-permute-start.22
  77.1 26.9 %collective-permute-done.22.refs_1_ = bf16[384,1024]{1,0:T(8,128)(2,1)S(1)} collective-permute-done((bf16[384,1024]{1,0:T(8,128)(2,1)S(1)}, bf16[384,1024]{1,0:T(8,128)(2,1)S(1)}, u32[]{:S(2)}, u32[]{:S(2)}) %collective-permute-start.22) | collective-permute-done | bytes 786464 | tf_op jit(solution)/shard_map/ppermute | solution.py:406
  104.0 1.8 %shard_map.184 = (f32[384,512]{1,0:T(8,128)S(1)}, bf16[384,1024]{1,0:T(8,128)(2,1)S(1)}, f32[264,512]{1,0:T(8,128)S(1)}, f32[256,512]{1,0:T(8,128)S(1)}, f32[256,512]{1,0:T(8,128)S(1)}, /*index=5*/f32[256,512]{1,0:T(8,128)S(1)}) custom-call(s32[2]{0:T(128)S(1)} %pad_add_fusion.place, bf16[384,1024]{1,0:T(8,128)(2,1)S(1)} %shard_map.183.refs_0_, ...), custom_call_target="tpu_custom_call" | custom-call | flops 1 | bytes 1 | tf_op jit(solution)/shard_map/pallas_call | solution.py:119
  105.8 0.8 copy-done.6
  106.5 0.8 copy-done.13
  107.4 1.3 collective-permute-start.21
  110.6 7.8 %collective-permute-done.24 = f16[256,512]{1,0:T(8,128)(2,1)S(1)} collective-permute-done((f16[256,512]{1,0:T(8,128)(2,1)S(1)}, f16[256,512]{1,0:T(8,128)(2,1)S(1)}, u32[]{:S(2)}, u32[]{:S(2)}) %collective-permute-start.24) | collective-permute-done | bytes 262176 | tf_op jit(solution)/shard_map/ppermute | solution.py:410
  118.4 11.7 %collective-permute-done.21.refs_1_ = bf16[384,1024]{1,0:T(8,128)(2,1)S(1)} collective-permute-done((bf16[384,1024]{1,0:T(8,128)(2,1)S(1)}, bf16[384,1024]{1,0:T(8,128)(2,1)S(1)}, u32[]{:S(2)}, u32[]{:S(2)}) %collective-permute-start.21) | collective-permute-done | bytes 786464 | tf_op jit(solution)/shard_map/ppermute | solution.py:406
  130.1 2.0 %shard_map.186 = (bf16[384,1024]{1,0:T(8,128)(2,1)S(1)}, bf16[384,512]{1,0:T(8,128)(2,1)S(1)}, f32[1,512]{1,0:T(1,128)S(1)}, f32[1,512]{1,0:T(1,128)S(1)}, f32[520,512]{1,0:T(8,128)S(1)}) custom-call(s32[2]{0:T(128)S(1)} %pad_add_fusion.place, bf16[384,1024]{1,0:T(8,128)(2,1)S(1)} %collective-permute-done.20.refs_8_.refs_0_, ...), custom_call_target="tpu_custom_call" | custom-call | flops 1 | bytes 1 | tf_op jit(solution)/shard_map/pallas_call | solution.py:119
  132.1 3.1 %shard_map.187 = (bf16[384,512]{1,0:T(8,128)(2,1)}, f32[512,512]{1,0:T(8,128)}, f32[512,512]{1,0:T(8,128)S(1)}, f32[512,512]{1,0:T(8,128)S(1)}, f32[256,512]{1,0...) custom-call(s32[2]{0:T(128)S(1)} %pad_add_fusion.place, ...), custom_call_target="tpu_custom_call" | custom-call | flops 1 | bytes 1 | tf_op jit(solution)/shard_map/pallas_call | solution.py:119
  135.8 0.9 shard_map.188
  136.7 0.9 convert_element_type.20
  138.1 0.7 collective-permute-done.25.refs_1_
  138.8 0.7 shard_map.189
  139.5 0.8 copy-done.5
  140.3 0.8 collective-permute-start.30
  141.1 1.2 collective-permute-start.32
  142.3 1.1 convert_element_type.19
  143.4 9.6 %collective-permute-done.30 = f32[16,512]{1,0:T(8,128)S(1)} collective-permute-done((f32[16,512]{1,0:T(8,128)S(1)}, f32[16,512]{1,0:T(8,128)S(1)}, u32[]{:S(2)}, u32[]{:S(2)}) %collective-permute-start.30) | collective-permute-done | bytes 32800 | tf_op jit(solution)/shard_map/ppermute | solution.py:410
  153.6 4.3 %divide_subtract_fusion = (f32[512,512]{1,0:T(8,128)}, f32[512,512]{1,0:T(8,128)}, f32[512,512]{1,0:T(8,128)}) fusion(f32[512,512]{1,0:T(8,128)S(1)} %copy-done.2, f32[512]{0:T(512)S(1)} %bitcast.15, f16[512,512]{1,0:T(8,128)(2,1)} %collective-permute-done.29, f32[512,512]{1,0:T(8,128)S(1)} %get-tuple-element.98, f32[512,512]{1,0:T(8,128)} %collective-permute-done.28, ...), kind=kLoop, calls=%fused_computation.2 | loop fusion | flops 4194304 | bytes 8914944 | tf_op jit(solution)/shard_map/sub | solution.py:27
  158.1 3.6 %collective-permute-done.27 = f16[256,512]{1,0:T(8,128)(2,1)S(1)} collective-permute-done((f16[256,512]{1,0:T(8,128)(2,1)S(1)}, f16[256,512]{1,0:T(8,128)(2,1)S(1)}, u32[]{:S(2)}, u32[]{:S(2)}) %collective-permute-start.27) | collective-permute-done | bytes 262176 | tf_op jit(solution)/shard_map/ppermute | solution.py:410
  162.4 2.9 %shard_map.190 = (f32[512,512]{1,0:T(8,128)}, f32[512,512]{1,0:T(8,128)}, f32[512,512]{1,0:T(8,128)}) custom-call(s32[2]{0:T(128)S(1)} %pad_add_fusion.place, f32[512,512]{1,0:T(8,128)S(1)} %copy-done, f32[512,512]{1,0:T(8,128)S(1)} %copy-done.3, f32[512,512]{1,0:T(8,128)S(1)} %copy-done.4, f32[256,512]{1,0:T(8,128)S(1)} %multiply_add_fusion.3.near, ...), custom_call_target="tpu_custom_call" | custom-call | flops 1 | bytes 1 | tf_op jit(solution)/shard_map/pallas_call | solution.py:598
  (82 shorter events, 9.6 us)
Async XLA Ops:
  0.6 16.4 %copy-start = (f32[512,512]{1,0:T(8,128)S(1)}, f32[512,512]{1,0:T(8,128)}, u32[]{:S(2)}) copy-start(f32[512,512]{1,0:T(8,128)} %param.20) | copy-start | bytes 3145732
  0.7 1.3 copy-start.1
  2.7 1.1 copy-start.10
  3.3 13.8 %collective-permute-start.5 = (bf16[528,512]{1,0:T(8,128)(2,1)S(1)}, bf16[528,512]{1,0:T(8,128)(2,1)S(1)}, u32[]{:S(2)}, u32[]{:S(2)}) collective-permute-start(bf16[528,512]{1,0:T(8,128)(2,1)S(1)} %shard_map.178.refs_6_), channel_id=1, source_target_pairs={{0,1},{1,0},{2,3},{3,2},{4,5},{5,4},{6,7},{7,6},{8,9},{9,8},{10,11... | collective-permute-start | bytes 1622024 | tf_op jit(solution)/shard_map/ppermute | solution.py:410
  3.8 14.5 %collective-permute-start = (bf16[384,512]{1,0:T(8,128)(2,1)S(1)}, bf16[384,512]{1,0:T(8,128)(2,1)S(1)}, u32[]{:S(2)}, u32[]{:S(2)}) collective-permute-start(bf16[384,512]{1,0:T(8,128)(2,1)S(1)} %copy-done.10), channel_id=1, source_target_pairs={{0,4},{4,8},{8,12},{1,5},{5,9},{9,13},{2,6},{6,10},{10,14},{3,7},{... | collective-permute-start | bytes 1179656 | tf_op jit(solution)/shard_map/ppermute | solution.py:406
  8.6 12.8 %collective-permute-start.1 = (bf16[384,512]{1,0:T(8,128)(2,1)S(1)}, bf16[384,512]{1,0:T(8,128)(2,1)S(1)}, u32[]{:S(2)}, u32[]{:S(2)}) collective-permute-start(bf16[384,512]{1,0:T(8,128)(2,1)S(1)} %copy-done.10), channel_id=1, source_target_pairs={{4,0},{8,4},{12,8},{5,1},{9,5},{13,9},{6,2},{10,6},{14,10},{7,3},{... | collective-permute-start | bytes 1179656 | tf_op jit(solution)/shard_map/ppermute | solution.py:406
  9.9 18.6 %collective-permute-start.2 = (bf16[384,512]{1,0:T(8,128)(2,1)S(1)}, bf16[384,512]{1,0:T(8,128)(2,1)S(1)}, u32[]{:S(2)}, u32[]{:S(2)}) collective-permute-start(bf16[384,512]{1,0:T(8,128)(2,1)S(1)} %copy-done.10), channel_id=1, source_target_pairs={{0,8},{12,4},{1,9},{13,5},{2,10},{14,6},{3,11},{15,7},{16,24},{28,... | collective-permute-start | bytes 1179656 | tf_op jit(solution)/shard_map/ppermute | solution.py:406
  15.5 15.3 %collective-permute-start.6 = (bf16[528,512]{1,0:T(8,128)(2,1)S(1)}, bf16[528,512]{1,0:T(8,128)(2,1)S(1)}, u32[]{:S(2)}, u32[]{:S(2)}) collective-permute-start(bf16[528,512]{1,0:T(8,128)(2,1)S(1)} %shard_map.178.refs_6_), channel_id=1, source_target_pairs={{0,2},{1,3},{2,0},{3,1},{4,6},{5,7},{6,4},{7,5},{8,10},{9,11},{10,... | collective-permute-start | bytes 1622024 | tf_op jit(solution)/shard_map/ppermute | solution.py:410
  17.7 23.3 %collective-permute-start.9 = (bf16[528,512]{1,0:T(8,128)(2,1)S(1)}, bf16[528,512]{1,0:T(8,128)(2,1)S(1)}, u32[]{:S(2)}, u32[]{:S(2)}) collective-permute-start(bf16[528,512]{1,0:T(8,128)(2,1)S(1)} %shard_map.179.refs_0_.refs_4_), channel_id=1, source_target_pairs={{0,2},{1,3},{2,0},{3,1},{4,6},{5,7},{6,4},{7,5},{8,10},{9,11},{10,... | collective-permute-start | bytes 1622024 | tf_op jit(solution)/shard_map/ppermute | solution.py:410
  22.0 17.5 %collective-permute-start.3 = (bf16[384,512]{1,0:T(8,128)(2,1)S(1)}, bf16[384,512]{1,0:T(8,128)(2,1)S(1)}, u32[]{:S(2)}, u32[]{:S(2)}) collective-permute-start(bf16[384,512]{1,0:T(8,128)(2,1)S(1)} %shard_map.177), channel_id=1, source_target_pairs={{4,0},{8,12},{5,1},{9,13},{6,2},{10,14},{7,3},{11,15},{20,16},{24,... | collective-permute-start | bytes 1179656 | tf_op jit(solution)/shard_map/ppermute | solution.py:406
  23.9 16.9 %collective-permute-start.8 = (bf16[256,512]{1,0:T(8,128)(2,1)S(1)}, bf16[256,512]{1,0:T(8,128)(2,1)S(1)}, u32[]{:S(2)}, u32[]{:S(2)}) collective-permute-start(bf16[256,512]{1,0:T(8,128)(2,1)S(1)} %get-tuple-element.66), channel_id=1, source_target_pairs={{0,4},{4,8},{1,5},{5,9},{2,6},{6,10},{3,7},{7,11},{16,20},{20,24},... | collective-permute-start | bytes 786440 | tf_op jit(solution)/shard_map/ppermute | solution.py:406
  28.5 12.9 %collective-permute-start.10 = (bf16[256,512]{1,0:T(8,128)(2,1)S(1)}, bf16[256,512]{1,0:T(8,128)(2,1)S(1)}, u32[]{:S(2)}, u32[]{:S(2)}) collective-permute-start(bf16[256,512]{1,0:T(8,128)(2,1)S(1)} %get-tuple-element.68), channel_id=1, source_target_pairs={{8,4},{12,8},{9,5},{13,9},{10,6},{14,10},{11,7},{15,11},{24,20},{2... | collective-permute-start | bytes 786440 | tf_op jit(solution)/shard_map/ppermute | solution.py:406
  30.8 12.6 %collective-permute-start.11 = (bf16[256,512]{1,0:T(8,128)(2,1)S(1)}, bf16[256,512]{1,0:T(8,128)(2,1)S(1)}, u32[]{:S(2)}, u32[]{:S(2)}) collective-permute-start(bf16[256,512]{1,0:T(8,128)(2,1)S(1)} %get-tuple-element.70), channel_id=1, source_target_pairs={{0,8},{12,4},{1,9},{13,5},{2,10},{14,6},{3,11},{15,7},{16,24},{28,... | collective-permute-start | bytes 786440 | tf_op jit(solution)/shard_map/ppermute | solution.py:406
  39.6 9.7 %collective-permute-start.4 = (bf16[384,512]{1,0:T(8,128)(2,1)S(1)}, bf16[384,512]{1,0:T(8,128)(2,1)S(1)}, u32[]{:S(2)}, u32[]{:S(2)}) collective-permute-start(bf16[384,512]{1,0:T(8,128)(2,1)S(1)} %collective-permute-done.2.refs_3_), channel_id=1, source_target_pairs={{4,0},{8,12},{5,1},{9,13},{6,2},{10,14},{7,3},{11,15},{20,16},{24,... | collective-permute-start | bytes 1179656 | tf_op jit(solution)/shard_map/ppermute | solution.py:406
  40.9 14.3 %collective-permute-start.15 = (bf16[528,512]{1,0:T(8,128)(2,1)S(1)}, bf16[528,512]{1,0:T(8,128)(2,1)S(1)}, u32[]{:S(2)}, u32[]{:S(2)}) collective-permute-start(bf16[528,512]{1,0:T(8,128)(2,1)S(1)} %shard_map.179.refs_0_.refs_4_), channel_id=1, source_target_pairs={{0,1},{1,0},{2,3},{3,2},{4,5},{5,4},{6,7},{7,6},{8,9},{9,8},{10,11... | collective-permute-start | bytes 1622024 | tf_op jit(solution)/shard_map/ppermute | solution.py:410
  41.0 8.3 %collective-permute-start.7 = (bf16[528,512]{1,0:T(8,128)(2,1)S(1)}, bf16[528,512]{1,0:T(8,128)(2,1)S(1)}, u32[]{:S(2)}, u32[]{:S(2)}) collective-permute-start(bf16[528,512]{1,0:T(8,128)(2,1)S(1)} %collective-permute-done.6.refs_8_), channel_id=1, source_target_pairs={{0,1},{1,0},{2,3},{3,2},{4,5},{5,4},{6,7},{7,6},{8,9},{9,8},{10,11... | collective-permute-start | bytes 1622024 | tf_op jit(solution)/shard_map/ppermute | solution.py:410
  43.4 28.5 %collective-permute-start.18 = (bf16[768,512]{1,0:T(8,128)(2,1)S(1)}, bf16[768,512]{1,0:T(8,128)(2,1)S(1)}, u32[]{:S(2)}, u32[]{:S(2)}) collective-permute-start(bf16[768,512]{1,0:T(8,128)(2,1)S(1)} %constant_dynamic-update-slice_fusion.refs_10_.refs_8_), channel_id=1, source_target_pairs={{4,6},{5,7},{6,4},{7,5},{8,10},{9,11},{10,8},{11,9},{20,22},{21,23... | collective-permute-start | bytes 2359304 | tf_op jit(solution)/shard_map/ppermute | solution.py:410
  44.2 16.7 %collective-permute-start.16 = (bf16[528,512]{1,0:T(8,128)(2,1)S(1)}, bf16[528,512]{1,0:T(8,128)(2,1)S(1)}, u32[]{:S(2)}, u32[]{:S(2)}) collective-permute-start(bf16[528,512]{1,0:T(8,128)(2,1)S(1)} %collective-permute-done.9.refs_6_), channel_id=1, source_target_pairs={{0,1},{1,0},{2,3},{3,2},{4,5},{5,4},{6,7},{7,6},{8,9},{9,8},{10,11... | collective-permute-start | bytes 1622024 | tf_op jit(solution)/shard_map/ppermute | solution.py:410
  51.0 12.9 %collective-permute-start.12 = (bf16[384,512]{1,0:T(8,128)(2,1)S(1)}, bf16[384,512]{1,0:T(8,128)(2,1)S(1)}, u32[]{:S(2)}, u32[]{:S(2)}) collective-permute-start(bf16[384,512]{1,0:T(8,128)(2,1)S(1)} %get-tuple-element.73.refs_0_.refs_2_.refs_4_), channel_id=1, source_target_pairs={{0,4},{4,8},{1,5},{5,9},{2,6},{6,10},{3,7},{7,11},{16,20},{20,24},... | collective-permute-start | bytes 1179656 | tf_op jit(solution)/shard_map/ppermute | solution.py:406
  54.5 9.4 %collective-permute-start.13 = (bf16[384,512]{1,0:T(8,128)(2,1)S(1)}, bf16[384,512]{1,0:T(8,128)(2,1)S(1)}, u32[]{:S(2)}, u32[]{:S(2)}) collective-permute-start(bf16[384,512]{1,0:T(8,128)(2,1)S(1)} %get-tuple-element.73.refs_0_.refs_2_.refs_4_), channel_id=1, source_target_pairs={{8,4},{12,8},{9,5},{13,9},{10,6},{14,10},{11,7},{15,11},{24,20},{2... | collective-permute-start | bytes 1179656 | tf_op jit(solution)/shard_map/ppermute | solution.py:406
  55.2 16.7 %collective-permute-start.14 = (bf16[384,512]{1,0:T(8,128)(2,1)S(1)}, bf16[384,512]{1,0:T(8,128)(2,1)S(1)}, u32[]{:S(2)}, u32[]{:S(2)}) collective-permute-start(bf16[384,512]{1,0:T(8,128)(2,1)S(1)} %get-tuple-element.73.refs_0_.refs_2_.refs_4_), channel_id=1, source_target_pairs={{0,8},{12,4},{1,9},{13,5},{2,10},{14,6},{3,11},{15,7},{16,24},{28,... | collective-permute-start | bytes 1179656 | tf_op jit(solution)/shard_map/ppermute | solution.py:406
  60.9 11.7 %collective-permute-start.17 = (bf16[768,512]{1,0:T(8,128)(2,1)S(1)}, bf16[768,512]{1,0:T(8,128)(2,1)S(1)}, u32[]{:S(2)}, u32[]{:S(2)}) collective-permute-start(bf16[768,512]{1,0:T(8,128)(2,1)S(1)} %constant_dynamic-update-slice_fusion.refs_10_.refs_8_), channel_id=1, source_target_pairs={{4,5},{5,4},{6,7},{7,6},{8,9},{9,8},{10,11},{11,10},{20,21},{21,20... | collective-permute-start | bytes 2359304 | tf_op jit(solution)/shard_map/ppermute | solution.py:410
  71.9 0.7 collective-permute-start.19
  75.1 2.0 %collective-permute-start.20 = (bf16[384,1024]{1,0:T(8,128)(2,1)S(1)}, bf16[384,1024]{1,0:T(8,128)(2,1)S(1)}, u32[]{:S(2)}, u32[]{:S(2)}) collective-permute-start(bf16[384,1024]{1,0:T(8,128)(2,1)S(1)} %shard_map.183.refs_0_), channel_id=1, source_target_pairs={{4,8},{8,4},{5,9},{9,5},{6,10},{10,6},{7,11},{11,7},{20,24},{24,20... | collective-permute-start | bytes 2359304 | tf_op jit(solution)/shard_map/ppermute | solution.py:406
  75.8 28.2 %collective-permute-start.22 = (bf16[384,1024]{1,0:T(8,128)(2,1)S(1)}, bf16[384,1024]{1,0:T(8,128)(2,1)S(1)}, u32[]{:S(2)}, u32[]{:S(2)}) collective-permute-start(bf16[384,1024]{1,0:T(8,128)(2,1)S(1)} %shard_map.183.refs_0_), channel_id=1, source_target_pairs={{4,0},{8,12},{5,1},{9,13},{6,2},{10,14},{7,3},{11,15},{20,16},{24,... | collective-permute-start | bytes 2359304 | tf_op jit(solution)/shard_map/ppermute | solution.py:406
  106.5 0.8 copy-start.13
  107.3 1.9 %collective-permute-start.23 = (f32[264,512]{1,0:T(8,128)S(1)}, f32[264,512]{1,0:T(8,128)S(1)}, u32[]{:S(2)}, u32[]{:S(2)}) collective-permute-start(f32[264,512]{1,0:T(8,128)S(1)} %get-tuple-element.79), channel_id=1, source_target_pairs={{0,1},{1,0},{2,3},{3,2},{4,5},{5,4},{6,7},{7,6},{8,9},{9,8},{10,11... | collective-permute-start | bytes 1622024 | tf_op jit(solution)/shard_map/ppermute | solution.py:410
  107.4 22.7 %collective-permute-start.21 = (bf16[384,1024]{1,0:T(8,128)(2,1)S(1)}, bf16[384,1024]{1,0:T(8,128)(2,1)S(1)}, u32[]{:S(2)}, u32[]{:S(2)}) collective-permute-start(bf16[384,1024]{1,0:T(8,128)(2,1)S(1)} %shard_map.183.refs_0_), channel_id=1, source_target_pairs={{8,0},{4,12},{9,1},{5,13},{10,2},{6,14},{11,3},{7,15},{24,16},{20,... | collective-permute-start | bytes 2359304 | tf_op jit(solution)/shard_map/ppermute | solution.py:406
  110.0 8.4 %collective-permute-start.24 = (f16[256,512]{1,0:T(8,128)(2,1)S(1)}, f16[256,512]{1,0:T(8,128)(2,1)S(1)}, u32[]{:S(2)}, u32[]{:S(2)}) collective-permute-start(f16[256,512]{1,0:T(8,128)(2,1)S(1)} %convert_element_type.18), channel_id=1, source_target_pairs={{0,2},{1,3},{2,0},{3,1},{4,6},{5,7},{6,4},{7,5},{8,10},{9,11},{10,... | collective-permute-start | bytes 786440 | tf_op jit(solution)/shard_map/ppermute | solution.py:410
  132.1 3.8 %collective-permute-start.26 = (f32[520,512]{1,0:T(8,128)S(1)}, f32[520,512]{1,0:T(8,128)S(1)}, u32[]{:S(2)}, u32[]{:S(2)}) collective-permute-start(f32[520,512]{1,0:T(8,128)S(1)} %get-tuple-element.90), channel_id=1, source_target_pairs={{0,1},{1,0},{2,3},{3,2},{4,5},{5,4},{6,7},{7,6},{8,9},{9,8},{10,11... | collective-permute-start | bytes 3194888 | tf_op jit(solution)/shard_map/ppermute | solution.py:410
  135.3 2.3 %copy-start.8 = (f32[256,512]{1,0:T(8,128)}, f32[256,512]{1,0:T(8,128)S(1)}, u32[]{:S(2)}) copy-start(f32[256,512]{1,0:T(8,128)S(1)} %get-tuple-element.113) | copy-start | bytes 1572868
  135.3 2.3 %copy-start.14 = (f32[256,512]{1,0:T(8,128)}, f32[256,512]{1,0:T(8,128)S(1)}, u32[]{:S(2)}) copy-start(f32[256,512]{1,0:T(8,128)S(1)} %get-tuple-element.114) | copy-start | bytes 1572868
  135.3 18.3 %collective-permute-start.28 = (f32[512,512]{1,0:T(8,128)}, f32[512,512]{1,0:T(8,128)}, u32[]{:S(2)}, u32[]{:S(2)}) collective-permute-start(f32[512,512]{1,0:T(8,128)} %get-tuple-element.99), channel_id=1, source_target_pairs={{0,1},{1,0},{2,3},{3,2},{4,5},{5,4},{6,7},{7,6},{8,9},{9,8},{10,11... | collective-permute-start | bytes 3145736 | tf_op jit(solution)/shard_map/ppermute | solution.py:410
  135.8 3.0 %collective-permute-start.25 = (f32[256,512]{1,0:T(8,128)S(1)}, f32[256,512]{1,0:T(8,128)S(1)}, u32[]{:S(2)}, u32[]{:S(2)}) collective-permute-start(f32[256,512]{1,0:T(8,128)S(1)} %get-tuple-element.88), channel_id=1, source_target_pairs={{0,1},{1,0},{2,3},{3,2},{4,5},{5,4},{6,7},{7,6},{8,9},{9,8},{10,11... | collective-permute-start | bytes 1572872 | tf_op jit(solution)/shard_map/ppermute | solution.py:410
  137.6 15.9 %copy-start.2 = (f32[512,512]{1,0:T(8,128)S(1)}, f32[512,512]{1,0:T(8,128)}, u32[]{:S(2)}) copy-start(f32[512,512]{1,0:T(8,128)} %refs_0_.3) | copy-start | bytes 3145732
  137.6 15.4 %collective-permute-start.29 = (f16[512,512]{1,0:T(8,128)(2,1)}, f16[512,512]{1,0:T(8,128)(2,1)}, u32[]{:S(2)}, u32[]{:S(2)}) collective-permute-start(f16[512,512]{1,0:T(8,128)(2,1)} %convert_element_type.20), channel_id=1, source_target_pairs={{0,2},{1,3},{2,0},{3,1},{4,6},{5,7},{6,4},{7,5},{8,10},{9,11},{10,... | collective-permute-start | bytes 1572872 | tf_op jit(solution)/shard_map/ppermute | solution.py:410
  140.3 12.7 %collective-permute-start.30 = (f32[16,512]{1,0:T(8,128)S(1)}, f32[16,512]{1,0:T(8,128)S(1)}, u32[]{:S(2)}, u32[]{:S(2)}) collective-permute-start(f32[16,512]{1,0:T(8,128)S(1)} %get-tuple-element.95), channel_id=1, source_target_pairs={{0,2},{1,3},{2,0},{3,1},{4,6},{5,7},{6,4},{7,5},{8,10},{9,11},{10,... | collective-permute-start | bytes 98312 | tf_op jit(solution)/shard_map/ppermute | solution.py:410
  141.1 12.4 %collective-permute-start.32 = (f32[8,512]{1,0:T(8,128)S(1)}, f32[8,512]{1,0:T(8,128)S(1)}, u32[]{:S(2)}, u32[]{:S(2)}) collective-permute-start(f32[8,512]{1,0:T(8,128)S(1)} %get-tuple-element.105), channel_id=1, source_target_pairs={{0,2},{1,3},{2,0},{3,1},{4,6},{5,7},{6,4},{7,5},{8,10},{9,11},{10,... | collective-permute-start | bytes 49160 | tf_op jit(solution)/shard_map/ppermute | solution.py:410
  142.3 15.6 %collective-permute-start.31 = (f32[256,512]{1,0:T(8,128)}, f32[256,512]{1,0:T(8,128)S(1)}, u32[]{:S(2)}, u32[]{:S(2)}) collective-permute-start(f32[256,512]{1,0:T(8,128)} %copy-done.13), channel_id=1, source_target_pairs={{0,1},{1,0},{2,3},{3,2},{4,5},{5,4},{6,7},{7,6},{8,9},{9,8},{10,11... | collective-permute-start | bytes 1572872 | tf_op jit(solution)/shard_map/ppermute | solution.py:410
  153.0 9.3 %collective-permute-start.33 = (f32[256,512]{1,0:T(8,128)}, f32[256,512]{1,0:T(8,128)S(1)}, u32[]{:S(2)}, u32[]{:S(2)}) collective-permute-start(f32[256,512]{1,0:T(8,128)} %copy-done.14), channel_id=1, source_target_pairs={{0,1},{1,0},{2,3},{3,2},{4,5},{5,4},{6,7},{7,6},{8,9},{9,8},{10,11... | collective-permute-start | bytes 1572872 | tf_op jit(solution)/shard_map/ppermute | solution.py:410
  153.0 8.7 %collective-permute-start.27 = (f16[256,512]{1,0:T(8,128)(2,1)S(1)}, f16[256,512]{1,0:T(8,128)(2,1)S(1)}, u32[]{:S(2)}, u32[]{:S(2)}) collective-permute-start(f16[256,512]{1,0:T(8,128)(2,1)S(1)} %convert_element_type.19), channel_id=1, source_target_pairs={{0,2},{1,3},{2,0},{3,1},{4,6},{5,7},{6,4},{7,5},{8,10},{9,11},{10,... | collective-permute-start | bytes 786440 | tf_op jit(solution)/shard_map/ppermute | solution.py:410
  153.5 4.3 %copy-start.7 = (f32[256,512]{1,0:T(8,128)S(1)}, f32[256,512]{1,0:T(8,128)}, u32[]{:S(2)}) copy-start(f32[256,512]{1,0:T(8,128)} %copy-done.6) | copy-start | bytes 1572868
  157.8 3.9 %copy-start.12 = (f32[128]{0:T(128)S(1)}, f32[128]{0:T(128)}, u32[]{:S(2)}) copy-start(f32[128]{0:T(128)} %param.12) | copy-start | bytes 1540
  157.8 3.9 %copy-start.15 = (f32[128]{0:T(128)S(1)}, f32[128]{0:T(128)}, u32[]{:S(2)}) copy-start(f32[128]{0:T(128)} %param.16) | copy-start | bytes 1540
  157.8 3.9 %copy-start.16 = (f32[128]{0:T(128)S(1)}, f32[128]{0:T(128)}, u32[]{:S(2)}) copy-start(f32[128]{0:T(128)} %param.17) | copy-start | bytes 1540
  157.8 4.4 %copy-start.9 = (f32[256,512]{1,0:T(8,128)S(1)}, f32[256,512]{1,0:T(8,128)}, u32[]{:S(2)}) copy-start(f32[256,512]{1,0:T(8,128)} %copy-done.8) | copy-start | bytes 1572868
  157.9 4.5 %copy-start.3 = (f32[512,512]{1,0:T(8,128)S(1)}, f32[512,512]{1,0:T(8,128)}, u32[]{:S(2)}) copy-start(f32[512,512]{1,0:T(8,128)} %moment) | copy-start | bytes 3145732
  157.9 4.5 %copy-start.4 = (f32[512,512]{1,0:T(8,128)S(1)}, f32[512,512]{1,0:T(8,128)}, u32[]{:S(2)}) copy-start(f32[512,512]{1,0:T(8,128)} %square) | copy-start | bytes 3145732
  (3 other events, 2.2 us)

commit v7 on v6

--- a/solution.py
+++ b/solution.py
@@ -1,4 +1,5 @@
 import functools
+import math
 
 import jax
 import jax.numpy as jnp
@@ -109,9 +110,10 @@
 SMEM = pl.BlockSpec(memory_space=pltpu.SMEM)
 ANY = pl.BlockSpec(memory_space=pl.ANY)
 EXTRA = 16
-
-
-def local_kernel(body, outs, place, *args, after=(), scratch=()):
+NOTABLE = 10**10
+
+
+def local_kernel(body, outs, place, *args, after=(), scratch=(), cost=1):
     def run(place, *refs):
         body(place, *refs[: len(args)], *refs[len(args) + len(after) :])
 
@@ -123,7 +125,7 @@
         out_specs=[VMEM] * len(outs),
         scratch_shapes=scratch,
         compiler_params=pltpu.CompilerParams(vmem_limit_bytes=held + 6 * 1024 * 1024),
-        cost_estimate=pl.CostEstimate(flops=1, bytes_accessed=1, transcendentals=0),
+        cost_estimate=pl.CostEstimate(flops=cost, bytes_accessed=1, transcendentals=0),
     )(place, *args, *after)
 
 
@@ -268,9 +270,9 @@
         out[...] = end[...]
 
 
-def decoder_grads(scale, i, error, codes, outs):
+def decoder_grads(scale, i, error, codes, slots, outs):
     half = error.shape[1] // 4
-    for out, slot in zip(outs, (3, 1, 2, 0)):
+    for slot, out in zip(slots, outs):
         out[:half] = scale * lax.dot_general(
             error[:, columns((i ^ slot) * half, half)],
             codes[...],
@@ -298,34 +300,23 @@
     z, i = place[0], place[1]
     half = mine.shape[1] // 4
     pick(place, mine, passed, near)
-    decoder_grads(-2.0 / rows, i, near, codes, outs)
+    decoder_grads(-2.0 / rows, i, near, codes, (3, 1, 2, 0), outs)
     outs[0][half:] = jnp.broadcast_to(active[...], (outs[0].shape[0] - half, active.shape[1]))
     part[...] = back_through(i, near, (dec0, dec1, dec2, dec3), jnp.where(z >= 2, half, 0))
 
 
+def far_error_body(rows, place, swapped, direct, codes, far, send):
+    pick(place, swapped, direct, far)
+    decoder_grads(-2.0 / rows, place[1], far, codes, (3,), (send,))
+
+
 def code_grad_body(
-    rows,
-    place,
-    swapped,
-    direct,
-    part,
-    mask,
-    dec0,
-    dec1,
-    dec2,
-    dec3,
-    turned,
-    far,
-    grad_low,
-    bias_sum,
-    norms,
-    send_far,
+    rows, place, far, part, mask, dec0, dec1, dec2, dec3, turned, grad_low, bias_sum, norms, send_far
 ):
     z, i = place[0], place[1]
     half = far.shape[1] // 4
     width = 2 * half
     decs = (dec0, dec1, dec2, dec3)
-    pick(place, swapped, direct, far)
     total = part[...] + back_through(i, far, decs, jnp.where(z >= 2, 0, half))
     squares = functools.reduce(jnp.add, [one_row(dec[width:, :]) for dec in decs])
     column_norms = jnp.sqrt(squares + 1e-06)
@@ -351,24 +342,42 @@
     half = far.shape[1] // 4
     shift = jnp.where(z >= 2, 0, half)
     encoder_grads(i, turned, grad_low, (2, 1, 0), (kept_far, send, kept))
-    decoder_grads(-2.0 / rows, i, far, codes, outs)
+    decoder_grads(-2.0 / rows, i, far, codes, (1, 2, 0), outs)
     home[:, columns(half - shift, half)] = near[:, columns(z * half, half)]
     home[:, columns(shift, half)] = far[:, columns(z * half, half)]
 
 
-def far_body(place, kept, received, row, *refs):
-    scaled, small = refs[-2:]
-    width = scaled.shape[0]
+def power(values):
+    largest = jnp.max(jnp.abs(values), axis=0, keepdims=True)
+    return jnp.ceil(jnp.log(jnp.maximum(largest, 1e-30)) * (1.0 / math.log(2.0)))
+
+
+def scale_of(exponent):
+    return jnp.exp(exponent * math.log(2.0))
+
+
+def pack_body(place, kept, received, row, packed, row_sum):
+    width = kept.shape[0]
     total = kept[...] + received[:width]
-    largest = jnp.maximum(jnp.max(jnp.abs(total), axis=0, keepdims=True), 1e-30)
-    scaled[...] = total * (16384.0 / largest)
-    rows = jnp.broadcast_to(row[...], (8, row.shape[1]))
+    exponent = power(total)
+    packed[:width] = total * scale_of(14.0 - exponent)
+    sums = row[...]
     if received.shape[0] > width:
-        rows += received[width:]
-    at = lax.broadcasted_iota(jnp.int32, rows.shape, 0)
-    small[:8] = jnp.where(at == 0, largest * (1.0 / 16384.0), rows)
-    for other in refs[:-2]:
-        small[8:] = other[...]
+        sums += received[width : width + 1]
+    row_sum[...] = sums
+    row_exponent = power(sums)
+    parts = three_rows(sums * scale_of(14.0 - row_exponent)).astype(F32)
+    at = lax.broadcasted_iota(jnp.int32, parts.shape, 0)
+    parts = jnp.where(at == 3, exponent, jnp.where(at == 4, row_exponent, parts))
+    packed[width:] = parts
+
+
+def unpack(packed):
+    width = packed.shape[0] - EXTRA
+    rows = packed[width:].astype(F32)
+    block = packed[:width].astype(F32) * scale_of(rows[3:4] - 14.0)
+    row = (rows[0:1] + rows[1:2] + rows[2:3]) * scale_of(rows[4:5] - 14.0)
+    return block, row
 
 
 def decoder_step_body(
@@ -435,7 +444,7 @@
     )
     relay1 = along(onward, ends)
     relay2 = along(across, ends)
-    enc = [enc_own, enc_core, enc_chip, flip(behind(enc_chip, relay1), 1)]
+    enc = [enc_own, enc_core, enc_chip, flip(behind(enc_chip, relay2), 1)]
 
     up, down, beyond = local_kernel(
         pieces_body, [shape((half, latents), BF16)] * 3, place, dec_own
@@ -496,18 +505,16 @@
     passed = along(own_error, [(1, 0), (2, 3)])
     direct = along(own_error, [(2, 0), (1, 3)])
 
-    def decoder_half(send_far, send_near, keep_far, keep_near, *others, after=()):
-        scaled, small = local_kernel(
-            far_body,
-            [shape((half, latents), F32), shape((8 + 8 * len(others), latents), F32)],
+    def across_chips(kept, send, row):
+        packed, row_sum = local_kernel(
+            pack_body,
+            [shape((kept.shape[0] + EXTRA, latents), F32), shape((1, latents), F32)],
             place,
-            keep_far,
-            flip(send_far, 1),
-            active,
-            *others,
-            after=after,
+            kept,
+            flip(send, 1),
+            row,
         )
-        return scaled, small, (keep_near, flip(send_near, 1))
+        return packed, flip(packed.astype(jnp.float16), 2), row_sum
 
     blocks = [shape((half + 8, latents), F32)] + [shape((half, latents), F32)] * 3
     part, near, *near_blocks = local_kernel(
@@ -521,30 +528,39 @@
         *dec,
         after=(swapped,),
     )
-    near_scaled, near_small, near_kept = decoder_half(*near_blocks)
-    near_received = flip(near_scaled.astype(jnp.float16), 2)
-    far, grad_low, bias_sum, norms, send_far = local_kernel(
+    send_far, send_near, keep_far, keep_near = near_blocks
+    near_packed, near_received, active_sum = across_chips(keep_far, send_far, active)
+    near_kept = keep_near, flip(send_near, 1)
+    far, far_send = local_kernel(
+        functools.partial(far_error_body, rows),
+        [shape((count, features // 2), BF16), shape((half, latents), F32)],
+        place,
+        swapped,
+        direct,
+        codes,
+        after=(near_packed,),
+        cost=NOTABLE,
+    )
+    grad_low, bias_sum, norms, send_far_enc = local_kernel(
         functools.partial(code_grad_body, rows),
         [
-            shape((count, features // 2), BF16),
             shape((count, latents), BF16),
             shape((1, latents), F32),
             shape((1, latents), F32),
             shape((width + 8, latents), F32),
         ],
         place,
-        swapped,
-        direct,
+        far,
         behind(part, near_received),
         mask,
         *dec,
         turned,
     )
-    error, send_near, keep_far, keep_near, *far_blocks = local_kernel(
+    error, enc_send_near, enc_keep_far, enc_keep_near, *far_blocks = local_kernel(
         functools.partial(rest_body, rows),
         [shape((count, width), BF16)]
         + [shape((width, latents), F32)] * 3
-        + [shape((half, latents), F32)] * 4,
+        + [shape((half, latents), F32)] * 3,
         place,
         turned,
         grad_low,
@@ -552,34 +568,25 @@
         far,
         codes,
     )
-    near_small_received = flip(behind(near_small, far), 2)
-    scaled, small = local_kernel(
-        far_body,
-        [shape((width, latents), F32), shape((8, latents), F32)],
-        place,
-        keep_far,
-        flip(send_far, 1),
-        bias_sum,
-    )
-    enc_received = flip(scaled.astype(jnp.float16), 2)
-    far_scaled, small, far_kept = decoder_half(*far_blocks, small, after=(scaled,))
-    far_received = flip(far_scaled.astype(jnp.float16), 2)
-    small_received = behind(flip(small, 2), enc_received)
+    send_near, keep_far, keep_near = far_blocks
+    far_packed, far_received, _ = across_chips(keep_far, far_send, active)
+    far_kept = keep_near, flip(send_near, 1)
+    enc_packed, enc_received, bias_here = across_chips(
+        behind(enc_keep_far, far_packed), send_far_enc, bias_sum
+    )
+    enc_kept = enc_keep_near, flip(enc_send_near, 1)
 
     decoder, dec_moment, dec_square, encoder, enc_moment, enc_square = lax.optimization_barrier(
-        (decoder, dec_moment, dec_square, encoder, enc_moment, enc_square, small)
+        (decoder, dec_moment, dec_square, encoder, enc_moment, enc_square, enc_packed)
     )[:6]
-
-    def added(kept, received, scale):
-        return kept[0] + kept[1] + received.astype(F32) * scale
-
-    near_received, near_small_received = lax.optimization_barrier(
-        (near_received, near_small_received, enc_received)
-    )[:2]
-    near_grad = added(near_kept, near_received, near_small_received[:1])
-    active_sum = near_small[1] + near_small_received[1]
-    grad_encoder = added((keep_near, flip(send_near, 1)), enc_received, small_received[8:9])
-    grad_bias = small[9] + small_received[9]
+    near_block, active_there = unpack(near_received)
+    far_block, _ = unpack(far_received)
+    enc_block, bias_there = unpack(enc_received)
+    near_grad = near_kept[0] + near_kept[1] + near_block
+    far_grad = far_kept[0] + far_kept[1] + far_block
+    active_sum = active_sum + active_there
+    grad_encoder = enc_kept[0] + enc_kept[1] + enc_block
+    grad_bias = (bias_here + bias_there).reshape(latents)
     grad_bias = lax.dynamic_slice(grad_bias, (i * enc_bias.shape[0],), (enc_bias.shape[0],))
     new_enc_bias, new_bias_moment, new_bias_square = adam_update(
         enc_bias, grad_bias, bias_moment, bias_square
@@ -587,10 +594,6 @@
     new_encoder, new_enc_moment, new_enc_square = adam_update(
         encoder, grad_encoder, enc_moment, enc_square
     )
-    far_received, new_encoder, near_grad = lax.optimization_barrier(
-        (far_received, new_encoder, near_grad)
-    )
-    far_grad = added(far_kept, far_received, small_received[:1])
     step = width // 4
     block = pl.BlockSpec((step, latents), lambda r: (r, 0))
     in_half = pl.BlockSpec((step, latents), lambda r: (r % 2, 0))
@@ -603,7 +606,7 @@
         out_specs=[block] * 3,
         compiler_params=pltpu.CompilerParams(vmem_limit_bytes=12 * 1024 * 1024),
         cost_estimate=pl.CostEstimate(flops=1, bytes_accessed=1, transcendentals=0),
-    )(place, decoder, dec_moment, dec_square, near_grad, far_grad, active_sum[None], norms)
+    )(place, decoder, dec_moment, dec_square, near_grad, far_grad, active_sum, norms)
     return (
         error,
         new_encoder,

time: 166 us -> 160 us (0.964)
  waiting for transfers between devices: 82.8 us -> 76.4 us
  starting transfers between devices: 50.2 us -> 46.1 us
  Pallas kernels: 19.5 us -> 23.5 us
  local copies, waits for them, and re-layouts: 4.46 us -> 7.43 us
  other arithmetic: 7.2 us -> 4.59 us
    ppermute x20 -> x18, waiting for transfers between devices: 23.9 us -> 16.1 us  [flip(): return lax.ppermute(value, ('latent', 'dp'), pairs)]
    pallas_call x13 -> x14, Pallas kernels: 16.6 us -> 20.6 us  [local_kernel(): pl.pallas_call(run, out_shape=outs, in_specs=[SMEM] + [VMEM] * len(args)...]
    ppermute x14, starting transfers between devices: 40.4 us -> 37.4 us  [along(): return lax.ppermute(value, 'latent', pairs)]
    unnamed x36 -> x50, local copies, waits for them, and re-layouts: 4.43 us -> 7.41 us
    sub x2, other arithmetic: 4.82 us -> 2.88 us  [adam_update(): param - learn_rate * (moment_new / first_fix) / (jnp.sqrt(square_new / se...]
    convert_element_type x3 -> x5, other arithmetic: 2.01 us -> 0.19 us  [the longest x3 0.18 us: across_chips(): return (packed, flip(packed.astype(jnp.float16), 2), row_sum)]
    ppermute x20 -> x18, starting transfers between devices: 9.77 us -> 8.73 us  [flip(): return lax.ppermute(value, ('latent', 'dp'), pairs)]
  transfers between devices with their start and end apart: 34 -> 32, of which waited for: 13 -> 12; matrix products, arithmetic and copies ran while one was open for 4% -> 1% of each run, Pallas kernels for 6% -> 11%
where the time goes in v7:
time: 160 us; the launch traced here: 159 us
  waiting for transfers between devices  76.4 us (48%)
  starting transfers between devices  46.1 us (29%)
  Pallas kernels  23.5 us (15%)
  local copies, waits for them, and re-layouts  7.43 us (5%)
  other arithmetic  4.59 us (3%)
    ppermute x14, waiting for transfers between devices, along(): return lax.ppermute(value, 'latent', pairs)  60.3 us
    ppermute x14, starting transfers between devices, along(): return lax.ppermute(value, 'latent', pairs)  37.4 us
    pallas_call x14, Pallas kernels, local_kernel(): pl.pallas_call(run, out_shape=outs, in_specs=[SMEM] + [VMEM] * len(args)...  20.6 us
    ppermute x18, waiting for transfers between devices, flip(): return lax.ppermute(value, ('latent', 'dp'), pairs)  16.1 us
    ppermute x18, starting transfers between devices, flip(): return lax.ppermute(value, ('latent', 'dp'), pairs)  8.73 us
    unnamed x50, local copies, waits for them, and re-layouts  7.41 us
  transfers between devices with their start and end apart: 32, of which 12 were waited for; matrix products, arithmetic and copies ran while one was open for 1% of the time, Pallas kernels for 11%

profile of v7, /device:TPU:0, one launch (start us, length us, event | category | flops | bytes accessed | tf_op | source)
XLA Modules:
  0.0 159.2 jit_solution(13003966307360204393)
XLA Ops:
  0.7 1.3 copy-done.1
  3.8 5.8 %collective-permute-start.2 = (bf16[384,512]{1,0:T(8,128)(2,1)S(1)}, bf16[384,512]{1,0:T(8,128)(2,1)S(1)}, u32[]{:S(2)}, u32[]{:S(2)}) collective-permute-start(bf16[384,512]{1,0:T(8,128)(2,1)S(1)} %copy-done.13), channel_id=1, source_target_pairs={{0,8},{12,4},{1,9},{13,5},{2,10},{14,6},{3,11},{15,7},{16,24},{28,... | collective-permute-start | bytes 1179656 | tf_op jit(solution)/shard_map/ppermute | solution.py:415
  9.6 1.3 collective-permute-start.1
  10.9 4.6 %collective-permute-start = (bf16[384,512]{1,0:T(8,128)(2,1)S(1)}, bf16[384,512]{1,0:T(8,128)(2,1)S(1)}, u32[]{:S(2)}, u32[]{:S(2)}) collective-permute-start(bf16[384,512]{1,0:T(8,128)(2,1)S(1)} %copy-done.13), channel_id=1, source_target_pairs={{0,4},{4,8},{8,12},{1,5},{5,9},{9,13},{2,6},{6,10},{10,14},{3,7},{... | collective-permute-start | bytes 1179656 | tf_op jit(solution)/shard_map/ppermute | solution.py:415
  15.5 1.6 collective-permute-start.6
  18.3 0.8 collective-permute-done.2.refs_3_
  19.1 1.3 collective-permute-start.4
  21.0 1.6 %collective-permute-done.1.refs_1_.refs_2_ = bf16[384,512]{1,0:T(8,128)(2,1)S(1)} collective-permute-done((bf16[384,512]{1,0:T(8,128)(2,1)S(1)}, bf16[384,512]{1,0:T(8,128)(2,1)S(1)}, u32[]{:S(2)}, u32[]{:S(2)}) %collective-permute-start.1) | collective-permute-done | bytes 393248 | tf_op jit(solution)/shard_map/ppermute | solution.py:415
  22.6 8.4 %collective-permute-start.8 = (bf16[256,512]{1,0:T(8,128)(2,1)S(1)}, bf16[256,512]{1,0:T(8,128)(2,1)S(1)}, u32[]{:S(2)}, u32[]{:S(2)}) collective-permute-start(bf16[256,512]{1,0:T(8,128)(2,1)S(1)} %get-tuple-element.59), channel_id=1, source_target_pairs={{0,4},{4,8},{1,5},{5,9},{2,6},{6,10},{3,7},{7,11},{16,20},{20,24},... | collective-permute-start | bytes 786440 | tf_op jit(solution)/shard_map/ppermute | solution.py:415
  31.7 5.2 %collective-permute-start.11 = (bf16[256,512]{1,0:T(8,128)(2,1)S(1)}, bf16[256,512]{1,0:T(8,128)(2,1)S(1)}, u32[]{:S(2)}, u32[]{:S(2)}) collective-permute-start(bf16[256,512]{1,0:T(8,128)(2,1)S(1)} %get-tuple-element.63), channel_id=1, source_target_pairs={{0,8},{12,4},{1,9},{13,5},{2,10},{14,6},{3,11},{15,7},{16,24},{28,... | collective-permute-start | bytes 786440 | tf_op jit(solution)/shard_map/ppermute | solution.py:415
  37.6 1.3 collective-permute-start.3
  38.9 1.8 %collective-permute-done.9.refs_6_.refs_5_ = bf16[528,512]{1,0:T(8,128)(2,1)S(1)} collective-permute-done((bf16[528,512]{1,0:T(8,128)(2,1)S(1)}, bf16[528,512]{1,0:T(8,128)(2,1)S(1)}, u32[]{:S(2)}, u32[]{:S(2)}) %collective-permute-start.9) | collective-permute-done | bytes 540704 | tf_op jit(solution)/shard_map/ppermute | solution.py:419
  40.8 1.6 %collective-permute-done.11 = bf16[256,512]{1,0:T(8,128)(2,1)S(1)} collective-permute-done((bf16[256,512]{1,0:T(8,128)(2,1)S(1)}, bf16[256,512]{1,0:T(8,128)(2,1)S(1)}, u32[]{:S(2)}, u32[]{:S(2)}) %collective-permute-start.11) | collective-permute-done | bytes 262176 | tf_op jit(solution)/shard_map/ppermute | solution.py:415
  42.4 0.7 collective-permute-start.18
  43.2 6.1 %collective-permute-done.3.refs_4_ = bf16[384,512]{1,0:T(8,128)(2,1)S(1)} collective-permute-done((bf16[384,512]{1,0:T(8,128)(2,1)S(1)}, bf16[384,512]{1,0:T(8,128)(2,1)S(1)}, u32[]{:S(2)}, u32[]{:S(2)}) %collective-permute-start.3) | collective-permute-done | bytes 393248 | tf_op jit(solution)/shard_map/ppermute | solution.py:415
  49.4 1.8 %shard_map.181 = (bf16[384,512]{1,0:T(8,128)(2,1)S(1)}, bf16[384,512]{1,0:T(8,128)(2,1)S(1)}, bf16[384,2048]{1,0:T(8,128)(2,1)S(1)}, f32[1,512]{1,0:T(1,128)S(1)}) custom-call(s32[2]{0:T(128)S(1)} %pad_add_fusion.place, bf16[384,512]{1,0:T(8,128)(2,1)S(1)} %copy-done.13, bf16[384,512]{1,0:T(8,128)(2,1)S(1)} %collective-permute-done.refs_0_.refs_1_, ...), custom_call_target="tpu_custom_call" | custom-call | flops 1 | bytes 1 | tf_op jit(solution)/shard_map/pallas_call | solution.py:121
  51.1 2.0 %collective-permute-start.14 = (bf16[384,512]{1,0:T(8,128)(2,1)S(1)}, bf16[384,512]{1,0:T(8,128)(2,1)S(1)}, u32[]{:S(2)}, u32[]{:S(2)}) collective-permute-start(bf16[384,512]{1,0:T(8,128)(2,1)S(1)} %get-tuple-element.66.refs_0_.refs_2_.refs_4_), channel_id=1, source_target_pairs={{0,8},{12,4},{1,9},{13,5},{2,10},{14,6},{3,11},{15,7},{16,24},{28,... | collective-permute-start | bytes 1179656 | tf_op jit(solution)/shard_map/ppermute | solution.py:415
  53.1 0.7 collective-permute-start.13
  53.8 2.9 %collective-permute-start.12 = (bf16[384,512]{1,0:T(8,128)(2,1)S(1)}, bf16[384,512]{1,0:T(8,128)(2,1)S(1)}, u32[]{:S(2)}, u32[]{:S(2)}) collective-permute-start(bf16[384,512]{1,0:T(8,128)(2,1)S(1)} %get-tuple-element.66.refs_0_.refs_2_.refs_4_), channel_id=1, source_target_pairs={{0,4},{4,8},{1,5},{5,9},{2,6},{6,10},{3,7},{7,11},{16,20},{20,24},... | collective-permute-start | bytes 1179656 | tf_op jit(solution)/shard_map/ppermute | solution.py:415
  56.7 1.0 shard_map.182.refs_7_.refs_0_
  57.7 0.7 collective-permute-start.17
  58.5 4.1 %collective-permute-done.14.refs_3_ = bf16[384,512]{1,0:T(8,128)(2,1)S(1)} collective-permute-done((bf16[384,512]{1,0:T(8,128)(2,1)S(1)}, bf16[384,512]{1,0:T(8,128)(2,1)S(1)}, u32[]{:S(2)}, u32[]{:S(2)}) %collective-permute-start.14) | collective-permute-done | bytes 393248 | tf_op jit(solution)/shard_map/ppermute | solution.py:415
  62.5 8.0 %collective-permute-done.12.refs_1_ = bf16[384,512]{1,0:T(8,128)(2,1)S(1)} collective-permute-done((bf16[384,512]{1,0:T(8,128)(2,1)S(1)}, bf16[384,512]{1,0:T(8,128)(2,1)S(1)}, u32[]{:S(2)}, u32[]{:S(2)}) %collective-permute-start.12) | collective-permute-done | bytes 393248 | tf_op jit(solution)/shard_map/ppermute | solution.py:415
  70.5 0.7 collective-permute-start.19
  71.3 2.4 %shard_map.183.refs_0_ = bf16[384,1024]{1,0:T(8,128)(2,1)S(1)} custom-call(s32[2]{0:T(128)S(1)} %pad_add_fusion.place, bf16[384,512]{1,0:T(8,128)(2,1)S(1)} %get-tuple-element.66.refs_0_.refs_2_.refs_4_, bf16[384,512]{1,0:T(8,128)(2,1)S(1)} %collective-permute-done.12.refs_1_, bf16[384,512]{1,0:T(8,128)(2,1)S(1)} %collective-permute-done.13.refs_2_, ...), custom_call_target="tpu_custom_call" | custom-call | flops 1 | bytes 1 | tf_op jit(solution)/shard_map/pallas_call | solution.py:121
  73.7 1.3 collective-permute-start.22
  75.0 0.7 collective-permute-start.20
  75.7 1.3 collective-permute-start.21
  77.0 23.6 %collective-permute-done.22.refs_1_ = bf16[384,1024]{1,0:T(8,128)(2,1)S(1)} collective-permute-done((bf16[384,1024]{1,0:T(8,128)(2,1)S(1)}, bf16[384,1024]{1,0:T(8,128)(2,1)S(1)}, u32[]{:S(2)}, u32[]{:S(2)}) %collective-permute-start.22) | collective-permute-done | bytes 786464 | tf_op jit(solution)/shard_map/ppermute | solution.py:415
  100.6 2.3 %shard_map.184 = (f32[384,512]{1,0:T(8,128)S(1)}, bf16[384,1024]{1,0:T(8,128)(2,1)S(1)}, f32[264,512]{1,0:T(8,128)S(1)}, f32[256,512]{1,0:T(8,128)}, f32[256,512]{1,0:T(8,128)S(1)}, /*index=5*/f32[256,512]{1,0:T(8,128)S(1)}) custom-call(s32[2]{0:T(128)S(1)} %pad_add_fusion.place, bf16[384,1024]{1,0:T(8,128)(2,1)S(1)} %shard_map.183.refs_0_, ...), custom_call_target="tpu_custom_call" | custom-call | flops 1 | bytes 1 | tf_op jit(solution)/shard_map/pallas_call | solution.py:121
  102.9 1.9 %collective-permute-done.23.refs_1_ = f32[264,512]{1,0:T(8,128)S(1)} collective-permute-done((f32[264,512]{1,0:T(8,128)S(1)}, f32[264,512]{1,0:T(8,128)S(1)}, u32[]{:S(2)}, u32[]{:S(2)}) %collective-permute-start.23) | collective-permute-done | bytes 540704 | tf_op jit(solution)/shard_map/ppermute | solution.py:419
  106.2 14.4 %collective-permute-done.21.refs_1_ = bf16[384,1024]{1,0:T(8,128)(2,1)S(1)} collective-permute-done((bf16[384,1024]{1,0:T(8,128)(2,1)S(1)}, bf16[384,1024]{1,0:T(8,128)(2,1)S(1)}, u32[]{:S(2)}, u32[]{:S(2)}) %collective-permute-start.21) | collective-permute-done | bytes 786464 | tf_op jit(solution)/shard_map/ppermute | solution.py:415
  120.6 1.9 %shard_map.186 = (bf16[384,1024]{1,0:T(8,128)(2,1)S(1)}, f32[256,512]{1,0:T(8,128)}) custom-call(s32[2]{0:T(128)S(1)} %pad_add_fusion.place, bf16[384,1024]{1,0:T(8,128)(2,1)S(1)} %collective-permute-done.20.refs_8_.refs_0_, bf16[384,1024]{1,0:T(8,128)(2,1)S(1)} %collective-permute-done.21.refs_1_, ...), custom_call_target="tpu_custom_call" | custom-call | flops 10000000000 | bytes 1 | tf_op jit(solution)/shard_map/pallas_call | solution.py:121
  122.6 0.7 copy-done.20
  123.3 2.8 %shard_map.187 = (bf16[384,512]{1,0:T(8,128)(2,1)S(1)}, f32[1,512]{1,0:T(1,128)S(1)}, f32[1,512]{1,0:T(1,128)S(1)}, f32[520,512]{1,0:T(8,128)}) custom-call(s32[2]{0:T(128)S(1)} %pad_add_fusion.place, bf16[384,1024]{1,0:T(8,128)(2,1)S(1)} %get-tuple-element.73.refs_0_.refs_3_, f32[384,512]{1,0:T(8,128)S(1)} %get-tuple-element.75.refs_1_, ...), custom_call_target="tpu_custom_call" | custom-call | flops 1 | bytes 1 | tf_op jit(solution)/shard_map/pallas_call | solution.py:121
  126.1 0.7 copy-done.11
  127.9 1.1 copy-done.4
  129.0 1.1 copy-done.8
  130.2 1.0 copy-done.12
  131.2 2.6 %shard_map.188 = (bf16[384,512]{1,0:T(8,128)(2,1)}, f32[512,512]{1,0:T(8,128)S(1)}, f32[512,512]{1,0:T(8,128)S(1)}, f32[512,512]{1,0:T(8,128)S(1)}, f32[256,512]...) custom-call(s32[2]{0:T(128)S(1)} %pad_add_fusion.place, ...), custom_call_target="tpu_custom_call" | custom-call | flops 1 | bytes 1 | tf_op jit(solution)/shard_map/pallas_call | solution.py:121
  134.4 1.2 shard_map.189
  136.2 1.5 shard_map.190
  137.8 1.5 collective-permute-start.28
  139.4 1.3 multiply_add_fusion.3.near
  140.7 4.4 %collective-permute-done.31 = f16[272,512]{1,0:T(8,128)(2,1)S(1)} collective-permute-done((f16[272,512]{1,0:T(8,128)(2,1)S(1)}, f16[272,512]{1,0:T(8,128)(2,1)S(1)}, u32[]{:S(2)}, u32[]{:S(2)}) %collective-permute-start.31) | collective-permute-done | bytes 278560 | tf_op jit(solution)/shard_map/ppermute | solution.py:419
  145.3 2.9 %shard_map.191 = (f32[512,512]{1,0:T(8,128)}, f32[512,512]{1,0:T(8,128)}, f32[512,512]{1,0:T(8,128)}) custom-call(s32[2]{0:T(128)S(1)} %pad_add_fusion.place, f32[512,512]{1,0:T(8,128)S(1)} %copy-done, f32[512,512]{1,0:T(8,128)S(1)} %copy-done.5, f32[512,512]{1,0:T(8,128)S(1)} %copy-done.6, f32[256,512]{1,0:T(8,128)S(1)} %multiply_add_fusion.3.near, ...), custom_call_target="tpu_custom_call" | custom-call | flops 1 | bytes 1 | tf_op jit(solution)/shard_map/pallas_call | solution.py:601
  148.3 8.0 %collective-permute-done.28 = f16[528,512]{1,0:T(8,128)(2,1)S(1)} collective-permute-done((f16[528,512]{1,0:T(8,128)(2,1)S(1)}, f16[528,512]{1,0:T(8,128)(2,1)S(1)}, u32[]{:S(2)}, u32[]{:S(2)}) %collective-permute-start.28) | collective-permute-done | bytes 540704 | tf_op jit(solution)/shard_map/ppermute | solution.py:419
  156.9 2.3 %divide_subtract_fusion = (f32[512,512]{1,0:T(8,128)}, f32[512,512]{1,0:T(8,128)}, f32[512,512]{1,0:T(8,128)}) fusion(f32[512,512]{1,0:T(8,128)S(1)} %copy-done.2, f32[512]{0:T(512)S(1)} %bitcast.9, f16[528,512]{1,0:T(8,128)(2,1)S(1)} %collective-permute-done.28, f32[512,512]{1,0:T(8,128)S(1)} %get-tuple-element.90, ...), kind=kLoop, calls=%fused_computation.2 | loop fusion | flops 4194304 | bytes 8914944 | tf_op jit(solution)/shard_map/sub | solution.py:28
  (95 shorter events, 9.7 us)
Async XLA Ops:
  0.6 16.4 %copy-start = (f32[512,512]{1,0:T(8,128)S(1)}, f32[512,512]{1,0:T(8,128)}, u32[]{:S(2)}) copy-start(f32[512,512]{1,0:T(8,128)} %param.20) | copy-start | bytes 3145732
  0.7 1.3 copy-start.1
  3.3 13.8 %collective-permute-start.5 = (bf16[528,512]{1,0:T(8,128)(2,1)S(1)}, bf16[528,512]{1,0:T(8,128)(2,1)S(1)}, u32[]{:S(2)}, u32[]{:S(2)}) collective-permute-start(bf16[528,512]{1,0:T(8,128)(2,1)S(1)} %shard_map.178.refs_6_), channel_id=1, source_target_pairs={{0,1},{1,0},{2,3},{3,2},{4,5},{5,4},{6,7},{7,6},{8,9},{9,8},{10,11... | collective-permute-start | bytes 1622024 | tf_op jit(solution)/shard_map/ppermute | solution.py:419
  3.8 15.3 %collective-permute-start.2 = (bf16[384,512]{1,0:T(8,128)(2,1)S(1)}, bf16[384,512]{1,0:T(8,128)(2,1)S(1)}, u32[]{:S(2)}, u32[]{:S(2)}) collective-permute-start(bf16[384,512]{1,0:T(8,128)(2,1)S(1)} %copy-done.13), channel_id=1, source_target_pairs={{0,8},{12,4},{1,9},{13,5},{2,10},{14,6},{3,11},{15,7},{16,24},{28,... | collective-permute-start | bytes 1179656 | tf_op jit(solution)/shard_map/ppermute | solution.py:415
  9.6 13.0 %collective-permute-start.1 = (bf16[384,512]{1,0:T(8,128)(2,1)S(1)}, bf16[384,512]{1,0:T(8,128)(2,1)S(1)}, u32[]{:S(2)}, u32[]{:S(2)}) collective-permute-start(bf16[384,512]{1,0:T(8,128)(2,1)S(1)} %copy-done.13), channel_id=1, source_target_pairs={{4,0},{8,4},{12,8},{5,1},{9,5},{13,9},{6,2},{10,6},{14,10},{7,3},{... | collective-permute-start | bytes 1179656 | tf_op jit(solution)/shard_map/ppermute | solution.py:415
  10.9 20.1 %collective-permute-start = (bf16[384,512]{1,0:T(8,128)(2,1)S(1)}, bf16[384,512]{1,0:T(8,128)(2,1)S(1)}, u32[]{:S(2)}, u32[]{:S(2)}) collective-permute-start(bf16[384,512]{1,0:T(8,128)(2,1)S(1)} %copy-done.13), channel_id=1, source_target_pairs={{0,4},{4,8},{8,12},{1,5},{5,9},{9,13},{2,6},{6,10},{10,14},{3,7},{... | collective-permute-start | bytes 1179656 | tf_op jit(solution)/shard_map/ppermute | solution.py:415
  15.5 16.2 %collective-permute-start.6 = (bf16[528,512]{1,0:T(8,128)(2,1)S(1)}, bf16[528,512]{1,0:T(8,128)(2,1)S(1)}, u32[]{:S(2)}, u32[]{:S(2)}) collective-permute-start(bf16[528,512]{1,0:T(8,128)(2,1)S(1)} %shard_map.178.refs_6_), channel_id=1, source_target_pairs={{0,2},{1,3},{2,0},{3,1},{4,6},{5,7},{6,4},{7,5},{8,10},{9,11},{10,... | collective-permute-start | bytes 1622024 | tf_op jit(solution)/shard_map/ppermute | solution.py:419
  17.7 23.0 %collective-permute-start.9 = (bf16[528,512]{1,0:T(8,128)(2,1)S(1)}, bf16[528,512]{1,0:T(8,128)(2,1)S(1)}, u32[]{:S(2)}, u32[]{:S(2)}) collective-permute-start(bf16[528,512]{1,0:T(8,128)(2,1)S(1)} %shard_map.179.refs_0_.refs_4_.refs_3_), channel_id=1, source_target_pairs={{0,2},{1,3},{2,0},{3,1},{4,6},{5,7},{6,4},{7,5},{8,10},{9,11},{10,... | collective-permute-start | bytes 1622024 | tf_op jit(solution)/shard_map/ppermute | solution.py:419
  19.1 18.4 %collective-permute-start.4 = (bf16[384,512]{1,0:T(8,128)(2,1)S(1)}, bf16[384,512]{1,0:T(8,128)(2,1)S(1)}, u32[]{:S(2)}, u32[]{:S(2)}) collective-permute-start(bf16[384,512]{1,0:T(8,128)(2,1)S(1)} %collective-permute-done.2.refs_3_), channel_id=1, source_target_pairs={{4,0},{8,12},{5,1},{9,13},{6,2},{10,14},{7,3},{11,15},{20,16},{24,... | collective-permute-start | bytes 1179656 | tf_op jit(solution)/shard_map/ppermute | solution.py:415
  22.6 16.2 %collective-permute-start.8 = (bf16[256,512]{1,0:T(8,128)(2,1)S(1)}, bf16[256,512]{1,0:T(8,128)(2,1)S(1)}, u32[]{:S(2)}, u32[]{:S(2)}) collective-permute-start(bf16[256,512]{1,0:T(8,128)(2,1)S(1)} %get-tuple-element.59), channel_id=1, source_target_pairs={{0,4},{4,8},{1,5},{5,9},{2,6},{6,10},{3,7},{7,11},{16,20},{20,24},... | collective-permute-start | bytes 786440 | tf_op jit(solution)/shard_map/ppermute | solution.py:415
  31.1 9.7 %collective-permute-start.10 = (bf16[256,512]{1,0:T(8,128)(2,1)S(1)}, bf16[256,512]{1,0:T(8,128)(2,1)S(1)}, u32[]{:S(2)}, u32[]{:S(2)}) collective-permute-start(bf16[256,512]{1,0:T(8,128)(2,1)S(1)} %get-tuple-element.61), channel_id=1, source_target_pairs={{8,4},{12,8},{9,5},{13,9},{10,6},{14,10},{11,7},{15,11},{24,20},{2... | collective-permute-start | bytes 786440 | tf_op jit(solution)/shard_map/ppermute | solution.py:415
  31.7 10.6 %collective-permute-start.11 = (bf16[256,512]{1,0:T(8,128)(2,1)S(1)}, bf16[256,512]{1,0:T(8,128)(2,1)S(1)}, u32[]{:S(2)}, u32[]{:S(2)}) collective-permute-start(bf16[256,512]{1,0:T(8,128)(2,1)S(1)} %get-tuple-element.63), channel_id=1, source_target_pairs={{0,8},{12,4},{1,9},{13,5},{2,10},{14,6},{3,11},{15,7},{16,24},{28,... | collective-permute-start | bytes 786440 | tf_op jit(solution)/shard_map/ppermute | solution.py:415
  37.6 11.8 %collective-permute-start.3 = (bf16[384,512]{1,0:T(8,128)(2,1)S(1)}, bf16[384,512]{1,0:T(8,128)(2,1)S(1)}, u32[]{:S(2)}, u32[]{:S(2)}) collective-permute-start(bf16[384,512]{1,0:T(8,128)(2,1)S(1)} %shard_map.177), channel_id=1, source_target_pairs={{4,0},{8,12},{5,1},{9,13},{6,2},{10,14},{7,3},{11,15},{20,16},{24,... | collective-permute-start | bytes 1179656 | tf_op jit(solution)/shard_map/ppermute | solution.py:415
  38.9 14.9 %collective-permute-start.15 = (bf16[528,512]{1,0:T(8,128)(2,1)S(1)}, bf16[528,512]{1,0:T(8,128)(2,1)S(1)}, u32[]{:S(2)}, u32[]{:S(2)}) collective-permute-start(bf16[528,512]{1,0:T(8,128)(2,1)S(1)} %shard_map.179.refs_0_.refs_4_.refs_3_), channel_id=1, source_target_pairs={{0,1},{1,0},{2,3},{3,2},{4,5},{5,4},{6,7},{7,6},{8,9},{9,8},{10,11... | collective-permute-start | bytes 1622024 | tf_op jit(solution)/shard_map/ppermute | solution.py:419
  40.7 8.7 %collective-permute-start.7 = (bf16[528,512]{1,0:T(8,128)(2,1)S(1)}, bf16[528,512]{1,0:T(8,128)(2,1)S(1)}, u32[]{:S(2)}, u32[]{:S(2)}) collective-permute-start(bf16[528,512]{1,0:T(8,128)(2,1)S(1)} %collective-permute-done.6.refs_8_), channel_id=1, source_target_pairs={{0,1},{1,0},{2,3},{3,2},{4,5},{5,4},{6,7},{7,6},{8,9},{9,8},{10,11... | collective-permute-start | bytes 1622024 | tf_op jit(solution)/shard_map/ppermute | solution.py:419
  42.4 28.1 %collective-permute-start.18 = (bf16[768,512]{1,0:T(8,128)(2,1)S(1)}, bf16[768,512]{1,0:T(8,128)(2,1)S(1)}, u32[]{:S(2)}, u32[]{:S(2)}) collective-permute-start(bf16[768,512]{1,0:T(8,128)(2,1)S(1)} %constant_dynamic-update-slice_fusion.refs_10_.refs_8_), channel_id=1, source_target_pairs={{4,6},{5,7},{6,4},{7,5},{8,10},{9,11},{10,8},{11,9},{20,22},{21,23... | collective-permute-start | bytes 2359304 | tf_op jit(solution)/shard_map/ppermute | solution.py:419
  43.1 14.6 %collective-permute-start.16 = (bf16[528,512]{1,0:T(8,128)(2,1)S(1)}, bf16[528,512]{1,0:T(8,128)(2,1)S(1)}, u32[]{:S(2)}, u32[]{:S(2)}) collective-permute-start(bf16[528,512]{1,0:T(8,128)(2,1)S(1)} %collective-permute-done.9.refs_6_.refs_5_), channel_id=1, source_target_pairs={{0,1},{1,0},{2,3},{3,2},{4,5},{5,4},{6,7},{7,6},{8,9},{9,8},{10,11... | collective-permute-start | bytes 1622024 | tf_op jit(solution)/shard_map/ppermute | solution.py:419
  51.1 11.4 %collective-permute-start.14 = (bf16[384,512]{1,0:T(8,128)(2,1)S(1)}, bf16[384,512]{1,0:T(8,128)(2,1)S(1)}, u32[]{:S(2)}, u32[]{:S(2)}) collective-permute-start(bf16[384,512]{1,0:T(8,128)(2,1)S(1)} %get-tuple-element.66.refs_0_.refs_2_.refs_4_), channel_id=1, source_target_pairs={{0,8},{12,4},{1,9},{13,5},{2,10},{14,6},{3,11},{15,7},{16,24},{28,... | collective-permute-start | bytes 1179656 | tf_op jit(solution)/shard_map/ppermute | solution.py:415
  53.1 9.4 %collective-permute-start.13 = (bf16[384,512]{1,0:T(8,128)(2,1)S(1)}, bf16[384,512]{1,0:T(8,128)(2,1)S(1)}, u32[]{:S(2)}, u32[]{:S(2)}) collective-permute-start(bf16[384,512]{1,0:T(8,128)(2,1)S(1)} %get-tuple-element.66.refs_0_.refs_2_.refs_4_), channel_id=1, source_target_pairs={{8,4},{12,8},{9,5},{13,9},{10,6},{14,10},{11,7},{15,11},{24,20},{2... | collective-permute-start | bytes 1179656 | tf_op jit(solution)/shard_map/ppermute | solution.py:415
  53.8 16.7 %collective-permute-start.12 = (bf16[384,512]{1,0:T(8,128)(2,1)S(1)}, bf16[384,512]{1,0:T(8,128)(2,1)S(1)}, u32[]{:S(2)}, u32[]{:S(2)}) collective-permute-start(bf16[384,512]{1,0:T(8,128)(2,1)S(1)} %get-tuple-element.66.refs_0_.refs_2_.refs_4_), channel_id=1, source_target_pairs={{0,4},{4,8},{1,5},{5,9},{2,6},{6,10},{3,7},{7,11},{16,20},{20,24},... | collective-permute-start | bytes 1179656 | tf_op jit(solution)/shard_map/ppermute | solution.py:415
  57.7 13.5 %collective-permute-start.17 = (bf16[768,512]{1,0:T(8,128)(2,1)S(1)}, bf16[768,512]{1,0:T(8,128)(2,1)S(1)}, u32[]{:S(2)}, u32[]{:S(2)}) collective-permute-start(bf16[768,512]{1,0:T(8,128)(2,1)S(1)} %constant_dynamic-update-slice_fusion.refs_10_.refs_8_), channel_id=1, source_target_pairs={{4,5},{5,4},{6,7},{7,6},{8,9},{9,8},{10,11},{11,10},{20,21},{21,20... | collective-permute-start | bytes 2359304 | tf_op jit(solution)/shard_map/ppermute | solution.py:419
  70.5 0.7 collective-permute-start.19
  73.7 26.9 %collective-permute-start.22 = (bf16[384,1024]{1,0:T(8,128)(2,1)S(1)}, bf16[384,1024]{1,0:T(8,128)(2,1)S(1)}, u32[]{:S(2)}, u32[]{:S(2)}) collective-permute-start(bf16[384,1024]{1,0:T(8,128)(2,1)S(1)} %shard_map.183.refs_0_), channel_id=1, source_target_pairs={{4,0},{8,12},{5,1},{9,13},{6,2},{10,14},{7,3},{11,15},{20,16},{24,... | collective-permute-start | bytes 2359304 | tf_op jit(solution)/shard_map/ppermute | solution.py:415
  75.0 25.6 %collective-permute-start.20 = (bf16[384,1024]{1,0:T(8,128)(2,1)S(1)}, bf16[384,1024]{1,0:T(8,128)(2,1)S(1)}, u32[]{:S(2)}, u32[]{:S(2)}) collective-permute-start(bf16[384,1024]{1,0:T(8,128)(2,1)S(1)} %shard_map.183.refs_0_), channel_id=1, source_target_pairs={{4,8},{8,4},{5,9},{9,5},{6,10},{10,6},{7,11},{11,7},{20,24},{24,20... | collective-permute-start | bytes 2359304 | tf_op jit(solution)/shard_map/ppermute | solution.py:415
  75.7 44.9 %collective-permute-start.21 = (bf16[384,1024]{1,0:T(8,128)(2,1)S(1)}, bf16[384,1024]{1,0:T(8,128)(2,1)S(1)}, u32[]{:S(2)}, u32[]{:S(2)}) collective-permute-start(bf16[384,1024]{1,0:T(8,128)(2,1)S(1)} %shard_map.183.refs_0_), channel_id=1, source_target_pairs={{8,0},{4,12},{9,1},{5,13},{10,2},{6,14},{11,3},{7,15},{24,16},{20,... | collective-permute-start | bytes 2359304 | tf_op jit(solution)/shard_map/ppermute | solution.py:415
  102.9 19.6 %copy-start.7 = (bf16[384,1024]{1,0:T(8,128)(2,1)}, bf16[384,1024]{1,0:T(8,128)(2,1)S(1)}, u32[]{:S(2)}) copy-start(bf16[384,1024]{1,0:T(8,128)(2,1)S(1)} %get-tuple-element.78.refs_2_) | copy-start | bytes 2359300
  102.9 19.6 %copy-start.9 = (f32[256,512]{1,0:T(8,128)}, f32[256,512]{1,0:T(8,128)S(1)}, u32[]{:S(2)}) copy-start(f32[256,512]{1,0:T(8,128)S(1)} %get-tuple-element.97) | copy-start | bytes 1572868
  102.9 1.9 %collective-permute-start.23 = (f32[264,512]{1,0:T(8,128)S(1)}, f32[264,512]{1,0:T(8,128)S(1)}, u32[]{:S(2)}, u32[]{:S(2)}) collective-permute-start(f32[264,512]{1,0:T(8,128)S(1)} %get-tuple-element.71), channel_id=1, source_target_pairs={{0,1},{1,0},{2,3},{3,2},{4,5},{5,4},{6,7},{7,6},{8,9},{9,8},{10,11... | collective-permute-start | bytes 1622024 | tf_op jit(solution)/shard_map/ppermute | solution.py:419
  105.6 16.9 %collective-permute-start.24 = (f16[272,512]{1,0:T(8,128)(2,1)S(1)}, f16[272,512]{1,0:T(8,128)(2,1)S(1)}, u32[]{:S(2)}, u32[]{:S(2)}) collective-permute-start(f16[272,512]{1,0:T(8,128)(2,1)S(1)} %convert_element_type.25), channel_id=1, source_target_pairs={{0,2},{1,3},{2,0},{3,1},{4,6},{5,7},{6,4},{7,5},{8,10},{9,11},{10,... | collective-permute-start | bytes 835592 | tf_op jit(solution)/shard_map/ppermute | solution.py:419
  122.5 3.5 %copy-start.3 = (bf16[384,1024]{1,0:T(8,128)(2,1)}, bf16[384,1024]{1,0:T(8,128)(2,1)S(1)}, u32[]{:S(2)}) copy-start(bf16[384,1024]{1,0:T(8,128)(2,1)S(1)} %get-tuple-element.73.refs_0_.refs_3_) | copy-start | bytes 2359300
  127.4 8.8 %collective-permute-start.26 = (f32[520,512]{1,0:T(8,128)}, f32[520,512]{1,0:T(8,128)}, u32[]{:S(2)}, u32[]{:S(2)}) collective-permute-start(f32[520,512]{1,0:T(8,128)} %get-tuple-element.85), channel_id=1, source_target_pairs={{0,1},{1,0},{2,3},{3,2},{4,5},{5,4},{6,7},{7,6},{8,9},{9,8},{10,11... | collective-permute-start | bytes 3194888 | tf_op jit(solution)/shard_map/ppermute | solution.py:419
  127.4 6.9 %collective-permute-start.25 = (f32[256,512]{1,0:T(8,128)}, f32[256,512]{1,0:T(8,128)S(1)}, u32[]{:S(2)}, u32[]{:S(2)}) collective-permute-start(f32[256,512]{1,0:T(8,128)} %get-tuple-element.82), channel_id=1, source_target_pairs={{0,1},{1,0},{2,3},{3,2},{4,5},{5,4},{6,7},{7,6},{8,9},{9,8},{10,11... | collective-permute-start | bytes 1572872 | tf_op jit(solution)/shard_map/ppermute | solution.py:419
  127.9 11.5 %collective-permute-start.29 = (f32[256,512]{1,0:T(8,128)}, f32[256,512]{1,0:T(8,128)}, u32[]{:S(2)}, u32[]{:S(2)}) collective-permute-start(f32[256,512]{1,0:T(8,128)} %get-tuple-element.98), channel_id=1, source_target_pairs={{0,1},{1,0},{2,3},{3,2},{4,5},{5,4},{6,7},{7,6},{8,9},{9,8},{10,11... | collective-permute-start | bytes 1572872 | tf_op jit(solution)/shard_map/ppermute | solution.py:419
  131.2 3.2 %copy-start.21 = (f16[272,512]{1,0:T(8,128)(2,1)S(1)}, f16[272,512]{1,0:T(8,128)(2,1)}, u32[]{:S(2)}) copy-start(f16[272,512]{1,0:T(8,128)(2,1)} %copy-done.20) | copy-start | bytes 835588
  133.8 2.4 %copy-start.17 = (f32[1,512]{1,0:T(1,128)S(1)}, f32[1,512]{1,0:T(1,128)}, u32[]{:S(2)}) copy-start(f32[1,512]{1,0:T(1,128)} %copy-done.16) | copy-start | bytes 6148
  133.8 11.3 %collective-permute-start.30 = (f32[256,512]{1,0:T(8,128)S(1)}, f32[256,512]{1,0:T(8,128)S(1)}, u32[]{:S(2)}, u32[]{:S(2)}) collective-permute-start(f32[256,512]{1,0:T(8,128)S(1)} %get-tuple-element.100), channel_id=1, source_target_pairs={{0,1},{1,0},{2,3},{3,2},{4,5},{5,4},{6,7},{7,6},{8,9},{9,8},{10,11... | collective-permute-start | bytes 1572872 | tf_op jit(solution)/shard_map/ppermute | solution.py:419
  134.3 22.6 %collective-permute-start.27 = (f32[512,512]{1,0:T(8,128)S(1)}, f32[512,512]{1,0:T(8,128)S(1)}, u32[]{:S(2)}, u32[]{:S(2)}) collective-permute-start(f32[512,512]{1,0:T(8,128)S(1)} %get-tuple-element.91), channel_id=1, source_target_pairs={{0,1},{1,0},{2,3},{3,2},{4,5},{5,4},{6,7},{7,6},{8,9},{9,8},{10,11... | collective-permute-start | bytes 3145736 | tf_op jit(solution)/shard_map/ppermute | solution.py:419
  135.6 9.5 %collective-permute-start.31 = (f16[272,512]{1,0:T(8,128)(2,1)S(1)}, f16[272,512]{1,0:T(8,128)(2,1)S(1)}, u32[]{:S(2)}, u32[]{:S(2)}) collective-permute-start(f16[272,512]{1,0:T(8,128)(2,1)S(1)} %convert_element_type.31), channel_id=1, source_target_pairs={{0,2},{1,3},{2,0},{3,1},{4,6},{5,7},{6,4},{7,5},{8,10},{9,11},{10,... | collective-permute-start | bytes 835592 | tf_op jit(solution)/shard_map/ppermute | solution.py:419
  137.7 1.7 %copy-start.10 = (f32[256,512]{1,0:T(8,128)S(1)}, f32[256,512]{1,0:T(8,128)}, u32[]{:S(2)}) copy-start(f32[256,512]{1,0:T(8,128)} %copy-done.9) | copy-start | bytes 1572868
  137.8 18.4 %collective-permute-start.28 = (f16[528,512]{1,0:T(8,128)(2,1)S(1)}, f16[528,512]{1,0:T(8,128)(2,1)S(1)}, u32[]{:S(2)}, u32[]{:S(2)}) collective-permute-start(f16[528,512]{1,0:T(8,128)(2,1)S(1)} %convert_element_type.26), channel_id=1, source_target_pairs={{0,2},{1,3},{2,0},{3,1},{4,6},{5,7},{6,4},{7,5},{8,10},{9,11},{10,... | collective-permute-start | bytes 1622024 | tf_op jit(solution)/shard_map/ppermute | solution.py:419
  139.4 5.9 %copy-start.6 = (f32[512,512]{1,0:T(8,128)S(1)}, f32[512,512]{1,0:T(8,128)}, u32[]{:S(2)}) copy-start(f32[512,512]{1,0:T(8,128)} %square) | copy-start | bytes 3145732
  140.7 4.6 %copy-start.5 = (f32[512,512]{1,0:T(8,128)S(1)}, f32[512,512]{1,0:T(8,128)}, u32[]{:S(2)}) copy-start(f32[512,512]{1,0:T(8,128)} %moment) | copy-start | bytes 3145732
  145.3 11.0 %copy-start.15 = (f32[128]{0:T(128)S(1)}, f32[128]{0:T(128)}, u32[]{:S(2)}) copy-start(f32[128]{0:T(128)} %param.12) | copy-start | bytes 1540
  145.3 11.0 %copy-start.22 = (f32[128]{0:T(128)S(1)}, f32[128]{0:T(128)}, u32[]{:S(2)}) copy-start(f32[128]{0:T(128)} %param.16) | copy-start | bytes 1540
  145.3 11.0 %copy-start.23 = (f32[128]{0:T(128)S(1)}, f32[128]{0:T(128)}, u32[]{:S(2)}) copy-start(f32[128]{0:T(128)} %param.17) | copy-start | bytes 1540
  145.3 11.6 %copy-start.2 = (f32[512,512]{1,0:T(8,128)S(1)}, f32[512,512]{1,0:T(8,128)}, u32[]{:S(2)}) copy-start(f32[512,512]{1,0:T(8,128)} %refs_0_.3) | copy-start | bytes 3145732
  145.3 11.6 %copy-start.18 = (f32[512,512]{1,0:T(8,128)S(1)}, f32[512,512]{1,0:T(8,128)}, u32[]{:S(2)}) copy-start(f32[512,512]{1,0:T(8,128)} %param.14) | copy-start | bytes 3145732
  145.3 11.6 %copy-start.19 = (f32[512,512]{1,0:T(8,128)S(1)}, f32[512,512]{1,0:T(8,128)}, u32[]{:S(2)}) copy-start(f32[512,512]{1,0:T(8,128)} %param.15) | copy-start | bytes 3145732
  (8 other events, 7.1 us)

commit v8 on v7

--- a/solution.py
+++ b/solution.py
@@ -380,6 +380,18 @@
     return block, row
 
 
+def bias_step_body(place, param, moment, square, here, there, param_out, moment_out, square_out):
+    width = param.shape[1]
+    grad = here[...] + there[...]
+    pieces = [grad[:, b * width : (b + 1) * width] for b in range(4)]
+    own = functools.reduce(
+        jnp.add, [jnp.where(place[1] == b, piece, 0.0) for b, piece in enumerate(pieces)]
+    )
+    param_out[...], moment_out[...], square_out[...] = adam_update(
+        param[...], own, moment[...], square[...]
+    )
+
+
 def decoder_step_body(
     rows, place, param, moment, square, near, far, active, norms, param_out, moment_out, square_out
 ):
@@ -586,11 +598,19 @@
     far_grad = far_kept[0] + far_kept[1] + far_block
     active_sum = active_sum + active_there
     grad_encoder = enc_kept[0] + enc_kept[1] + enc_block
-    grad_bias = (bias_here + bias_there).reshape(latents)
-    grad_bias = lax.dynamic_slice(grad_bias, (i * enc_bias.shape[0],), (enc_bias.shape[0],))
-    new_enc_bias, new_bias_moment, new_bias_square = adam_update(
-        enc_bias, grad_bias, bias_moment, bias_square
-    )
+    new_enc_bias, new_bias_moment, new_bias_square = [
+        value.reshape(-1)
+        for value in local_kernel(
+            bias_step_body,
+            [shape((1, enc_bias.shape[0]), F32)] * 3,
+            place,
+            enc_bias.reshape(1, -1),
+            bias_moment.reshape(1, -1),
+            bias_square.reshape(1, -1),
+            bias_here,
+            bias_there,
+        )
+    ]
     new_encoder, new_enc_moment, new_enc_square = adam_update(
         encoder, grad_encoder, enc_moment, enc_square
     )

time: 160 us -> 153 us (0.956)
  local copies, waits for them, and re-layouts: 7.43 us -> 2.06 us
  waiting for transfers between devices: 76.4 us -> 78.7 us
  Pallas kernels: 23.5 us -> 21.5 us
  other arithmetic: 4.59 us -> 2.92 us
    unnamed x50 -> x26, local copies, waits for them, and re-layouts: 7.41 us -> 2.04 us
    pallas_call x14 -> x15, Pallas kernels: 20.6 us -> 18.6 us  [local_kernel(): pl.pallas_call(run, out_shape=outs, in_specs=[SMEM] + [VMEM] * len(args)...]
    ppermute x18, waiting for transfers between devices: 16.1 us -> 17.9 us  [flip(): return lax.ppermute(value, ('latent', 'dp'), pairs)]
  transfers between devices with their start and end apart: 32 -> 32, of which waited for: 12 -> 12; matrix products, arithmetic and copies ran while one was open for 1% -> 0% of each run, Pallas kernels for 11% -> 11%
where the time goes in v8:
time: 153 us
  waiting for transfers between devices  78.7 us (51%)
  starting transfers between devices  46.3 us (30%)
  Pallas kernels  21.5 us (14%)
  other arithmetic  2.92 us (2%)
  local copies, waits for them, and re-layouts  2.06 us (1%)
    ppermute x14, waiting for transfers between devices, along(): return lax.ppermute(value, 'latent', pairs)  60.8 us
    ppermute x14, starting transfers between devices, along(): return lax.ppermute(value, 'latent', pairs)  37.4 us
    pallas_call x15, Pallas kernels, local_kernel(): pl.pallas_call(run, out_shape=outs, in_specs=[SMEM] + [VMEM] * len(args)...  18.6 us
    ppermute x18, waiting for transfers between devices, flip(): return lax.ppermute(value, ('latent', 'dp'), pairs)  17.9 us
    ppermute x18, starting transfers between devices, flip(): return lax.ppermute(value, ('latent', 'dp'), pairs)  8.92 us
  transfers between devices with their start and end apart: 32, of which 12 were waited for; matrix products, arithmetic and copies ran while one was open for 0% of the time, Pallas kernels for 11%

profile of v8, /device:TPU:0, one launch (start us, length us, event | category | flops | bytes accessed | tf_op | source)
XLA Modules:
  0.0 152.7 jit_solution(7545424225886839621)
XLA Ops:
  0.7 1.3 copy-done.1
  2.0 0.7 copy-done.6
  3.8 5.8 %collective-permute-start.2 = (bf16[384,512]{1,0:T(8,128)(2,1)S(1)}, bf16[384,512]{1,0:T(8,128)(2,1)S(1)}, u32[]{:S(2)}, u32[]{:S(2)}) collective-permute-start(bf16[384,512]{1,0:T(8,128)(2,1)S(1)} %copy-done.5), channel_id=1, source_target_pairs={{0,8},{12,4},{1,9},{13,5},{2,10},{14,6},{3,11},{15,7},{16,24},{28,... | collective-permute-start | bytes 1179656 | tf_op jit(solution)/shard_map/ppermute | solution.py:427
  9.6 1.3 collective-permute-start.1
  10.9 4.6 %collective-permute-start = (bf16[384,512]{1,0:T(8,128)(2,1)S(1)}, bf16[384,512]{1,0:T(8,128)(2,1)S(1)}, u32[]{:S(2)}, u32[]{:S(2)}) collective-permute-start(bf16[384,512]{1,0:T(8,128)(2,1)S(1)} %copy-done.5), channel_id=1, source_target_pairs={{0,4},{4,8},{8,12},{1,5},{5,9},{9,13},{2,6},{6,10},{10,14},{3,7},{... | collective-permute-start | bytes 1179656 | tf_op jit(solution)/shard_map/ppermute | solution.py:427
  15.5 1.6 %collective-permute-start.6 = (bf16[528,512]{1,0:T(8,128)(2,1)S(1)}, bf16[528,512]{1,0:T(8,128)(2,1)S(1)}, u32[]{:S(2)}, u32[]{:S(2)}) collective-permute-start(bf16[528,512]{1,0:T(8,128)(2,1)S(1)} %shard_map.178.refs_6_), channel_id=1, source_target_pairs={{0,2},{1,3},{2,0},{3,1},{4,6},{5,7},{6,4},{7,5},{8,10},{9,11},{10,... | collective-permute-start | bytes 1622024 | tf_op jit(solution)/shard_map/ppermute | solution.py:431
  17.1 0.6 shard_map.179.refs_0_.refs_4_.refs_3_
  18.3 0.8 collective-permute-done.2.refs_3_
  19.1 1.3 collective-permute-start.4
  21.0 1.6 %collective-permute-done.1.refs_1_.refs_2_ = bf16[384,512]{1,0:T(8,128)(2,1)S(1)} collective-permute-done((bf16[384,512]{1,0:T(8,128)(2,1)S(1)}, bf16[384,512]{1,0:T(8,128)(2,1)S(1)}, u32[]{:S(2)}, u32[]{:S(2)}) %collective-permute-start.1) | collective-permute-done | bytes 393248 | tf_op jit(solution)/shard_map/ppermute | solution.py:427
  22.6 8.4 %collective-permute-start.8 = (bf16[256,512]{1,0:T(8,128)(2,1)S(1)}, bf16[256,512]{1,0:T(8,128)(2,1)S(1)}, u32[]{:S(2)}, u32[]{:S(2)}) collective-permute-start(bf16[256,512]{1,0:T(8,128)(2,1)S(1)} %get-tuple-element.62), channel_id=1, source_target_pairs={{0,4},{4,8},{1,5},{5,9},{2,6},{6,10},{3,7},{7,11},{16,20},{20,24},... | collective-permute-start | bytes 786440 | tf_op jit(solution)/shard_map/ppermute | solution.py:427
  31.0 0.7 collective-permute-start.10
  31.7 5.2 %collective-permute-start.11 = (bf16[256,512]{1,0:T(8,128)(2,1)S(1)}, bf16[256,512]{1,0:T(8,128)(2,1)S(1)}, u32[]{:S(2)}, u32[]{:S(2)}) collective-permute-start(bf16[256,512]{1,0:T(8,128)(2,1)S(1)} %get-tuple-element.66), channel_id=1, source_target_pairs={{0,8},{12,4},{1,9},{13,5},{2,10},{14,6},{3,11},{15,7},{16,24},{28,... | collective-permute-start | bytes 786440 | tf_op jit(solution)/shard_map/ppermute | solution.py:427
  37.6 1.3 collective-permute-start.3
  38.9 1.8 %collective-permute-done.9.refs_6_.refs_5_ = bf16[528,512]{1,0:T(8,128)(2,1)S(1)} collective-permute-done((bf16[528,512]{1,0:T(8,128)(2,1)S(1)}, bf16[528,512]{1,0:T(8,128)(2,1)S(1)}, u32[]{:S(2)}, u32[]{:S(2)}) %collective-permute-start.9) | collective-permute-done | bytes 540704 | tf_op jit(solution)/shard_map/ppermute | solution.py:431
  40.8 1.6 %collective-permute-done.11 = bf16[256,512]{1,0:T(8,128)(2,1)S(1)} collective-permute-done((bf16[256,512]{1,0:T(8,128)(2,1)S(1)}, bf16[256,512]{1,0:T(8,128)(2,1)S(1)}, u32[]{:S(2)}, u32[]{:S(2)}) %collective-permute-start.11) | collective-permute-done | bytes 262176 | tf_op jit(solution)/shard_map/ppermute | solution.py:427
  42.4 0.7 collective-permute-start.18
  43.2 6.1 %collective-permute-done.3.refs_4_ = bf16[384,512]{1,0:T(8,128)(2,1)S(1)} collective-permute-done((bf16[384,512]{1,0:T(8,128)(2,1)S(1)}, bf16[384,512]{1,0:T(8,128)(2,1)S(1)}, u32[]{:S(2)}, u32[]{:S(2)}) %collective-permute-start.3) | collective-permute-done | bytes 393248 | tf_op jit(solution)/shard_map/ppermute | solution.py:427
  49.4 1.8 %shard_map.181 = (bf16[384,512]{1,0:T(8,128)(2,1)S(1)}, bf16[384,512]{1,0:T(8,128)(2,1)S(1)}, bf16[384,2048]{1,0:T(8,128)(2,1)S(1)}, f32[1,512]{1,0:T(1,128)S(1)}) custom-call(s32[2]{0:T(128)S(1)} %pad_add_fusion.place, bf16[384,512]{1,0:T(8,128)(2,1)S(1)} %copy-done.5, bf16[384,512]{1,0:T(8,128)(2,1)S(1)} %collective-permute-done.refs_0_.refs_1_, ...), custom_call_target="tpu_custom_call" | custom-call | flops 1 | bytes 1 | tf_op jit(solution)/shard_map/pallas_call | solution.py:121
  51.1 2.0 %collective-permute-start.14 = (bf16[384,512]{1,0:T(8,128)(2,1)S(1)}, bf16[384,512]{1,0:T(8,128)(2,1)S(1)}, u32[]{:S(2)}, u32[]{:S(2)}) collective-permute-start(bf16[384,512]{1,0:T(8,128)(2,1)S(1)} %get-tuple-element.69.refs_0_.refs_2_.refs_4_), channel_id=1, source_target_pairs={{0,8},{12,4},{1,9},{13,5},{2,10},{14,6},{3,11},{15,7},{16,24},{28,... | collective-permute-start | bytes 1179656 | tf_op jit(solution)/shard_map/ppermute | solution.py:427
  53.1 0.7 collective-permute-start.13
  53.8 2.9 %collective-permute-start.12 = (bf16[384,512]{1,0:T(8,128)(2,1)S(1)}, bf16[384,512]{1,0:T(8,128)(2,1)S(1)}, u32[]{:S(2)}, u32[]{:S(2)}) collective-permute-start(bf16[384,512]{1,0:T(8,128)(2,1)S(1)} %get-tuple-element.69.refs_0_.refs_2_.refs_4_), channel_id=1, source_target_pairs={{0,4},{4,8},{1,5},{5,9},{2,6},{6,10},{3,7},{7,11},{16,20},{20,24},... | collective-permute-start | bytes 1179656 | tf_op jit(solution)/shard_map/ppermute | solution.py:427
  56.7 1.0 shard_map.182.refs_7_.refs_0_
  57.7 0.7 collective-permute-start.17
  58.5 4.1 %collective-permute-done.14.refs_3_ = bf16[384,512]{1,0:T(8,128)(2,1)S(1)} collective-permute-done((bf16[384,512]{1,0:T(8,128)(2,1)S(1)}, bf16[384,512]{1,0:T(8,128)(2,1)S(1)}, u32[]{:S(2)}, u32[]{:S(2)}) %collective-permute-start.14) | collective-permute-done | bytes 393248 | tf_op jit(solution)/shard_map/ppermute | solution.py:427
  62.5 8.0 %collective-permute-done.12.refs_1_ = bf16[384,512]{1,0:T(8,128)(2,1)S(1)} collective-permute-done((bf16[384,512]{1,0:T(8,128)(2,1)S(1)}, bf16[384,512]{1,0:T(8,128)(2,1)S(1)}, u32[]{:S(2)}, u32[]{:S(2)}) %collective-permute-start.12) | collective-permute-done | bytes 393248 | tf_op jit(solution)/shard_map/ppermute | solution.py:427
  70.5 0.7 collective-permute-start.19
  71.3 2.4 %shard_map.183.refs_0_ = bf16[384,1024]{1,0:T(8,128)(2,1)S(1)} custom-call(s32[2]{0:T(128)S(1)} %pad_add_fusion.place, bf16[384,512]{1,0:T(8,128)(2,1)S(1)} %get-tuple-element.69.refs_0_.refs_2_.refs_4_, bf16[384,512]{1,0:T(8,128)(2,1)S(1)} %collective-permute-done.12.refs_1_, bf16[384,512]{1,0:T(8,128)(2,1)S(1)} %collective-permute-done.13.refs_2_, ...), custom_call_target="tpu_custom_call" | custom-call | flops 1 | bytes 1 | tf_op jit(solution)/shard_map/pallas_call | solution.py:121
  73.7 1.3 collective-permute-start.22
  75.0 0.7 collective-permute-start.20
  75.7 1.3 collective-permute-start.21
  77.0 23.6 %collective-permute-done.22.refs_1_ = bf16[384,1024]{1,0:T(8,128)(2,1)S(1)} collective-permute-done((bf16[384,1024]{1,0:T(8,128)(2,1)S(1)}, bf16[384,1024]{1,0:T(8,128)(2,1)S(1)}, u32[]{:S(2)}, u32[]{:S(2)}) %collective-permute-start.22) | collective-permute-done | bytes 786464 | tf_op jit(solution)/shard_map/ppermute | solution.py:427
  100.6 1.8 %shard_map.184 = (f32[384,512]{1,0:T(8,128)S(1)}, bf16[384,1024]{1,0:T(8,128)(2,1)S(1)}, f32[264,512]{1,0:T(8,128)S(1)}, f32[256,512]{1,0:T(8,128)S(1)}, f32[256,512]{1,0:T(8,128)S(1)}, /*index=5*/f32[256,512]{1,0:T(8,128)S(1)}) custom-call(s32[2]{0:T(128)S(1)} %pad_add_fusion.place, bf16[384,1024]{1,0:T(8,128)(2,1)S(1)} %shard_map.183.refs_0_, ...), custom_call_target="tpu_custom_call" | custom-call | flops 1 | bytes 1 | tf_op jit(solution)/shard_map/pallas_call | solution.py:121
  102.5 1.9 %collective-permute-done.23.refs_1_ = f32[264,512]{1,0:T(8,128)S(1)} collective-permute-done((f32[264,512]{1,0:T(8,128)S(1)}, f32[264,512]{1,0:T(8,128)S(1)}, u32[]{:S(2)}, u32[]{:S(2)}) %collective-permute-start.23) | collective-permute-done | bytes 540704 | tf_op jit(solution)/shard_map/ppermute | solution.py:431
  104.4 0.7 shard_map.185
  105.7 14.9 %collective-permute-done.21.refs_1_ = bf16[384,1024]{1,0:T(8,128)(2,1)S(1)} collective-permute-done((bf16[384,1024]{1,0:T(8,128)(2,1)S(1)}, bf16[384,1024]{1,0:T(8,128)(2,1)S(1)}, u32[]{:S(2)}, u32[]{:S(2)}) %collective-permute-start.21) | collective-permute-done | bytes 786464 | tf_op jit(solution)/shard_map/ppermute | solution.py:427
  120.6 1.1 shard_map.186
  121.7 1.7 %shard_map.187 = (bf16[384,512]{1,0:T(8,128)(2,1)S(1)}, f32[1,512]{1,0:T(1,128)S(1)}, f32[1,512]{1,0:T(1,128)S(1)}, f32[520,512]{1,0:T(8,128)S(1)}) custom-call(s32[2]{0:T(128)S(1)} %pad_add_fusion.place, bf16[384,1024]{1,0:T(8,128)(2,1)S(1)} %get-tuple-element.76.refs_0_.refs_3_, f32[384,512]{1,0:T(8,128)S(1)} %get-tuple-element.78.refs_1_, ...), custom_call_target="tpu_custom_call" | custom-call | flops 1 | bytes 1 | tf_op jit(solution)/shard_map/pallas_call | solution.py:121
  124.1 2.6 %shard_map.188 = (bf16[384,512]{1,0:T(8,128)(2,1)}, f32[512,512]{1,0:T(8,128)S(1)}, f32[512,512]{1,0:T(8,128)S(1)}, f32[512,512]{1,0:T(8,128)S(1)}, f32[256,512]...) custom-call(s32[2]{0:T(128)S(1)} %pad_add_fusion.place, ...), custom_call_target="tpu_custom_call" | custom-call | flops 1 | bytes 1 | tf_op jit(solution)/shard_map/pallas_call | solution.py:121
  127.3 1.2 shard_map.189
  128.5 0.6 collective-permute-start.31
  129.1 0.8 shard_map.190
  130.1 1.6 %collective-permute-start.28 = (f16[528,512]{1,0:T(8,128)(2,1)S(1)}, f16[528,512]{1,0:T(8,128)(2,1)S(1)}, u32[]{:S(2)}, u32[]{:S(2)}) collective-permute-start(f16[528,512]{1,0:T(8,128)(2,1)S(1)} %convert_element_type.26), channel_id=1, source_target_pairs={{0,2},{1,3},{2,0},{3,1},{4,6},{5,7},{6,4},{7,5},{8,10},{9,11},{10,... | collective-permute-start | bytes 1622024 | tf_op jit(solution)/shard_map/ppermute | solution.py:431
  131.8 6.3 %collective-permute-done.31 = f16[272,512]{1,0:T(8,128)(2,1)S(1)} collective-permute-done((f16[272,512]{1,0:T(8,128)(2,1)S(1)}, f16[272,512]{1,0:T(8,128)(2,1)S(1)}, u32[]{:S(2)}, u32[]{:S(2)}) %collective-permute-start.31) | collective-permute-done | bytes 278560 | tf_op jit(solution)/shard_map/ppermute | solution.py:431
  138.3 2.9 %shard_map.192 = (f32[512,512]{1,0:T(8,128)}, f32[512,512]{1,0:T(8,128)}, f32[512,512]{1,0:T(8,128)}) custom-call(s32[2]{0:T(128)S(1)} %pad_add_fusion.place, f32[512,512]{1,0:T(8,128)S(1)} %copy-done, f32[512,512]{1,0:T(8,128)S(1)} %copy-done.3, f32[512,512]{1,0:T(8,128)S(1)} %copy-done.4, f32[256,512]{1,0:T(8,128)S(1)} %multiply_add_fusion.3.near, ...), custom_call_target="tpu_custom_call" | custom-call | flops 1 | bytes 1 | tf_op jit(solution)/shard_map/pallas_call | solution.py:621
  141.2 7.9 %collective-permute-done.28 = f16[528,512]{1,0:T(8,128)(2,1)S(1)} collective-permute-done((f16[528,512]{1,0:T(8,128)(2,1)S(1)}, f16[528,512]{1,0:T(8,128)(2,1)S(1)}, u32[]{:S(2)}, u32[]{:S(2)}) %collective-permute-start.28) | collective-permute-done | bytes 540704 | tf_op jit(solution)/shard_map/ppermute | solution.py:431
  149.2 1.1 shard_map.191
  150.3 2.3 %divide_subtract_fusion = (f32[512,512]{1,0:T(8,128)}, f32[512,512]{1,0:T(8,128)}, f32[512,512]{1,0:T(8,128)}) fusion(f32[512,512]{1,0:T(8,128)S(1)} %copy-done.2, f32[512]{0:T(512)S(1)} %bitcast.15, f16[528,512]{1,0:T(8,128)(2,1)S(1)} %collective-permute-done.28, f32[512,512]{1,0:T(8,128)S(1)} %get-tuple-element.93, ...), kind=kLoop, calls=%fused_computation.2 | loop fusion | flops 4194304 | bytes 8914944 | tf_op jit(solution)/shard_map/sub | solution.py:28
  (71 shorter events, 5.6 us)
Async XLA Ops:
  0.6 16.4 %copy-start = (f32[512,512]{1,0:T(8,128)S(1)}, f32[512,512]{1,0:T(8,128)}, u32[]{:S(2)}) copy-start(f32[512,512]{1,0:T(8,128)} %param.20) | copy-start | bytes 3145732
  0.7 1.3 copy-start.1
  2.0 0.7 copy-start.6
  2.7 1.1 copy-start.5
  3.3 13.8 %collective-permute-start.5 = (bf16[528,512]{1,0:T(8,128)(2,1)S(1)}, bf16[528,512]{1,0:T(8,128)(2,1)S(1)}, u32[]{:S(2)}, u32[]{:S(2)}) collective-permute-start(bf16[528,512]{1,0:T(8,128)(2,1)S(1)} %shard_map.178.refs_6_), channel_id=1, source_target_pairs={{0,1},{1,0},{2,3},{3,2},{4,5},{5,4},{6,7},{7,6},{8,9},{9,8},{10,11... | collective-permute-start | bytes 1622024 | tf_op jit(solution)/shard_map/ppermute | solution.py:431
  3.8 15.3 %collective-permute-start.2 = (bf16[384,512]{1,0:T(8,128)(2,1)S(1)}, bf16[384,512]{1,0:T(8,128)(2,1)S(1)}, u32[]{:S(2)}, u32[]{:S(2)}) collective-permute-start(bf16[384,512]{1,0:T(8,128)(2,1)S(1)} %copy-done.5), channel_id=1, source_target_pairs={{0,8},{12,4},{1,9},{13,5},{2,10},{14,6},{3,11},{15,7},{16,24},{28,... | collective-permute-start | bytes 1179656 | tf_op jit(solution)/shard_map/ppermute | solution.py:427
  9.6 13.0 %collective-permute-start.1 = (bf16[384,512]{1,0:T(8,128)(2,1)S(1)}, bf16[384,512]{1,0:T(8,128)(2,1)S(1)}, u32[]{:S(2)}, u32[]{:S(2)}) collective-permute-start(bf16[384,512]{1,0:T(8,128)(2,1)S(1)} %copy-done.5), channel_id=1, source_target_pairs={{4,0},{8,4},{12,8},{5,1},{9,5},{13,9},{6,2},{10,6},{14,10},{7,3},{... | collective-permute-start | bytes 1179656 | tf_op jit(solution)/shard_map/ppermute | solution.py:427
  10.9 20.1 %collective-permute-start = (bf16[384,512]{1,0:T(8,128)(2,1)S(1)}, bf16[384,512]{1,0:T(8,128)(2,1)S(1)}, u32[]{:S(2)}, u32[]{:S(2)}) collective-permute-start(bf16[384,512]{1,0:T(8,128)(2,1)S(1)} %copy-done.5), channel_id=1, source_target_pairs={{0,4},{4,8},{8,12},{1,5},{5,9},{9,13},{2,6},{6,10},{10,14},{3,7},{... | collective-permute-start | bytes 1179656 | tf_op jit(solution)/shard_map/ppermute | solution.py:427
  15.5 16.2 %collective-permute-start.6 = (bf16[528,512]{1,0:T(8,128)(2,1)S(1)}, bf16[528,512]{1,0:T(8,128)(2,1)S(1)}, u32[]{:S(2)}, u32[]{:S(2)}) collective-permute-start(bf16[528,512]{1,0:T(8,128)(2,1)S(1)} %shard_map.178.refs_6_), channel_id=1, source_target_pairs={{0,2},{1,3},{2,0},{3,1},{4,6},{5,7},{6,4},{7,5},{8,10},{9,11},{10,... | collective-permute-start | bytes 1622024 | tf_op jit(solution)/shard_map/ppermute | solution.py:431
  17.7 23.0 %collective-permute-start.9 = (bf16[528,512]{1,0:T(8,128)(2,1)S(1)}, bf16[528,512]{1,0:T(8,128)(2,1)S(1)}, u32[]{:S(2)}, u32[]{:S(2)}) collective-permute-start(bf16[528,512]{1,0:T(8,128)(2,1)S(1)} %shard_map.179.refs_0_.refs_4_.refs_3_), channel_id=1, source_target_pairs={{0,2},{1,3},{2,0},{3,1},{4,6},{5,7},{6,4},{7,5},{8,10},{9,11},{10,... | collective-permute-start | bytes 1622024 | tf_op jit(solution)/shard_map/ppermute | solution.py:431
  19.1 18.4 %collective-permute-start.4 = (bf16[384,512]{1,0:T(8,128)(2,1)S(1)}, bf16[384,512]{1,0:T(8,128)(2,1)S(1)}, u32[]{:S(2)}, u32[]{:S(2)}) collective-permute-start(bf16[384,512]{1,0:T(8,128)(2,1)S(1)} %collective-permute-done.2.refs_3_), channel_id=1, source_target_pairs={{4,0},{8,12},{5,1},{9,13},{6,2},{10,14},{7,3},{11,15},{20,16},{24,... | collective-permute-start | bytes 1179656 | tf_op jit(solution)/shard_map/ppermute | solution.py:427
  22.6 16.2 %collective-permute-start.8 = (bf16[256,512]{1,0:T(8,128)(2,1)S(1)}, bf16[256,512]{1,0:T(8,128)(2,1)S(1)}, u32[]{:S(2)}, u32[]{:S(2)}) collective-permute-start(bf16[256,512]{1,0:T(8,128)(2,1)S(1)} %get-tuple-element.62), channel_id=1, source_target_pairs={{0,4},{4,8},{1,5},{5,9},{2,6},{6,10},{3,7},{7,11},{16,20},{20,24},... | collective-permute-start | bytes 786440 | tf_op jit(solution)/shard_map/ppermute | solution.py:427
  31.0 9.7 %collective-permute-start.10 = (bf16[256,512]{1,0:T(8,128)(2,1)S(1)}, bf16[256,512]{1,0:T(8,128)(2,1)S(1)}, u32[]{:S(2)}, u32[]{:S(2)}) collective-permute-start(bf16[256,512]{1,0:T(8,128)(2,1)S(1)} %get-tuple-element.64), channel_id=1, source_target_pairs={{8,4},{12,8},{9,5},{13,9},{10,6},{14,10},{11,7},{15,11},{24,20},{2... | collective-permute-start | bytes 786440 | tf_op jit(solution)/shard_map/ppermute | solution.py:427
  31.7 10.6 %collective-permute-start.11 = (bf16[256,512]{1,0:T(8,128)(2,1)S(1)}, bf16[256,512]{1,0:T(8,128)(2,1)S(1)}, u32[]{:S(2)}, u32[]{:S(2)}) collective-permute-start(bf16[256,512]{1,0:T(8,128)(2,1)S(1)} %get-tuple-element.66), channel_id=1, source_target_pairs={{0,8},{12,4},{1,9},{13,5},{2,10},{14,6},{3,11},{15,7},{16,24},{28,... | collective-permute-start | bytes 786440 | tf_op jit(solution)/shard_map/ppermute | solution.py:427
  37.6 11.8 %collective-permute-start.3 = (bf16[384,512]{1,0:T(8,128)(2,1)S(1)}, bf16[384,512]{1,0:T(8,128)(2,1)S(1)}, u32[]{:S(2)}, u32[]{:S(2)}) collective-permute-start(bf16[384,512]{1,0:T(8,128)(2,1)S(1)} %shard_map.177), channel_id=1, source_target_pairs={{4,0},{8,12},{5,1},{9,13},{6,2},{10,14},{7,3},{11,15},{20,16},{24,... | collective-permute-start | bytes 1179656 | tf_op jit(solution)/shard_map/ppermute | solution.py:427
  38.9 14.9 %collective-permute-start.15 = (bf16[528,512]{1,0:T(8,128)(2,1)S(1)}, bf16[528,512]{1,0:T(8,128)(2,1)S(1)}, u32[]{:S(2)}, u32[]{:S(2)}) collective-permute-start(bf16[528,512]{1,0:T(8,128)(2,1)S(1)} %shard_map.179.refs_0_.refs_4_.refs_3_), channel_id=1, source_target_pairs={{0,1},{1,0},{2,3},{3,2},{4,5},{5,4},{6,7},{7,6},{8,9},{9,8},{10,11... | collective-permute-start | bytes 1622024 | tf_op jit(solution)/shard_map/ppermute | solution.py:431
  40.7 8.7 %collective-permute-start.7 = (bf16[528,512]{1,0:T(8,128)(2,1)S(1)}, bf16[528,512]{1,0:T(8,128)(2,1)S(1)}, u32[]{:S(2)}, u32[]{:S(2)}) collective-permute-start(bf16[528,512]{1,0:T(8,128)(2,1)S(1)} %collective-permute-done.6.refs_8_), channel_id=1, source_target_pairs={{0,1},{1,0},{2,3},{3,2},{4,5},{5,4},{6,7},{7,6},{8,9},{9,8},{10,11... | collective-permute-start | bytes 1622024 | tf_op jit(solution)/shard_map/ppermute | solution.py:431
  42.4 28.1 %collective-permute-start.18 = (bf16[768,512]{1,0:T(8,128)(2,1)S(1)}, bf16[768,512]{1,0:T(8,128)(2,1)S(1)}, u32[]{:S(2)}, u32[]{:S(2)}) collective-permute-start(bf16[768,512]{1,0:T(8,128)(2,1)S(1)} %constant_dynamic-update-slice_fusion.refs_10_.refs_8_), channel_id=1, source_target_pairs={{4,6},{5,7},{6,4},{7,5},{8,10},{9,11},{10,8},{11,9},{20,22},{21,23... | collective-permute-start | bytes 2359304 | tf_op jit(solution)/shard_map/ppermute | solution.py:431
  43.1 14.6 %collective-permute-start.16 = (bf16[528,512]{1,0:T(8,128)(2,1)S(1)}, bf16[528,512]{1,0:T(8,128)(2,1)S(1)}, u32[]{:S(2)}, u32[]{:S(2)}) collective-permute-start(bf16[528,512]{1,0:T(8,128)(2,1)S(1)} %collective-permute-done.9.refs_6_.refs_5_), channel_id=1, source_target_pairs={{0,1},{1,0},{2,3},{3,2},{4,5},{5,4},{6,7},{7,6},{8,9},{9,8},{10,11... | collective-permute-start | bytes 1622024 | tf_op jit(solution)/shard_map/ppermute | solution.py:431
  51.1 11.4 %collective-permute-start.14 = (bf16[384,512]{1,0:T(8,128)(2,1)S(1)}, bf16[384,512]{1,0:T(8,128)(2,1)S(1)}, u32[]{:S(2)}, u32[]{:S(2)}) collective-permute-start(bf16[384,512]{1,0:T(8,128)(2,1)S(1)} %get-tuple-element.69.refs_0_.refs_2_.refs_4_), channel_id=1, source_target_pairs={{0,8},{12,4},{1,9},{13,5},{2,10},{14,6},{3,11},{15,7},{16,24},{28,... | collective-permute-start | bytes 1179656 | tf_op jit(solution)/shard_map/ppermute | solution.py:427
  53.1 9.4 %collective-permute-start.13 = (bf16[384,512]{1,0:T(8,128)(2,1)S(1)}, bf16[384,512]{1,0:T(8,128)(2,1)S(1)}, u32[]{:S(2)}, u32[]{:S(2)}) collective-permute-start(bf16[384,512]{1,0:T(8,128)(2,1)S(1)} %get-tuple-element.69.refs_0_.refs_2_.refs_4_), channel_id=1, source_target_pairs={{8,4},{12,8},{9,5},{13,9},{10,6},{14,10},{11,7},{15,11},{24,20},{2... | collective-permute-start | bytes 1179656 | tf_op jit(solution)/shard_map/ppermute | solution.py:427
  53.8 16.7 %collective-permute-start.12 = (bf16[384,512]{1,0:T(8,128)(2,1)S(1)}, bf16[384,512]{1,0:T(8,128)(2,1)S(1)}, u32[]{:S(2)}, u32[]{:S(2)}) collective-permute-start(bf16[384,512]{1,0:T(8,128)(2,1)S(1)} %get-tuple-element.69.refs_0_.refs_2_.refs_4_), channel_id=1, source_target_pairs={{0,4},{4,8},{1,5},{5,9},{2,6},{6,10},{3,7},{7,11},{16,20},{20,24},... | collective-permute-start | bytes 1179656 | tf_op jit(solution)/shard_map/ppermute | solution.py:427
  57.7 13.5 %collective-permute-start.17 = (bf16[768,512]{1,0:T(8,128)(2,1)S(1)}, bf16[768,512]{1,0:T(8,128)(2,1)S(1)}, u32[]{:S(2)}, u32[]{:S(2)}) collective-permute-start(bf16[768,512]{1,0:T(8,128)(2,1)S(1)} %constant_dynamic-update-slice_fusion.refs_10_.refs_8_), channel_id=1, source_target_pairs={{4,5},{5,4},{6,7},{7,6},{8,9},{9,8},{10,11},{11,10},{20,21},{21,20... | collective-permute-start | bytes 2359304 | tf_op jit(solution)/shard_map/ppermute | solution.py:431
  70.5 0.7 collective-permute-start.19
  73.7 26.9 %collective-permute-start.22 = (bf16[384,1024]{1,0:T(8,128)(2,1)S(1)}, bf16[384,1024]{1,0:T(8,128)(2,1)S(1)}, u32[]{:S(2)}, u32[]{:S(2)}) collective-permute-start(bf16[384,1024]{1,0:T(8,128)(2,1)S(1)} %shard_map.183.refs_0_), channel_id=1, source_target_pairs={{4,0},{8,12},{5,1},{9,13},{6,2},{10,14},{7,3},{11,15},{20,16},{24,... | collective-permute-start | bytes 2359304 | tf_op jit(solution)/shard_map/ppermute | solution.py:427
  75.0 25.6 %collective-permute-start.20 = (bf16[384,1024]{1,0:T(8,128)(2,1)S(1)}, bf16[384,1024]{1,0:T(8,128)(2,1)S(1)}, u32[]{:S(2)}, u32[]{:S(2)}) collective-permute-start(bf16[384,1024]{1,0:T(8,128)(2,1)S(1)} %shard_map.183.refs_0_), channel_id=1, source_target_pairs={{4,8},{8,4},{5,9},{9,5},{6,10},{10,6},{7,11},{11,7},{20,24},{24,20... | collective-permute-start | bytes 2359304 | tf_op jit(solution)/shard_map/ppermute | solution.py:427
  75.7 44.9 %collective-permute-start.21 = (bf16[384,1024]{1,0:T(8,128)(2,1)S(1)}, bf16[384,1024]{1,0:T(8,128)(2,1)S(1)}, u32[]{:S(2)}, u32[]{:S(2)}) collective-permute-start(bf16[384,1024]{1,0:T(8,128)(2,1)S(1)} %shard_map.183.refs_0_), channel_id=1, source_target_pairs={{8,0},{4,12},{9,1},{5,13},{10,2},{6,14},{11,3},{7,15},{24,16},{20,... | collective-permute-start | bytes 2359304 | tf_op jit(solution)/shard_map/ppermute | solution.py:427
  102.4 2.0 %collective-permute-start.23 = (f32[264,512]{1,0:T(8,128)S(1)}, f32[264,512]{1,0:T(8,128)S(1)}, u32[]{:S(2)}, u32[]{:S(2)}) collective-permute-start(f32[264,512]{1,0:T(8,128)S(1)} %get-tuple-element.74), channel_id=1, source_target_pairs={{0,1},{1,0},{2,3},{3,2},{4,5},{5,4},{6,7},{7,6},{8,9},{9,8},{10,11... | collective-permute-start | bytes 1622024 | tf_op jit(solution)/shard_map/ppermute | solution.py:431
  105.1 16.6 %collective-permute-start.24 = (f16[272,512]{1,0:T(8,128)(2,1)S(1)}, f16[272,512]{1,0:T(8,128)(2,1)S(1)}, u32[]{:S(2)}, u32[]{:S(2)}) collective-permute-start(f16[272,512]{1,0:T(8,128)(2,1)S(1)} %convert_element_type.25), channel_id=1, source_target_pairs={{0,2},{1,3},{2,0},{3,1},{4,6},{5,7},{6,4},{7,5},{8,10},{9,11},{10,... | collective-permute-start | bytes 835592 | tf_op jit(solution)/shard_map/ppermute | solution.py:431
  123.5 5.7 %collective-permute-start.26 = (f32[520,512]{1,0:T(8,128)S(1)}, f32[520,512]{1,0:T(8,128)S(1)}, u32[]{:S(2)}, u32[]{:S(2)}) collective-permute-start(f32[520,512]{1,0:T(8,128)S(1)} %get-tuple-element.88), channel_id=1, source_target_pairs={{0,1},{1,0},{2,3},{3,2},{4,5},{5,4},{6,7},{7,6},{8,9},{9,8},{10,11... | collective-permute-start | bytes 3194888 | tf_op jit(solution)/shard_map/ppermute | solution.py:431
  123.5 3.7 %collective-permute-start.25 = (f32[256,512]{1,0:T(8,128)S(1)}, f32[256,512]{1,0:T(8,128)S(1)}, u32[]{:S(2)}, u32[]{:S(2)}) collective-permute-start(f32[256,512]{1,0:T(8,128)S(1)} %get-tuple-element.85), channel_id=1, source_target_pairs={{0,1},{1,0},{2,3},{3,2},{4,5},{5,4},{6,7},{7,6},{8,9},{9,8},{10,11... | collective-permute-start | bytes 1572872 | tf_op jit(solution)/shard_map/ppermute | solution.py:431
  124.0 7.6 %collective-permute-start.29 = (f32[256,512]{1,0:T(8,128)S(1)}, f32[256,512]{1,0:T(8,128)S(1)}, u32[]{:S(2)}, u32[]{:S(2)}) collective-permute-start(f32[256,512]{1,0:T(8,128)S(1)} %get-tuple-element.102), channel_id=1, source_target_pairs={{0,1},{1,0},{2,3},{3,2},{4,5},{5,4},{6,7},{7,6},{8,9},{9,8},{10,11... | collective-permute-start | bytes 1572872 | tf_op jit(solution)/shard_map/ppermute | solution.py:431
  126.8 11.3 %collective-permute-start.30 = (f32[256,512]{1,0:T(8,128)S(1)}, f32[256,512]{1,0:T(8,128)S(1)}, u32[]{:S(2)}, u32[]{:S(2)}) collective-permute-start(f32[256,512]{1,0:T(8,128)S(1)} %get-tuple-element.104), channel_id=1, source_target_pairs={{0,1},{1,0},{2,3},{3,2},{4,5},{5,4},{6,7},{7,6},{8,9},{9,8},{10,11... | collective-permute-start | bytes 1572872 | tf_op jit(solution)/shard_map/ppermute | solution.py:431
  127.2 23.1 %collective-permute-start.27 = (f32[512,512]{1,0:T(8,128)S(1)}, f32[512,512]{1,0:T(8,128)S(1)}, u32[]{:S(2)}, u32[]{:S(2)}) collective-permute-start(f32[512,512]{1,0:T(8,128)S(1)} %get-tuple-element.94), channel_id=1, source_target_pairs={{0,1},{1,0},{2,3},{3,2},{4,5},{5,4},{6,7},{7,6},{8,9},{9,8},{10,11... | collective-permute-start | bytes 3145736 | tf_op jit(solution)/shard_map/ppermute | solution.py:431
  128.5 9.5 %collective-permute-start.31 = (f16[272,512]{1,0:T(8,128)(2,1)S(1)}, f16[272,512]{1,0:T(8,128)(2,1)S(1)}, u32[]{:S(2)}, u32[]{:S(2)}) collective-permute-start(f16[272,512]{1,0:T(8,128)(2,1)S(1)} %convert_element_type.31), channel_id=1, source_target_pairs={{0,2},{1,3},{2,0},{3,1},{4,6},{5,7},{6,4},{7,5},{8,10},{9,11},{10,... | collective-permute-start | bytes 835592 | tf_op jit(solution)/shard_map/ppermute | solution.py:431
  130.1 19.1 %collective-permute-start.28 = (f16[528,512]{1,0:T(8,128)(2,1)S(1)}, f16[528,512]{1,0:T(8,128)(2,1)S(1)}, u32[]{:S(2)}, u32[]{:S(2)}) collective-permute-start(f16[528,512]{1,0:T(8,128)(2,1)S(1)} %convert_element_type.26), channel_id=1, source_target_pairs={{0,2},{1,3},{2,0},{3,1},{4,6},{5,7},{6,4},{7,5},{8,10},{9,11},{10,... | collective-permute-start | bytes 1622024 | tf_op jit(solution)/shard_map/ppermute | solution.py:431
  131.6 6.6 %copy-start.4 = (f32[512,512]{1,0:T(8,128)S(1)}, f32[512,512]{1,0:T(8,128)}, u32[]{:S(2)}) copy-start(f32[512,512]{1,0:T(8,128)} %square) | copy-start | bytes 3145732
  131.7 6.5 %copy-start.3 = (f32[512,512]{1,0:T(8,128)S(1)}, f32[512,512]{1,0:T(8,128)}, u32[]{:S(2)}) copy-start(f32[512,512]{1,0:T(8,128)} %moment) | copy-start | bytes 3145732
  138.2 11.0 %copy-start.7 = (f32[128]{0:T(128)S(1)}, f32[128]{0:T(128)}, u32[]{:S(2)}) copy-start(f32[128]{0:T(128)} %param.12) | copy-start | bytes 1540
  138.2 11.0 %copy-start.8 = (f32[128]{0:T(128)S(1)}, f32[128]{0:T(128)}, u32[]{:S(2)}) copy-start(f32[128]{0:T(128)} %param.16) | copy-start | bytes 1540
  138.2 11.0 %copy-start.9 = (f32[128]{0:T(128)S(1)}, f32[128]{0:T(128)}, u32[]{:S(2)}) copy-start(f32[128]{0:T(128)} %param.17) | copy-start | bytes 1540
  138.3 12.0 %copy-start.2 = (f32[512,512]{1,0:T(8,128)S(1)}, f32[512,512]{1,0:T(8,128)}, u32[]{:S(2)}) copy-start(f32[512,512]{1,0:T(8,128)} %refs_0_.3) | copy-start | bytes 3145732
  138.3 12.0 %copy-start.10 = (f32[512,512]{1,0:T(8,128)S(1)}, f32[512,512]{1,0:T(8,128)}, u32[]{:S(2)}) copy-start(f32[512,512]{1,0:T(8,128)} %param.14) | copy-start | bytes 3145732
  138.3 12.0 %copy-start.11 = (f32[512,512]{1,0:T(8,128)S(1)}, f32[512,512]{1,0:T(8,128)}, u32[]{:S(2)}) copy-start(f32[512,512]{1,0:T(8,128)} %param.15) | copy-start | bytes 3145732

commit v9 on v8

--- a/solution.py
+++ b/solution.py
@@ -305,13 +305,13 @@
     part[...] = back_through(i, near, (dec0, dec1, dec2, dec3), jnp.where(z >= 2, half, 0))
 
 
-def far_error_body(rows, place, swapped, direct, codes, far, send):
+def far_error_body(rows, place, swapped, direct, codes, far, send, kept):
     pick(place, swapped, direct, far)
-    decoder_grads(-2.0 / rows, place[1], far, codes, (3,), (send,))
+    decoder_grads(-2.0 / rows, place[1], far, codes, (3, 2), (send, kept))
 
 
 def code_grad_body(
-    rows, place, far, part, mask, dec0, dec1, dec2, dec3, turned, grad_low, bias_sum, norms, send_far
+    rows, place, far, part, mask, dec0, dec1, dec2, dec3, turned, grad_low, bias_sum, norms, *sends
 ):
     z, i = place[0], place[1]
     half = far.shape[1] // 4
@@ -326,8 +326,11 @@
     grad_low[...] = grad.astype(BF16)
     row = jnp.sum(grad, axis=0, keepdims=True)
     bias_sum[...] = row
-    encoder_grads(i, turned, grad_low, (3,), (send_far,))
-    send_far[width:] = jnp.broadcast_to(row, (send_far.shape[0] - width, row.shape[1]))
+    at = pl.multiple_of((i ^ 3) * width, width)
+    block = jnp.dot(turned[pl.ds(at, width), :], grad_low[...], preferred_element_type=F32)
+    sends[0][:half] = block[:half]
+    sends[0][half:] = jnp.broadcast_to(row, (sends[0].shape[0] - half, row.shape[1]))
+    sends[1][...] = block[half:]
 
 
 def encoder_grads(i, turned, grad_low, slots, outs):
@@ -342,7 +345,7 @@
     half = far.shape[1] // 4
     shift = jnp.where(z >= 2, 0, half)
     encoder_grads(i, turned, grad_low, (2, 1, 0), (kept_far, send, kept))
-    decoder_grads(-2.0 / rows, i, far, codes, (1, 2, 0), outs)
+    decoder_grads(-2.0 / rows, i, far, codes, (1, 0), outs)
     home[:, columns(half - shift, half)] = near[:, columns(z * half, half)]
     home[:, columns(shift, half)] = far[:, columns(z * half, half)]
 
@@ -356,14 +359,16 @@
     return jnp.exp(exponent * math.log(2.0))
 
 
-def pack_body(place, kept, received, row, packed, row_sum):
+def pack_body(place, kept, row, *refs):
+    received, (packed, row_sum) = refs[:-2], refs[-2:]
     width = kept.shape[0]
-    total = kept[...] + received[:width]
+    block = width // len(received)
+    total = jnp.concatenate([piece[:block] for piece in received], axis=0) + kept[...]
     exponent = power(total)
     packed[:width] = total * scale_of(14.0 - exponent)
     sums = row[...]
-    if received.shape[0] > width:
-        sums += received[width : width + 1]
+    if received[0].shape[0] > block:
+        sums += received[0][block : block + 1]
     row_sum[...] = sums
     row_exponent = power(sums)
     parts = three_rows(sums * scale_of(14.0 - row_exponent)).astype(F32)
@@ -491,7 +496,9 @@
     codes_low = along(codes, [(0, 1), (1, 2)])
     codes_high = along(codes, [(2, 1), (3, 2)])
     codes_across = along(codes, [(0, 2), (3, 1)])
-    (turned,) = local_kernel(turn_body, [shape((features, count), BF16)], place, inputs)
+    (turned,) = local_kernel(
+        turn_body, [shape((features, count), BF16)], place, inputs
+    )
     rows_chip = flip(rows_own, 2, (1, 2))
     rows_core = flip(behind(rows_own, turned), 1, (1, 2))
     rows_both = flip(
@@ -517,14 +524,14 @@
     passed = along(own_error, [(1, 0), (2, 3)])
     direct = along(own_error, [(2, 0), (1, 3)])
 
-    def across_chips(kept, send, row):
+    def across_chips(kept, row, *send):
         packed, row_sum = local_kernel(
             pack_body,
             [shape((kept.shape[0] + EXTRA, latents), F32), shape((1, latents), F32)],
             place,
             kept,
-            flip(send, 1),
             row,
+            *[flip(piece, 1) for piece in send],
         )
         return packed, flip(packed.astype(jnp.float16), 2), row_sum
 
@@ -541,11 +548,11 @@
         after=(swapped,),
     )
     send_far, send_near, keep_far, keep_near = near_blocks
-    near_packed, near_received, active_sum = across_chips(keep_far, send_far, active)
+    near_packed, near_received, active_sum = across_chips(keep_far, active, send_far)
     near_kept = keep_near, flip(send_near, 1)
-    far, far_send = local_kernel(
+    far, far_send, far_keep = local_kernel(
         functools.partial(far_error_body, rows),
-        [shape((count, features // 2), BF16), shape((half, latents), F32)],
+        [shape((count, features // 2), BF16)] + [shape((half, latents), F32)] * 2,
         place,
         swapped,
         direct,
@@ -553,13 +560,14 @@
         after=(near_packed,),
         cost=NOTABLE,
     )
-    grad_low, bias_sum, norms, send_far_enc = local_kernel(
+    grad_low, bias_sum, norms, *send_far_enc = local_kernel(
         functools.partial(code_grad_body, rows),
         [
             shape((count, latents), BF16),
             shape((1, latents), F32),
             shape((1, latents), F32),
-            shape((width + 8, latents), F32),
+            shape((half + 8, latents), F32),
+            shape((half, latents), F32),
         ],
         place,
         far,
@@ -567,25 +575,24 @@
         mask,
         *dec,
         turned,
-    )
-    error, enc_send_near, enc_keep_far, enc_keep_near, *far_blocks = local_kernel(
+        cost=NOTABLE,
+    )
+    far_packed, far_received, _ = across_chips(far_keep, active, far_send)
+    error, enc_send_near, enc_keep_far, enc_keep_near, send_near, keep_near = local_kernel(
         functools.partial(rest_body, rows),
         [shape((count, width), BF16)]
         + [shape((width, latents), F32)] * 3
-        + [shape((half, latents), F32)] * 3,
+        + [shape((half, latents), F32)] * 2,
         place,
         turned,
         grad_low,
         near,
         far,
         codes,
-    )
-    send_near, keep_far, keep_near = far_blocks
-    far_packed, far_received, _ = across_chips(keep_far, far_send, active)
+        after=(far_packed,),
+    )
     far_kept = keep_near, flip(send_near, 1)
-    enc_packed, enc_received, bias_here = across_chips(
-        behind(enc_keep_far, far_packed), send_far_enc, bias_sum
-    )
+    enc_packed, enc_received, bias_here = across_chips(enc_keep_far, bias_sum, *send_far_enc)
     enc_kept = enc_keep_near, flip(enc_send_near, 1)
 
     decoder, dec_moment, dec_square, encoder, enc_moment, enc_square = lax.optimization_barrier(

time: 153 us -> 150 us (0.980)
  waiting for transfers between devices: 78.7 us -> 75.2 us
    ppermute x18 -> x19, waiting for transfers between devices: 17.9 us -> 14.5 us  [flip(): return lax.ppermute(value, ('latent', 'dp'), pairs)]
    ppermute x18 -> x19, starting transfers between devices: 8.92 us -> 9.47 us  [flip(): return lax.ppermute(value, ('latent', 'dp'), pairs)]
  transfers between devices with their start and end apart: 32 -> 33, of which waited for: 12 -> 12; matrix products, arithmetic and copies ran while one was open for 0% -> 0% of each run, Pallas kernels for 11% -> 12%
where the time goes in v9:
time: 150 us
  waiting for transfers between devices  75.2 us (50%)
  starting transfers between devices  46.8 us (31%)
  Pallas kernels  21.5 us (14%)
  other arithmetic  2.9 us (2%)
  local copies, waits for them, and re-layouts  2.06 us (1%)
    ppermute x14, waiting for transfers between devices, along(): return lax.ppermute(value, 'latent', pairs)  60.8 us
    ppermute x14, starting transfers between devices, along(): return lax.ppermute(value, 'latent', pairs)  37.4 us
    pallas_call x15, Pallas kernels, local_kernel(): pl.pallas_call(run, out_shape=outs, in_specs=[SMEM] + [VMEM] * len(args)...  18.6 us
    ppermute x19, waiting for transfers between devices, flip(): return lax.ppermute(value, ('latent', 'dp'), pairs)  14.5 us
    ppermute x19, starting transfers between devices, flip(): return lax.ppermute(value, ('latent', 'dp'), pairs)  9.47 us
  transfers between devices with their start and end apart: 33, of which 12 were waited for; matrix products, arithmetic and copies ran while one was open for 0% of the time, Pallas kernels for 12%

profile of v9, /device:TPU:0, one launch (start us, length us, event | category | flops | bytes accessed | tf_op | source)
XLA Modules:
  0.0 149.8 jit_solution(3002849643693132471)
XLA Ops:
  0.7 1.3 copy-done.1
  2.0 0.7 copy-done.6
  2.7 0.6 shard_map.178.refs_6_
  3.8 5.8 %collective-permute-start.2 = (bf16[384,512]{1,0:T(8,128)(2,1)S(1)}, bf16[384,512]{1,0:T(8,128)(2,1)S(1)}, u32[]{:S(2)}, u32[]{:S(2)}) collective-permute-start(bf16[384,512]{1,0:T(8,128)(2,1)S(1)} %copy-done.5), channel_id=1, source_target_pairs={{0,8},{12,4},{1,9},{13,5},{2,10},{14,6},{3,11},{15,7},{16,24},{28,... | collective-permute-start | bytes 1179656 | tf_op jit(solution)/shard_map/ppermute | solution.py:432
  9.6 1.3 collective-permute-start.1
  10.9 4.6 %collective-permute-start = (bf16[384,512]{1,0:T(8,128)(2,1)S(1)}, bf16[384,512]{1,0:T(8,128)(2,1)S(1)}, u32[]{:S(2)}, u32[]{:S(2)}) collective-permute-start(bf16[384,512]{1,0:T(8,128)(2,1)S(1)} %copy-done.5), channel_id=1, source_target_pairs={{0,4},{4,8},{8,12},{1,5},{5,9},{9,13},{2,6},{6,10},{10,14},{3,7},{... | collective-permute-start | bytes 1179656 | tf_op jit(solution)/shard_map/ppermute | solution.py:432
  15.5 1.6 %collective-permute-start.6 = (bf16[528,512]{1,0:T(8,128)(2,1)S(1)}, bf16[528,512]{1,0:T(8,128)(2,1)S(1)}, u32[]{:S(2)}, u32[]{:S(2)}) collective-permute-start(bf16[528,512]{1,0:T(8,128)(2,1)S(1)} %shard_map.178.refs_6_), channel_id=1, source_target_pairs={{0,2},{1,3},{2,0},{3,1},{4,6},{5,7},{6,4},{7,5},{8,10},{9,11},{10,... | collective-permute-start | bytes 1622024 | tf_op jit(solution)/shard_map/ppermute | solution.py:436
  17.1 0.6 shard_map.179.refs_0_.refs_4_.refs_3_
  18.3 0.8 collective-permute-done.2.refs_3_
  19.1 1.3 collective-permute-start.4
  21.0 1.6 %collective-permute-done.1.refs_1_.refs_2_ = bf16[384,512]{1,0:T(8,128)(2,1)S(1)} collective-permute-done((bf16[384,512]{1,0:T(8,128)(2,1)S(1)}, bf16[384,512]{1,0:T(8,128)(2,1)S(1)}, u32[]{:S(2)}, u32[]{:S(2)}) %collective-permute-start.1) | collective-permute-done | bytes 393248 | tf_op jit(solution)/shard_map/ppermute | solution.py:432
  22.6 8.4 %collective-permute-start.8 = (bf16[256,512]{1,0:T(8,128)(2,1)S(1)}, bf16[256,512]{1,0:T(8,128)(2,1)S(1)}, u32[]{:S(2)}, u32[]{:S(2)}) collective-permute-start(bf16[256,512]{1,0:T(8,128)(2,1)S(1)} %get-tuple-element.62), channel_id=1, source_target_pairs={{0,4},{4,8},{1,5},{5,9},{2,6},{6,10},{3,7},{7,11},{16,20},{20,24},... | collective-permute-start | bytes 786440 | tf_op jit(solution)/shard_map/ppermute | solution.py:432
  31.0 0.7 collective-permute-start.10
  31.7 5.2 %collective-permute-start.11 = (bf16[256,512]{1,0:T(8,128)(2,1)S(1)}, bf16[256,512]{1,0:T(8,128)(2,1)S(1)}, u32[]{:S(2)}, u32[]{:S(2)}) collective-permute-start(bf16[256,512]{1,0:T(8,128)(2,1)S(1)} %get-tuple-element.66), channel_id=1, source_target_pairs={{0,8},{12,4},{1,9},{13,5},{2,10},{14,6},{3,11},{15,7},{16,24},{28,... | collective-permute-start | bytes 786440 | tf_op jit(solution)/shard_map/ppermute | solution.py:432
  37.6 1.3 collective-permute-start.3
  38.9 1.8 %collective-permute-done.9.refs_6_.refs_5_ = bf16[528,512]{1,0:T(8,128)(2,1)S(1)} collective-permute-done((bf16[528,512]{1,0:T(8,128)(2,1)S(1)}, bf16[528,512]{1,0:T(8,128)(2,1)S(1)}, u32[]{:S(2)}, u32[]{:S(2)}) %collective-permute-start.9) | collective-permute-done | bytes 540704 | tf_op jit(solution)/shard_map/ppermute | solution.py:436
  40.8 1.6 %collective-permute-done.11 = bf16[256,512]{1,0:T(8,128)(2,1)S(1)} collective-permute-done((bf16[256,512]{1,0:T(8,128)(2,1)S(1)}, bf16[256,512]{1,0:T(8,128)(2,1)S(1)}, u32[]{:S(2)}, u32[]{:S(2)}) %collective-permute-start.11) | collective-permute-done | bytes 262176 | tf_op jit(solution)/shard_map/ppermute | solution.py:432
  42.4 0.7 collective-permute-start.18
  43.2 6.1 %collective-permute-done.3.refs_4_ = bf16[384,512]{1,0:T(8,128)(2,1)S(1)} collective-permute-done((bf16[384,512]{1,0:T(8,128)(2,1)S(1)}, bf16[384,512]{1,0:T(8,128)(2,1)S(1)}, u32[]{:S(2)}, u32[]{:S(2)}) %collective-permute-start.3) | collective-permute-done | bytes 393248 | tf_op jit(solution)/shard_map/ppermute | solution.py:432
  49.4 1.8 %shard_map.181 = (bf16[384,512]{1,0:T(8,128)(2,1)S(1)}, bf16[384,512]{1,0:T(8,128)(2,1)S(1)}, bf16[384,2048]{1,0:T(8,128)(2,1)S(1)}, f32[1,512]{1,0:T(1,128)S(1)}) custom-call(s32[2]{0:T(128)S(1)} %pad_add_fusion.place, bf16[384,512]{1,0:T(8,128)(2,1)S(1)} %copy-done.5, bf16[384,512]{1,0:T(8,128)(2,1)S(1)} %collective-permute-done.refs_0_.refs_1_, ...), custom_call_target="tpu_custom_call" | custom-call | flops 1 | bytes 1 | tf_op jit(solution)/shard_map/pallas_call | solution.py:121
  51.1 2.0 %collective-permute-start.14 = (bf16[384,512]{1,0:T(8,128)(2,1)S(1)}, bf16[384,512]{1,0:T(8,128)(2,1)S(1)}, u32[]{:S(2)}, u32[]{:S(2)}) collective-permute-start(bf16[384,512]{1,0:T(8,128)(2,1)S(1)} %get-tuple-element.69.refs_0_.refs_2_.refs_4_), channel_id=1, source_target_pairs={{0,8},{12,4},{1,9},{13,5},{2,10},{14,6},{3,11},{15,7},{16,24},{28,... | collective-permute-start | bytes 1179656 | tf_op jit(solution)/shard_map/ppermute | solution.py:432
  53.1 0.7 collective-permute-start.13
  53.8 2.9 %collective-permute-start.12 = (bf16[384,512]{1,0:T(8,128)(2,1)S(1)}, bf16[384,512]{1,0:T(8,128)(2,1)S(1)}, u32[]{:S(2)}, u32[]{:S(2)}) collective-permute-start(bf16[384,512]{1,0:T(8,128)(2,1)S(1)} %get-tuple-element.69.refs_0_.refs_2_.refs_4_), channel_id=1, source_target_pairs={{0,4},{4,8},{1,5},{5,9},{2,6},{6,10},{3,7},{7,11},{16,20},{20,24},... | collective-permute-start | bytes 1179656 | tf_op jit(solution)/shard_map/ppermute | solution.py:432
  56.7 1.0 shard_map.182.refs_7_.refs_0_
  57.7 0.7 collective-permute-start.17
  58.5 4.1 %collective-permute-done.14.refs_3_ = bf16[384,512]{1,0:T(8,128)(2,1)S(1)} collective-permute-done((bf16[384,512]{1,0:T(8,128)(2,1)S(1)}, bf16[384,512]{1,0:T(8,128)(2,1)S(1)}, u32[]{:S(2)}, u32[]{:S(2)}) %collective-permute-start.14) | collective-permute-done | bytes 393248 | tf_op jit(solution)/shard_map/ppermute | solution.py:432
  62.5 8.0 %collective-permute-done.12.refs_1_ = bf16[384,512]{1,0:T(8,128)(2,1)S(1)} collective-permute-done((bf16[384,512]{1,0:T(8,128)(2,1)S(1)}, bf16[384,512]{1,0:T(8,128)(2,1)S(1)}, u32[]{:S(2)}, u32[]{:S(2)}) %collective-permute-start.12) | collective-permute-done | bytes 393248 | tf_op jit(solution)/shard_map/ppermute | solution.py:432
  70.6 0.7 collective-permute-start.19
  71.3 2.4 %shard_map.183.refs_0_ = bf16[384,1024]{1,0:T(8,128)(2,1)S(1)} custom-call(s32[2]{0:T(128)S(1)} %pad_add_fusion.place, bf16[384,512]{1,0:T(8,128)(2,1)S(1)} %get-tuple-element.69.refs_0_.refs_2_.refs_4_, bf16[384,512]{1,0:T(8,128)(2,1)S(1)} %collective-permute-done.12.refs_1_, bf16[384,512]{1,0:T(8,128)(2,1)S(1)} %collective-permute-done.13.refs_2_, ...), custom_call_target="tpu_custom_call" | custom-call | flops 1 | bytes 1 | tf_op jit(solution)/shard_map/pallas_call | solution.py:121
  73.7 1.3 collective-permute-start.22
  75.0 0.7 collective-permute-start.20
  75.7 1.3 collective-permute-start.21
  77.0 23.6 %collective-permute-done.22.refs_1_ = bf16[384,1024]{1,0:T(8,128)(2,1)S(1)} collective-permute-done((bf16[384,1024]{1,0:T(8,128)(2,1)S(1)}, bf16[384,1024]{1,0:T(8,128)(2,1)S(1)}, u32[]{:S(2)}, u32[]{:S(2)}) %collective-permute-start.22) | collective-permute-done | bytes 786464 | tf_op jit(solution)/shard_map/ppermute | solution.py:432
  100.6 1.8 %shard_map.184 = (f32[384,512]{1,0:T(8,128)S(1)}, bf16[384,1024]{1,0:T(8,128)(2,1)S(1)}, f32[264,512]{1,0:T(8,128)S(1)}, f32[256,512]{1,0:T(8,128)S(1)}, f32[256,512]{1,0:T(8,128)S(1)}, /*index=5*/f32[256,512]{1,0:T(8,128)S(1)}) custom-call(s32[2]{0:T(128)S(1)} %pad_add_fusion.place, bf16[384,1024]{1,0:T(8,128)(2,1)S(1)} %shard_map.183.refs_0_, ...), custom_call_target="tpu_custom_call" | custom-call | flops 1 | bytes 1 | tf_op jit(solution)/shard_map/pallas_call | solution.py:121
  102.5 1.9 %collective-permute-done.23.refs_2_ = f32[264,512]{1,0:T(8,128)S(1)} collective-permute-done((f32[264,512]{1,0:T(8,128)S(1)}, f32[264,512]{1,0:T(8,128)S(1)}, u32[]{:S(2)}, u32[]{:S(2)}) %collective-permute-start.23) | collective-permute-done | bytes 540704 | tf_op jit(solution)/shard_map/ppermute | solution.py:436
  104.4 0.7 shard_map.185
  105.7 14.9 %collective-permute-done.21.refs_1_ = bf16[384,1024]{1,0:T(8,128)(2,1)S(1)} collective-permute-done((bf16[384,1024]{1,0:T(8,128)(2,1)S(1)}, bf16[384,1024]{1,0:T(8,128)(2,1)S(1)}, u32[]{:S(2)}, u32[]{:S(2)}) %collective-permute-start.21) | collective-permute-done | bytes 786464 | tf_op jit(solution)/shard_map/ppermute | solution.py:432
  120.6 1.3 shard_map.186
  122.0 1.7 %shard_map.187 = (bf16[384,512]{1,0:T(8,128)(2,1)S(1)}, f32[1,512]{1,0:T(1,128)S(1)}, f32[1,512]{1,0:T(1,128)S(1)}, f32[264,512]{1,0:T(8,128)S(1)}, f32[256,512]{1,0:T(8,128)S(1)}) custom-call(s32[2]{0:T(128)S(1)} %pad_add_fusion.place, bf16[384,1024]{1,0:T(8,128)(2,1)S(1)} %get-tuple-element.76.refs_0_.refs_3_, f32[384,512]{1,0:T(8,128)S(1)} %get-tuple-element.78.refs_1_, ...), custom_call_target="tpu_custom_call" | custom-call | flops 10000000000 | bytes 1 | tf_op jit(solution)/shard_map/pallas_call | solution.py:121
  124.8 1.2 shard_map.188
  126.6 2.5 %shard_map.189 = (bf16[384,512]{1,0:T(8,128)(2,1)}, f32[512,512]{1,0:T(8,128)S(1)}, f32[512,512]{1,0:T(8,128)S(1)}, f32[512,512]{1,0:T(8,128)S(1)}, f32[256,512]{1,0:T(8,128)S(1)}, /*index=5*/f32[256,512]{1,0:T(8,128)S(1)}) custom-call(s32[2]{0:T(128)S(1)} %pad_add_fusion.place, bf16[2048,384]{1,0:T(8,128)(2,1)S(1)} %shard_map.182.refs_7_.refs_0_, ...), custom_call_target="tpu_custom_call" | custom-call | flops 1 | bytes 1 | tf_op jit(solution)/shard_map/pallas_call | solution.py:121
  129.7 0.8 shard_map.190
  130.6 1.6 %collective-permute-start.29 = (f16[528,512]{1,0:T(8,128)(2,1)S(1)}, f16[528,512]{1,0:T(8,128)(2,1)S(1)}, u32[]{:S(2)}, u32[]{:S(2)}) collective-permute-start(f16[528,512]{1,0:T(8,128)(2,1)S(1)} %convert_element_type.26), channel_id=1, source_target_pairs={{0,2},{1,3},{2,0},{3,1},{4,6},{5,7},{6,4},{7,5},{8,10},{9,11},{10,... | collective-permute-start | bytes 1622024 | tf_op jit(solution)/shard_map/ppermute | solution.py:436
  132.3 3.2 %collective-permute-done.32 = f16[272,512]{1,0:T(8,128)(2,1)S(1)} collective-permute-done((f16[272,512]{1,0:T(8,128)(2,1)S(1)}, f16[272,512]{1,0:T(8,128)(2,1)S(1)}, u32[]{:S(2)}, u32[]{:S(2)}) %collective-permute-start.32) | collective-permute-done | bytes 278560 | tf_op jit(solution)/shard_map/ppermute | solution.py:436
  135.8 2.9 %shard_map.192 = (f32[512,512]{1,0:T(8,128)}, f32[512,512]{1,0:T(8,128)}, f32[512,512]{1,0:T(8,128)}) custom-call(s32[2]{0:T(128)S(1)} %pad_add_fusion.place, f32[512,512]{1,0:T(8,128)S(1)} %copy-done, f32[512,512]{1,0:T(8,128)S(1)} %copy-done.3, f32[512,512]{1,0:T(8,128)S(1)} %copy-done.4, f32[256,512]{1,0:T(8,128)S(1)} %multiply_add_fusion.3.near, ...), custom_call_target="tpu_custom_call" | custom-call | flops 1 | bytes 1 | tf_op jit(solution)/shard_map/pallas_call | solution.py:628
  138.8 7.5 %collective-permute-done.29 = f16[528,512]{1,0:T(8,128)(2,1)S(1)} collective-permute-done((f16[528,512]{1,0:T(8,128)(2,1)S(1)}, f16[528,512]{1,0:T(8,128)(2,1)S(1)}, u32[]{:S(2)}, u32[]{:S(2)}) %collective-permute-start.29) | collective-permute-done | bytes 540704 | tf_op jit(solution)/shard_map/ppermute | solution.py:436
  146.3 1.1 shard_map.191
  147.5 2.3 %divide_subtract_fusion = (f32[512,512]{1,0:T(8,128)}, f32[512,512]{1,0:T(8,128)}, f32[512,512]{1,0:T(8,128)}) fusion(f32[512,512]{1,0:T(8,128)S(1)} %copy-done.2, f32[512]{0:T(512)S(1)} %bitcast.15, f16[528,512]{1,0:T(8,128)(2,1)S(1)} %collective-permute-done.29, f32[512,512]{1,0:T(8,128)S(1)} %get-tuple-element.93, ...), kind=kLoop, calls=%fused_computation.2 | loop fusion | flops 4194304 | bytes 8914944 | tf_op jit(solution)/shard_map/sub | solution.py:28
  (73 shorter events, 6.2 us)
Async XLA Ops:
  0.6 16.4 %copy-start = (f32[512,512]{1,0:T(8,128)S(1)}, f32[512,512]{1,0:T(8,128)}, u32[]{:S(2)}) copy-start(f32[512,512]{1,0:T(8,128)} %param.20) | copy-start | bytes 3145732
  0.7 1.3 copy-start.1
  2.0 0.7 copy-start.6
  2.7 1.1 copy-start.5
  3.3 13.8 %collective-permute-start.5 = (bf16[528,512]{1,0:T(8,128)(2,1)S(1)}, bf16[528,512]{1,0:T(8,128)(2,1)S(1)}, u32[]{:S(2)}, u32[]{:S(2)}) collective-permute-start(bf16[528,512]{1,0:T(8,128)(2,1)S(1)} %shard_map.178.refs_6_), channel_id=1, source_target_pairs={{0,1},{1,0},{2,3},{3,2},{4,5},{5,4},{6,7},{7,6},{8,9},{9,8},{10,11... | collective-permute-start | bytes 1622024 | tf_op jit(solution)/shard_map/ppermute | solution.py:436
  3.8 15.3 %collective-permute-start.2 = (bf16[384,512]{1,0:T(8,128)(2,1)S(1)}, bf16[384,512]{1,0:T(8,128)(2,1)S(1)}, u32[]{:S(2)}, u32[]{:S(2)}) collective-permute-start(bf16[384,512]{1,0:T(8,128)(2,1)S(1)} %copy-done.5), channel_id=1, source_target_pairs={{0,8},{12,4},{1,9},{13,5},{2,10},{14,6},{3,11},{15,7},{16,24},{28,... | collective-permute-start | bytes 1179656 | tf_op jit(solution)/shard_map/ppermute | solution.py:432
  9.6 13.0 %collective-permute-start.1 = (bf16[384,512]{1,0:T(8,128)(2,1)S(1)}, bf16[384,512]{1,0:T(8,128)(2,1)S(1)}, u32[]{:S(2)}, u32[]{:S(2)}) collective-permute-start(bf16[384,512]{1,0:T(8,128)(2,1)S(1)} %copy-done.5), channel_id=1, source_target_pairs={{4,0},{8,4},{12,8},{5,1},{9,5},{13,9},{6,2},{10,6},{14,10},{7,3},{... | collective-permute-start | bytes 1179656 | tf_op jit(solution)/shard_map/ppermute | solution.py:432
  10.9 20.1 %collective-permute-start = (bf16[384,512]{1,0:T(8,128)(2,1)S(1)}, bf16[384,512]{1,0:T(8,128)(2,1)S(1)}, u32[]{:S(2)}, u32[]{:S(2)}) collective-permute-start(bf16[384,512]{1,0:T(8,128)(2,1)S(1)} %copy-done.5), channel_id=1, source_target_pairs={{0,4},{4,8},{8,12},{1,5},{5,9},{9,13},{2,6},{6,10},{10,14},{3,7},{... | collective-permute-start | bytes 1179656 | tf_op jit(solution)/shard_map/ppermute | solution.py:432
  15.5 16.2 %collective-permute-start.6 = (bf16[528,512]{1,0:T(8,128)(2,1)S(1)}, bf16[528,512]{1,0:T(8,128)(2,1)S(1)}, u32[]{:S(2)}, u32[]{:S(2)}) collective-permute-start(bf16[528,512]{1,0:T(8,128)(2,1)S(1)} %shard_map.178.refs_6_), channel_id=1, source_target_pairs={{0,2},{1,3},{2,0},{3,1},{4,6},{5,7},{6,4},{7,5},{8,10},{9,11},{10,... | collective-permute-start | bytes 1622024 | tf_op jit(solution)/shard_map/ppermute | solution.py:436
  17.7 23.0 %collective-permute-start.9 = (bf16[528,512]{1,0:T(8,128)(2,1)S(1)}, bf16[528,512]{1,0:T(8,128)(2,1)S(1)}, u32[]{:S(2)}, u32[]{:S(2)}) collective-permute-start(bf16[528,512]{1,0:T(8,128)(2,1)S(1)} %shard_map.179.refs_0_.refs_4_.refs_3_), channel_id=1, source_target_pairs={{0,2},{1,3},{2,0},{3,1},{4,6},{5,7},{6,4},{7,5},{8,10},{9,11},{10,... | collective-permute-start | bytes 1622024 | tf_op jit(solution)/shard_map/ppermute | solution.py:436
  19.1 18.4 %collective-permute-start.4 = (bf16[384,512]{1,0:T(8,128)(2,1)S(1)}, bf16[384,512]{1,0:T(8,128)(2,1)S(1)}, u32[]{:S(2)}, u32[]{:S(2)}) collective-permute-start(bf16[384,512]{1,0:T(8,128)(2,1)S(1)} %collective-permute-done.2.refs_3_), channel_id=1, source_target_pairs={{4,0},{8,12},{5,1},{9,13},{6,2},{10,14},{7,3},{11,15},{20,16},{24,... | collective-permute-start | bytes 1179656 | tf_op jit(solution)/shard_map/ppermute | solution.py:432
  22.6 16.2 %collective-permute-start.8 = (bf16[256,512]{1,0:T(8,128)(2,1)S(1)}, bf16[256,512]{1,0:T(8,128)(2,1)S(1)}, u32[]{:S(2)}, u32[]{:S(2)}) collective-permute-start(bf16[256,512]{1,0:T(8,128)(2,1)S(1)} %get-tuple-element.62), channel_id=1, source_target_pairs={{0,4},{4,8},{1,5},{5,9},{2,6},{6,10},{3,7},{7,11},{16,20},{20,24},... | collective-permute-start | bytes 786440 | tf_op jit(solution)/shard_map/ppermute | solution.py:432
  31.0 9.7 %collective-permute-start.10 = (bf16[256,512]{1,0:T(8,128)(2,1)S(1)}, bf16[256,512]{1,0:T(8,128)(2,1)S(1)}, u32[]{:S(2)}, u32[]{:S(2)}) collective-permute-start(bf16[256,512]{1,0:T(8,128)(2,1)S(1)} %get-tuple-element.64), channel_id=1, source_target_pairs={{8,4},{12,8},{9,5},{13,9},{10,6},{14,10},{11,7},{15,11},{24,20},{2... | collective-permute-start | bytes 786440 | tf_op jit(solution)/shard_map/ppermute | solution.py:432
  31.7 10.6 %collective-permute-start.11 = (bf16[256,512]{1,0:T(8,128)(2,1)S(1)}, bf16[256,512]{1,0:T(8,128)(2,1)S(1)}, u32[]{:S(2)}, u32[]{:S(2)}) collective-permute-start(bf16[256,512]{1,0:T(8,128)(2,1)S(1)} %get-tuple-element.66), channel_id=1, source_target_pairs={{0,8},{12,4},{1,9},{13,5},{2,10},{14,6},{3,11},{15,7},{16,24},{28,... | collective-permute-start | bytes 786440 | tf_op jit(solution)/shard_map/ppermute | solution.py:432
  37.6 11.8 %collective-permute-start.3 = (bf16[384,512]{1,0:T(8,128)(2,1)S(1)}, bf16[384,512]{1,0:T(8,128)(2,1)S(1)}, u32[]{:S(2)}, u32[]{:S(2)}) collective-permute-start(bf16[384,512]{1,0:T(8,128)(2,1)S(1)} %shard_map.177), channel_id=1, source_target_pairs={{4,0},{8,12},{5,1},{9,13},{6,2},{10,14},{7,3},{11,15},{20,16},{24,... | collective-permute-start | bytes 1179656 | tf_op jit(solution)/shard_map/ppermute | solution.py:432
  38.9 14.9 %collective-permute-start.15 = (bf16[528,512]{1,0:T(8,128)(2,1)S(1)}, bf16[528,512]{1,0:T(8,128)(2,1)S(1)}, u32[]{:S(2)}, u32[]{:S(2)}) collective-permute-start(bf16[528,512]{1,0:T(8,128)(2,1)S(1)} %shard_map.179.refs_0_.refs_4_.refs_3_), channel_id=1, source_target_pairs={{0,1},{1,0},{2,3},{3,2},{4,5},{5,4},{6,7},{7,6},{8,9},{9,8},{10,11... | collective-permute-start | bytes 1622024 | tf_op jit(solution)/shard_map/ppermute | solution.py:436
  40.7 8.7 %collective-permute-start.7 = (bf16[528,512]{1,0:T(8,128)(2,1)S(1)}, bf16[528,512]{1,0:T(8,128)(2,1)S(1)}, u32[]{:S(2)}, u32[]{:S(2)}) collective-permute-start(bf16[528,512]{1,0:T(8,128)(2,1)S(1)} %collective-permute-done.6.refs_8_), channel_id=1, source_target_pairs={{0,1},{1,0},{2,3},{3,2},{4,5},{5,4},{6,7},{7,6},{8,9},{9,8},{10,11... | collective-permute-start | bytes 1622024 | tf_op jit(solution)/shard_map/ppermute | solution.py:436
  42.4 28.1 %collective-permute-start.18 = (bf16[768,512]{1,0:T(8,128)(2,1)S(1)}, bf16[768,512]{1,0:T(8,128)(2,1)S(1)}, u32[]{:S(2)}, u32[]{:S(2)}) collective-permute-start(bf16[768,512]{1,0:T(8,128)(2,1)S(1)} %constant_dynamic-update-slice_fusion.refs_10_.refs_8_), channel_id=1, source_target_pairs={{4,6},{5,7},{6,4},{7,5},{8,10},{9,11},{10,8},{11,9},{20,22},{21,23... | collective-permute-start | bytes 2359304 | tf_op jit(solution)/shard_map/ppermute | solution.py:436
  43.1 14.6 %collective-permute-start.16 = (bf16[528,512]{1,0:T(8,128)(2,1)S(1)}, bf16[528,512]{1,0:T(8,128)(2,1)S(1)}, u32[]{:S(2)}, u32[]{:S(2)}) collective-permute-start(bf16[528,512]{1,0:T(8,128)(2,1)S(1)} %collective-permute-done.9.refs_6_.refs_5_), channel_id=1, source_target_pairs={{0,1},{1,0},{2,3},{3,2},{4,5},{5,4},{6,7},{7,6},{8,9},{9,8},{10,11... | collective-permute-start | bytes 1622024 | tf_op jit(solution)/shard_map/ppermute | solution.py:436
  51.1 11.4 %collective-permute-start.14 = (bf16[384,512]{1,0:T(8,128)(2,1)S(1)}, bf16[384,512]{1,0:T(8,128)(2,1)S(1)}, u32[]{:S(2)}, u32[]{:S(2)}) collective-permute-start(bf16[384,512]{1,0:T(8,128)(2,1)S(1)} %get-tuple-element.69.refs_0_.refs_2_.refs_4_), channel_id=1, source_target_pairs={{0,8},{12,4},{1,9},{13,5},{2,10},{14,6},{3,11},{15,7},{16,24},{28,... | collective-permute-start | bytes 1179656 | tf_op jit(solution)/shard_map/ppermute | solution.py:432
  53.1 9.4 %collective-permute-start.13 = (bf16[384,512]{1,0:T(8,128)(2,1)S(1)}, bf16[384,512]{1,0:T(8,128)(2,1)S(1)}, u32[]{:S(2)}, u32[]{:S(2)}) collective-permute-start(bf16[384,512]{1,0:T(8,128)(2,1)S(1)} %get-tuple-element.69.refs_0_.refs_2_.refs_4_), channel_id=1, source_target_pairs={{8,4},{12,8},{9,5},{13,9},{10,6},{14,10},{11,7},{15,11},{24,20},{2... | collective-permute-start | bytes 1179656 | tf_op jit(solution)/shard_map/ppermute | solution.py:432
  53.8 16.7 %collective-permute-start.12 = (bf16[384,512]{1,0:T(8,128)(2,1)S(1)}, bf16[384,512]{1,0:T(8,128)(2,1)S(1)}, u32[]{:S(2)}, u32[]{:S(2)}) collective-permute-start(bf16[384,512]{1,0:T(8,128)(2,1)S(1)} %get-tuple-element.69.refs_0_.refs_2_.refs_4_), channel_id=1, source_target_pairs={{0,4},{4,8},{1,5},{5,9},{2,6},{6,10},{3,7},{7,11},{16,20},{20,24},... | collective-permute-start | bytes 1179656 | tf_op jit(solution)/shard_map/ppermute | solution.py:432
  57.7 13.5 %collective-permute-start.17 = (bf16[768,512]{1,0:T(8,128)(2,1)S(1)}, bf16[768,512]{1,0:T(8,128)(2,1)S(1)}, u32[]{:S(2)}, u32[]{:S(2)}) collective-permute-start(bf16[768,512]{1,0:T(8,128)(2,1)S(1)} %constant_dynamic-update-slice_fusion.refs_10_.refs_8_), channel_id=1, source_target_pairs={{4,5},{5,4},{6,7},{7,6},{8,9},{9,8},{10,11},{11,10},{20,21},{21,20... | collective-permute-start | bytes 2359304 | tf_op jit(solution)/shard_map/ppermute | solution.py:436
  70.6 0.7 collective-permute-start.19
  73.7 26.9 %collective-permute-start.22 = (bf16[384,1024]{1,0:T(8,128)(2,1)S(1)}, bf16[384,1024]{1,0:T(8,128)(2,1)S(1)}, u32[]{:S(2)}, u32[]{:S(2)}) collective-permute-start(bf16[384,1024]{1,0:T(8,128)(2,1)S(1)} %shard_map.183.refs_0_), channel_id=1, source_target_pairs={{4,0},{8,12},{5,1},{9,13},{6,2},{10,14},{7,3},{11,15},{20,16},{24,... | collective-permute-start | bytes 2359304 | tf_op jit(solution)/shard_map/ppermute | solution.py:432
  75.0 25.6 %collective-permute-start.20 = (bf16[384,1024]{1,0:T(8,128)(2,1)S(1)}, bf16[384,1024]{1,0:T(8,128)(2,1)S(1)}, u32[]{:S(2)}, u32[]{:S(2)}) collective-permute-start(bf16[384,1024]{1,0:T(8,128)(2,1)S(1)} %shard_map.183.refs_0_), channel_id=1, source_target_pairs={{4,8},{8,4},{5,9},{9,5},{6,10},{10,6},{7,11},{11,7},{20,24},{24,20... | collective-permute-start | bytes 2359304 | tf_op jit(solution)/shard_map/ppermute | solution.py:432
  75.7 44.9 %collective-permute-start.21 = (bf16[384,1024]{1,0:T(8,128)(2,1)S(1)}, bf16[384,1024]{1,0:T(8,128)(2,1)S(1)}, u32[]{:S(2)}, u32[]{:S(2)}) collective-permute-start(bf16[384,1024]{1,0:T(8,128)(2,1)S(1)} %shard_map.183.refs_0_), channel_id=1, source_target_pairs={{8,0},{4,12},{9,1},{5,13},{10,2},{6,14},{11,3},{7,15},{24,16},{20,... | collective-permute-start | bytes 2359304 | tf_op jit(solution)/shard_map/ppermute | solution.py:432
  102.4 2.0 %collective-permute-start.23 = (f32[264,512]{1,0:T(8,128)S(1)}, f32[264,512]{1,0:T(8,128)S(1)}, u32[]{:S(2)}, u32[]{:S(2)}) collective-permute-start(f32[264,512]{1,0:T(8,128)S(1)} %get-tuple-element.74), channel_id=1, source_target_pairs={{0,1},{1,0},{2,3},{3,2},{4,5},{5,4},{6,7},{7,6},{8,9},{9,8},{10,11... | collective-permute-start | bytes 1622024 | tf_op jit(solution)/shard_map/ppermute | solution.py:436
  105.1 16.9 %collective-permute-start.24 = (f16[272,512]{1,0:T(8,128)(2,1)S(1)}, f16[272,512]{1,0:T(8,128)(2,1)S(1)}, u32[]{:S(2)}, u32[]{:S(2)}) collective-permute-start(f16[272,512]{1,0:T(8,128)(2,1)S(1)} %convert_element_type.25), channel_id=1, source_target_pairs={{0,2},{1,3},{2,0},{3,1},{4,6},{5,7},{6,4},{7,5},{8,10},{9,11},{10,... | collective-permute-start | bytes 835592 | tf_op jit(solution)/shard_map/ppermute | solution.py:436
  121.9 2.9 %collective-permute-start.25 = (f32[256,512]{1,0:T(8,128)S(1)}, f32[256,512]{1,0:T(8,128)S(1)}, u32[]{:S(2)}, u32[]{:S(2)}) collective-permute-start(f32[256,512]{1,0:T(8,128)S(1)} %get-tuple-element.83), channel_id=1, source_target_pairs={{0,1},{1,0},{2,3},{3,2},{4,5},{5,4},{6,7},{7,6},{8,9},{9,8},{10,11... | collective-permute-start | bytes 1572872 | tf_op jit(solution)/shard_map/ppermute | solution.py:436
  123.7 6.0 %collective-permute-start.26 = (f32[264,512]{1,0:T(8,128)S(1)}, f32[264,512]{1,0:T(8,128)S(1)}, u32[]{:S(2)}, u32[]{:S(2)}) collective-permute-start(f32[264,512]{1,0:T(8,128)S(1)} %get-tuple-element.88), channel_id=1, source_target_pairs={{0,1},{1,0},{2,3},{3,2},{4,5},{5,4},{6,7},{7,6},{8,9},{9,8},{10,11... | collective-permute-start | bytes 1622024 | tf_op jit(solution)/shard_map/ppermute | solution.py:436
  124.3 4.9 %collective-permute-start.27 = (f32[256,512]{1,0:T(8,128)S(1)}, f32[256,512]{1,0:T(8,128)S(1)}, u32[]{:S(2)}, u32[]{:S(2)}) collective-permute-start(f32[256,512]{1,0:T(8,128)S(1)} %get-tuple-element.89), channel_id=1, source_target_pairs={{0,1},{1,0},{2,3},{3,2},{4,5},{5,4},{6,7},{7,6},{8,9},{9,8},{10,11... | collective-permute-start | bytes 1572872 | tf_op jit(solution)/shard_map/ppermute | solution.py:436
  124.3 7.9 %collective-permute-start.30 = (f32[256,512]{1,0:T(8,128)S(1)}, f32[256,512]{1,0:T(8,128)S(1)}, u32[]{:S(2)}, u32[]{:S(2)}) collective-permute-start(f32[256,512]{1,0:T(8,128)S(1)} %get-tuple-element.102), channel_id=1, source_target_pairs={{0,1},{1,0},{2,3},{3,2},{4,5},{5,4},{6,7},{7,6},{8,9},{9,8},{10,11... | collective-permute-start | bytes 1572872 | tf_op jit(solution)/shard_map/ppermute | solution.py:436
  126.0 9.6 %collective-permute-start.32 = (f16[272,512]{1,0:T(8,128)(2,1)S(1)}, f16[272,512]{1,0:T(8,128)(2,1)S(1)}, u32[]{:S(2)}, u32[]{:S(2)}) collective-permute-start(f16[272,512]{1,0:T(8,128)(2,1)S(1)} %convert_element_type.31), channel_id=1, source_target_pairs={{0,2},{1,3},{2,0},{3,1},{4,6},{5,7},{6,4},{7,5},{8,10},{9,11},{10,... | collective-permute-start | bytes 835592 | tf_op jit(solution)/shard_map/ppermute | solution.py:436
  129.1 6.5 %collective-permute-start.31 = (f32[256,512]{1,0:T(8,128)S(1)}, f32[256,512]{1,0:T(8,128)S(1)}, u32[]{:S(2)}, u32[]{:S(2)}) collective-permute-start(f32[256,512]{1,0:T(8,128)S(1)} %get-tuple-element.104), channel_id=1, source_target_pairs={{0,1},{1,0},{2,3},{3,2},{4,5},{5,4},{6,7},{7,6},{8,9},{9,8},{10,11... | collective-permute-start | bytes 1572872 | tf_op jit(solution)/shard_map/ppermute | solution.py:436
  129.1 18.3 %collective-permute-start.28 = (f32[512,512]{1,0:T(8,128)S(1)}, f32[512,512]{1,0:T(8,128)S(1)}, u32[]{:S(2)}, u32[]{:S(2)}) collective-permute-start(f32[512,512]{1,0:T(8,128)S(1)} %get-tuple-element.94), channel_id=1, source_target_pairs={{0,1},{1,0},{2,3},{3,2},{4,5},{5,4},{6,7},{7,6},{8,9},{9,8},{10,11... | collective-permute-start | bytes 3145736 | tf_op jit(solution)/shard_map/ppermute | solution.py:436
  130.6 15.7 %collective-permute-start.29 = (f16[528,512]{1,0:T(8,128)(2,1)S(1)}, f16[528,512]{1,0:T(8,128)(2,1)S(1)}, u32[]{:S(2)}, u32[]{:S(2)}) collective-permute-start(f16[528,512]{1,0:T(8,128)(2,1)S(1)} %convert_element_type.26), channel_id=1, source_target_pairs={{0,2},{1,3},{2,0},{3,1},{4,6},{5,7},{6,4},{7,5},{8,10},{9,11},{10,... | collective-permute-start | bytes 1622024 | tf_op jit(solution)/shard_map/ppermute | solution.py:436
  132.2 3.6 %copy-start.3 = (f32[512,512]{1,0:T(8,128)S(1)}, f32[512,512]{1,0:T(8,128)}, u32[]{:S(2)}) copy-start(f32[512,512]{1,0:T(8,128)} %moment) | copy-start | bytes 3145732
  132.2 3.6 %copy-start.4 = (f32[512,512]{1,0:T(8,128)S(1)}, f32[512,512]{1,0:T(8,128)}, u32[]{:S(2)}) copy-start(f32[512,512]{1,0:T(8,128)} %square) | copy-start | bytes 3145732
  135.8 10.6 %copy-start.7 = (f32[128]{0:T(128)S(1)}, f32[128]{0:T(128)}, u32[]{:S(2)}) copy-start(f32[128]{0:T(128)} %param.12) | copy-start | bytes 1540
  135.8 10.6 %copy-start.8 = (f32[128]{0:T(128)S(1)}, f32[128]{0:T(128)}, u32[]{:S(2)}) copy-start(f32[128]{0:T(128)} %param.16) | copy-start | bytes 1540
  135.8 10.5 %copy-start.9 = (f32[128]{0:T(128)S(1)}, f32[128]{0:T(128)}, u32[]{:S(2)}) copy-start(f32[128]{0:T(128)} %param.17) | copy-start | bytes 1540
  135.8 11.6 %copy-start.2 = (f32[512,512]{1,0:T(8,128)S(1)}, f32[512,512]{1,0:T(8,128)}, u32[]{:S(2)}) copy-start(f32[512,512]{1,0:T(8,128)} %refs_0_.3) | copy-start | bytes 3145732
  135.8 11.6 %copy-start.10 = (f32[512,512]{1,0:T(8,128)S(1)}, f32[512,512]{1,0:T(8,128)}, u32[]{:S(2)}) copy-start(f32[512,512]{1,0:T(8,128)} %param.14) | copy-start | bytes 3145732
  135.8 11.6 %copy-start.11 = (f32[512,512]{1,0:T(8,128)S(1)}, f32[512,512]{1,0:T(8,128)}, u32[]{:S(2)}) copy-start(f32[512,512]{1,0:T(8,128)} %param.15) | copy-start | bytes 3145732

commit v10 on v9

--- a/solution.py
+++ b/solution.py
@@ -233,20 +233,34 @@
         out[...] = dec[pl.ds(pl.multiple_of(jnp.where(second, half, 0), half), half), :]
 
 
+def split_body(place, rows, first, second):
+    edge = first.shape[0]
+    first[...] = rows[:edge]
+    second[...] = rows[edge:]
+
+
 def turn_body(place, full, turned):
     turned[...] = full[...].T
 
 
 def error_body(
-    place, own, low, high, across, dec0, dec1, dec2, dec3, row0, row1, row2, row3, inputs, error
+    place, own, low, high, across, dec0, dec1, dec2, dec3, row0, row1, row2, *refs
 ):
+    first, second, inputs, error = refs
     z, i = place[0], place[1]
     half = row0.shape[0] // 3
+    edge = first.shape[0]
     shift = pl.multiple_of(jnp.where(z >= 2, half, 0), half)
     for t in range(4):
-        dec, row = (dec0, dec1, dec2, dec3)[t], (row0, row1, row2, row3)[t]
+        dec = (dec0, dec1, dec2, dec3)[t]
         lefts = (own, low, high, across)
-        rights = [dec[pl.ds(shift, half), :]] + [row[m * half : (m + 1) * half, :] for m in range(3)]
+        if t < 3:
+            row = (row0, row1, row2)[t]
+            rights = [row[m * half : (m + 1) * half, :] for m in range(3)]
+        else:
+            middle = jnp.concatenate([first[half:], second[: edge - half]], axis=0)
+            rights = [first[:half], middle, second[edge - half :]]
+        rights = [dec[pl.ds(shift, half), :]] + rights
         total = jnp.zeros((own.shape[0], half), F32)
         for left, right in zip(lefts, rights):
             total += lax.dot_general(
@@ -490,7 +504,7 @@
         relay1,
         relay2,
         *enc,
-        after=(rows_own,),
+        after=(rows_own, dec[1], dec[3]),
         scratch=[pltpu.VMEM((1, latents), F32)],
     )
     codes_low = along(codes, [(0, 1), (1, 2)])
@@ -501,9 +515,14 @@
     )
     rows_chip = flip(rows_own, 2, (1, 2))
     rows_core = flip(behind(rows_own, turned), 1, (1, 2))
-    rows_both = flip(
-        behind(rows_chip, codes_low, codes_high, codes_across, dec[1], dec[3]), 1, (1, 2)
-    )
+    halves = local_kernel(
+        split_body,
+        [shape((3 * half // 2, latents), BF16)] * 2,
+        place,
+        rows_chip,
+        after=(codes_across,),
+    )
+    rows_both = [flip(piece, 1, (1, 2)) for piece in halves]
 
     (own_error,) = local_kernel(
         error_body,
@@ -517,7 +536,7 @@
         rows_own,
         rows_core,
         rows_chip,
-        rows_both,
+        *rows_both,
         inputs,
     )
     swapped = along(own_error, [(1, 2), (2, 1)])

time: 150 us -> 147 us (0.980)
  waiting for transfers between devices: 75.2 us -> 67.4 us
  starting transfers between devices: 46.8 us -> 50.3 us
    ppermute x14, waiting for transfers between devices: 60.8 us -> 52.9 us  [along(): return lax.ppermute(value, 'latent', pairs)]
    ppermute x19 -> x20, starting transfers between devices: 9.47 us -> 11.5 us  [flip(): return lax.ppermute(value, ('latent', 'dp'), pairs)]
    pallas_call x15 -> x16, Pallas kernels: 18.6 us -> 19.2 us  [local_kernel(): pl.pallas_call(run, out_shape=outs, in_specs=[SMEM] + [VMEM] * len(args)...]
    ppermute x19 -> x20, waiting for transfers between devices: 14.5 us -> 14.4 us  [flip(): return lax.ppermute(value, ('latent', 'dp'), pairs)]
  transfers between devices with their start and end apart: 33 -> 34, of which waited for: 12 -> 12; matrix products, arithmetic and copies ran while one was open for 0% -> 0% of each run, Pallas kernels for 12% -> 13%
where the time goes in v10:
time: 147 us; the launch traced here: 146 us
  waiting for transfers between devices  67.4 us (46%)
  starting transfers between devices  50.3 us (34%)
  Pallas kernels  22.2 us (15%)
  other arithmetic  2.91 us (2%)
  local copies, waits for them, and re-layouts  2.06 us (1%)
    ppermute x14, waiting for transfers between devices, along(): return lax.ppermute(value, 'latent', pairs)  52.9 us
    ppermute x14, starting transfers between devices, along(): return lax.ppermute(value, 'latent', pairs)  38.7 us
    pallas_call x16, Pallas kernels, local_kernel(): pl.pallas_call(run, out_shape=outs, in_specs=[SMEM] + [VMEM] * len(args)...  19.2 us
    ppermute x20, waiting for transfers between devices, flip(): return lax.ppermute(value, ('latent', 'dp'), pairs)  14.4 us
    ppermute x20, starting transfers between devices, flip(): return lax.ppermute(value, ('latent', 'dp'), pairs)  11.5 us
  transfers between devices with their start and end apart: 34, of which 12 were waited for; matrix products, arithmetic and copies ran while one was open for 0% of the time, Pallas kernels for 13%

profile of v10, /device:TPU:0, one launch (start us, length us, event | category | flops | bytes accessed | tf_op | source)
XLA Modules:
  0.0 146.0 jit_solution(16193892595895290082)
XLA Ops:
  0.7 1.3 copy-done.1
  2.0 0.7 copy-done.6
  3.8 5.8 %collective-permute-start.2 = (bf16[384,512]{1,0:T(8,128)(2,1)S(1)}, bf16[384,512]{1,0:T(8,128)(2,1)S(1)}, u32[]{:S(2)}, u32[]{:S(2)}) collective-permute-start(bf16[384,512]{1,0:T(8,128)(2,1)S(1)} %copy-done.5), channel_id=1, source_target_pairs={{0,8},{12,4},{1,9},{13,5},{2,10},{14,6},{3,11},{15,7},{16,24},{28,... | collective-permute-start | bytes 1179656 | tf_op jit(solution)/shard_map/ppermute | solution.py:446
  9.6 1.3 collective-permute-start.1
  10.9 4.6 %collective-permute-start = (bf16[384,512]{1,0:T(8,128)(2,1)S(1)}, bf16[384,512]{1,0:T(8,128)(2,1)S(1)}, u32[]{:S(2)}, u32[]{:S(2)}) collective-permute-start(bf16[384,512]{1,0:T(8,128)(2,1)S(1)} %copy-done.5), channel_id=1, source_target_pairs={{0,4},{4,8},{8,12},{1,5},{5,9},{9,13},{2,6},{6,10},{10,14},{3,7},{... | collective-permute-start | bytes 1179656 | tf_op jit(solution)/shard_map/ppermute | solution.py:446
  15.5 1.6 %collective-permute-start.6 = (bf16[528,512]{1,0:T(8,128)(2,1)S(1)}, bf16[528,512]{1,0:T(8,128)(2,1)S(1)}, u32[]{:S(2)}, u32[]{:S(2)}) collective-permute-start(bf16[528,512]{1,0:T(8,128)(2,1)S(1)} %shard_map.178.refs_6_), channel_id=1, source_target_pairs={{0,2},{1,3},{2,0},{3,1},{4,6},{5,7},{6,4},{7,5},{8,10},{9,11},{10,... | collective-permute-start | bytes 1622024 | tf_op jit(solution)/shard_map/ppermute | solution.py:450
  18.3 0.8 collective-permute-done.2.refs_3_
  19.1 1.3 collective-permute-start.4
  21.0 1.6 %collective-permute-done.1.refs_1_.refs_2_ = bf16[384,512]{1,0:T(8,128)(2,1)S(1)} collective-permute-done((bf16[384,512]{1,0:T(8,128)(2,1)S(1)}, bf16[384,512]{1,0:T(8,128)(2,1)S(1)}, u32[]{:S(2)}, u32[]{:S(2)}) %collective-permute-start.1) | collective-permute-done | bytes 393248 | tf_op jit(solution)/shard_map/ppermute | solution.py:446
  22.6 8.4 %collective-permute-start.8 = (bf16[256,512]{1,0:T(8,128)(2,1)S(1)}, bf16[256,512]{1,0:T(8,128)(2,1)S(1)}, u32[]{:S(2)}, u32[]{:S(2)}) collective-permute-start(bf16[256,512]{1,0:T(8,128)(2,1)S(1)} %get-tuple-element.63), channel_id=1, source_target_pairs={{0,4},{4,8},{1,5},{5,9},{2,6},{6,10},{3,7},{7,11},{16,20},{20,24},... | collective-permute-start | bytes 786440 | tf_op jit(solution)/shard_map/ppermute | solution.py:446
  31.0 0.7 collective-permute-start.10
  31.7 5.2 %collective-permute-start.11 = (bf16[256,512]{1,0:T(8,128)(2,1)S(1)}, bf16[256,512]{1,0:T(8,128)(2,1)S(1)}, u32[]{:S(2)}, u32[]{:S(2)}) collective-permute-start(bf16[256,512]{1,0:T(8,128)(2,1)S(1)} %get-tuple-element.67), channel_id=1, source_target_pairs={{0,8},{12,4},{1,9},{13,5},{2,10},{14,6},{3,11},{15,7},{16,24},{28,... | collective-permute-start | bytes 786440 | tf_op jit(solution)/shard_map/ppermute | solution.py:446
  37.6 1.3 collective-permute-start.3
  38.9 1.8 %collective-permute-done.9.refs_6_.refs_5_ = bf16[528,512]{1,0:T(8,128)(2,1)S(1)} collective-permute-done((bf16[528,512]{1,0:T(8,128)(2,1)S(1)}, bf16[528,512]{1,0:T(8,128)(2,1)S(1)}, u32[]{:S(2)}, u32[]{:S(2)}) %collective-permute-start.9) | collective-permute-done | bytes 540704 | tf_op jit(solution)/shard_map/ppermute | solution.py:450
  41.3 1.1 collective-permute-done.11
  42.4 0.7 collective-permute-start.18
  43.1 6.2 %collective-permute-done.3.refs_4_ = bf16[384,512]{1,0:T(8,128)(2,1)S(1)} collective-permute-done((bf16[384,512]{1,0:T(8,128)(2,1)S(1)}, bf16[384,512]{1,0:T(8,128)(2,1)S(1)}, u32[]{:S(2)}, u32[]{:S(2)}) %collective-permute-start.3) | collective-permute-done | bytes 393248 | tf_op jit(solution)/shard_map/ppermute | solution.py:446
  49.4 1.8 %shard_map.181 = (bf16[384,512]{1,0:T(8,128)(2,1)S(1)}, bf16[384,512]{1,0:T(8,128)(2,1)S(1)}, bf16[384,2048]{1,0:T(8,128)(2,1)S(1)}, f32[1,512]{1,0:T(1,128)S(1)}) custom-call(s32[2]{0:T(128)S(1)} %pad_add_fusion.place, bf16[384,512]{1,0:T(8,128)(2,1)S(1)} %copy-done.5, bf16[384,512]{1,0:T(8,128)(2,1)S(1)} %collective-permute-done.refs_0_.refs_1_, ...), custom_call_target="tpu_custom_call" | custom-call | flops 1 | bytes 1 | tf_op jit(solution)/shard_map/pallas_call | solution.py:121
  51.2 1.9 %collective-permute-start.16 = (bf16[384,512]{1,0:T(8,128)(2,1)S(1)}, bf16[384,512]{1,0:T(8,128)(2,1)S(1)}, u32[]{:S(2)}, u32[]{:S(2)}) collective-permute-start(bf16[384,512]{1,0:T(8,128)(2,1)S(1)} %get-tuple-element.70.refs_0_.refs_2_.refs_4_), channel_id=1, source_target_pairs={{0,8},{12,4},{1,9},{13,5},{2,10},{14,6},{3,11},{15,7},{16,24},{28,... | collective-permute-start | bytes 1179656 | tf_op jit(solution)/shard_map/ppermute | solution.py:446
  53.1 1.0 shard_map.182.refs_7_.refs_0_
  54.1 0.7 collective-permute-start.17
  54.8 0.7 collective-permute-start.15
  55.5 4.3 %collective-permute-start.14 = (bf16[384,512]{1,0:T(8,128)(2,1)S(1)}, bf16[384,512]{1,0:T(8,128)(2,1)S(1)}, u32[]{:S(2)}, u32[]{:S(2)}) collective-permute-start(bf16[384,512]{1,0:T(8,128)(2,1)S(1)} %get-tuple-element.70.refs_0_.refs_2_.refs_4_), channel_id=1, source_target_pairs={{0,4},{4,8},{1,5},{5,9},{2,6},{6,10},{3,7},{7,11},{16,20},{20,24},... | collective-permute-start | bytes 1179656 | tf_op jit(solution)/shard_map/ppermute | solution.py:446
  59.8 2.6 %collective-permute-done.16.refs_1_.refs_3_ = bf16[384,512]{1,0:T(8,128)(2,1)S(1)} collective-permute-done((bf16[384,512]{1,0:T(8,128)(2,1)S(1)}, bf16[384,512]{1,0:T(8,128)(2,1)S(1)}, u32[]{:S(2)}, u32[]{:S(2)}) %collective-permute-start.16) | collective-permute-done | bytes 393248 | tf_op jit(solution)/shard_map/ppermute | solution.py:446
  63.1 0.7 collective-permute-start.19
  63.8 0.7 collective-permute-start.20
  64.5 5.7 %collective-permute-done.14.refs_1_ = bf16[384,512]{1,0:T(8,128)(2,1)S(1)} collective-permute-done((bf16[384,512]{1,0:T(8,128)(2,1)S(1)}, bf16[384,512]{1,0:T(8,128)(2,1)S(1)}, u32[]{:S(2)}, u32[]{:S(2)}) %collective-permute-start.14) | collective-permute-done | bytes 393248 | tf_op jit(solution)/shard_map/ppermute | solution.py:446
  70.2 2.4 %shard_map.184.refs_0_ = bf16[384,1024]{1,0:T(8,128)(2,1)S(1)} custom-call(s32[2]{0:T(128)S(1)} %pad_add_fusion.place, bf16[384,512]{1,0:T(8,128)(2,1)S(1)} %get-tuple-element.70.refs_0_.refs_2_.refs_4_, bf16[384,512]{1,0:T(8,128)(2,1)S(1)} %collective-permute-done.14.refs_1_, bf16[384,512]{1,0:T(8,128)(2,1)S(1)} %collective-permute-done.15.refs_2_, ...), custom_call_target="tpu_custom_call" | custom-call | flops 1 | bytes 1 | tf_op jit(solution)/shard_map/pallas_call | solution.py:121
  72.7 1.3 collective-permute-start.23
  74.0 0.7 collective-permute-start.21
  74.7 1.3 collective-permute-start.22
  76.0 20.8 %collective-permute-done.23.refs_1_ = bf16[384,1024]{1,0:T(8,128)(2,1)S(1)} collective-permute-done((bf16[384,1024]{1,0:T(8,128)(2,1)S(1)}, bf16[384,1024]{1,0:T(8,128)(2,1)S(1)}, u32[]{:S(2)}, u32[]{:S(2)}) %collective-permute-start.23) | collective-permute-done | bytes 786464 | tf_op jit(solution)/shard_map/ppermute | solution.py:446
  96.8 1.8 %shard_map.185 = (f32[384,512]{1,0:T(8,128)S(1)}, bf16[384,1024]{1,0:T(8,128)(2,1)S(1)}, f32[264,512]{1,0:T(8,128)S(1)}, f32[256,512]{1,0:T(8,128)S(1)}, f32[256,512]{1,0:T(8,128)S(1)}, /*index=5*/f32[256,512]{1,0:T(8,128)S(1)}) custom-call(s32[2]{0:T(128)S(1)} %pad_add_fusion.place, bf16[384,1024]{1,0:T(8,128)(2,1)S(1)} %shard_map.184.refs_0_, ...), custom_call_target="tpu_custom_call" | custom-call | flops 1 | bytes 1 | tf_op jit(solution)/shard_map/pallas_call | solution.py:121
  98.7 1.9 %collective-permute-done.24.refs_2_ = f32[264,512]{1,0:T(8,128)S(1)} collective-permute-done((f32[264,512]{1,0:T(8,128)S(1)}, f32[264,512]{1,0:T(8,128)S(1)}, u32[]{:S(2)}, u32[]{:S(2)}) %collective-permute-start.24) | collective-permute-done | bytes 540704 | tf_op jit(solution)/shard_map/ppermute | solution.py:450
  100.6 0.7 shard_map.186
  101.3 1.6 %collective-permute-start.25 = (f16[272,512]{1,0:T(8,128)(2,1)S(1)}, f16[272,512]{1,0:T(8,128)(2,1)S(1)}, u32[]{:S(2)}, u32[]{:S(2)}) collective-permute-start(f16[272,512]{1,0:T(8,128)(2,1)S(1)} %convert_element_type.25), channel_id=1, source_target_pairs={{0,2},{1,3},{2,0},{3,1},{4,6},{5,7},{6,4},{7,5},{8,10},{9,11},{10,... | collective-permute-start | bytes 835592 | tf_op jit(solution)/shard_map/ppermute | solution.py:450
  102.9 14.0 %collective-permute-done.22.refs_1_ = bf16[384,1024]{1,0:T(8,128)(2,1)S(1)} collective-permute-done((bf16[384,1024]{1,0:T(8,128)(2,1)S(1)}, bf16[384,1024]{1,0:T(8,128)(2,1)S(1)}, u32[]{:S(2)}, u32[]{:S(2)}) %collective-permute-start.22) | collective-permute-done | bytes 786464 | tf_op jit(solution)/shard_map/ppermute | solution.py:446
  116.8 1.3 shard_map.187
  118.2 1.7 %shard_map.188 = (bf16[384,512]{1,0:T(8,128)(2,1)S(1)}, f32[1,512]{1,0:T(1,128)S(1)}, f32[1,512]{1,0:T(1,128)S(1)}, f32[264,512]{1,0:T(8,128)S(1)}, f32[256,512]{1,0:T(8,128)S(1)}) custom-call(s32[2]{0:T(128)S(1)} %pad_add_fusion.place, bf16[384,1024]{1,0:T(8,128)(2,1)S(1)} %get-tuple-element.78.refs_0_.refs_3_, f32[384,512]{1,0:T(8,128)S(1)} %get-tuple-element.80.refs_1_, ...), custom_call_target="tpu_custom_call" | custom-call | flops 10000000000 | bytes 1 | tf_op jit(solution)/shard_map/pallas_call | solution.py:121
  121.0 1.2 shard_map.189
  122.2 1.6 %collective-permute-start.33 = (f16[272,512]{1,0:T(8,128)(2,1)S(1)}, f16[272,512]{1,0:T(8,128)(2,1)S(1)}, u32[]{:S(2)}, u32[]{:S(2)}) collective-permute-start(f16[272,512]{1,0:T(8,128)(2,1)S(1)} %convert_element_type.31), channel_id=1, source_target_pairs={{0,2},{1,3},{2,0},{3,1},{4,6},{5,7},{6,4},{7,5},{8,10},{9,11},{10,... | collective-permute-start | bytes 835592 | tf_op jit(solution)/shard_map/ppermute | solution.py:450
  123.8 2.5 %shard_map.190 = (bf16[384,512]{1,0:T(8,128)(2,1)}, f32[512,512]{1,0:T(8,128)S(1)}, f32[512,512]{1,0:T(8,128)S(1)}, f32[512,512]{1,0:T(8,128)S(1)}, f32[256,512]{1,0:T(8,128)S(1)}, /*index=5*/f32[256,512]{1,0:T(8,128)S(1)}) custom-call(s32[2]{0:T(128)S(1)} %pad_add_fusion.place, bf16[2048,384]{1,0:T(8,128)(2,1)S(1)} %shard_map.182.refs_7_.refs_0_, ...), custom_call_target="tpu_custom_call" | custom-call | flops 1 | bytes 1 | tf_op jit(solution)/shard_map/pallas_call | solution.py:121
  126.9 0.8 shard_map.191
  128.6 2.7 %collective-permute-done.33 = f16[272,512]{1,0:T(8,128)(2,1)S(1)} collective-permute-done((f16[272,512]{1,0:T(8,128)(2,1)S(1)}, f16[272,512]{1,0:T(8,128)(2,1)S(1)}, u32[]{:S(2)}, u32[]{:S(2)}) %collective-permute-start.33) | collective-permute-done | bytes 278560 | tf_op jit(solution)/shard_map/ppermute | solution.py:450
  131.5 2.9 %shard_map.193 = (f32[512,512]{1,0:T(8,128)}, f32[512,512]{1,0:T(8,128)}, f32[512,512]{1,0:T(8,128)}) custom-call(s32[2]{0:T(128)S(1)} %pad_add_fusion.place, f32[512,512]{1,0:T(8,128)S(1)} %copy-done, f32[512,512]{1,0:T(8,128)S(1)} %copy-done.3, f32[512,512]{1,0:T(8,128)S(1)} %copy-done.4, f32[256,512]{1,0:T(8,128)S(1)} %multiply_add_fusion.3.near, ...), custom_call_target="tpu_custom_call" | custom-call | flops 1 | bytes 1 | tf_op jit(solution)/shard_map/pallas_call | solution.py:647
  134.5 8.0 %collective-permute-done.30 = f16[528,512]{1,0:T(8,128)(2,1)S(1)} collective-permute-done((f16[528,512]{1,0:T(8,128)(2,1)S(1)}, f16[528,512]{1,0:T(8,128)(2,1)S(1)}, u32[]{:S(2)}, u32[]{:S(2)}) %collective-permute-start.30) | collective-permute-done | bytes 540704 | tf_op jit(solution)/shard_map/ppermute | solution.py:450
  142.6 1.1 shard_map.192
  143.7 2.3 %divide_subtract_fusion = (f32[512,512]{1,0:T(8,128)}, f32[512,512]{1,0:T(8,128)}, f32[512,512]{1,0:T(8,128)}) fusion(f32[512,512]{1,0:T(8,128)S(1)} %copy-done.2, f32[512]{0:T(512)S(1)} %bitcast.15, f16[528,512]{1,0:T(8,128)(2,1)S(1)} %collective-permute-done.30, f32[512,512]{1,0:T(8,128)S(1)} %get-tuple-element.95, ...), kind=kLoop, calls=%fused_computation.2 | loop fusion | flops 4194304 | bytes 8914944 | tf_op jit(solution)/shard_map/sub | solution.py:28
  (76 shorter events, 7.9 us)
Async XLA Ops:
  0.6 16.4 %copy-start = (f32[512,512]{1,0:T(8,128)S(1)}, f32[512,512]{1,0:T(8,128)}, u32[]{:S(2)}) copy-start(f32[512,512]{1,0:T(8,128)} %param.20) | copy-start | bytes 3145732
  0.7 1.3 copy-start.1
  2.0 0.7 copy-start.6
  2.7 1.1 copy-start.5
  3.3 13.8 %collective-permute-start.5 = (bf16[528,512]{1,0:T(8,128)(2,1)S(1)}, bf16[528,512]{1,0:T(8,128)(2,1)S(1)}, u32[]{:S(2)}, u32[]{:S(2)}) collective-permute-start(bf16[528,512]{1,0:T(8,128)(2,1)S(1)} %shard_map.178.refs_6_), channel_id=1, source_target_pairs={{0,1},{1,0},{2,3},{3,2},{4,5},{5,4},{6,7},{7,6},{8,9},{9,8},{10,11... | collective-permute-start | bytes 1622024 | tf_op jit(solution)/shard_map/ppermute | solution.py:450
  3.8 15.3 %collective-permute-start.2 = (bf16[384,512]{1,0:T(8,128)(2,1)S(1)}, bf16[384,512]{1,0:T(8,128)(2,1)S(1)}, u32[]{:S(2)}, u32[]{:S(2)}) collective-permute-start(bf16[384,512]{1,0:T(8,128)(2,1)S(1)} %copy-done.5), channel_id=1, source_target_pairs={{0,8},{12,4},{1,9},{13,5},{2,10},{14,6},{3,11},{15,7},{16,24},{28,... | collective-permute-start | bytes 1179656 | tf_op jit(solution)/shard_map/ppermute | solution.py:446
  9.6 13.0 %collective-permute-start.1 = (bf16[384,512]{1,0:T(8,128)(2,1)S(1)}, bf16[384,512]{1,0:T(8,128)(2,1)S(1)}, u32[]{:S(2)}, u32[]{:S(2)}) collective-permute-start(bf16[384,512]{1,0:T(8,128)(2,1)S(1)} %copy-done.5), channel_id=1, source_target_pairs={{4,0},{8,4},{12,8},{5,1},{9,5},{13,9},{6,2},{10,6},{14,10},{7,3},{... | collective-permute-start | bytes 1179656 | tf_op jit(solution)/shard_map/ppermute | solution.py:446
  10.9 20.1 %collective-permute-start = (bf16[384,512]{1,0:T(8,128)(2,1)S(1)}, bf16[384,512]{1,0:T(8,128)(2,1)S(1)}, u32[]{:S(2)}, u32[]{:S(2)}) collective-permute-start(bf16[384,512]{1,0:T(8,128)(2,1)S(1)} %copy-done.5), channel_id=1, source_target_pairs={{0,4},{4,8},{8,12},{1,5},{5,9},{9,13},{2,6},{6,10},{10,14},{3,7},{... | collective-permute-start | bytes 1179656 | tf_op jit(solution)/shard_map/ppermute | solution.py:446
  15.5 16.2 %collective-permute-start.6 = (bf16[528,512]{1,0:T(8,128)(2,1)S(1)}, bf16[528,512]{1,0:T(8,128)(2,1)S(1)}, u32[]{:S(2)}, u32[]{:S(2)}) collective-permute-start(bf16[528,512]{1,0:T(8,128)(2,1)S(1)} %shard_map.178.refs_6_), channel_id=1, source_target_pairs={{0,2},{1,3},{2,0},{3,1},{4,6},{5,7},{6,4},{7,5},{8,10},{9,11},{10,... | collective-permute-start | bytes 1622024 | tf_op jit(solution)/shard_map/ppermute | solution.py:450
  17.7 23.0 %collective-permute-start.9 = (bf16[528,512]{1,0:T(8,128)(2,1)S(1)}, bf16[528,512]{1,0:T(8,128)(2,1)S(1)}, u32[]{:S(2)}, u32[]{:S(2)}) collective-permute-start(bf16[528,512]{1,0:T(8,128)(2,1)S(1)} %shard_map.179.refs_0_.refs_4_.refs_3_), channel_id=1, source_target_pairs={{0,2},{1,3},{2,0},{3,1},{4,6},{5,7},{6,4},{7,5},{8,10},{9,11},{10,... | collective-permute-start | bytes 1622024 | tf_op jit(solution)/shard_map/ppermute | solution.py:450
  19.1 18.4 %collective-permute-start.4 = (bf16[384,512]{1,0:T(8,128)(2,1)S(1)}, bf16[384,512]{1,0:T(8,128)(2,1)S(1)}, u32[]{:S(2)}, u32[]{:S(2)}) collective-permute-start(bf16[384,512]{1,0:T(8,128)(2,1)S(1)} %collective-permute-done.2.refs_3_), channel_id=1, source_target_pairs={{4,0},{8,12},{5,1},{9,13},{6,2},{10,14},{7,3},{11,15},{20,16},{24,... | collective-permute-start | bytes 1179656 | tf_op jit(solution)/shard_map/ppermute | solution.py:446
  22.6 16.2 %collective-permute-start.8 = (bf16[256,512]{1,0:T(8,128)(2,1)S(1)}, bf16[256,512]{1,0:T(8,128)(2,1)S(1)}, u32[]{:S(2)}, u32[]{:S(2)}) collective-permute-start(bf16[256,512]{1,0:T(8,128)(2,1)S(1)} %get-tuple-element.63), channel_id=1, source_target_pairs={{0,4},{4,8},{1,5},{5,9},{2,6},{6,10},{3,7},{7,11},{16,20},{20,24},... | collective-permute-start | bytes 786440 | tf_op jit(solution)/shard_map/ppermute | solution.py:446
  31.0 9.7 %collective-permute-start.10 = (bf16[256,512]{1,0:T(8,128)(2,1)S(1)}, bf16[256,512]{1,0:T(8,128)(2,1)S(1)}, u32[]{:S(2)}, u32[]{:S(2)}) collective-permute-start(bf16[256,512]{1,0:T(8,128)(2,1)S(1)} %get-tuple-element.65), channel_id=1, source_target_pairs={{8,4},{12,8},{9,5},{13,9},{10,6},{14,10},{11,7},{15,11},{24,20},{2... | collective-permute-start | bytes 786440 | tf_op jit(solution)/shard_map/ppermute | solution.py:446
  31.7 10.6 %collective-permute-start.11 = (bf16[256,512]{1,0:T(8,128)(2,1)S(1)}, bf16[256,512]{1,0:T(8,128)(2,1)S(1)}, u32[]{:S(2)}, u32[]{:S(2)}) collective-permute-start(bf16[256,512]{1,0:T(8,128)(2,1)S(1)} %get-tuple-element.67), channel_id=1, source_target_pairs={{0,8},{12,4},{1,9},{13,5},{2,10},{14,6},{3,11},{15,7},{16,24},{28,... | collective-permute-start | bytes 786440 | tf_op jit(solution)/shard_map/ppermute | solution.py:446
  37.6 11.8 %collective-permute-start.3 = (bf16[384,512]{1,0:T(8,128)(2,1)S(1)}, bf16[384,512]{1,0:T(8,128)(2,1)S(1)}, u32[]{:S(2)}, u32[]{:S(2)}) collective-permute-start(bf16[384,512]{1,0:T(8,128)(2,1)S(1)} %shard_map.177), channel_id=1, source_target_pairs={{4,0},{8,12},{5,1},{9,13},{6,2},{10,14},{7,3},{11,15},{20,16},{24,... | collective-permute-start | bytes 1179656 | tf_op jit(solution)/shard_map/ppermute | solution.py:446
  38.9 10.5 %collective-permute-start.12 = (bf16[528,512]{1,0:T(8,128)(2,1)S(1)}, bf16[528,512]{1,0:T(8,128)(2,1)S(1)}, u32[]{:S(2)}, u32[]{:S(2)}) collective-permute-start(bf16[528,512]{1,0:T(8,128)(2,1)S(1)} %shard_map.179.refs_0_.refs_4_.refs_3_), channel_id=1, source_target_pairs={{0,1},{1,0},{2,3},{3,2},{4,5},{5,4},{6,7},{7,6},{8,9},{9,8},{10,11... | collective-permute-start | bytes 1622024 | tf_op jit(solution)/shard_map/ppermute | solution.py:450
  40.7 8.7 %collective-permute-start.7 = (bf16[528,512]{1,0:T(8,128)(2,1)S(1)}, bf16[528,512]{1,0:T(8,128)(2,1)S(1)}, u32[]{:S(2)}, u32[]{:S(2)}) collective-permute-start(bf16[528,512]{1,0:T(8,128)(2,1)S(1)} %collective-permute-done.6.refs_8_), channel_id=1, source_target_pairs={{0,1},{1,0},{2,3},{3,2},{4,5},{5,4},{6,7},{7,6},{8,9},{9,8},{10,11... | collective-permute-start | bytes 1622024 | tf_op jit(solution)/shard_map/ppermute | solution.py:450
  40.7 8.7 %collective-permute-start.13 = (bf16[528,512]{1,0:T(8,128)(2,1)S(1)}, bf16[528,512]{1,0:T(8,128)(2,1)S(1)}, u32[]{:S(2)}, u32[]{:S(2)}) collective-permute-start(bf16[528,512]{1,0:T(8,128)(2,1)S(1)} %collective-permute-done.9.refs_6_.refs_5_), channel_id=1, source_target_pairs={{0,1},{1,0},{2,3},{3,2},{4,5},{5,4},{6,7},{7,6},{8,9},{9,8},{10,11... | collective-permute-start | bytes 1622024 | tf_op jit(solution)/shard_map/ppermute | solution.py:450
  42.4 17.4 %collective-permute-start.18 = (bf16[768,512]{1,0:T(8,128)(2,1)S(1)}, bf16[768,512]{1,0:T(8,128)(2,1)S(1)}, u32[]{:S(2)}, u32[]{:S(2)}) collective-permute-start(bf16[768,512]{1,0:T(8,128)(2,1)S(1)} %constant_dynamic-update-slice_fusion.refs_10_.refs_8_), channel_id=1, source_target_pairs={{4,6},{5,7},{6,4},{7,5},{8,10},{9,11},{10,8},{11,9},{20,22},{21,23... | collective-permute-start | bytes 2359304 | tf_op jit(solution)/shard_map/ppermute | solution.py:450
  51.2 11.3 %collective-permute-start.16 = (bf16[384,512]{1,0:T(8,128)(2,1)S(1)}, bf16[384,512]{1,0:T(8,128)(2,1)S(1)}, u32[]{:S(2)}, u32[]{:S(2)}) collective-permute-start(bf16[384,512]{1,0:T(8,128)(2,1)S(1)} %get-tuple-element.70.refs_0_.refs_2_.refs_4_), channel_id=1, source_target_pairs={{0,8},{12,4},{1,9},{13,5},{2,10},{14,6},{3,11},{15,7},{16,24},{28,... | collective-permute-start | bytes 1179656 | tf_op jit(solution)/shard_map/ppermute | solution.py:446
  54.1 16.2 %collective-permute-start.17 = (bf16[768,512]{1,0:T(8,128)(2,1)S(1)}, bf16[768,512]{1,0:T(8,128)(2,1)S(1)}, u32[]{:S(2)}, u32[]{:S(2)}) collective-permute-start(bf16[768,512]{1,0:T(8,128)(2,1)S(1)} %constant_dynamic-update-slice_fusion.refs_10_.refs_8_), channel_id=1, source_target_pairs={{4,5},{5,4},{6,7},{7,6},{8,9},{9,8},{10,11},{11,10},{20,21},{21,20... | collective-permute-start | bytes 2359304 | tf_op jit(solution)/shard_map/ppermute | solution.py:450
  54.8 9.7 %collective-permute-start.15 = (bf16[384,512]{1,0:T(8,128)(2,1)S(1)}, bf16[384,512]{1,0:T(8,128)(2,1)S(1)}, u32[]{:S(2)}, u32[]{:S(2)}) collective-permute-start(bf16[384,512]{1,0:T(8,128)(2,1)S(1)} %get-tuple-element.70.refs_0_.refs_2_.refs_4_), channel_id=1, source_target_pairs={{8,4},{12,8},{9,5},{13,9},{10,6},{14,10},{11,7},{15,11},{24,20},{2... | collective-permute-start | bytes 1179656 | tf_op jit(solution)/shard_map/ppermute | solution.py:446
  55.5 14.7 %collective-permute-start.14 = (bf16[384,512]{1,0:T(8,128)(2,1)S(1)}, bf16[384,512]{1,0:T(8,128)(2,1)S(1)}, u32[]{:S(2)}, u32[]{:S(2)}) collective-permute-start(bf16[384,512]{1,0:T(8,128)(2,1)S(1)} %get-tuple-element.70.refs_0_.refs_2_.refs_4_), channel_id=1, source_target_pairs={{0,4},{4,8},{1,5},{5,9},{2,6},{6,10},{3,7},{7,11},{16,20},{20,24},... | collective-permute-start | bytes 1179656 | tf_op jit(solution)/shard_map/ppermute | solution.py:446
  63.1 7.1 %collective-permute-start.19 = (bf16[384,512]{1,0:T(8,128)(2,1)S(1)}, bf16[384,512]{1,0:T(8,128)(2,1)S(1)}, u32[]{:S(2)}, u32[]{:S(2)}) collective-permute-start(bf16[384,512]{1,0:T(8,128)(2,1)S(1)} %get-tuple-element.72), channel_id=1, source_target_pairs={{4,5},{5,4},{6,7},{7,6},{8,9},{9,8},{10,11},{11,10},{20,21},{21,20... | collective-permute-start | bytes 1179656 | tf_op jit(solution)/shard_map/ppermute | solution.py:450
  63.8 6.4 %collective-permute-start.20 = (bf16[384,512]{1,0:T(8,128)(2,1)S(1)}, bf16[384,512]{1,0:T(8,128)(2,1)S(1)}, u32[]{:S(2)}, u32[]{:S(2)}) collective-permute-start(bf16[384,512]{1,0:T(8,128)(2,1)S(1)} %get-tuple-element.73), channel_id=1, source_target_pairs={{4,5},{5,4},{6,7},{7,6},{8,9},{9,8},{10,11},{11,10},{20,21},{21,20... | collective-permute-start | bytes 1179656 | tf_op jit(solution)/shard_map/ppermute | solution.py:450
  72.7 24.2 %collective-permute-start.23 = (bf16[384,1024]{1,0:T(8,128)(2,1)S(1)}, bf16[384,1024]{1,0:T(8,128)(2,1)S(1)}, u32[]{:S(2)}, u32[]{:S(2)}) collective-permute-start(bf16[384,1024]{1,0:T(8,128)(2,1)S(1)} %shard_map.184.refs_0_), channel_id=1, source_target_pairs={{4,0},{8,12},{5,1},{9,13},{6,2},{10,14},{7,3},{11,15},{20,16},{24,... | collective-permute-start | bytes 2359304 | tf_op jit(solution)/shard_map/ppermute | solution.py:446
  74.0 22.9 %collective-permute-start.21 = (bf16[384,1024]{1,0:T(8,128)(2,1)S(1)}, bf16[384,1024]{1,0:T(8,128)(2,1)S(1)}, u32[]{:S(2)}, u32[]{:S(2)}) collective-permute-start(bf16[384,1024]{1,0:T(8,128)(2,1)S(1)} %shard_map.184.refs_0_), channel_id=1, source_target_pairs={{4,8},{8,4},{5,9},{9,5},{6,10},{10,6},{7,11},{11,7},{20,24},{24,20... | collective-permute-start | bytes 2359304 | tf_op jit(solution)/shard_map/ppermute | solution.py:446
  74.7 42.1 %collective-permute-start.22 = (bf16[384,1024]{1,0:T(8,128)(2,1)S(1)}, bf16[384,1024]{1,0:T(8,128)(2,1)S(1)}, u32[]{:S(2)}, u32[]{:S(2)}) collective-permute-start(bf16[384,1024]{1,0:T(8,128)(2,1)S(1)} %shard_map.184.refs_0_), channel_id=1, source_target_pairs={{8,0},{4,12},{9,1},{5,13},{10,2},{6,14},{11,3},{7,15},{24,16},{20,... | collective-permute-start | bytes 2359304 | tf_op jit(solution)/shard_map/ppermute | solution.py:446
  98.6 2.0 %collective-permute-start.24 = (f32[264,512]{1,0:T(8,128)S(1)}, f32[264,512]{1,0:T(8,128)S(1)}, u32[]{:S(2)}, u32[]{:S(2)}) collective-permute-start(f32[264,512]{1,0:T(8,128)S(1)} %get-tuple-element.76), channel_id=1, source_target_pairs={{0,1},{1,0},{2,3},{3,2},{4,5},{5,4},{6,7},{7,6},{8,9},{9,8},{10,11... | collective-permute-start | bytes 1622024 | tf_op jit(solution)/shard_map/ppermute | solution.py:450
  101.3 16.9 %collective-permute-start.25 = (f16[272,512]{1,0:T(8,128)(2,1)S(1)}, f16[272,512]{1,0:T(8,128)(2,1)S(1)}, u32[]{:S(2)}, u32[]{:S(2)}) collective-permute-start(f16[272,512]{1,0:T(8,128)(2,1)S(1)} %convert_element_type.25), channel_id=1, source_target_pairs={{0,2},{1,3},{2,0},{3,1},{4,6},{5,7},{6,4},{7,5},{8,10},{9,11},{10,... | collective-permute-start | bytes 835592 | tf_op jit(solution)/shard_map/ppermute | solution.py:450
  118.1 2.9 %collective-permute-start.26 = (f32[256,512]{1,0:T(8,128)S(1)}, f32[256,512]{1,0:T(8,128)S(1)}, u32[]{:S(2)}, u32[]{:S(2)}) collective-permute-start(f32[256,512]{1,0:T(8,128)S(1)} %get-tuple-element.85), channel_id=1, source_target_pairs={{0,1},{1,0},{2,3},{3,2},{4,5},{5,4},{6,7},{7,6},{8,9},{9,8},{10,11... | collective-permute-start | bytes 1572872 | tf_op jit(solution)/shard_map/ppermute | solution.py:450
  119.9 7.0 %collective-permute-start.27 = (f32[264,512]{1,0:T(8,128)S(1)}, f32[264,512]{1,0:T(8,128)S(1)}, u32[]{:S(2)}, u32[]{:S(2)}) collective-permute-start(f32[264,512]{1,0:T(8,128)S(1)} %get-tuple-element.90), channel_id=1, source_target_pairs={{0,1},{1,0},{2,3},{3,2},{4,5},{5,4},{6,7},{7,6},{8,9},{9,8},{10,11... | collective-permute-start | bytes 1622024 | tf_op jit(solution)/shard_map/ppermute | solution.py:450
  120.4 5.8 %collective-permute-start.28 = (f32[256,512]{1,0:T(8,128)S(1)}, f32[256,512]{1,0:T(8,128)S(1)}, u32[]{:S(2)}, u32[]{:S(2)}) collective-permute-start(f32[256,512]{1,0:T(8,128)S(1)} %get-tuple-element.91), channel_id=1, source_target_pairs={{0,1},{1,0},{2,3},{3,2},{4,5},{5,4},{6,7},{7,6},{8,9},{9,8},{10,11... | collective-permute-start | bytes 1572872 | tf_op jit(solution)/shard_map/ppermute | solution.py:450
  120.5 7.9 %collective-permute-start.31 = (f32[256,512]{1,0:T(8,128)S(1)}, f32[256,512]{1,0:T(8,128)S(1)}, u32[]{:S(2)}, u32[]{:S(2)}) collective-permute-start(f32[256,512]{1,0:T(8,128)S(1)} %get-tuple-element.104), channel_id=1, source_target_pairs={{0,1},{1,0},{2,3},{3,2},{4,5},{5,4},{6,7},{7,6},{8,9},{9,8},{10,11... | collective-permute-start | bytes 1572872 | tf_op jit(solution)/shard_map/ppermute | solution.py:450
  122.2 9.1 %collective-permute-start.33 = (f16[272,512]{1,0:T(8,128)(2,1)S(1)}, f16[272,512]{1,0:T(8,128)(2,1)S(1)}, u32[]{:S(2)}, u32[]{:S(2)}) collective-permute-start(f16[272,512]{1,0:T(8,128)(2,1)S(1)} %convert_element_type.31), channel_id=1, source_target_pairs={{0,2},{1,3},{2,0},{3,1},{4,6},{5,7},{6,4},{7,5},{8,10},{9,11},{10,... | collective-permute-start | bytes 835592 | tf_op jit(solution)/shard_map/ppermute | solution.py:450
  126.3 5.0 %collective-permute-start.32 = (f32[256,512]{1,0:T(8,128)S(1)}, f32[256,512]{1,0:T(8,128)S(1)}, u32[]{:S(2)}, u32[]{:S(2)}) collective-permute-start(f32[256,512]{1,0:T(8,128)S(1)} %get-tuple-element.106), channel_id=1, source_target_pairs={{0,1},{1,0},{2,3},{3,2},{4,5},{5,4},{6,7},{7,6},{8,9},{9,8},{10,11... | collective-permute-start | bytes 1572872 | tf_op jit(solution)/shard_map/ppermute | solution.py:450
  126.3 17.3 %collective-permute-start.29 = (f32[512,512]{1,0:T(8,128)S(1)}, f32[512,512]{1,0:T(8,128)S(1)}, u32[]{:S(2)}, u32[]{:S(2)}) collective-permute-start(f32[512,512]{1,0:T(8,128)S(1)} %get-tuple-element.96), channel_id=1, source_target_pairs={{0,1},{1,0},{2,3},{3,2},{4,5},{5,4},{6,7},{7,6},{8,9},{9,8},{10,11... | collective-permute-start | bytes 3145736 | tf_op jit(solution)/shard_map/ppermute | solution.py:450
  127.8 14.7 %collective-permute-start.30 = (f16[528,512]{1,0:T(8,128)(2,1)S(1)}, f16[528,512]{1,0:T(8,128)(2,1)S(1)}, u32[]{:S(2)}, u32[]{:S(2)}) collective-permute-start(f16[528,512]{1,0:T(8,128)(2,1)S(1)} %convert_element_type.26), channel_id=1, source_target_pairs={{0,2},{1,3},{2,0},{3,1},{4,6},{5,7},{6,4},{7,5},{8,10},{9,11},{10,... | collective-permute-start | bytes 1622024 | tf_op jit(solution)/shard_map/ppermute | solution.py:450
  128.4 3.0 %copy-start.3 = (f32[512,512]{1,0:T(8,128)S(1)}, f32[512,512]{1,0:T(8,128)}, u32[]{:S(2)}) copy-start(f32[512,512]{1,0:T(8,128)} %moment) | copy-start | bytes 3145732
  128.4 3.1 %copy-start.4 = (f32[512,512]{1,0:T(8,128)S(1)}, f32[512,512]{1,0:T(8,128)}, u32[]{:S(2)}) copy-start(f32[512,512]{1,0:T(8,128)} %square) | copy-start | bytes 3145732
  131.5 11.1 %copy-start.7 = (f32[128]{0:T(128)S(1)}, f32[128]{0:T(128)}, u32[]{:S(2)}) copy-start(f32[128]{0:T(128)} %param.12) | copy-start | bytes 1540
  131.5 11.1 %copy-start.8 = (f32[128]{0:T(128)S(1)}, f32[128]{0:T(128)}, u32[]{:S(2)}) copy-start(f32[128]{0:T(128)} %param.16) | copy-start | bytes 1540
  131.5 11.1 %copy-start.9 = (f32[128]{0:T(128)S(1)}, f32[128]{0:T(128)}, u32[]{:S(2)}) copy-start(f32[128]{0:T(128)} %param.17) | copy-start | bytes 1540
  131.5 12.1 %copy-start.2 = (f32[512,512]{1,0:T(8,128)S(1)}, f32[512,512]{1,0:T(8,128)}, u32[]{:S(2)}) copy-start(f32[512,512]{1,0:T(8,128)} %refs_0_.3) | copy-start | bytes 3145732
  131.5 12.1 %copy-start.10 = (f32[512,512]{1,0:T(8,128)S(1)}, f32[512,512]{1,0:T(8,128)}, u32[]{:S(2)}) copy-start(f32[512,512]{1,0:T(8,128)} %param.14) | copy-start | bytes 3145732
  131.5 12.1 %copy-start.11 = (f32[512,512]{1,0:T(8,128)S(1)}, f32[512,512]{1,0:T(8,128)}, u32[]{:S(2)}) copy-start(f32[512,512]{1,0:T(8,128)} %param.15) | copy-start | bytes 3145732

commit v11 on v9

--- a/solution.py
+++ b/solution.py
@@ -233,20 +233,30 @@
         out[...] = dec[pl.ds(pl.multiple_of(jnp.where(second, half, 0), half), half), :]
 
 
+def stack_body(place, piece0, piece1, piece2, first, second):
+    size = piece0.shape[0]
+    edge = first.shape[0]
+    first[:size] = piece0[...]
+    first[size:] = piece1[: edge - size]
+    second[: edge - size] = piece1[edge - size :]
+    second[edge - size :] = piece2[...]
+
+
 def turn_body(place, full, turned):
     turned[...] = full[...].T
 
 
-def error_body(
-    place, own, low, high, across, dec0, dec1, dec2, dec3, row0, row1, row2, row3, inputs, error
-):
+def error_body(place, own, low, high, across, dec0, dec1, dec2, dec3, *refs):
+    *rows, inputs, error = refs
     z, i = place[0], place[1]
-    half = row0.shape[0] // 3
+    edge = rows[0].shape[0]
+    half = 2 * edge // 3
     shift = pl.multiple_of(jnp.where(z >= 2, half, 0), half)
-    for t in range(4):
-        dec, row = (dec0, dec1, dec2, dec3)[t], (row0, row1, row2, row3)[t]
+    for t, dec in enumerate((dec0, dec1, dec2, dec3)):
+        first, second = rows[2 * t], rows[2 * t + 1]
+        between = jnp.concatenate([first[half:], second[: edge - half]], axis=0)
         lefts = (own, low, high, across)
-        rights = [dec[pl.ds(shift, half), :]] + [row[m * half : (m + 1) * half, :] for m in range(3)]
+        rights = [dec[pl.ds(shift, half), :], first[:half], between, second[edge - half :]]
         total = jnp.zeros((own.shape[0], half), F32)
         for left, right in zip(lefts, rights):
             total += lax.dot_general(
@@ -455,13 +465,13 @@
         decoder,
         after=(enc_core,),
     )
-    dec_chip, dec_core = flip(dec_own, 2), flip(dec_own, 1)
+    dec_late = behind(dec_own, enc_chip)
+    dec_chip, dec_core = flip(dec_late, 2), flip(dec_late, 1)
     (onward,) = local_kernel(
         onward_body, [shape((count, width), BF16)], place, low, high
     )
     relay1 = along(onward, ends)
     relay2 = along(across, ends)
-    enc = [enc_own, enc_core, enc_chip, flip(behind(enc_chip, relay2), 1)]
 
     up, down, beyond = local_kernel(
         pieces_body, [shape((half, latents), BF16)] * 3, place, dec_own
@@ -471,9 +481,18 @@
         along(down, [(2, 1), (3, 2)]),
         along(beyond, [(0, 2), (3, 1)]),
     ]
+    enc_both = flip(behind(enc_chip, relay1, relay2, *dec_pieces), 1)
+    enc = [enc_own, enc_core, enc_chip, enc_both]
     dec = [dec_own, dec_core, dec_chip, flip(dec_chip, 1)]
 
-    rows_own = jnp.concatenate([behind(piece, dec_chip) for piece in dec_pieces], axis=0)
+    rows_own = local_kernel(
+        stack_body,
+        [shape((3 * half // 2, latents), BF16)] * 2,
+        place,
+        *dec_pieces,
+        after=(dec_chip,),
+    )
+    rows_chip = [flip(piece, 2, (1, 2)) for piece in rows_own]
     codes, mask, inputs, active = local_kernel(
         codes_body,
         [
@@ -490,7 +509,7 @@
         relay1,
         relay2,
         *enc,
-        after=(rows_own,),
+        after=(*rows_own, dec[1], dec[3]),
         scratch=[pltpu.VMEM((1, latents), F32)],
     )
     codes_low = along(codes, [(0, 1), (1, 2)])
@@ -499,11 +518,8 @@
     (turned,) = local_kernel(
         turn_body, [shape((features, count), BF16)], place, inputs
     )
-    rows_chip = flip(rows_own, 2, (1, 2))
-    rows_core = flip(behind(rows_own, turned), 1, (1, 2))
-    rows_both = flip(
-        behind(rows_chip, codes_low, codes_high, codes_across, dec[1], dec[3]), 1, (1, 2)
-    )
+    rows_core = [flip(behind(piece, turned), 1, (1, 2)) for piece in rows_own]
+    rows_both = [flip(behind(piece, codes_across), 1, (1, 2)) for piece in rows_chip]
 
     (own_error,) = local_kernel(
         error_body,
@@ -514,10 +530,10 @@
         codes_high,
         codes_across,
         *dec,
-        rows_own,
-        rows_core,
-        rows_chip,
-        rows_both,
+        *rows_own,
+        *rows_core,
+        *rows_chip,
+        *rows_both,
         inputs,
     )
     swapped = along(own_error, [(1, 2), (2, 1)])

time: 150 us -> 154 us (1.027)
  starting transfers between devices: 46.8 us -> 53.5 us
  waiting for transfers between devices: 75.2 us -> 72.1 us
    ppermute x14, starting transfers between devices: 37.4 us -> 40.8 us  [along(): return lax.ppermute(value, 'latent', pairs)]
    ppermute x19 -> x22, starting transfers between devices: 9.47 us -> 12.7 us  [flip(): return lax.ppermute(value, ('latent', 'dp'), pairs)]
    ppermute x14, waiting for transfers between devices: 60.8 us -> 58.5 us  [along(): return lax.ppermute(value, 'latent', pairs)]
    ppermute x19 -> x22, waiting for transfers between devices: 14.5 us -> 13.6 us  [flip(): return lax.ppermute(value, ('latent', 'dp'), pairs)]
    pallas_call x15 -> x16, Pallas kernels: 18.6 us -> 19.2 us  [local_kernel(): pl.pallas_call(run, out_shape=outs, in_specs=[SMEM] + [VMEM] * len(args)...]
  transfers between devices with their start and end apart: 33 -> 36, of which waited for: 12 -> 13; matrix products, arithmetic and copies ran while one was open for 0% -> 0% of each run, Pallas kernels for 12% -> 12%
where the time goes in v11:
time: 154 us
  waiting for transfers between devices  72.1 us (47%)
  starting transfers between devices  53.5 us (35%)
  Pallas kernels  22.1 us (14%)
  other arithmetic  2.9 us (2%)
  local copies, waits for them, and re-layouts  2 us (1%)
    ppermute x14, waiting for transfers between devices, along(): return lax.ppermute(value, 'latent', pairs)  58.5 us
    ppermute x14, starting transfers between devices, along(): return lax.ppermute(value, 'latent', pairs)  40.8 us
    pallas_call x16, Pallas kernels, local_kernel(): pl.pallas_call(run, out_shape=outs, in_specs=[SMEM] + [VMEM] * len(args)...  19.2 us
    ppermute x22, waiting for transfers between devices, flip(): return lax.ppermute(value, ('latent', 'dp'), pairs)  13.6 us
    ppermute x22, starting transfers between devices, flip(): return lax.ppermute(value, ('latent', 'dp'), pairs)  12.7 us
  transfers between devices with their start and end apart: 36, of which 13 were waited for; matrix products, arithmetic and copies ran while one was open for 0% of the time, Pallas kernels for 12%

profile of v11, /device:TPU:0, one launch (start us, length us, event | category | flops | bytes accessed | tf_op | source)
XLA Modules:
  0.0 153.9 jit_solution(6087553514870811351)
XLA Ops:
  0.7 1.3 copy-done.1
  3.8 2.6 %collective-permute-start.6 = (bf16[528,512]{1,0:T(8,128)(2,1)S(1)}, bf16[528,512]{1,0:T(8,128)(2,1)S(1)}, u32[]{:S(2)}, u32[]{:S(2)}) collective-permute-start(bf16[528,512]{1,0:T(8,128)(2,1)S(1)} %shard_map.178.refs_6_), channel_id=1, source_target_pairs={{0,2},{1,3},{2,0},{3,1},{4,6},{5,7},{6,4},{7,5},{8,10},{9,11},{10,... | collective-permute-start | bytes 1622024 | tf_op jit(solution)/shard_map/ppermute | solution.py:446
  6.4 1.3 collective-permute-start.1
  7.7 4.6 %collective-permute-start = (bf16[384,512]{1,0:T(8,128)(2,1)S(1)}, bf16[384,512]{1,0:T(8,128)(2,1)S(1)}, u32[]{:S(2)}, u32[]{:S(2)}) collective-permute-start(bf16[384,512]{1,0:T(8,128)(2,1)S(1)} %copy-done.5), channel_id=1, source_target_pairs={{0,4},{4,8},{8,12},{1,5},{5,9},{9,13},{2,6},{6,10},{10,14},{3,7},{... | collective-permute-start | bytes 1179656 | tf_op jit(solution)/shard_map/ppermute | solution.py:442
  12.2 4.5 %collective-permute-start.2 = (bf16[384,512]{1,0:T(8,128)(2,1)S(1)}, bf16[384,512]{1,0:T(8,128)(2,1)S(1)}, u32[]{:S(2)}, u32[]{:S(2)}) collective-permute-start(bf16[384,512]{1,0:T(8,128)(2,1)S(1)} %copy-done.5), channel_id=1, source_target_pairs={{0,8},{12,4},{1,9},{13,5},{2,10},{14,6},{3,11},{15,7},{16,24},{28,... | collective-permute-start | bytes 1179656 | tf_op jit(solution)/shard_map/ppermute | solution.py:442
  16.8 2.7 %collective-permute-done.1.refs_1_.refs_2_ = bf16[384,512]{1,0:T(8,128)(2,1)S(1)} collective-permute-done((bf16[384,512]{1,0:T(8,128)(2,1)S(1)}, bf16[384,512]{1,0:T(8,128)(2,1)S(1)}, u32[]{:S(2)}, u32[]{:S(2)}) %collective-permute-start.1) | collective-permute-done | bytes 393248 | tf_op jit(solution)/shard_map/ppermute | solution.py:442
  19.4 2.3 %collective-permute-done.refs_0_.refs_1_ = bf16[384,512]{1,0:T(8,128)(2,1)S(1)} collective-permute-done((bf16[384,512]{1,0:T(8,128)(2,1)S(1)}, bf16[384,512]{1,0:T(8,128)(2,1)S(1)}, u32[]{:S(2)}, u32[]{:S(2)}) %collective-permute-start) | collective-permute-done | bytes 393248 | tf_op jit(solution)/shard_map/ppermute | solution.py:442
  22.3 1.3 collective-permute-start.3
  24.6 4.5 %collective-permute-done.2.refs_3_ = bf16[384,512]{1,0:T(8,128)(2,1)S(1)} collective-permute-done((bf16[384,512]{1,0:T(8,128)(2,1)S(1)}, bf16[384,512]{1,0:T(8,128)(2,1)S(1)}, u32[]{:S(2)}, u32[]{:S(2)}) %collective-permute-start.2) | collective-permute-done | bytes 393248 | tf_op jit(solution)/shard_map/ppermute | solution.py:442
  29.1 1.3 collective-permute-start.4
  31.0 4.6 %collective-permute-start.7 = (bf16[256,512]{1,0:T(8,128)(2,1)S(1)}, bf16[256,512]{1,0:T(8,128)(2,1)S(1)}, u32[]{:S(2)}, u32[]{:S(2)}) collective-permute-start(bf16[256,512]{1,0:T(8,128)(2,1)S(1)} %get-tuple-element.63), channel_id=1, source_target_pairs={{0,4},{4,8},{1,5},{5,9},{2,6},{6,10},{3,7},{7,11},{16,20},{20,24},... | collective-permute-start | bytes 786440 | tf_op jit(solution)/shard_map/ppermute | solution.py:442
  35.6 0.7 collective-permute-start.8
  36.3 9.2 %collective-permute-start.9 = (bf16[256,512]{1,0:T(8,128)(2,1)S(1)}, bf16[256,512]{1,0:T(8,128)(2,1)S(1)}, u32[]{:S(2)}, u32[]{:S(2)}) collective-permute-start(bf16[256,512]{1,0:T(8,128)(2,1)S(1)} %get-tuple-element.65), channel_id=1, source_target_pairs={{0,8},{12,4},{1,9},{13,5},{2,10},{14,6},{3,11},{15,7},{16,24},{28,... | collective-permute-start | bytes 786440 | tf_op jit(solution)/shard_map/ppermute | solution.py:442
  45.6 3.7 %collective-permute-done.9.refs_2_ = bf16[256,512]{1,0:T(8,128)(2,1)S(1)} collective-permute-done((bf16[256,512]{1,0:T(8,128)(2,1)S(1)}, bf16[256,512]{1,0:T(8,128)(2,1)S(1)}, u32[]{:S(2)}, u32[]{:S(2)}) %collective-permute-start.9) | collective-permute-done | bytes 262176 | tf_op jit(solution)/shard_map/ppermute | solution.py:442
  50.4 0.7 collective-permute-start.19
  51.2 0.8 collective-permute-done.13.refs_13_.refs_7_.refs_6_
  52.0 1.8 %shard_map.182 = (bf16[384,512]{1,0:T(8,128)(2,1)S(1)}, bf16[384,512]{1,0:T(8,128)(2,1)S(1)}, bf16[384,2048]{1,0:T(8,128)(2,1)S(1)}, f32[1,512]{1,0:T(1,128)S(1)}) custom-call(s32[2]{0:T(128)S(1)} %pad_add_fusion.place, bf16[384,512]{1,0:T(8,128)(2,1)S(1)} %copy-done.5, bf16[384,512]{1,0:T(8,128)(2,1)S(1)} %collective-permute-done.refs_0_.refs_1_, ...), custom_call_target="tpu_custom_call" | custom-call | flops 1 | bytes 1 | tf_op jit(solution)/shard_map/pallas_call | solution.py:121
  53.8 7.2 %collective-permute-start.16 = (bf16[384,512]{1,0:T(8,128)(2,1)S(1)}, bf16[384,512]{1,0:T(8,128)(2,1)S(1)}, u32[]{:S(2)}, u32[]{:S(2)}) collective-permute-start(bf16[384,512]{1,0:T(8,128)(2,1)S(1)} %get-tuple-element.71.refs_0_.refs_2_.refs_4_), channel_id=1, source_target_pairs={{0,8},{12,4},{1,9},{13,5},{2,10},{14,6},{3,11},{15,7},{16,24},{28,... | collective-permute-start | bytes 1179656 | tf_op jit(solution)/shard_map/ppermute | solution.py:442
  61.0 0.7 collective-permute-start.20
  61.7 0.7 collective-permute-start.15
  62.4 2.3 %collective-permute-start.14 = (bf16[384,512]{1,0:T(8,128)(2,1)S(1)}, bf16[384,512]{1,0:T(8,128)(2,1)S(1)}, u32[]{:S(2)}, u32[]{:S(2)}) collective-permute-start(bf16[384,512]{1,0:T(8,128)(2,1)S(1)} %get-tuple-element.71.refs_0_.refs_2_.refs_4_), channel_id=1, source_target_pairs={{0,4},{4,8},{1,5},{5,9},{2,6},{6,10},{3,7},{7,11},{16,20},{20,24},... | collective-permute-start | bytes 1179656 | tf_op jit(solution)/shard_map/ppermute | solution.py:442
  64.7 1.0 shard_map.183.refs_7_.refs_0_
  65.7 0.7 collective-permute-start.17
  66.4 4.1 %collective-permute-done.16.refs_3_ = bf16[384,512]{1,0:T(8,128)(2,1)S(1)} collective-permute-done((bf16[384,512]{1,0:T(8,128)(2,1)S(1)}, bf16[384,512]{1,0:T(8,128)(2,1)S(1)}, u32[]{:S(2)}, u32[]{:S(2)}) %collective-permute-start.16) | collective-permute-done | bytes 393248 | tf_op jit(solution)/shard_map/ppermute | solution.py:442
  71.2 0.7 collective-permute-start.21
  71.9 0.7 collective-permute-start.22
  72.6 5.1 %collective-permute-done.14.refs_1_ = bf16[384,512]{1,0:T(8,128)(2,1)S(1)} collective-permute-done((bf16[384,512]{1,0:T(8,128)(2,1)S(1)}, bf16[384,512]{1,0:T(8,128)(2,1)S(1)}, u32[]{:S(2)}, u32[]{:S(2)}) %collective-permute-start.14) | collective-permute-done | bytes 393248 | tf_op jit(solution)/shard_map/ppermute | solution.py:442
  77.7 2.4 %shard_map.184.refs_0_ = bf16[384,1024]{1,0:T(8,128)(2,1)S(1)} custom-call(s32[2]{0:T(128)S(1)} %pad_add_fusion.place, bf16[384,512]{1,0:T(8,128)(2,1)S(1)} %get-tuple-element.71.refs_0_.refs_2_.refs_4_, bf16[384,512]{1,0:T(8,128)(2,1)S(1)} %collective-permute-done.14.refs_1_, bf16[384,512]{1,0:T(8,128)(2,1)S(1)} %collective-permute-done.15.refs_2_, ...), custom_call_target="tpu_custom_call" | custom-call | flops 1 | bytes 1 | tf_op jit(solution)/shard_map/pallas_call | solution.py:121
  80.1 1.3 collective-permute-start.25
  81.4 0.7 collective-permute-start.23
  82.1 1.3 collective-permute-start.24
  83.4 21.3 %collective-permute-done.25.refs_1_ = bf16[384,1024]{1,0:T(8,128)(2,1)S(1)} collective-permute-done((bf16[384,1024]{1,0:T(8,128)(2,1)S(1)}, bf16[384,1024]{1,0:T(8,128)(2,1)S(1)}, u32[]{:S(2)}, u32[]{:S(2)}) %collective-permute-start.25) | collective-permute-done | bytes 786464 | tf_op jit(solution)/shard_map/ppermute | solution.py:442
  104.7 1.8 %shard_map.185 = (f32[384,512]{1,0:T(8,128)S(1)}, bf16[384,1024]{1,0:T(8,128)(2,1)S(1)}, f32[264,512]{1,0:T(8,128)S(1)}, f32[256,512]{1,0:T(8,128)S(1)}, f32[256,512]{1,0:T(8,128)S(1)}, /*index=5*/f32[256,512]{1,0:T(8,128)S(1)}) custom-call(s32[2]{0:T(128)S(1)} %pad_add_fusion.place, bf16[384,1024]{1,0:T(8,128)(2,1)S(1)} %shard_map.184.refs_0_, ...), custom_call_target="tpu_custom_call" | custom-call | flops 1 | bytes 1 | tf_op jit(solution)/shard_map/pallas_call | solution.py:121
  106.6 1.9 %collective-permute-done.26.refs_2_ = f32[264,512]{1,0:T(8,128)S(1)} collective-permute-done((f32[264,512]{1,0:T(8,128)S(1)}, f32[264,512]{1,0:T(8,128)S(1)}, u32[]{:S(2)}, u32[]{:S(2)}) %collective-permute-start.26) | collective-permute-done | bytes 540704 | tf_op jit(solution)/shard_map/ppermute | solution.py:446
  109.2 0.7 collective-permute-start.27
  110.0 14.8 %collective-permute-done.24.refs_1_ = bf16[384,1024]{1,0:T(8,128)(2,1)S(1)} collective-permute-done((bf16[384,1024]{1,0:T(8,128)(2,1)S(1)}, bf16[384,1024]{1,0:T(8,128)(2,1)S(1)}, u32[]{:S(2)}, u32[]{:S(2)}) %collective-permute-start.24) | collective-permute-done | bytes 786464 | tf_op jit(solution)/shard_map/ppermute | solution.py:442
  124.7 1.3 shard_map.187
  126.1 1.7 %shard_map.188 = (bf16[384,512]{1,0:T(8,128)(2,1)S(1)}, f32[1,512]{1,0:T(1,128)S(1)}, f32[1,512]{1,0:T(1,128)S(1)}, f32[264,512]{1,0:T(8,128)S(1)}, f32[256,512]{1,0:T(8,128)S(1)}) custom-call(s32[2]{0:T(128)S(1)} %pad_add_fusion.place, bf16[384,1024]{1,0:T(8,128)(2,1)S(1)} %get-tuple-element.80.refs_0_.refs_3_, f32[384,512]{1,0:T(8,128)S(1)} %get-tuple-element.82.refs_1_, ...), custom_call_target="tpu_custom_call" | custom-call | flops 10000000000 | bytes 1 | tf_op jit(solution)/shard_map/pallas_call | solution.py:121
  128.9 1.2 shard_map.189
  130.1 0.7 collective-permute-start.35
  130.8 2.5 %shard_map.190 = (bf16[384,512]{1,0:T(8,128)(2,1)}, f32[512,512]{1,0:T(8,128)S(1)}, f32[512,512]{1,0:T(8,128)S(1)}, f32[512,512]{1,0:T(8,128)S(1)}, f32[256,512]{1,0:T(8,128)S(1)}, /*index=5*/f32[256,512]{1,0:T(8,128)S(1)}) custom-call(s32[2]{0:T(128)S(1)} %pad_add_fusion.place, bf16[2048,384]{1,0:T(8,128)(2,1)S(1)} %shard_map.183.refs_7_.refs_0_, ...), custom_call_target="tpu_custom_call" | custom-call | flops 1 | bytes 1 | tf_op jit(solution)/shard_map/pallas_call | solution.py:121
  133.9 0.8 shard_map.191
  134.9 1.4 collective-permute-start.32
  136.4 3.2 %collective-permute-done.35 = f16[272,512]{1,0:T(8,128)(2,1)S(1)} collective-permute-done((f16[272,512]{1,0:T(8,128)(2,1)S(1)}, f16[272,512]{1,0:T(8,128)(2,1)S(1)}, u32[]{:S(2)}, u32[]{:S(2)}) %collective-permute-start.35) | collective-permute-done | bytes 278560 | tf_op jit(solution)/shard_map/ppermute | solution.py:446
  139.9 2.9 %shard_map.193 = (f32[512,512]{1,0:T(8,128)}, f32[512,512]{1,0:T(8,128)}, f32[512,512]{1,0:T(8,128)}) custom-call(s32[2]{0:T(128)S(1)} %pad_add_fusion.place, f32[512,512]{1,0:T(8,128)S(1)} %copy-done, f32[512,512]{1,0:T(8,128)S(1)} %copy-done.3, f32[512,512]{1,0:T(8,128)S(1)} %copy-done.4, f32[256,512]{1,0:T(8,128)S(1)} %multiply_add_fusion.3.near, ...), custom_call_target="tpu_custom_call" | custom-call | flops 1 | bytes 1 | tf_op jit(solution)/shard_map/pallas_call | solution.py:644
  142.9 7.5 %collective-permute-done.32 = f16[528,512]{1,0:T(8,128)(2,1)S(1)} collective-permute-done((f16[528,512]{1,0:T(8,128)(2,1)S(1)}, f16[528,512]{1,0:T(8,128)(2,1)S(1)}, u32[]{:S(2)}, u32[]{:S(2)}) %collective-permute-start.32) | collective-permute-done | bytes 540704 | tf_op jit(solution)/shard_map/ppermute | solution.py:446
  150.5 1.1 shard_map.192
  151.6 2.3 %divide_subtract_fusion = (f32[512,512]{1,0:T(8,128)}, f32[512,512]{1,0:T(8,128)}, f32[512,512]{1,0:T(8,128)}) fusion(f32[512,512]{1,0:T(8,128)S(1)} %copy-done.2, f32[512]{0:T(512)S(1)} %bitcast.15, f16[528,512]{1,0:T(8,128)(2,1)S(1)} %collective-permute-done.32, f32[512,512]{1,0:T(8,128)S(1)} %get-tuple-element.97, ...), kind=kLoop, calls=%fused_computation.2 | loop fusion | flops 4194304 | bytes 8914944 | tf_op jit(solution)/shard_map/sub | solution.py:28
  (77 shorter events, 9.0 us)
Async XLA Ops:
  0.6 23.0 %copy-start = (f32[512,512]{1,0:T(8,128)S(1)}, f32[512,512]{1,0:T(8,128)}, u32[]{:S(2)}) copy-start(f32[512,512]{1,0:T(8,128)} %param.20) | copy-start | bytes 3145732
  0.7 1.3 copy-start.1
  2.0 0.7 copy-start.6
  2.7 3.7 %copy-start.5 = (bf16[384,512]{1,0:T(8,128)(2,1)S(1)}, bf16[384,512]{1,0:T(8,128)(2,1)}, u32[]{:S(2)}) copy-start(bf16[384,512]{1,0:T(8,128)(2,1)} %refs_0_.5) | copy-start | bytes 1179652
  3.3 20.3 %collective-permute-start.5 = (bf16[528,512]{1,0:T(8,128)(2,1)S(1)}, bf16[528,512]{1,0:T(8,128)(2,1)S(1)}, u32[]{:S(2)}, u32[]{:S(2)}) collective-permute-start(bf16[528,512]{1,0:T(8,128)(2,1)S(1)} %shard_map.178.refs_6_), channel_id=1, source_target_pairs={{0,1},{1,0},{2,3},{3,2},{4,5},{5,4},{6,7},{7,6},{8,9},{9,8},{10,11... | collective-permute-start | bytes 1622024 | tf_op jit(solution)/shard_map/ppermute | solution.py:446
  3.8 20.5 %collective-permute-start.6 = (bf16[528,512]{1,0:T(8,128)(2,1)S(1)}, bf16[528,512]{1,0:T(8,128)(2,1)S(1)}, u32[]{:S(2)}, u32[]{:S(2)}) collective-permute-start(bf16[528,512]{1,0:T(8,128)(2,1)S(1)} %shard_map.178.refs_6_), channel_id=1, source_target_pairs={{0,2},{1,3},{2,0},{3,1},{4,6},{5,7},{6,4},{7,5},{8,10},{9,11},{10,... | collective-permute-start | bytes 1622024 | tf_op jit(solution)/shard_map/ppermute | solution.py:446
  6.4 13.1 %collective-permute-start.1 = (bf16[384,512]{1,0:T(8,128)(2,1)S(1)}, bf16[384,512]{1,0:T(8,128)(2,1)S(1)}, u32[]{:S(2)}, u32[]{:S(2)}) collective-permute-start(bf16[384,512]{1,0:T(8,128)(2,1)S(1)} %copy-done.5), channel_id=1, source_target_pairs={{4,0},{8,4},{12,8},{5,1},{9,5},{13,9},{6,2},{10,6},{14,10},{7,3},{... | collective-permute-start | bytes 1179656 | tf_op jit(solution)/shard_map/ppermute | solution.py:442
  7.7 14.1 %collective-permute-start = (bf16[384,512]{1,0:T(8,128)(2,1)S(1)}, bf16[384,512]{1,0:T(8,128)(2,1)S(1)}, u32[]{:S(2)}, u32[]{:S(2)}) collective-permute-start(bf16[384,512]{1,0:T(8,128)(2,1)S(1)} %copy-done.5), channel_id=1, source_target_pairs={{0,4},{4,8},{8,12},{1,5},{5,9},{9,13},{2,6},{6,10},{10,14},{3,7},{... | collective-permute-start | bytes 1179656 | tf_op jit(solution)/shard_map/ppermute | solution.py:442
  12.2 16.9 %collective-permute-start.2 = (bf16[384,512]{1,0:T(8,128)(2,1)S(1)}, bf16[384,512]{1,0:T(8,128)(2,1)S(1)}, u32[]{:S(2)}, u32[]{:S(2)}) collective-permute-start(bf16[384,512]{1,0:T(8,128)(2,1)S(1)} %copy-done.5), channel_id=1, source_target_pairs={{0,8},{12,4},{1,9},{13,5},{2,10},{14,6},{3,11},{15,7},{16,24},{28,... | collective-permute-start | bytes 1179656 | tf_op jit(solution)/shard_map/ppermute | solution.py:442
  22.3 14.0 %collective-permute-start.3 = (bf16[384,512]{1,0:T(8,128)(2,1)S(1)}, bf16[384,512]{1,0:T(8,128)(2,1)S(1)}, u32[]{:S(2)}, u32[]{:S(2)}) collective-permute-start(bf16[384,512]{1,0:T(8,128)(2,1)S(1)} %shard_map.177), channel_id=1, source_target_pairs={{4,0},{8,12},{5,1},{9,13},{6,2},{10,14},{7,3},{11,15},{20,16},{24,... | collective-permute-start | bytes 1179656 | tf_op jit(solution)/shard_map/ppermute | solution.py:442
  24.3 25.0 %collective-permute-start.11 = (bf16[528,512]{1,0:T(8,128)(2,1)S(1)}, bf16[528,512]{1,0:T(8,128)(2,1)S(1)}, u32[]{:S(2)}, u32[]{:S(2)}) collective-permute-start(bf16[528,512]{1,0:T(8,128)(2,1)S(1)} %shard_map.179.refs_0_.refs_4_.refs_3_), channel_id=1, source_target_pairs={{0,2},{1,3},{2,0},{3,1},{4,6},{5,7},{6,4},{7,5},{8,10},{9,11},{10,... | collective-permute-start | bytes 1622024 | tf_op jit(solution)/shard_map/ppermute | solution.py:446
  29.1 16.4 %collective-permute-start.4 = (bf16[384,512]{1,0:T(8,128)(2,1)S(1)}, bf16[384,512]{1,0:T(8,128)(2,1)S(1)}, u32[]{:S(2)}, u32[]{:S(2)}) collective-permute-start(bf16[384,512]{1,0:T(8,128)(2,1)S(1)} %collective-permute-done.2.refs_3_), channel_id=1, source_target_pairs={{4,0},{8,12},{5,1},{9,13},{6,2},{10,14},{7,3},{11,15},{20,16},{24,... | collective-permute-start | bytes 1179656 | tf_op jit(solution)/shard_map/ppermute | solution.py:442
  31.0 14.6 %collective-permute-start.7 = (bf16[256,512]{1,0:T(8,128)(2,1)S(1)}, bf16[256,512]{1,0:T(8,128)(2,1)S(1)}, u32[]{:S(2)}, u32[]{:S(2)}) collective-permute-start(bf16[256,512]{1,0:T(8,128)(2,1)S(1)} %get-tuple-element.63), channel_id=1, source_target_pairs={{0,4},{4,8},{1,5},{5,9},{2,6},{6,10},{3,7},{7,11},{16,20},{20,24},... | collective-permute-start | bytes 786440 | tf_op jit(solution)/shard_map/ppermute | solution.py:442
  35.6 10.0 %collective-permute-start.8 = (bf16[256,512]{1,0:T(8,128)(2,1)S(1)}, bf16[256,512]{1,0:T(8,128)(2,1)S(1)}, u32[]{:S(2)}, u32[]{:S(2)}) collective-permute-start(bf16[256,512]{1,0:T(8,128)(2,1)S(1)} %get-tuple-element.64), channel_id=1, source_target_pairs={{8,4},{12,8},{9,5},{13,9},{10,6},{14,10},{11,7},{15,11},{24,20},{2... | collective-permute-start | bytes 786440 | tf_op jit(solution)/shard_map/ppermute | solution.py:442
  36.3 13.0 %collective-permute-start.9 = (bf16[256,512]{1,0:T(8,128)(2,1)S(1)}, bf16[256,512]{1,0:T(8,128)(2,1)S(1)}, u32[]{:S(2)}, u32[]{:S(2)}) collective-permute-start(bf16[256,512]{1,0:T(8,128)(2,1)S(1)} %get-tuple-element.65), channel_id=1, source_target_pairs={{0,8},{12,4},{1,9},{13,5},{2,10},{14,6},{3,11},{15,7},{16,24},{28,... | collective-permute-start | bytes 786440 | tf_op jit(solution)/shard_map/ppermute | solution.py:442
  45.5 5.7 %collective-permute-start.12 = (bf16[528,512]{1,0:T(8,128)(2,1)S(1)}, bf16[528,512]{1,0:T(8,128)(2,1)S(1)}, u32[]{:S(2)}, u32[]{:S(2)}) collective-permute-start(bf16[528,512]{1,0:T(8,128)(2,1)S(1)} %shard_map.179.refs_0_.refs_4_.refs_3_), channel_id=1, source_target_pairs={{0,1},{1,0},{2,3},{3,2},{4,5},{5,4},{6,7},{7,6},{8,9},{9,8},{10,11... | collective-permute-start | bytes 1622024 | tf_op jit(solution)/shard_map/ppermute | solution.py:446
  49.3 1.9 %collective-permute-start.10 = (bf16[528,512]{1,0:T(8,128)(2,1)S(1)}, bf16[528,512]{1,0:T(8,128)(2,1)S(1)}, u32[]{:S(2)}, u32[]{:S(2)}) collective-permute-start(bf16[528,512]{1,0:T(8,128)(2,1)S(1)} %collective-permute-done.6.refs_8_), channel_id=1, source_target_pairs={{0,1},{1,0},{2,3},{3,2},{4,5},{5,4},{6,7},{7,6},{8,9},{9,8},{10,11... | collective-permute-start | bytes 1622024 | tf_op jit(solution)/shard_map/ppermute | solution.py:446
  49.3 2.7 %collective-permute-start.13 = (bf16[528,512]{1,0:T(8,128)(2,1)S(1)}, bf16[528,512]{1,0:T(8,128)(2,1)S(1)}, u32[]{:S(2)}, u32[]{:S(2)}) collective-permute-start(bf16[528,512]{1,0:T(8,128)(2,1)S(1)} %collective-permute-done.11.refs_3_.refs_6_.refs_5_), channel_id=1, source_target_pairs={{0,1},{1,0},{2,3},{3,2},{4,5},{5,4},{6,7},{7,6},{8,9},{9,8},{10,11... | collective-permute-start | bytes 1622024 | tf_op jit(solution)/shard_map/ppermute | solution.py:446
  50.4 15.3 %collective-permute-start.19 = (bf16[384,512]{1,0:T(8,128)(2,1)S(1)}, bf16[384,512]{1,0:T(8,128)(2,1)S(1)}, u32[]{:S(2)}, u32[]{:S(2)}) collective-permute-start(bf16[384,512]{1,0:T(8,128)(2,1)S(1)} %get-tuple-element.72.refs_10_.refs_8_), channel_id=1, source_target_pairs={{4,6},{5,7},{6,4},{7,5},{8,10},{9,11},{10,8},{11,9},{20,22},{21,23... | collective-permute-start | bytes 1179656 | tf_op jit(solution)/shard_map/ppermute | solution.py:446
  53.8 16.7 %collective-permute-start.16 = (bf16[384,512]{1,0:T(8,128)(2,1)S(1)}, bf16[384,512]{1,0:T(8,128)(2,1)S(1)}, u32[]{:S(2)}, u32[]{:S(2)}) collective-permute-start(bf16[384,512]{1,0:T(8,128)(2,1)S(1)} %get-tuple-element.71.refs_0_.refs_2_.refs_4_), channel_id=1, source_target_pairs={{0,8},{12,4},{1,9},{13,5},{2,10},{14,6},{3,11},{15,7},{16,24},{28,... | collective-permute-start | bytes 1179656 | tf_op jit(solution)/shard_map/ppermute | solution.py:442
  61.0 10.2 %collective-permute-start.20 = (bf16[384,512]{1,0:T(8,128)(2,1)S(1)}, bf16[384,512]{1,0:T(8,128)(2,1)S(1)}, u32[]{:S(2)}, u32[]{:S(2)}) collective-permute-start(bf16[384,512]{1,0:T(8,128)(2,1)S(1)} %get-tuple-element.73.refs_11_.refs_9_), channel_id=1, source_target_pairs={{4,6},{5,7},{6,4},{7,5},{8,10},{9,11},{10,8},{11,9},{20,22},{21,23... | collective-permute-start | bytes 1179656 | tf_op jit(solution)/shard_map/ppermute | solution.py:446
  61.7 10.2 %collective-permute-start.15 = (bf16[384,512]{1,0:T(8,128)(2,1)S(1)}, bf16[384,512]{1,0:T(8,128)(2,1)S(1)}, u32[]{:S(2)}, u32[]{:S(2)}) collective-permute-start(bf16[384,512]{1,0:T(8,128)(2,1)S(1)} %get-tuple-element.71.refs_0_.refs_2_.refs_4_), channel_id=1, source_target_pairs={{8,4},{12,8},{9,5},{13,9},{10,6},{14,10},{11,7},{15,11},{24,20},{2... | collective-permute-start | bytes 1179656 | tf_op jit(solution)/shard_map/ppermute | solution.py:442
  62.4 15.3 %collective-permute-start.14 = (bf16[384,512]{1,0:T(8,128)(2,1)S(1)}, bf16[384,512]{1,0:T(8,128)(2,1)S(1)}, u32[]{:S(2)}, u32[]{:S(2)}) collective-permute-start(bf16[384,512]{1,0:T(8,128)(2,1)S(1)} %get-tuple-element.71.refs_0_.refs_2_.refs_4_), channel_id=1, source_target_pairs={{0,4},{4,8},{1,5},{5,9},{2,6},{6,10},{3,7},{7,11},{16,20},{20,24},... | collective-permute-start | bytes 1179656 | tf_op jit(solution)/shard_map/ppermute | solution.py:442
  65.7 12.0 %collective-permute-start.17 = (bf16[384,512]{1,0:T(8,128)(2,1)S(1)}, bf16[384,512]{1,0:T(8,128)(2,1)S(1)}, u32[]{:S(2)}, u32[]{:S(2)}) collective-permute-start(bf16[384,512]{1,0:T(8,128)(2,1)S(1)} %get-tuple-element.72.refs_10_.refs_8_), channel_id=1, source_target_pairs={{4,5},{5,4},{6,7},{7,6},{8,9},{9,8},{10,11},{11,10},{20,21},{21,20... | collective-permute-start | bytes 1179656 | tf_op jit(solution)/shard_map/ppermute | solution.py:446
  70.5 7.2 %collective-permute-start.18 = (bf16[384,512]{1,0:T(8,128)(2,1)S(1)}, bf16[384,512]{1,0:T(8,128)(2,1)S(1)}, u32[]{:S(2)}, u32[]{:S(2)}) collective-permute-start(bf16[384,512]{1,0:T(8,128)(2,1)S(1)} %get-tuple-element.73.refs_11_.refs_9_), channel_id=1, source_target_pairs={{4,5},{5,4},{6,7},{7,6},{8,9},{9,8},{10,11},{11,10},{20,21},{21,20... | collective-permute-start | bytes 1179656 | tf_op jit(solution)/shard_map/ppermute | solution.py:446
  71.2 6.5 %collective-permute-start.21 = (bf16[384,512]{1,0:T(8,128)(2,1)S(1)}, bf16[384,512]{1,0:T(8,128)(2,1)S(1)}, u32[]{:S(2)}, u32[]{:S(2)}) collective-permute-start(bf16[384,512]{1,0:T(8,128)(2,1)S(1)} %collective-permute-done.19.refs_12_), channel_id=1, source_target_pairs={{4,5},{5,4},{6,7},{7,6},{8,9},{9,8},{10,11},{11,10},{20,21},{21,20... | collective-permute-start | bytes 1179656 | tf_op jit(solution)/shard_map/ppermute | solution.py:446
  71.9 5.8 %collective-permute-start.22 = (bf16[384,512]{1,0:T(8,128)(2,1)S(1)}, bf16[384,512]{1,0:T(8,128)(2,1)S(1)}, u32[]{:S(2)}, u32[]{:S(2)}) collective-permute-start(bf16[384,512]{1,0:T(8,128)(2,1)S(1)} %collective-permute-done.20.refs_13_), channel_id=1, source_target_pairs={{4,5},{5,4},{6,7},{7,6},{8,9},{9,8},{10,11},{11,10},{20,21},{21,20... | collective-permute-start | bytes 1179656 | tf_op jit(solution)/shard_map/ppermute | solution.py:446
  80.1 24.6 %collective-permute-start.25 = (bf16[384,1024]{1,0:T(8,128)(2,1)S(1)}, bf16[384,1024]{1,0:T(8,128)(2,1)S(1)}, u32[]{:S(2)}, u32[]{:S(2)}) collective-permute-start(bf16[384,1024]{1,0:T(8,128)(2,1)S(1)} %shard_map.184.refs_0_), channel_id=1, source_target_pairs={{4,0},{8,12},{5,1},{9,13},{6,2},{10,14},{7,3},{11,15},{20,16},{24,... | collective-permute-start | bytes 2359304 | tf_op jit(solution)/shard_map/ppermute | solution.py:442
  81.4 23.3 %collective-permute-start.23 = (bf16[384,1024]{1,0:T(8,128)(2,1)S(1)}, bf16[384,1024]{1,0:T(8,128)(2,1)S(1)}, u32[]{:S(2)}, u32[]{:S(2)}) collective-permute-start(bf16[384,1024]{1,0:T(8,128)(2,1)S(1)} %shard_map.184.refs_0_), channel_id=1, source_target_pairs={{4,8},{8,4},{5,9},{9,5},{6,10},{10,6},{7,11},{11,7},{20,24},{24,20... | collective-permute-start | bytes 2359304 | tf_op jit(solution)/shard_map/ppermute | solution.py:442
  82.1 42.6 %collective-permute-start.24 = (bf16[384,1024]{1,0:T(8,128)(2,1)S(1)}, bf16[384,1024]{1,0:T(8,128)(2,1)S(1)}, u32[]{:S(2)}, u32[]{:S(2)}) collective-permute-start(bf16[384,1024]{1,0:T(8,128)(2,1)S(1)} %shard_map.184.refs_0_), channel_id=1, source_target_pairs={{8,0},{4,12},{9,1},{5,13},{10,2},{6,14},{11,3},{7,15},{24,16},{20,... | collective-permute-start | bytes 2359304 | tf_op jit(solution)/shard_map/ppermute | solution.py:442
  106.5 2.0 %collective-permute-start.26 = (f32[264,512]{1,0:T(8,128)S(1)}, f32[264,512]{1,0:T(8,128)S(1)}, u32[]{:S(2)}, u32[]{:S(2)}) collective-permute-start(f32[264,512]{1,0:T(8,128)S(1)} %get-tuple-element.78), channel_id=1, source_target_pairs={{0,1},{1,0},{2,3},{3,2},{4,5},{5,4},{6,7},{7,6},{8,9},{9,8},{10,11... | collective-permute-start | bytes 1622024 | tf_op jit(solution)/shard_map/ppermute | solution.py:446
  109.2 16.9 %collective-permute-start.27 = (f16[272,512]{1,0:T(8,128)(2,1)S(1)}, f16[272,512]{1,0:T(8,128)(2,1)S(1)}, u32[]{:S(2)}, u32[]{:S(2)}) collective-permute-start(f16[272,512]{1,0:T(8,128)(2,1)S(1)} %convert_element_type.25), channel_id=1, source_target_pairs={{0,2},{1,3},{2,0},{3,1},{4,6},{5,7},{6,4},{7,5},{8,10},{9,11},{10,... | collective-permute-start | bytes 835592 | tf_op jit(solution)/shard_map/ppermute | solution.py:446
  126.0 2.9 %collective-permute-start.28 = (f32[256,512]{1,0:T(8,128)S(1)}, f32[256,512]{1,0:T(8,128)S(1)}, u32[]{:S(2)}, u32[]{:S(2)}) collective-permute-start(f32[256,512]{1,0:T(8,128)S(1)} %get-tuple-element.87), channel_id=1, source_target_pairs={{0,1},{1,0},{2,3},{3,2},{4,5},{5,4},{6,7},{7,6},{8,9},{9,8},{10,11... | collective-permute-start | bytes 1572872 | tf_op jit(solution)/shard_map/ppermute | solution.py:446
  127.8 6.1 %collective-permute-start.29 = (f32[264,512]{1,0:T(8,128)S(1)}, f32[264,512]{1,0:T(8,128)S(1)}, u32[]{:S(2)}, u32[]{:S(2)}) collective-permute-start(f32[264,512]{1,0:T(8,128)S(1)} %get-tuple-element.92), channel_id=1, source_target_pairs={{0,1},{1,0},{2,3},{3,2},{4,5},{5,4},{6,7},{7,6},{8,9},{9,8},{10,11... | collective-permute-start | bytes 1622024 | tf_op jit(solution)/shard_map/ppermute | solution.py:446
  128.4 5.0 %collective-permute-start.30 = (f32[256,512]{1,0:T(8,128)S(1)}, f32[256,512]{1,0:T(8,128)S(1)}, u32[]{:S(2)}, u32[]{:S(2)}) collective-permute-start(f32[256,512]{1,0:T(8,128)S(1)} %get-tuple-element.93), channel_id=1, source_target_pairs={{0,1},{1,0},{2,3},{3,2},{4,5},{5,4},{6,7},{7,6},{8,9},{9,8},{10,11... | collective-permute-start | bytes 1572872 | tf_op jit(solution)/shard_map/ppermute | solution.py:446
  128.4 7.8 %collective-permute-start.33 = (f32[256,512]{1,0:T(8,128)S(1)}, f32[256,512]{1,0:T(8,128)S(1)}, u32[]{:S(2)}, u32[]{:S(2)}) collective-permute-start(f32[256,512]{1,0:T(8,128)S(1)} %get-tuple-element.106), channel_id=1, source_target_pairs={{0,1},{1,0},{2,3},{3,2},{4,5},{5,4},{6,7},{7,6},{8,9},{9,8},{10,11... | collective-permute-start | bytes 1572872 | tf_op jit(solution)/shard_map/ppermute | solution.py:446
  130.1 9.6 %collective-permute-start.35 = (f16[272,512]{1,0:T(8,128)(2,1)S(1)}, f16[272,512]{1,0:T(8,128)(2,1)S(1)}, u32[]{:S(2)}, u32[]{:S(2)}) collective-permute-start(f16[272,512]{1,0:T(8,128)(2,1)S(1)} %convert_element_type.31), channel_id=1, source_target_pairs={{0,2},{1,3},{2,0},{3,1},{4,6},{5,7},{6,4},{7,5},{8,10},{9,11},{10,... | collective-permute-start | bytes 835592 | tf_op jit(solution)/shard_map/ppermute | solution.py:446
  133.3 6.4 %collective-permute-start.34 = (f32[256,512]{1,0:T(8,128)S(1)}, f32[256,512]{1,0:T(8,128)S(1)}, u32[]{:S(2)}, u32[]{:S(2)}) collective-permute-start(f32[256,512]{1,0:T(8,128)S(1)} %get-tuple-element.108), channel_id=1, source_target_pairs={{0,1},{1,0},{2,3},{3,2},{4,5},{5,4},{6,7},{7,6},{8,9},{9,8},{10,11... | collective-permute-start | bytes 1572872 | tf_op jit(solution)/shard_map/ppermute | solution.py:446
  133.4 18.2 %collective-permute-start.31 = (f32[512,512]{1,0:T(8,128)S(1)}, f32[512,512]{1,0:T(8,128)S(1)}, u32[]{:S(2)}, u32[]{:S(2)}) collective-permute-start(f32[512,512]{1,0:T(8,128)S(1)} %get-tuple-element.98), channel_id=1, source_target_pairs={{0,1},{1,0},{2,3},{3,2},{4,5},{5,4},{6,7},{7,6},{8,9},{9,8},{10,11... | collective-permute-start | bytes 3145736 | tf_op jit(solution)/shard_map/ppermute | solution.py:446
  134.9 15.5 %collective-permute-start.32 = (f16[528,512]{1,0:T(8,128)(2,1)S(1)}, f16[528,512]{1,0:T(8,128)(2,1)S(1)}, u32[]{:S(2)}, u32[]{:S(2)}) collective-permute-start(f16[528,512]{1,0:T(8,128)(2,1)S(1)} %convert_element_type.26), channel_id=1, source_target_pairs={{0,2},{1,3},{2,0},{3,1},{4,6},{5,7},{6,4},{7,5},{8,10},{9,11},{10,... | collective-permute-start | bytes 1622024 | tf_op jit(solution)/shard_map/ppermute | solution.py:446
  136.3 3.6 %copy-start.3 = (f32[512,512]{1,0:T(8,128)S(1)}, f32[512,512]{1,0:T(8,128)}, u32[]{:S(2)}) copy-start(f32[512,512]{1,0:T(8,128)} %moment) | copy-start | bytes 3145732
  136.3 3.6 %copy-start.4 = (f32[512,512]{1,0:T(8,128)S(1)}, f32[512,512]{1,0:T(8,128)}, u32[]{:S(2)}) copy-start(f32[512,512]{1,0:T(8,128)} %square) | copy-start | bytes 3145732
  139.9 10.6 %copy-start.7 = (f32[128]{0:T(128)S(1)}, f32[128]{0:T(128)}, u32[]{:S(2)}) copy-start(f32[128]{0:T(128)} %param.12) | copy-start | bytes 1540
  139.9 10.6 %copy-start.8 = (f32[128]{0:T(128)S(1)}, f32[128]{0:T(128)}, u32[]{:S(2)}) copy-start(f32[128]{0:T(128)} %param.16) | copy-start | bytes 1540
  139.9 10.5 %copy-start.9 = (f32[128]{0:T(128)S(1)}, f32[128]{0:T(128)}, u32[]{:S(2)}) copy-start(f32[128]{0:T(128)} %param.17) | copy-start | bytes 1540
  139.9 11.6 %copy-start.2 = (f32[512,512]{1,0:T(8,128)S(1)}, f32[512,512]{1,0:T(8,128)}, u32[]{:S(2)}) copy-start(f32[512,512]{1,0:T(8,128)} %refs_0_.3) | copy-start | bytes 3145732
  139.9 11.6 %copy-start.10 = (f32[512,512]{1,0:T(8,128)S(1)}, f32[512,512]{1,0:T(8,128)}, u32[]{:S(2)}) copy-start(f32[512,512]{1,0:T(8,128)} %param.14) | copy-start | bytes 3145732
  139.9 11.6 %copy-start.11 = (f32[512,512]{1,0:T(8,128)S(1)}, f32[512,512]{1,0:T(8,128)}, u32[]{:S(2)}) copy-start(f32[512,512]{1,0:T(8,128)} %param.15) | copy-start | bytes 3145732

commit v12 on v9

--- a/solution.py
+++ b/solution.py
@@ -167,40 +167,9 @@
     out[depth:] = three_rows(jnp.sum(value * value, axis=0, keepdims=True))
 
 
-def codes_body(
-    place,
-    own,
-    low,
-    high,
-    across,
-    relay1,
-    relay2,
-    enc0,
-    enc1,
-    enc2,
-    enc3,
-    codes,
-    mask,
-    full,
-    active,
-    bias,
-):
-    z, i = place[0], place[1]
-    width = own.shape[1]
-    for at, blocks in enumerate(
-        (
-            (own, high, relay1, relay2),
-            (low, own, high, across),
-            (across, low, own, high),
-            (relay2, relay1, low, own),
-        )
-    ):
-
-        @pl.when(z == at)
-        def _(blocks=blocks):
-            for b, block in enumerate(blocks):
-                full[:, b * width : (b + 1) * width] = block[...]
-
+def codes_body(place, full, enc0, enc1, enc2, enc3, codes, mask, active, bias):
+    i = place[1]
+    width = full.shape[1] // 4
     total = jnp.zeros(codes.shape, F32)
     piece = codes.shape[1] // 4
     for t, enc in enumerate((enc0, enc1, enc2, enc3)):
@@ -216,16 +185,6 @@
     active[...] = jnp.sum(low_codes.astype(F32), axis=0, keepdims=True)
 
 
-def onward_body(place, low, high, out):
-    @pl.when(place[0] == 1)
-    def _():
-        out[...] = high[...]
-
-    @pl.when(place[0] != 1)
-    def _():
-        out[...] = low[...]
-
-
 def pieces_body(place, dec, up, down, across):
     z = place[0]
     half = up.shape[0]
@@ -233,22 +192,27 @@
         out[...] = dec[pl.ds(pl.multiple_of(jnp.where(second, half, 0), half), half), :]
 
 
+def stack_body(place, *refs):
+    *pieces, out = refs
+    size = pieces[0].shape[0]
+    for k, piece in enumerate(pieces):
+        out[k * size : (k + 1) * size] = piece[...]
+
+
 def turn_body(place, full, turned):
     turned[...] = full[...].T
 
 
-def error_body(
-    place, own, low, high, across, dec0, dec1, dec2, dec3, row0, row1, row2, row3, inputs, error
-):
+def error_body(place, own, low, high, across, dec0, dec1, dec2, dec3, *refs):
+    *rows, inputs, error = refs
     z, i = place[0], place[1]
-    half = row0.shape[0] // 3
+    half = rows[0].shape[0] // 3
     shift = pl.multiple_of(jnp.where(z >= 2, half, 0), half)
-    for t in range(4):
-        dec, row = (dec0, dec1, dec2, dec3)[t], (row0, row1, row2, row3)[t]
+    for t, dec in enumerate((dec0, dec1, dec2, dec3)):
         lefts = (own, low, high, across)
-        rights = [dec[pl.ds(shift, half), :]] + [row[m * half : (m + 1) * half, :] for m in range(3)]
+        rights = [rows[t][m * half : (m + 1) * half, :] for m in range(3)]
         total = jnp.zeros((own.shape[0], half), F32)
-        for left, right in zip(lefts, rights):
+        for left, right in zip(lefts, [dec[pl.ds(shift, half), :]] + rights):
             total += lax.dot_general(
                 left[...], right, (((1,), (1,)), ((), ())), preferred_element_type=F32
             )
@@ -435,62 +399,47 @@
         pairs = [(4 * p + k, 4 * p + (k ^ bits)) for p in planes for k in range(4)]
         return lax.ppermute(value, ("latent", "dp"), pairs)
 
-    ends = [(1, 0), (2, 3)]
-    low = along(activations, [(0, 1), (1, 2), (2, 3)])
-    high = along(activations, [(1, 0), (2, 1), (3, 2)])
-    across = along(activations, [(0, 2), (3, 1)])
-
+    inputs = lax.all_gather(activations, "latent", axis=1, tiled=True)
+
+    (dec_own,) = local_kernel(
+        decoder_body, [shape((width + EXTRA, latents), BF16)], place, decoder
+    )
+    pieces = local_kernel(pieces_body, [shape((half, latents), BF16)] * 3, place, dec_own)
+    dec_pieces = [
+        along(pieces[0], [(0, 1), (1, 2)]),
+        along(pieces[1], [(2, 1), (3, 2)]),
+        along(pieces[2], [(0, 2), (3, 1)]),
+    ]
     (enc_own,) = local_kernel(
         encoder_body,
         [shape((width + EXTRA, latents), BF16)],
         place,
         encoder,
         enc_bias.reshape(1, -1),
+        after=(pieces[0],),
     )
     enc_chip, enc_core = flip(enc_own, 2), flip(enc_own, 1)
-    (dec_own,) = local_kernel(
-        decoder_body,
-        [shape((width + EXTRA, latents), BF16)],
-        place,
-        decoder,
-        after=(enc_core,),
-    )
-    dec_chip, dec_core = flip(dec_own, 2), flip(dec_own, 1)
-    (onward,) = local_kernel(
-        onward_body, [shape((count, width), BF16)], place, low, high
-    )
-    relay1 = along(onward, ends)
-    relay2 = along(across, ends)
-    enc = [enc_own, enc_core, enc_chip, flip(behind(enc_chip, relay2), 1)]
-
-    up, down, beyond = local_kernel(
-        pieces_body, [shape((half, latents), BF16)] * 3, place, dec_own
-    )
-    dec_pieces = [
-        along(up, [(0, 1), (1, 2)]),
-        along(down, [(2, 1), (3, 2)]),
-        along(beyond, [(0, 2), (3, 1)]),
-    ]
+    enc = [enc_own, enc_core, enc_chip, flip(enc_chip, 1)]
+    (rows_own,) = local_kernel(
+        stack_body, [shape((3 * half, latents), BF16)], place, *dec_pieces, after=(enc_chip,)
+    )
+    rows_chip, rows_core = flip(rows_own, 2, (1, 2)), flip(rows_own, 1, (1, 2))
+    dec_late = behind(dec_own, rows_core)
+    dec_chip, dec_core = flip(dec_late, 2), flip(dec_late, 1)
     dec = [dec_own, dec_core, dec_chip, flip(dec_chip, 1)]
-
-    rows_own = jnp.concatenate([behind(piece, dec_chip) for piece in dec_pieces], axis=0)
-    codes, mask, inputs, active = local_kernel(
+    rows_both = flip(rows_chip, 1, (1, 2))
+
+    codes, mask, active = local_kernel(
         codes_body,
         [
             shape((count, latents), BF16),
             shape((count, latents), BF16),
-            shape((count, features), BF16),
             shape((1, latents), F32),
         ],
         place,
-        activations,
-        low,
-        high,
-        across,
-        relay1,
-        relay2,
+        inputs,
         *enc,
-        after=(rows_own,),
+        after=(rows_both,),
         scratch=[pltpu.VMEM((1, latents), F32)],
     )
     codes_low = along(codes, [(0, 1), (1, 2)])
@@ -499,12 +448,6 @@
     (turned,) = local_kernel(
         turn_body, [shape((features, count), BF16)], place, inputs
     )
-    rows_chip = flip(rows_own, 2, (1, 2))
-    rows_core = flip(behind(rows_own, turned), 1, (1, 2))
-    rows_both = flip(
-        behind(rows_chip, codes_low, codes_high, codes_across, dec[1], dec[3]), 1, (1, 2)
-    )
-
     (own_error,) = local_kernel(
         error_body,
         [shape((count, features // 2), BF16)],

time: 150 us -> 198 us (1.32)
  waiting for transfers between devices: 75.2 us -> 93.6 us
  between operations: 1.17 us -> 14.5 us
  local copies, waits for them, and re-layouts: 2.06 us -> 10.2 us
  starting transfers between devices: 46.8 us -> 51.9 us
  Pallas kernels: 21.5 us -> 23.8 us
    ppermute x19, waiting for transfers between devices: 14.5 us -> 23.8 us  [flip(): return lax.ppermute(value, ('latent', 'dp'), pairs)]
    ppermute x14 -> x9, waiting for transfers between devices: 60.8 us -> 69.1 us  [along(): return lax.ppermute(value, 'latent', pairs)]
    unnamed x26 -> x48, local copies, waits for them, and re-layouts: 2.04 us -> 10.2 us
    ppermute x14 -> x9, starting transfers between devices: 37.4 us -> 41.9 us  [along(): return lax.ppermute(value, 'latent', pairs)]
    pallas_call x15, Pallas kernels: 18.6 us -> 20.8 us  [local_kernel(): pl.pallas_call(run, out_shape=outs, in_specs=[SMEM] + [VMEM] * len(args)...]
  transfers between devices with their start and end apart: 33 -> 29, of which waited for: 12 -> 10; matrix products, arithmetic and copies ran while one was open for 0% -> 0% of each run, Pallas kernels for 12% -> 10%
where the time goes in v12:
time: 198 us; the launch traced here: 197 us
  waiting for transfers between devices  93.6 us (47%)
  starting transfers between devices  51.9 us (26%)
  Pallas kernels  23.8 us (12%)
  between operations  14.5 us (7%)
  local copies, waits for them, and re-layouts  10.2 us (5%)
  other arithmetic  2.93 us (1%)
    ppermute x9, waiting for transfers between devices, along(): return lax.ppermute(value, 'latent', pairs)  69.1 us
    ppermute x9, starting transfers between devices, along(): return lax.ppermute(value, 'latent', pairs)  41.9 us
    ppermute x19, waiting for transfers between devices, flip(): return lax.ppermute(value, ('latent', 'dp'), pairs)  23.8 us
    pallas_call x15, Pallas kernels, local_kernel(): pl.pallas_call(run, out_shape=outs, in_specs=[SMEM] + [VMEM] * len(args)...  20.8 us
    unnamed x48, local copies, waits for them, and re-layouts  10.2 us
    ppermute x19, starting transfers between devices, flip(): return lax.ppermute(value, ('latent', 'dp'), pairs)  9.96 us
  transfers between devices with their start and end apart: 29, of which 10 were waited for; matrix products, arithmetic and copies ran while one was open for 0% of the time, Pallas kernels for 10%

profile of v12, /device:TPU:0, one launch (start us, length us, event | category | flops | bytes accessed | tf_op | source)
XLA Modules:
  0.0 196.9 jit_solution(4939235433569240708)
XLA Ops:
  7.2 0.7 all-gather.2.cloned.1.call-update
  8.0 1.2 copy-done.2
  11.1 3.0 %collective-permute-start.1 = (bf16[528,512]{1,0:T(8,128)(2,1)S(1)}, bf16[528,512]{1,0:T(8,128)(2,1)S(1)}, u32[]{:S(2)}, u32[]{:S(2)}) collective-permute-start(bf16[528,512]{1,0:T(8,128)(2,1)S(1)} %shard_map.180.refs_1_), channel_id=1, source_target_pairs={{0,2},{1,3},{2,0},{3,1},{4,6},{5,7},{6,4},{7,5},{8,10},{9,11},{10,... | collective-permute-start | bytes 1622024 | tf_op jit(solution)/shard_map/ppermute | solution.py:400
  14.1 0.7 collective-permute-start.4
  14.8 6.2 %collective-permute-start.5 = (bf16[256,512]{1,0:T(8,128)(2,1)S(1)}, bf16[256,512]{1,0:T(8,128)(2,1)S(1)}, u32[]{:S(2)}, u32[]{:S(2)}) collective-permute-start(bf16[256,512]{1,0:T(8,128)(2,1)S(1)} %get-tuple-element.57), channel_id=1, source_target_pairs={{0,8},{12,4},{1,9},{13,5},{2,10},{14,6},{3,11},{15,7},{16,24},{28,... | collective-permute-start | bytes 786440 | tf_op jit(solution)/shard_map/ppermute | solution.py:396
  21.0 1.3 collective-permute-start.3
  22.3 10.8 %collective-permute-done.5.refs_2_ = bf16[256,512]{1,0:T(8,128)(2,1)S(1)} collective-permute-done((bf16[256,512]{1,0:T(8,128)(2,1)S(1)}, bf16[256,512]{1,0:T(8,128)(2,1)S(1)}, u32[]{:S(2)}, u32[]{:S(2)}) %collective-permute-start.5) | collective-permute-done | bytes 262176 | tf_op jit(solution)/shard_map/ppermute | solution.py:396
  33.1 10.7 %collective-permute-done.3.refs_0_ = bf16[256,512]{1,0:T(8,128)(2,1)S(1)} collective-permute-done((bf16[256,512]{1,0:T(8,128)(2,1)S(1)}, bf16[256,512]{1,0:T(8,128)(2,1)S(1)}, u32[]{:S(2)}, u32[]{:S(2)}) %collective-permute-start.3) | collective-permute-done | bytes 262176 | tf_op jit(solution)/shard_map/ppermute | solution.py:396
  44.4 0.7 collective-permute-start.6
  45.1 0.7 collective-permute-start.11
  45.8 0.7 collective-permute-start.7
  46.6 0.9 copy-done.11
  47.4 0.9 copy-done.13
  48.8 12.2 %collective-permute-done.13.refs_6_.refs_5_ = bf16[528,512]{1,0:T(8,128)(2,1)} collective-permute-done((bf16[528,512]{1,0:T(8,128)(2,1)S(1)}, bf16[528,512]{1,0:T(8,128)(2,1)}, u32[]{:S(2)}, u32[]{:S(2)}) %collective-permute-start.13) | collective-permute-done | bytes 540704 | tf_op jit(solution)/shard_map/ppermute | solution.py:400
  61.0 0.8 copy-done.15
  61.8 0.8 copy-done.17
  62.6 1.4 copy-done
  64.0 1.0 copy-done.6
  65.1 1.0 copy-done.8
  66.1 1.0 copy-done.16
  67.2 1.0 copy-done.18
  68.2 1.6 shard_map.182
  69.8 28.4 %collective-permute-start.10 = (bf16[384,512]{1,0:T(8,128)(2,1)S(1)}, bf16[384,512]{1,0:T(8,128)(2,1)S(1)}, u32[]{:S(2)}, u32[]{:S(2)}) collective-permute-start(bf16[384,512]{1,0:T(8,128)(2,1)S(1)} %get-tuple-element.58.refs_0_.refs_2_.refs_4_), channel_id=1, source_target_pairs={{0,8},{12,4},{1,9},{13,5},{2,10},{14,6},{3,11},{15,7},{16,24},{28,... | collective-permute-start | bytes 1179656 | tf_op jit(solution)/shard_map/ppermute | solution.py:396
  98.3 0.7 collective-permute-start.9
  99.0 1.3 collective-permute-start.8
  100.3 7.4 %collective-permute-done.10.refs_3_ = bf16[384,512]{1,0:T(8,128)(2,1)S(1)} collective-permute-done((bf16[384,512]{1,0:T(8,128)(2,1)S(1)}, bf16[384,512]{1,0:T(8,128)(2,1)S(1)}, u32[]{:S(2)}, u32[]{:S(2)}) %collective-permute-start.10) | collective-permute-done | bytes 393248 | tf_op jit(solution)/shard_map/ppermute | solution.py:396
  107.7 8.0 %collective-permute-done.8.refs_1_ = bf16[384,512]{1,0:T(8,128)(2,1)S(1)} collective-permute-done((bf16[384,512]{1,0:T(8,128)(2,1)S(1)}, bf16[384,512]{1,0:T(8,128)(2,1)S(1)}, u32[]{:S(2)}, u32[]{:S(2)}) %collective-permute-start.8) | collective-permute-done | bytes 393248 | tf_op jit(solution)/shard_map/ppermute | solution.py:396
  115.8 3.3 %shard_map.183.refs_0_ = bf16[384,1024]{1,0:T(8,128)(2,1)S(1)} custom-call(s32[2]{0:T(128)S(1)} %pad_add_fusion.place, bf16[384,512]{1,0:T(8,128)(2,1)S(1)} %get-tuple-element.58.refs_0_.refs_2_.refs_4_, bf16[384,512]{1,0:T(8,128)(2,1)S(1)} %collective-permute-done.8.refs_1_, bf16[384,512]{1,0:T(8,128)(2,1)S(1)} %collective-permute-done.9.refs_2_, ...), custom_call_target="tpu_custom_call" | custom-call | flops 1 | bytes 1 | tf_op jit(solution)/shard_map/pallas_call | solution.py:121
  119.1 1.3 collective-permute-start.17
  120.4 0.7 collective-permute-start.15
  121.1 1.3 collective-permute-start.16
  122.4 17.9 %collective-permute-done.17.refs_1_ = bf16[384,1024]{1,0:T(8,128)(2,1)S(1)} collective-permute-done((bf16[384,1024]{1,0:T(8,128)(2,1)S(1)}, bf16[384,1024]{1,0:T(8,128)(2,1)S(1)}, u32[]{:S(2)}, u32[]{:S(2)}) %collective-permute-start.17) | collective-permute-done | bytes 786464 | tf_op jit(solution)/shard_map/ppermute | solution.py:396
  140.2 2.6 %shard_map.184 = (f32[384,512]{1,0:T(8,128)S(1)}, bf16[384,1024]{1,0:T(8,128)(2,1)S(1)}, f32[264,512]{1,0:T(8,128)S(1)}, f32[256,512]{1,0:T(8,128)S(1)}, f32[256,512]{1,0:T(8,128)S(1)}, /*index=5*/f32[256,512]{1,0:T(8,128)S(1)}) custom-call(s32[2]{0:T(128)S(1)} %pad_add_fusion.place, bf16[384,1024]{1,0:T(8,128)(2,1)S(1)} %shard_map.183.refs_0_, ...), custom_call_target="tpu_custom_call" | custom-call | flops 1 | bytes 1 | tf_op jit(solution)/shard_map/pallas_call | solution.py:121
  142.9 1.0 shard_map.177.refs_7_.refs_0_
  143.9 0.9 collective-permute-done.18.refs_2_
  144.8 0.7 shard_map.185
  146.0 14.3 %collective-permute-done.16.refs_1_ = bf16[384,1024]{1,0:T(8,128)(2,1)S(1)} collective-permute-done((bf16[384,1024]{1,0:T(8,128)(2,1)S(1)}, bf16[384,1024]{1,0:T(8,128)(2,1)S(1)}, u32[]{:S(2)}, u32[]{:S(2)}) %collective-permute-start.16) | collective-permute-done | bytes 786464 | tf_op jit(solution)/shard_map/ppermute | solution.py:396
  160.3 1.1 shard_map.186
  161.4 2.6 %shard_map.187 = (bf16[384,512]{1,0:T(8,128)(2,1)S(1)}, f32[1,512]{1,0:T(1,128)S(1)}, f32[1,512]{1,0:T(1,128)S(1)}, f32[264,512]{1,0:T(8,128)S(1)}, f32[256,512]{1,0:T(8,128)S(1)}) custom-call(s32[2]{0:T(128)S(1)} %pad_add_fusion.place, bf16[384,1024]{1,0:T(8,128)(2,1)S(1)} %get-tuple-element.64.refs_0_.refs_3_, f32[384,512]{1,0:T(8,128)S(1)} %get-tuple-element.66.refs_1_, ...), custom_call_target="tpu_custom_call" | custom-call | flops 10000000000 | bytes 1 | tf_op jit(solution)/shard_map/pallas_call | solution.py:121
  165.1 1.2 shard_map.188
  166.6 2.5 %shard_map.189 = (bf16[384,512]{1,0:T(8,128)(2,1)}, f32[512,512]{1,0:T(8,128)S(1)}, f32[512,512]{1,0:T(8,128)S(1)}, f32[512,512]{1,0:T(8,128)S(1)}, f32[256,512]{1,0:T(8,128)S(1)}, /*index=5*/f32[256,512]{1,0:T(8,128)S(1)}) custom-call(s32[2]{0:T(128)S(1)} %pad_add_fusion.place, bf16[2048,384]{1,0:T(8,128)(2,1)S(1)} %shard_map.177.refs_7_.refs_0_, ...), custom_call_target="tpu_custom_call" | custom-call | flops 1 | bytes 1 | tf_op jit(solution)/shard_map/pallas_call | solution.py:121
  169.8 0.8 shard_map.190
  170.7 1.8 collective-permute-start.24
  172.7 3.2 %collective-permute-done.27 = f16[272,512]{1,0:T(8,128)(2,1)S(1)} collective-permute-done((f16[272,512]{1,0:T(8,128)(2,1)S(1)}, f16[272,512]{1,0:T(8,128)(2,1)S(1)}, u32[]{:S(2)}, u32[]{:S(2)}) %collective-permute-start.27) | collective-permute-done | bytes 278560 | tf_op jit(solution)/shard_map/ppermute | solution.py:400
  176.1 3.0 %shard_map.192 = (f32[512,512]{1,0:T(8,128)}, f32[512,512]{1,0:T(8,128)}, f32[512,512]{1,0:T(8,128)}) custom-call(s32[2]{0:T(128)S(1)} %pad_add_fusion.place, f32[512,512]{1,0:T(8,128)S(1)} %copy-done.3, f32[512,512]{1,0:T(8,128)S(1)} %copy-done.9, f32[512,512]{1,0:T(8,128)S(1)} %copy-done.10, f32[256,512]{1,0:T(8,128)S(1)} %multiply_add_fusion.3.near, ...), custom_call_target="tpu_custom_call" | custom-call | flops 1 | bytes 1 | tf_op jit(solution)/shard_map/pallas_call | solution.py:571
  179.1 7.5 %collective-permute-done.24 = f16[528,512]{1,0:T(8,128)(2,1)S(1)} collective-permute-done((f16[528,512]{1,0:T(8,128)(2,1)S(1)}, f16[528,512]{1,0:T(8,128)(2,1)S(1)}, u32[]{:S(2)}, u32[]{:S(2)}) %collective-permute-start.24) | collective-permute-done | bytes 540704 | tf_op jit(solution)/shard_map/ppermute | solution.py:400
  186.6 1.1 shard_map.191
  187.7 2.3 %divide_subtract_fusion = (f32[512,512]{1,0:T(8,128)}, f32[512,512]{1,0:T(8,128)}, f32[512,512]{1,0:T(8,128)}) fusion(f32[512,512]{1,0:T(8,128)S(1)} %copy-done.4, f32[512]{0:T(512)S(1)} %bitcast.15, f16[528,512]{1,0:T(8,128)(2,1)S(1)} %collective-permute-done.24, f32[512,512]{1,0:T(8,128)S(1)} %get-tuple-element.81, ...), kind=kLoop, calls=%fused_computation.2 | loop fusion | flops 4194304 | bytes 8914944 | tf_op jit(solution)/shard_map/sub | solution.py:28
  (87 shorter events, 6.2 us)
Async XLA Ops:
  7.2 3.3 %copy-start.19 = (f32[128]{0:T(128)S(1)}, f32[128]{0:T(128)}, u32[]{:S(2)}) copy-start(f32[128]{0:T(128)} %param.12) | copy-start | bytes 1540
  7.2 55.4 %all-gather.2.cloned.1.call-start = ((), (), s32[]{:S(2)}) async-start(), calls=%async_computation | async-start | bytes 1966080 | tf_op jit(solution)/shard_map/all_gather | solution.py:402
  8.0 1.2 copy-start.2
  9.2 1.3 copy-start.4
  11.1 49.9 %copy-start.5 = (bf16[528,512]{1,0:T(8,128)(2,1)}, bf16[528,512]{1,0:T(8,128)(2,1)S(1)}, u32[]{:S(2)}) copy-start(bf16[528,512]{1,0:T(8,128)(2,1)S(1)} %shard_map.180.refs_1_) | copy-start | bytes 1622020
  11.1 32.6 %collective-permute-start.1 = (bf16[528,512]{1,0:T(8,128)(2,1)S(1)}, bf16[528,512]{1,0:T(8,128)(2,1)S(1)}, u32[]{:S(2)}, u32[]{:S(2)}) collective-permute-start(bf16[528,512]{1,0:T(8,128)(2,1)S(1)} %shard_map.180.refs_1_), channel_id=1, source_target_pairs={{0,2},{1,3},{2,0},{3,1},{4,6},{5,7},{6,4},{7,5},{8,10},{9,11},{10,... | collective-permute-start | bytes 1622024 | tf_op jit(solution)/shard_map/ppermute | solution.py:400
  14.1 8.2 %collective-permute-start.4 = (bf16[256,512]{1,0:T(8,128)(2,1)S(1)}, bf16[256,512]{1,0:T(8,128)(2,1)S(1)}, u32[]{:S(2)}, u32[]{:S(2)}) collective-permute-start(bf16[256,512]{1,0:T(8,128)(2,1)S(1)} %get-tuple-element.56), channel_id=1, source_target_pairs={{8,4},{12,8},{9,5},{13,9},{10,6},{14,10},{11,7},{15,11},{24,20},{2... | collective-permute-start | bytes 786440 | tf_op jit(solution)/shard_map/ppermute | solution.py:396
  14.8 18.3 %collective-permute-start.5 = (bf16[256,512]{1,0:T(8,128)(2,1)S(1)}, bf16[256,512]{1,0:T(8,128)(2,1)S(1)}, u32[]{:S(2)}, u32[]{:S(2)}) collective-permute-start(bf16[256,512]{1,0:T(8,128)(2,1)S(1)} %get-tuple-element.57), channel_id=1, source_target_pairs={{0,8},{12,4},{1,9},{13,5},{2,10},{14,6},{3,11},{15,7},{16,24},{28,... | collective-permute-start | bytes 786440 | tf_op jit(solution)/shard_map/ppermute | solution.py:396
  21.0 22.8 %collective-permute-start.3 = (bf16[256,512]{1,0:T(8,128)(2,1)S(1)}, bf16[256,512]{1,0:T(8,128)(2,1)S(1)}, u32[]{:S(2)}, u32[]{:S(2)}) collective-permute-start(bf16[256,512]{1,0:T(8,128)(2,1)S(1)} %get-tuple-element.55.refs_2_), channel_id=1, source_target_pairs={{0,4},{4,8},{1,5},{5,9},{2,6},{6,10},{3,7},{7,11},{16,20},{20,24},... | collective-permute-start | bytes 786440 | tf_op jit(solution)/shard_map/ppermute | solution.py:396
  43.8 18.0 %copy-start.7 = (bf16[528,512]{1,0:T(8,128)(2,1)}, bf16[528,512]{1,0:T(8,128)(2,1)S(1)}, u32[]{:S(2)}) copy-start(bf16[528,512]{1,0:T(8,128)(2,1)S(1)} %collective-permute-done.1.refs_3_) | copy-start | bytes 1622020
  44.4 1.4 collective-permute-start.6
  45.1 2.3 %collective-permute-start.11 = (bf16[768,512]{1,0:T(8,128)(2,1)S(1)}, bf16[768,512]{1,0:T(8,128)(2,1)S(1)}, u32[]{:S(2)}, u32[]{:S(2)}) collective-permute-start(bf16[768,512]{1,0:T(8,128)(2,1)S(1)} %shard_map.181.refs_8_), channel_id=1, source_target_pairs={{4,5},{5,4},{6,7},{7,6},{8,9},{9,8},{10,11},{11,10},{20,21},{21,20... | collective-permute-start | bytes 2359304 | tf_op jit(solution)/shard_map/ppermute | solution.py:400
  45.8 16.8 %collective-permute-start.7 = (bf16[768,512]{1,0:T(8,128)(2,1)S(1)}, bf16[768,512]{1,0:T(8,128)(2,1)S(1)}, u32[]{:S(2)}, u32[]{:S(2)}) collective-permute-start(bf16[768,512]{1,0:T(8,128)(2,1)S(1)} %collective-permute-done.6.refs_10_), channel_id=1, source_target_pairs={{4,5},{5,4},{6,7},{7,6},{8,9},{9,8},{10,11},{11,10},{20,21},{21,20... | collective-permute-start | bytes 2359304 | tf_op jit(solution)/shard_map/ppermute | solution.py:400
  48.3 12.7 %collective-permute-start.13 = (bf16[528,512]{1,0:T(8,128)(2,1)S(1)}, bf16[528,512]{1,0:T(8,128)(2,1)}, u32[]{:S(2)}, u32[]{:S(2)}) collective-permute-start(bf16[528,512]{1,0:T(8,128)(2,1)S(1)} %shard_map.178.refs_0_.refs_4_.refs_3_), channel_id=1, source_target_pairs={{0,2},{1,3},{2,0},{3,1},{4,6},{5,7},{6,4},{7,5},{8,10},{9,11},{10,... | collective-permute-start | bytes 1622024 | tf_op jit(solution)/shard_map/ppermute | solution.py:400
  48.3 12.7 %collective-permute-start = (bf16[528,512]{1,0:T(8,128)(2,1)S(1)}, bf16[528,512]{1,0:T(8,128)(2,1)S(1)}, u32[]{:S(2)}, u32[]{:S(2)}) collective-permute-start(bf16[528,512]{1,0:T(8,128)(2,1)S(1)} %shard_map.180.refs_1_), channel_id=1, source_target_pairs={{0,1},{1,0},{2,3},{3,2},{4,5},{5,4},{6,7},{7,6},{8,9},{9,8},{10,11... | collective-permute-start | bytes 1622024 | tf_op jit(solution)/shard_map/ppermute | solution.py:400
  48.3 13.5 %collective-permute-start.2 = (bf16[528,512]{1,0:T(8,128)(2,1)S(1)}, bf16[528,512]{1,0:T(8,128)(2,1)S(1)}, u32[]{:S(2)}, u32[]{:S(2)}) collective-permute-start(bf16[528,512]{1,0:T(8,128)(2,1)S(1)} %collective-permute-done.1.refs_3_), channel_id=1, source_target_pairs={{0,1},{1,0},{2,3},{3,2},{4,5},{5,4},{6,7},{7,6},{8,9},{9,8},{10,11... | collective-permute-start | bytes 1622024 | tf_op jit(solution)/shard_map/ppermute | solution.py:400
  48.8 51.5 %collective-permute-start.12 = (bf16[528,512]{1,0:T(8,128)(2,1)S(1)}, bf16[528,512]{1,0:T(8,128)(2,1)}, u32[]{:S(2)}, u32[]{:S(2)}) collective-permute-start(bf16[528,512]{1,0:T(8,128)(2,1)S(1)} %shard_map.178.refs_0_.refs_4_.refs_3_), channel_id=1, source_target_pairs={{0,1},{1,0},{2,3},{3,2},{4,5},{5,4},{6,7},{7,6},{8,9},{9,8},{10,11... | collective-permute-start | bytes 1622024 | tf_op jit(solution)/shard_map/ppermute | solution.py:400
  61.0 39.3 %collective-permute-start.14 = (bf16[528,512]{1,0:T(8,128)(2,1)}, bf16[528,512]{1,0:T(8,128)(2,1)}, u32[]{:S(2)}, u32[]{:S(2)}) collective-permute-start(bf16[528,512]{1,0:T(8,128)(2,1)} %collective-permute-done.13.refs_6_.refs_5_), channel_id=1, source_target_pairs={{0,1},{1,0},{2,3},{3,2},{4,5},{5,4},{6,7},{7,6},{8,9},{9,8},{10,11... | collective-permute-start | bytes 1622024 | tf_op jit(solution)/shard_map/ppermute | solution.py:400
  62.6 1.4 copy-start
  64.0 1.0 copy-start.6
  65.1 1.0 copy-start.8
  67.2 1.0 copy-start.18
  68.2 47.6 %copy-start.1 = (bf16[384,2048]{1,0:T(8,128)(2,1)S(1)}, bf16[384,2048]{1,0:T(8,128)(2,1)}, u32[]{:S(2)}) copy-start(bf16[384,2048]{1,0:T(8,128)(2,1)} %all-gather.2.cloned.1.call-done.refs_0_.refs_12_) | copy-start | bytes 4718596
  68.2 47.6 %copy-start.12 = (bf16[768,512]{1,0:T(8,128)(2,1)S(1)}, bf16[768,512]{1,0:T(8,128)(2,1)}, u32[]{:S(2)}) copy-start(bf16[768,512]{1,0:T(8,128)(2,1)} %copy-done.11) | copy-start | bytes 2359300
  68.2 47.6 %copy-start.14 = (bf16[768,512]{1,0:T(8,128)(2,1)S(1)}, bf16[768,512]{1,0:T(8,128)(2,1)}, u32[]{:S(2)}) copy-start(bf16[768,512]{1,0:T(8,128)(2,1)} %copy-done.13) | copy-start | bytes 2359300
  69.8 37.9 %collective-permute-start.10 = (bf16[384,512]{1,0:T(8,128)(2,1)S(1)}, bf16[384,512]{1,0:T(8,128)(2,1)S(1)}, u32[]{:S(2)}, u32[]{:S(2)}) collective-permute-start(bf16[384,512]{1,0:T(8,128)(2,1)S(1)} %get-tuple-element.58.refs_0_.refs_2_.refs_4_), channel_id=1, source_target_pairs={{0,8},{12,4},{1,9},{13,5},{2,10},{14,6},{3,11},{15,7},{16,24},{28,... | collective-permute-start | bytes 1179656 | tf_op jit(solution)/shard_map/ppermute | solution.py:396
  98.3 9.4 %collective-permute-start.9 = (bf16[384,512]{1,0:T(8,128)(2,1)S(1)}, bf16[384,512]{1,0:T(8,128)(2,1)S(1)}, u32[]{:S(2)}, u32[]{:S(2)}) collective-permute-start(bf16[384,512]{1,0:T(8,128)(2,1)S(1)} %get-tuple-element.58.refs_0_.refs_2_.refs_4_), channel_id=1, source_target_pairs={{8,4},{12,8},{9,5},{13,9},{10,6},{14,10},{11,7},{15,11},{24,20},{2... | collective-permute-start | bytes 1179656 | tf_op jit(solution)/shard_map/ppermute | solution.py:396
  99.0 16.8 %collective-permute-start.8 = (bf16[384,512]{1,0:T(8,128)(2,1)S(1)}, bf16[384,512]{1,0:T(8,128)(2,1)S(1)}, u32[]{:S(2)}, u32[]{:S(2)}) collective-permute-start(bf16[384,512]{1,0:T(8,128)(2,1)S(1)} %get-tuple-element.58.refs_0_.refs_2_.refs_4_), channel_id=1, source_target_pairs={{0,4},{4,8},{1,5},{5,9},{2,6},{6,10},{3,7},{7,11},{16,20},{20,24},... | collective-permute-start | bytes 1179656 | tf_op jit(solution)/shard_map/ppermute | solution.py:396
  119.1 21.2 %collective-permute-start.17 = (bf16[384,1024]{1,0:T(8,128)(2,1)S(1)}, bf16[384,1024]{1,0:T(8,128)(2,1)S(1)}, u32[]{:S(2)}, u32[]{:S(2)}) collective-permute-start(bf16[384,1024]{1,0:T(8,128)(2,1)S(1)} %shard_map.183.refs_0_), channel_id=1, source_target_pairs={{4,0},{8,12},{5,1},{9,13},{6,2},{10,14},{7,3},{11,15},{20,16},{24,... | collective-permute-start | bytes 2359304 | tf_op jit(solution)/shard_map/ppermute | solution.py:396
  120.4 19.9 %collective-permute-start.15 = (bf16[384,1024]{1,0:T(8,128)(2,1)S(1)}, bf16[384,1024]{1,0:T(8,128)(2,1)S(1)}, u32[]{:S(2)}, u32[]{:S(2)}) collective-permute-start(bf16[384,1024]{1,0:T(8,128)(2,1)S(1)} %shard_map.183.refs_0_), channel_id=1, source_target_pairs={{4,8},{8,4},{5,9},{9,5},{6,10},{10,6},{7,11},{11,7},{20,24},{24,20... | collective-permute-start | bytes 2359304 | tf_op jit(solution)/shard_map/ppermute | solution.py:396
  121.1 39.2 %collective-permute-start.16 = (bf16[384,1024]{1,0:T(8,128)(2,1)S(1)}, bf16[384,1024]{1,0:T(8,128)(2,1)S(1)}, u32[]{:S(2)}, u32[]{:S(2)}) collective-permute-start(bf16[384,1024]{1,0:T(8,128)(2,1)S(1)} %shard_map.183.refs_0_), channel_id=1, source_target_pairs={{8,0},{4,12},{9,1},{5,13},{10,2},{6,14},{11,3},{7,15},{24,16},{20,... | collective-permute-start | bytes 2359304 | tf_op jit(solution)/shard_map/ppermute | solution.py:396
  142.8 2.0 %collective-permute-start.18 = (f32[264,512]{1,0:T(8,128)S(1)}, f32[264,512]{1,0:T(8,128)S(1)}, u32[]{:S(2)}, u32[]{:S(2)}) collective-permute-start(f32[264,512]{1,0:T(8,128)S(1)} %get-tuple-element.62), channel_id=1, source_target_pairs={{0,1},{1,0},{2,3},{3,2},{4,5},{5,4},{6,7},{7,6},{8,9},{9,8},{10,11... | collective-permute-start | bytes 1622024 | tf_op jit(solution)/shard_map/ppermute | solution.py:400
  145.6 15.8 %collective-permute-start.19 = (f16[272,512]{1,0:T(8,128)(2,1)S(1)}, f16[272,512]{1,0:T(8,128)(2,1)S(1)}, u32[]{:S(2)}, u32[]{:S(2)}) collective-permute-start(f16[272,512]{1,0:T(8,128)(2,1)S(1)} %convert_element_type.25), channel_id=1, source_target_pairs={{0,2},{1,3},{2,0},{3,1},{4,6},{5,7},{6,4},{7,5},{8,10},{9,11},{10,... | collective-permute-start | bytes 835592 | tf_op jit(solution)/shard_map/ppermute | solution.py:400
  161.4 3.7 %collective-permute-start.20 = (f32[256,512]{1,0:T(8,128)S(1)}, f32[256,512]{1,0:T(8,128)S(1)}, u32[]{:S(2)}, u32[]{:S(2)}) collective-permute-start(f32[256,512]{1,0:T(8,128)S(1)} %get-tuple-element.71), channel_id=1, source_target_pairs={{0,1},{1,0},{2,3},{3,2},{4,5},{5,4},{6,7},{7,6},{8,9},{9,8},{10,11... | collective-permute-start | bytes 1572872 | tf_op jit(solution)/shard_map/ppermute | solution.py:400
  164.0 5.8 %collective-permute-start.21 = (f32[264,512]{1,0:T(8,128)S(1)}, f32[264,512]{1,0:T(8,128)S(1)}, u32[]{:S(2)}, u32[]{:S(2)}) collective-permute-start(f32[264,512]{1,0:T(8,128)S(1)} %get-tuple-element.76), channel_id=1, source_target_pairs={{0,1},{1,0},{2,3},{3,2},{4,5},{5,4},{6,7},{7,6},{8,9},{9,8},{10,11... | collective-permute-start | bytes 1622024 | tf_op jit(solution)/shard_map/ppermute | solution.py:400
  164.6 4.6 %collective-permute-start.22 = (f32[256,512]{1,0:T(8,128)S(1)}, f32[256,512]{1,0:T(8,128)S(1)}, u32[]{:S(2)}, u32[]{:S(2)}) collective-permute-start(f32[256,512]{1,0:T(8,128)S(1)} %get-tuple-element.77), channel_id=1, source_target_pairs={{0,1},{1,0},{2,3},{3,2},{4,5},{5,4},{6,7},{7,6},{8,9},{9,8},{10,11... | collective-permute-start | bytes 1572872 | tf_op jit(solution)/shard_map/ppermute | solution.py:400
  164.6 7.9 %collective-permute-start.25 = (f32[256,512]{1,0:T(8,128)S(1)}, f32[256,512]{1,0:T(8,128)S(1)}, u32[]{:S(2)}, u32[]{:S(2)}) collective-permute-start(f32[256,512]{1,0:T(8,128)S(1)} %get-tuple-element.90), channel_id=1, source_target_pairs={{0,1},{1,0},{2,3},{3,2},{4,5},{5,4},{6,7},{7,6},{8,9},{9,8},{10,11... | collective-permute-start | bytes 1572872 | tf_op jit(solution)/shard_map/ppermute | solution.py:400
  166.3 9.6 %collective-permute-start.27 = (f16[272,512]{1,0:T(8,128)(2,1)S(1)}, f16[272,512]{1,0:T(8,128)(2,1)S(1)}, u32[]{:S(2)}, u32[]{:S(2)}) collective-permute-start(f16[272,512]{1,0:T(8,128)(2,1)S(1)} %convert_element_type.31), channel_id=1, source_target_pairs={{0,2},{1,3},{2,0},{3,1},{4,6},{5,7},{6,4},{7,5},{8,10},{9,11},{10,... | collective-permute-start | bytes 835592 | tf_op jit(solution)/shard_map/ppermute | solution.py:400
  169.1 6.7 %collective-permute-start.26 = (f32[256,512]{1,0:T(8,128)S(1)}, f32[256,512]{1,0:T(8,128)S(1)}, u32[]{:S(2)}, u32[]{:S(2)}) collective-permute-start(f32[256,512]{1,0:T(8,128)S(1)} %get-tuple-element.92), channel_id=1, source_target_pairs={{0,1},{1,0},{2,3},{3,2},{4,5},{5,4},{6,7},{7,6},{8,9},{9,8},{10,11... | collective-permute-start | bytes 1572872 | tf_op jit(solution)/shard_map/ppermute | solution.py:400
  169.2 18.5 %collective-permute-start.23 = (f32[512,512]{1,0:T(8,128)S(1)}, f32[512,512]{1,0:T(8,128)S(1)}, u32[]{:S(2)}, u32[]{:S(2)}) collective-permute-start(f32[512,512]{1,0:T(8,128)S(1)} %get-tuple-element.82), channel_id=1, source_target_pairs={{0,1},{1,0},{2,3},{3,2},{4,5},{5,4},{6,7},{7,6},{8,9},{9,8},{10,11... | collective-permute-start | bytes 3145736 | tf_op jit(solution)/shard_map/ppermute | solution.py:400
  170.7 15.9 %collective-permute-start.24 = (f16[528,512]{1,0:T(8,128)(2,1)S(1)}, f16[528,512]{1,0:T(8,128)(2,1)S(1)}, u32[]{:S(2)}, u32[]{:S(2)}) collective-permute-start(f16[528,512]{1,0:T(8,128)(2,1)S(1)} %convert_element_type.26), channel_id=1, source_target_pairs={{0,2},{1,3},{2,0},{3,1},{4,6},{5,7},{6,4},{7,5},{8,10},{9,11},{10,... | collective-permute-start | bytes 1622024 | tf_op jit(solution)/shard_map/ppermute | solution.py:400
  172.5 3.6 %copy-start.3 = (f32[512,512]{1,0:T(8,128)S(1)}, f32[512,512]{1,0:T(8,128)}, u32[]{:S(2)}) copy-start(f32[512,512]{1,0:T(8,128)} %param.20) | copy-start | bytes 3145732
  172.5 3.6 %copy-start.9 = (f32[512,512]{1,0:T(8,128)S(1)}, f32[512,512]{1,0:T(8,128)}, u32[]{:S(2)}) copy-start(f32[512,512]{1,0:T(8,128)} %moment) | copy-start | bytes 3145732
  172.5 3.6 %copy-start.10 = (f32[512,512]{1,0:T(8,128)S(1)}, f32[512,512]{1,0:T(8,128)}, u32[]{:S(2)}) copy-start(f32[512,512]{1,0:T(8,128)} %square) | copy-start | bytes 3145732
  176.1 10.5 %copy-start.20 = (f32[128]{0:T(128)S(1)}, f32[128]{0:T(128)}, u32[]{:S(2)}) copy-start(f32[128]{0:T(128)} %param.16) | copy-start | bytes 1540
  176.1 10.5 %copy-start.21 = (f32[128]{0:T(128)S(1)}, f32[128]{0:T(128)}, u32[]{:S(2)}) copy-start(f32[128]{0:T(128)} %param.17) | copy-start | bytes 1540
  176.1 11.6 %copy-start.22 = (f32[512,512]{1,0:T(8,128)S(1)}, f32[512,512]{1,0:T(8,128)}, u32[]{:S(2)}) copy-start(f32[512,512]{1,0:T(8,128)} %param.14) | copy-start | bytes 3145732
  176.1 11.6 %copy-start.23 = (f32[512,512]{1,0:T(8,128)S(1)}, f32[512,512]{1,0:T(8,128)}, u32[]{:S(2)}) copy-start(f32[512,512]{1,0:T(8,128)} %param.15) | copy-start | bytes 3145732
  (5 other events, 4.4 us)
Sparse Core Ops, SparseCore 0:
  9.6 47.6 all-gather.1

commit v13 on v10

--- a/solution.py
+++ b/solution.py
@@ -374,8 +374,9 @@
 
 
 def pack_body(place, kept, row, *refs):
-    received, (packed, row_sum) = refs[:-2], refs[-2:]
     width = kept.shape[0]
+    at = [ref.shape[0] == width + EXTRA for ref in refs].index(True)
+    received, packed, row_sums = refs[:at], refs[at], refs[at + 1 :]
     block = width // len(received)
     total = jnp.concatenate([piece[:block] for piece in received], axis=0) + kept[...]
     exponent = power(total)
@@ -383,7 +384,8 @@
     sums = row[...]
     if received[0].shape[0] > block:
         sums += received[0][block : block + 1]
-    row_sum[...] = sums
+    for row_sum in row_sums:
+        row_sum[...] = sums
     row_exponent = power(sums)
     parts = three_rows(sums * scale_of(14.0 - row_exponent)).astype(F32)
     at = lax.broadcasted_iota(jnp.int32, parts.shape, 0)
@@ -511,10 +513,10 @@
     codes_high = along(codes, [(2, 1), (3, 2)])
     codes_across = along(codes, [(0, 2), (3, 1)])
     (turned,) = local_kernel(
-        turn_body, [shape((features, count), BF16)], place, inputs
+        turn_body, [shape((features, count), BF16)], place, inputs, after=(codes_across,)
     )
     rows_chip = flip(rows_own, 2, (1, 2))
-    rows_core = flip(behind(rows_own, turned), 1, (1, 2))
+    rows_core = flip(behind(rows_own, codes), 1, (1, 2))
     halves = local_kernel(
         split_body,
         [shape((3 * half // 2, latents), BF16)] * 2,
@@ -543,16 +545,16 @@
     passed = along(own_error, [(1, 0), (2, 3)])
     direct = along(own_error, [(2, 0), (1, 3)])
 
-    def across_chips(kept, row, *send):
-        packed, row_sum = local_kernel(
+    def across_chips(kept, row, *send, keep_row=True):
+        packed, *row_sum = local_kernel(
             pack_body,
-            [shape((kept.shape[0] + EXTRA, latents), F32), shape((1, latents), F32)],
+            [shape((kept.shape[0] + EXTRA, latents), F32)] + [shape((1, latents), F32)] * keep_row,
             place,
             kept,
             row,
             *[flip(piece, 1) for piece in send],
         )
-        return packed, flip(packed.astype(jnp.float16), 2), row_sum
+        return packed, flip(packed.astype(jnp.float16), 2), *row_sum
 
     blocks = [shape((half + 8, latents), F32)] + [shape((half, latents), F32)] * 3
     part, near, *near_blocks = local_kernel(
@@ -576,7 +578,7 @@
         swapped,
         direct,
         codes,
-        after=(near_packed,),
+        after=(near_packed, near_kept[1]),
         cost=NOTABLE,
     )
     grad_low, bias_sum, norms, *send_far_enc = local_kernel(
@@ -596,7 +598,7 @@
         turned,
         cost=NOTABLE,
     )
-    far_packed, far_received, _ = across_chips(far_keep, active, far_send)
+    far_packed, far_received = across_chips(far_keep, active, far_send, keep_row=False)
     error, enc_send_near, enc_keep_far, enc_keep_near, send_near, keep_near = local_kernel(
         functools.partial(rest_body, rows),
         [shape((count, width), BF16)]

time: 147 us -> 146 us (level)
  no operation moved by 1% of the time
where the time goes in v13:
time: 146 us; the launch traced here: 145 us
  waiting for transfers between devices  67.3 us (46%)
  starting transfers between devices  50.3 us (34%)
  Pallas kernels  21.7 us (15%)
  other arithmetic  2.88 us (2%)
  local copies, waits for them, and re-layouts  2.06 us (1%)
    ppermute x14, waiting for transfers between devices, along(): return lax.ppermute(value, 'latent', pairs)  53.9 us
    ppermute x14, starting transfers between devices, along(): return lax.ppermute(value, 'latent', pairs)  38.7 us
    pallas_call x16, Pallas kernels, local_kernel(): pl.pallas_call(run, out_shape=outs, in_specs=[SMEM] + [VMEM] * len(args)...  18.8 us
    ppermute x20, waiting for transfers between devices, flip(): return lax.ppermute(value, ('latent', 'dp'), pairs)  13.3 us
    ppermute x20, starting transfers between devices, flip(): return lax.ppermute(value, ('latent', 'dp'), pairs)  11.6 us
    pallas_call x1, Pallas kernels, line_shards(): pl.pallas_call(functools.partial(decoder_step_body, rows), grid=(4,), out...  2.94 us
  transfers between devices with their start and end apart: 34, of which 12 were waited for; matrix products, arithmetic and copies ran while one was open for 0% of the time, Pallas kernels for 13%

profile of v13, /device:TPU:0, one launch (start us, length us, event | category | flops | bytes accessed | tf_op | source)
XLA Modules:
  0.0 145.4 jit_solution(10887928414339650723)
XLA Ops:
  0.7 1.3 copy-done.1
  2.0 0.7 copy-done.6
  3.8 5.8 %collective-permute-start.2 = (bf16[384,512]{1,0:T(8,128)(2,1)S(1)}, bf16[384,512]{1,0:T(8,128)(2,1)S(1)}, u32[]{:S(2)}, u32[]{:S(2)}) collective-permute-start(bf16[384,512]{1,0:T(8,128)(2,1)S(1)} %copy-done.5), channel_id=1, source_target_pairs={{0,8},{12,4},{1,9},{13,5},{2,10},{14,6},{3,11},{15,7},{16,24},{28,... | collective-permute-start | bytes 1179656 | tf_op jit(solution)/shard_map/ppermute | solution.py:448
  9.6 1.3 collective-permute-start.1
  10.9 4.6 %collective-permute-start = (bf16[384,512]{1,0:T(8,128)(2,1)S(1)}, bf16[384,512]{1,0:T(8,128)(2,1)S(1)}, u32[]{:S(2)}, u32[]{:S(2)}) collective-permute-start(bf16[384,512]{1,0:T(8,128)(2,1)S(1)} %copy-done.5), channel_id=1, source_target_pairs={{0,4},{4,8},{8,12},{1,5},{5,9},{9,13},{2,6},{6,10},{10,14},{3,7},{... | collective-permute-start | bytes 1179656 | tf_op jit(solution)/shard_map/ppermute | solution.py:448
  15.5 1.6 %collective-permute-start.6 = (bf16[528,512]{1,0:T(8,128)(2,1)S(1)}, bf16[528,512]{1,0:T(8,128)(2,1)S(1)}, u32[]{:S(2)}, u32[]{:S(2)}) collective-permute-start(bf16[528,512]{1,0:T(8,128)(2,1)S(1)} %shard_map.178.refs_6_), channel_id=1, source_target_pairs={{0,2},{1,3},{2,0},{3,1},{4,6},{5,7},{6,4},{7,5},{8,10},{9,11},{10,... | collective-permute-start | bytes 1622024 | tf_op jit(solution)/shard_map/ppermute | solution.py:452
  17.1 0.6 shard_map.179.refs_0_.refs_4_.refs_3_
  18.3 0.8 collective-permute-done.2.refs_3_
  19.1 1.3 collective-permute-start.4
  21.0 1.6 %collective-permute-done.1.refs_1_.refs_2_ = bf16[384,512]{1,0:T(8,128)(2,1)S(1)} collective-permute-done((bf16[384,512]{1,0:T(8,128)(2,1)S(1)}, bf16[384,512]{1,0:T(8,128)(2,1)S(1)}, u32[]{:S(2)}, u32[]{:S(2)}) %collective-permute-start.1) | collective-permute-done | bytes 393248 | tf_op jit(solution)/shard_map/ppermute | solution.py:448
  22.6 8.4 %collective-permute-start.8 = (bf16[256,512]{1,0:T(8,128)(2,1)S(1)}, bf16[256,512]{1,0:T(8,128)(2,1)S(1)}, u32[]{:S(2)}, u32[]{:S(2)}) collective-permute-start(bf16[256,512]{1,0:T(8,128)(2,1)S(1)} %get-tuple-element.62), channel_id=1, source_target_pairs={{0,4},{4,8},{1,5},{5,9},{2,6},{6,10},{3,7},{7,11},{16,20},{20,24},... | collective-permute-start | bytes 786440 | tf_op jit(solution)/shard_map/ppermute | solution.py:448
  31.0 0.7 collective-permute-start.10
  31.7 5.2 %collective-permute-start.11 = (bf16[256,512]{1,0:T(8,128)(2,1)S(1)}, bf16[256,512]{1,0:T(8,128)(2,1)S(1)}, u32[]{:S(2)}, u32[]{:S(2)}) collective-permute-start(bf16[256,512]{1,0:T(8,128)(2,1)S(1)} %get-tuple-element.66), channel_id=1, source_target_pairs={{0,8},{12,4},{1,9},{13,5},{2,10},{14,6},{3,11},{15,7},{16,24},{28,... | collective-permute-start | bytes 786440 | tf_op jit(solution)/shard_map/ppermute | solution.py:448
  37.6 1.3 collective-permute-start.3
  38.9 1.8 %collective-permute-done.9.refs_6_.refs_5_ = bf16[528,512]{1,0:T(8,128)(2,1)S(1)} collective-permute-done((bf16[528,512]{1,0:T(8,128)(2,1)S(1)}, bf16[528,512]{1,0:T(8,128)(2,1)S(1)}, u32[]{:S(2)}, u32[]{:S(2)}) %collective-permute-start.9) | collective-permute-done | bytes 540704 | tf_op jit(solution)/shard_map/ppermute | solution.py:452
  41.3 1.1 collective-permute-done.11
  42.4 0.7 collective-permute-start.18
  43.1 6.2 %collective-permute-done.3.refs_4_ = bf16[384,512]{1,0:T(8,128)(2,1)S(1)} collective-permute-done((bf16[384,512]{1,0:T(8,128)(2,1)S(1)}, bf16[384,512]{1,0:T(8,128)(2,1)S(1)}, u32[]{:S(2)}, u32[]{:S(2)}) %collective-permute-start.3) | collective-permute-done | bytes 393248 | tf_op jit(solution)/shard_map/ppermute | solution.py:448
  49.4 1.8 %shard_map.181 = (bf16[384,512]{1,0:T(8,128)(2,1)S(1)}, bf16[384,512]{1,0:T(8,128)(2,1)S(1)}, bf16[384,2048]{1,0:T(8,128)(2,1)S(1)}, f32[1,512]{1,0:T(1,128)S(1)}) custom-call(s32[2]{0:T(128)S(1)} %pad_add_fusion.place, bf16[384,512]{1,0:T(8,128)(2,1)S(1)} %copy-done.5, bf16[384,512]{1,0:T(8,128)(2,1)S(1)} %collective-permute-done.refs_0_.refs_1_, ...), custom_call_target="tpu_custom_call" | custom-call | flops 1 | bytes 1 | tf_op jit(solution)/shard_map/pallas_call | solution.py:121
  51.2 1.9 %collective-permute-start.14 = (bf16[384,512]{1,0:T(8,128)(2,1)S(1)}, bf16[384,512]{1,0:T(8,128)(2,1)S(1)}, u32[]{:S(2)}, u32[]{:S(2)}) collective-permute-start(bf16[384,512]{1,0:T(8,128)(2,1)S(1)} %get-tuple-element.69.refs_0_.refs_2_.refs_4_), channel_id=1, source_target_pairs={{0,8},{12,4},{1,9},{13,5},{2,10},{14,6},{3,11},{15,7},{16,24},{28,... | collective-permute-start | bytes 1179656 | tf_op jit(solution)/shard_map/ppermute | solution.py:448
  53.1 0.7 collective-permute-start.17
  53.8 0.7 collective-permute-start.16
  54.5 4.3 %collective-permute-start.15 = (bf16[384,512]{1,0:T(8,128)(2,1)S(1)}, bf16[384,512]{1,0:T(8,128)(2,1)S(1)}, u32[]{:S(2)}, u32[]{:S(2)}) collective-permute-start(bf16[384,512]{1,0:T(8,128)(2,1)S(1)} %get-tuple-element.69.refs_0_.refs_2_.refs_4_), channel_id=1, source_target_pairs={{0,4},{4,8},{1,5},{5,9},{2,6},{6,10},{3,7},{7,11},{16,20},{20,24},... | collective-permute-start | bytes 1179656 | tf_op jit(solution)/shard_map/ppermute | solution.py:448
  58.8 3.7 %collective-permute-done.14.refs_1_.refs_3_ = bf16[384,512]{1,0:T(8,128)(2,1)S(1)} collective-permute-done((bf16[384,512]{1,0:T(8,128)(2,1)S(1)}, bf16[384,512]{1,0:T(8,128)(2,1)S(1)}, u32[]{:S(2)}, u32[]{:S(2)}) %collective-permute-start.14) | collective-permute-done | bytes 393248 | tf_op jit(solution)/shard_map/ppermute | solution.py:448
  63.1 0.7 collective-permute-start.19
  63.8 0.7 collective-permute-start.20
  64.5 5.7 %collective-permute-done.15.refs_1_ = bf16[384,512]{1,0:T(8,128)(2,1)S(1)} collective-permute-done((bf16[384,512]{1,0:T(8,128)(2,1)S(1)}, bf16[384,512]{1,0:T(8,128)(2,1)S(1)}, u32[]{:S(2)}, u32[]{:S(2)}) %collective-permute-start.15) | collective-permute-done | bytes 393248 | tf_op jit(solution)/shard_map/ppermute | solution.py:448
  70.2 2.4 %shard_map.184.refs_0_ = bf16[384,1024]{1,0:T(8,128)(2,1)S(1)} custom-call(s32[2]{0:T(128)S(1)} %pad_add_fusion.place, bf16[384,512]{1,0:T(8,128)(2,1)S(1)} %get-tuple-element.69.refs_0_.refs_2_.refs_4_, bf16[384,512]{1,0:T(8,128)(2,1)S(1)} %collective-permute-done.15.refs_1_, bf16[384,512]{1,0:T(8,128)(2,1)S(1)} %collective-permute-done.16.refs_2_, ...), custom_call_target="tpu_custom_call" | custom-call | flops 1 | bytes 1 | tf_op jit(solution)/shard_map/pallas_call | solution.py:121
  72.7 1.3 collective-permute-start.23
  74.0 0.7 collective-permute-start.21
  74.7 1.3 collective-permute-start.22
  76.0 20.8 %collective-permute-done.23.refs_1_ = bf16[384,1024]{1,0:T(8,128)(2,1)S(1)} collective-permute-done((bf16[384,1024]{1,0:T(8,128)(2,1)S(1)}, bf16[384,1024]{1,0:T(8,128)(2,1)S(1)}, u32[]{:S(2)}, u32[]{:S(2)}) %collective-permute-start.23) | collective-permute-done | bytes 786464 | tf_op jit(solution)/shard_map/ppermute | solution.py:448
  96.8 1.8 %shard_map.185 = (f32[384,512]{1,0:T(8,128)S(1)}, bf16[384,1024]{1,0:T(8,128)(2,1)S(1)}, f32[264,512]{1,0:T(8,128)S(1)}, f32[256,512]{1,0:T(8,128)S(1)}, f32[256,512]{1,0:T(8,128)S(1)}, /*index=5*/f32[256,512]{1,0:T(8,128)S(1)}) custom-call(s32[2]{0:T(128)S(1)} %pad_add_fusion.place, bf16[384,1024]{1,0:T(8,128)(2,1)S(1)} %shard_map.184.refs_0_, ...), custom_call_target="tpu_custom_call" | custom-call | flops 1 | bytes 1 | tf_op jit(solution)/shard_map/pallas_call | solution.py:121
  99.2 1.0 shard_map.182.refs_7_.refs_0_
  100.6 0.7 shard_map.186
  101.3 1.5 %collective-permute-start.26 = (f16[272,512]{1,0:T(8,128)(2,1)S(1)}, f16[272,512]{1,0:T(8,128)(2,1)S(1)}, u32[]{:S(2)}, u32[]{:S(2)}) collective-permute-start(f16[272,512]{1,0:T(8,128)(2,1)S(1)} %convert_element_type.25), channel_id=1, source_target_pairs={{0,2},{1,3},{2,0},{3,1},{4,6},{5,7},{6,4},{7,5},{8,10},{9,11},{10,... | collective-permute-start | bytes 835592 | tf_op jit(solution)/shard_map/ppermute | solution.py:452
  102.9 13.9 %collective-permute-done.22.refs_1_ = bf16[384,1024]{1,0:T(8,128)(2,1)S(1)} collective-permute-done((bf16[384,1024]{1,0:T(8,128)(2,1)S(1)}, bf16[384,1024]{1,0:T(8,128)(2,1)S(1)}, u32[]{:S(2)}, u32[]{:S(2)}) %collective-permute-start.22) | collective-permute-done | bytes 786464 | tf_op jit(solution)/shard_map/ppermute | solution.py:448
  116.8 1.3 shard_map.187
  118.2 1.7 %shard_map.188 = (bf16[384,512]{1,0:T(8,128)(2,1)S(1)}, f32[1,512]{1,0:T(1,128)S(1)}, f32[1,512]{1,0:T(1,128)S(1)}, f32[264,512]{1,0:T(8,128)S(1)}, f32[256,512]{1,0:T(8,128)S(1)}) custom-call(s32[2]{0:T(128)S(1)} %pad_add_fusion.place, bf16[384,1024]{1,0:T(8,128)(2,1)S(1)} %get-tuple-element.78.refs_0_.refs_3_, f32[384,512]{1,0:T(8,128)S(1)} %get-tuple-element.80.refs_1_, ...), custom_call_target="tpu_custom_call" | custom-call | flops 10000000000 | bytes 1 | tf_op jit(solution)/shard_map/pallas_call | solution.py:121
  120.5 0.7 shard_map.189.refs_5_
  121.3 1.5 %collective-permute-start.33 = (f16[272,512]{1,0:T(8,128)(2,1)S(1)}, f16[272,512]{1,0:T(8,128)(2,1)S(1)}, u32[]{:S(2)}, u32[]{:S(2)}) collective-permute-start(f16[272,512]{1,0:T(8,128)(2,1)S(1)} %convert_element_type.31), channel_id=1, source_target_pairs={{0,2},{1,3},{2,0},{3,1},{4,6},{5,7},{6,4},{7,5},{8,10},{9,11},{10,... | collective-permute-start | bytes 835592 | tf_op jit(solution)/shard_map/ppermute | solution.py:452
  122.8 2.5 %shard_map.190 = (bf16[384,512]{1,0:T(8,128)(2,1)}, f32[512,512]{1,0:T(8,128)S(1)}, f32[512,512]{1,0:T(8,128)S(1)}, f32[512,512]{1,0:T(8,128)S(1)}, f32[256,512]{1,0:T(8,128)S(1)}, /*index=5*/f32[256,512]{1,0:T(8,128)S(1)}) custom-call(s32[2]{0:T(128)S(1)} %pad_add_fusion.place, bf16[2048,384]{1,0:T(8,128)(2,1)S(1)} %shard_map.182.refs_7_.refs_0_, ...), custom_call_target="tpu_custom_call" | custom-call | flops 1 | bytes 1 | tf_op jit(solution)/shard_map/pallas_call | solution.py:121
  125.9 0.8 shard_map.191
  127.6 3.2 %collective-permute-done.33 = f16[272,512]{1,0:T(8,128)(2,1)S(1)} collective-permute-done((f16[272,512]{1,0:T(8,128)(2,1)S(1)}, f16[272,512]{1,0:T(8,128)(2,1)S(1)}, u32[]{:S(2)}, u32[]{:S(2)}) %collective-permute-start.33) | collective-permute-done | bytes 278560 | tf_op jit(solution)/shard_map/ppermute | solution.py:452
  131.1 2.9 %shard_map.193 = (f32[512,512]{1,0:T(8,128)}, f32[512,512]{1,0:T(8,128)}, f32[512,512]{1,0:T(8,128)}) custom-call(s32[2]{0:T(128)S(1)} %pad_add_fusion.place, f32[512,512]{1,0:T(8,128)S(1)} %copy-done, f32[512,512]{1,0:T(8,128)S(1)} %copy-done.3, f32[512,512]{1,0:T(8,128)S(1)} %copy-done.4, f32[256,512]{1,0:T(8,128)S(1)} %multiply_add_fusion.3.near, ...), custom_call_target="tpu_custom_call" | custom-call | flops 1 | bytes 1 | tf_op jit(solution)/shard_map/pallas_call | solution.py:649
  134.0 7.9 %collective-permute-done.31 = f16[528,512]{1,0:T(8,128)(2,1)S(1)} collective-permute-done((f16[528,512]{1,0:T(8,128)(2,1)S(1)}, f16[528,512]{1,0:T(8,128)(2,1)S(1)}, u32[]{:S(2)}, u32[]{:S(2)}) %collective-permute-start.31) | collective-permute-done | bytes 540704 | tf_op jit(solution)/shard_map/ppermute | solution.py:452
  142.0 1.1 shard_map.192
  143.1 2.3 %divide_subtract_fusion = (f32[512,512]{1,0:T(8,128)}, f32[512,512]{1,0:T(8,128)}, f32[512,512]{1,0:T(8,128)}) fusion(f32[512,512]{1,0:T(8,128)S(1)} %copy-done.2, f32[512]{0:T(512)S(1)} %bitcast.15, f16[528,512]{1,0:T(8,128)(2,1)S(1)} %collective-permute-done.31, f32[512,512]{1,0:T(8,128)S(1)} %get-tuple-element.94, ...), kind=kLoop, calls=%fused_computation.2 | loop fusion | flops 4194304 | bytes 8914944 | tf_op jit(solution)/shard_map/sub | solution.py:28
  (76 shorter events, 7.7 us)
Async XLA Ops:
  0.6 16.4 %copy-start = (f32[512,512]{1,0:T(8,128)S(1)}, f32[512,512]{1,0:T(8,128)}, u32[]{:S(2)}) copy-start(f32[512,512]{1,0:T(8,128)} %param.20) | copy-start | bytes 3145732
  0.7 1.3 copy-start.1
  2.0 0.7 copy-start.6
  2.7 1.1 copy-start.5
  3.3 13.8 %collective-permute-start.5 = (bf16[528,512]{1,0:T(8,128)(2,1)S(1)}, bf16[528,512]{1,0:T(8,128)(2,1)S(1)}, u32[]{:S(2)}, u32[]{:S(2)}) collective-permute-start(bf16[528,512]{1,0:T(8,128)(2,1)S(1)} %shard_map.178.refs_6_), channel_id=1, source_target_pairs={{0,1},{1,0},{2,3},{3,2},{4,5},{5,4},{6,7},{7,6},{8,9},{9,8},{10,11... | collective-permute-start | bytes 1622024 | tf_op jit(solution)/shard_map/ppermute | solution.py:452
  3.8 15.3 %collective-permute-start.2 = (bf16[384,512]{1,0:T(8,128)(2,1)S(1)}, bf16[384,512]{1,0:T(8,128)(2,1)S(1)}, u32[]{:S(2)}, u32[]{:S(2)}) collective-permute-start(bf16[384,512]{1,0:T(8,128)(2,1)S(1)} %copy-done.5), channel_id=1, source_target_pairs={{0,8},{12,4},{1,9},{13,5},{2,10},{14,6},{3,11},{15,7},{16,24},{28,... | collective-permute-start | bytes 1179656 | tf_op jit(solution)/shard_map/ppermute | solution.py:448
  9.6 13.0 %collective-permute-start.1 = (bf16[384,512]{1,0:T(8,128)(2,1)S(1)}, bf16[384,512]{1,0:T(8,128)(2,1)S(1)}, u32[]{:S(2)}, u32[]{:S(2)}) collective-permute-start(bf16[384,512]{1,0:T(8,128)(2,1)S(1)} %copy-done.5), channel_id=1, source_target_pairs={{4,0},{8,4},{12,8},{5,1},{9,5},{13,9},{6,2},{10,6},{14,10},{7,3},{... | collective-permute-start | bytes 1179656 | tf_op jit(solution)/shard_map/ppermute | solution.py:448
  10.9 20.1 %collective-permute-start = (bf16[384,512]{1,0:T(8,128)(2,1)S(1)}, bf16[384,512]{1,0:T(8,128)(2,1)S(1)}, u32[]{:S(2)}, u32[]{:S(2)}) collective-permute-start(bf16[384,512]{1,0:T(8,128)(2,1)S(1)} %copy-done.5), channel_id=1, source_target_pairs={{0,4},{4,8},{8,12},{1,5},{5,9},{9,13},{2,6},{6,10},{10,14},{3,7},{... | collective-permute-start | bytes 1179656 | tf_op jit(solution)/shard_map/ppermute | solution.py:448
  15.5 16.2 %collective-permute-start.6 = (bf16[528,512]{1,0:T(8,128)(2,1)S(1)}, bf16[528,512]{1,0:T(8,128)(2,1)S(1)}, u32[]{:S(2)}, u32[]{:S(2)}) collective-permute-start(bf16[528,512]{1,0:T(8,128)(2,1)S(1)} %shard_map.178.refs_6_), channel_id=1, source_target_pairs={{0,2},{1,3},{2,0},{3,1},{4,6},{5,7},{6,4},{7,5},{8,10},{9,11},{10,... | collective-permute-start | bytes 1622024 | tf_op jit(solution)/shard_map/ppermute | solution.py:452
  17.7 23.0 %collective-permute-start.9 = (bf16[528,512]{1,0:T(8,128)(2,1)S(1)}, bf16[528,512]{1,0:T(8,128)(2,1)S(1)}, u32[]{:S(2)}, u32[]{:S(2)}) collective-permute-start(bf16[528,512]{1,0:T(8,128)(2,1)S(1)} %shard_map.179.refs_0_.refs_4_.refs_3_), channel_id=1, source_target_pairs={{0,2},{1,3},{2,0},{3,1},{4,6},{5,7},{6,4},{7,5},{8,10},{9,11},{10,... | collective-permute-start | bytes 1622024 | tf_op jit(solution)/shard_map/ppermute | solution.py:452
  19.1 18.4 %collective-permute-start.4 = (bf16[384,512]{1,0:T(8,128)(2,1)S(1)}, bf16[384,512]{1,0:T(8,128)(2,1)S(1)}, u32[]{:S(2)}, u32[]{:S(2)}) collective-permute-start(bf16[384,512]{1,0:T(8,128)(2,1)S(1)} %collective-permute-done.2.refs_3_), channel_id=1, source_target_pairs={{4,0},{8,12},{5,1},{9,13},{6,2},{10,14},{7,3},{11,15},{20,16},{24,... | collective-permute-start | bytes 1179656 | tf_op jit(solution)/shard_map/ppermute | solution.py:448
  22.6 16.2 %collective-permute-start.8 = (bf16[256,512]{1,0:T(8,128)(2,1)S(1)}, bf16[256,512]{1,0:T(8,128)(2,1)S(1)}, u32[]{:S(2)}, u32[]{:S(2)}) collective-permute-start(bf16[256,512]{1,0:T(8,128)(2,1)S(1)} %get-tuple-element.62), channel_id=1, source_target_pairs={{0,4},{4,8},{1,5},{5,9},{2,6},{6,10},{3,7},{7,11},{16,20},{20,24},... | collective-permute-start | bytes 786440 | tf_op jit(solution)/shard_map/ppermute | solution.py:448
  31.0 9.7 %collective-permute-start.10 = (bf16[256,512]{1,0:T(8,128)(2,1)S(1)}, bf16[256,512]{1,0:T(8,128)(2,1)S(1)}, u32[]{:S(2)}, u32[]{:S(2)}) collective-permute-start(bf16[256,512]{1,0:T(8,128)(2,1)S(1)} %get-tuple-element.64), channel_id=1, source_target_pairs={{8,4},{12,8},{9,5},{13,9},{10,6},{14,10},{11,7},{15,11},{24,20},{2... | collective-permute-start | bytes 786440 | tf_op jit(solution)/shard_map/ppermute | solution.py:448
  31.7 10.6 %collective-permute-start.11 = (bf16[256,512]{1,0:T(8,128)(2,1)S(1)}, bf16[256,512]{1,0:T(8,128)(2,1)S(1)}, u32[]{:S(2)}, u32[]{:S(2)}) collective-permute-start(bf16[256,512]{1,0:T(8,128)(2,1)S(1)} %get-tuple-element.66), channel_id=1, source_target_pairs={{0,8},{12,4},{1,9},{13,5},{2,10},{14,6},{3,11},{15,7},{16,24},{28,... | collective-permute-start | bytes 786440 | tf_op jit(solution)/shard_map/ppermute | solution.py:448
  37.6 11.8 %collective-permute-start.3 = (bf16[384,512]{1,0:T(8,128)(2,1)S(1)}, bf16[384,512]{1,0:T(8,128)(2,1)S(1)}, u32[]{:S(2)}, u32[]{:S(2)}) collective-permute-start(bf16[384,512]{1,0:T(8,128)(2,1)S(1)} %shard_map.177), channel_id=1, source_target_pairs={{4,0},{8,12},{5,1},{9,13},{6,2},{10,14},{7,3},{11,15},{20,16},{24,... | collective-permute-start | bytes 1179656 | tf_op jit(solution)/shard_map/ppermute | solution.py:448
  38.9 10.5 %collective-permute-start.12 = (bf16[528,512]{1,0:T(8,128)(2,1)S(1)}, bf16[528,512]{1,0:T(8,128)(2,1)S(1)}, u32[]{:S(2)}, u32[]{:S(2)}) collective-permute-start(bf16[528,512]{1,0:T(8,128)(2,1)S(1)} %shard_map.179.refs_0_.refs_4_.refs_3_), channel_id=1, source_target_pairs={{0,1},{1,0},{2,3},{3,2},{4,5},{5,4},{6,7},{7,6},{8,9},{9,8},{10,11... | collective-permute-start | bytes 1622024 | tf_op jit(solution)/shard_map/ppermute | solution.py:452
  40.7 8.7 %collective-permute-start.7 = (bf16[528,512]{1,0:T(8,128)(2,1)S(1)}, bf16[528,512]{1,0:T(8,128)(2,1)S(1)}, u32[]{:S(2)}, u32[]{:S(2)}) collective-permute-start(bf16[528,512]{1,0:T(8,128)(2,1)S(1)} %collective-permute-done.6.refs_8_), channel_id=1, source_target_pairs={{0,1},{1,0},{2,3},{3,2},{4,5},{5,4},{6,7},{7,6},{8,9},{9,8},{10,11... | collective-permute-start | bytes 1622024 | tf_op jit(solution)/shard_map/ppermute | solution.py:452
  40.7 8.7 %collective-permute-start.13 = (bf16[528,512]{1,0:T(8,128)(2,1)S(1)}, bf16[528,512]{1,0:T(8,128)(2,1)S(1)}, u32[]{:S(2)}, u32[]{:S(2)}) collective-permute-start(bf16[528,512]{1,0:T(8,128)(2,1)S(1)} %collective-permute-done.9.refs_6_.refs_5_), channel_id=1, source_target_pairs={{0,1},{1,0},{2,3},{3,2},{4,5},{5,4},{6,7},{7,6},{8,9},{9,8},{10,11... | collective-permute-start | bytes 1622024 | tf_op jit(solution)/shard_map/ppermute | solution.py:452
  42.4 16.4 %collective-permute-start.18 = (bf16[768,512]{1,0:T(8,128)(2,1)S(1)}, bf16[768,512]{1,0:T(8,128)(2,1)S(1)}, u32[]{:S(2)}, u32[]{:S(2)}) collective-permute-start(bf16[768,512]{1,0:T(8,128)(2,1)S(1)} %constant_dynamic-update-slice_fusion.refs_10_.refs_8_), channel_id=1, source_target_pairs={{4,6},{5,7},{6,4},{7,5},{8,10},{9,11},{10,8},{11,9},{20,22},{21,23... | collective-permute-start | bytes 2359304 | tf_op jit(solution)/shard_map/ppermute | solution.py:452
  51.2 11.3 %collective-permute-start.14 = (bf16[384,512]{1,0:T(8,128)(2,1)S(1)}, bf16[384,512]{1,0:T(8,128)(2,1)S(1)}, u32[]{:S(2)}, u32[]{:S(2)}) collective-permute-start(bf16[384,512]{1,0:T(8,128)(2,1)S(1)} %get-tuple-element.69.refs_0_.refs_2_.refs_4_), channel_id=1, source_target_pairs={{0,8},{12,4},{1,9},{13,5},{2,10},{14,6},{3,11},{15,7},{16,24},{28,... | collective-permute-start | bytes 1179656 | tf_op jit(solution)/shard_map/ppermute | solution.py:448
  53.1 17.2 %collective-permute-start.17 = (bf16[768,512]{1,0:T(8,128)(2,1)S(1)}, bf16[768,512]{1,0:T(8,128)(2,1)S(1)}, u32[]{:S(2)}, u32[]{:S(2)}) collective-permute-start(bf16[768,512]{1,0:T(8,128)(2,1)S(1)} %constant_dynamic-update-slice_fusion.refs_10_.refs_8_), channel_id=1, source_target_pairs={{4,5},{5,4},{6,7},{7,6},{8,9},{9,8},{10,11},{11,10},{20,21},{21,20... | collective-permute-start | bytes 2359304 | tf_op jit(solution)/shard_map/ppermute | solution.py:452
  53.8 10.7 %collective-permute-start.16 = (bf16[384,512]{1,0:T(8,128)(2,1)S(1)}, bf16[384,512]{1,0:T(8,128)(2,1)S(1)}, u32[]{:S(2)}, u32[]{:S(2)}) collective-permute-start(bf16[384,512]{1,0:T(8,128)(2,1)S(1)} %get-tuple-element.69.refs_0_.refs_2_.refs_4_), channel_id=1, source_target_pairs={{8,4},{12,8},{9,5},{13,9},{10,6},{14,10},{11,7},{15,11},{24,20},{2... | collective-permute-start | bytes 1179656 | tf_op jit(solution)/shard_map/ppermute | solution.py:448
  54.5 15.7 %collective-permute-start.15 = (bf16[384,512]{1,0:T(8,128)(2,1)S(1)}, bf16[384,512]{1,0:T(8,128)(2,1)S(1)}, u32[]{:S(2)}, u32[]{:S(2)}) collective-permute-start(bf16[384,512]{1,0:T(8,128)(2,1)S(1)} %get-tuple-element.69.refs_0_.refs_2_.refs_4_), channel_id=1, source_target_pairs={{0,4},{4,8},{1,5},{5,9},{2,6},{6,10},{3,7},{7,11},{16,20},{20,24},... | collective-permute-start | bytes 1179656 | tf_op jit(solution)/shard_map/ppermute | solution.py:448
  63.1 7.1 %collective-permute-start.19 = (bf16[384,512]{1,0:T(8,128)(2,1)S(1)}, bf16[384,512]{1,0:T(8,128)(2,1)S(1)}, u32[]{:S(2)}, u32[]{:S(2)}) collective-permute-start(bf16[384,512]{1,0:T(8,128)(2,1)S(1)} %get-tuple-element.71), channel_id=1, source_target_pairs={{4,5},{5,4},{6,7},{7,6},{8,9},{9,8},{10,11},{11,10},{20,21},{21,20... | collective-permute-start | bytes 1179656 | tf_op jit(solution)/shard_map/ppermute | solution.py:452
  63.8 6.4 %collective-permute-start.20 = (bf16[384,512]{1,0:T(8,128)(2,1)S(1)}, bf16[384,512]{1,0:T(8,128)(2,1)S(1)}, u32[]{:S(2)}, u32[]{:S(2)}) collective-permute-start(bf16[384,512]{1,0:T(8,128)(2,1)S(1)} %get-tuple-element.72), channel_id=1, source_target_pairs={{4,5},{5,4},{6,7},{7,6},{8,9},{9,8},{10,11},{11,10},{20,21},{21,20... | collective-permute-start | bytes 1179656 | tf_op jit(solution)/shard_map/ppermute | solution.py:452
  72.7 24.1 %collective-permute-start.23 = (bf16[384,1024]{1,0:T(8,128)(2,1)S(1)}, bf16[384,1024]{1,0:T(8,128)(2,1)S(1)}, u32[]{:S(2)}, u32[]{:S(2)}) collective-permute-start(bf16[384,1024]{1,0:T(8,128)(2,1)S(1)} %shard_map.184.refs_0_), channel_id=1, source_target_pairs={{4,0},{8,12},{5,1},{9,13},{6,2},{10,14},{7,3},{11,15},{20,16},{24,... | collective-permute-start | bytes 2359304 | tf_op jit(solution)/shard_map/ppermute | solution.py:448
  74.0 22.9 %collective-permute-start.21 = (bf16[384,1024]{1,0:T(8,128)(2,1)S(1)}, bf16[384,1024]{1,0:T(8,128)(2,1)S(1)}, u32[]{:S(2)}, u32[]{:S(2)}) collective-permute-start(bf16[384,1024]{1,0:T(8,128)(2,1)S(1)} %shard_map.184.refs_0_), channel_id=1, source_target_pairs={{4,8},{8,4},{5,9},{9,5},{6,10},{10,6},{7,11},{11,7},{20,24},{24,20... | collective-permute-start | bytes 2359304 | tf_op jit(solution)/shard_map/ppermute | solution.py:448
  74.7 42.1 %collective-permute-start.22 = (bf16[384,1024]{1,0:T(8,128)(2,1)S(1)}, bf16[384,1024]{1,0:T(8,128)(2,1)S(1)}, u32[]{:S(2)}, u32[]{:S(2)}) collective-permute-start(bf16[384,1024]{1,0:T(8,128)(2,1)S(1)} %shard_map.184.refs_0_), channel_id=1, source_target_pairs={{8,0},{4,12},{9,1},{5,13},{10,2},{6,14},{11,3},{7,15},{24,16},{20,... | collective-permute-start | bytes 2359304 | tf_op jit(solution)/shard_map/ppermute | solution.py:448
  98.6 2.0 %collective-permute-start.24 = (f32[264,512]{1,0:T(8,128)S(1)}, f32[264,512]{1,0:T(8,128)S(1)}, u32[]{:S(2)}, u32[]{:S(2)}) collective-permute-start(f32[264,512]{1,0:T(8,128)S(1)} %get-tuple-element.75), channel_id=1, source_target_pairs={{0,1},{1,0},{2,3},{3,2},{4,5},{5,4},{6,7},{7,6},{8,9},{9,8},{10,11... | collective-permute-start | bytes 1622024 | tf_op jit(solution)/shard_map/ppermute | solution.py:452
  98.7 18.2 %collective-permute-start.25 = (f32[256,512]{1,0:T(8,128)S(1)}, f32[256,512]{1,0:T(8,128)S(1)}, u32[]{:S(2)}, u32[]{:S(2)}) collective-permute-start(f32[256,512]{1,0:T(8,128)S(1)} %get-tuple-element.77), channel_id=1, source_target_pairs={{0,1},{1,0},{2,3},{3,2},{4,5},{5,4},{6,7},{7,6},{8,9},{9,8},{10,11... | collective-permute-start | bytes 1572872 | tf_op jit(solution)/shard_map/ppermute | solution.py:452
  101.3 16.8 %collective-permute-start.26 = (f16[272,512]{1,0:T(8,128)(2,1)S(1)}, f16[272,512]{1,0:T(8,128)(2,1)S(1)}, u32[]{:S(2)}, u32[]{:S(2)}) collective-permute-start(f16[272,512]{1,0:T(8,128)(2,1)S(1)} %convert_element_type.25), channel_id=1, source_target_pairs={{0,2},{1,3},{2,0},{3,1},{4,6},{5,7},{6,4},{7,5},{8,10},{9,11},{10,... | collective-permute-start | bytes 835592 | tf_op jit(solution)/shard_map/ppermute | solution.py:452
  118.1 2.5 %collective-permute-start.27 = (f32[256,512]{1,0:T(8,128)S(1)}, f32[256,512]{1,0:T(8,128)S(1)}, u32[]{:S(2)}, u32[]{:S(2)}) collective-permute-start(f32[256,512]{1,0:T(8,128)S(1)} %get-tuple-element.85), channel_id=1, source_target_pairs={{0,1},{1,0},{2,3},{3,2},{4,5},{5,4},{6,7},{7,6},{8,9},{9,8},{10,11... | collective-permute-start | bytes 1572872 | tf_op jit(solution)/shard_map/ppermute | solution.py:452
  119.9 6.0 %collective-permute-start.28 = (f32[264,512]{1,0:T(8,128)S(1)}, f32[264,512]{1,0:T(8,128)S(1)}, u32[]{:S(2)}, u32[]{:S(2)}) collective-permute-start(f32[264,512]{1,0:T(8,128)S(1)} %get-tuple-element.89), channel_id=1, source_target_pairs={{0,1},{1,0},{2,3},{3,2},{4,5},{5,4},{6,7},{7,6},{8,9},{9,8},{10,11... | collective-permute-start | bytes 1622024 | tf_op jit(solution)/shard_map/ppermute | solution.py:452
  120.4 5.5 %collective-permute-start.29 = (f32[256,512]{1,0:T(8,128)S(1)}, f32[256,512]{1,0:T(8,128)S(1)}, u32[]{:S(2)}, u32[]{:S(2)}) collective-permute-start(f32[256,512]{1,0:T(8,128)S(1)} %get-tuple-element.90), channel_id=1, source_target_pairs={{0,1},{1,0},{2,3},{3,2},{4,5},{5,4},{6,7},{7,6},{8,9},{9,8},{10,11... | collective-permute-start | bytes 1572872 | tf_op jit(solution)/shard_map/ppermute | solution.py:452
  121.3 9.5 %collective-permute-start.33 = (f16[272,512]{1,0:T(8,128)(2,1)S(1)}, f16[272,512]{1,0:T(8,128)(2,1)S(1)}, u32[]{:S(2)}, u32[]{:S(2)}) collective-permute-start(f16[272,512]{1,0:T(8,128)(2,1)S(1)} %convert_element_type.31), channel_id=1, source_target_pairs={{0,2},{1,3},{2,0},{3,1},{4,6},{5,7},{6,4},{7,5},{8,10},{9,11},{10,... | collective-permute-start | bytes 835592 | tf_op jit(solution)/shard_map/ppermute | solution.py:452
  125.3 5.5 %collective-permute-start.32 = (f32[256,512]{1,0:T(8,128)S(1)}, f32[256,512]{1,0:T(8,128)S(1)}, u32[]{:S(2)}, u32[]{:S(2)}) collective-permute-start(f32[256,512]{1,0:T(8,128)S(1)} %get-tuple-element.104), channel_id=1, source_target_pairs={{0,1},{1,0},{2,3},{3,2},{4,5},{5,4},{6,7},{7,6},{8,9},{9,8},{10,11... | collective-permute-start | bytes 1572872 | tf_op jit(solution)/shard_map/ppermute | solution.py:452
  125.5 17.6 %collective-permute-start.30 = (f32[512,512]{1,0:T(8,128)S(1)}, f32[512,512]{1,0:T(8,128)S(1)}, u32[]{:S(2)}, u32[]{:S(2)}) collective-permute-start(f32[512,512]{1,0:T(8,128)S(1)} %get-tuple-element.95), channel_id=1, source_target_pairs={{0,1},{1,0},{2,3},{3,2},{4,5},{5,4},{6,7},{7,6},{8,9},{9,8},{10,11... | collective-permute-start | bytes 3145736 | tf_op jit(solution)/shard_map/ppermute | solution.py:452
  126.9 15.1 %collective-permute-start.31 = (f16[528,512]{1,0:T(8,128)(2,1)S(1)}, f16[528,512]{1,0:T(8,128)(2,1)S(1)}, u32[]{:S(2)}, u32[]{:S(2)}) collective-permute-start(f16[528,512]{1,0:T(8,128)(2,1)S(1)} %convert_element_type.26), channel_id=1, source_target_pairs={{0,2},{1,3},{2,0},{3,1},{4,6},{5,7},{6,4},{7,5},{8,10},{9,11},{10,... | collective-permute-start | bytes 1622024 | tf_op jit(solution)/shard_map/ppermute | solution.py:452
  127.5 3.5 %copy-start.3 = (f32[512,512]{1,0:T(8,128)S(1)}, f32[512,512]{1,0:T(8,128)}, u32[]{:S(2)}) copy-start(f32[512,512]{1,0:T(8,128)} %moment) | copy-start | bytes 3145732
  127.5 3.5 %copy-start.4 = (f32[512,512]{1,0:T(8,128)S(1)}, f32[512,512]{1,0:T(8,128)}, u32[]{:S(2)}) copy-start(f32[512,512]{1,0:T(8,128)} %square) | copy-start | bytes 3145732
  131.0 11.0 %copy-start.7 = (f32[128]{0:T(128)S(1)}, f32[128]{0:T(128)}, u32[]{:S(2)}) copy-start(f32[128]{0:T(128)} %param.12) | copy-start | bytes 1540
  131.0 11.0 %copy-start.8 = (f32[128]{0:T(128)S(1)}, f32[128]{0:T(128)}, u32[]{:S(2)}) copy-start(f32[128]{0:T(128)} %param.16) | copy-start | bytes 1540
  131.0 11.0 %copy-start.9 = (f32[128]{0:T(128)S(1)}, f32[128]{0:T(128)}, u32[]{:S(2)}) copy-start(f32[128]{0:T(128)} %param.17) | copy-start | bytes 1540
  131.0 12.1 %copy-start.2 = (f32[512,512]{1,0:T(8,128)S(1)}, f32[512,512]{1,0:T(8,128)}, u32[]{:S(2)}) copy-start(f32[512,512]{1,0:T(8,128)} %refs_0_.3) | copy-start | bytes 3145732
  131.0 12.1 %copy-start.10 = (f32[512,512]{1,0:T(8,128)S(1)}, f32[512,512]{1,0:T(8,128)}, u32[]{:S(2)}) copy-start(f32[512,512]{1,0:T(8,128)} %param.14) | copy-start | bytes 3145732
  131.1 12.1 %copy-start.11 = (f32[512,512]{1,0:T(8,128)S(1)}, f32[512,512]{1,0:T(8,128)}, u32[]{:S(2)}) copy-start(f32[512,512]{1,0:T(8,128)} %param.15) | copy-start | bytes 3145732

commit v14 on v13

--- a/solution.py
+++ b/solution.py
@@ -233,42 +233,39 @@
         out[...] = dec[pl.ds(pl.multiple_of(jnp.where(second, half, 0), half), half), :]
 
 
-def split_body(place, rows, first, second):
-    edge = first.shape[0]
-    first[...] = rows[:edge]
-    second[...] = rows[edge:]
-
-
 def turn_body(place, full, turned):
     turned[...] = full[...].T
 
 
-def error_body(
-    place, own, low, high, across, dec0, dec1, dec2, dec3, row0, row1, row2, *refs
-):
-    first, second, inputs, error = refs
+def rebuilt_error(place, t, codes, dec, row, inputs):
     z, i = place[0], place[1]
-    half = row0.shape[0] // 3
-    edge = first.shape[0]
+    half = row.shape[0] // 3
     shift = pl.multiple_of(jnp.where(z >= 2, half, 0), half)
-    for t in range(4):
-        dec = (dec0, dec1, dec2, dec3)[t]
-        lefts = (own, low, high, across)
-        if t < 3:
-            row = (row0, row1, row2)[t]
-            rights = [row[m * half : (m + 1) * half, :] for m in range(3)]
-        else:
-            middle = jnp.concatenate([first[half:], second[: edge - half]], axis=0)
-            rights = [first[:half], middle, second[edge - half :]]
-        rights = [dec[pl.ds(shift, half), :]] + rights
-        total = jnp.zeros((own.shape[0], half), F32)
-        for left, right in zip(lefts, rights):
-            total += lax.dot_general(
-                left[...], right, (((1,), (1,)), ((), ())), preferred_element_type=F32
-            )
-        q = i ^ t
-        given = inputs[:, columns(q * 2 * half + shift, half)].astype(F32)
-        error[:, columns(q * half, half)] = (given - total).astype(BF16)
+    rights = [dec[pl.ds(shift, half), :]] + [row[m * half : (m + 1) * half, :] for m in range(3)]
+    total = jnp.zeros((codes[0].shape[0], half), F32)
+    for left, right in zip(codes, rights):
+        total += lax.dot_general(
+            left[...], right, (((1,), (1,)), ((), ())), preferred_element_type=F32
+        )
+    given = inputs[:, columns((i ^ t) * 2 * half + shift, half)].astype(F32)
+    return (given - total).astype(BF16)
+
+
+def own_error_body(place, own, low, high, across, dec0, dec2, row0, row2, inputs, out):
+    half = out.shape[1] // 2
+    codes = (own, low, high, across)
+    out[:, :half] = rebuilt_error(place, 0, codes, dec0, row0, inputs)
+    out[:, half:] = rebuilt_error(place, 2, codes, dec2, row2, inputs)
+
+
+def error_body(place, own, low, high, across, dec1, dec3, row1, row3, inputs, made, error):
+    i = place[1]
+    half = error.shape[1] // 4
+    codes = (own, low, high, across)
+    error[:, columns(i * half, half)] = made[:, :half]
+    error[:, columns((i ^ 2) * half, half)] = made[:, half:]
+    error[:, columns((i ^ 1) * half, half)] = rebuilt_error(place, 1, codes, dec1, row1, inputs)
+    error[:, columns((i ^ 3) * half, half)] = rebuilt_error(place, 3, codes, dec3, row3, inputs)
 
 
 def pick(place, middle, end, out):
@@ -517,29 +514,32 @@
     )
     rows_chip = flip(rows_own, 2, (1, 2))
     rows_core = flip(behind(rows_own, codes), 1, (1, 2))
-    halves = local_kernel(
-        split_body,
-        [shape((3 * half // 2, latents), BF16)] * 2,
-        place,
+    rows_both = flip(behind(rows_chip, codes_across), 1, (1, 2))
+
+    all_codes = codes, codes_low, codes_high, codes_across
+    (made,) = local_kernel(
+        own_error_body,
+        [shape((count, features // 4), BF16)],
+        place,
+        *all_codes,
+        dec[0],
+        dec[2],
+        rows_own,
         rows_chip,
-        after=(codes_across,),
-    )
-    rows_both = [flip(piece, 1, (1, 2)) for piece in halves]
-
+        inputs,
+        cost=NOTABLE,
+    )
     (own_error,) = local_kernel(
         error_body,
         [shape((count, features // 2), BF16)],
         place,
-        codes,
-        codes_low,
-        codes_high,
-        codes_across,
-        *dec,
-        rows_own,
+        *all_codes,
+        dec[1],
+        dec[3],
         rows_core,
-        rows_chip,
-        *rows_both,
+        rows_both,
         inputs,
+        made,
     )
     swapped = along(own_error, [(1, 2), (2, 1)])
     passed = along(own_error, [(1, 0), (2, 3)])

time: 146 us -> 146 us (level)
  starting transfers between devices: 50.3 us -> 47.3 us
  waiting for transfers between devices: 67.3 us -> 70.1 us
    ppermute x14, waiting for transfers between devices: 53.9 us -> 56.8 us  [along(): return lax.ppermute(value, 'latent', pairs)]
    ppermute x20 -> x19, starting transfers between devices: 11.6 us -> 9.98 us  [flip(): return lax.ppermute(value, ('latent', 'dp'), pairs)]
    ppermute x20 -> x19, waiting for transfers between devices: 13.3 us -> 13.3 us  [flip(): return lax.ppermute(value, ('latent', 'dp'), pairs)]
  transfers between devices with their start and end apart: 34 -> 33, of which waited for: 12 -> 12; matrix products, arithmetic and copies ran while one was open for 0% -> 0% of each run, Pallas kernels for 13% -> 13%
where the time goes in v14:
time: 146 us; the launch traced here: 145 us
  waiting for transfers between devices  70.1 us (48%)
  starting transfers between devices  47.3 us (32%)
  Pallas kernels  21.8 us (15%)
  other arithmetic  2.92 us (2%)
  local copies, waits for them, and re-layouts  2.06 us (1%)
    ppermute x14, waiting for transfers between devices, along(): return lax.ppermute(value, 'latent', pairs)  56.8 us
    ppermute x14, starting transfers between devices, along(): return lax.ppermute(value, 'latent', pairs)  37.3 us
    pallas_call x16, Pallas kernels, local_kernel(): pl.pallas_call(run, out_shape=outs, in_specs=[SMEM] + [VMEM] * len(args)...  18.9 us
    ppermute x19, waiting for transfers between devices, flip(): return lax.ppermute(value, ('latent', 'dp'), pairs)  13.3 us
    ppermute x19, starting transfers between devices, flip(): return lax.ppermute(value, ('latent', 'dp'), pairs)  9.98 us
    pallas_call x1, Pallas kernels, line_shards(): pl.pallas_call(functools.partial(decoder_step_body, rows), grid=(4,), out...  2.94 us
  transfers between devices with their start and end apart: 33, of which 12 were waited for; matrix products, arithmetic and copies ran while one was open for 0% of the time, Pallas kernels for 13%

profile of v14, /device:TPU:0, one launch (start us, length us, event | category | flops | bytes accessed | tf_op | source)
XLA Modules:
  0.0 145.4 jit_solution(1196725089408650048)
XLA Ops:
  0.7 1.3 copy-done.1
  2.0 0.7 copy-done.6
  2.7 0.6 shard_map.178.refs_6_
  3.8 5.8 %collective-permute-start.2 = (bf16[384,512]{1,0:T(8,128)(2,1)S(1)}, bf16[384,512]{1,0:T(8,128)(2,1)S(1)}, u32[]{:S(2)}, u32[]{:S(2)}) collective-permute-start(bf16[384,512]{1,0:T(8,128)(2,1)S(1)} %copy-done.5), channel_id=1, source_target_pairs={{0,8},{12,4},{1,9},{13,5},{2,10},{14,6},{3,11},{15,7},{16,24},{28,... | collective-permute-start | bytes 1179656 | tf_op jit(solution)/shard_map/ppermute | solution.py:445
  9.6 1.3 collective-permute-start.1
  10.9 4.6 %collective-permute-start = (bf16[384,512]{1,0:T(8,128)(2,1)S(1)}, bf16[384,512]{1,0:T(8,128)(2,1)S(1)}, u32[]{:S(2)}, u32[]{:S(2)}) collective-permute-start(bf16[384,512]{1,0:T(8,128)(2,1)S(1)} %copy-done.5), channel_id=1, source_target_pairs={{0,4},{4,8},{8,12},{1,5},{5,9},{9,13},{2,6},{6,10},{10,14},{3,7},{... | collective-permute-start | bytes 1179656 | tf_op jit(solution)/shard_map/ppermute | solution.py:445
  15.5 1.6 %collective-permute-start.6 = (bf16[528,512]{1,0:T(8,128)(2,1)S(1)}, bf16[528,512]{1,0:T(8,128)(2,1)S(1)}, u32[]{:S(2)}, u32[]{:S(2)}) collective-permute-start(bf16[528,512]{1,0:T(8,128)(2,1)S(1)} %shard_map.178.refs_6_), channel_id=1, source_target_pairs={{0,2},{1,3},{2,0},{3,1},{4,6},{5,7},{6,4},{7,5},{8,10},{9,11},{10,... | collective-permute-start | bytes 1622024 | tf_op jit(solution)/shard_map/ppermute | solution.py:449
  17.1 0.6 shard_map.179.refs_0_.refs_4_.refs_3_
  18.3 0.8 collective-permute-done.2.refs_3_
  19.1 1.3 collective-permute-start.4
  21.0 1.6 %collective-permute-done.1.refs_1_.refs_2_ = bf16[384,512]{1,0:T(8,128)(2,1)S(1)} collective-permute-done((bf16[384,512]{1,0:T(8,128)(2,1)S(1)}, bf16[384,512]{1,0:T(8,128)(2,1)S(1)}, u32[]{:S(2)}, u32[]{:S(2)}) %collective-permute-start.1) | collective-permute-done | bytes 393248 | tf_op jit(solution)/shard_map/ppermute | solution.py:445
  22.6 8.4 %collective-permute-start.8 = (bf16[256,512]{1,0:T(8,128)(2,1)S(1)}, bf16[256,512]{1,0:T(8,128)(2,1)S(1)}, u32[]{:S(2)}, u32[]{:S(2)}) collective-permute-start(bf16[256,512]{1,0:T(8,128)(2,1)S(1)} %get-tuple-element.61), channel_id=1, source_target_pairs={{0,4},{4,8},{1,5},{5,9},{2,6},{6,10},{3,7},{7,11},{16,20},{20,24},... | collective-permute-start | bytes 786440 | tf_op jit(solution)/shard_map/ppermute | solution.py:445
  31.0 0.7 collective-permute-start.10
  31.7 5.2 %collective-permute-start.11 = (bf16[256,512]{1,0:T(8,128)(2,1)S(1)}, bf16[256,512]{1,0:T(8,128)(2,1)S(1)}, u32[]{:S(2)}, u32[]{:S(2)}) collective-permute-start(bf16[256,512]{1,0:T(8,128)(2,1)S(1)} %get-tuple-element.65), channel_id=1, source_target_pairs={{0,8},{12,4},{1,9},{13,5},{2,10},{14,6},{3,11},{15,7},{16,24},{28,... | collective-permute-start | bytes 786440 | tf_op jit(solution)/shard_map/ppermute | solution.py:445
  37.6 1.3 collective-permute-start.3
  38.9 1.8 %collective-permute-done.9.refs_5_.refs_6_ = bf16[528,512]{1,0:T(8,128)(2,1)S(1)} collective-permute-done((bf16[528,512]{1,0:T(8,128)(2,1)S(1)}, bf16[528,512]{1,0:T(8,128)(2,1)S(1)}, u32[]{:S(2)}, u32[]{:S(2)}) %collective-permute-start.9) | collective-permute-done | bytes 540704 | tf_op jit(solution)/shard_map/ppermute | solution.py:449
  41.3 1.1 collective-permute-done.11
  42.4 0.7 collective-permute-start.18
  43.1 6.2 %collective-permute-done.3.refs_4_ = bf16[384,512]{1,0:T(8,128)(2,1)S(1)} collective-permute-done((bf16[384,512]{1,0:T(8,128)(2,1)S(1)}, bf16[384,512]{1,0:T(8,128)(2,1)S(1)}, u32[]{:S(2)}, u32[]{:S(2)}) %collective-permute-start.3) | collective-permute-done | bytes 393248 | tf_op jit(solution)/shard_map/ppermute | solution.py:445
  49.4 1.8 %shard_map.181 = (bf16[384,512]{1,0:T(8,128)(2,1)S(1)}, bf16[384,512]{1,0:T(8,128)(2,1)S(1)}, bf16[384,2048]{1,0:T(8,128)(2,1)S(1)}, f32[1,512]{1,0:T(1,128)S(1)}) custom-call(s32[2]{0:T(128)S(1)} %pad_add_fusion.place, bf16[384,512]{1,0:T(8,128)(2,1)S(1)} %copy-done.5, bf16[384,512]{1,0:T(8,128)(2,1)S(1)} %collective-permute-done.refs_0_.refs_1_, ...), custom_call_target="tpu_custom_call" | custom-call | flops 1 | bytes 1 | tf_op jit(solution)/shard_map/pallas_call | solution.py:121
  51.2 1.9 %collective-permute-start.14 = (bf16[384,512]{1,0:T(8,128)(2,1)S(1)}, bf16[384,512]{1,0:T(8,128)(2,1)S(1)}, u32[]{:S(2)}, u32[]{:S(2)}) collective-permute-start(bf16[384,512]{1,0:T(8,128)(2,1)S(1)} %get-tuple-element.68.refs_0_.refs_2_.refs_4_), channel_id=1, source_target_pairs={{0,8},{12,4},{1,9},{13,5},{2,10},{14,6},{3,11},{15,7},{16,24},{28,... | collective-permute-start | bytes 1179656 | tf_op jit(solution)/shard_map/ppermute | solution.py:445
  53.0 0.7 collective-permute-start.16
  53.7 2.9 %collective-permute-start.15 = (bf16[384,512]{1,0:T(8,128)(2,1)S(1)}, bf16[384,512]{1,0:T(8,128)(2,1)S(1)}, u32[]{:S(2)}, u32[]{:S(2)}) collective-permute-start(bf16[384,512]{1,0:T(8,128)(2,1)S(1)} %get-tuple-element.68.refs_0_.refs_2_.refs_4_), channel_id=1, source_target_pairs={{0,4},{4,8},{1,5},{5,9},{2,6},{6,10},{3,7},{7,11},{16,20},{20,24},... | collective-permute-start | bytes 1179656 | tf_op jit(solution)/shard_map/ppermute | solution.py:445
  56.7 0.7 collective-permute-start.17
  57.4 5.1 %collective-permute-done.14.refs_1_.refs_3_ = bf16[384,512]{1,0:T(8,128)(2,1)S(1)} collective-permute-done((bf16[384,512]{1,0:T(8,128)(2,1)S(1)}, bf16[384,512]{1,0:T(8,128)(2,1)S(1)}, u32[]{:S(2)}, u32[]{:S(2)}) %collective-permute-start.14) | collective-permute-done | bytes 393248 | tf_op jit(solution)/shard_map/ppermute | solution.py:445
  62.5 0.7 collective-permute-start.19
  63.2 7.0 %collective-permute-done.15.refs_1_ = bf16[384,512]{1,0:T(8,128)(2,1)S(1)} collective-permute-done((bf16[384,512]{1,0:T(8,128)(2,1)S(1)}, bf16[384,512]{1,0:T(8,128)(2,1)S(1)}, u32[]{:S(2)}, u32[]{:S(2)}) %collective-permute-start.15) | collective-permute-done | bytes 393248 | tf_op jit(solution)/shard_map/ppermute | solution.py:445
  70.2 1.5 %shard_map.183.refs_9_ = bf16[384,512]{1,0:T(8,128)(2,1)S(1)} custom-call(s32[2]{0:T(128)S(1)} %pad_add_fusion.place, bf16[384,512]{1,0:T(8,128)(2,1)S(1)} %get-tuple-element.68.refs_0_.refs_2_.refs_4_, bf16[384,512]{1,0:T(8,128)(2,1)S(1)} %collective-permute-done.15.refs_1_, bf16[384,512]{1,0:T(8,128)(2,1)S(1)} %collective-permute-done.16.refs_2_, ...), custom_call_target="tpu_custom_call" | custom-call | flops 10000000000 | bytes 1 | tf_op jit(solution)/shard_map/pallas_call | solution.py:121
  71.8 1.6 %shard_map.184.refs_0_ = bf16[384,1024]{1,0:T(8,128)(2,1)S(1)} custom-call(s32[2]{0:T(128)S(1)} %pad_add_fusion.place, bf16[384,512]{1,0:T(8,128)(2,1)S(1)} %get-tuple-element.68.refs_0_.refs_2_.refs_4_, bf16[384,512]{1,0:T(8,128)(2,1)S(1)} %collective-permute-done.15.refs_1_, bf16[384,512]{1,0:T(8,128)(2,1)S(1)} %collective-permute-done.16.refs_2_, ...), custom_call_target="tpu_custom_call" | custom-call | flops 1 | bytes 1 | tf_op jit(solution)/shard_map/pallas_call | solution.py:121
  73.4 1.3 collective-permute-start.22
  74.7 0.7 collective-permute-start.20
  75.4 1.3 collective-permute-start.21
  76.7 20.1 %collective-permute-done.22.refs_1_ = bf16[384,1024]{1,0:T(8,128)(2,1)S(1)} collective-permute-done((bf16[384,1024]{1,0:T(8,128)(2,1)S(1)}, bf16[384,1024]{1,0:T(8,128)(2,1)S(1)}, u32[]{:S(2)}, u32[]{:S(2)}) %collective-permute-start.22) | collective-permute-done | bytes 786464 | tf_op jit(solution)/shard_map/ppermute | solution.py:445
  96.8 1.8 %shard_map.185 = (f32[384,512]{1,0:T(8,128)S(1)}, bf16[384,1024]{1,0:T(8,128)(2,1)S(1)}, f32[264,512]{1,0:T(8,128)S(1)}, f32[256,512]{1,0:T(8,128)S(1)}, f32[256,512]{1,0:T(8,128)S(1)}, /*index=5*/f32[256,512]{1,0:T(8,128)S(1)}) custom-call(s32[2]{0:T(128)S(1)} %pad_add_fusion.place, bf16[384,1024]{1,0:T(8,128)(2,1)S(1)} %shard_map.184.refs_0_, ...), custom_call_target="tpu_custom_call" | custom-call | flops 1 | bytes 1 | tf_op jit(solution)/shard_map/pallas_call | solution.py:121
  99.1 1.0 shard_map.182.refs_7_.refs_0_
  100.5 0.7 shard_map.186
  101.9 14.9 %collective-permute-done.21.refs_1_ = bf16[384,1024]{1,0:T(8,128)(2,1)S(1)} collective-permute-done((bf16[384,1024]{1,0:T(8,128)(2,1)S(1)}, bf16[384,1024]{1,0:T(8,128)(2,1)S(1)}, u32[]{:S(2)}, u32[]{:S(2)}) %collective-permute-start.21) | collective-permute-done | bytes 786464 | tf_op jit(solution)/shard_map/ppermute | solution.py:445
  116.8 1.3 shard_map.187
  118.1 1.7 %shard_map.188 = (bf16[384,512]{1,0:T(8,128)(2,1)S(1)}, f32[1,512]{1,0:T(1,128)S(1)}, f32[1,512]{1,0:T(1,128)S(1)}, f32[264,512]{1,0:T(8,128)S(1)}, f32[256,512]{1,0:T(8,128)S(1)}) custom-call(s32[2]{0:T(128)S(1)} %pad_add_fusion.place, bf16[384,1024]{1,0:T(8,128)(2,1)S(1)} %get-tuple-element.76.refs_0_.refs_3_, f32[384,512]{1,0:T(8,128)S(1)} %get-tuple-element.78.refs_1_, ...), custom_call_target="tpu_custom_call" | custom-call | flops 10000000000 | bytes 1 | tf_op jit(solution)/shard_map/pallas_call | solution.py:121
  120.5 0.7 shard_map.189.refs_5_
  121.8 2.5 %shard_map.190 = (bf16[384,512]{1,0:T(8,128)(2,1)}, f32[512,512]{1,0:T(8,128)S(1)}, f32[512,512]{1,0:T(8,128)S(1)}, f32[512,512]{1,0:T(8,128)S(1)}, f32[256,512]{1,0:T(8,128)S(1)}, /*index=5*/f32[256,512]{1,0:T(8,128)S(1)}) custom-call(s32[2]{0:T(128)S(1)} %pad_add_fusion.place, bf16[2048,384]{1,0:T(8,128)(2,1)S(1)} %shard_map.182.refs_7_.refs_0_, ...), custom_call_target="tpu_custom_call" | custom-call | flops 1 | bytes 1 | tf_op jit(solution)/shard_map/pallas_call | solution.py:121
  124.9 0.8 shard_map.191
  125.9 1.6 %collective-permute-start.30 = (f16[528,512]{1,0:T(8,128)(2,1)S(1)}, f16[528,512]{1,0:T(8,128)(2,1)S(1)}, u32[]{:S(2)}, u32[]{:S(2)}) collective-permute-start(f16[528,512]{1,0:T(8,128)(2,1)S(1)} %convert_element_type.26), channel_id=1, source_target_pairs={{0,2},{1,3},{2,0},{3,1},{4,6},{5,7},{6,4},{7,5},{8,10},{9,11},{10,... | collective-permute-start | bytes 1622024 | tf_op jit(solution)/shard_map/ppermute | solution.py:449
  127.6 3.2 %collective-permute-done.32 = f16[272,512]{1,0:T(8,128)(2,1)S(1)} collective-permute-done((f16[272,512]{1,0:T(8,128)(2,1)S(1)}, f16[272,512]{1,0:T(8,128)(2,1)S(1)}, u32[]{:S(2)}, u32[]{:S(2)}) %collective-permute-start.32) | collective-permute-done | bytes 278560 | tf_op jit(solution)/shard_map/ppermute | solution.py:449
  131.0 2.9 %shard_map.193 = (f32[512,512]{1,0:T(8,128)}, f32[512,512]{1,0:T(8,128)}, f32[512,512]{1,0:T(8,128)}) custom-call(s32[2]{0:T(128)S(1)} %pad_add_fusion.place, f32[512,512]{1,0:T(8,128)S(1)} %copy-done, f32[512,512]{1,0:T(8,128)S(1)} %copy-done.3, f32[512,512]{1,0:T(8,128)S(1)} %copy-done.4, f32[256,512]{1,0:T(8,128)S(1)} %multiply_add_fusion.3.near, ...), custom_call_target="tpu_custom_call" | custom-call | flops 1 | bytes 1 | tf_op jit(solution)/shard_map/pallas_call | solution.py:649
  134.0 7.9 %collective-permute-done.30 = f16[528,512]{1,0:T(8,128)(2,1)S(1)} collective-permute-done((f16[528,512]{1,0:T(8,128)(2,1)S(1)}, f16[528,512]{1,0:T(8,128)(2,1)S(1)}, u32[]{:S(2)}, u32[]{:S(2)}) %collective-permute-start.30) | collective-permute-done | bytes 540704 | tf_op jit(solution)/shard_map/ppermute | solution.py:449
  142.0 1.1 shard_map.192
  143.1 2.3 %divide_subtract_fusion = (f32[512,512]{1,0:T(8,128)}, f32[512,512]{1,0:T(8,128)}, f32[512,512]{1,0:T(8,128)}) fusion(f32[512,512]{1,0:T(8,128)S(1)} %copy-done.2, f32[512]{0:T(512)S(1)} %bitcast.15, f16[528,512]{1,0:T(8,128)(2,1)S(1)} %collective-permute-done.30, f32[512,512]{1,0:T(8,128)S(1)} %get-tuple-element.92, ...), kind=kLoop, calls=%fused_computation.2 | loop fusion | flops 4194304 | bytes 8914944 | tf_op jit(solution)/shard_map/sub | solution.py:28
  (74 shorter events, 7.1 us)
Async XLA Ops:
  0.6 16.4 %copy-start = (f32[512,512]{1,0:T(8,128)S(1)}, f32[512,512]{1,0:T(8,128)}, u32[]{:S(2)}) copy-start(f32[512,512]{1,0:T(8,128)} %param.20) | copy-start | bytes 3145732
  0.7 1.3 copy-start.1
  2.0 0.7 copy-start.6
  2.7 1.1 copy-start.5
  3.3 13.8 %collective-permute-start.5 = (bf16[528,512]{1,0:T(8,128)(2,1)S(1)}, bf16[528,512]{1,0:T(8,128)(2,1)S(1)}, u32[]{:S(2)}, u32[]{:S(2)}) collective-permute-start(bf16[528,512]{1,0:T(8,128)(2,1)S(1)} %shard_map.178.refs_6_), channel_id=1, source_target_pairs={{0,1},{1,0},{2,3},{3,2},{4,5},{5,4},{6,7},{7,6},{8,9},{9,8},{10,11... | collective-permute-start | bytes 1622024 | tf_op jit(solution)/shard_map/ppermute | solution.py:449
  3.8 15.3 %collective-permute-start.2 = (bf16[384,512]{1,0:T(8,128)(2,1)S(1)}, bf16[384,512]{1,0:T(8,128)(2,1)S(1)}, u32[]{:S(2)}, u32[]{:S(2)}) collective-permute-start(bf16[384,512]{1,0:T(8,128)(2,1)S(1)} %copy-done.5), channel_id=1, source_target_pairs={{0,8},{12,4},{1,9},{13,5},{2,10},{14,6},{3,11},{15,7},{16,24},{28,... | collective-permute-start | bytes 1179656 | tf_op jit(solution)/shard_map/ppermute | solution.py:445
  9.6 13.0 %collective-permute-start.1 = (bf16[384,512]{1,0:T(8,128)(2,1)S(1)}, bf16[384,512]{1,0:T(8,128)(2,1)S(1)}, u32[]{:S(2)}, u32[]{:S(2)}) collective-permute-start(bf16[384,512]{1,0:T(8,128)(2,1)S(1)} %copy-done.5), channel_id=1, source_target_pairs={{4,0},{8,4},{12,8},{5,1},{9,5},{13,9},{6,2},{10,6},{14,10},{7,3},{... | collective-permute-start | bytes 1179656 | tf_op jit(solution)/shard_map/ppermute | solution.py:445
  10.9 20.1 %collective-permute-start = (bf16[384,512]{1,0:T(8,128)(2,1)S(1)}, bf16[384,512]{1,0:T(8,128)(2,1)S(1)}, u32[]{:S(2)}, u32[]{:S(2)}) collective-permute-start(bf16[384,512]{1,0:T(8,128)(2,1)S(1)} %copy-done.5), channel_id=1, source_target_pairs={{0,4},{4,8},{8,12},{1,5},{5,9},{9,13},{2,6},{6,10},{10,14},{3,7},{... | collective-permute-start | bytes 1179656 | tf_op jit(solution)/shard_map/ppermute | solution.py:445
  15.5 16.2 %collective-permute-start.6 = (bf16[528,512]{1,0:T(8,128)(2,1)S(1)}, bf16[528,512]{1,0:T(8,128)(2,1)S(1)}, u32[]{:S(2)}, u32[]{:S(2)}) collective-permute-start(bf16[528,512]{1,0:T(8,128)(2,1)S(1)} %shard_map.178.refs_6_), channel_id=1, source_target_pairs={{0,2},{1,3},{2,0},{3,1},{4,6},{5,7},{6,4},{7,5},{8,10},{9,11},{10,... | collective-permute-start | bytes 1622024 | tf_op jit(solution)/shard_map/ppermute | solution.py:449
  17.7 23.0 %collective-permute-start.9 = (bf16[528,512]{1,0:T(8,128)(2,1)S(1)}, bf16[528,512]{1,0:T(8,128)(2,1)S(1)}, u32[]{:S(2)}, u32[]{:S(2)}) collective-permute-start(bf16[528,512]{1,0:T(8,128)(2,1)S(1)} %shard_map.179.refs_0_.refs_4_.refs_3_), channel_id=1, source_target_pairs={{0,2},{1,3},{2,0},{3,1},{4,6},{5,7},{6,4},{7,5},{8,10},{9,11},{10,... | collective-permute-start | bytes 1622024 | tf_op jit(solution)/shard_map/ppermute | solution.py:449
  19.1 18.4 %collective-permute-start.4 = (bf16[384,512]{1,0:T(8,128)(2,1)S(1)}, bf16[384,512]{1,0:T(8,128)(2,1)S(1)}, u32[]{:S(2)}, u32[]{:S(2)}) collective-permute-start(bf16[384,512]{1,0:T(8,128)(2,1)S(1)} %collective-permute-done.2.refs_3_), channel_id=1, source_target_pairs={{4,0},{8,12},{5,1},{9,13},{6,2},{10,14},{7,3},{11,15},{20,16},{24,... | collective-permute-start | bytes 1179656 | tf_op jit(solution)/shard_map/ppermute | solution.py:445
  22.6 16.2 %collective-permute-start.8 = (bf16[256,512]{1,0:T(8,128)(2,1)S(1)}, bf16[256,512]{1,0:T(8,128)(2,1)S(1)}, u32[]{:S(2)}, u32[]{:S(2)}) collective-permute-start(bf16[256,512]{1,0:T(8,128)(2,1)S(1)} %get-tuple-element.61), channel_id=1, source_target_pairs={{0,4},{4,8},{1,5},{5,9},{2,6},{6,10},{3,7},{7,11},{16,20},{20,24},... | collective-permute-start | bytes 786440 | tf_op jit(solution)/shard_map/ppermute | solution.py:445
  31.0 9.7 %collective-permute-start.10 = (bf16[256,512]{1,0:T(8,128)(2,1)S(1)}, bf16[256,512]{1,0:T(8,128)(2,1)S(1)}, u32[]{:S(2)}, u32[]{:S(2)}) collective-permute-start(bf16[256,512]{1,0:T(8,128)(2,1)S(1)} %get-tuple-element.63), channel_id=1, source_target_pairs={{8,4},{12,8},{9,5},{13,9},{10,6},{14,10},{11,7},{15,11},{24,20},{2... | collective-permute-start | bytes 786440 | tf_op jit(solution)/shard_map/ppermute | solution.py:445
  31.7 10.6 %collective-permute-start.11 = (bf16[256,512]{1,0:T(8,128)(2,1)S(1)}, bf16[256,512]{1,0:T(8,128)(2,1)S(1)}, u32[]{:S(2)}, u32[]{:S(2)}) collective-permute-start(bf16[256,512]{1,0:T(8,128)(2,1)S(1)} %get-tuple-element.65), channel_id=1, source_target_pairs={{0,8},{12,4},{1,9},{13,5},{2,10},{14,6},{3,11},{15,7},{16,24},{28,... | collective-permute-start | bytes 786440 | tf_op jit(solution)/shard_map/ppermute | solution.py:445
  37.6 11.8 %collective-permute-start.3 = (bf16[384,512]{1,0:T(8,128)(2,1)S(1)}, bf16[384,512]{1,0:T(8,128)(2,1)S(1)}, u32[]{:S(2)}, u32[]{:S(2)}) collective-permute-start(bf16[384,512]{1,0:T(8,128)(2,1)S(1)} %shard_map.177), channel_id=1, source_target_pairs={{4,0},{8,12},{5,1},{9,13},{6,2},{10,14},{7,3},{11,15},{20,16},{24,... | collective-permute-start | bytes 1179656 | tf_op jit(solution)/shard_map/ppermute | solution.py:445
  38.9 10.5 %collective-permute-start.12 = (bf16[528,512]{1,0:T(8,128)(2,1)S(1)}, bf16[528,512]{1,0:T(8,128)(2,1)S(1)}, u32[]{:S(2)}, u32[]{:S(2)}) collective-permute-start(bf16[528,512]{1,0:T(8,128)(2,1)S(1)} %shard_map.179.refs_0_.refs_4_.refs_3_), channel_id=1, source_target_pairs={{0,1},{1,0},{2,3},{3,2},{4,5},{5,4},{6,7},{7,6},{8,9},{9,8},{10,11... | collective-permute-start | bytes 1622024 | tf_op jit(solution)/shard_map/ppermute | solution.py:449
  40.7 8.7 %collective-permute-start.7 = (bf16[528,512]{1,0:T(8,128)(2,1)S(1)}, bf16[528,512]{1,0:T(8,128)(2,1)S(1)}, u32[]{:S(2)}, u32[]{:S(2)}) collective-permute-start(bf16[528,512]{1,0:T(8,128)(2,1)S(1)} %collective-permute-done.6.refs_8_), channel_id=1, source_target_pairs={{0,1},{1,0},{2,3},{3,2},{4,5},{5,4},{6,7},{7,6},{8,9},{9,8},{10,11... | collective-permute-start | bytes 1622024 | tf_op jit(solution)/shard_map/ppermute | solution.py:449
  40.7 8.7 %collective-permute-start.13 = (bf16[528,512]{1,0:T(8,128)(2,1)S(1)}, bf16[528,512]{1,0:T(8,128)(2,1)S(1)}, u32[]{:S(2)}, u32[]{:S(2)}) collective-permute-start(bf16[528,512]{1,0:T(8,128)(2,1)S(1)} %collective-permute-done.9.refs_5_.refs_6_), channel_id=1, source_target_pairs={{0,1},{1,0},{2,3},{3,2},{4,5},{5,4},{6,7},{7,6},{8,9},{9,8},{10,11... | collective-permute-start | bytes 1622024 | tf_op jit(solution)/shard_map/ppermute | solution.py:449
  42.4 15.0 %collective-permute-start.18 = (bf16[768,512]{1,0:T(8,128)(2,1)S(1)}, bf16[768,512]{1,0:T(8,128)(2,1)S(1)}, u32[]{:S(2)}, u32[]{:S(2)}) collective-permute-start(bf16[768,512]{1,0:T(8,128)(2,1)S(1)} %constant_dynamic-update-slice_fusion.refs_10_.refs_6_), channel_id=1, source_target_pairs={{4,6},{5,7},{6,4},{7,5},{8,10},{9,11},{10,8},{11,9},{20,22},{21,23... | collective-permute-start | bytes 2359304 | tf_op jit(solution)/shard_map/ppermute | solution.py:449
  51.2 11.4 %collective-permute-start.14 = (bf16[384,512]{1,0:T(8,128)(2,1)S(1)}, bf16[384,512]{1,0:T(8,128)(2,1)S(1)}, u32[]{:S(2)}, u32[]{:S(2)}) collective-permute-start(bf16[384,512]{1,0:T(8,128)(2,1)S(1)} %get-tuple-element.68.refs_0_.refs_2_.refs_4_), channel_id=1, source_target_pairs={{0,8},{12,4},{1,9},{13,5},{2,10},{14,6},{3,11},{15,7},{16,24},{28,... | collective-permute-start | bytes 1179656 | tf_op jit(solution)/shard_map/ppermute | solution.py:445
  53.0 10.2 %collective-permute-start.16 = (bf16[384,512]{1,0:T(8,128)(2,1)S(1)}, bf16[384,512]{1,0:T(8,128)(2,1)S(1)}, u32[]{:S(2)}, u32[]{:S(2)}) collective-permute-start(bf16[384,512]{1,0:T(8,128)(2,1)S(1)} %get-tuple-element.68.refs_0_.refs_2_.refs_4_), channel_id=1, source_target_pairs={{8,4},{12,8},{9,5},{13,9},{10,6},{14,10},{11,7},{15,11},{24,20},{2... | collective-permute-start | bytes 1179656 | tf_op jit(solution)/shard_map/ppermute | solution.py:445
  53.7 16.5 %collective-permute-start.15 = (bf16[384,512]{1,0:T(8,128)(2,1)S(1)}, bf16[384,512]{1,0:T(8,128)(2,1)S(1)}, u32[]{:S(2)}, u32[]{:S(2)}) collective-permute-start(bf16[384,512]{1,0:T(8,128)(2,1)S(1)} %get-tuple-element.68.refs_0_.refs_2_.refs_4_), channel_id=1, source_target_pairs={{0,4},{4,8},{1,5},{5,9},{2,6},{6,10},{3,7},{7,11},{16,20},{20,24},... | collective-permute-start | bytes 1179656 | tf_op jit(solution)/shard_map/ppermute | solution.py:445
  56.7 15.1 %collective-permute-start.17 = (bf16[768,512]{1,0:T(8,128)(2,1)S(1)}, bf16[768,512]{1,0:T(8,128)(2,1)S(1)}, u32[]{:S(2)}, u32[]{:S(2)}) collective-permute-start(bf16[768,512]{1,0:T(8,128)(2,1)S(1)} %constant_dynamic-update-slice_fusion.refs_10_.refs_6_), channel_id=1, source_target_pairs={{4,5},{5,4},{6,7},{7,6},{8,9},{9,8},{10,11},{11,10},{20,21},{21,20... | collective-permute-start | bytes 2359304 | tf_op jit(solution)/shard_map/ppermute | solution.py:449
  62.5 9.3 %collective-permute-start.19 = (bf16[768,512]{1,0:T(8,128)(2,1)S(1)}, bf16[768,512]{1,0:T(8,128)(2,1)S(1)}, u32[]{:S(2)}, u32[]{:S(2)}) collective-permute-start(bf16[768,512]{1,0:T(8,128)(2,1)S(1)} %collective-permute-done.18.refs_7_), channel_id=1, source_target_pairs={{4,5},{5,4},{6,7},{7,6},{8,9},{9,8},{10,11},{11,10},{20,21},{21,20... | collective-permute-start | bytes 2359304 | tf_op jit(solution)/shard_map/ppermute | solution.py:449
  73.4 23.4 %collective-permute-start.22 = (bf16[384,1024]{1,0:T(8,128)(2,1)S(1)}, bf16[384,1024]{1,0:T(8,128)(2,1)S(1)}, u32[]{:S(2)}, u32[]{:S(2)}) collective-permute-start(bf16[384,1024]{1,0:T(8,128)(2,1)S(1)} %shard_map.184.refs_0_), channel_id=1, source_target_pairs={{4,0},{8,12},{5,1},{9,13},{6,2},{10,14},{7,3},{11,15},{20,16},{24,... | collective-permute-start | bytes 2359304 | tf_op jit(solution)/shard_map/ppermute | solution.py:445
  74.7 22.1 %collective-permute-start.20 = (bf16[384,1024]{1,0:T(8,128)(2,1)S(1)}, bf16[384,1024]{1,0:T(8,128)(2,1)S(1)}, u32[]{:S(2)}, u32[]{:S(2)}) collective-permute-start(bf16[384,1024]{1,0:T(8,128)(2,1)S(1)} %shard_map.184.refs_0_), channel_id=1, source_target_pairs={{4,8},{8,4},{5,9},{9,5},{6,10},{10,6},{7,11},{11,7},{20,24},{24,20... | collective-permute-start | bytes 2359304 | tf_op jit(solution)/shard_map/ppermute | solution.py:445
  75.4 41.4 %collective-permute-start.21 = (bf16[384,1024]{1,0:T(8,128)(2,1)S(1)}, bf16[384,1024]{1,0:T(8,128)(2,1)S(1)}, u32[]{:S(2)}, u32[]{:S(2)}) collective-permute-start(bf16[384,1024]{1,0:T(8,128)(2,1)S(1)} %shard_map.184.refs_0_), channel_id=1, source_target_pairs={{8,0},{4,12},{9,1},{5,13},{10,2},{6,14},{11,3},{7,15},{24,16},{20,... | collective-permute-start | bytes 2359304 | tf_op jit(solution)/shard_map/ppermute | solution.py:445
  98.5 2.0 %collective-permute-start.23 = (f32[264,512]{1,0:T(8,128)S(1)}, f32[264,512]{1,0:T(8,128)S(1)}, u32[]{:S(2)}, u32[]{:S(2)}) collective-permute-start(f32[264,512]{1,0:T(8,128)S(1)} %get-tuple-element.73), channel_id=1, source_target_pairs={{0,1},{1,0},{2,3},{3,2},{4,5},{5,4},{6,7},{7,6},{8,9},{9,8},{10,11... | collective-permute-start | bytes 1622024 | tf_op jit(solution)/shard_map/ppermute | solution.py:449
  98.6 18.2 %collective-permute-start.24 = (f32[256,512]{1,0:T(8,128)S(1)}, f32[256,512]{1,0:T(8,128)S(1)}, u32[]{:S(2)}, u32[]{:S(2)}) collective-permute-start(f32[256,512]{1,0:T(8,128)S(1)} %get-tuple-element.75), channel_id=1, source_target_pairs={{0,1},{1,0},{2,3},{3,2},{4,5},{5,4},{6,7},{7,6},{8,9},{9,8},{10,11... | collective-permute-start | bytes 1572872 | tf_op jit(solution)/shard_map/ppermute | solution.py:449
  101.3 16.8 %collective-permute-start.25 = (f16[272,512]{1,0:T(8,128)(2,1)S(1)}, f16[272,512]{1,0:T(8,128)(2,1)S(1)}, u32[]{:S(2)}, u32[]{:S(2)}) collective-permute-start(f16[272,512]{1,0:T(8,128)(2,1)S(1)} %convert_element_type.25), channel_id=1, source_target_pairs={{0,2},{1,3},{2,0},{3,1},{4,6},{5,7},{6,4},{7,5},{8,10},{9,11},{10,... | collective-permute-start | bytes 835592 | tf_op jit(solution)/shard_map/ppermute | solution.py:449
  118.0 2.5 %collective-permute-start.26 = (f32[256,512]{1,0:T(8,128)S(1)}, f32[256,512]{1,0:T(8,128)S(1)}, u32[]{:S(2)}, u32[]{:S(2)}) collective-permute-start(f32[256,512]{1,0:T(8,128)S(1)} %get-tuple-element.83), channel_id=1, source_target_pairs={{0,1},{1,0},{2,3},{3,2},{4,5},{5,4},{6,7},{7,6},{8,9},{9,8},{10,11... | collective-permute-start | bytes 1572872 | tf_op jit(solution)/shard_map/ppermute | solution.py:449
  119.9 5.1 %collective-permute-start.27 = (f32[264,512]{1,0:T(8,128)S(1)}, f32[264,512]{1,0:T(8,128)S(1)}, u32[]{:S(2)}, u32[]{:S(2)}) collective-permute-start(f32[264,512]{1,0:T(8,128)S(1)} %get-tuple-element.87), channel_id=1, source_target_pairs={{0,1},{1,0},{2,3},{3,2},{4,5},{5,4},{6,7},{7,6},{8,9},{9,8},{10,11... | collective-permute-start | bytes 1622024 | tf_op jit(solution)/shard_map/ppermute | solution.py:449
  120.4 4.5 %collective-permute-start.28 = (f32[256,512]{1,0:T(8,128)S(1)}, f32[256,512]{1,0:T(8,128)S(1)}, u32[]{:S(2)}, u32[]{:S(2)}) collective-permute-start(f32[256,512]{1,0:T(8,128)S(1)} %get-tuple-element.88), channel_id=1, source_target_pairs={{0,1},{1,0},{2,3},{3,2},{4,5},{5,4},{6,7},{7,6},{8,9},{9,8},{10,11... | collective-permute-start | bytes 1572872 | tf_op jit(solution)/shard_map/ppermute | solution.py:449
  121.2 9.5 %collective-permute-start.32 = (f16[272,512]{1,0:T(8,128)(2,1)S(1)}, f16[272,512]{1,0:T(8,128)(2,1)S(1)}, u32[]{:S(2)}, u32[]{:S(2)}) collective-permute-start(f16[272,512]{1,0:T(8,128)(2,1)S(1)} %convert_element_type.31), channel_id=1, source_target_pairs={{0,2},{1,3},{2,0},{3,1},{4,6},{5,7},{6,4},{7,5},{8,10},{9,11},{10,... | collective-permute-start | bytes 835592 | tf_op jit(solution)/shard_map/ppermute | solution.py:449
  124.3 6.4 %collective-permute-start.31 = (f32[256,512]{1,0:T(8,128)S(1)}, f32[256,512]{1,0:T(8,128)S(1)}, u32[]{:S(2)}, u32[]{:S(2)}) collective-permute-start(f32[256,512]{1,0:T(8,128)S(1)} %get-tuple-element.102), channel_id=1, source_target_pairs={{0,1},{1,0},{2,3},{3,2},{4,5},{5,4},{6,7},{7,6},{8,9},{9,8},{10,11... | collective-permute-start | bytes 1572872 | tf_op jit(solution)/shard_map/ppermute | solution.py:449
  124.5 18.5 %collective-permute-start.29 = (f32[512,512]{1,0:T(8,128)S(1)}, f32[512,512]{1,0:T(8,128)S(1)}, u32[]{:S(2)}, u32[]{:S(2)}) collective-permute-start(f32[512,512]{1,0:T(8,128)S(1)} %get-tuple-element.93), channel_id=1, source_target_pairs={{0,1},{1,0},{2,3},{3,2},{4,5},{5,4},{6,7},{7,6},{8,9},{9,8},{10,11... | collective-permute-start | bytes 3145736 | tf_op jit(solution)/shard_map/ppermute | solution.py:449
  125.9 16.0 %collective-permute-start.30 = (f16[528,512]{1,0:T(8,128)(2,1)S(1)}, f16[528,512]{1,0:T(8,128)(2,1)S(1)}, u32[]{:S(2)}, u32[]{:S(2)}) collective-permute-start(f16[528,512]{1,0:T(8,128)(2,1)S(1)} %convert_element_type.26), channel_id=1, source_target_pairs={{0,2},{1,3},{2,0},{3,1},{4,6},{5,7},{6,4},{7,5},{8,10},{9,11},{10,... | collective-permute-start | bytes 1622024 | tf_op jit(solution)/shard_map/ppermute | solution.py:449
  127.5 3.5 %copy-start.3 = (f32[512,512]{1,0:T(8,128)S(1)}, f32[512,512]{1,0:T(8,128)}, u32[]{:S(2)}) copy-start(f32[512,512]{1,0:T(8,128)} %moment) | copy-start | bytes 3145732
  127.5 3.5 %copy-start.4 = (f32[512,512]{1,0:T(8,128)S(1)}, f32[512,512]{1,0:T(8,128)}, u32[]{:S(2)}) copy-start(f32[512,512]{1,0:T(8,128)} %square) | copy-start | bytes 3145732
  131.0 11.0 %copy-start.7 = (f32[128]{0:T(128)S(1)}, f32[128]{0:T(128)}, u32[]{:S(2)}) copy-start(f32[128]{0:T(128)} %param.12) | copy-start | bytes 1540
  131.0 11.0 %copy-start.8 = (f32[128]{0:T(128)S(1)}, f32[128]{0:T(128)}, u32[]{:S(2)}) copy-start(f32[128]{0:T(128)} %param.16) | copy-start | bytes 1540
  131.0 11.0 %copy-start.9 = (f32[128]{0:T(128)S(1)}, f32[128]{0:T(128)}, u32[]{:S(2)}) copy-start(f32[128]{0:T(128)} %param.17) | copy-start | bytes 1540
  131.0 12.1 %copy-start.2 = (f32[512,512]{1,0:T(8,128)S(1)}, f32[512,512]{1,0:T(8,128)}, u32[]{:S(2)}) copy-start(f32[512,512]{1,0:T(8,128)} %refs_0_.3) | copy-start | bytes 3145732
  131.0 12.0 %copy-start.10 = (f32[512,512]{1,0:T(8,128)S(1)}, f32[512,512]{1,0:T(8,128)}, u32[]{:S(2)}) copy-start(f32[512,512]{1,0:T(8,128)} %param.14) | copy-start | bytes 3145732
  131.0 12.0 %copy-start.11 = (f32[512,512]{1,0:T(8,128)S(1)}, f32[512,512]{1,0:T(8,128)}, u32[]{:S(2)}) copy-start(f32[512,512]{1,0:T(8,128)} %param.15) | copy-start | bytes 3145732

commit v15 on v14

--- a/solution.py
+++ b/solution.py
@@ -241,7 +241,13 @@
     z, i = place[0], place[1]
     half = row.shape[0] // 3
     shift = pl.multiple_of(jnp.where(z >= 2, half, 0), half)
-    rights = [dec[pl.ds(shift, half), :]] + [row[m * half : (m + 1) * half, :] for m in range(3)]
+    below = pl.multiple_of(jnp.where(z == 1, 0, half), half)
+    rights = [
+        dec[pl.ds(shift, half), :],
+        row[2 * half :, :],
+        row[pl.ds(half - below, half), :],
+        row[pl.ds(below, half), :],
+    ]
     total = jnp.zeros((codes[0].shape[0], half), F32)
     for left, right in zip(codes, rights):
         total += lax.dot_general(
@@ -251,17 +257,17 @@
     return (given - total).astype(BF16)
 
 
-def own_error_body(place, own, low, high, across, dec0, dec2, row0, row2, inputs, out):
+def own_error_body(place, own, across, middle, near, dec0, dec2, row0, row2, inputs, out):
     half = out.shape[1] // 2
-    codes = (own, low, high, across)
+    codes = (own, across, middle, near)
     out[:, :half] = rebuilt_error(place, 0, codes, dec0, row0, inputs)
     out[:, half:] = rebuilt_error(place, 2, codes, dec2, row2, inputs)
 
 
-def error_body(place, own, low, high, across, dec1, dec3, row1, row3, inputs, made, error):
+def error_body(place, own, across, middle, near, dec1, dec3, row1, row3, inputs, made, error):
     i = place[1]
     half = error.shape[1] // 4
-    codes = (own, low, high, across)
+    codes = (own, across, middle, near)
     error[:, columns(i * half, half)] = made[:, :half]
     error[:, columns((i ^ 2) * half, half)] = made[:, half:]
     error[:, columns((i ^ 1) * half, half)] = rebuilt_error(place, 1, codes, dec1, row1, inputs)
@@ -506,17 +512,17 @@
         after=(rows_own, dec[1], dec[3]),
         scratch=[pltpu.VMEM((1, latents), F32)],
     )
-    codes_low = along(codes, [(0, 1), (1, 2)])
-    codes_high = along(codes, [(2, 1), (3, 2)])
+    codes_near = along(codes, [(0, 1), (3, 2)])
+    codes_middle = along(codes, [(1, 2), (2, 1)])
     codes_across = along(codes, [(0, 2), (3, 1)])
     (turned,) = local_kernel(
         turn_body, [shape((features, count), BF16)], place, inputs, after=(codes_across,)
     )
     rows_chip = flip(rows_own, 2, (1, 2))
     rows_core = flip(behind(rows_own, codes), 1, (1, 2))
-    rows_both = flip(behind(rows_chip, codes_across), 1, (1, 2))
-
-    all_codes = codes, codes_low, codes_high, codes_across
+    rows_both = flip(behind(rows_chip, codes_middle), 1, (1, 2))
+
+    all_codes = codes, codes_across, codes_middle, codes_near
     (made,) = local_kernel(
         own_error_body,
         [shape((count, features // 4), BF16)],

time: 146 us -> 147 us (level)
  starting transfers between devices: 47.3 us -> 49.4 us
    ppermute x14, starting transfers between devices: 37.3 us -> 39.4 us  [along(): return lax.ppermute(value, 'latent', pairs)]
where the time goes in v15:
time: 147 us
  waiting for transfers between devices  69.3 us (47%)
  starting transfers between devices  49.4 us (34%)
  Pallas kernels  21.8 us (15%)
  other arithmetic  2.89 us (2%)
  local copies, waits for them, and re-layouts  2.06 us (1%)
    ppermute x14, waiting for transfers between devices, along(): return lax.ppermute(value, 'latent', pairs)  56 us
    ppermute x14, starting transfers between devices, along(): return lax.ppermute(value, 'latent', pairs)  39.4 us
    pallas_call x16, Pallas kernels, local_kernel(): pl.pallas_call(run, out_shape=outs, in_specs=[SMEM] + [VMEM] * len(args)...  18.8 us
    ppermute x19, waiting for transfers between devices, flip(): return lax.ppermute(value, ('latent', 'dp'), pairs)  13.3 us
    ppermute x19, starting transfers between devices, flip(): return lax.ppermute(value, ('latent', 'dp'), pairs)  9.99 us
  transfers between devices with their start and end apart: 33, of which 12 were waited for; matrix products, arithmetic and copies ran while one was open for 0% of the time, Pallas kernels for 13%

profile of v15, /device:TPU:0, one launch (start us, length us, event | category | flops | bytes accessed | tf_op | source)
XLA Modules:
  0.0 146.6 jit_solution(5312470457304528362)
XLA Ops:
  0.7 1.3 copy-done.1
  2.0 0.7 copy-done.6
  3.8 5.8 %collective-permute-start.2 = (bf16[384,512]{1,0:T(8,128)(2,1)S(1)}, bf16[384,512]{1,0:T(8,128)(2,1)S(1)}, u32[]{:S(2)}, u32[]{:S(2)}) collective-permute-start(bf16[384,512]{1,0:T(8,128)(2,1)S(1)} %copy-done.5), channel_id=1, source_target_pairs={{0,8},{12,4},{1,9},{13,5},{2,10},{14,6},{3,11},{15,7},{16,24},{28,... | collective-permute-start | bytes 1179656 | tf_op jit(solution)/shard_map/ppermute | solution.py:451
  9.6 1.3 collective-permute-start.1
  10.9 4.6 %collective-permute-start = (bf16[384,512]{1,0:T(8,128)(2,1)S(1)}, bf16[384,512]{1,0:T(8,128)(2,1)S(1)}, u32[]{:S(2)}, u32[]{:S(2)}) collective-permute-start(bf16[384,512]{1,0:T(8,128)(2,1)S(1)} %copy-done.5), channel_id=1, source_target_pairs={{0,4},{4,8},{8,12},{1,5},{5,9},{9,13},{2,6},{6,10},{10,14},{3,7},{... | collective-permute-start | bytes 1179656 | tf_op jit(solution)/shard_map/ppermute | solution.py:451
  15.5 1.6 %collective-permute-start.6 = (bf16[528,512]{1,0:T(8,128)(2,1)S(1)}, bf16[528,512]{1,0:T(8,128)(2,1)S(1)}, u32[]{:S(2)}, u32[]{:S(2)}) collective-permute-start(bf16[528,512]{1,0:T(8,128)(2,1)S(1)} %shard_map.178.refs_6_), channel_id=1, source_target_pairs={{0,2},{1,3},{2,0},{3,1},{4,6},{5,7},{6,4},{7,5},{8,10},{9,11},{10,... | collective-permute-start | bytes 1622024 | tf_op jit(solution)/shard_map/ppermute | solution.py:455
  17.1 0.6 shard_map.179.refs_0_.refs_4_.refs_3_
  18.3 0.8 collective-permute-done.2.refs_3_
  19.1 1.3 collective-permute-start.4
  21.0 1.6 %collective-permute-done.1.refs_1_.refs_2_ = bf16[384,512]{1,0:T(8,128)(2,1)S(1)} collective-permute-done((bf16[384,512]{1,0:T(8,128)(2,1)S(1)}, bf16[384,512]{1,0:T(8,128)(2,1)S(1)}, u32[]{:S(2)}, u32[]{:S(2)}) %collective-permute-start.1) | collective-permute-done | bytes 393248 | tf_op jit(solution)/shard_map/ppermute | solution.py:451
  22.6 8.4 %collective-permute-start.8 = (bf16[256,512]{1,0:T(8,128)(2,1)S(1)}, bf16[256,512]{1,0:T(8,128)(2,1)S(1)}, u32[]{:S(2)}, u32[]{:S(2)}) collective-permute-start(bf16[256,512]{1,0:T(8,128)(2,1)S(1)} %get-tuple-element.61), channel_id=1, source_target_pairs={{0,4},{4,8},{1,5},{5,9},{2,6},{6,10},{3,7},{7,11},{16,20},{20,24},... | collective-permute-start | bytes 786440 | tf_op jit(solution)/shard_map/ppermute | solution.py:451
  31.0 0.7 collective-permute-start.10
  31.7 5.2 %collective-permute-start.11 = (bf16[256,512]{1,0:T(8,128)(2,1)S(1)}, bf16[256,512]{1,0:T(8,128)(2,1)S(1)}, u32[]{:S(2)}, u32[]{:S(2)}) collective-permute-start(bf16[256,512]{1,0:T(8,128)(2,1)S(1)} %get-tuple-element.65), channel_id=1, source_target_pairs={{0,8},{12,4},{1,9},{13,5},{2,10},{14,6},{3,11},{15,7},{16,24},{28,... | collective-permute-start | bytes 786440 | tf_op jit(solution)/shard_map/ppermute | solution.py:451
  37.6 1.3 collective-permute-start.3
  38.9 1.8 %collective-permute-done.9.refs_5_.refs_6_ = bf16[528,512]{1,0:T(8,128)(2,1)S(1)} collective-permute-done((bf16[528,512]{1,0:T(8,128)(2,1)S(1)}, bf16[528,512]{1,0:T(8,128)(2,1)S(1)}, u32[]{:S(2)}, u32[]{:S(2)}) %collective-permute-start.9) | collective-permute-done | bytes 540704 | tf_op jit(solution)/shard_map/ppermute | solution.py:455
  41.3 1.1 collective-permute-done.11
  42.4 0.7 collective-permute-start.18
  43.1 6.2 %collective-permute-done.3.refs_4_ = bf16[384,512]{1,0:T(8,128)(2,1)S(1)} collective-permute-done((bf16[384,512]{1,0:T(8,128)(2,1)S(1)}, bf16[384,512]{1,0:T(8,128)(2,1)S(1)}, u32[]{:S(2)}, u32[]{:S(2)}) %collective-permute-start.3) | collective-permute-done | bytes 393248 | tf_op jit(solution)/shard_map/ppermute | solution.py:451
  49.4 1.8 %shard_map.181 = (bf16[384,512]{1,0:T(8,128)(2,1)S(1)}, bf16[384,512]{1,0:T(8,128)(2,1)S(1)}, bf16[384,2048]{1,0:T(8,128)(2,1)S(1)}, f32[1,512]{1,0:T(1,128)S(1)}) custom-call(s32[2]{0:T(128)S(1)} %pad_add_fusion.place, bf16[384,512]{1,0:T(8,128)(2,1)S(1)} %copy-done.5, bf16[384,512]{1,0:T(8,128)(2,1)S(1)} %collective-permute-done.refs_0_.refs_1_, ...), custom_call_target="tpu_custom_call" | custom-call | flops 1 | bytes 1 | tf_op jit(solution)/shard_map/pallas_call | solution.py:121
  51.2 0.7 collective-permute-start.15
  51.8 4.1 %collective-permute-start.16 = (bf16[384,512]{1,0:T(8,128)(2,1)S(1)}, bf16[384,512]{1,0:T(8,128)(2,1)S(1)}, u32[]{:S(2)}, u32[]{:S(2)}) collective-permute-start(bf16[384,512]{1,0:T(8,128)(2,1)S(1)} %get-tuple-element.68.refs_0_.refs_2_.refs_4_), channel_id=1, source_target_pairs={{0,4},{12,8},{1,5},{13,9},{2,6},{14,10},{3,7},{15,11},{16,20},{28,... | collective-permute-start | bytes 1179656 | tf_op jit(solution)/shard_map/ppermute | solution.py:451
  56.0 2.7 %collective-permute-start.14 = (bf16[384,512]{1,0:T(8,128)(2,1)S(1)}, bf16[384,512]{1,0:T(8,128)(2,1)S(1)}, u32[]{:S(2)}, u32[]{:S(2)}) collective-permute-start(bf16[384,512]{1,0:T(8,128)(2,1)S(1)} %get-tuple-element.68.refs_0_.refs_2_.refs_4_), channel_id=1, source_target_pairs={{0,8},{12,4},{1,9},{13,5},{2,10},{14,6},{3,11},{15,7},{16,24},{28,... | collective-permute-start | bytes 1179656 | tf_op jit(solution)/shard_map/ppermute | solution.py:451
  58.7 0.7 collective-permute-start.17
  59.5 0.7 collective-permute-start.19
  60.2 5.2 %collective-permute-done.16.refs_3_ = bf16[384,512]{1,0:T(8,128)(2,1)S(1)} collective-permute-done((bf16[384,512]{1,0:T(8,128)(2,1)S(1)}, bf16[384,512]{1,0:T(8,128)(2,1)S(1)}, u32[]{:S(2)}, u32[]{:S(2)}) %collective-permute-start.16) | collective-permute-done | bytes 393248 | tf_op jit(solution)/shard_map/ppermute | solution.py:451
  65.4 7.7 %collective-permute-done.14.refs_1_ = bf16[384,512]{1,0:T(8,128)(2,1)S(1)} collective-permute-done((bf16[384,512]{1,0:T(8,128)(2,1)S(1)}, bf16[384,512]{1,0:T(8,128)(2,1)S(1)}, u32[]{:S(2)}, u32[]{:S(2)}) %collective-permute-start.14) | collective-permute-done | bytes 393248 | tf_op jit(solution)/shard_map/ppermute | solution.py:451
  73.1 1.5 %shard_map.183.refs_9_ = bf16[384,512]{1,0:T(8,128)(2,1)S(1)} custom-call(s32[2]{0:T(128)S(1)} %pad_add_fusion.place, bf16[384,512]{1,0:T(8,128)(2,1)S(1)} %get-tuple-element.68.refs_0_.refs_2_.refs_4_, bf16[384,512]{1,0:T(8,128)(2,1)S(1)} %collective-permute-done.14.refs_1_, bf16[384,512]{1,0:T(8,128)(2,1)S(1)} %collective-permute-done.15.refs_2_, ...), custom_call_target="tpu_custom_call" | custom-call | flops 10000000000 | bytes 1 | tf_op jit(solution)/shard_map/pallas_call | solution.py:121
  74.7 1.6 %shard_map.184.refs_0_ = bf16[384,1024]{1,0:T(8,128)(2,1)S(1)} custom-call(s32[2]{0:T(128)S(1)} %pad_add_fusion.place, bf16[384,512]{1,0:T(8,128)(2,1)S(1)} %get-tuple-element.68.refs_0_.refs_2_.refs_4_, bf16[384,512]{1,0:T(8,128)(2,1)S(1)} %collective-permute-done.14.refs_1_, bf16[384,512]{1,0:T(8,128)(2,1)S(1)} %collective-permute-done.15.refs_2_, ...), custom_call_target="tpu_custom_call" | custom-call | flops 1 | bytes 1 | tf_op jit(solution)/shard_map/pallas_call | solution.py:121
  76.3 1.3 collective-permute-start.22
  77.6 0.7 collective-permute-start.20
  78.3 1.3 collective-permute-start.21
  79.6 18.4 %collective-permute-done.22.refs_1_ = bf16[384,1024]{1,0:T(8,128)(2,1)S(1)} collective-permute-done((bf16[384,1024]{1,0:T(8,128)(2,1)S(1)}, bf16[384,1024]{1,0:T(8,128)(2,1)S(1)}, u32[]{:S(2)}, u32[]{:S(2)}) %collective-permute-start.22) | collective-permute-done | bytes 786464 | tf_op jit(solution)/shard_map/ppermute | solution.py:451
  98.0 1.8 %shard_map.185 = (f32[384,512]{1,0:T(8,128)S(1)}, bf16[384,1024]{1,0:T(8,128)(2,1)S(1)}, f32[264,512]{1,0:T(8,128)S(1)}, f32[256,512]{1,0:T(8,128)S(1)}, f32[256,512]{1,0:T(8,128)S(1)}, /*index=5*/f32[256,512]{1,0:T(8,128)S(1)}) custom-call(s32[2]{0:T(128)S(1)} %pad_add_fusion.place, bf16[384,1024]{1,0:T(8,128)(2,1)S(1)} %shard_map.184.refs_0_, ...), custom_call_target="tpu_custom_call" | custom-call | flops 1 | bytes 1 | tf_op jit(solution)/shard_map/pallas_call | solution.py:121
  100.4 1.0 shard_map.182.refs_7_.refs_0_
  101.8 0.7 shard_map.186
  103.2 14.9 %collective-permute-done.21.refs_1_ = bf16[384,1024]{1,0:T(8,128)(2,1)S(1)} collective-permute-done((bf16[384,1024]{1,0:T(8,128)(2,1)S(1)}, bf16[384,1024]{1,0:T(8,128)(2,1)S(1)}, u32[]{:S(2)}, u32[]{:S(2)}) %collective-permute-start.21) | collective-permute-done | bytes 786464 | tf_op jit(solution)/shard_map/ppermute | solution.py:451
  118.0 1.3 shard_map.187
  119.4 1.7 %shard_map.188 = (bf16[384,512]{1,0:T(8,128)(2,1)S(1)}, f32[1,512]{1,0:T(1,128)S(1)}, f32[1,512]{1,0:T(1,128)S(1)}, f32[264,512]{1,0:T(8,128)S(1)}, f32[256,512]{1,0:T(8,128)S(1)}) custom-call(s32[2]{0:T(128)S(1)} %pad_add_fusion.place, bf16[384,1024]{1,0:T(8,128)(2,1)S(1)} %get-tuple-element.76.refs_0_.refs_3_, f32[384,512]{1,0:T(8,128)S(1)} %get-tuple-element.78.refs_1_, ...), custom_call_target="tpu_custom_call" | custom-call | flops 10000000000 | bytes 1 | tf_op jit(solution)/shard_map/pallas_call | solution.py:121
  121.7 0.7 shard_map.189.refs_5_
  122.5 0.6 collective-permute-start.32
  123.1 2.5 %shard_map.190 = (bf16[384,512]{1,0:T(8,128)(2,1)}, f32[512,512]{1,0:T(8,128)S(1)}, f32[512,512]{1,0:T(8,128)S(1)}, f32[512,512]{1,0:T(8,128)S(1)}, f32[256,512]{1,0:T(8,128)S(1)}, /*index=5*/f32[256,512]{1,0:T(8,128)S(1)}) custom-call(s32[2]{0:T(128)S(1)} %pad_add_fusion.place, bf16[2048,384]{1,0:T(8,128)(2,1)S(1)} %shard_map.182.refs_7_.refs_0_, ...), custom_call_target="tpu_custom_call" | custom-call | flops 1 | bytes 1 | tf_op jit(solution)/shard_map/pallas_call | solution.py:121
  126.2 0.8 shard_map.191
  127.1 1.5 %collective-permute-start.30 = (f16[528,512]{1,0:T(8,128)(2,1)S(1)}, f16[528,512]{1,0:T(8,128)(2,1)S(1)}, u32[]{:S(2)}, u32[]{:S(2)}) collective-permute-start(f16[528,512]{1,0:T(8,128)(2,1)S(1)} %convert_element_type.26), channel_id=1, source_target_pairs={{0,2},{1,3},{2,0},{3,1},{4,6},{5,7},{6,4},{7,5},{8,10},{9,11},{10,... | collective-permute-start | bytes 1622024 | tf_op jit(solution)/shard_map/ppermute | solution.py:455
  128.8 3.2 %collective-permute-done.32 = f16[272,512]{1,0:T(8,128)(2,1)S(1)} collective-permute-done((f16[272,512]{1,0:T(8,128)(2,1)S(1)}, f16[272,512]{1,0:T(8,128)(2,1)S(1)}, u32[]{:S(2)}, u32[]{:S(2)}) %collective-permute-start.32) | collective-permute-done | bytes 278560 | tf_op jit(solution)/shard_map/ppermute | solution.py:455
  132.3 2.9 %shard_map.193 = (f32[512,512]{1,0:T(8,128)}, f32[512,512]{1,0:T(8,128)}, f32[512,512]{1,0:T(8,128)}) custom-call(s32[2]{0:T(128)S(1)} %pad_add_fusion.place, f32[512,512]{1,0:T(8,128)S(1)} %copy-done, f32[512,512]{1,0:T(8,128)S(1)} %copy-done.3, f32[512,512]{1,0:T(8,128)S(1)} %copy-done.4, f32[256,512]{1,0:T(8,128)S(1)} %multiply_add_fusion.3.near, ...), custom_call_target="tpu_custom_call" | custom-call | flops 1 | bytes 1 | tf_op jit(solution)/shard_map/pallas_call | solution.py:655
  135.2 7.9 %collective-permute-done.30 = f16[528,512]{1,0:T(8,128)(2,1)S(1)} collective-permute-done((f16[528,512]{1,0:T(8,128)(2,1)S(1)}, f16[528,512]{1,0:T(8,128)(2,1)S(1)}, u32[]{:S(2)}, u32[]{:S(2)}) %collective-permute-start.30) | collective-permute-done | bytes 540704 | tf_op jit(solution)/shard_map/ppermute | solution.py:455
  143.2 1.1 shard_map.192
  144.3 2.3 %divide_subtract_fusion = (f32[512,512]{1,0:T(8,128)}, f32[512,512]{1,0:T(8,128)}, f32[512,512]{1,0:T(8,128)}) fusion(f32[512,512]{1,0:T(8,128)S(1)} %copy-done.2, f32[512]{0:T(512)S(1)} %bitcast.15, f16[528,512]{1,0:T(8,128)(2,1)S(1)} %collective-permute-done.30, f32[512,512]{1,0:T(8,128)S(1)} %get-tuple-element.92, ...), kind=kLoop, calls=%fused_computation.2 | loop fusion | flops 4194304 | bytes 8914944 | tf_op jit(solution)/shard_map/sub | solution.py:28
  (74 shorter events, 7.1 us)
Async XLA Ops:
  0.6 16.4 %copy-start = (f32[512,512]{1,0:T(8,128)S(1)}, f32[512,512]{1,0:T(8,128)}, u32[]{:S(2)}) copy-start(f32[512,512]{1,0:T(8,128)} %param.20) | copy-start | bytes 3145732
  0.7 1.3 copy-start.1
  2.0 0.7 copy-start.6
  2.7 1.1 copy-start.5
  3.3 13.8 %collective-permute-start.5 = (bf16[528,512]{1,0:T(8,128)(2,1)S(1)}, bf16[528,512]{1,0:T(8,128)(2,1)S(1)}, u32[]{:S(2)}, u32[]{:S(2)}) collective-permute-start(bf16[528,512]{1,0:T(8,128)(2,1)S(1)} %shard_map.178.refs_6_), channel_id=1, source_target_pairs={{0,1},{1,0},{2,3},{3,2},{4,5},{5,4},{6,7},{7,6},{8,9},{9,8},{10,11... | collective-permute-start | bytes 1622024 | tf_op jit(solution)/shard_map/ppermute | solution.py:455
  3.8 15.3 %collective-permute-start.2 = (bf16[384,512]{1,0:T(8,128)(2,1)S(1)}, bf16[384,512]{1,0:T(8,128)(2,1)S(1)}, u32[]{:S(2)}, u32[]{:S(2)}) collective-permute-start(bf16[384,512]{1,0:T(8,128)(2,1)S(1)} %copy-done.5), channel_id=1, source_target_pairs={{0,8},{12,4},{1,9},{13,5},{2,10},{14,6},{3,11},{15,7},{16,24},{28,... | collective-permute-start | bytes 1179656 | tf_op jit(solution)/shard_map/ppermute | solution.py:451
  9.6 13.0 %collective-permute-start.1 = (bf16[384,512]{1,0:T(8,128)(2,1)S(1)}, bf16[384,512]{1,0:T(8,128)(2,1)S(1)}, u32[]{:S(2)}, u32[]{:S(2)}) collective-permute-start(bf16[384,512]{1,0:T(8,128)(2,1)S(1)} %copy-done.5), channel_id=1, source_target_pairs={{4,0},{8,4},{12,8},{5,1},{9,5},{13,9},{6,2},{10,6},{14,10},{7,3},{... | collective-permute-start | bytes 1179656 | tf_op jit(solution)/shard_map/ppermute | solution.py:451
  10.9 20.1 %collective-permute-start = (bf16[384,512]{1,0:T(8,128)(2,1)S(1)}, bf16[384,512]{1,0:T(8,128)(2,1)S(1)}, u32[]{:S(2)}, u32[]{:S(2)}) collective-permute-start(bf16[384,512]{1,0:T(8,128)(2,1)S(1)} %copy-done.5), channel_id=1, source_target_pairs={{0,4},{4,8},{8,12},{1,5},{5,9},{9,13},{2,6},{6,10},{10,14},{3,7},{... | collective-permute-start | bytes 1179656 | tf_op jit(solution)/shard_map/ppermute | solution.py:451
  15.5 16.2 %collective-permute-start.6 = (bf16[528,512]{1,0:T(8,128)(2,1)S(1)}, bf16[528,512]{1,0:T(8,128)(2,1)S(1)}, u32[]{:S(2)}, u32[]{:S(2)}) collective-permute-start(bf16[528,512]{1,0:T(8,128)(2,1)S(1)} %shard_map.178.refs_6_), channel_id=1, source_target_pairs={{0,2},{1,3},{2,0},{3,1},{4,6},{5,7},{6,4},{7,5},{8,10},{9,11},{10,... | collective-permute-start | bytes 1622024 | tf_op jit(solution)/shard_map/ppermute | solution.py:455
  17.7 23.0 %collective-permute-start.9 = (bf16[528,512]{1,0:T(8,128)(2,1)S(1)}, bf16[528,512]{1,0:T(8,128)(2,1)S(1)}, u32[]{:S(2)}, u32[]{:S(2)}) collective-permute-start(bf16[528,512]{1,0:T(8,128)(2,1)S(1)} %shard_map.179.refs_0_.refs_4_.refs_3_), channel_id=1, source_target_pairs={{0,2},{1,3},{2,0},{3,1},{4,6},{5,7},{6,4},{7,5},{8,10},{9,11},{10,... | collective-permute-start | bytes 1622024 | tf_op jit(solution)/shard_map/ppermute | solution.py:455
  19.1 18.4 %collective-permute-start.4 = (bf16[384,512]{1,0:T(8,128)(2,1)S(1)}, bf16[384,512]{1,0:T(8,128)(2,1)S(1)}, u32[]{:S(2)}, u32[]{:S(2)}) collective-permute-start(bf16[384,512]{1,0:T(8,128)(2,1)S(1)} %collective-permute-done.2.refs_3_), channel_id=1, source_target_pairs={{4,0},{8,12},{5,1},{9,13},{6,2},{10,14},{7,3},{11,15},{20,16},{24,... | collective-permute-start | bytes 1179656 | tf_op jit(solution)/shard_map/ppermute | solution.py:451
  22.6 16.2 %collective-permute-start.8 = (bf16[256,512]{1,0:T(8,128)(2,1)S(1)}, bf16[256,512]{1,0:T(8,128)(2,1)S(1)}, u32[]{:S(2)}, u32[]{:S(2)}) collective-permute-start(bf16[256,512]{1,0:T(8,128)(2,1)S(1)} %get-tuple-element.61), channel_id=1, source_target_pairs={{0,4},{4,8},{1,5},{5,9},{2,6},{6,10},{3,7},{7,11},{16,20},{20,24},... | collective-permute-start | bytes 786440 | tf_op jit(solution)/shard_map/ppermute | solution.py:451
  31.0 9.7 %collective-permute-start.10 = (bf16[256,512]{1,0:T(8,128)(2,1)S(1)}, bf16[256,512]{1,0:T(8,128)(2,1)S(1)}, u32[]{:S(2)}, u32[]{:S(2)}) collective-permute-start(bf16[256,512]{1,0:T(8,128)(2,1)S(1)} %get-tuple-element.63), channel_id=1, source_target_pairs={{8,4},{12,8},{9,5},{13,9},{10,6},{14,10},{11,7},{15,11},{24,20},{2... | collective-permute-start | bytes 786440 | tf_op jit(solution)/shard_map/ppermute | solution.py:451
  31.7 10.6 %collective-permute-start.11 = (bf16[256,512]{1,0:T(8,128)(2,1)S(1)}, bf16[256,512]{1,0:T(8,128)(2,1)S(1)}, u32[]{:S(2)}, u32[]{:S(2)}) collective-permute-start(bf16[256,512]{1,0:T(8,128)(2,1)S(1)} %get-tuple-element.65), channel_id=1, source_target_pairs={{0,8},{12,4},{1,9},{13,5},{2,10},{14,6},{3,11},{15,7},{16,24},{28,... | collective-permute-start | bytes 786440 | tf_op jit(solution)/shard_map/ppermute | solution.py:451
  37.6 11.8 %collective-permute-start.3 = (bf16[384,512]{1,0:T(8,128)(2,1)S(1)}, bf16[384,512]{1,0:T(8,128)(2,1)S(1)}, u32[]{:S(2)}, u32[]{:S(2)}) collective-permute-start(bf16[384,512]{1,0:T(8,128)(2,1)S(1)} %shard_map.177), channel_id=1, source_target_pairs={{4,0},{8,12},{5,1},{9,13},{6,2},{10,14},{7,3},{11,15},{20,16},{24,... | collective-permute-start | bytes 1179656 | tf_op jit(solution)/shard_map/ppermute | solution.py:451
  38.9 10.5 %collective-permute-start.12 = (bf16[528,512]{1,0:T(8,128)(2,1)S(1)}, bf16[528,512]{1,0:T(8,128)(2,1)S(1)}, u32[]{:S(2)}, u32[]{:S(2)}) collective-permute-start(bf16[528,512]{1,0:T(8,128)(2,1)S(1)} %shard_map.179.refs_0_.refs_4_.refs_3_), channel_id=1, source_target_pairs={{0,1},{1,0},{2,3},{3,2},{4,5},{5,4},{6,7},{7,6},{8,9},{9,8},{10,11... | collective-permute-start | bytes 1622024 | tf_op jit(solution)/shard_map/ppermute | solution.py:455
  40.7 8.7 %collective-permute-start.7 = (bf16[528,512]{1,0:T(8,128)(2,1)S(1)}, bf16[528,512]{1,0:T(8,128)(2,1)S(1)}, u32[]{:S(2)}, u32[]{:S(2)}) collective-permute-start(bf16[528,512]{1,0:T(8,128)(2,1)S(1)} %collective-permute-done.6.refs_8_), channel_id=1, source_target_pairs={{0,1},{1,0},{2,3},{3,2},{4,5},{5,4},{6,7},{7,6},{8,9},{9,8},{10,11... | collective-permute-start | bytes 1622024 | tf_op jit(solution)/shard_map/ppermute | solution.py:455
  40.7 8.7 %collective-permute-start.13 = (bf16[528,512]{1,0:T(8,128)(2,1)S(1)}, bf16[528,512]{1,0:T(8,128)(2,1)S(1)}, u32[]{:S(2)}, u32[]{:S(2)}) collective-permute-start(bf16[528,512]{1,0:T(8,128)(2,1)S(1)} %collective-permute-done.9.refs_5_.refs_6_), channel_id=1, source_target_pairs={{0,1},{1,0},{2,3},{3,2},{4,5},{5,4},{6,7},{7,6},{8,9},{9,8},{10,11... | collective-permute-start | bytes 1622024 | tf_op jit(solution)/shard_map/ppermute | solution.py:455
  42.4 17.1 %collective-permute-start.18 = (bf16[768,512]{1,0:T(8,128)(2,1)S(1)}, bf16[768,512]{1,0:T(8,128)(2,1)S(1)}, u32[]{:S(2)}, u32[]{:S(2)}) collective-permute-start(bf16[768,512]{1,0:T(8,128)(2,1)S(1)} %constant_dynamic-update-slice_fusion.refs_10_.refs_6_), channel_id=1, source_target_pairs={{4,6},{5,7},{6,4},{7,5},{8,10},{9,11},{10,8},{11,9},{20,22},{21,23... | collective-permute-start | bytes 2359304 | tf_op jit(solution)/shard_map/ppermute | solution.py:455
  51.2 8.3 %collective-permute-start.15 = (bf16[384,512]{1,0:T(8,128)(2,1)S(1)}, bf16[384,512]{1,0:T(8,128)(2,1)S(1)}, u32[]{:S(2)}, u32[]{:S(2)}) collective-permute-start(bf16[384,512]{1,0:T(8,128)(2,1)S(1)} %get-tuple-element.68.refs_0_.refs_2_.refs_4_), channel_id=1, source_target_pairs={{4,8},{8,4},{5,9},{9,5},{6,10},{10,6},{7,11},{11,7},{20,24},{24,20... | collective-permute-start | bytes 1179656 | tf_op jit(solution)/shard_map/ppermute | solution.py:451
  51.8 13.6 %collective-permute-start.16 = (bf16[384,512]{1,0:T(8,128)(2,1)S(1)}, bf16[384,512]{1,0:T(8,128)(2,1)S(1)}, u32[]{:S(2)}, u32[]{:S(2)}) collective-permute-start(bf16[384,512]{1,0:T(8,128)(2,1)S(1)} %get-tuple-element.68.refs_0_.refs_2_.refs_4_), channel_id=1, source_target_pairs={{0,4},{12,8},{1,5},{13,9},{2,6},{14,10},{3,7},{15,11},{16,20},{28,... | collective-permute-start | bytes 1179656 | tf_op jit(solution)/shard_map/ppermute | solution.py:451
  56.0 17.1 %collective-permute-start.14 = (bf16[384,512]{1,0:T(8,128)(2,1)S(1)}, bf16[384,512]{1,0:T(8,128)(2,1)S(1)}, u32[]{:S(2)}, u32[]{:S(2)}) collective-permute-start(bf16[384,512]{1,0:T(8,128)(2,1)S(1)} %get-tuple-element.68.refs_0_.refs_2_.refs_4_), channel_id=1, source_target_pairs={{0,8},{12,4},{1,9},{13,5},{2,10},{14,6},{3,11},{15,7},{16,24},{28,... | collective-permute-start | bytes 1179656 | tf_op jit(solution)/shard_map/ppermute | solution.py:451
  58.7 16.0 %collective-permute-start.17 = (bf16[768,512]{1,0:T(8,128)(2,1)S(1)}, bf16[768,512]{1,0:T(8,128)(2,1)S(1)}, u32[]{:S(2)}, u32[]{:S(2)}) collective-permute-start(bf16[768,512]{1,0:T(8,128)(2,1)S(1)} %constant_dynamic-update-slice_fusion.refs_10_.refs_6_), channel_id=1, source_target_pairs={{4,5},{5,4},{6,7},{7,6},{8,9},{9,8},{10,11},{11,10},{20,21},{21,20... | collective-permute-start | bytes 2359304 | tf_op jit(solution)/shard_map/ppermute | solution.py:455
  59.5 15.2 %collective-permute-start.19 = (bf16[768,512]{1,0:T(8,128)(2,1)S(1)}, bf16[768,512]{1,0:T(8,128)(2,1)S(1)}, u32[]{:S(2)}, u32[]{:S(2)}) collective-permute-start(bf16[768,512]{1,0:T(8,128)(2,1)S(1)} %collective-permute-done.18.refs_7_), channel_id=1, source_target_pairs={{4,5},{5,4},{6,7},{7,6},{8,9},{9,8},{10,11},{11,10},{20,21},{21,20... | collective-permute-start | bytes 2359304 | tf_op jit(solution)/shard_map/ppermute | solution.py:455
  76.3 21.7 %collective-permute-start.22 = (bf16[384,1024]{1,0:T(8,128)(2,1)S(1)}, bf16[384,1024]{1,0:T(8,128)(2,1)S(1)}, u32[]{:S(2)}, u32[]{:S(2)}) collective-permute-start(bf16[384,1024]{1,0:T(8,128)(2,1)S(1)} %shard_map.184.refs_0_), channel_id=1, source_target_pairs={{4,0},{8,12},{5,1},{9,13},{6,2},{10,14},{7,3},{11,15},{20,16},{24,... | collective-permute-start | bytes 2359304 | tf_op jit(solution)/shard_map/ppermute | solution.py:451
  77.6 20.4 %collective-permute-start.20 = (bf16[384,1024]{1,0:T(8,128)(2,1)S(1)}, bf16[384,1024]{1,0:T(8,128)(2,1)S(1)}, u32[]{:S(2)}, u32[]{:S(2)}) collective-permute-start(bf16[384,1024]{1,0:T(8,128)(2,1)S(1)} %shard_map.184.refs_0_), channel_id=1, source_target_pairs={{4,8},{8,4},{5,9},{9,5},{6,10},{10,6},{7,11},{11,7},{20,24},{24,20... | collective-permute-start | bytes 2359304 | tf_op jit(solution)/shard_map/ppermute | solution.py:451
  78.3 39.7 %collective-permute-start.21 = (bf16[384,1024]{1,0:T(8,128)(2,1)S(1)}, bf16[384,1024]{1,0:T(8,128)(2,1)S(1)}, u32[]{:S(2)}, u32[]{:S(2)}) collective-permute-start(bf16[384,1024]{1,0:T(8,128)(2,1)S(1)} %shard_map.184.refs_0_), channel_id=1, source_target_pairs={{8,0},{4,12},{9,1},{5,13},{10,2},{6,14},{11,3},{7,15},{24,16},{20,... | collective-permute-start | bytes 2359304 | tf_op jit(solution)/shard_map/ppermute | solution.py:451
  99.8 2.0 %collective-permute-start.23 = (f32[264,512]{1,0:T(8,128)S(1)}, f32[264,512]{1,0:T(8,128)S(1)}, u32[]{:S(2)}, u32[]{:S(2)}) collective-permute-start(f32[264,512]{1,0:T(8,128)S(1)} %get-tuple-element.73), channel_id=1, source_target_pairs={{0,1},{1,0},{2,3},{3,2},{4,5},{5,4},{6,7},{7,6},{8,9},{9,8},{10,11... | collective-permute-start | bytes 1622024 | tf_op jit(solution)/shard_map/ppermute | solution.py:455
  99.9 18.2 %collective-permute-start.24 = (f32[256,512]{1,0:T(8,128)S(1)}, f32[256,512]{1,0:T(8,128)S(1)}, u32[]{:S(2)}, u32[]{:S(2)}) collective-permute-start(f32[256,512]{1,0:T(8,128)S(1)} %get-tuple-element.75), channel_id=1, source_target_pairs={{0,1},{1,0},{2,3},{3,2},{4,5},{5,4},{6,7},{7,6},{8,9},{9,8},{10,11... | collective-permute-start | bytes 1572872 | tf_op jit(solution)/shard_map/ppermute | solution.py:455
  102.5 16.8 %collective-permute-start.25 = (f16[272,512]{1,0:T(8,128)(2,1)S(1)}, f16[272,512]{1,0:T(8,128)(2,1)S(1)}, u32[]{:S(2)}, u32[]{:S(2)}) collective-permute-start(f16[272,512]{1,0:T(8,128)(2,1)S(1)} %convert_element_type.25), channel_id=1, source_target_pairs={{0,2},{1,3},{2,0},{3,1},{4,6},{5,7},{6,4},{7,5},{8,10},{9,11},{10,... | collective-permute-start | bytes 835592 | tf_op jit(solution)/shard_map/ppermute | solution.py:455
  119.3 2.5 %collective-permute-start.26 = (f32[256,512]{1,0:T(8,128)S(1)}, f32[256,512]{1,0:T(8,128)S(1)}, u32[]{:S(2)}, u32[]{:S(2)}) collective-permute-start(f32[256,512]{1,0:T(8,128)S(1)} %get-tuple-element.83), channel_id=1, source_target_pairs={{0,1},{1,0},{2,3},{3,2},{4,5},{5,4},{6,7},{7,6},{8,9},{9,8},{10,11... | collective-permute-start | bytes 1572872 | tf_op jit(solution)/shard_map/ppermute | solution.py:455
  121.1 5.1 %collective-permute-start.27 = (f32[264,512]{1,0:T(8,128)S(1)}, f32[264,512]{1,0:T(8,128)S(1)}, u32[]{:S(2)}, u32[]{:S(2)}) collective-permute-start(f32[264,512]{1,0:T(8,128)S(1)} %get-tuple-element.87), channel_id=1, source_target_pairs={{0,1},{1,0},{2,3},{3,2},{4,5},{5,4},{6,7},{7,6},{8,9},{9,8},{10,11... | collective-permute-start | bytes 1622024 | tf_op jit(solution)/shard_map/ppermute | solution.py:455
  121.7 4.5 %collective-permute-start.28 = (f32[256,512]{1,0:T(8,128)S(1)}, f32[256,512]{1,0:T(8,128)S(1)}, u32[]{:S(2)}, u32[]{:S(2)}) collective-permute-start(f32[256,512]{1,0:T(8,128)S(1)} %get-tuple-element.88), channel_id=1, source_target_pairs={{0,1},{1,0},{2,3},{3,2},{4,5},{5,4},{6,7},{7,6},{8,9},{9,8},{10,11... | collective-permute-start | bytes 1572872 | tf_op jit(solution)/shard_map/ppermute | solution.py:455
  122.5 9.5 %collective-permute-start.32 = (f16[272,512]{1,0:T(8,128)(2,1)S(1)}, f16[272,512]{1,0:T(8,128)(2,1)S(1)}, u32[]{:S(2)}, u32[]{:S(2)}) collective-permute-start(f16[272,512]{1,0:T(8,128)(2,1)S(1)} %convert_element_type.31), channel_id=1, source_target_pairs={{0,2},{1,3},{2,0},{3,1},{4,6},{5,7},{6,4},{7,5},{8,10},{9,11},{10,... | collective-permute-start | bytes 835592 | tf_op jit(solution)/shard_map/ppermute | solution.py:455
  125.6 6.4 %collective-permute-start.31 = (f32[256,512]{1,0:T(8,128)S(1)}, f32[256,512]{1,0:T(8,128)S(1)}, u32[]{:S(2)}, u32[]{:S(2)}) collective-permute-start(f32[256,512]{1,0:T(8,128)S(1)} %get-tuple-element.102), channel_id=1, source_target_pairs={{0,1},{1,0},{2,3},{3,2},{4,5},{5,4},{6,7},{7,6},{8,9},{9,8},{10,11... | collective-permute-start | bytes 1572872 | tf_op jit(solution)/shard_map/ppermute | solution.py:455
  125.8 18.5 %collective-permute-start.29 = (f32[512,512]{1,0:T(8,128)S(1)}, f32[512,512]{1,0:T(8,128)S(1)}, u32[]{:S(2)}, u32[]{:S(2)}) collective-permute-start(f32[512,512]{1,0:T(8,128)S(1)} %get-tuple-element.93), channel_id=1, source_target_pairs={{0,1},{1,0},{2,3},{3,2},{4,5},{5,4},{6,7},{7,6},{8,9},{9,8},{10,11... | collective-permute-start | bytes 3145736 | tf_op jit(solution)/shard_map/ppermute | solution.py:455
  127.1 16.0 %collective-permute-start.30 = (f16[528,512]{1,0:T(8,128)(2,1)S(1)}, f16[528,512]{1,0:T(8,128)(2,1)S(1)}, u32[]{:S(2)}, u32[]{:S(2)}) collective-permute-start(f16[528,512]{1,0:T(8,128)(2,1)S(1)} %convert_element_type.26), channel_id=1, source_target_pairs={{0,2},{1,3},{2,0},{3,1},{4,6},{5,7},{6,4},{7,5},{8,10},{9,11},{10,... | collective-permute-start | bytes 1622024 | tf_op jit(solution)/shard_map/ppermute | solution.py:455
  128.7 3.5 %copy-start.3 = (f32[512,512]{1,0:T(8,128)S(1)}, f32[512,512]{1,0:T(8,128)}, u32[]{:S(2)}) copy-start(f32[512,512]{1,0:T(8,128)} %moment) | copy-start | bytes 3145732
  128.7 3.5 %copy-start.4 = (f32[512,512]{1,0:T(8,128)S(1)}, f32[512,512]{1,0:T(8,128)}, u32[]{:S(2)}) copy-start(f32[512,512]{1,0:T(8,128)} %square) | copy-start | bytes 3145732
  132.2 11.0 %copy-start.7 = (f32[128]{0:T(128)S(1)}, f32[128]{0:T(128)}, u32[]{:S(2)}) copy-start(f32[128]{0:T(128)} %param.12) | copy-start | bytes 1540
  132.2 11.0 %copy-start.8 = (f32[128]{0:T(128)S(1)}, f32[128]{0:T(128)}, u32[]{:S(2)}) copy-start(f32[128]{0:T(128)} %param.16) | copy-start | bytes 1540
  132.2 11.0 %copy-start.9 = (f32[128]{0:T(128)S(1)}, f32[128]{0:T(128)}, u32[]{:S(2)}) copy-start(f32[128]{0:T(128)} %param.17) | copy-start | bytes 1540
  132.2 12.1 %copy-start.2 = (f32[512,512]{1,0:T(8,128)S(1)}, f32[512,512]{1,0:T(8,128)}, u32[]{:S(2)}) copy-start(f32[512,512]{1,0:T(8,128)} %refs_0_.3) | copy-start | bytes 3145732
  132.2 12.1 %copy-start.10 = (f32[512,512]{1,0:T(8,128)S(1)}, f32[512,512]{1,0:T(8,128)}, u32[]{:S(2)}) copy-start(f32[512,512]{1,0:T(8,128)} %param.14) | copy-start | bytes 3145732
  132.3 12.0 %copy-start.11 = (f32[512,512]{1,0:T(8,128)S(1)}, f32[512,512]{1,0:T(8,128)}, u32[]{:S(2)}) copy-start(f32[512,512]{1,0:T(8,128)} %param.15) | copy-start | bytes 3145732

commit v16 on v15

--- a/solution.py
+++ b/solution.py
@@ -244,9 +244,9 @@
     below = pl.multiple_of(jnp.where(z == 1, 0, half), half)
     rights = [
         dec[pl.ds(shift, half), :],
+        row[pl.ds(below, half), :],
         row[2 * half :, :],
         row[pl.ds(half - below, half), :],
-        row[pl.ds(below, half), :],
     ]
     total = jnp.zeros((codes[0].shape[0], half), F32)
     for left, right in zip(codes, rights):
@@ -257,17 +257,17 @@
     return (given - total).astype(BF16)
 
 
-def own_error_body(place, own, across, middle, near, dec0, dec2, row0, row2, inputs, out):
+def own_error_body(place, own, near, across, middle, dec0, dec2, row0, row2, inputs, out):
     half = out.shape[1] // 2
-    codes = (own, across, middle, near)
+    codes = (own, near, across, middle)
     out[:, :half] = rebuilt_error(place, 0, codes, dec0, row0, inputs)
     out[:, half:] = rebuilt_error(place, 2, codes, dec2, row2, inputs)
 
 
-def error_body(place, own, across, middle, near, dec1, dec3, row1, row3, inputs, made, error):
+def error_body(place, own, near, across, middle, dec1, dec3, row1, row3, inputs, made, error):
     i = place[1]
     half = error.shape[1] // 4
-    codes = (own, across, middle, near)
+    codes = (own, near, across, middle)
     error[:, columns(i * half, half)] = made[:, :half]
     error[:, columns((i ^ 2) * half, half)] = made[:, half:]
     error[:, columns((i ^ 1) * half, half)] = rebuilt_error(place, 1, codes, dec1, row1, inputs)
@@ -520,9 +520,9 @@
     )
     rows_chip = flip(rows_own, 2, (1, 2))
     rows_core = flip(behind(rows_own, codes), 1, (1, 2))
-    rows_both = flip(behind(rows_chip, codes_middle), 1, (1, 2))
-
-    all_codes = codes, codes_across, codes_middle, codes_near
+    rows_both = flip(behind(rows_chip, codes_across), 1, (1, 2))
+
+    all_codes = codes, codes_near, codes_across, codes_middle
     (made,) = local_kernel(
         own_error_body,
         [shape((count, features // 4), BF16)],

time: 147 us -> 146 us (level)
  starting transfers between devices: 49.4 us -> 47.9 us
where the time goes in v16:
time: 146 us; the launch traced here: 145 us
  waiting for transfers between devices  69.5 us (48%)
  starting transfers between devices  47.9 us (33%)
  Pallas kernels  21.8 us (15%)
  other arithmetic  2.92 us (2%)
  local copies, waits for them, and re-layouts  2.06 us (1%)
    ppermute x14, waiting for transfers between devices, along(): return lax.ppermute(value, 'latent', pairs)  56.2 us
    ppermute x14, starting transfers between devices, along(): return lax.ppermute(value, 'latent', pairs)  37.9 us
    pallas_call x16, Pallas kernels, local_kernel(): pl.pallas_call(run, out_shape=outs, in_specs=[SMEM] + [VMEM] * len(args)...  18.9 us
    ppermute x19, waiting for transfers between devices, flip(): return lax.ppermute(value, ('latent', 'dp'), pairs)  13.3 us
    ppermute x19, starting transfers between devices, flip(): return lax.ppermute(value, ('latent', 'dp'), pairs)  9.98 us
    pallas_call x1, Pallas kernels, line_shards(): pl.pallas_call(functools.partial(decoder_step_body, rows), grid=(4,), out...  2.94 us
  transfers between devices with their start and end apart: 33, of which 12 were waited for; matrix products, arithmetic and copies ran while one was open for 0% of the time, Pallas kernels for 13%

profile of v16, /device:TPU:0, one launch (start us, length us, event | category | flops | bytes accessed | tf_op | source)
XLA Modules:
  0.0 145.4 jit_solution(1172456211985094995)
XLA Ops:
  0.7 1.3 copy-done.1
  2.0 0.7 copy-done.6
  3.8 5.8 %collective-permute-start.2 = (bf16[384,512]{1,0:T(8,128)(2,1)S(1)}, bf16[384,512]{1,0:T(8,128)(2,1)S(1)}, u32[]{:S(2)}, u32[]{:S(2)}) collective-permute-start(bf16[384,512]{1,0:T(8,128)(2,1)S(1)} %copy-done.5), channel_id=1, source_target_pairs={{0,8},{12,4},{1,9},{13,5},{2,10},{14,6},{3,11},{15,7},{16,24},{28,... | collective-permute-start | bytes 1179656 | tf_op jit(solution)/shard_map/ppermute | solution.py:451
  9.6 1.3 collective-permute-start.1
  10.9 4.6 %collective-permute-start = (bf16[384,512]{1,0:T(8,128)(2,1)S(1)}, bf16[384,512]{1,0:T(8,128)(2,1)S(1)}, u32[]{:S(2)}, u32[]{:S(2)}) collective-permute-start(bf16[384,512]{1,0:T(8,128)(2,1)S(1)} %copy-done.5), channel_id=1, source_target_pairs={{0,4},{4,8},{8,12},{1,5},{5,9},{9,13},{2,6},{6,10},{10,14},{3,7},{... | collective-permute-start | bytes 1179656 | tf_op jit(solution)/shard_map/ppermute | solution.py:451
  15.5 1.6 %collective-permute-start.6 = (bf16[528,512]{1,0:T(8,128)(2,1)S(1)}, bf16[528,512]{1,0:T(8,128)(2,1)S(1)}, u32[]{:S(2)}, u32[]{:S(2)}) collective-permute-start(bf16[528,512]{1,0:T(8,128)(2,1)S(1)} %shard_map.178.refs_6_), channel_id=1, source_target_pairs={{0,2},{1,3},{2,0},{3,1},{4,6},{5,7},{6,4},{7,5},{8,10},{9,11},{10,... | collective-permute-start | bytes 1622024 | tf_op jit(solution)/shard_map/ppermute | solution.py:455
  17.1 0.6 shard_map.179.refs_0_.refs_4_.refs_3_
  18.3 0.8 collective-permute-done.2.refs_3_
  19.1 1.3 collective-permute-start.4
  21.0 1.6 %collective-permute-done.1.refs_1_.refs_2_ = bf16[384,512]{1,0:T(8,128)(2,1)S(1)} collective-permute-done((bf16[384,512]{1,0:T(8,128)(2,1)S(1)}, bf16[384,512]{1,0:T(8,128)(2,1)S(1)}, u32[]{:S(2)}, u32[]{:S(2)}) %collective-permute-start.1) | collective-permute-done | bytes 393248 | tf_op jit(solution)/shard_map/ppermute | solution.py:451
  22.6 8.4 %collective-permute-start.8 = (bf16[256,512]{1,0:T(8,128)(2,1)S(1)}, bf16[256,512]{1,0:T(8,128)(2,1)S(1)}, u32[]{:S(2)}, u32[]{:S(2)}) collective-permute-start(bf16[256,512]{1,0:T(8,128)(2,1)S(1)} %get-tuple-element.61), channel_id=1, source_target_pairs={{0,4},{4,8},{1,5},{5,9},{2,6},{6,10},{3,7},{7,11},{16,20},{20,24},... | collective-permute-start | bytes 786440 | tf_op jit(solution)/shard_map/ppermute | solution.py:451
  31.0 0.7 collective-permute-start.10
  31.7 5.2 %collective-permute-start.11 = (bf16[256,512]{1,0:T(8,128)(2,1)S(1)}, bf16[256,512]{1,0:T(8,128)(2,1)S(1)}, u32[]{:S(2)}, u32[]{:S(2)}) collective-permute-start(bf16[256,512]{1,0:T(8,128)(2,1)S(1)} %get-tuple-element.65), channel_id=1, source_target_pairs={{0,8},{12,4},{1,9},{13,5},{2,10},{14,6},{3,11},{15,7},{16,24},{28,... | collective-permute-start | bytes 786440 | tf_op jit(solution)/shard_map/ppermute | solution.py:451
  37.6 1.3 collective-permute-start.3
  38.9 1.8 %collective-permute-done.9.refs_5_.refs_6_ = bf16[528,512]{1,0:T(8,128)(2,1)S(1)} collective-permute-done((bf16[528,512]{1,0:T(8,128)(2,1)S(1)}, bf16[528,512]{1,0:T(8,128)(2,1)S(1)}, u32[]{:S(2)}, u32[]{:S(2)}) %collective-permute-start.9) | collective-permute-done | bytes 540704 | tf_op jit(solution)/shard_map/ppermute | solution.py:455
  41.3 1.1 collective-permute-done.11
  42.4 0.7 collective-permute-start.18
  43.1 6.2 %collective-permute-done.3.refs_4_ = bf16[384,512]{1,0:T(8,128)(2,1)S(1)} collective-permute-done((bf16[384,512]{1,0:T(8,128)(2,1)S(1)}, bf16[384,512]{1,0:T(8,128)(2,1)S(1)}, u32[]{:S(2)}, u32[]{:S(2)}) %collective-permute-start.3) | collective-permute-done | bytes 393248 | tf_op jit(solution)/shard_map/ppermute | solution.py:451
  49.4 1.8 %shard_map.181 = (bf16[384,512]{1,0:T(8,128)(2,1)S(1)}, bf16[384,512]{1,0:T(8,128)(2,1)S(1)}, bf16[384,2048]{1,0:T(8,128)(2,1)S(1)}, f32[1,512]{1,0:T(1,128)S(1)}) custom-call(s32[2]{0:T(128)S(1)} %pad_add_fusion.place, bf16[384,512]{1,0:T(8,128)(2,1)S(1)} %copy-done.5, bf16[384,512]{1,0:T(8,128)(2,1)S(1)} %collective-permute-done.refs_0_.refs_1_, ...), custom_call_target="tpu_custom_call" | custom-call | flops 1 | bytes 1 | tf_op jit(solution)/shard_map/pallas_call | solution.py:121
  51.2 1.9 %collective-permute-start.14 = (bf16[384,512]{1,0:T(8,128)(2,1)S(1)}, bf16[384,512]{1,0:T(8,128)(2,1)S(1)}, u32[]{:S(2)}, u32[]{:S(2)}) collective-permute-start(bf16[384,512]{1,0:T(8,128)(2,1)S(1)} %get-tuple-element.68.refs_0_.refs_2_.refs_4_), channel_id=1, source_target_pairs={{0,8},{12,4},{1,9},{13,5},{2,10},{14,6},{3,11},{15,7},{16,24},{28,... | collective-permute-start | bytes 1179656 | tf_op jit(solution)/shard_map/ppermute | solution.py:451
  53.0 0.7 collective-permute-start.16
  53.7 3.5 %collective-permute-start.15 = (bf16[384,512]{1,0:T(8,128)(2,1)S(1)}, bf16[384,512]{1,0:T(8,128)(2,1)S(1)}, u32[]{:S(2)}, u32[]{:S(2)}) collective-permute-start(bf16[384,512]{1,0:T(8,128)(2,1)S(1)} %get-tuple-element.68.refs_0_.refs_2_.refs_4_), channel_id=1, source_target_pairs={{0,4},{12,8},{1,5},{13,9},{2,6},{14,10},{3,7},{15,11},{16,20},{28,... | collective-permute-start | bytes 1179656 | tf_op jit(solution)/shard_map/ppermute | solution.py:451
  57.3 0.7 collective-permute-start.17
  58.0 4.5 %collective-permute-done.14.refs_1_.refs_2_ = bf16[384,512]{1,0:T(8,128)(2,1)S(1)} collective-permute-done((bf16[384,512]{1,0:T(8,128)(2,1)S(1)}, bf16[384,512]{1,0:T(8,128)(2,1)S(1)}, u32[]{:S(2)}, u32[]{:S(2)}) %collective-permute-start.14) | collective-permute-done | bytes 393248 | tf_op jit(solution)/shard_map/ppermute | solution.py:451
  62.5 0.7 collective-permute-start.19
  63.2 7.0 %collective-permute-done.15.refs_1_ = bf16[384,512]{1,0:T(8,128)(2,1)S(1)} collective-permute-done((bf16[384,512]{1,0:T(8,128)(2,1)S(1)}, bf16[384,512]{1,0:T(8,128)(2,1)S(1)}, u32[]{:S(2)}, u32[]{:S(2)}) %collective-permute-start.15) | collective-permute-done | bytes 393248 | tf_op jit(solution)/shard_map/ppermute | solution.py:451
  70.2 1.5 %shard_map.183.refs_9_ = bf16[384,512]{1,0:T(8,128)(2,1)S(1)} custom-call(s32[2]{0:T(128)S(1)} %pad_add_fusion.place, bf16[384,512]{1,0:T(8,128)(2,1)S(1)} %get-tuple-element.68.refs_0_.refs_2_.refs_4_, bf16[384,512]{1,0:T(8,128)(2,1)S(1)} %collective-permute-done.15.refs_1_, bf16[384,512]{1,0:T(8,128)(2,1)S(1)} %collective-permute-done.14.refs_1_.refs_2_, ...), custom_call_target="tpu_custom_call" | custom-call | flops 10000000000 | bytes 1 | tf_op jit(solution)/shard_map/pallas_call | solution.py:121
  71.8 1.6 %shard_map.184.refs_0_ = bf16[384,1024]{1,0:T(8,128)(2,1)S(1)} custom-call(s32[2]{0:T(128)S(1)} %pad_add_fusion.place, bf16[384,512]{1,0:T(8,128)(2,1)S(1)} %get-tuple-element.68.refs_0_.refs_2_.refs_4_, bf16[384,512]{1,0:T(8,128)(2,1)S(1)} %collective-permute-done.15.refs_1_, bf16[384,512]{1,0:T(8,128)(2,1)S(1)} %collective-permute-done.14.refs_1_.refs_2_, ...), custom_call_target="tpu_custom_call" | custom-call | flops 1 | bytes 1 | tf_op jit(solution)/shard_map/pallas_call | solution.py:121
  73.4 1.3 collective-permute-start.22
  74.7 0.7 collective-permute-start.20
  75.4 1.3 collective-permute-start.21
  76.7 20.1 %collective-permute-done.22.refs_1_ = bf16[384,1024]{1,0:T(8,128)(2,1)S(1)} collective-permute-done((bf16[384,1024]{1,0:T(8,128)(2,1)S(1)}, bf16[384,1024]{1,0:T(8,128)(2,1)S(1)}, u32[]{:S(2)}, u32[]{:S(2)}) %collective-permute-start.22) | collective-permute-done | bytes 786464 | tf_op jit(solution)/shard_map/ppermute | solution.py:451
  96.8 1.8 %shard_map.185 = (f32[384,512]{1,0:T(8,128)S(1)}, bf16[384,1024]{1,0:T(8,128)(2,1)S(1)}, f32[264,512]{1,0:T(8,128)S(1)}, f32[256,512]{1,0:T(8,128)S(1)}, f32[256,512]{1,0:T(8,128)S(1)}, /*index=5*/f32[256,512]{1,0:T(8,128)S(1)}) custom-call(s32[2]{0:T(128)S(1)} %pad_add_fusion.place, bf16[384,1024]{1,0:T(8,128)(2,1)S(1)} %shard_map.184.refs_0_, ...), custom_call_target="tpu_custom_call" | custom-call | flops 1 | bytes 1 | tf_op jit(solution)/shard_map/pallas_call | solution.py:121
  99.1 1.0 shard_map.182.refs_7_.refs_0_
  100.6 0.7 shard_map.186
  101.9 14.9 %collective-permute-done.21.refs_1_ = bf16[384,1024]{1,0:T(8,128)(2,1)S(1)} collective-permute-done((bf16[384,1024]{1,0:T(8,128)(2,1)S(1)}, bf16[384,1024]{1,0:T(8,128)(2,1)S(1)}, u32[]{:S(2)}, u32[]{:S(2)}) %collective-permute-start.21) | collective-permute-done | bytes 786464 | tf_op jit(solution)/shard_map/ppermute | solution.py:451
  116.8 1.3 shard_map.187
  118.2 1.7 %shard_map.188 = (bf16[384,512]{1,0:T(8,128)(2,1)S(1)}, f32[1,512]{1,0:T(1,128)S(1)}, f32[1,512]{1,0:T(1,128)S(1)}, f32[264,512]{1,0:T(8,128)S(1)}, f32[256,512]{1,0:T(8,128)S(1)}) custom-call(s32[2]{0:T(128)S(1)} %pad_add_fusion.place, bf16[384,1024]{1,0:T(8,128)(2,1)S(1)} %get-tuple-element.76.refs_0_.refs_3_, f32[384,512]{1,0:T(8,128)S(1)} %get-tuple-element.78.refs_1_, ...), custom_call_target="tpu_custom_call" | custom-call | flops 10000000000 | bytes 1 | tf_op jit(solution)/shard_map/pallas_call | solution.py:121
  120.5 0.7 shard_map.189.refs_5_
  121.2 0.6 collective-permute-start.32
  121.9 2.5 %shard_map.190 = (bf16[384,512]{1,0:T(8,128)(2,1)}, f32[512,512]{1,0:T(8,128)S(1)}, f32[512,512]{1,0:T(8,128)S(1)}, f32[512,512]{1,0:T(8,128)S(1)}, f32[256,512]{1,0:T(8,128)S(1)}, /*index=5*/f32[256,512]{1,0:T(8,128)S(1)}) custom-call(s32[2]{0:T(128)S(1)} %pad_add_fusion.place, bf16[2048,384]{1,0:T(8,128)(2,1)S(1)} %shard_map.182.refs_7_.refs_0_, ...), custom_call_target="tpu_custom_call" | custom-call | flops 1 | bytes 1 | tf_op jit(solution)/shard_map/pallas_call | solution.py:121
  125.0 0.8 shard_map.191
  125.9 1.6 %collective-permute-start.30 = (f16[528,512]{1,0:T(8,128)(2,1)S(1)}, f16[528,512]{1,0:T(8,128)(2,1)S(1)}, u32[]{:S(2)}, u32[]{:S(2)}) collective-permute-start(f16[528,512]{1,0:T(8,128)(2,1)S(1)} %convert_element_type.26), channel_id=1, source_target_pairs={{0,2},{1,3},{2,0},{3,1},{4,6},{5,7},{6,4},{7,5},{8,10},{9,11},{10,... | collective-permute-start | bytes 1622024 | tf_op jit(solution)/shard_map/ppermute | solution.py:455
  127.6 3.2 %collective-permute-done.32 = f16[272,512]{1,0:T(8,128)(2,1)S(1)} collective-permute-done((f16[272,512]{1,0:T(8,128)(2,1)S(1)}, f16[272,512]{1,0:T(8,128)(2,1)S(1)}, u32[]{:S(2)}, u32[]{:S(2)}) %collective-permute-start.32) | collective-permute-done | bytes 278560 | tf_op jit(solution)/shard_map/ppermute | solution.py:455
  131.0 2.9 %shard_map.193 = (f32[512,512]{1,0:T(8,128)}, f32[512,512]{1,0:T(8,128)}, f32[512,512]{1,0:T(8,128)}) custom-call(s32[2]{0:T(128)S(1)} %pad_add_fusion.place, f32[512,512]{1,0:T(8,128)S(1)} %copy-done, f32[512,512]{1,0:T(8,128)S(1)} %copy-done.3, f32[512,512]{1,0:T(8,128)S(1)} %copy-done.4, f32[256,512]{1,0:T(8,128)S(1)} %multiply_add_fusion.3.near, ...), custom_call_target="tpu_custom_call" | custom-call | flops 1 | bytes 1 | tf_op jit(solution)/shard_map/pallas_call | solution.py:655
  134.0 7.9 %collective-permute-done.30 = f16[528,512]{1,0:T(8,128)(2,1)S(1)} collective-permute-done((f16[528,512]{1,0:T(8,128)(2,1)S(1)}, f16[528,512]{1,0:T(8,128)(2,1)S(1)}, u32[]{:S(2)}, u32[]{:S(2)}) %collective-permute-start.30) | collective-permute-done | bytes 540704 | tf_op jit(solution)/shard_map/ppermute | solution.py:455
  142.0 1.1 shard_map.192
  143.1 2.3 %divide_subtract_fusion = (f32[512,512]{1,0:T(8,128)}, f32[512,512]{1,0:T(8,128)}, f32[512,512]{1,0:T(8,128)}) fusion(f32[512,512]{1,0:T(8,128)S(1)} %copy-done.2, f32[512]{0:T(512)S(1)} %bitcast.15, f16[528,512]{1,0:T(8,128)(2,1)S(1)} %collective-permute-done.30, f32[512,512]{1,0:T(8,128)S(1)} %get-tuple-element.92, ...), kind=kLoop, calls=%fused_computation.2 | loop fusion | flops 4194304 | bytes 8914944 | tf_op jit(solution)/shard_map/sub | solution.py:28
  (74 shorter events, 7.1 us)
Async XLA Ops:
  0.6 16.4 %copy-start = (f32[512,512]{1,0:T(8,128)S(1)}, f32[512,512]{1,0:T(8,128)}, u32[]{:S(2)}) copy-start(f32[512,512]{1,0:T(8,128)} %param.20) | copy-start | bytes 3145732
  0.7 1.3 copy-start.1
  2.0 0.7 copy-start.6
  2.7 1.1 copy-start.5
  3.3 13.8 %collective-permute-start.5 = (bf16[528,512]{1,0:T(8,128)(2,1)S(1)}, bf16[528,512]{1,0:T(8,128)(2,1)S(1)}, u32[]{:S(2)}, u32[]{:S(2)}) collective-permute-start(bf16[528,512]{1,0:T(8,128)(2,1)S(1)} %shard_map.178.refs_6_), channel_id=1, source_target_pairs={{0,1},{1,0},{2,3},{3,2},{4,5},{5,4},{6,7},{7,6},{8,9},{9,8},{10,11... | collective-permute-start | bytes 1622024 | tf_op jit(solution)/shard_map/ppermute | solution.py:455
  3.8 15.3 %collective-permute-start.2 = (bf16[384,512]{1,0:T(8,128)(2,1)S(1)}, bf16[384,512]{1,0:T(8,128)(2,1)S(1)}, u32[]{:S(2)}, u32[]{:S(2)}) collective-permute-start(bf16[384,512]{1,0:T(8,128)(2,1)S(1)} %copy-done.5), channel_id=1, source_target_pairs={{0,8},{12,4},{1,9},{13,5},{2,10},{14,6},{3,11},{15,7},{16,24},{28,... | collective-permute-start | bytes 1179656 | tf_op jit(solution)/shard_map/ppermute | solution.py:451
  9.6 13.0 %collective-permute-start.1 = (bf16[384,512]{1,0:T(8,128)(2,1)S(1)}, bf16[384,512]{1,0:T(8,128)(2,1)S(1)}, u32[]{:S(2)}, u32[]{:S(2)}) collective-permute-start(bf16[384,512]{1,0:T(8,128)(2,1)S(1)} %copy-done.5), channel_id=1, source_target_pairs={{4,0},{8,4},{12,8},{5,1},{9,5},{13,9},{6,2},{10,6},{14,10},{7,3},{... | collective-permute-start | bytes 1179656 | tf_op jit(solution)/shard_map/ppermute | solution.py:451
  10.9 20.1 %collective-permute-start = (bf16[384,512]{1,0:T(8,128)(2,1)S(1)}, bf16[384,512]{1,0:T(8,128)(2,1)S(1)}, u32[]{:S(2)}, u32[]{:S(2)}) collective-permute-start(bf16[384,512]{1,0:T(8,128)(2,1)S(1)} %copy-done.5), channel_id=1, source_target_pairs={{0,4},{4,8},{8,12},{1,5},{5,9},{9,13},{2,6},{6,10},{10,14},{3,7},{... | collective-permute-start | bytes 1179656 | tf_op jit(solution)/shard_map/ppermute | solution.py:451
  15.5 16.2 %collective-permute-start.6 = (bf16[528,512]{1,0:T(8,128)(2,1)S(1)}, bf16[528,512]{1,0:T(8,128)(2,1)S(1)}, u32[]{:S(2)}, u32[]{:S(2)}) collective-permute-start(bf16[528,512]{1,0:T(8,128)(2,1)S(1)} %shard_map.178.refs_6_), channel_id=1, source_target_pairs={{0,2},{1,3},{2,0},{3,1},{4,6},{5,7},{6,4},{7,5},{8,10},{9,11},{10,... | collective-permute-start | bytes 1622024 | tf_op jit(solution)/shard_map/ppermute | solution.py:455
  17.7 23.0 %collective-permute-start.9 = (bf16[528,512]{1,0:T(8,128)(2,1)S(1)}, bf16[528,512]{1,0:T(8,128)(2,1)S(1)}, u32[]{:S(2)}, u32[]{:S(2)}) collective-permute-start(bf16[528,512]{1,0:T(8,128)(2,1)S(1)} %shard_map.179.refs_0_.refs_4_.refs_3_), channel_id=1, source_target_pairs={{0,2},{1,3},{2,0},{3,1},{4,6},{5,7},{6,4},{7,5},{8,10},{9,11},{10,... | collective-permute-start | bytes 1622024 | tf_op jit(solution)/shard_map/ppermute | solution.py:455
  19.1 18.4 %collective-permute-start.4 = (bf16[384,512]{1,0:T(8,128)(2,1)S(1)}, bf16[384,512]{1,0:T(8,128)(2,1)S(1)}, u32[]{:S(2)}, u32[]{:S(2)}) collective-permute-start(bf16[384,512]{1,0:T(8,128)(2,1)S(1)} %collective-permute-done.2.refs_3_), channel_id=1, source_target_pairs={{4,0},{8,12},{5,1},{9,13},{6,2},{10,14},{7,3},{11,15},{20,16},{24,... | collective-permute-start | bytes 1179656 | tf_op jit(solution)/shard_map/ppermute | solution.py:451
  22.6 16.2 %collective-permute-start.8 = (bf16[256,512]{1,0:T(8,128)(2,1)S(1)}, bf16[256,512]{1,0:T(8,128)(2,1)S(1)}, u32[]{:S(2)}, u32[]{:S(2)}) collective-permute-start(bf16[256,512]{1,0:T(8,128)(2,1)S(1)} %get-tuple-element.61), channel_id=1, source_target_pairs={{0,4},{4,8},{1,5},{5,9},{2,6},{6,10},{3,7},{7,11},{16,20},{20,24},... | collective-permute-start | bytes 786440 | tf_op jit(solution)/shard_map/ppermute | solution.py:451
  31.0 9.7 %collective-permute-start.10 = (bf16[256,512]{1,0:T(8,128)(2,1)S(1)}, bf16[256,512]{1,0:T(8,128)(2,1)S(1)}, u32[]{:S(2)}, u32[]{:S(2)}) collective-permute-start(bf16[256,512]{1,0:T(8,128)(2,1)S(1)} %get-tuple-element.63), channel_id=1, source_target_pairs={{8,4},{12,8},{9,5},{13,9},{10,6},{14,10},{11,7},{15,11},{24,20},{2... | collective-permute-start | bytes 786440 | tf_op jit(solution)/shard_map/ppermute | solution.py:451
  31.7 10.6 %collective-permute-start.11 = (bf16[256,512]{1,0:T(8,128)(2,1)S(1)}, bf16[256,512]{1,0:T(8,128)(2,1)S(1)}, u32[]{:S(2)}, u32[]{:S(2)}) collective-permute-start(bf16[256,512]{1,0:T(8,128)(2,1)S(1)} %get-tuple-element.65), channel_id=1, source_target_pairs={{0,8},{12,4},{1,9},{13,5},{2,10},{14,6},{3,11},{15,7},{16,24},{28,... | collective-permute-start | bytes 786440 | tf_op jit(solution)/shard_map/ppermute | solution.py:451
  37.6 11.8 %collective-permute-start.3 = (bf16[384,512]{1,0:T(8,128)(2,1)S(1)}, bf16[384,512]{1,0:T(8,128)(2,1)S(1)}, u32[]{:S(2)}, u32[]{:S(2)}) collective-permute-start(bf16[384,512]{1,0:T(8,128)(2,1)S(1)} %shard_map.177), channel_id=1, source_target_pairs={{4,0},{8,12},{5,1},{9,13},{6,2},{10,14},{7,3},{11,15},{20,16},{24,... | collective-permute-start | bytes 1179656 | tf_op jit(solution)/shard_map/ppermute | solution.py:451
  38.9 10.5 %collective-permute-start.12 = (bf16[528,512]{1,0:T(8,128)(2,1)S(1)}, bf16[528,512]{1,0:T(8,128)(2,1)S(1)}, u32[]{:S(2)}, u32[]{:S(2)}) collective-permute-start(bf16[528,512]{1,0:T(8,128)(2,1)S(1)} %shard_map.179.refs_0_.refs_4_.refs_3_), channel_id=1, source_target_pairs={{0,1},{1,0},{2,3},{3,2},{4,5},{5,4},{6,7},{7,6},{8,9},{9,8},{10,11... | collective-permute-start | bytes 1622024 | tf_op jit(solution)/shard_map/ppermute | solution.py:455
  40.7 8.7 %collective-permute-start.7 = (bf16[528,512]{1,0:T(8,128)(2,1)S(1)}, bf16[528,512]{1,0:T(8,128)(2,1)S(1)}, u32[]{:S(2)}, u32[]{:S(2)}) collective-permute-start(bf16[528,512]{1,0:T(8,128)(2,1)S(1)} %collective-permute-done.6.refs_8_), channel_id=1, source_target_pairs={{0,1},{1,0},{2,3},{3,2},{4,5},{5,4},{6,7},{7,6},{8,9},{9,8},{10,11... | collective-permute-start | bytes 1622024 | tf_op jit(solution)/shard_map/ppermute | solution.py:455
  40.7 8.7 %collective-permute-start.13 = (bf16[528,512]{1,0:T(8,128)(2,1)S(1)}, bf16[528,512]{1,0:T(8,128)(2,1)S(1)}, u32[]{:S(2)}, u32[]{:S(2)}) collective-permute-start(bf16[528,512]{1,0:T(8,128)(2,1)S(1)} %collective-permute-done.9.refs_5_.refs_6_), channel_id=1, source_target_pairs={{0,1},{1,0},{2,3},{3,2},{4,5},{5,4},{6,7},{7,6},{8,9},{9,8},{10,11... | collective-permute-start | bytes 1622024 | tf_op jit(solution)/shard_map/ppermute | solution.py:455
  42.4 15.6 %collective-permute-start.18 = (bf16[768,512]{1,0:T(8,128)(2,1)S(1)}, bf16[768,512]{1,0:T(8,128)(2,1)S(1)}, u32[]{:S(2)}, u32[]{:S(2)}) collective-permute-start(bf16[768,512]{1,0:T(8,128)(2,1)S(1)} %constant_dynamic-update-slice_fusion.refs_10_.refs_6_), channel_id=1, source_target_pairs={{4,6},{5,7},{6,4},{7,5},{8,10},{9,11},{10,8},{11,9},{20,22},{21,23... | collective-permute-start | bytes 2359304 | tf_op jit(solution)/shard_map/ppermute | solution.py:455
  51.2 11.4 %collective-permute-start.14 = (bf16[384,512]{1,0:T(8,128)(2,1)S(1)}, bf16[384,512]{1,0:T(8,128)(2,1)S(1)}, u32[]{:S(2)}, u32[]{:S(2)}) collective-permute-start(bf16[384,512]{1,0:T(8,128)(2,1)S(1)} %get-tuple-element.68.refs_0_.refs_2_.refs_4_), channel_id=1, source_target_pairs={{0,8},{12,4},{1,9},{13,5},{2,10},{14,6},{3,11},{15,7},{16,24},{28,... | collective-permute-start | bytes 1179656 | tf_op jit(solution)/shard_map/ppermute | solution.py:451
  53.0 10.2 %collective-permute-start.16 = (bf16[384,512]{1,0:T(8,128)(2,1)S(1)}, bf16[384,512]{1,0:T(8,128)(2,1)S(1)}, u32[]{:S(2)}, u32[]{:S(2)}) collective-permute-start(bf16[384,512]{1,0:T(8,128)(2,1)S(1)} %get-tuple-element.68.refs_0_.refs_2_.refs_4_), channel_id=1, source_target_pairs={{4,8},{8,4},{5,9},{9,5},{6,10},{10,6},{7,11},{11,7},{20,24},{24,20... | collective-permute-start | bytes 1179656 | tf_op jit(solution)/shard_map/ppermute | solution.py:451
  53.7 16.5 %collective-permute-start.15 = (bf16[384,512]{1,0:T(8,128)(2,1)S(1)}, bf16[384,512]{1,0:T(8,128)(2,1)S(1)}, u32[]{:S(2)}, u32[]{:S(2)}) collective-permute-start(bf16[384,512]{1,0:T(8,128)(2,1)S(1)} %get-tuple-element.68.refs_0_.refs_2_.refs_4_), channel_id=1, source_target_pairs={{0,4},{12,8},{1,5},{13,9},{2,6},{14,10},{3,7},{15,11},{16,20},{28,... | collective-permute-start | bytes 1179656 | tf_op jit(solution)/shard_map/ppermute | solution.py:451
  57.3 14.5 %collective-permute-start.17 = (bf16[768,512]{1,0:T(8,128)(2,1)S(1)}, bf16[768,512]{1,0:T(8,128)(2,1)S(1)}, u32[]{:S(2)}, u32[]{:S(2)}) collective-permute-start(bf16[768,512]{1,0:T(8,128)(2,1)S(1)} %constant_dynamic-update-slice_fusion.refs_10_.refs_6_), channel_id=1, source_target_pairs={{4,5},{5,4},{6,7},{7,6},{8,9},{9,8},{10,11},{11,10},{20,21},{21,20... | collective-permute-start | bytes 2359304 | tf_op jit(solution)/shard_map/ppermute | solution.py:455
  62.5 9.3 %collective-permute-start.19 = (bf16[768,512]{1,0:T(8,128)(2,1)S(1)}, bf16[768,512]{1,0:T(8,128)(2,1)S(1)}, u32[]{:S(2)}, u32[]{:S(2)}) collective-permute-start(bf16[768,512]{1,0:T(8,128)(2,1)S(1)} %collective-permute-done.18.refs_7_), channel_id=1, source_target_pairs={{4,5},{5,4},{6,7},{7,6},{8,9},{9,8},{10,11},{11,10},{20,21},{21,20... | collective-permute-start | bytes 2359304 | tf_op jit(solution)/shard_map/ppermute | solution.py:455
  73.4 23.4 %collective-permute-start.22 = (bf16[384,1024]{1,0:T(8,128)(2,1)S(1)}, bf16[384,1024]{1,0:T(8,128)(2,1)S(1)}, u32[]{:S(2)}, u32[]{:S(2)}) collective-permute-start(bf16[384,1024]{1,0:T(8,128)(2,1)S(1)} %shard_map.184.refs_0_), channel_id=1, source_target_pairs={{4,0},{8,12},{5,1},{9,13},{6,2},{10,14},{7,3},{11,15},{20,16},{24,... | collective-permute-start | bytes 2359304 | tf_op jit(solution)/shard_map/ppermute | solution.py:451
  74.7 22.1 %collective-permute-start.20 = (bf16[384,1024]{1,0:T(8,128)(2,1)S(1)}, bf16[384,1024]{1,0:T(8,128)(2,1)S(1)}, u32[]{:S(2)}, u32[]{:S(2)}) collective-permute-start(bf16[384,1024]{1,0:T(8,128)(2,1)S(1)} %shard_map.184.refs_0_), channel_id=1, source_target_pairs={{4,8},{8,4},{5,9},{9,5},{6,10},{10,6},{7,11},{11,7},{20,24},{24,20... | collective-permute-start | bytes 2359304 | tf_op jit(solution)/shard_map/ppermute | solution.py:451
  75.4 41.4 %collective-permute-start.21 = (bf16[384,1024]{1,0:T(8,128)(2,1)S(1)}, bf16[384,1024]{1,0:T(8,128)(2,1)S(1)}, u32[]{:S(2)}, u32[]{:S(2)}) collective-permute-start(bf16[384,1024]{1,0:T(8,128)(2,1)S(1)} %shard_map.184.refs_0_), channel_id=1, source_target_pairs={{8,0},{4,12},{9,1},{5,13},{10,2},{6,14},{11,3},{7,15},{24,16},{20,... | collective-permute-start | bytes 2359304 | tf_op jit(solution)/shard_map/ppermute | solution.py:451
  98.6 2.0 %collective-permute-start.23 = (f32[264,512]{1,0:T(8,128)S(1)}, f32[264,512]{1,0:T(8,128)S(1)}, u32[]{:S(2)}, u32[]{:S(2)}) collective-permute-start(f32[264,512]{1,0:T(8,128)S(1)} %get-tuple-element.73), channel_id=1, source_target_pairs={{0,1},{1,0},{2,3},{3,2},{4,5},{5,4},{6,7},{7,6},{8,9},{9,8},{10,11... | collective-permute-start | bytes 1622024 | tf_op jit(solution)/shard_map/ppermute | solution.py:455
  98.6 18.2 %collective-permute-start.24 = (f32[256,512]{1,0:T(8,128)S(1)}, f32[256,512]{1,0:T(8,128)S(1)}, u32[]{:S(2)}, u32[]{:S(2)}) collective-permute-start(f32[256,512]{1,0:T(8,128)S(1)} %get-tuple-element.75), channel_id=1, source_target_pairs={{0,1},{1,0},{2,3},{3,2},{4,5},{5,4},{6,7},{7,6},{8,9},{9,8},{10,11... | collective-permute-start | bytes 1572872 | tf_op jit(solution)/shard_map/ppermute | solution.py:455
  101.3 16.8 %collective-permute-start.25 = (f16[272,512]{1,0:T(8,128)(2,1)S(1)}, f16[272,512]{1,0:T(8,128)(2,1)S(1)}, u32[]{:S(2)}, u32[]{:S(2)}) collective-permute-start(f16[272,512]{1,0:T(8,128)(2,1)S(1)} %convert_element_type.25), channel_id=1, source_target_pairs={{0,2},{1,3},{2,0},{3,1},{4,6},{5,7},{6,4},{7,5},{8,10},{9,11},{10,... | collective-permute-start | bytes 835592 | tf_op jit(solution)/shard_map/ppermute | solution.py:455
  118.1 2.5 %collective-permute-start.26 = (f32[256,512]{1,0:T(8,128)S(1)}, f32[256,512]{1,0:T(8,128)S(1)}, u32[]{:S(2)}, u32[]{:S(2)}) collective-permute-start(f32[256,512]{1,0:T(8,128)S(1)} %get-tuple-element.83), channel_id=1, source_target_pairs={{0,1},{1,0},{2,3},{3,2},{4,5},{5,4},{6,7},{7,6},{8,9},{9,8},{10,11... | collective-permute-start | bytes 1572872 | tf_op jit(solution)/shard_map/ppermute | solution.py:455
  119.9 5.1 %collective-permute-start.27 = (f32[264,512]{1,0:T(8,128)S(1)}, f32[264,512]{1,0:T(8,128)S(1)}, u32[]{:S(2)}, u32[]{:S(2)}) collective-permute-start(f32[264,512]{1,0:T(8,128)S(1)} %get-tuple-element.87), channel_id=1, source_target_pairs={{0,1},{1,0},{2,3},{3,2},{4,5},{5,4},{6,7},{7,6},{8,9},{9,8},{10,11... | collective-permute-start | bytes 1622024 | tf_op jit(solution)/shard_map/ppermute | solution.py:455
  120.4 4.5 %collective-permute-start.28 = (f32[256,512]{1,0:T(8,128)S(1)}, f32[256,512]{1,0:T(8,128)S(1)}, u32[]{:S(2)}, u32[]{:S(2)}) collective-permute-start(f32[256,512]{1,0:T(8,128)S(1)} %get-tuple-element.88), channel_id=1, source_target_pairs={{0,1},{1,0},{2,3},{3,2},{4,5},{5,4},{6,7},{7,6},{8,9},{9,8},{10,11... | collective-permute-start | bytes 1572872 | tf_op jit(solution)/shard_map/ppermute | solution.py:455
  121.2 9.5 %collective-permute-start.32 = (f16[272,512]{1,0:T(8,128)(2,1)S(1)}, f16[272,512]{1,0:T(8,128)(2,1)S(1)}, u32[]{:S(2)}, u32[]{:S(2)}) collective-permute-start(f16[272,512]{1,0:T(8,128)(2,1)S(1)} %convert_element_type.31), channel_id=1, source_target_pairs={{0,2},{1,3},{2,0},{3,1},{4,6},{5,7},{6,4},{7,5},{8,10},{9,11},{10,... | collective-permute-start | bytes 835592 | tf_op jit(solution)/shard_map/ppermute | solution.py:455
  124.4 6.4 %collective-permute-start.31 = (f32[256,512]{1,0:T(8,128)S(1)}, f32[256,512]{1,0:T(8,128)S(1)}, u32[]{:S(2)}, u32[]{:S(2)}) collective-permute-start(f32[256,512]{1,0:T(8,128)S(1)} %get-tuple-element.102), channel_id=1, source_target_pairs={{0,1},{1,0},{2,3},{3,2},{4,5},{5,4},{6,7},{7,6},{8,9},{9,8},{10,11... | collective-permute-start | bytes 1572872 | tf_op jit(solution)/shard_map/ppermute | solution.py:455
  124.5 18.5 %collective-permute-start.29 = (f32[512,512]{1,0:T(8,128)S(1)}, f32[512,512]{1,0:T(8,128)S(1)}, u32[]{:S(2)}, u32[]{:S(2)}) collective-permute-start(f32[512,512]{1,0:T(8,128)S(1)} %get-tuple-element.93), channel_id=1, source_target_pairs={{0,1},{1,0},{2,3},{3,2},{4,5},{5,4},{6,7},{7,6},{8,9},{9,8},{10,11... | collective-permute-start | bytes 3145736 | tf_op jit(solution)/shard_map/ppermute | solution.py:455
  125.9 16.0 %collective-permute-start.30 = (f16[528,512]{1,0:T(8,128)(2,1)S(1)}, f16[528,512]{1,0:T(8,128)(2,1)S(1)}, u32[]{:S(2)}, u32[]{:S(2)}) collective-permute-start(f16[528,512]{1,0:T(8,128)(2,1)S(1)} %convert_element_type.26), channel_id=1, source_target_pairs={{0,2},{1,3},{2,0},{3,1},{4,6},{5,7},{6,4},{7,5},{8,10},{9,11},{10,... | collective-permute-start | bytes 1622024 | tf_op jit(solution)/shard_map/ppermute | solution.py:455
  127.5 3.5 %copy-start.3 = (f32[512,512]{1,0:T(8,128)S(1)}, f32[512,512]{1,0:T(8,128)}, u32[]{:S(2)}) copy-start(f32[512,512]{1,0:T(8,128)} %moment) | copy-start | bytes 3145732
  127.5 3.5 %copy-start.4 = (f32[512,512]{1,0:T(8,128)S(1)}, f32[512,512]{1,0:T(8,128)}, u32[]{:S(2)}) copy-start(f32[512,512]{1,0:T(8,128)} %square) | copy-start | bytes 3145732
  131.0 11.0 %copy-start.7 = (f32[128]{0:T(128)S(1)}, f32[128]{0:T(128)}, u32[]{:S(2)}) copy-start(f32[128]{0:T(128)} %param.12) | copy-start | bytes 1540
  131.0 11.0 %copy-start.8 = (f32[128]{0:T(128)S(1)}, f32[128]{0:T(128)}, u32[]{:S(2)}) copy-start(f32[128]{0:T(128)} %param.16) | copy-start | bytes 1540
  131.0 11.0 %copy-start.9 = (f32[128]{0:T(128)S(1)}, f32[128]{0:T(128)}, u32[]{:S(2)}) copy-start(f32[128]{0:T(128)} %param.17) | copy-start | bytes 1540
  131.0 12.1 %copy-start.2 = (f32[512,512]{1,0:T(8,128)S(1)}, f32[512,512]{1,0:T(8,128)}, u32[]{:S(2)}) copy-start(f32[512,512]{1,0:T(8,128)} %refs_0_.3) | copy-start | bytes 3145732
  131.0 12.0 %copy-start.10 = (f32[512,512]{1,0:T(8,128)S(1)}, f32[512,512]{1,0:T(8,128)}, u32[]{:S(2)}) copy-start(f32[512,512]{1,0:T(8,128)} %param.14) | copy-start | bytes 3145732
  131.0 12.0 %copy-start.11 = (f32[512,512]{1,0:T(8,128)S(1)}, f32[512,512]{1,0:T(8,128)}, u32[]{:S(2)}) copy-start(f32[512,512]{1,0:T(8,128)} %param.15) | copy-start | bytes 3145732

commit v17 on v16

--- a/solution.py
+++ b/solution.py
@@ -113,20 +113,21 @@
 NOTABLE = 10**10
 
 
-def local_kernel(body, outs, place, *args, after=(), scratch=(), cost=1):
+def local_kernel(body, outs, place, *args, ahead=(), after=(), scratch=(), cost=1):
     def run(place, *refs):
+        refs = refs[len(ahead) :]
         body(place, *refs[: len(args)], *refs[len(args) + len(after) :])
 
     held = sum(a.size * jnp.dtype(a.dtype).itemsize for a in (*args, *outs))
     return pl.pallas_call(
         run,
         out_shape=outs,
-        in_specs=[SMEM] + [VMEM] * len(args) + [ANY] * len(after),
+        in_specs=[SMEM] + [ANY] * len(ahead) + [VMEM] * len(args) + [ANY] * len(after),
         out_specs=[VMEM] * len(outs),
         scratch_shapes=scratch,
         compiler_params=pltpu.CompilerParams(vmem_limit_bytes=held + 6 * 1024 * 1024),
         cost_estimate=pl.CostEstimate(flops=cost, bytes_accessed=1, transcendentals=0),
-    )(place, *args, *after)
+    )(place, *ahead, *args, *after)
 
 
 def shape(dims, dtype):
@@ -584,7 +585,7 @@
         swapped,
         direct,
         codes,
-        after=(near_packed, near_kept[1]),
+        ahead=(near_packed, near_kept[1]),
         cost=NOTABLE,
     )
     grad_low, bias_sum, norms, *send_far_enc = local_kernel(

time: 146 us -> 156 us (1.068)
  waiting for transfers between devices: 69.5 us -> 79.9 us
    ppermute x19, waiting for transfers between devices: 13.3 us -> 19.7 us  [flip(): return lax.ppermute(value, ('latent', 'dp'), pairs)]
    ppermute x14, waiting for transfers between devices: 56.2 us -> 60.1 us  [along(): return lax.ppermute(value, 'latent', pairs)]
where the time goes in v17:
time: 156 us
  waiting for transfers between devices  79.9 us (51%)
  starting transfers between devices  47.9 us (31%)
  Pallas kernels  21.8 us (14%)
  other arithmetic  2.92 us (2%)
  local copies, waits for them, and re-layouts  2.06 us (1%)
    ppermute x14, waiting for transfers between devices, along(): return lax.ppermute(value, 'latent', pairs)  60.1 us
    ppermute x14, starting transfers between devices, along(): return lax.ppermute(value, 'latent', pairs)  37.9 us
    ppermute x19, waiting for transfers between devices, flip(): return lax.ppermute(value, ('latent', 'dp'), pairs)  19.7 us
    pallas_call x16, Pallas kernels, local_kernel(): pl.pallas_call(run, out_shape=outs, in_specs=[SMEM] + [ANY] * len(ahead)...  18.9 us
    ppermute x19, starting transfers between devices, flip(): return lax.ppermute(value, ('latent', 'dp'), pairs)  9.91 us
  transfers between devices with their start and end apart: 33, of which 12 were waited for; matrix products, arithmetic and copies ran while one was open for 0% of the time, Pallas kernels for 13%

profile of v17, /device:TPU:0, one launch (start us, length us, event | category | flops | bytes accessed | tf_op | source)
XLA Modules:
  0.0 155.7 jit_solution(2345459720756737221)
XLA Ops:
  0.7 1.3 copy-done.1
  2.0 0.7 copy-done.6
  3.8 5.8 %collective-permute-start.2 = (bf16[384,512]{1,0:T(8,128)(2,1)S(1)}, bf16[384,512]{1,0:T(8,128)(2,1)S(1)}, u32[]{:S(2)}, u32[]{:S(2)}) collective-permute-start(bf16[384,512]{1,0:T(8,128)(2,1)S(1)} %copy-done.5), channel_id=1, source_target_pairs={{0,8},{12,4},{1,9},{13,5},{2,10},{14,6},{3,11},{15,7},{16,24},{28,... | collective-permute-start | bytes 1179656 | tf_op jit(solution)/shard_map/ppermute | solution.py:452
  9.6 1.3 collective-permute-start.1
  10.9 4.6 %collective-permute-start = (bf16[384,512]{1,0:T(8,128)(2,1)S(1)}, bf16[384,512]{1,0:T(8,128)(2,1)S(1)}, u32[]{:S(2)}, u32[]{:S(2)}) collective-permute-start(bf16[384,512]{1,0:T(8,128)(2,1)S(1)} %copy-done.5), channel_id=1, source_target_pairs={{0,4},{4,8},{8,12},{1,5},{5,9},{9,13},{2,6},{6,10},{10,14},{3,7},{... | collective-permute-start | bytes 1179656 | tf_op jit(solution)/shard_map/ppermute | solution.py:452
  15.5 1.6 collective-permute-start.6
  17.1 0.6 shard_map.179.refs_0_.refs_4_.refs_3_
  18.3 0.8 collective-permute-done.2.refs_3_
  19.1 1.3 collective-permute-start.4
  21.0 1.6 %collective-permute-done.1.refs_1_.refs_2_ = bf16[384,512]{1,0:T(8,128)(2,1)S(1)} collective-permute-done((bf16[384,512]{1,0:T(8,128)(2,1)S(1)}, bf16[384,512]{1,0:T(8,128)(2,1)S(1)}, u32[]{:S(2)}, u32[]{:S(2)}) %collective-permute-start.1) | collective-permute-done | bytes 393248 | tf_op jit(solution)/shard_map/ppermute | solution.py:452
  22.6 8.4 %collective-permute-start.8 = (bf16[256,512]{1,0:T(8,128)(2,1)S(1)}, bf16[256,512]{1,0:T(8,128)(2,1)S(1)}, u32[]{:S(2)}, u32[]{:S(2)}) collective-permute-start(bf16[256,512]{1,0:T(8,128)(2,1)S(1)} %get-tuple-element.61), channel_id=1, source_target_pairs={{0,4},{4,8},{1,5},{5,9},{2,6},{6,10},{3,7},{7,11},{16,20},{20,24},... | collective-permute-start | bytes 786440 | tf_op jit(solution)/shard_map/ppermute | solution.py:452
  31.0 0.7 collective-permute-start.10
  31.7 5.2 %collective-permute-start.11 = (bf16[256,512]{1,0:T(8,128)(2,1)S(1)}, bf16[256,512]{1,0:T(8,128)(2,1)S(1)}, u32[]{:S(2)}, u32[]{:S(2)}) collective-permute-start(bf16[256,512]{1,0:T(8,128)(2,1)S(1)} %get-tuple-element.65), channel_id=1, source_target_pairs={{0,8},{12,4},{1,9},{13,5},{2,10},{14,6},{3,11},{15,7},{16,24},{28,... | collective-permute-start | bytes 786440 | tf_op jit(solution)/shard_map/ppermute | solution.py:452
  37.6 1.3 collective-permute-start.3
  38.9 1.8 %collective-permute-done.9.refs_5_.refs_6_ = bf16[528,512]{1,0:T(8,128)(2,1)S(1)} collective-permute-done((bf16[528,512]{1,0:T(8,128)(2,1)S(1)}, bf16[528,512]{1,0:T(8,128)(2,1)S(1)}, u32[]{:S(2)}, u32[]{:S(2)}) %collective-permute-start.9) | collective-permute-done | bytes 540704 | tf_op jit(solution)/shard_map/ppermute | solution.py:456
  41.3 1.1 collective-permute-done.11
  42.4 0.7 collective-permute-start.18
  43.1 6.2 %collective-permute-done.3.refs_4_ = bf16[384,512]{1,0:T(8,128)(2,1)S(1)} collective-permute-done((bf16[384,512]{1,0:T(8,128)(2,1)S(1)}, bf16[384,512]{1,0:T(8,128)(2,1)S(1)}, u32[]{:S(2)}, u32[]{:S(2)}) %collective-permute-start.3) | collective-permute-done | bytes 393248 | tf_op jit(solution)/shard_map/ppermute | solution.py:452
  49.4 1.8 %shard_map.181 = (bf16[384,512]{1,0:T(8,128)(2,1)S(1)}, bf16[384,512]{1,0:T(8,128)(2,1)S(1)}, bf16[384,2048]{1,0:T(8,128)(2,1)S(1)}, f32[1,512]{1,0:T(1,128)S(1)}) custom-call(s32[2]{0:T(128)S(1)} %pad_add_fusion.place, bf16[384,512]{1,0:T(8,128)(2,1)S(1)} %copy-done.5, bf16[384,512]{1,0:T(8,128)(2,1)S(1)} %collective-permute-done.refs_0_.refs_1_, ...), custom_call_target="tpu_custom_call" | custom-call | flops 1 | bytes 1 | tf_op jit(solution)/shard_map/pallas_call | solution.py:122
  51.2 1.9 %collective-permute-start.14 = (bf16[384,512]{1,0:T(8,128)(2,1)S(1)}, bf16[384,512]{1,0:T(8,128)(2,1)S(1)}, u32[]{:S(2)}, u32[]{:S(2)}) collective-permute-start(bf16[384,512]{1,0:T(8,128)(2,1)S(1)} %get-tuple-element.68.refs_0_.refs_2_.refs_4_), channel_id=1, source_target_pairs={{0,8},{12,4},{1,9},{13,5},{2,10},{14,6},{3,11},{15,7},{16,24},{28,... | collective-permute-start | bytes 1179656 | tf_op jit(solution)/shard_map/ppermute | solution.py:452
  53.0 0.7 collective-permute-start.16
  53.7 3.5 %collective-permute-start.15 = (bf16[384,512]{1,0:T(8,128)(2,1)S(1)}, bf16[384,512]{1,0:T(8,128)(2,1)S(1)}, u32[]{:S(2)}, u32[]{:S(2)}) collective-permute-start(bf16[384,512]{1,0:T(8,128)(2,1)S(1)} %get-tuple-element.68.refs_0_.refs_2_.refs_4_), channel_id=1, source_target_pairs={{0,4},{12,8},{1,5},{13,9},{2,6},{14,10},{3,7},{15,11},{16,20},{28,... | collective-permute-start | bytes 1179656 | tf_op jit(solution)/shard_map/ppermute | solution.py:452
  57.3 0.7 collective-permute-start.17
  58.0 4.5 %collective-permute-done.14.refs_1_.refs_2_ = bf16[384,512]{1,0:T(8,128)(2,1)S(1)} collective-permute-done((bf16[384,512]{1,0:T(8,128)(2,1)S(1)}, bf16[384,512]{1,0:T(8,128)(2,1)S(1)}, u32[]{:S(2)}, u32[]{:S(2)}) %collective-permute-start.14) | collective-permute-done | bytes 393248 | tf_op jit(solution)/shard_map/ppermute | solution.py:452
  62.5 0.7 collective-permute-start.19
  63.2 7.0 %collective-permute-done.15.refs_1_ = bf16[384,512]{1,0:T(8,128)(2,1)S(1)} collective-permute-done((bf16[384,512]{1,0:T(8,128)(2,1)S(1)}, bf16[384,512]{1,0:T(8,128)(2,1)S(1)}, u32[]{:S(2)}, u32[]{:S(2)}) %collective-permute-start.15) | collective-permute-done | bytes 393248 | tf_op jit(solution)/shard_map/ppermute | solution.py:452
  70.2 1.5 shard_map.183.refs_9_
  71.8 1.6 %shard_map.184.refs_0_ = bf16[384,1024]{1,0:T(8,128)(2,1)S(1)} custom-call(s32[2]{0:T(128)S(1)} %pad_add_fusion.place, bf16[384,512]{1,0:T(8,128)(2,1)S(1)} %get-tuple-element.68.refs_0_.refs_2_.refs_4_, bf16[384,512]{1,0:T(8,128)(2,1)S(1)} %collective-permute-done.15.refs_1_, bf16[384,512]{1,0:T(8,128)(2,1)S(1)} %collective-permute-done.14.refs_1_.refs_2_, ...), custom_call_target="tpu_custom_call" | custom-call | flops 1 | bytes 1 | tf_op jit(solution)/shard_map/pallas_call | solution.py:122
  73.4 0.7 collective-permute-start.21
  74.1 1.3 collective-permute-start.20
  75.4 1.3 collective-permute-start.24
  76.7 38.8 %collective-permute-done.20.refs_1_ = bf16[384,1024]{1,0:T(8,128)(2,1)S(1)} collective-permute-done((bf16[384,1024]{1,0:T(8,128)(2,1)S(1)}, bf16[384,1024]{1,0:T(8,128)(2,1)S(1)}, u32[]{:S(2)}, u32[]{:S(2)}) %collective-permute-start.20) | collective-permute-done | bytes 786464 | tf_op jit(solution)/shard_map/ppermute | solution.py:452
  115.6 1.8 %shard_map.185 = (f32[384,512]{1,0:T(8,128)S(1)}, bf16[384,1024]{1,0:T(8,128)(2,1)S(1)}, f32[264,512]{1,0:T(8,128)S(1)}, f32[256,512]{1,0:T(8,128)S(1)}, f32[256,512]{1,0:T(8,128)S(1)}, /*index=5*/f32[256,512]{1,0:T(8,128)S(1)}) custom-call(s32[2]{0:T(128)S(1)} %pad_add_fusion.place, bf16[384,1024]{1,0:T(8,128)(2,1)S(1)} %shard_map.184.refs_0_, ...), custom_call_target="tpu_custom_call" | custom-call | flops 1 | bytes 1 | tf_op jit(solution)/shard_map/pallas_call | solution.py:122
  117.9 1.0 shard_map.182.refs_7_.refs_0_
  119.3 0.7 shard_map.186
  120.1 0.6 collective-permute-start.25
  120.7 1.3 shard_map.187
  122.0 6.8 %collective-permute-done.25 = f16[272,512]{1,0:T(8,128)(2,1)S(1)} collective-permute-done((f16[272,512]{1,0:T(8,128)(2,1)S(1)}, f16[272,512]{1,0:T(8,128)(2,1)S(1)}, u32[]{:S(2)}, u32[]{:S(2)}) %collective-permute-start.25) | collective-permute-done | bytes 278560 | tf_op jit(solution)/shard_map/ppermute | solution.py:456
  128.9 1.7 %shard_map.188 = (bf16[384,512]{1,0:T(8,128)(2,1)S(1)}, f32[1,512]{1,0:T(1,128)S(1)}, f32[1,512]{1,0:T(1,128)S(1)}, f32[264,512]{1,0:T(8,128)S(1)}, f32[256,512]{1,0:T(8,128)S(1)}) custom-call(s32[2]{0:T(128)S(1)} %pad_add_fusion.place, bf16[384,1024]{1,0:T(8,128)(2,1)S(1)} %get-tuple-element.76.refs_0_.refs_3_, f32[384,512]{1,0:T(8,128)S(1)} %get-tuple-element.78.refs_1_, ...), custom_call_target="tpu_custom_call" | custom-call | flops 10000000000 | bytes 1 | tf_op jit(solution)/shard_map/pallas_call | solution.py:122
  131.2 0.7 shard_map.189.refs_5_
  132.5 2.5 %shard_map.190 = (bf16[384,512]{1,0:T(8,128)(2,1)}, f32[512,512]{1,0:T(8,128)S(1)}, f32[512,512]{1,0:T(8,128)S(1)}, f32[512,512]{1,0:T(8,128)S(1)}, f32[256,512]{1,0:T(8,128)S(1)}, /*index=5*/f32[256,512]{1,0:T(8,128)S(1)}) custom-call(s32[2]{0:T(128)S(1)} %pad_add_fusion.place, bf16[2048,384]{1,0:T(8,128)(2,1)S(1)} %shard_map.182.refs_7_.refs_0_, ...), custom_call_target="tpu_custom_call" | custom-call | flops 1 | bytes 1 | tf_op jit(solution)/shard_map/pallas_call | solution.py:122
  135.6 0.8 shard_map.191
  136.6 1.6 collective-permute-start.30
  138.3 3.2 %collective-permute-done.32 = f16[272,512]{1,0:T(8,128)(2,1)S(1)} collective-permute-done((f16[272,512]{1,0:T(8,128)(2,1)S(1)}, f16[272,512]{1,0:T(8,128)(2,1)S(1)}, u32[]{:S(2)}, u32[]{:S(2)}) %collective-permute-start.32) | collective-permute-done | bytes 278560 | tf_op jit(solution)/shard_map/ppermute | solution.py:456
  141.8 2.9 %shard_map.193 = (f32[512,512]{1,0:T(8,128)}, f32[512,512]{1,0:T(8,128)}, f32[512,512]{1,0:T(8,128)}) custom-call(s32[2]{0:T(128)S(1)} %pad_add_fusion.place, f32[512,512]{1,0:T(8,128)S(1)} %copy-done, f32[512,512]{1,0:T(8,128)S(1)} %copy-done.3, f32[512,512]{1,0:T(8,128)S(1)} %copy-done.4, f32[256,512]{1,0:T(8,128)S(1)} %multiply_add_fusion.3.near, ...), custom_call_target="tpu_custom_call" | custom-call | flops 1 | bytes 1 | tf_op jit(solution)/shard_map/pallas_call | solution.py:656
  144.7 7.5 %collective-permute-done.30 = f16[528,512]{1,0:T(8,128)(2,1)S(1)} collective-permute-done((f16[528,512]{1,0:T(8,128)(2,1)S(1)}, f16[528,512]{1,0:T(8,128)(2,1)S(1)}, u32[]{:S(2)}, u32[]{:S(2)}) %collective-permute-start.30) | collective-permute-done | bytes 540704 | tf_op jit(solution)/shard_map/ppermute | solution.py:456
  152.3 1.1 shard_map.192
  153.4 2.3 %divide_subtract_fusion = (f32[512,512]{1,0:T(8,128)}, f32[512,512]{1,0:T(8,128)}, f32[512,512]{1,0:T(8,128)}) fusion(f32[512,512]{1,0:T(8,128)S(1)} %copy-done.2, f32[512]{0:T(512)S(1)} %bitcast.15, f16[528,512]{1,0:T(8,128)(2,1)S(1)} %collective-permute-done.30, f32[512,512]{1,0:T(8,128)S(1)} %get-tuple-element.92, ...), kind=kLoop, calls=%fused_computation.2 | loop fusion | flops 4194304 | bytes 8914944 | tf_op jit(solution)/shard_map/sub | solution.py:28
  (74 shorter events, 7.1 us)
Async XLA Ops:
  0.6 16.4 %copy-start = (f32[512,512]{1,0:T(8,128)S(1)}, f32[512,512]{1,0:T(8,128)}, u32[]{:S(2)}) copy-start(f32[512,512]{1,0:T(8,128)} %param.20) | copy-start | bytes 3145732
  0.7 1.3 copy-start.1
  2.0 0.7 copy-start.6
  2.7 1.1 copy-start.5
  3.3 13.8 %collective-permute-start.5 = (bf16[528,512]{1,0:T(8,128)(2,1)S(1)}, bf16[528,512]{1,0:T(8,128)(2,1)S(1)}, u32[]{:S(2)}, u32[]{:S(2)}) collective-permute-start(bf16[528,512]{1,0:T(8,128)(2,1)S(1)} %shard_map.178.refs_6_), channel_id=1, source_target_pairs={{0,1},{1,0},{2,3},{3,2},{4,5},{5,4},{6,7},{7,6},{8,9},{9,8},{10,11... | collective-permute-start | bytes 1622024 | tf_op jit(solution)/shard_map/ppermute | solution.py:456
  3.8 15.3 %collective-permute-start.2 = (bf16[384,512]{1,0:T(8,128)(2,1)S(1)}, bf16[384,512]{1,0:T(8,128)(2,1)S(1)}, u32[]{:S(2)}, u32[]{:S(2)}) collective-permute-start(bf16[384,512]{1,0:T(8,128)(2,1)S(1)} %copy-done.5), channel_id=1, source_target_pairs={{0,8},{12,4},{1,9},{13,5},{2,10},{14,6},{3,11},{15,7},{16,24},{28,... | collective-permute-start | bytes 1179656 | tf_op jit(solution)/shard_map/ppermute | solution.py:452
  9.6 13.0 %collective-permute-start.1 = (bf16[384,512]{1,0:T(8,128)(2,1)S(1)}, bf16[384,512]{1,0:T(8,128)(2,1)S(1)}, u32[]{:S(2)}, u32[]{:S(2)}) collective-permute-start(bf16[384,512]{1,0:T(8,128)(2,1)S(1)} %copy-done.5), channel_id=1, source_target_pairs={{4,0},{8,4},{12,8},{5,1},{9,5},{13,9},{6,2},{10,6},{14,10},{7,3},{... | collective-permute-start | bytes 1179656 | tf_op jit(solution)/shard_map/ppermute | solution.py:452
  10.9 20.1 %collective-permute-start = (bf16[384,512]{1,0:T(8,128)(2,1)S(1)}, bf16[384,512]{1,0:T(8,128)(2,1)S(1)}, u32[]{:S(2)}, u32[]{:S(2)}) collective-permute-start(bf16[384,512]{1,0:T(8,128)(2,1)S(1)} %copy-done.5), channel_id=1, source_target_pairs={{0,4},{4,8},{8,12},{1,5},{5,9},{9,13},{2,6},{6,10},{10,14},{3,7},{... | collective-permute-start | bytes 1179656 | tf_op jit(solution)/shard_map/ppermute | solution.py:452
  15.5 16.2 %collective-permute-start.6 = (bf16[528,512]{1,0:T(8,128)(2,1)S(1)}, bf16[528,512]{1,0:T(8,128)(2,1)S(1)}, u32[]{:S(2)}, u32[]{:S(2)}) collective-permute-start(bf16[528,512]{1,0:T(8,128)(2,1)S(1)} %shard_map.178.refs_6_), channel_id=1, source_target_pairs={{0,2},{1,3},{2,0},{3,1},{4,6},{5,7},{6,4},{7,5},{8,10},{9,11},{10,... | collective-permute-start | bytes 1622024 | tf_op jit(solution)/shard_map/ppermute | solution.py:456
  17.7 23.0 %collective-permute-start.9 = (bf16[528,512]{1,0:T(8,128)(2,1)S(1)}, bf16[528,512]{1,0:T(8,128)(2,1)S(1)}, u32[]{:S(2)}, u32[]{:S(2)}) collective-permute-start(bf16[528,512]{1,0:T(8,128)(2,1)S(1)} %shard_map.179.refs_0_.refs_4_.refs_3_), channel_id=1, source_target_pairs={{0,2},{1,3},{2,0},{3,1},{4,6},{5,7},{6,4},{7,5},{8,10},{9,11},{10,... | collective-permute-start | bytes 1622024 | tf_op jit(solution)/shard_map/ppermute | solution.py:456
  19.1 18.4 %collective-permute-start.4 = (bf16[384,512]{1,0:T(8,128)(2,1)S(1)}, bf16[384,512]{1,0:T(8,128)(2,1)S(1)}, u32[]{:S(2)}, u32[]{:S(2)}) collective-permute-start(bf16[384,512]{1,0:T(8,128)(2,1)S(1)} %collective-permute-done.2.refs_3_), channel_id=1, source_target_pairs={{4,0},{8,12},{5,1},{9,13},{6,2},{10,14},{7,3},{11,15},{20,16},{24,... | collective-permute-start | bytes 1179656 | tf_op jit(solution)/shard_map/ppermute | solution.py:452
  22.6 16.2 %collective-permute-start.8 = (bf16[256,512]{1,0:T(8,128)(2,1)S(1)}, bf16[256,512]{1,0:T(8,128)(2,1)S(1)}, u32[]{:S(2)}, u32[]{:S(2)}) collective-permute-start(bf16[256,512]{1,0:T(8,128)(2,1)S(1)} %get-tuple-element.61), channel_id=1, source_target_pairs={{0,4},{4,8},{1,5},{5,9},{2,6},{6,10},{3,7},{7,11},{16,20},{20,24},... | collective-permute-start | bytes 786440 | tf_op jit(solution)/shard_map/ppermute | solution.py:452
  31.0 9.7 %collective-permute-start.10 = (bf16[256,512]{1,0:T(8,128)(2,1)S(1)}, bf16[256,512]{1,0:T(8,128)(2,1)S(1)}, u32[]{:S(2)}, u32[]{:S(2)}) collective-permute-start(bf16[256,512]{1,0:T(8,128)(2,1)S(1)} %get-tuple-element.63), channel_id=1, source_target_pairs={{8,4},{12,8},{9,5},{13,9},{10,6},{14,10},{11,7},{15,11},{24,20},{2... | collective-permute-start | bytes 786440 | tf_op jit(solution)/shard_map/ppermute | solution.py:452
  31.7 10.6 %collective-permute-start.11 = (bf16[256,512]{1,0:T(8,128)(2,1)S(1)}, bf16[256,512]{1,0:T(8,128)(2,1)S(1)}, u32[]{:S(2)}, u32[]{:S(2)}) collective-permute-start(bf16[256,512]{1,0:T(8,128)(2,1)S(1)} %get-tuple-element.65), channel_id=1, source_target_pairs={{0,8},{12,4},{1,9},{13,5},{2,10},{14,6},{3,11},{15,7},{16,24},{28,... | collective-permute-start | bytes 786440 | tf_op jit(solution)/shard_map/ppermute | solution.py:452
  37.6 11.8 %collective-permute-start.3 = (bf16[384,512]{1,0:T(8,128)(2,1)S(1)}, bf16[384,512]{1,0:T(8,128)(2,1)S(1)}, u32[]{:S(2)}, u32[]{:S(2)}) collective-permute-start(bf16[384,512]{1,0:T(8,128)(2,1)S(1)} %shard_map.177), channel_id=1, source_target_pairs={{4,0},{8,12},{5,1},{9,13},{6,2},{10,14},{7,3},{11,15},{20,16},{24,... | collective-permute-start | bytes 1179656 | tf_op jit(solution)/shard_map/ppermute | solution.py:452
  38.9 10.5 %collective-permute-start.12 = (bf16[528,512]{1,0:T(8,128)(2,1)S(1)}, bf16[528,512]{1,0:T(8,128)(2,1)S(1)}, u32[]{:S(2)}, u32[]{:S(2)}) collective-permute-start(bf16[528,512]{1,0:T(8,128)(2,1)S(1)} %shard_map.179.refs_0_.refs_4_.refs_3_), channel_id=1, source_target_pairs={{0,1},{1,0},{2,3},{3,2},{4,5},{5,4},{6,7},{7,6},{8,9},{9,8},{10,11... | collective-permute-start | bytes 1622024 | tf_op jit(solution)/shard_map/ppermute | solution.py:456
  40.7 8.7 %collective-permute-start.7 = (bf16[528,512]{1,0:T(8,128)(2,1)S(1)}, bf16[528,512]{1,0:T(8,128)(2,1)S(1)}, u32[]{:S(2)}, u32[]{:S(2)}) collective-permute-start(bf16[528,512]{1,0:T(8,128)(2,1)S(1)} %collective-permute-done.6.refs_8_), channel_id=1, source_target_pairs={{0,1},{1,0},{2,3},{3,2},{4,5},{5,4},{6,7},{7,6},{8,9},{9,8},{10,11... | collective-permute-start | bytes 1622024 | tf_op jit(solution)/shard_map/ppermute | solution.py:456
  40.7 8.7 %collective-permute-start.13 = (bf16[528,512]{1,0:T(8,128)(2,1)S(1)}, bf16[528,512]{1,0:T(8,128)(2,1)S(1)}, u32[]{:S(2)}, u32[]{:S(2)}) collective-permute-start(bf16[528,512]{1,0:T(8,128)(2,1)S(1)} %collective-permute-done.9.refs_5_.refs_6_), channel_id=1, source_target_pairs={{0,1},{1,0},{2,3},{3,2},{4,5},{5,4},{6,7},{7,6},{8,9},{9,8},{10,11... | collective-permute-start | bytes 1622024 | tf_op jit(solution)/shard_map/ppermute | solution.py:456
  42.4 15.6 %collective-permute-start.18 = (bf16[768,512]{1,0:T(8,128)(2,1)S(1)}, bf16[768,512]{1,0:T(8,128)(2,1)S(1)}, u32[]{:S(2)}, u32[]{:S(2)}) collective-permute-start(bf16[768,512]{1,0:T(8,128)(2,1)S(1)} %constant_dynamic-update-slice_fusion.refs_10_.refs_6_), channel_id=1, source_target_pairs={{4,6},{5,7},{6,4},{7,5},{8,10},{9,11},{10,8},{11,9},{20,22},{21,23... | collective-permute-start | bytes 2359304 | tf_op jit(solution)/shard_map/ppermute | solution.py:456
  51.2 11.4 %collective-permute-start.14 = (bf16[384,512]{1,0:T(8,128)(2,1)S(1)}, bf16[384,512]{1,0:T(8,128)(2,1)S(1)}, u32[]{:S(2)}, u32[]{:S(2)}) collective-permute-start(bf16[384,512]{1,0:T(8,128)(2,1)S(1)} %get-tuple-element.68.refs_0_.refs_2_.refs_4_), channel_id=1, source_target_pairs={{0,8},{12,4},{1,9},{13,5},{2,10},{14,6},{3,11},{15,7},{16,24},{28,... | collective-permute-start | bytes 1179656 | tf_op jit(solution)/shard_map/ppermute | solution.py:452
  53.0 10.2 %collective-permute-start.16 = (bf16[384,512]{1,0:T(8,128)(2,1)S(1)}, bf16[384,512]{1,0:T(8,128)(2,1)S(1)}, u32[]{:S(2)}, u32[]{:S(2)}) collective-permute-start(bf16[384,512]{1,0:T(8,128)(2,1)S(1)} %get-tuple-element.68.refs_0_.refs_2_.refs_4_), channel_id=1, source_target_pairs={{4,8},{8,4},{5,9},{9,5},{6,10},{10,6},{7,11},{11,7},{20,24},{24,20... | collective-permute-start | bytes 1179656 | tf_op jit(solution)/shard_map/ppermute | solution.py:452
  53.7 16.5 %collective-permute-start.15 = (bf16[384,512]{1,0:T(8,128)(2,1)S(1)}, bf16[384,512]{1,0:T(8,128)(2,1)S(1)}, u32[]{:S(2)}, u32[]{:S(2)}) collective-permute-start(bf16[384,512]{1,0:T(8,128)(2,1)S(1)} %get-tuple-element.68.refs_0_.refs_2_.refs_4_), channel_id=1, source_target_pairs={{0,4},{12,8},{1,5},{13,9},{2,6},{14,10},{3,7},{15,11},{16,20},{28,... | collective-permute-start | bytes 1179656 | tf_op jit(solution)/shard_map/ppermute | solution.py:452
  57.3 14.5 %collective-permute-start.17 = (bf16[768,512]{1,0:T(8,128)(2,1)S(1)}, bf16[768,512]{1,0:T(8,128)(2,1)S(1)}, u32[]{:S(2)}, u32[]{:S(2)}) collective-permute-start(bf16[768,512]{1,0:T(8,128)(2,1)S(1)} %constant_dynamic-update-slice_fusion.refs_10_.refs_6_), channel_id=1, source_target_pairs={{4,5},{5,4},{6,7},{7,6},{8,9},{9,8},{10,11},{11,10},{20,21},{21,20... | collective-permute-start | bytes 2359304 | tf_op jit(solution)/shard_map/ppermute | solution.py:456
  62.5 9.3 %collective-permute-start.19 = (bf16[768,512]{1,0:T(8,128)(2,1)S(1)}, bf16[768,512]{1,0:T(8,128)(2,1)S(1)}, u32[]{:S(2)}, u32[]{:S(2)}) collective-permute-start(bf16[768,512]{1,0:T(8,128)(2,1)S(1)} %collective-permute-done.18.refs_7_), channel_id=1, source_target_pairs={{4,5},{5,4},{6,7},{7,6},{8,9},{9,8},{10,11},{11,10},{20,21},{21,20... | collective-permute-start | bytes 2359304 | tf_op jit(solution)/shard_map/ppermute | solution.py:456
  73.4 3.3 %collective-permute-start.21 = (bf16[384,1024]{1,0:T(8,128)(2,1)S(1)}, bf16[384,1024]{1,0:T(8,128)(2,1)S(1)}, u32[]{:S(2)}, u32[]{:S(2)}) collective-permute-start(bf16[384,1024]{1,0:T(8,128)(2,1)S(1)} %shard_map.184.refs_0_), channel_id=1, source_target_pairs={{4,8},{8,4},{5,9},{9,5},{6,10},{10,6},{7,11},{11,7},{20,24},{24,20... | collective-permute-start | bytes 2359304 | tf_op jit(solution)/shard_map/ppermute | solution.py:452
  74.1 41.4 %collective-permute-start.20 = (bf16[384,1024]{1,0:T(8,128)(2,1)S(1)}, bf16[384,1024]{1,0:T(8,128)(2,1)S(1)}, u32[]{:S(2)}, u32[]{:S(2)}) collective-permute-start(bf16[384,1024]{1,0:T(8,128)(2,1)S(1)} %shard_map.184.refs_0_), channel_id=1, source_target_pairs={{4,0},{8,12},{5,1},{9,13},{6,2},{10,14},{7,3},{11,15},{20,16},{24,... | collective-permute-start | bytes 2359304 | tf_op jit(solution)/shard_map/ppermute | solution.py:452
  75.4 45.3 %collective-permute-start.24 = (bf16[384,1024]{1,0:T(8,128)(2,1)S(1)}, bf16[384,1024]{1,0:T(8,128)(2,1)S(1)}, u32[]{:S(2)}, u32[]{:S(2)}) collective-permute-start(bf16[384,1024]{1,0:T(8,128)(2,1)S(1)} %shard_map.184.refs_0_), channel_id=1, source_target_pairs={{8,0},{4,12},{9,1},{5,13},{10,2},{6,14},{11,3},{7,15},{24,16},{20,... | collective-permute-start | bytes 2359304 | tf_op jit(solution)/shard_map/ppermute | solution.py:452
  117.3 2.0 %collective-permute-start.22 = (f32[264,512]{1,0:T(8,128)S(1)}, f32[264,512]{1,0:T(8,128)S(1)}, u32[]{:S(2)}, u32[]{:S(2)}) collective-permute-start(f32[264,512]{1,0:T(8,128)S(1)} %get-tuple-element.73), channel_id=1, source_target_pairs={{0,1},{1,0},{2,3},{3,2},{4,5},{5,4},{6,7},{7,6},{8,9},{9,8},{10,11... | collective-permute-start | bytes 1622024 | tf_op jit(solution)/shard_map/ppermute | solution.py:456
  117.4 3.3 %collective-permute-start.23 = (f32[256,512]{1,0:T(8,128)S(1)}, f32[256,512]{1,0:T(8,128)S(1)}, u32[]{:S(2)}, u32[]{:S(2)}) collective-permute-start(f32[256,512]{1,0:T(8,128)S(1)} %get-tuple-element.75), channel_id=1, source_target_pairs={{0,1},{1,0},{2,3},{3,2},{4,5},{5,4},{6,7},{7,6},{8,9},{9,8},{10,11... | collective-permute-start | bytes 1572872 | tf_op jit(solution)/shard_map/ppermute | solution.py:456
  120.1 8.8 %collective-permute-start.25 = (f16[272,512]{1,0:T(8,128)(2,1)S(1)}, f16[272,512]{1,0:T(8,128)(2,1)S(1)}, u32[]{:S(2)}, u32[]{:S(2)}) collective-permute-start(f16[272,512]{1,0:T(8,128)(2,1)S(1)} %convert_element_type.25), channel_id=1, source_target_pairs={{0,2},{1,3},{2,0},{3,1},{4,6},{5,7},{6,4},{7,5},{8,10},{9,11},{10,... | collective-permute-start | bytes 835592 | tf_op jit(solution)/shard_map/ppermute | solution.py:456
  122.0 9.2 %collective-permute-start.26 = (f32[256,512]{1,0:T(8,128)S(1)}, f32[256,512]{1,0:T(8,128)S(1)}, u32[]{:S(2)}, u32[]{:S(2)}) collective-permute-start(f32[256,512]{1,0:T(8,128)S(1)} %get-tuple-element.83), channel_id=1, source_target_pairs={{0,1},{1,0},{2,3},{3,2},{4,5},{5,4},{6,7},{7,6},{8,9},{9,8},{10,11... | collective-permute-start | bytes 1572872 | tf_op jit(solution)/shard_map/ppermute | solution.py:456
  130.6 5.0 %collective-permute-start.27 = (f32[264,512]{1,0:T(8,128)S(1)}, f32[264,512]{1,0:T(8,128)S(1)}, u32[]{:S(2)}, u32[]{:S(2)}) collective-permute-start(f32[264,512]{1,0:T(8,128)S(1)} %get-tuple-element.87), channel_id=1, source_target_pairs={{0,1},{1,0},{2,3},{3,2},{4,5},{5,4},{6,7},{7,6},{8,9},{9,8},{10,11... | collective-permute-start | bytes 1622024 | tf_op jit(solution)/shard_map/ppermute | solution.py:456
  130.7 4.9 %collective-permute-start.28 = (f32[256,512]{1,0:T(8,128)S(1)}, f32[256,512]{1,0:T(8,128)S(1)}, u32[]{:S(2)}, u32[]{:S(2)}) collective-permute-start(f32[256,512]{1,0:T(8,128)S(1)} %get-tuple-element.88), channel_id=1, source_target_pairs={{0,1},{1,0},{2,3},{3,2},{4,5},{5,4},{6,7},{7,6},{8,9},{9,8},{10,11... | collective-permute-start | bytes 1572872 | tf_op jit(solution)/shard_map/ppermute | solution.py:456
  131.9 9.6 %collective-permute-start.32 = (f16[272,512]{1,0:T(8,128)(2,1)S(1)}, f16[272,512]{1,0:T(8,128)(2,1)S(1)}, u32[]{:S(2)}, u32[]{:S(2)}) collective-permute-start(f16[272,512]{1,0:T(8,128)(2,1)S(1)} %convert_element_type.31), channel_id=1, source_target_pairs={{0,2},{1,3},{2,0},{3,1},{4,6},{5,7},{6,4},{7,5},{8,10},{9,11},{10,... | collective-permute-start | bytes 835592 | tf_op jit(solution)/shard_map/ppermute | solution.py:456
  135.0 6.5 %collective-permute-start.31 = (f32[256,512]{1,0:T(8,128)S(1)}, f32[256,512]{1,0:T(8,128)S(1)}, u32[]{:S(2)}, u32[]{:S(2)}) collective-permute-start(f32[256,512]{1,0:T(8,128)S(1)} %get-tuple-element.102), channel_id=1, source_target_pairs={{0,1},{1,0},{2,3},{3,2},{4,5},{5,4},{6,7},{7,6},{8,9},{9,8},{10,11... | collective-permute-start | bytes 1572872 | tf_op jit(solution)/shard_map/ppermute | solution.py:456
  135.0 18.3 %collective-permute-start.29 = (f32[512,512]{1,0:T(8,128)S(1)}, f32[512,512]{1,0:T(8,128)S(1)}, u32[]{:S(2)}, u32[]{:S(2)}) collective-permute-start(f32[512,512]{1,0:T(8,128)S(1)} %get-tuple-element.93), channel_id=1, source_target_pairs={{0,1},{1,0},{2,3},{3,2},{4,5},{5,4},{6,7},{7,6},{8,9},{9,8},{10,11... | collective-permute-start | bytes 3145736 | tf_op jit(solution)/shard_map/ppermute | solution.py:456
  136.6 15.6 %collective-permute-start.30 = (f16[528,512]{1,0:T(8,128)(2,1)S(1)}, f16[528,512]{1,0:T(8,128)(2,1)S(1)}, u32[]{:S(2)}, u32[]{:S(2)}) collective-permute-start(f16[528,512]{1,0:T(8,128)(2,1)S(1)} %convert_element_type.26), channel_id=1, source_target_pairs={{0,2},{1,3},{2,0},{3,1},{4,6},{5,7},{6,4},{7,5},{8,10},{9,11},{10,... | collective-permute-start | bytes 1622024 | tf_op jit(solution)/shard_map/ppermute | solution.py:456
  138.1 3.6 %copy-start.3 = (f32[512,512]{1,0:T(8,128)S(1)}, f32[512,512]{1,0:T(8,128)}, u32[]{:S(2)}) copy-start(f32[512,512]{1,0:T(8,128)} %moment) | copy-start | bytes 3145732
  138.1 3.6 %copy-start.4 = (f32[512,512]{1,0:T(8,128)S(1)}, f32[512,512]{1,0:T(8,128)}, u32[]{:S(2)}) copy-start(f32[512,512]{1,0:T(8,128)} %square) | copy-start | bytes 3145732
  141.7 10.5 %copy-start.7 = (f32[128]{0:T(128)S(1)}, f32[128]{0:T(128)}, u32[]{:S(2)}) copy-start(f32[128]{0:T(128)} %param.12) | copy-start | bytes 1540
  141.7 10.5 %copy-start.8 = (f32[128]{0:T(128)S(1)}, f32[128]{0:T(128)}, u32[]{:S(2)}) copy-start(f32[128]{0:T(128)} %param.16) | copy-start | bytes 1540
  141.7 10.5 %copy-start.9 = (f32[128]{0:T(128)S(1)}, f32[128]{0:T(128)}, u32[]{:S(2)}) copy-start(f32[128]{0:T(128)} %param.17) | copy-start | bytes 1540
  141.7 11.6 %copy-start.2 = (f32[512,512]{1,0:T(8,128)S(1)}, f32[512,512]{1,0:T(8,128)}, u32[]{:S(2)}) copy-start(f32[512,512]{1,0:T(8,128)} %refs_0_.3) | copy-start | bytes 3145732
  141.7 11.6 %copy-start.10 = (f32[512,512]{1,0:T(8,128)S(1)}, f32[512,512]{1,0:T(8,128)}, u32[]{:S(2)}) copy-start(f32[512,512]{1,0:T(8,128)} %param.14) | copy-start | bytes 3145732
  141.7 11.6 %copy-start.11 = (f32[512,512]{1,0:T(8,128)S(1)}, f32[512,512]{1,0:T(8,128)}, u32[]{:S(2)}) copy-start(f32[512,512]{1,0:T(8,128)} %param.15) | copy-start | bytes 3145732

commit v18 on v16

--- a/solution.py
+++ b/solution.py
@@ -154,17 +154,18 @@
     return jnp.sum(rows.astype(F32), axis=0, keepdims=True)
 
 
-def encoder_body(place, encoder, bias, out):
+def encoder_body(place, encoder, out):
     depth = encoder.shape[0]
     out[:depth] = encoder[...].astype(BF16)
-    out[depth:] = three_rows(jnp.concatenate([bias[...]] * 4, axis=1))
-
-
-def decoder_body(place, decoder, out):
+    out[depth:] = jnp.zeros((out.shape[0] - depth, out.shape[1]), BF16)
+
+
+def decoder_body(place, decoder, bias, out):
     depth = decoder.shape[0]
     value = decoder[...]
     out[:depth] = value.astype(BF16)
-    out[depth:] = three_rows(jnp.sum(value * value, axis=0, keepdims=True))
+    out[depth : depth + EXTRA] = three_rows(jnp.sum(value * value, axis=0, keepdims=True))
+    out[depth + EXTRA :] = three_rows(jnp.concatenate([bias[...]] * 4, axis=1))
 
 
 def codes_body(
@@ -179,6 +180,10 @@
     enc1,
     enc2,
     enc3,
+    dec0,
+    dec1,
+    dec2,
+    dec3,
     codes,
     mask,
     full,
@@ -203,12 +208,13 @@
 
     total = jnp.zeros(codes.shape, F32)
     piece = codes.shape[1] // 4
+    decs = (dec0, dec1, dec2, dec3)
     for t, enc in enumerate((enc0, enc1, enc2, enc3)):
         b = i ^ t
         total += jnp.dot(
             full[:, columns(b * width, width)], enc[:width, :], preferred_element_type=F32
         )
-        bias[:, columns(b * piece, piece)] = one_row(enc[width:, :piece])
+        bias[:, columns(b * piece, piece)] = one_row(decs[t][width + EXTRA :, :piece])
     preact = total + bias[...]
     low_codes = jnp.maximum(preact, 0.0).astype(BF16)
     codes[...] = low_codes
@@ -335,7 +341,7 @@
     width = 2 * half
     decs = (dec0, dec1, dec2, dec3)
     total = part[...] + back_through(i, far, decs, jnp.where(z >= 2, 0, half))
-    squares = functools.reduce(jnp.add, [one_row(dec[width:, :]) for dec in decs])
+    squares = functools.reduce(jnp.add, [one_row(dec[width : width + EXTRA, :]) for dec in decs])
     column_norms = jnp.sqrt(squares + 1e-06)
     norms[...] = column_norms
     code_grad = (-2.0 / rows) * total + column_norms / rows
@@ -461,17 +467,17 @@
 
     (enc_own,) = local_kernel(
         encoder_body,
-        [shape((width + EXTRA, latents), BF16)],
+        [shape((width + 2 * EXTRA, latents), BF16)],
         place,
         encoder,
-        enc_bias.reshape(1, -1),
     )
     enc_chip, enc_core = flip(enc_own, 2), flip(enc_own, 1)
     (dec_own,) = local_kernel(
         decoder_body,
-        [shape((width + EXTRA, latents), BF16)],
+        [shape((width + 2 * EXTRA, latents), BF16)],
         place,
         decoder,
+        enc_bias.reshape(1, -1),
         after=(enc_core,),
     )
     dec_chip, dec_core = flip(dec_own, 2), flip(dec_own, 1)
@@ -509,7 +515,8 @@
         relay1,
         relay2,
         *enc,
-        after=(rows_own, dec[1], dec[3]),
+        *dec,
+        after=(rows_own,),
         scratch=[pltpu.VMEM((1, latents), F32)],
     )
     codes_near = along(codes, [(0, 1), (3, 2)])

time: 146 us -> 145 us (level)
  transfers between devices with their start and end apart: 33 -> 33, of which waited for: 12 -> 12; matrix products, arithmetic and copies ran while one was open for 0% -> 0% of each run, Pallas kernels for 13% -> 14%
where the time goes in v18:
time: 145 us
  waiting for transfers between devices  69.5 us (48%)
  starting transfers between devices  47.9 us (33%)
  Pallas kernels  21.8 us (15%)
  other arithmetic  2.89 us (2%)
    ppermute x14, waiting for transfers between devices, along(): return lax.ppermute(value, 'latent', pairs)  55.5 us
    ppermute x14, starting transfers between devices, along(): return lax.ppermute(value, 'latent', pairs)  37.9 us
    pallas_call x16, Pallas kernels, local_kernel(): pl.pallas_call(run, out_shape=outs, in_specs=[SMEM] + [VMEM] * len(args)...  18.9 us
    ppermute x19, waiting for transfers between devices, flip(): return lax.ppermute(value, ('latent', 'dp'), pairs)  14 us
    ppermute x19, starting transfers between devices, flip(): return lax.ppermute(value, ('latent', 'dp'), pairs)  9.99 us
    pallas_call x1, Pallas kernels, line_shards(): pl.pallas_call(functools.partial(decoder_step_body, rows), grid=(4,), out...  2.94 us
  transfers between devices with their start and end apart: 33, of which 12 were waited for; matrix products, arithmetic and copies ran while one was open for 0% of the time, Pallas kernels for 14%

profile of v18, /device:TPU:0, one launch (start us, length us, event | category | flops | bytes accessed | tf_op | source)
XLA Modules:
  0.0 144.7 jit_solution(5726526419359081989)
XLA Ops:
  0.7 1.2 copy-done
  3.1 5.8 %collective-permute-start.2 = (bf16[384,512]{1,0:T(8,128)(2,1)S(1)}, bf16[384,512]{1,0:T(8,128)(2,1)S(1)}, u32[]{:S(2)}, u32[]{:S(2)}) collective-permute-start(bf16[384,512]{1,0:T(8,128)(2,1)S(1)} %copy-done.5), channel_id=1, source_target_pairs={{0,8},{12,4},{1,9},{13,5},{2,10},{14,6},{3,11},{15,7},{16,24},{28,... | collective-permute-start | bytes 1179656 | tf_op jit(solution)/shard_map/ppermute | solution.py:457
  8.9 1.3 collective-permute-start.1
  10.2 4.6 %collective-permute-start = (bf16[384,512]{1,0:T(8,128)(2,1)S(1)}, bf16[384,512]{1,0:T(8,128)(2,1)S(1)}, u32[]{:S(2)}, u32[]{:S(2)}) collective-permute-start(bf16[384,512]{1,0:T(8,128)(2,1)S(1)} %copy-done.5), channel_id=1, source_target_pairs={{0,4},{4,8},{8,12},{1,5},{5,9},{9,13},{2,6},{6,10},{10,14},{3,7},{... | collective-permute-start | bytes 1179656 | tf_op jit(solution)/shard_map/ppermute | solution.py:457
  14.8 1.6 %collective-permute-start.6 = (bf16[544,512]{1,0:T(8,128)(2,1)S(1)}, bf16[544,512]{1,0:T(8,128)(2,1)S(1)}, u32[]{:S(2)}, u32[]{:S(2)}) collective-permute-start(bf16[544,512]{1,0:T(8,128)(2,1)S(1)} %shard_map.178.refs_6_), channel_id=1, source_target_pairs={{0,2},{1,3},{2,0},{3,1},{4,6},{5,7},{6,4},{7,5},{8,10},{9,11},{10,... | collective-permute-start | bytes 1671176 | tf_op jit(solution)/shard_map/ppermute | solution.py:461
  16.4 0.6 shard_map.179.refs_0_.refs_10_.refs_4_.refs_3_
  17.0 0.6 collective-permute-start.9
  17.6 0.8 collective-permute-done.2.refs_3_
  18.4 1.3 collective-permute-start.4
  20.3 1.6 %collective-permute-done.1.refs_1_.refs_2_ = bf16[384,512]{1,0:T(8,128)(2,1)S(1)} collective-permute-done((bf16[384,512]{1,0:T(8,128)(2,1)S(1)}, bf16[384,512]{1,0:T(8,128)(2,1)S(1)}, u32[]{:S(2)}, u32[]{:S(2)}) %collective-permute-start.1) | collective-permute-done | bytes 393248 | tf_op jit(solution)/shard_map/ppermute | solution.py:457
  21.9 8.4 %collective-permute-start.11 = (bf16[256,512]{1,0:T(8,128)(2,1)S(1)}, bf16[256,512]{1,0:T(8,128)(2,1)S(1)}, u32[]{:S(2)}, u32[]{:S(2)}) collective-permute-start(bf16[256,512]{1,0:T(8,128)(2,1)S(1)} %get-tuple-element.61), channel_id=1, source_target_pairs={{0,4},{4,8},{1,5},{5,9},{2,6},{6,10},{3,7},{7,11},{16,20},{20,24},... | collective-permute-start | bytes 786440 | tf_op jit(solution)/shard_map/ppermute | solution.py:457
  30.3 0.7 collective-permute-start.12
  31.0 5.2 %collective-permute-start.13 = (bf16[256,512]{1,0:T(8,128)(2,1)S(1)}, bf16[256,512]{1,0:T(8,128)(2,1)S(1)}, u32[]{:S(2)}, u32[]{:S(2)}) collective-permute-start(bf16[256,512]{1,0:T(8,128)(2,1)S(1)} %get-tuple-element.65), channel_id=1, source_target_pairs={{0,8},{12,4},{1,9},{13,5},{2,10},{14,6},{3,11},{15,7},{16,24},{28,... | collective-permute-start | bytes 786440 | tf_op jit(solution)/shard_map/ppermute | solution.py:457
  36.8 1.3 collective-permute-start.3
  38.2 2.5 %collective-permute-done.9.refs_12_.refs_5_.refs_6_ = bf16[544,512]{1,0:T(8,128)(2,1)S(1)} collective-permute-done((bf16[544,512]{1,0:T(8,128)(2,1)S(1)}, bf16[544,512]{1,0:T(8,128)(2,1)S(1)}, u32[]{:S(2)}, u32[]{:S(2)}) %collective-permute-start.9) | collective-permute-done | bytes 557088 | tf_op jit(solution)/shard_map/ppermute | solution.py:461
  41.7 0.7 collective-permute-start.18
  42.4 6.2 %collective-permute-done.3.refs_4_ = bf16[384,512]{1,0:T(8,128)(2,1)S(1)} collective-permute-done((bf16[384,512]{1,0:T(8,128)(2,1)S(1)}, bf16[384,512]{1,0:T(8,128)(2,1)S(1)}, u32[]{:S(2)}, u32[]{:S(2)}) %collective-permute-start.3) | collective-permute-done | bytes 393248 | tf_op jit(solution)/shard_map/ppermute | solution.py:457
  48.6 1.8 %shard_map.181 = (bf16[384,512]{1,0:T(8,128)(2,1)S(1)}, bf16[384,512]{1,0:T(8,128)(2,1)S(1)}, bf16[384,2048]{1,0:T(8,128)(2,1)S(1)}, f32[1,512]{1,0:T(1,128)S(1)}) custom-call(s32[2]{0:T(128)S(1)} %pad_add_fusion.place, bf16[384,512]{1,0:T(8,128)(2,1)S(1)} %copy-done.5, bf16[384,512]{1,0:T(8,128)(2,1)S(1)} %collective-permute-done.refs_0_.refs_1_, ...), custom_call_target="tpu_custom_call" | custom-call | flops 1 | bytes 1 | tf_op jit(solution)/shard_map/pallas_call | solution.py:121
  50.4 1.9 %collective-permute-start.14 = (bf16[384,512]{1,0:T(8,128)(2,1)S(1)}, bf16[384,512]{1,0:T(8,128)(2,1)S(1)}, u32[]{:S(2)}, u32[]{:S(2)}) collective-permute-start(bf16[384,512]{1,0:T(8,128)(2,1)S(1)} %get-tuple-element.68.refs_0_.refs_2_.refs_4_), channel_id=1, source_target_pairs={{0,8},{12,4},{1,9},{13,5},{2,10},{14,6},{3,11},{15,7},{16,24},{28,... | collective-permute-start | bytes 1179656 | tf_op jit(solution)/shard_map/ppermute | solution.py:457
  52.3 0.7 collective-permute-start.16
  53.0 3.5 %collective-permute-start.15 = (bf16[384,512]{1,0:T(8,128)(2,1)S(1)}, bf16[384,512]{1,0:T(8,128)(2,1)S(1)}, u32[]{:S(2)}, u32[]{:S(2)}) collective-permute-start(bf16[384,512]{1,0:T(8,128)(2,1)S(1)} %get-tuple-element.68.refs_0_.refs_2_.refs_4_), channel_id=1, source_target_pairs={{0,4},{12,8},{1,5},{13,9},{2,6},{14,10},{3,7},{15,11},{16,20},{28,... | collective-permute-start | bytes 1179656 | tf_op jit(solution)/shard_map/ppermute | solution.py:457
  56.6 0.7 collective-permute-start.17
  57.3 4.5 %collective-permute-done.14.refs_1_.refs_2_ = bf16[384,512]{1,0:T(8,128)(2,1)S(1)} collective-permute-done((bf16[384,512]{1,0:T(8,128)(2,1)S(1)}, bf16[384,512]{1,0:T(8,128)(2,1)S(1)}, u32[]{:S(2)}, u32[]{:S(2)}) %collective-permute-start.14) | collective-permute-done | bytes 393248 | tf_op jit(solution)/shard_map/ppermute | solution.py:457
  61.8 0.7 collective-permute-start.19
  62.5 7.0 %collective-permute-done.15.refs_1_ = bf16[384,512]{1,0:T(8,128)(2,1)S(1)} collective-permute-done((bf16[384,512]{1,0:T(8,128)(2,1)S(1)}, bf16[384,512]{1,0:T(8,128)(2,1)S(1)}, u32[]{:S(2)}, u32[]{:S(2)}) %collective-permute-start.15) | collective-permute-done | bytes 393248 | tf_op jit(solution)/shard_map/ppermute | solution.py:457
  69.5 1.6 %shard_map.183.refs_9_ = bf16[384,512]{1,0:T(8,128)(2,1)S(1)} custom-call(s32[2]{0:T(128)S(1)} %pad_add_fusion.place, bf16[384,512]{1,0:T(8,128)(2,1)S(1)} %get-tuple-element.68.refs_0_.refs_2_.refs_4_, bf16[384,512]{1,0:T(8,128)(2,1)S(1)} %collective-permute-done.15.refs_1_, bf16[384,512]{1,0:T(8,128)(2,1)S(1)} %collective-permute-done.14.refs_1_.refs_2_, ...), custom_call_target="tpu_custom_call" | custom-call | flops 10000000000 | bytes 1 | tf_op jit(solution)/shard_map/pallas_call | solution.py:121
  71.1 1.6 %shard_map.184.refs_0_ = bf16[384,1024]{1,0:T(8,128)(2,1)S(1)} custom-call(s32[2]{0:T(128)S(1)} %pad_add_fusion.place, bf16[384,512]{1,0:T(8,128)(2,1)S(1)} %get-tuple-element.68.refs_0_.refs_2_.refs_4_, bf16[384,512]{1,0:T(8,128)(2,1)S(1)} %collective-permute-done.15.refs_1_, bf16[384,512]{1,0:T(8,128)(2,1)S(1)} %collective-permute-done.14.refs_1_.refs_2_, ...), custom_call_target="tpu_custom_call" | custom-call | flops 1 | bytes 1 | tf_op jit(solution)/shard_map/pallas_call | solution.py:121
  72.7 1.3 collective-permute-start.22
  74.0 0.7 collective-permute-start.20
  74.7 1.3 collective-permute-start.21
  76.0 20.1 %collective-permute-done.22.refs_1_ = bf16[384,1024]{1,0:T(8,128)(2,1)S(1)} collective-permute-done((bf16[384,1024]{1,0:T(8,128)(2,1)S(1)}, bf16[384,1024]{1,0:T(8,128)(2,1)S(1)}, u32[]{:S(2)}, u32[]{:S(2)}) %collective-permute-start.22) | collective-permute-done | bytes 786464 | tf_op jit(solution)/shard_map/ppermute | solution.py:457
  96.1 1.8 %shard_map.185 = (f32[384,512]{1,0:T(8,128)S(1)}, bf16[384,1024]{1,0:T(8,128)(2,1)S(1)}, f32[264,512]{1,0:T(8,128)S(1)}, f32[256,512]{1,0:T(8,128)S(1)}, f32[256,512]{1,0:T(8,128)S(1)}, /*index=5*/f32[256,512]{1,0:T(8,128)S(1)}) custom-call(s32[2]{0:T(128)S(1)} %pad_add_fusion.place, bf16[384,1024]{1,0:T(8,128)(2,1)S(1)} %shard_map.184.refs_0_, ...), custom_call_target="tpu_custom_call" | custom-call | flops 1 | bytes 1 | tf_op jit(solution)/shard_map/pallas_call | solution.py:121
  98.4 1.0 shard_map.182.refs_7_.refs_0_
  99.8 0.7 shard_map.186
  100.6 0.6 collective-permute-start.25
  101.2 14.9 %collective-permute-done.21.refs_1_ = bf16[384,1024]{1,0:T(8,128)(2,1)S(1)} collective-permute-done((bf16[384,1024]{1,0:T(8,128)(2,1)S(1)}, bf16[384,1024]{1,0:T(8,128)(2,1)S(1)}, u32[]{:S(2)}, u32[]{:S(2)}) %collective-permute-start.21) | collective-permute-done | bytes 786464 | tf_op jit(solution)/shard_map/ppermute | solution.py:457
  116.1 1.3 shard_map.187
  117.4 1.7 %shard_map.188 = (bf16[384,512]{1,0:T(8,128)(2,1)S(1)}, f32[1,512]{1,0:T(1,128)S(1)}, f32[1,512]{1,0:T(1,128)S(1)}, f32[264,512]{1,0:T(8,128)S(1)}, f32[256,512]{1,0:T(8,128)S(1)}) custom-call(s32[2]{0:T(128)S(1)} %pad_add_fusion.place, bf16[384,1024]{1,0:T(8,128)(2,1)S(1)} %get-tuple-element.76.refs_0_.refs_3_, f32[384,512]{1,0:T(8,128)S(1)} %get-tuple-element.78.refs_1_, ...), custom_call_target="tpu_custom_call" | custom-call | flops 10000000000 | bytes 1 | tf_op jit(solution)/shard_map/pallas_call | solution.py:121
  119.8 0.7 shard_map.189.refs_5_
  120.6 0.6 collective-permute-start.32
  121.2 2.5 %shard_map.190 = (bf16[384,512]{1,0:T(8,128)(2,1)}, f32[512,512]{1,0:T(8,128)S(1)}, f32[512,512]{1,0:T(8,128)S(1)}, f32[512,512]{1,0:T(8,128)S(1)}, f32[256,512]{1,0:T(8,128)S(1)}, /*index=5*/f32[256,512]{1,0:T(8,128)S(1)}) custom-call(s32[2]{0:T(128)S(1)} %pad_add_fusion.place, bf16[2048,384]{1,0:T(8,128)(2,1)S(1)} %shard_map.182.refs_7_.refs_0_, ...), custom_call_target="tpu_custom_call" | custom-call | flops 1 | bytes 1 | tf_op jit(solution)/shard_map/pallas_call | solution.py:121
  124.3 0.8 shard_map.191
  125.2 1.5 %collective-permute-start.30 = (f16[528,512]{1,0:T(8,128)(2,1)S(1)}, f16[528,512]{1,0:T(8,128)(2,1)S(1)}, u32[]{:S(2)}, u32[]{:S(2)}) collective-permute-start(f16[528,512]{1,0:T(8,128)(2,1)S(1)} %convert_element_type.26), channel_id=1, source_target_pairs={{0,2},{1,3},{2,0},{3,1},{4,6},{5,7},{6,4},{7,5},{8,10},{9,11},{10,... | collective-permute-start | bytes 1622024 | tf_op jit(solution)/shard_map/ppermute | solution.py:461
  126.9 3.2 %collective-permute-done.32 = f16[272,512]{1,0:T(8,128)(2,1)S(1)} collective-permute-done((f16[272,512]{1,0:T(8,128)(2,1)S(1)}, f16[272,512]{1,0:T(8,128)(2,1)S(1)}, u32[]{:S(2)}, u32[]{:S(2)}) %collective-permute-start.32) | collective-permute-done | bytes 278560 | tf_op jit(solution)/shard_map/ppermute | solution.py:461
  130.3 2.9 %shard_map.193 = (f32[512,512]{1,0:T(8,128)}, f32[512,512]{1,0:T(8,128)}, f32[512,512]{1,0:T(8,128)}) custom-call(s32[2]{0:T(128)S(1)} %pad_add_fusion.place, f32[512,512]{1,0:T(8,128)S(1)} %copy-done.2, f32[512,512]{1,0:T(8,128)S(1)} %copy-done.3, f32[512,512]{1,0:T(8,128)S(1)} %copy-done.4, f32[256,512]{1,0:T(8,128)S(1)} %multiply_add_fusion.3.near, ...), custom_call_target="tpu_custom_call" | custom-call | flops 1 | bytes 1 | tf_op jit(solution)/shard_map/pallas_call | solution.py:662
  133.3 7.9 %collective-permute-done.30 = f16[528,512]{1,0:T(8,128)(2,1)S(1)} collective-permute-done((f16[528,512]{1,0:T(8,128)(2,1)S(1)}, f16[528,512]{1,0:T(8,128)(2,1)S(1)}, u32[]{:S(2)}, u32[]{:S(2)}) %collective-permute-start.30) | collective-permute-done | bytes 540704 | tf_op jit(solution)/shard_map/ppermute | solution.py:461
  141.3 1.1 shard_map.192
  142.4 2.3 %divide_subtract_fusion = (f32[512,512]{1,0:T(8,128)}, f32[512,512]{1,0:T(8,128)}, f32[512,512]{1,0:T(8,128)}) fusion(f32[512,512]{1,0:T(8,128)S(1)} %copy-done.1, f32[512]{0:T(512)S(1)} %bitcast.15, f16[528,512]{1,0:T(8,128)(2,1)S(1)} %collective-permute-done.30, f32[512,512]{1,0:T(8,128)S(1)} %get-tuple-element.92, ...), kind=kLoop, calls=%fused_computation.2 | loop fusion | flops 4194304 | bytes 8914944 | tf_op jit(solution)/shard_map/sub | solution.py:28
  (72 shorter events, 6.3 us)
Async XLA Ops:
  0.6 15.7 %copy-start.6 = (f32[128]{0:T(128)S(1)}, f32[128]{0:T(128)}, u32[]{:S(2)}) copy-start(f32[128]{0:T(128)} %param.12) | copy-start | bytes 1540
  0.7 1.2 copy-start
  2.0 1.1 copy-start.5
  2.0 14.4 %copy-start.2 = (f32[512,512]{1,0:T(8,128)S(1)}, f32[512,512]{1,0:T(8,128)}, u32[]{:S(2)}) copy-start(f32[512,512]{1,0:T(8,128)} %param.20) | copy-start | bytes 3145732
  2.6 13.8 %collective-permute-start.5 = (bf16[544,512]{1,0:T(8,128)(2,1)S(1)}, bf16[544,512]{1,0:T(8,128)(2,1)S(1)}, u32[]{:S(2)}, u32[]{:S(2)}) collective-permute-start(bf16[544,512]{1,0:T(8,128)(2,1)S(1)} %shard_map.178.refs_6_), channel_id=1, source_target_pairs={{0,1},{1,0},{2,3},{3,2},{4,5},{5,4},{6,7},{7,6},{8,9},{9,8},{10,11... | collective-permute-start | bytes 1671176 | tf_op jit(solution)/shard_map/ppermute | solution.py:461
  3.1 15.3 %collective-permute-start.2 = (bf16[384,512]{1,0:T(8,128)(2,1)S(1)}, bf16[384,512]{1,0:T(8,128)(2,1)S(1)}, u32[]{:S(2)}, u32[]{:S(2)}) collective-permute-start(bf16[384,512]{1,0:T(8,128)(2,1)S(1)} %copy-done.5), channel_id=1, source_target_pairs={{0,8},{12,4},{1,9},{13,5},{2,10},{14,6},{3,11},{15,7},{16,24},{28,... | collective-permute-start | bytes 1179656 | tf_op jit(solution)/shard_map/ppermute | solution.py:457
  8.9 13.0 %collective-permute-start.1 = (bf16[384,512]{1,0:T(8,128)(2,1)S(1)}, bf16[384,512]{1,0:T(8,128)(2,1)S(1)}, u32[]{:S(2)}, u32[]{:S(2)}) collective-permute-start(bf16[384,512]{1,0:T(8,128)(2,1)S(1)} %copy-done.5), channel_id=1, source_target_pairs={{4,0},{8,4},{12,8},{5,1},{9,5},{13,9},{6,2},{10,6},{14,10},{7,3},{... | collective-permute-start | bytes 1179656 | tf_op jit(solution)/shard_map/ppermute | solution.py:457
  10.2 20.1 %collective-permute-start = (bf16[384,512]{1,0:T(8,128)(2,1)S(1)}, bf16[384,512]{1,0:T(8,128)(2,1)S(1)}, u32[]{:S(2)}, u32[]{:S(2)}) collective-permute-start(bf16[384,512]{1,0:T(8,128)(2,1)S(1)} %copy-done.5), channel_id=1, source_target_pairs={{0,4},{4,8},{8,12},{1,5},{5,9},{9,13},{2,6},{6,10},{10,14},{3,7},{... | collective-permute-start | bytes 1179656 | tf_op jit(solution)/shard_map/ppermute | solution.py:457
  14.8 16.2 %collective-permute-start.6 = (bf16[544,512]{1,0:T(8,128)(2,1)S(1)}, bf16[544,512]{1,0:T(8,128)(2,1)S(1)}, u32[]{:S(2)}, u32[]{:S(2)}) collective-permute-start(bf16[544,512]{1,0:T(8,128)(2,1)S(1)} %shard_map.178.refs_6_), channel_id=1, source_target_pairs={{0,2},{1,3},{2,0},{3,1},{4,6},{5,7},{6,4},{7,5},{8,10},{9,11},{10,... | collective-permute-start | bytes 1671176 | tf_op jit(solution)/shard_map/ppermute | solution.py:461
  17.0 23.7 %collective-permute-start.9 = (bf16[544,512]{1,0:T(8,128)(2,1)S(1)}, bf16[544,512]{1,0:T(8,128)(2,1)S(1)}, u32[]{:S(2)}, u32[]{:S(2)}) collective-permute-start(bf16[544,512]{1,0:T(8,128)(2,1)S(1)} %shard_map.179.refs_0_.refs_10_.refs_4_.refs_3_), channel_id=1, source_target_pairs={{0,2},{1,3},{2,0},{3,1},{4,6},{5,7},{6,4},{7,5},{8,10},{9,11},{10,... | collective-permute-start | bytes 1671176 | tf_op jit(solution)/shard_map/ppermute | solution.py:461
  18.4 18.4 %collective-permute-start.4 = (bf16[384,512]{1,0:T(8,128)(2,1)S(1)}, bf16[384,512]{1,0:T(8,128)(2,1)S(1)}, u32[]{:S(2)}, u32[]{:S(2)}) collective-permute-start(bf16[384,512]{1,0:T(8,128)(2,1)S(1)} %collective-permute-done.2.refs_3_), channel_id=1, source_target_pairs={{4,0},{8,12},{5,1},{9,13},{6,2},{10,14},{7,3},{11,15},{20,16},{24,... | collective-permute-start | bytes 1179656 | tf_op jit(solution)/shard_map/ppermute | solution.py:457
  21.9 16.2 %collective-permute-start.11 = (bf16[256,512]{1,0:T(8,128)(2,1)S(1)}, bf16[256,512]{1,0:T(8,128)(2,1)S(1)}, u32[]{:S(2)}, u32[]{:S(2)}) collective-permute-start(bf16[256,512]{1,0:T(8,128)(2,1)S(1)} %get-tuple-element.61), channel_id=1, source_target_pairs={{0,4},{4,8},{1,5},{5,9},{2,6},{6,10},{3,7},{7,11},{16,20},{20,24},... | collective-permute-start | bytes 786440 | tf_op jit(solution)/shard_map/ppermute | solution.py:457
  30.3 10.4 %collective-permute-start.12 = (bf16[256,512]{1,0:T(8,128)(2,1)S(1)}, bf16[256,512]{1,0:T(8,128)(2,1)S(1)}, u32[]{:S(2)}, u32[]{:S(2)}) collective-permute-start(bf16[256,512]{1,0:T(8,128)(2,1)S(1)} %get-tuple-element.63), channel_id=1, source_target_pairs={{8,4},{12,8},{9,5},{13,9},{10,6},{14,10},{11,7},{15,11},{24,20},{2... | collective-permute-start | bytes 786440 | tf_op jit(solution)/shard_map/ppermute | solution.py:457
  31.0 10.6 %collective-permute-start.13 = (bf16[256,512]{1,0:T(8,128)(2,1)S(1)}, bf16[256,512]{1,0:T(8,128)(2,1)S(1)}, u32[]{:S(2)}, u32[]{:S(2)}) collective-permute-start(bf16[256,512]{1,0:T(8,128)(2,1)S(1)} %get-tuple-element.65), channel_id=1, source_target_pairs={{0,8},{12,4},{1,9},{13,5},{2,10},{14,6},{3,11},{15,7},{16,24},{28,... | collective-permute-start | bytes 786440 | tf_op jit(solution)/shard_map/ppermute | solution.py:457
  36.8 11.8 %collective-permute-start.3 = (bf16[384,512]{1,0:T(8,128)(2,1)S(1)}, bf16[384,512]{1,0:T(8,128)(2,1)S(1)}, u32[]{:S(2)}, u32[]{:S(2)}) collective-permute-start(bf16[384,512]{1,0:T(8,128)(2,1)S(1)} %shard_map.177), channel_id=1, source_target_pairs={{4,0},{8,12},{5,1},{9,13},{6,2},{10,14},{7,3},{11,15},{20,16},{24,... | collective-permute-start | bytes 1179656 | tf_op jit(solution)/shard_map/ppermute | solution.py:457
  38.1 10.5 %collective-permute-start.8 = (bf16[544,512]{1,0:T(8,128)(2,1)S(1)}, bf16[544,512]{1,0:T(8,128)(2,1)S(1)}, u32[]{:S(2)}, u32[]{:S(2)}) collective-permute-start(bf16[544,512]{1,0:T(8,128)(2,1)S(1)} %shard_map.179.refs_0_.refs_10_.refs_4_.refs_3_), channel_id=1, source_target_pairs={{0,1},{1,0},{2,3},{3,2},{4,5},{5,4},{6,7},{7,6},{8,9},{9,8},{10,11... | collective-permute-start | bytes 1671176 | tf_op jit(solution)/shard_map/ppermute | solution.py:461
  40.7 8.0 %collective-permute-start.7 = (bf16[544,512]{1,0:T(8,128)(2,1)S(1)}, bf16[544,512]{1,0:T(8,128)(2,1)S(1)}, u32[]{:S(2)}, u32[]{:S(2)}) collective-permute-start(bf16[544,512]{1,0:T(8,128)(2,1)S(1)} %collective-permute-done.6.refs_8_), channel_id=1, source_target_pairs={{0,1},{1,0},{2,3},{3,2},{4,5},{5,4},{6,7},{7,6},{8,9},{9,8},{10,11... | collective-permute-start | bytes 1671176 | tf_op jit(solution)/shard_map/ppermute | solution.py:461
  40.7 8.0 %collective-permute-start.10 = (bf16[544,512]{1,0:T(8,128)(2,1)S(1)}, bf16[544,512]{1,0:T(8,128)(2,1)S(1)}, u32[]{:S(2)}, u32[]{:S(2)}) collective-permute-start(bf16[544,512]{1,0:T(8,128)(2,1)S(1)} %collective-permute-done.9.refs_12_.refs_5_.refs_6_), channel_id=1, source_target_pairs={{0,1},{1,0},{2,3},{3,2},{4,5},{5,4},{6,7},{7,6},{8,9},{9,8},{10,11... | collective-permute-start | bytes 1671176 | tf_op jit(solution)/shard_map/ppermute | solution.py:461
  41.7 15.6 %collective-permute-start.18 = (bf16[768,512]{1,0:T(8,128)(2,1)S(1)}, bf16[768,512]{1,0:T(8,128)(2,1)S(1)}, u32[]{:S(2)}, u32[]{:S(2)}) collective-permute-start(bf16[768,512]{1,0:T(8,128)(2,1)S(1)} %constant_dynamic-update-slice_fusion.refs_14_.refs_6_), channel_id=1, source_target_pairs={{4,6},{5,7},{6,4},{7,5},{8,10},{9,11},{10,8},{11,9},{20,22},{21,23... | collective-permute-start | bytes 2359304 | tf_op jit(solution)/shard_map/ppermute | solution.py:461
  50.4 11.4 %collective-permute-start.14 = (bf16[384,512]{1,0:T(8,128)(2,1)S(1)}, bf16[384,512]{1,0:T(8,128)(2,1)S(1)}, u32[]{:S(2)}, u32[]{:S(2)}) collective-permute-start(bf16[384,512]{1,0:T(8,128)(2,1)S(1)} %get-tuple-element.68.refs_0_.refs_2_.refs_4_), channel_id=1, source_target_pairs={{0,8},{12,4},{1,9},{13,5},{2,10},{14,6},{3,11},{15,7},{16,24},{28,... | collective-permute-start | bytes 1179656 | tf_op jit(solution)/shard_map/ppermute | solution.py:457
  52.3 10.2 %collective-permute-start.16 = (bf16[384,512]{1,0:T(8,128)(2,1)S(1)}, bf16[384,512]{1,0:T(8,128)(2,1)S(1)}, u32[]{:S(2)}, u32[]{:S(2)}) collective-permute-start(bf16[384,512]{1,0:T(8,128)(2,1)S(1)} %get-tuple-element.68.refs_0_.refs_2_.refs_4_), channel_id=1, source_target_pairs={{4,8},{8,4},{5,9},{9,5},{6,10},{10,6},{7,11},{11,7},{20,24},{24,20... | collective-permute-start | bytes 1179656 | tf_op jit(solution)/shard_map/ppermute | solution.py:457
  53.0 16.5 %collective-permute-start.15 = (bf16[384,512]{1,0:T(8,128)(2,1)S(1)}, bf16[384,512]{1,0:T(8,128)(2,1)S(1)}, u32[]{:S(2)}, u32[]{:S(2)}) collective-permute-start(bf16[384,512]{1,0:T(8,128)(2,1)S(1)} %get-tuple-element.68.refs_0_.refs_2_.refs_4_), channel_id=1, source_target_pairs={{0,4},{12,8},{1,5},{13,9},{2,6},{14,10},{3,7},{15,11},{16,20},{28,... | collective-permute-start | bytes 1179656 | tf_op jit(solution)/shard_map/ppermute | solution.py:457
  56.6 14.5 %collective-permute-start.17 = (bf16[768,512]{1,0:T(8,128)(2,1)S(1)}, bf16[768,512]{1,0:T(8,128)(2,1)S(1)}, u32[]{:S(2)}, u32[]{:S(2)}) collective-permute-start(bf16[768,512]{1,0:T(8,128)(2,1)S(1)} %constant_dynamic-update-slice_fusion.refs_14_.refs_6_), channel_id=1, source_target_pairs={{4,5},{5,4},{6,7},{7,6},{8,9},{9,8},{10,11},{11,10},{20,21},{21,20... | collective-permute-start | bytes 2359304 | tf_op jit(solution)/shard_map/ppermute | solution.py:461
  61.8 9.3 %collective-permute-start.19 = (bf16[768,512]{1,0:T(8,128)(2,1)S(1)}, bf16[768,512]{1,0:T(8,128)(2,1)S(1)}, u32[]{:S(2)}, u32[]{:S(2)}) collective-permute-start(bf16[768,512]{1,0:T(8,128)(2,1)S(1)} %collective-permute-done.18.refs_7_), channel_id=1, source_target_pairs={{4,5},{5,4},{6,7},{7,6},{8,9},{9,8},{10,11},{11,10},{20,21},{21,20... | collective-permute-start | bytes 2359304 | tf_op jit(solution)/shard_map/ppermute | solution.py:461
  72.7 23.4 %collective-permute-start.22 = (bf16[384,1024]{1,0:T(8,128)(2,1)S(1)}, bf16[384,1024]{1,0:T(8,128)(2,1)S(1)}, u32[]{:S(2)}, u32[]{:S(2)}) collective-permute-start(bf16[384,1024]{1,0:T(8,128)(2,1)S(1)} %shard_map.184.refs_0_), channel_id=1, source_target_pairs={{4,0},{8,12},{5,1},{9,13},{6,2},{10,14},{7,3},{11,15},{20,16},{24,... | collective-permute-start | bytes 2359304 | tf_op jit(solution)/shard_map/ppermute | solution.py:457
  74.0 22.1 %collective-permute-start.20 = (bf16[384,1024]{1,0:T(8,128)(2,1)S(1)}, bf16[384,1024]{1,0:T(8,128)(2,1)S(1)}, u32[]{:S(2)}, u32[]{:S(2)}) collective-permute-start(bf16[384,1024]{1,0:T(8,128)(2,1)S(1)} %shard_map.184.refs_0_), channel_id=1, source_target_pairs={{4,8},{8,4},{5,9},{9,5},{6,10},{10,6},{7,11},{11,7},{20,24},{24,20... | collective-permute-start | bytes 2359304 | tf_op jit(solution)/shard_map/ppermute | solution.py:457
  74.7 41.4 %collective-permute-start.21 = (bf16[384,1024]{1,0:T(8,128)(2,1)S(1)}, bf16[384,1024]{1,0:T(8,128)(2,1)S(1)}, u32[]{:S(2)}, u32[]{:S(2)}) collective-permute-start(bf16[384,1024]{1,0:T(8,128)(2,1)S(1)} %shard_map.184.refs_0_), channel_id=1, source_target_pairs={{8,0},{4,12},{9,1},{5,13},{10,2},{6,14},{11,3},{7,15},{24,16},{20,... | collective-permute-start | bytes 2359304 | tf_op jit(solution)/shard_map/ppermute | solution.py:457
  97.8 2.0 %collective-permute-start.23 = (f32[264,512]{1,0:T(8,128)S(1)}, f32[264,512]{1,0:T(8,128)S(1)}, u32[]{:S(2)}, u32[]{:S(2)}) collective-permute-start(f32[264,512]{1,0:T(8,128)S(1)} %get-tuple-element.73), channel_id=1, source_target_pairs={{0,1},{1,0},{2,3},{3,2},{4,5},{5,4},{6,7},{7,6},{8,9},{9,8},{10,11... | collective-permute-start | bytes 1622024 | tf_op jit(solution)/shard_map/ppermute | solution.py:461
  97.9 18.2 %collective-permute-start.24 = (f32[256,512]{1,0:T(8,128)S(1)}, f32[256,512]{1,0:T(8,128)S(1)}, u32[]{:S(2)}, u32[]{:S(2)}) collective-permute-start(f32[256,512]{1,0:T(8,128)S(1)} %get-tuple-element.75), channel_id=1, source_target_pairs={{0,1},{1,0},{2,3},{3,2},{4,5},{5,4},{6,7},{7,6},{8,9},{9,8},{10,11... | collective-permute-start | bytes 1572872 | tf_op jit(solution)/shard_map/ppermute | solution.py:461
  100.6 16.8 %collective-permute-start.25 = (f16[272,512]{1,0:T(8,128)(2,1)S(1)}, f16[272,512]{1,0:T(8,128)(2,1)S(1)}, u32[]{:S(2)}, u32[]{:S(2)}) collective-permute-start(f16[272,512]{1,0:T(8,128)(2,1)S(1)} %convert_element_type.25), channel_id=1, source_target_pairs={{0,2},{1,3},{2,0},{3,1},{4,6},{5,7},{6,4},{7,5},{8,10},{9,11},{10,... | collective-permute-start | bytes 835592 | tf_op jit(solution)/shard_map/ppermute | solution.py:461
  117.3 2.5 %collective-permute-start.26 = (f32[256,512]{1,0:T(8,128)S(1)}, f32[256,512]{1,0:T(8,128)S(1)}, u32[]{:S(2)}, u32[]{:S(2)}) collective-permute-start(f32[256,512]{1,0:T(8,128)S(1)} %get-tuple-element.83), channel_id=1, source_target_pairs={{0,1},{1,0},{2,3},{3,2},{4,5},{5,4},{6,7},{7,6},{8,9},{9,8},{10,11... | collective-permute-start | bytes 1572872 | tf_op jit(solution)/shard_map/ppermute | solution.py:461
  119.2 5.1 %collective-permute-start.27 = (f32[264,512]{1,0:T(8,128)S(1)}, f32[264,512]{1,0:T(8,128)S(1)}, u32[]{:S(2)}, u32[]{:S(2)}) collective-permute-start(f32[264,512]{1,0:T(8,128)S(1)} %get-tuple-element.87), channel_id=1, source_target_pairs={{0,1},{1,0},{2,3},{3,2},{4,5},{5,4},{6,7},{7,6},{8,9},{9,8},{10,11... | collective-permute-start | bytes 1622024 | tf_op jit(solution)/shard_map/ppermute | solution.py:461
  119.7 4.5 %collective-permute-start.28 = (f32[256,512]{1,0:T(8,128)S(1)}, f32[256,512]{1,0:T(8,128)S(1)}, u32[]{:S(2)}, u32[]{:S(2)}) collective-permute-start(f32[256,512]{1,0:T(8,128)S(1)} %get-tuple-element.88), channel_id=1, source_target_pairs={{0,1},{1,0},{2,3},{3,2},{4,5},{5,4},{6,7},{7,6},{8,9},{9,8},{10,11... | collective-permute-start | bytes 1572872 | tf_op jit(solution)/shard_map/ppermute | solution.py:461
  120.6 9.5 %collective-permute-start.32 = (f16[272,512]{1,0:T(8,128)(2,1)S(1)}, f16[272,512]{1,0:T(8,128)(2,1)S(1)}, u32[]{:S(2)}, u32[]{:S(2)}) collective-permute-start(f16[272,512]{1,0:T(8,128)(2,1)S(1)} %convert_element_type.31), channel_id=1, source_target_pairs={{0,2},{1,3},{2,0},{3,1},{4,6},{5,7},{6,4},{7,5},{8,10},{9,11},{10,... | collective-permute-start | bytes 835592 | tf_op jit(solution)/shard_map/ppermute | solution.py:461
  123.7 6.4 %collective-permute-start.31 = (f32[256,512]{1,0:T(8,128)S(1)}, f32[256,512]{1,0:T(8,128)S(1)}, u32[]{:S(2)}, u32[]{:S(2)}) collective-permute-start(f32[256,512]{1,0:T(8,128)S(1)} %get-tuple-element.102), channel_id=1, source_target_pairs={{0,1},{1,0},{2,3},{3,2},{4,5},{5,4},{6,7},{7,6},{8,9},{9,8},{10,11... | collective-permute-start | bytes 1572872 | tf_op jit(solution)/shard_map/ppermute | solution.py:461
  123.9 18.5 %collective-permute-start.29 = (f32[512,512]{1,0:T(8,128)S(1)}, f32[512,512]{1,0:T(8,128)S(1)}, u32[]{:S(2)}, u32[]{:S(2)}) collective-permute-start(f32[512,512]{1,0:T(8,128)S(1)} %get-tuple-element.93), channel_id=1, source_target_pairs={{0,1},{1,0},{2,3},{3,2},{4,5},{5,4},{6,7},{7,6},{8,9},{9,8},{10,11... | collective-permute-start | bytes 3145736 | tf_op jit(solution)/shard_map/ppermute | solution.py:461
  125.2 16.0 %collective-permute-start.30 = (f16[528,512]{1,0:T(8,128)(2,1)S(1)}, f16[528,512]{1,0:T(8,128)(2,1)S(1)}, u32[]{:S(2)}, u32[]{:S(2)}) collective-permute-start(f16[528,512]{1,0:T(8,128)(2,1)S(1)} %convert_element_type.26), channel_id=1, source_target_pairs={{0,2},{1,3},{2,0},{3,1},{4,6},{5,7},{6,4},{7,5},{8,10},{9,11},{10,... | collective-permute-start | bytes 1622024 | tf_op jit(solution)/shard_map/ppermute | solution.py:461
  126.8 3.5 %copy-start.3 = (f32[512,512]{1,0:T(8,128)S(1)}, f32[512,512]{1,0:T(8,128)}, u32[]{:S(2)}) copy-start(f32[512,512]{1,0:T(8,128)} %moment) | copy-start | bytes 3145732
  126.8 3.5 %copy-start.4 = (f32[512,512]{1,0:T(8,128)S(1)}, f32[512,512]{1,0:T(8,128)}, u32[]{:S(2)}) copy-start(f32[512,512]{1,0:T(8,128)} %square) | copy-start | bytes 3145732
  130.3 11.0 %copy-start.7 = (f32[128]{0:T(128)S(1)}, f32[128]{0:T(128)}, u32[]{:S(2)}) copy-start(f32[128]{0:T(128)} %param.16) | copy-start | bytes 1540
  130.3 11.0 %copy-start.8 = (f32[128]{0:T(128)S(1)}, f32[128]{0:T(128)}, u32[]{:S(2)}) copy-start(f32[128]{0:T(128)} %param.17) | copy-start | bytes 1540
  130.3 12.1 %copy-start.1 = (f32[512,512]{1,0:T(8,128)S(1)}, f32[512,512]{1,0:T(8,128)}, u32[]{:S(2)}) copy-start(f32[512,512]{1,0:T(8,128)} %refs_0_.3) | copy-start | bytes 3145732
  130.3 12.1 %copy-start.9 = (f32[512,512]{1,0:T(8,128)S(1)}, f32[512,512]{1,0:T(8,128)}, u32[]{:S(2)}) copy-start(f32[512,512]{1,0:T(8,128)} %param.14) | copy-start | bytes 3145732
  130.3 12.0 %copy-start.10 = (f32[512,512]{1,0:T(8,128)S(1)}, f32[512,512]{1,0:T(8,128)}, u32[]{:S(2)}) copy-start(f32[512,512]{1,0:T(8,128)} %param.15) | copy-start | bytes 3145732

commit v19 on v18

--- a/solution.py
+++ b/solution.py
@@ -347,12 +347,10 @@
     code_grad = (-2.0 / rows) * total + column_norms / rows
     grad = jnp.where(mask[...] > 0, code_grad, 0.0)
     grad_low[...] = grad.astype(BF16)
-    row = jnp.sum(grad, axis=0, keepdims=True)
-    bias_sum[...] = row
+    bias_sum[...] = jnp.sum(grad, axis=0, keepdims=True)
     at = pl.multiple_of((i ^ 3) * width, width)
     block = jnp.dot(turned[pl.ds(at, width), :], grad_low[...], preferred_element_type=F32)
-    sends[0][:half] = block[:half]
-    sends[0][half:] = jnp.broadcast_to(row, (sends[0].shape[0] - half, row.shape[1]))
+    sends[0][...] = block[:half]
     sends[1][...] = block[half:]
 
 
@@ -600,7 +598,7 @@
             shape((count, latents), BF16),
             shape((1, latents), F32),
             shape((1, latents), F32),
-            shape((half + 8, latents), F32),
+            shape((half, latents), F32),
             shape((half, latents), F32),
         ],
         place,
@@ -611,7 +609,7 @@
         turned,
         cost=NOTABLE,
     )
-    far_packed, far_received = across_chips(far_keep, active, far_send, keep_row=False)
+    far_packed, far_received = across_chips(far_keep, bias_sum, far_send, keep_row=False)
     error, enc_send_near, enc_keep_far, enc_keep_near, send_near, keep_near = local_kernel(
         functools.partial(rest_body, rows),
         [shape((count, width), BF16)]
@@ -626,32 +624,19 @@
         after=(far_packed,),
     )
     far_kept = keep_near, flip(send_near, 1)
-    enc_packed, enc_received, bias_here = across_chips(enc_keep_far, bias_sum, *send_far_enc)
+    enc_packed, enc_received = across_chips(enc_keep_far, bias_sum, *send_far_enc, keep_row=False)
     enc_kept = enc_keep_near, flip(enc_send_near, 1)
 
     decoder, dec_moment, dec_square, encoder, enc_moment, enc_square = lax.optimization_barrier(
         (decoder, dec_moment, dec_square, encoder, enc_moment, enc_square, enc_packed)
     )[:6]
     near_block, active_there = unpack(near_received)
-    far_block, _ = unpack(far_received)
-    enc_block, bias_there = unpack(enc_received)
+    far_block, bias_there = unpack(far_received)
+    enc_block, _ = unpack(enc_received)
     near_grad = near_kept[0] + near_kept[1] + near_block
     far_grad = far_kept[0] + far_kept[1] + far_block
     active_sum = active_sum + active_there
     grad_encoder = enc_kept[0] + enc_kept[1] + enc_block
-    new_enc_bias, new_bias_moment, new_bias_square = [
-        value.reshape(-1)
-        for value in local_kernel(
-            bias_step_body,
-            [shape((1, enc_bias.shape[0]), F32)] * 3,
-            place,
-            enc_bias.reshape(1, -1),
-            bias_moment.reshape(1, -1),
-            bias_square.reshape(1, -1),
-            bias_here,
-            bias_there,
-        )
-    ]
     new_encoder, new_enc_moment, new_enc_square = adam_update(
         encoder, grad_encoder, enc_moment, enc_square
     )
@@ -668,6 +653,21 @@
         compiler_params=pltpu.CompilerParams(vmem_limit_bytes=12 * 1024 * 1024),
         cost_estimate=pl.CostEstimate(flops=1, bytes_accessed=1, transcendentals=0),
     )(place, decoder, dec_moment, dec_square, near_grad, far_grad, active_sum, norms)
+    bias_chips = bias_sum + bias_there
+    new_enc_bias, new_bias_moment, new_bias_square = [
+        value.reshape(-1)
+        for value in local_kernel(
+            bias_step_body,
+            [shape((1, enc_bias.shape[0]), F32)] * 3,
+            place,
+            enc_bias.reshape(1, -1),
+            bias_moment.reshape(1, -1),
+            bias_square.reshape(1, -1),
+            bias_chips,
+            flip(bias_chips, 1),
+            after=(new_decoder,),
+        )
+    ]
     return (
         error,
         new_encoder,

time: 145 us -> 144 us (level)
  waiting for transfers between devices: 69.5 us -> 67.1 us
    ppermute x19 -> x20, waiting for transfers between devices: 14 us -> 11.6 us  [flip(): return lax.ppermute(value, ('latent', 'dp'), pairs)]
    ppermute x19 -> x20, starting transfers between devices: 9.99 us -> 9.98 us  [flip(): return lax.ppermute(value, ('latent', 'dp'), pairs)]
  transfers between devices with their start and end apart: 33 -> 34, of which waited for: 12 -> 12; matrix products, arithmetic and copies ran while one was open for 0% -> 0% of each run, Pallas kernels for 14% -> 14%
where the time goes in v19:
time: 144 us
  waiting for transfers between devices  67.1 us (47%)
  starting transfers between devices  47.9 us (33%)
  Pallas kernels  21.8 us (15%)
  other arithmetic  2.9 us (2%)
  local copies, waits for them, and re-layouts  2.64 us (2%)
    ppermute x14, waiting for transfers between devices, along(): return lax.ppermute(value, 'latent', pairs)  55.5 us
    ppermute x14, starting transfers between devices, along(): return lax.ppermute(value, 'latent', pairs)  38 us
    pallas_call x16, Pallas kernels, local_kernel(): pl.pallas_call(run, out_shape=outs, in_specs=[SMEM] + [VMEM] * len(args)...  18.9 us
    ppermute x20, waiting for transfers between devices, flip(): return lax.ppermute(value, ('latent', 'dp'), pairs)  11.6 us
    ppermute x20, starting transfers between devices, flip(): return lax.ppermute(value, ('latent', 'dp'), pairs)  9.98 us
    pallas_call x1, Pallas kernels, line_shards(): pl.pallas_call(functools.partial(decoder_step_body, rows), grid=(4,), out...  2.94 us
  transfers between devices with their start and end apart: 34, of which 12 were waited for; matrix products, arithmetic and copies ran while one was open for 0% of the time, Pallas kernels for 14%

profile of v19, /device:TPU:0, one launch (start us, length us, event | category | flops | bytes accessed | tf_op | source)
XLA Modules:
  0.0 143.6 jit_solution(15671026334884466950)
XLA Ops:
  0.7 1.2 copy-done
  3.1 5.8 %collective-permute-start.2 = (bf16[384,512]{1,0:T(8,128)(2,1)S(1)}, bf16[384,512]{1,0:T(8,128)(2,1)S(1)}, u32[]{:S(2)}, u32[]{:S(2)}) collective-permute-start(bf16[384,512]{1,0:T(8,128)(2,1)S(1)} %copy-done.6), channel_id=1, source_target_pairs={{0,8},{12,4},{1,9},{13,5},{2,10},{14,6},{3,11},{15,7},{16,24},{28,... | collective-permute-start | bytes 1179656 | tf_op jit(solution)/shard_map/ppermute | solution.py:455
  8.9 1.3 collective-permute-start.1
  10.2 4.6 %collective-permute-start = (bf16[384,512]{1,0:T(8,128)(2,1)S(1)}, bf16[384,512]{1,0:T(8,128)(2,1)S(1)}, u32[]{:S(2)}, u32[]{:S(2)}) collective-permute-start(bf16[384,512]{1,0:T(8,128)(2,1)S(1)} %copy-done.6), channel_id=1, source_target_pairs={{0,4},{4,8},{8,12},{1,5},{5,9},{9,13},{2,6},{6,10},{10,14},{3,7},{... | collective-permute-start | bytes 1179656 | tf_op jit(solution)/shard_map/ppermute | solution.py:455
  14.8 1.6 %collective-permute-start.6 = (bf16[544,512]{1,0:T(8,128)(2,1)S(1)}, bf16[544,512]{1,0:T(8,128)(2,1)S(1)}, u32[]{:S(2)}, u32[]{:S(2)}) collective-permute-start(bf16[544,512]{1,0:T(8,128)(2,1)S(1)} %shard_map.178.refs_6_), channel_id=1, source_target_pairs={{0,2},{1,3},{2,0},{3,1},{4,6},{5,7},{6,4},{7,5},{8,10},{9,11},{10,... | collective-permute-start | bytes 1671176 | tf_op jit(solution)/shard_map/ppermute | solution.py:459
  16.4 0.6 shard_map.179.refs_0_.refs_10_.refs_4_.refs_3_
  17.6 0.8 collective-permute-done.2.refs_3_
  18.4 1.3 collective-permute-start.4
  20.3 1.6 %collective-permute-done.1.refs_1_.refs_2_ = bf16[384,512]{1,0:T(8,128)(2,1)S(1)} collective-permute-done((bf16[384,512]{1,0:T(8,128)(2,1)S(1)}, bf16[384,512]{1,0:T(8,128)(2,1)S(1)}, u32[]{:S(2)}, u32[]{:S(2)}) %collective-permute-start.1) | collective-permute-done | bytes 393248 | tf_op jit(solution)/shard_map/ppermute | solution.py:455
  21.9 8.4 %collective-permute-start.11 = (bf16[256,512]{1,0:T(8,128)(2,1)S(1)}, bf16[256,512]{1,0:T(8,128)(2,1)S(1)}, u32[]{:S(2)}, u32[]{:S(2)}) collective-permute-start(bf16[256,512]{1,0:T(8,128)(2,1)S(1)} %get-tuple-element.59), channel_id=1, source_target_pairs={{0,4},{4,8},{1,5},{5,9},{2,6},{6,10},{3,7},{7,11},{16,20},{20,24},... | collective-permute-start | bytes 786440 | tf_op jit(solution)/shard_map/ppermute | solution.py:455
  30.3 0.7 collective-permute-start.12
  31.0 5.2 %collective-permute-start.13 = (bf16[256,512]{1,0:T(8,128)(2,1)S(1)}, bf16[256,512]{1,0:T(8,128)(2,1)S(1)}, u32[]{:S(2)}, u32[]{:S(2)}) collective-permute-start(bf16[256,512]{1,0:T(8,128)(2,1)S(1)} %get-tuple-element.63), channel_id=1, source_target_pairs={{0,8},{12,4},{1,9},{13,5},{2,10},{14,6},{3,11},{15,7},{16,24},{28,... | collective-permute-start | bytes 786440 | tf_op jit(solution)/shard_map/ppermute | solution.py:455
  36.8 1.3 collective-permute-start.3
  38.2 2.5 %collective-permute-done.9.refs_12_.refs_5_.refs_6_ = bf16[544,512]{1,0:T(8,128)(2,1)S(1)} collective-permute-done((bf16[544,512]{1,0:T(8,128)(2,1)S(1)}, bf16[544,512]{1,0:T(8,128)(2,1)S(1)}, u32[]{:S(2)}, u32[]{:S(2)}) %collective-permute-start.9) | collective-permute-done | bytes 557088 | tf_op jit(solution)/shard_map/ppermute | solution.py:459
  41.7 0.7 collective-permute-start.18
  42.4 6.2 %collective-permute-done.3.refs_4_ = bf16[384,512]{1,0:T(8,128)(2,1)S(1)} collective-permute-done((bf16[384,512]{1,0:T(8,128)(2,1)S(1)}, bf16[384,512]{1,0:T(8,128)(2,1)S(1)}, u32[]{:S(2)}, u32[]{:S(2)}) %collective-permute-start.3) | collective-permute-done | bytes 393248 | tf_op jit(solution)/shard_map/ppermute | solution.py:455
  48.6 1.8 %shard_map.181 = (bf16[384,512]{1,0:T(8,128)(2,1)S(1)}, bf16[384,512]{1,0:T(8,128)(2,1)S(1)}, bf16[384,2048]{1,0:T(8,128)(2,1)S(1)}, f32[1,512]{1,0:T(1,128)S(1)}) custom-call(s32[2]{0:T(128)S(1)} %pad_add_fusion.place, bf16[384,512]{1,0:T(8,128)(2,1)S(1)} %copy-done.6, bf16[384,512]{1,0:T(8,128)(2,1)S(1)} %collective-permute-done.refs_0_.refs_1_, ...), custom_call_target="tpu_custom_call" | custom-call | flops 1 | bytes 1 | tf_op jit(solution)/shard_map/pallas_call | solution.py:121
  50.4 1.9 %collective-permute-start.14 = (bf16[384,512]{1,0:T(8,128)(2,1)S(1)}, bf16[384,512]{1,0:T(8,128)(2,1)S(1)}, u32[]{:S(2)}, u32[]{:S(2)}) collective-permute-start(bf16[384,512]{1,0:T(8,128)(2,1)S(1)} %get-tuple-element.66.refs_0_.refs_2_.refs_4_), channel_id=1, source_target_pairs={{0,8},{12,4},{1,9},{13,5},{2,10},{14,6},{3,11},{15,7},{16,24},{28,... | collective-permute-start | bytes 1179656 | tf_op jit(solution)/shard_map/ppermute | solution.py:455
  52.3 0.7 collective-permute-start.16
  53.0 3.5 %collective-permute-start.15 = (bf16[384,512]{1,0:T(8,128)(2,1)S(1)}, bf16[384,512]{1,0:T(8,128)(2,1)S(1)}, u32[]{:S(2)}, u32[]{:S(2)}) collective-permute-start(bf16[384,512]{1,0:T(8,128)(2,1)S(1)} %get-tuple-element.66.refs_0_.refs_2_.refs_4_), channel_id=1, source_target_pairs={{0,4},{12,8},{1,5},{13,9},{2,6},{14,10},{3,7},{15,11},{16,20},{28,... | collective-permute-start | bytes 1179656 | tf_op jit(solution)/shard_map/ppermute | solution.py:455
  56.6 0.7 collective-permute-start.17
  57.3 4.5 %collective-permute-done.14.refs_1_.refs_2_ = bf16[384,512]{1,0:T(8,128)(2,1)S(1)} collective-permute-done((bf16[384,512]{1,0:T(8,128)(2,1)S(1)}, bf16[384,512]{1,0:T(8,128)(2,1)S(1)}, u32[]{:S(2)}, u32[]{:S(2)}) %collective-permute-start.14) | collective-permute-done | bytes 393248 | tf_op jit(solution)/shard_map/ppermute | solution.py:455
  61.8 0.7 collective-permute-start.19
  62.5 7.0 %collective-permute-done.15.refs_1_ = bf16[384,512]{1,0:T(8,128)(2,1)S(1)} collective-permute-done((bf16[384,512]{1,0:T(8,128)(2,1)S(1)}, bf16[384,512]{1,0:T(8,128)(2,1)S(1)}, u32[]{:S(2)}, u32[]{:S(2)}) %collective-permute-start.15) | collective-permute-done | bytes 393248 | tf_op jit(solution)/shard_map/ppermute | solution.py:455
  69.5 1.6 %shard_map.183.refs_9_ = bf16[384,512]{1,0:T(8,128)(2,1)S(1)} custom-call(s32[2]{0:T(128)S(1)} %pad_add_fusion.place, bf16[384,512]{1,0:T(8,128)(2,1)S(1)} %get-tuple-element.66.refs_0_.refs_2_.refs_4_, bf16[384,512]{1,0:T(8,128)(2,1)S(1)} %collective-permute-done.15.refs_1_, bf16[384,512]{1,0:T(8,128)(2,1)S(1)} %collective-permute-done.14.refs_1_.refs_2_, ...), custom_call_target="tpu_custom_call" | custom-call | flops 10000000000 | bytes 1 | tf_op jit(solution)/shard_map/pallas_call | solution.py:121
  71.1 1.6 %shard_map.184.refs_0_ = bf16[384,1024]{1,0:T(8,128)(2,1)S(1)} custom-call(s32[2]{0:T(128)S(1)} %pad_add_fusion.place, bf16[384,512]{1,0:T(8,128)(2,1)S(1)} %get-tuple-element.66.refs_0_.refs_2_.refs_4_, bf16[384,512]{1,0:T(8,128)(2,1)S(1)} %collective-permute-done.15.refs_1_, bf16[384,512]{1,0:T(8,128)(2,1)S(1)} %collective-permute-done.14.refs_1_.refs_2_, ...), custom_call_target="tpu_custom_call" | custom-call | flops 1 | bytes 1 | tf_op jit(solution)/shard_map/pallas_call | solution.py:121
  72.7 1.3 collective-permute-start.22
  74.0 0.7 collective-permute-start.20
  74.7 1.3 collective-permute-start.21
  76.0 20.1 %collective-permute-done.22.refs_1_ = bf16[384,1024]{1,0:T(8,128)(2,1)S(1)} collective-permute-done((bf16[384,1024]{1,0:T(8,128)(2,1)S(1)}, bf16[384,1024]{1,0:T(8,128)(2,1)S(1)}, u32[]{:S(2)}, u32[]{:S(2)}) %collective-permute-start.22) | collective-permute-done | bytes 786464 | tf_op jit(solution)/shard_map/ppermute | solution.py:455
  96.1 1.8 %shard_map.185 = (f32[384,512]{1,0:T(8,128)S(1)}, bf16[384,1024]{1,0:T(8,128)(2,1)S(1)}, f32[264,512]{1,0:T(8,128)S(1)}, f32[256,512]{1,0:T(8,128)S(1)}, f32[256,512]{1,0:T(8,128)S(1)}, /*index=5*/f32[256,512]{1,0:T(8,128)S(1)}) custom-call(s32[2]{0:T(128)S(1)} %pad_add_fusion.place, bf16[384,1024]{1,0:T(8,128)(2,1)S(1)} %shard_map.184.refs_0_, ...), custom_call_target="tpu_custom_call" | custom-call | flops 1 | bytes 1 | tf_op jit(solution)/shard_map/pallas_call | solution.py:121
  98.4 1.0 shard_map.182.refs_7_.refs_0_
  99.8 0.7 shard_map.186
  100.6 0.6 collective-permute-start.25
  101.2 14.9 %collective-permute-done.21.refs_1_ = bf16[384,1024]{1,0:T(8,128)(2,1)S(1)} collective-permute-done((bf16[384,1024]{1,0:T(8,128)(2,1)S(1)}, bf16[384,1024]{1,0:T(8,128)(2,1)S(1)}, u32[]{:S(2)}, u32[]{:S(2)}) %collective-permute-start.21) | collective-permute-done | bytes 786464 | tf_op jit(solution)/shard_map/ppermute | solution.py:455
  116.1 1.3 shard_map.187
  117.4 1.7 %shard_map.188 = (bf16[384,512]{1,0:T(8,128)(2,1)S(1)}, f32[1,512]{1,0:T(1,128)S(1)}, f32[1,512]{1,0:T(1,128)S(1)}, f32[256,512]{1,0:T(8,128)S(1)}, f32[256,512]{1,0:T(8,128)S(1)}) custom-call(s32[2]{0:T(128)S(1)} %pad_add_fusion.place, bf16[384,1024]{1,0:T(8,128)(2,1)S(1)} %get-tuple-element.74.refs_0_.refs_3_, f32[384,512]{1,0:T(8,128)S(1)} %get-tuple-element.76.refs_1_, ...), custom_call_target="tpu_custom_call" | custom-call | flops 10000000000 | bytes 1 | tf_op jit(solution)/shard_map/pallas_call | solution.py:121
  119.8 0.7 shard_map.189.refs_5_
  120.5 0.6 collective-permute-start.31
  121.2 2.5 %shard_map.190 = (bf16[384,512]{1,0:T(8,128)(2,1)}, f32[512,512]{1,0:T(8,128)S(1)}, f32[512,512]{1,0:T(8,128)S(1)}, f32[512,512]{1,0:T(8,128)S(1)}, f32[256,512]{1,0:T(8,128)S(1)}, /*index=5*/f32[256,512]{1,0:T(8,128)S(1)}) custom-call(s32[2]{0:T(128)S(1)} %pad_add_fusion.place, bf16[2048,384]{1,0:T(8,128)(2,1)S(1)} %shard_map.182.refs_7_.refs_0_, ...), custom_call_target="tpu_custom_call" | custom-call | flops 1 | bytes 1 | tf_op jit(solution)/shard_map/pallas_call | solution.py:121
  124.4 0.8 shard_map.191
  125.3 1.6 %collective-permute-start.30 = (f16[528,512]{1,0:T(8,128)(2,1)S(1)}, f16[528,512]{1,0:T(8,128)(2,1)S(1)}, u32[]{:S(2)}, u32[]{:S(2)}) collective-permute-start(f16[528,512]{1,0:T(8,128)(2,1)S(1)} %convert_element_type.26), channel_id=1, source_target_pairs={{0,2},{1,3},{2,0},{3,1},{4,6},{5,7},{6,4},{7,5},{8,10},{9,11},{10,... | collective-permute-start | bytes 1622024 | tf_op jit(solution)/shard_map/ppermute | solution.py:459
  126.9 3.2 %collective-permute-done.31 = f16[272,512]{1,0:T(8,128)(2,1)S(1)} collective-permute-done((f16[272,512]{1,0:T(8,128)(2,1)S(1)}, f16[272,512]{1,0:T(8,128)(2,1)S(1)}, u32[]{:S(2)}, u32[]{:S(2)}) %collective-permute-start.31) | collective-permute-done | bytes 278560 | tf_op jit(solution)/shard_map/ppermute | solution.py:459
  130.4 2.9 %shard_map.192 = (f32[512,512]{1,0:T(8,128)}, f32[512,512]{1,0:T(8,128)}, f32[512,512]{1,0:T(8,128)}) custom-call(s32[2]{0:T(128)S(1)} %pad_add_fusion.place, f32[512,512]{1,0:T(8,128)S(1)} %copy-done.2, f32[512,512]{1,0:T(8,128)S(1)} %copy-done.3, f32[512,512]{1,0:T(8,128)S(1)} %copy-done.4, f32[256,512]{1,0:T(8,128)S(1)} %multiply_add_fusion.3.near, ...), custom_call_target="tpu_custom_call" | custom-call | flops 1 | bytes 1 | tf_op jit(solution)/shard_map/pallas_call | solution.py:647
  133.4 1.3 copy-done.5
  134.7 1.1 shard_map.193
  135.8 5.4 %collective-permute-done.30 = f16[528,512]{1,0:T(8,128)(2,1)S(1)} collective-permute-done((f16[528,512]{1,0:T(8,128)(2,1)S(1)}, f16[528,512]{1,0:T(8,128)(2,1)S(1)}, u32[]{:S(2)}, u32[]{:S(2)}) %collective-permute-start.30) | collective-permute-done | bytes 540704 | tf_op jit(solution)/shard_map/ppermute | solution.py:459
  141.3 2.3 %divide_subtract_fusion = (f32[512,512]{1,0:T(8,128)}, f32[512,512]{1,0:T(8,128)}, f32[512,512]{1,0:T(8,128)}) fusion(f32[512,512]{1,0:T(8,128)S(1)} %copy-done.1, f32[512]{0:T(512)S(1)} %bitcast.15, f16[528,512]{1,0:T(8,128)(2,1)S(1)} %collective-permute-done.30, f32[512,512]{1,0:T(8,128)S(1)} %get-tuple-element.89, ...), kind=kLoop, calls=%fused_computation.2 | loop fusion | flops 4194304 | bytes 8914944 | tf_op jit(solution)/shard_map/sub | solution.py:28
  (76 shorter events, 6.9 us)
Async XLA Ops:
  0.6 15.7 %copy-start.7 = (f32[128]{0:T(128)S(1)}, f32[128]{0:T(128)}, u32[]{:S(2)}) copy-start(f32[128]{0:T(128)} %param.12) | copy-start | bytes 1540
  0.7 1.2 copy-start
  2.0 1.1 copy-start.6
  2.0 14.4 %copy-start.2 = (f32[512,512]{1,0:T(8,128)S(1)}, f32[512,512]{1,0:T(8,128)}, u32[]{:S(2)}) copy-start(f32[512,512]{1,0:T(8,128)} %param.20) | copy-start | bytes 3145732
  2.6 13.8 %collective-permute-start.5 = (bf16[544,512]{1,0:T(8,128)(2,1)S(1)}, bf16[544,512]{1,0:T(8,128)(2,1)S(1)}, u32[]{:S(2)}, u32[]{:S(2)}) collective-permute-start(bf16[544,512]{1,0:T(8,128)(2,1)S(1)} %shard_map.178.refs_6_), channel_id=1, source_target_pairs={{0,1},{1,0},{2,3},{3,2},{4,5},{5,4},{6,7},{7,6},{8,9},{9,8},{10,11... | collective-permute-start | bytes 1671176 | tf_op jit(solution)/shard_map/ppermute | solution.py:459
  3.1 15.3 %collective-permute-start.2 = (bf16[384,512]{1,0:T(8,128)(2,1)S(1)}, bf16[384,512]{1,0:T(8,128)(2,1)S(1)}, u32[]{:S(2)}, u32[]{:S(2)}) collective-permute-start(bf16[384,512]{1,0:T(8,128)(2,1)S(1)} %copy-done.6), channel_id=1, source_target_pairs={{0,8},{12,4},{1,9},{13,5},{2,10},{14,6},{3,11},{15,7},{16,24},{28,... | collective-permute-start | bytes 1179656 | tf_op jit(solution)/shard_map/ppermute | solution.py:455
  8.9 13.0 %collective-permute-start.1 = (bf16[384,512]{1,0:T(8,128)(2,1)S(1)}, bf16[384,512]{1,0:T(8,128)(2,1)S(1)}, u32[]{:S(2)}, u32[]{:S(2)}) collective-permute-start(bf16[384,512]{1,0:T(8,128)(2,1)S(1)} %copy-done.6), channel_id=1, source_target_pairs={{4,0},{8,4},{12,8},{5,1},{9,5},{13,9},{6,2},{10,6},{14,10},{7,3},{... | collective-permute-start | bytes 1179656 | tf_op jit(solution)/shard_map/ppermute | solution.py:455
  10.2 20.1 %collective-permute-start = (bf16[384,512]{1,0:T(8,128)(2,1)S(1)}, bf16[384,512]{1,0:T(8,128)(2,1)S(1)}, u32[]{:S(2)}, u32[]{:S(2)}) collective-permute-start(bf16[384,512]{1,0:T(8,128)(2,1)S(1)} %copy-done.6), channel_id=1, source_target_pairs={{0,4},{4,8},{8,12},{1,5},{5,9},{9,13},{2,6},{6,10},{10,14},{3,7},{... | collective-permute-start | bytes 1179656 | tf_op jit(solution)/shard_map/ppermute | solution.py:455
  14.8 16.2 %collective-permute-start.6 = (bf16[544,512]{1,0:T(8,128)(2,1)S(1)}, bf16[544,512]{1,0:T(8,128)(2,1)S(1)}, u32[]{:S(2)}, u32[]{:S(2)}) collective-permute-start(bf16[544,512]{1,0:T(8,128)(2,1)S(1)} %shard_map.178.refs_6_), channel_id=1, source_target_pairs={{0,2},{1,3},{2,0},{3,1},{4,6},{5,7},{6,4},{7,5},{8,10},{9,11},{10,... | collective-permute-start | bytes 1671176 | tf_op jit(solution)/shard_map/ppermute | solution.py:459
  17.0 23.7 %collective-permute-start.9 = (bf16[544,512]{1,0:T(8,128)(2,1)S(1)}, bf16[544,512]{1,0:T(8,128)(2,1)S(1)}, u32[]{:S(2)}, u32[]{:S(2)}) collective-permute-start(bf16[544,512]{1,0:T(8,128)(2,1)S(1)} %shard_map.179.refs_0_.refs_10_.refs_4_.refs_3_), channel_id=1, source_target_pairs={{0,2},{1,3},{2,0},{3,1},{4,6},{5,7},{6,4},{7,5},{8,10},{9,11},{10,... | collective-permute-start | bytes 1671176 | tf_op jit(solution)/shard_map/ppermute | solution.py:459
  18.4 18.4 %collective-permute-start.4 = (bf16[384,512]{1,0:T(8,128)(2,1)S(1)}, bf16[384,512]{1,0:T(8,128)(2,1)S(1)}, u32[]{:S(2)}, u32[]{:S(2)}) collective-permute-start(bf16[384,512]{1,0:T(8,128)(2,1)S(1)} %collective-permute-done.2.refs_3_), channel_id=1, source_target_pairs={{4,0},{8,12},{5,1},{9,13},{6,2},{10,14},{7,3},{11,15},{20,16},{24,... | collective-permute-start | bytes 1179656 | tf_op jit(solution)/shard_map/ppermute | solution.py:455
  21.9 16.2 %collective-permute-start.11 = (bf16[256,512]{1,0:T(8,128)(2,1)S(1)}, bf16[256,512]{1,0:T(8,128)(2,1)S(1)}, u32[]{:S(2)}, u32[]{:S(2)}) collective-permute-start(bf16[256,512]{1,0:T(8,128)(2,1)S(1)} %get-tuple-element.59), channel_id=1, source_target_pairs={{0,4},{4,8},{1,5},{5,9},{2,6},{6,10},{3,7},{7,11},{16,20},{20,24},... | collective-permute-start | bytes 786440 | tf_op jit(solution)/shard_map/ppermute | solution.py:455
  30.3 10.4 %collective-permute-start.12 = (bf16[256,512]{1,0:T(8,128)(2,1)S(1)}, bf16[256,512]{1,0:T(8,128)(2,1)S(1)}, u32[]{:S(2)}, u32[]{:S(2)}) collective-permute-start(bf16[256,512]{1,0:T(8,128)(2,1)S(1)} %get-tuple-element.61), channel_id=1, source_target_pairs={{8,4},{12,8},{9,5},{13,9},{10,6},{14,10},{11,7},{15,11},{24,20},{2... | collective-permute-start | bytes 786440 | tf_op jit(solution)/shard_map/ppermute | solution.py:455
  31.0 10.6 %collective-permute-start.13 = (bf16[256,512]{1,0:T(8,128)(2,1)S(1)}, bf16[256,512]{1,0:T(8,128)(2,1)S(1)}, u32[]{:S(2)}, u32[]{:S(2)}) collective-permute-start(bf16[256,512]{1,0:T(8,128)(2,1)S(1)} %get-tuple-element.63), channel_id=1, source_target_pairs={{0,8},{12,4},{1,9},{13,5},{2,10},{14,6},{3,11},{15,7},{16,24},{28,... | collective-permute-start | bytes 786440 | tf_op jit(solution)/shard_map/ppermute | solution.py:455
  36.8 11.8 %collective-permute-start.3 = (bf16[384,512]{1,0:T(8,128)(2,1)S(1)}, bf16[384,512]{1,0:T(8,128)(2,1)S(1)}, u32[]{:S(2)}, u32[]{:S(2)}) collective-permute-start(bf16[384,512]{1,0:T(8,128)(2,1)S(1)} %shard_map.177), channel_id=1, source_target_pairs={{4,0},{8,12},{5,1},{9,13},{6,2},{10,14},{7,3},{11,15},{20,16},{24,... | collective-permute-start | bytes 1179656 | tf_op jit(solution)/shard_map/ppermute | solution.py:455
  38.1 10.5 %collective-permute-start.8 = (bf16[544,512]{1,0:T(8,128)(2,1)S(1)}, bf16[544,512]{1,0:T(8,128)(2,1)S(1)}, u32[]{:S(2)}, u32[]{:S(2)}) collective-permute-start(bf16[544,512]{1,0:T(8,128)(2,1)S(1)} %shard_map.179.refs_0_.refs_10_.refs_4_.refs_3_), channel_id=1, source_target_pairs={{0,1},{1,0},{2,3},{3,2},{4,5},{5,4},{6,7},{7,6},{8,9},{9,8},{10,11... | collective-permute-start | bytes 1671176 | tf_op jit(solution)/shard_map/ppermute | solution.py:459
  40.7 8.0 %collective-permute-start.7 = (bf16[544,512]{1,0:T(8,128)(2,1)S(1)}, bf16[544,512]{1,0:T(8,128)(2,1)S(1)}, u32[]{:S(2)}, u32[]{:S(2)}) collective-permute-start(bf16[544,512]{1,0:T(8,128)(2,1)S(1)} %collective-permute-done.6.refs_8_), channel_id=1, source_target_pairs={{0,1},{1,0},{2,3},{3,2},{4,5},{5,4},{6,7},{7,6},{8,9},{9,8},{10,11... | collective-permute-start | bytes 1671176 | tf_op jit(solution)/shard_map/ppermute | solution.py:459
  40.7 8.0 %collective-permute-start.10 = (bf16[544,512]{1,0:T(8,128)(2,1)S(1)}, bf16[544,512]{1,0:T(8,128)(2,1)S(1)}, u32[]{:S(2)}, u32[]{:S(2)}) collective-permute-start(bf16[544,512]{1,0:T(8,128)(2,1)S(1)} %collective-permute-done.9.refs_12_.refs_5_.refs_6_), channel_id=1, source_target_pairs={{0,1},{1,0},{2,3},{3,2},{4,5},{5,4},{6,7},{7,6},{8,9},{9,8},{10,11... | collective-permute-start | bytes 1671176 | tf_op jit(solution)/shard_map/ppermute | solution.py:459
  41.7 15.6 %collective-permute-start.18 = (bf16[768,512]{1,0:T(8,128)(2,1)S(1)}, bf16[768,512]{1,0:T(8,128)(2,1)S(1)}, u32[]{:S(2)}, u32[]{:S(2)}) collective-permute-start(bf16[768,512]{1,0:T(8,128)(2,1)S(1)} %constant_dynamic-update-slice_fusion.refs_14_.refs_6_), channel_id=1, source_target_pairs={{4,6},{5,7},{6,4},{7,5},{8,10},{9,11},{10,8},{11,9},{20,22},{21,23... | collective-permute-start | bytes 2359304 | tf_op jit(solution)/shard_map/ppermute | solution.py:459
  50.4 11.4 %collective-permute-start.14 = (bf16[384,512]{1,0:T(8,128)(2,1)S(1)}, bf16[384,512]{1,0:T(8,128)(2,1)S(1)}, u32[]{:S(2)}, u32[]{:S(2)}) collective-permute-start(bf16[384,512]{1,0:T(8,128)(2,1)S(1)} %get-tuple-element.66.refs_0_.refs_2_.refs_4_), channel_id=1, source_target_pairs={{0,8},{12,4},{1,9},{13,5},{2,10},{14,6},{3,11},{15,7},{16,24},{28,... | collective-permute-start | bytes 1179656 | tf_op jit(solution)/shard_map/ppermute | solution.py:455
  52.3 10.2 %collective-permute-start.16 = (bf16[384,512]{1,0:T(8,128)(2,1)S(1)}, bf16[384,512]{1,0:T(8,128)(2,1)S(1)}, u32[]{:S(2)}, u32[]{:S(2)}) collective-permute-start(bf16[384,512]{1,0:T(8,128)(2,1)S(1)} %get-tuple-element.66.refs_0_.refs_2_.refs_4_), channel_id=1, source_target_pairs={{4,8},{8,4},{5,9},{9,5},{6,10},{10,6},{7,11},{11,7},{20,24},{24,20... | collective-permute-start | bytes 1179656 | tf_op jit(solution)/shard_map/ppermute | solution.py:455
  53.0 16.5 %collective-permute-start.15 = (bf16[384,512]{1,0:T(8,128)(2,1)S(1)}, bf16[384,512]{1,0:T(8,128)(2,1)S(1)}, u32[]{:S(2)}, u32[]{:S(2)}) collective-permute-start(bf16[384,512]{1,0:T(8,128)(2,1)S(1)} %get-tuple-element.66.refs_0_.refs_2_.refs_4_), channel_id=1, source_target_pairs={{0,4},{12,8},{1,5},{13,9},{2,6},{14,10},{3,7},{15,11},{16,20},{28,... | collective-permute-start | bytes 1179656 | tf_op jit(solution)/shard_map/ppermute | solution.py:455
  56.6 14.5 %collective-permute-start.17 = (bf16[768,512]{1,0:T(8,128)(2,1)S(1)}, bf16[768,512]{1,0:T(8,128)(2,1)S(1)}, u32[]{:S(2)}, u32[]{:S(2)}) collective-permute-start(bf16[768,512]{1,0:T(8,128)(2,1)S(1)} %constant_dynamic-update-slice_fusion.refs_14_.refs_6_), channel_id=1, source_target_pairs={{4,5},{5,4},{6,7},{7,6},{8,9},{9,8},{10,11},{11,10},{20,21},{21,20... | collective-permute-start | bytes 2359304 | tf_op jit(solution)/shard_map/ppermute | solution.py:459
  61.8 9.3 %collective-permute-start.19 = (bf16[768,512]{1,0:T(8,128)(2,1)S(1)}, bf16[768,512]{1,0:T(8,128)(2,1)S(1)}, u32[]{:S(2)}, u32[]{:S(2)}) collective-permute-start(bf16[768,512]{1,0:T(8,128)(2,1)S(1)} %collective-permute-done.18.refs_7_), channel_id=1, source_target_pairs={{4,5},{5,4},{6,7},{7,6},{8,9},{9,8},{10,11},{11,10},{20,21},{21,20... | collective-permute-start | bytes 2359304 | tf_op jit(solution)/shard_map/ppermute | solution.py:459
  72.7 23.4 %collective-permute-start.22 = (bf16[384,1024]{1,0:T(8,128)(2,1)S(1)}, bf16[384,1024]{1,0:T(8,128)(2,1)S(1)}, u32[]{:S(2)}, u32[]{:S(2)}) collective-permute-start(bf16[384,1024]{1,0:T(8,128)(2,1)S(1)} %shard_map.184.refs_0_), channel_id=1, source_target_pairs={{4,0},{8,12},{5,1},{9,13},{6,2},{10,14},{7,3},{11,15},{20,16},{24,... | collective-permute-start | bytes 2359304 | tf_op jit(solution)/shard_map/ppermute | solution.py:455
  74.0 22.1 %collective-permute-start.20 = (bf16[384,1024]{1,0:T(8,128)(2,1)S(1)}, bf16[384,1024]{1,0:T(8,128)(2,1)S(1)}, u32[]{:S(2)}, u32[]{:S(2)}) collective-permute-start(bf16[384,1024]{1,0:T(8,128)(2,1)S(1)} %shard_map.184.refs_0_), channel_id=1, source_target_pairs={{4,8},{8,4},{5,9},{9,5},{6,10},{10,6},{7,11},{11,7},{20,24},{24,20... | collective-permute-start | bytes 2359304 | tf_op jit(solution)/shard_map/ppermute | solution.py:455
  74.7 41.4 %collective-permute-start.21 = (bf16[384,1024]{1,0:T(8,128)(2,1)S(1)}, bf16[384,1024]{1,0:T(8,128)(2,1)S(1)}, u32[]{:S(2)}, u32[]{:S(2)}) collective-permute-start(bf16[384,1024]{1,0:T(8,128)(2,1)S(1)} %shard_map.184.refs_0_), channel_id=1, source_target_pairs={{8,0},{4,12},{9,1},{5,13},{10,2},{6,14},{11,3},{7,15},{24,16},{20,... | collective-permute-start | bytes 2359304 | tf_op jit(solution)/shard_map/ppermute | solution.py:455
  97.8 2.0 %collective-permute-start.23 = (f32[264,512]{1,0:T(8,128)S(1)}, f32[264,512]{1,0:T(8,128)S(1)}, u32[]{:S(2)}, u32[]{:S(2)}) collective-permute-start(f32[264,512]{1,0:T(8,128)S(1)} %get-tuple-element.71), channel_id=1, source_target_pairs={{0,1},{1,0},{2,3},{3,2},{4,5},{5,4},{6,7},{7,6},{8,9},{9,8},{10,11... | collective-permute-start | bytes 1622024 | tf_op jit(solution)/shard_map/ppermute | solution.py:459
  97.9 18.2 %collective-permute-start.24 = (f32[256,512]{1,0:T(8,128)S(1)}, f32[256,512]{1,0:T(8,128)S(1)}, u32[]{:S(2)}, u32[]{:S(2)}) collective-permute-start(f32[256,512]{1,0:T(8,128)S(1)} %get-tuple-element.73), channel_id=1, source_target_pairs={{0,1},{1,0},{2,3},{3,2},{4,5},{5,4},{6,7},{7,6},{8,9},{9,8},{10,11... | collective-permute-start | bytes 1572872 | tf_op jit(solution)/shard_map/ppermute | solution.py:459
  100.6 16.8 %collective-permute-start.25 = (f16[272,512]{1,0:T(8,128)(2,1)S(1)}, f16[272,512]{1,0:T(8,128)(2,1)S(1)}, u32[]{:S(2)}, u32[]{:S(2)}) collective-permute-start(f16[272,512]{1,0:T(8,128)(2,1)S(1)} %convert_element_type.25), channel_id=1, source_target_pairs={{0,2},{1,3},{2,0},{3,1},{4,6},{5,7},{6,4},{7,5},{8,10},{9,11},{10,... | collective-permute-start | bytes 835592 | tf_op jit(solution)/shard_map/ppermute | solution.py:459
  117.3 2.5 %collective-permute-start.26 = (f32[256,512]{1,0:T(8,128)S(1)}, f32[256,512]{1,0:T(8,128)S(1)}, u32[]{:S(2)}, u32[]{:S(2)}) collective-permute-start(f32[256,512]{1,0:T(8,128)S(1)} %get-tuple-element.82), channel_id=1, source_target_pairs={{0,1},{1,0},{2,3},{3,2},{4,5},{5,4},{6,7},{7,6},{8,9},{9,8},{10,11... | collective-permute-start | bytes 1572872 | tf_op jit(solution)/shard_map/ppermute | solution.py:459
  119.2 5.2 %collective-permute-start.27 = (f32[256,512]{1,0:T(8,128)S(1)}, f32[256,512]{1,0:T(8,128)S(1)}, u32[]{:S(2)}, u32[]{:S(2)}) collective-permute-start(f32[256,512]{1,0:T(8,128)S(1)} %get-tuple-element.85), channel_id=1, source_target_pairs={{0,1},{1,0},{2,3},{3,2},{4,5},{5,4},{6,7},{7,6},{8,9},{9,8},{10,11... | collective-permute-start | bytes 1572872 | tf_op jit(solution)/shard_map/ppermute | solution.py:459
  119.7 4.6 %collective-permute-start.28 = (f32[256,512]{1,0:T(8,128)S(1)}, f32[256,512]{1,0:T(8,128)S(1)}, u32[]{:S(2)}, u32[]{:S(2)}) collective-permute-start(f32[256,512]{1,0:T(8,128)S(1)} %get-tuple-element.86), channel_id=1, source_target_pairs={{0,1},{1,0},{2,3},{3,2},{4,5},{5,4},{6,7},{7,6},{8,9},{9,8},{10,11... | collective-permute-start | bytes 1572872 | tf_op jit(solution)/shard_map/ppermute | solution.py:459
  120.5 9.5 %collective-permute-start.31 = (f16[272,512]{1,0:T(8,128)(2,1)S(1)}, f16[272,512]{1,0:T(8,128)(2,1)S(1)}, u32[]{:S(2)}, u32[]{:S(2)}) collective-permute-start(f16[272,512]{1,0:T(8,128)(2,1)S(1)} %convert_element_type.28), channel_id=1, source_target_pairs={{0,2},{1,3},{2,0},{3,1},{4,6},{5,7},{6,4},{7,5},{8,10},{9,11},{10,... | collective-permute-start | bytes 835592 | tf_op jit(solution)/shard_map/ppermute | solution.py:459
  123.7 6.5 %collective-permute-start.33 = (f32[256,512]{1,0:T(8,128)S(1)}, f32[256,512]{1,0:T(8,128)S(1)}, u32[]{:S(2)}, u32[]{:S(2)}) collective-permute-start(f32[256,512]{1,0:T(8,128)S(1)} %get-tuple-element.97), channel_id=1, source_target_pairs={{0,1},{1,0},{2,3},{3,2},{4,5},{5,4},{6,7},{7,6},{8,9},{9,8},{10,11... | collective-permute-start | bytes 1572872 | tf_op jit(solution)/shard_map/ppermute | solution.py:459
  123.8 17.4 %collective-permute-start.29 = (f32[512,512]{1,0:T(8,128)S(1)}, f32[512,512]{1,0:T(8,128)S(1)}, u32[]{:S(2)}, u32[]{:S(2)}) collective-permute-start(f32[512,512]{1,0:T(8,128)S(1)} %get-tuple-element.90), channel_id=1, source_target_pairs={{0,1},{1,0},{2,3},{3,2},{4,5},{5,4},{6,7},{7,6},{8,9},{9,8},{10,11... | collective-permute-start | bytes 3145736 | tf_op jit(solution)/shard_map/ppermute | solution.py:459
  125.2 5.2 %copy-start.3 = (f32[512,512]{1,0:T(8,128)S(1)}, f32[512,512]{1,0:T(8,128)}, u32[]{:S(2)}) copy-start(f32[512,512]{1,0:T(8,128)} %moment) | copy-start | bytes 3145732
  125.2 5.2 %copy-start.4 = (f32[512,512]{1,0:T(8,128)S(1)}, f32[512,512]{1,0:T(8,128)}, u32[]{:S(2)}) copy-start(f32[512,512]{1,0:T(8,128)} %square) | copy-start | bytes 3145732
  125.3 15.9 %collective-permute-start.30 = (f16[528,512]{1,0:T(8,128)(2,1)S(1)}, f16[528,512]{1,0:T(8,128)(2,1)S(1)}, u32[]{:S(2)}, u32[]{:S(2)}) collective-permute-start(f16[528,512]{1,0:T(8,128)(2,1)S(1)} %convert_element_type.26), channel_id=1, source_target_pairs={{0,2},{1,3},{2,0},{3,1},{4,6},{5,7},{6,4},{7,5},{8,10},{9,11},{10,... | collective-permute-start | bytes 1622024 | tf_op jit(solution)/shard_map/ppermute | solution.py:459
  130.1 3.2 %collective-permute-start.32 = (f32[1,512]{1,0:T(1,128)S(1)}, f32[1,512]{1,0:T(1,128)S(1)}, u32[]{:S(2)}, u32[]{:S(2)}) collective-permute-start(f32[1,512]{1,0:T(1,128)S(1)} %get-tuple-element.112.refs_3_), channel_id=1, source_target_pairs={{0,1},{1,0},{2,3},{3,2},{4,5},{5,4},{6,7},{7,6},{8,9},{9,8},{10,11... | collective-permute-start | bytes 6152 | tf_op jit(solution)/shard_map/ppermute | solution.py:459
  130.3 3.0 %copy-start.8 = (f32[128]{0:T(128)S(1)}, f32[128]{0:T(128)}, u32[]{:S(2)}) copy-start(f32[128]{0:T(128)} %param.16) | copy-start | bytes 1540
  130.4 3.0 %copy-start.9 = (f32[128]{0:T(128)S(1)}, f32[128]{0:T(128)}, u32[]{:S(2)}) copy-start(f32[128]{0:T(128)} %param.17) | copy-start | bytes 1540
  130.4 10.9 %copy-start.10 = (f32[512,512]{1,0:T(8,128)S(1)}, f32[512,512]{1,0:T(8,128)}, u32[]{:S(2)}) copy-start(f32[512,512]{1,0:T(8,128)} %param.14) | copy-start | bytes 3145732
  130.4 10.9 %copy-start.11 = (f32[512,512]{1,0:T(8,128)S(1)}, f32[512,512]{1,0:T(8,128)}, u32[]{:S(2)}) copy-start(f32[512,512]{1,0:T(8,128)} %param.15) | copy-start | bytes 3145732
  133.3 7.9 %copy-start.1 = (f32[512,512]{1,0:T(8,128)S(1)}, f32[512,512]{1,0:T(8,128)}, u32[]{:S(2)}) copy-start(f32[512,512]{1,0:T(8,128)} %refs_0_.3) | copy-start | bytes 3145732
  133.4 1.3 copy-start.5

commit v20 on v19

--- a/solution.py
+++ b/solution.py
@@ -263,21 +263,19 @@
     return (given - total).astype(BF16)
 
 
-def own_error_body(place, own, near, across, middle, dec0, dec2, row0, row2, inputs, out):
-    half = out.shape[1] // 2
-    codes = (own, near, across, middle)
-    out[:, :half] = rebuilt_error(place, 0, codes, dec0, row0, inputs)
-    out[:, half:] = rebuilt_error(place, 2, codes, dec2, row2, inputs)
-
-
-def error_body(place, own, near, across, middle, dec1, dec3, row1, row3, inputs, made, error):
-    i = place[1]
+def met_body(place, out):
+    out[...] = jnp.zeros(out.shape, F32)
+
+
+def error_body(
+    place, own, near, across, middle, dec0, dec1, dec2, dec3, row0, row1, row2, row3, inputs, error
+):
     half = error.shape[1] // 4
     codes = (own, near, across, middle)
-    error[:, columns(i * half, half)] = made[:, :half]
-    error[:, columns((i ^ 2) * half, half)] = made[:, half:]
-    error[:, columns((i ^ 1) * half, half)] = rebuilt_error(place, 1, codes, dec1, row1, inputs)
-    error[:, columns((i ^ 3) * half, half)] = rebuilt_error(place, 3, codes, dec3, row3, inputs)
+    decs, rows = (dec0, dec1, dec2, dec3), (row0, row1, row2, row3)
+    for t in range(4):
+        block = rebuilt_error(place, t, codes, decs[t], rows[t], inputs)
+        error[:, columns((place[1] ^ t) * half, half)] = block
 
 
 def pick(place, middle, end, out):
@@ -528,29 +526,21 @@
     rows_both = flip(behind(rows_chip, codes_across), 1, (1, 2))
 
     all_codes = codes, codes_near, codes_across, codes_middle
-    (made,) = local_kernel(
-        own_error_body,
-        [shape((count, features // 4), BF16)],
-        place,
-        *all_codes,
-        dec[0],
-        dec[2],
-        rows_own,
-        rows_chip,
-        inputs,
-        cost=NOTABLE,
+    (met,) = local_kernel(
+        met_body, [shape((8, 128), F32)], place, after=(*all_codes, rows_chip), cost=NOTABLE
     )
     (own_error,) = local_kernel(
         error_body,
         [shape((count, features // 2), BF16)],
         place,
         *all_codes,
-        dec[1],
-        dec[3],
+        *dec,
+        rows_own,
         rows_core,
+        rows_chip,
         rows_both,
         inputs,
-        made,
+        after=(met,),
     )
     swapped = along(own_error, [(1, 2), (2, 1)])
     passed = along(own_error, [(1, 0), (2, 3)])

time: 144 us -> 144 us (level)
  transfers between devices with their start and end apart: 34 -> 34, of which waited for: 12 -> 12; matrix products, arithmetic and copies ran while one was open for 0% -> 0% of each run, Pallas kernels for 14% -> 13%
where the time goes in v20:
time: 144 us; the launch traced here: 143 us
  waiting for transfers between devices  67.1 us (47%)
  starting transfers between devices  47.9 us (33%)
  Pallas kernels  21.6 us (15%)
  other arithmetic  2.88 us (2%)
  local copies, waits for them, and re-layouts  2.64 us (2%)
    ppermute x14, waiting for transfers between devices, along(): return lax.ppermute(value, 'latent', pairs)  55.5 us
    ppermute x14, starting transfers between devices, along(): return lax.ppermute(value, 'latent', pairs)  38 us
    pallas_call x16, Pallas kernels, local_kernel(): pl.pallas_call(run, out_shape=outs, in_specs=[SMEM] + [VMEM] * len(args)...  18.7 us
    ppermute x20, waiting for transfers between devices, flip(): return lax.ppermute(value, ('latent', 'dp'), pairs)  11.6 us
    ppermute x20, starting transfers between devices, flip(): return lax.ppermute(value, ('latent', 'dp'), pairs)  9.98 us
    pallas_call x1, Pallas kernels, line_shards(): pl.pallas_call(functools.partial(decoder_step_body, rows), grid=(4,), out...  2.94 us
  transfers between devices with their start and end apart: 34, of which 12 were waited for; matrix products, arithmetic and copies ran while one was open for 0% of the time, Pallas kernels for 13%

profile of v20, /device:TPU:0, one launch (start us, length us, event | category | flops | bytes accessed | tf_op | source)
XLA Modules:
  0.0 143.4 jit_solution(2375041018332139701)
XLA Ops:
  0.7 1.2 copy-done
  3.1 5.8 %collective-permute-start.2 = (bf16[384,512]{1,0:T(8,128)(2,1)S(1)}, bf16[384,512]{1,0:T(8,128)(2,1)S(1)}, u32[]{:S(2)}, u32[]{:S(2)}) collective-permute-start(bf16[384,512]{1,0:T(8,128)(2,1)S(1)} %copy-done.6), channel_id=1, source_target_pairs={{0,8},{12,4},{1,9},{13,5},{2,10},{14,6},{3,11},{15,7},{16,24},{28,... | collective-permute-start | bytes 1179656 | tf_op jit(solution)/shard_map/ppermute | solution.py:453
  8.9 1.3 collective-permute-start.1
  10.2 4.6 %collective-permute-start = (bf16[384,512]{1,0:T(8,128)(2,1)S(1)}, bf16[384,512]{1,0:T(8,128)(2,1)S(1)}, u32[]{:S(2)}, u32[]{:S(2)}) collective-permute-start(bf16[384,512]{1,0:T(8,128)(2,1)S(1)} %copy-done.6), channel_id=1, source_target_pairs={{0,4},{4,8},{8,12},{1,5},{5,9},{9,13},{2,6},{6,10},{10,14},{3,7},{... | collective-permute-start | bytes 1179656 | tf_op jit(solution)/shard_map/ppermute | solution.py:453
  14.8 1.6 %collective-permute-start.6 = (bf16[544,512]{1,0:T(8,128)(2,1)S(1)}, bf16[544,512]{1,0:T(8,128)(2,1)S(1)}, u32[]{:S(2)}, u32[]{:S(2)}) collective-permute-start(bf16[544,512]{1,0:T(8,128)(2,1)S(1)} %shard_map.178.refs_6_), channel_id=1, source_target_pairs={{0,2},{1,3},{2,0},{3,1},{4,6},{5,7},{6,4},{7,5},{8,10},{9,11},{10,... | collective-permute-start | bytes 1671176 | tf_op jit(solution)/shard_map/ppermute | solution.py:457
  16.4 0.6 shard_map.179.refs_0_.refs_10_.refs_4_.refs_3_
  17.0 0.6 collective-permute-start.9
  17.6 0.8 collective-permute-done.2.refs_3_
  18.4 1.3 collective-permute-start.4
  20.3 1.6 %collective-permute-done.1.refs_1_.refs_2_ = bf16[384,512]{1,0:T(8,128)(2,1)S(1)} collective-permute-done((bf16[384,512]{1,0:T(8,128)(2,1)S(1)}, bf16[384,512]{1,0:T(8,128)(2,1)S(1)}, u32[]{:S(2)}, u32[]{:S(2)}) %collective-permute-start.1) | collective-permute-done | bytes 393248 | tf_op jit(solution)/shard_map/ppermute | solution.py:453
  21.9 8.4 %collective-permute-start.11 = (bf16[256,512]{1,0:T(8,128)(2,1)S(1)}, bf16[256,512]{1,0:T(8,128)(2,1)S(1)}, u32[]{:S(2)}, u32[]{:S(2)}) collective-permute-start(bf16[256,512]{1,0:T(8,128)(2,1)S(1)} %get-tuple-element.59), channel_id=1, source_target_pairs={{0,4},{4,8},{1,5},{5,9},{2,6},{6,10},{3,7},{7,11},{16,20},{20,24},... | collective-permute-start | bytes 786440 | tf_op jit(solution)/shard_map/ppermute | solution.py:453
  30.3 0.7 collective-permute-start.12
  31.0 5.2 %collective-permute-start.13 = (bf16[256,512]{1,0:T(8,128)(2,1)S(1)}, bf16[256,512]{1,0:T(8,128)(2,1)S(1)}, u32[]{:S(2)}, u32[]{:S(2)}) collective-permute-start(bf16[256,512]{1,0:T(8,128)(2,1)S(1)} %get-tuple-element.63), channel_id=1, source_target_pairs={{0,8},{12,4},{1,9},{13,5},{2,10},{14,6},{3,11},{15,7},{16,24},{28,... | collective-permute-start | bytes 786440 | tf_op jit(solution)/shard_map/ppermute | solution.py:453
  36.8 1.3 collective-permute-start.3
  38.2 2.5 %collective-permute-done.9.refs_12_.refs_6_.refs_5_ = bf16[544,512]{1,0:T(8,128)(2,1)S(1)} collective-permute-done((bf16[544,512]{1,0:T(8,128)(2,1)S(1)}, bf16[544,512]{1,0:T(8,128)(2,1)S(1)}, u32[]{:S(2)}, u32[]{:S(2)}) %collective-permute-start.9) | collective-permute-done | bytes 557088 | tf_op jit(solution)/shard_map/ppermute | solution.py:457
  41.7 0.7 collective-permute-start.18
  42.4 6.2 %collective-permute-done.3.refs_4_ = bf16[384,512]{1,0:T(8,128)(2,1)S(1)} collective-permute-done((bf16[384,512]{1,0:T(8,128)(2,1)S(1)}, bf16[384,512]{1,0:T(8,128)(2,1)S(1)}, u32[]{:S(2)}, u32[]{:S(2)}) %collective-permute-start.3) | collective-permute-done | bytes 393248 | tf_op jit(solution)/shard_map/ppermute | solution.py:453
  48.6 1.8 %shard_map.181 = (bf16[384,512]{1,0:T(8,128)(2,1)S(1)}, bf16[384,512]{1,0:T(8,128)(2,1)S(1)}, bf16[384,2048]{1,0:T(8,128)(2,1)S(1)}, f32[1,512]{1,0:T(1,128)S(1)}) custom-call(s32[2]{0:T(128)S(1)} %pad_add_fusion.place, bf16[384,512]{1,0:T(8,128)(2,1)S(1)} %copy-done.6, bf16[384,512]{1,0:T(8,128)(2,1)S(1)} %collective-permute-done.refs_0_.refs_1_, ...), custom_call_target="tpu_custom_call" | custom-call | flops 1 | bytes 1 | tf_op jit(solution)/shard_map/pallas_call | solution.py:121
  50.4 1.9 %collective-permute-start.14 = (bf16[384,512]{1,0:T(8,128)(2,1)S(1)}, bf16[384,512]{1,0:T(8,128)(2,1)S(1)}, u32[]{:S(2)}, u32[]{:S(2)}) collective-permute-start(bf16[384,512]{1,0:T(8,128)(2,1)S(1)} %get-tuple-element.66.refs_0_.refs_2_.refs_4_), channel_id=1, source_target_pairs={{0,8},{12,4},{1,9},{13,5},{2,10},{14,6},{3,11},{15,7},{16,24},{28,... | collective-permute-start | bytes 1179656 | tf_op jit(solution)/shard_map/ppermute | solution.py:453
  52.3 0.7 collective-permute-start.16
  53.0 3.5 %collective-permute-start.15 = (bf16[384,512]{1,0:T(8,128)(2,1)S(1)}, bf16[384,512]{1,0:T(8,128)(2,1)S(1)}, u32[]{:S(2)}, u32[]{:S(2)}) collective-permute-start(bf16[384,512]{1,0:T(8,128)(2,1)S(1)} %get-tuple-element.66.refs_0_.refs_2_.refs_4_), channel_id=1, source_target_pairs={{0,4},{12,8},{1,5},{13,9},{2,6},{14,10},{3,7},{15,11},{16,20},{28,... | collective-permute-start | bytes 1179656 | tf_op jit(solution)/shard_map/ppermute | solution.py:453
  56.6 0.7 collective-permute-start.17
  57.3 4.5 %collective-permute-done.14.refs_1_.refs_2_ = bf16[384,512]{1,0:T(8,128)(2,1)S(1)} collective-permute-done((bf16[384,512]{1,0:T(8,128)(2,1)S(1)}, bf16[384,512]{1,0:T(8,128)(2,1)S(1)}, u32[]{:S(2)}, u32[]{:S(2)}) %collective-permute-start.14) | collective-permute-done | bytes 393248 | tf_op jit(solution)/shard_map/ppermute | solution.py:453
  61.8 0.7 collective-permute-start.19
  62.5 7.0 %collective-permute-done.15.refs_1_ = bf16[384,512]{1,0:T(8,128)(2,1)S(1)} collective-permute-done((bf16[384,512]{1,0:T(8,128)(2,1)S(1)}, bf16[384,512]{1,0:T(8,128)(2,1)S(1)}, u32[]{:S(2)}, u32[]{:S(2)}) %collective-permute-start.15) | collective-permute-done | bytes 393248 | tf_op jit(solution)/shard_map/ppermute | solution.py:453
  70.1 2.4 %shard_map.184.refs_0_ = bf16[384,1024]{1,0:T(8,128)(2,1)S(1)} custom-call(s32[2]{0:T(128)S(1)} %pad_add_fusion.place, bf16[384,512]{1,0:T(8,128)(2,1)S(1)} %get-tuple-element.66.refs_0_.refs_2_.refs_4_, bf16[384,512]{1,0:T(8,128)(2,1)S(1)} %collective-permute-done.15.refs_1_, bf16[384,512]{1,0:T(8,128)(2,1)S(1)} %collective-permute-done.14.refs_1_.refs_2_, ...), custom_call_target="tpu_custom_call" | custom-call | flops 1 | bytes 1 | tf_op jit(solution)/shard_map/pallas_call | solution.py:121
  72.5 1.3 collective-permute-start.22
  73.8 0.7 collective-permute-start.20
  74.5 1.3 collective-permute-start.21
  75.8 20.1 %collective-permute-done.22.refs_1_ = bf16[384,1024]{1,0:T(8,128)(2,1)S(1)} collective-permute-done((bf16[384,1024]{1,0:T(8,128)(2,1)S(1)}, bf16[384,1024]{1,0:T(8,128)(2,1)S(1)}, u32[]{:S(2)}, u32[]{:S(2)}) %collective-permute-start.22) | collective-permute-done | bytes 786464 | tf_op jit(solution)/shard_map/ppermute | solution.py:453
  95.9 1.8 %shard_map.185 = (f32[384,512]{1,0:T(8,128)S(1)}, bf16[384,1024]{1,0:T(8,128)(2,1)S(1)}, f32[264,512]{1,0:T(8,128)S(1)}, f32[256,512]{1,0:T(8,128)S(1)}, f32[256,512]{1,0:T(8,128)S(1)}, /*index=5*/f32[256,512]{1,0:T(8,128)S(1)}) custom-call(s32[2]{0:T(128)S(1)} %pad_add_fusion.place, bf16[384,1024]{1,0:T(8,128)(2,1)S(1)} %shard_map.184.refs_0_, ...), custom_call_target="tpu_custom_call" | custom-call | flops 1 | bytes 1 | tf_op jit(solution)/shard_map/pallas_call | solution.py:121
  98.3 1.0 shard_map.182.refs_7_.refs_0_
  99.7 0.7 shard_map.186
  100.4 0.6 collective-permute-start.25
  101.0 14.9 %collective-permute-done.21.refs_1_ = bf16[384,1024]{1,0:T(8,128)(2,1)S(1)} collective-permute-done((bf16[384,1024]{1,0:T(8,128)(2,1)S(1)}, bf16[384,1024]{1,0:T(8,128)(2,1)S(1)}, u32[]{:S(2)}, u32[]{:S(2)}) %collective-permute-start.21) | collective-permute-done | bytes 786464 | tf_op jit(solution)/shard_map/ppermute | solution.py:453
  115.9 1.3 shard_map.187
  117.3 1.7 %shard_map.188 = (bf16[384,512]{1,0:T(8,128)(2,1)S(1)}, f32[1,512]{1,0:T(1,128)S(1)}, f32[1,512]{1,0:T(1,128)S(1)}, f32[256,512]{1,0:T(8,128)S(1)}, f32[256,512]{1,0:T(8,128)S(1)}) custom-call(s32[2]{0:T(128)S(1)} %pad_add_fusion.place, bf16[384,1024]{1,0:T(8,128)(2,1)S(1)} %get-tuple-element.74.refs_0_.refs_3_, f32[384,512]{1,0:T(8,128)S(1)} %get-tuple-element.76.refs_1_, ...), custom_call_target="tpu_custom_call" | custom-call | flops 10000000000 | bytes 1 | tf_op jit(solution)/shard_map/pallas_call | solution.py:121
  119.6 0.7 shard_map.189.refs_5_
  120.4 0.6 collective-permute-start.31
  121.0 2.5 %shard_map.190 = (bf16[384,512]{1,0:T(8,128)(2,1)}, f32[512,512]{1,0:T(8,128)S(1)}, f32[512,512]{1,0:T(8,128)S(1)}, f32[512,512]{1,0:T(8,128)S(1)}, f32[256,512]{1,0:T(8,128)S(1)}, /*index=5*/f32[256,512]{1,0:T(8,128)S(1)}) custom-call(s32[2]{0:T(128)S(1)} %pad_add_fusion.place, bf16[2048,384]{1,0:T(8,128)(2,1)S(1)} %shard_map.182.refs_7_.refs_0_, ...), custom_call_target="tpu_custom_call" | custom-call | flops 1 | bytes 1 | tf_op jit(solution)/shard_map/pallas_call | solution.py:121
  124.2 0.8 shard_map.191
  125.2 1.6 %collective-permute-start.30 = (f16[528,512]{1,0:T(8,128)(2,1)S(1)}, f16[528,512]{1,0:T(8,128)(2,1)S(1)}, u32[]{:S(2)}, u32[]{:S(2)}) collective-permute-start(f16[528,512]{1,0:T(8,128)(2,1)S(1)} %convert_element_type.26), channel_id=1, source_target_pairs={{0,2},{1,3},{2,0},{3,1},{4,6},{5,7},{6,4},{7,5},{8,10},{9,11},{10,... | collective-permute-start | bytes 1622024 | tf_op jit(solution)/shard_map/ppermute | solution.py:457
  126.7 3.2 %collective-permute-done.31 = f16[272,512]{1,0:T(8,128)(2,1)S(1)} collective-permute-done((f16[272,512]{1,0:T(8,128)(2,1)S(1)}, f16[272,512]{1,0:T(8,128)(2,1)S(1)}, u32[]{:S(2)}, u32[]{:S(2)}) %collective-permute-start.31) | collective-permute-done | bytes 278560 | tf_op jit(solution)/shard_map/ppermute | solution.py:457
  130.2 2.9 %shard_map.192 = (f32[512,512]{1,0:T(8,128)}, f32[512,512]{1,0:T(8,128)}, f32[512,512]{1,0:T(8,128)}) custom-call(s32[2]{0:T(128)S(1)} %pad_add_fusion.place, f32[512,512]{1,0:T(8,128)S(1)} %copy-done.2, f32[512,512]{1,0:T(8,128)S(1)} %copy-done.3, f32[512,512]{1,0:T(8,128)S(1)} %copy-done.4, f32[256,512]{1,0:T(8,128)S(1)} %multiply_add_fusion.3.near, ...), custom_call_target="tpu_custom_call" | custom-call | flops 1 | bytes 1 | tf_op jit(solution)/shard_map/pallas_call | solution.py:637
  133.2 1.3 copy-done.5
  134.5 1.1 shard_map.193
  135.6 5.5 %collective-permute-done.30 = f16[528,512]{1,0:T(8,128)(2,1)S(1)} collective-permute-done((f16[528,512]{1,0:T(8,128)(2,1)S(1)}, f16[528,512]{1,0:T(8,128)(2,1)S(1)}, u32[]{:S(2)}, u32[]{:S(2)}) %collective-permute-start.30) | collective-permute-done | bytes 540704 | tf_op jit(solution)/shard_map/ppermute | solution.py:457
  141.1 2.3 %divide_subtract_fusion = (f32[512,512]{1,0:T(8,128)}, f32[512,512]{1,0:T(8,128)}, f32[512,512]{1,0:T(8,128)}) fusion(f32[512,512]{1,0:T(8,128)S(1)} %copy-done.1, f32[512]{0:T(512)S(1)} %bitcast.15, f16[528,512]{1,0:T(8,128)(2,1)S(1)} %collective-permute-done.30, f32[512,512]{1,0:T(8,128)S(1)} %get-tuple-element.89, ...), kind=kLoop, calls=%fused_computation.2 | loop fusion | flops 4194304 | bytes 8914944 | tf_op jit(solution)/shard_map/sub | solution.py:28
  (76 shorter events, 6.8 us)
Async XLA Ops:
  0.6 15.7 %copy-start.7 = (f32[128]{0:T(128)S(1)}, f32[128]{0:T(128)}, u32[]{:S(2)}) copy-start(f32[128]{0:T(128)} %param.12) | copy-start | bytes 1540
  0.7 1.2 copy-start
  2.0 1.1 copy-start.6
  2.0 14.4 %copy-start.2 = (f32[512,512]{1,0:T(8,128)S(1)}, f32[512,512]{1,0:T(8,128)}, u32[]{:S(2)}) copy-start(f32[512,512]{1,0:T(8,128)} %param.20) | copy-start | bytes 3145732
  2.6 13.8 %collective-permute-start.5 = (bf16[544,512]{1,0:T(8,128)(2,1)S(1)}, bf16[544,512]{1,0:T(8,128)(2,1)S(1)}, u32[]{:S(2)}, u32[]{:S(2)}) collective-permute-start(bf16[544,512]{1,0:T(8,128)(2,1)S(1)} %shard_map.178.refs_6_), channel_id=1, source_target_pairs={{0,1},{1,0},{2,3},{3,2},{4,5},{5,4},{6,7},{7,6},{8,9},{9,8},{10,11... | collective-permute-start | bytes 1671176 | tf_op jit(solution)/shard_map/ppermute | solution.py:457
  3.1 15.3 %collective-permute-start.2 = (bf16[384,512]{1,0:T(8,128)(2,1)S(1)}, bf16[384,512]{1,0:T(8,128)(2,1)S(1)}, u32[]{:S(2)}, u32[]{:S(2)}) collective-permute-start(bf16[384,512]{1,0:T(8,128)(2,1)S(1)} %copy-done.6), channel_id=1, source_target_pairs={{0,8},{12,4},{1,9},{13,5},{2,10},{14,6},{3,11},{15,7},{16,24},{28,... | collective-permute-start | bytes 1179656 | tf_op jit(solution)/shard_map/ppermute | solution.py:453
  8.9 13.0 %collective-permute-start.1 = (bf16[384,512]{1,0:T(8,128)(2,1)S(1)}, bf16[384,512]{1,0:T(8,128)(2,1)S(1)}, u32[]{:S(2)}, u32[]{:S(2)}) collective-permute-start(bf16[384,512]{1,0:T(8,128)(2,1)S(1)} %copy-done.6), channel_id=1, source_target_pairs={{4,0},{8,4},{12,8},{5,1},{9,5},{13,9},{6,2},{10,6},{14,10},{7,3},{... | collective-permute-start | bytes 1179656 | tf_op jit(solution)/shard_map/ppermute | solution.py:453
  10.2 20.1 %collective-permute-start = (bf16[384,512]{1,0:T(8,128)(2,1)S(1)}, bf16[384,512]{1,0:T(8,128)(2,1)S(1)}, u32[]{:S(2)}, u32[]{:S(2)}) collective-permute-start(bf16[384,512]{1,0:T(8,128)(2,1)S(1)} %copy-done.6), channel_id=1, source_target_pairs={{0,4},{4,8},{8,12},{1,5},{5,9},{9,13},{2,6},{6,10},{10,14},{3,7},{... | collective-permute-start | bytes 1179656 | tf_op jit(solution)/shard_map/ppermute | solution.py:453
  14.8 16.2 %collective-permute-start.6 = (bf16[544,512]{1,0:T(8,128)(2,1)S(1)}, bf16[544,512]{1,0:T(8,128)(2,1)S(1)}, u32[]{:S(2)}, u32[]{:S(2)}) collective-permute-start(bf16[544,512]{1,0:T(8,128)(2,1)S(1)} %shard_map.178.refs_6_), channel_id=1, source_target_pairs={{0,2},{1,3},{2,0},{3,1},{4,6},{5,7},{6,4},{7,5},{8,10},{9,11},{10,... | collective-permute-start | bytes 1671176 | tf_op jit(solution)/shard_map/ppermute | solution.py:457
  17.0 23.7 %collective-permute-start.9 = (bf16[544,512]{1,0:T(8,128)(2,1)S(1)}, bf16[544,512]{1,0:T(8,128)(2,1)S(1)}, u32[]{:S(2)}, u32[]{:S(2)}) collective-permute-start(bf16[544,512]{1,0:T(8,128)(2,1)S(1)} %shard_map.179.refs_0_.refs_10_.refs_4_.refs_3_), channel_id=1, source_target_pairs={{0,2},{1,3},{2,0},{3,1},{4,6},{5,7},{6,4},{7,5},{8,10},{9,11},{10,... | collective-permute-start | bytes 1671176 | tf_op jit(solution)/shard_map/ppermute | solution.py:457
  18.4 18.4 %collective-permute-start.4 = (bf16[384,512]{1,0:T(8,128)(2,1)S(1)}, bf16[384,512]{1,0:T(8,128)(2,1)S(1)}, u32[]{:S(2)}, u32[]{:S(2)}) collective-permute-start(bf16[384,512]{1,0:T(8,128)(2,1)S(1)} %collective-permute-done.2.refs_3_), channel_id=1, source_target_pairs={{4,0},{8,12},{5,1},{9,13},{6,2},{10,14},{7,3},{11,15},{20,16},{24,... | collective-permute-start | bytes 1179656 | tf_op jit(solution)/shard_map/ppermute | solution.py:453
  21.9 16.2 %collective-permute-start.11 = (bf16[256,512]{1,0:T(8,128)(2,1)S(1)}, bf16[256,512]{1,0:T(8,128)(2,1)S(1)}, u32[]{:S(2)}, u32[]{:S(2)}) collective-permute-start(bf16[256,512]{1,0:T(8,128)(2,1)S(1)} %get-tuple-element.59), channel_id=1, source_target_pairs={{0,4},{4,8},{1,5},{5,9},{2,6},{6,10},{3,7},{7,11},{16,20},{20,24},... | collective-permute-start | bytes 786440 | tf_op jit(solution)/shard_map/ppermute | solution.py:453
  30.3 10.4 %collective-permute-start.12 = (bf16[256,512]{1,0:T(8,128)(2,1)S(1)}, bf16[256,512]{1,0:T(8,128)(2,1)S(1)}, u32[]{:S(2)}, u32[]{:S(2)}) collective-permute-start(bf16[256,512]{1,0:T(8,128)(2,1)S(1)} %get-tuple-element.61), channel_id=1, source_target_pairs={{8,4},{12,8},{9,5},{13,9},{10,6},{14,10},{11,7},{15,11},{24,20},{2... | collective-permute-start | bytes 786440 | tf_op jit(solution)/shard_map/ppermute | solution.py:453
  31.0 10.6 %collective-permute-start.13 = (bf16[256,512]{1,0:T(8,128)(2,1)S(1)}, bf16[256,512]{1,0:T(8,128)(2,1)S(1)}, u32[]{:S(2)}, u32[]{:S(2)}) collective-permute-start(bf16[256,512]{1,0:T(8,128)(2,1)S(1)} %get-tuple-element.63), channel_id=1, source_target_pairs={{0,8},{12,4},{1,9},{13,5},{2,10},{14,6},{3,11},{15,7},{16,24},{28,... | collective-permute-start | bytes 786440 | tf_op jit(solution)/shard_map/ppermute | solution.py:453
  36.8 11.8 %collective-permute-start.3 = (bf16[384,512]{1,0:T(8,128)(2,1)S(1)}, bf16[384,512]{1,0:T(8,128)(2,1)S(1)}, u32[]{:S(2)}, u32[]{:S(2)}) collective-permute-start(bf16[384,512]{1,0:T(8,128)(2,1)S(1)} %shard_map.177), channel_id=1, source_target_pairs={{4,0},{8,12},{5,1},{9,13},{6,2},{10,14},{7,3},{11,15},{20,16},{24,... | collective-permute-start | bytes 1179656 | tf_op jit(solution)/shard_map/ppermute | solution.py:453
  38.1 10.5 %collective-permute-start.8 = (bf16[544,512]{1,0:T(8,128)(2,1)S(1)}, bf16[544,512]{1,0:T(8,128)(2,1)S(1)}, u32[]{:S(2)}, u32[]{:S(2)}) collective-permute-start(bf16[544,512]{1,0:T(8,128)(2,1)S(1)} %shard_map.179.refs_0_.refs_10_.refs_4_.refs_3_), channel_id=1, source_target_pairs={{0,1},{1,0},{2,3},{3,2},{4,5},{5,4},{6,7},{7,6},{8,9},{9,8},{10,11... | collective-permute-start | bytes 1671176 | tf_op jit(solution)/shard_map/ppermute | solution.py:457
  40.7 8.0 %collective-permute-start.7 = (bf16[544,512]{1,0:T(8,128)(2,1)S(1)}, bf16[544,512]{1,0:T(8,128)(2,1)S(1)}, u32[]{:S(2)}, u32[]{:S(2)}) collective-permute-start(bf16[544,512]{1,0:T(8,128)(2,1)S(1)} %collective-permute-done.6.refs_8_), channel_id=1, source_target_pairs={{0,1},{1,0},{2,3},{3,2},{4,5},{5,4},{6,7},{7,6},{8,9},{9,8},{10,11... | collective-permute-start | bytes 1671176 | tf_op jit(solution)/shard_map/ppermute | solution.py:457
  40.7 8.0 %collective-permute-start.10 = (bf16[544,512]{1,0:T(8,128)(2,1)S(1)}, bf16[544,512]{1,0:T(8,128)(2,1)S(1)}, u32[]{:S(2)}, u32[]{:S(2)}) collective-permute-start(bf16[544,512]{1,0:T(8,128)(2,1)S(1)} %collective-permute-done.9.refs_12_.refs_6_.refs_5_), channel_id=1, source_target_pairs={{0,1},{1,0},{2,3},{3,2},{4,5},{5,4},{6,7},{7,6},{8,9},{9,8},{10,11... | collective-permute-start | bytes 1671176 | tf_op jit(solution)/shard_map/ppermute | solution.py:457
  41.7 15.6 %collective-permute-start.18 = (bf16[768,512]{1,0:T(8,128)(2,1)S(1)}, bf16[768,512]{1,0:T(8,128)(2,1)S(1)}, u32[]{:S(2)}, u32[]{:S(2)}) collective-permute-start(bf16[768,512]{1,0:T(8,128)(2,1)S(1)} %constant_dynamic-update-slice_fusion.refs_14_.refs_8_), channel_id=1, source_target_pairs={{4,6},{5,7},{6,4},{7,5},{8,10},{9,11},{10,8},{11,9},{20,22},{21,23... | collective-permute-start | bytes 2359304 | tf_op jit(solution)/shard_map/ppermute | solution.py:457
  50.4 11.4 %collective-permute-start.14 = (bf16[384,512]{1,0:T(8,128)(2,1)S(1)}, bf16[384,512]{1,0:T(8,128)(2,1)S(1)}, u32[]{:S(2)}, u32[]{:S(2)}) collective-permute-start(bf16[384,512]{1,0:T(8,128)(2,1)S(1)} %get-tuple-element.66.refs_0_.refs_2_.refs_4_), channel_id=1, source_target_pairs={{0,8},{12,4},{1,9},{13,5},{2,10},{14,6},{3,11},{15,7},{16,24},{28,... | collective-permute-start | bytes 1179656 | tf_op jit(solution)/shard_map/ppermute | solution.py:453
  52.3 10.2 %collective-permute-start.16 = (bf16[384,512]{1,0:T(8,128)(2,1)S(1)}, bf16[384,512]{1,0:T(8,128)(2,1)S(1)}, u32[]{:S(2)}, u32[]{:S(2)}) collective-permute-start(bf16[384,512]{1,0:T(8,128)(2,1)S(1)} %get-tuple-element.66.refs_0_.refs_2_.refs_4_), channel_id=1, source_target_pairs={{4,8},{8,4},{5,9},{9,5},{6,10},{10,6},{7,11},{11,7},{20,24},{24,20... | collective-permute-start | bytes 1179656 | tf_op jit(solution)/shard_map/ppermute | solution.py:453
  53.0 16.5 %collective-permute-start.15 = (bf16[384,512]{1,0:T(8,128)(2,1)S(1)}, bf16[384,512]{1,0:T(8,128)(2,1)S(1)}, u32[]{:S(2)}, u32[]{:S(2)}) collective-permute-start(bf16[384,512]{1,0:T(8,128)(2,1)S(1)} %get-tuple-element.66.refs_0_.refs_2_.refs_4_), channel_id=1, source_target_pairs={{0,4},{12,8},{1,5},{13,9},{2,6},{14,10},{3,7},{15,11},{16,20},{28,... | collective-permute-start | bytes 1179656 | tf_op jit(solution)/shard_map/ppermute | solution.py:453
  56.6 13.5 %collective-permute-start.17 = (bf16[768,512]{1,0:T(8,128)(2,1)S(1)}, bf16[768,512]{1,0:T(8,128)(2,1)S(1)}, u32[]{:S(2)}, u32[]{:S(2)}) collective-permute-start(bf16[768,512]{1,0:T(8,128)(2,1)S(1)} %constant_dynamic-update-slice_fusion.refs_14_.refs_8_), channel_id=1, source_target_pairs={{4,5},{5,4},{6,7},{7,6},{8,9},{9,8},{10,11},{11,10},{20,21},{21,20... | collective-permute-start | bytes 2359304 | tf_op jit(solution)/shard_map/ppermute | solution.py:457
  61.8 8.3 %collective-permute-start.19 = (bf16[768,512]{1,0:T(8,128)(2,1)S(1)}, bf16[768,512]{1,0:T(8,128)(2,1)S(1)}, u32[]{:S(2)}, u32[]{:S(2)}) collective-permute-start(bf16[768,512]{1,0:T(8,128)(2,1)S(1)} %collective-permute-done.18.refs_4_.refs_10_), channel_id=1, source_target_pairs={{4,5},{5,4},{6,7},{7,6},{8,9},{9,8},{10,11},{11,10},{20,21},{21,20... | collective-permute-start | bytes 2359304 | tf_op jit(solution)/shard_map/ppermute | solution.py:457
  72.5 23.4 %collective-permute-start.22 = (bf16[384,1024]{1,0:T(8,128)(2,1)S(1)}, bf16[384,1024]{1,0:T(8,128)(2,1)S(1)}, u32[]{:S(2)}, u32[]{:S(2)}) collective-permute-start(bf16[384,1024]{1,0:T(8,128)(2,1)S(1)} %shard_map.184.refs_0_), channel_id=1, source_target_pairs={{4,0},{8,12},{5,1},{9,13},{6,2},{10,14},{7,3},{11,15},{20,16},{24,... | collective-permute-start | bytes 2359304 | tf_op jit(solution)/shard_map/ppermute | solution.py:453
  73.8 22.1 %collective-permute-start.20 = (bf16[384,1024]{1,0:T(8,128)(2,1)S(1)}, bf16[384,1024]{1,0:T(8,128)(2,1)S(1)}, u32[]{:S(2)}, u32[]{:S(2)}) collective-permute-start(bf16[384,1024]{1,0:T(8,128)(2,1)S(1)} %shard_map.184.refs_0_), channel_id=1, source_target_pairs={{4,8},{8,4},{5,9},{9,5},{6,10},{10,6},{7,11},{11,7},{20,24},{24,20... | collective-permute-start | bytes 2359304 | tf_op jit(solution)/shard_map/ppermute | solution.py:453
  74.5 41.4 %collective-permute-start.21 = (bf16[384,1024]{1,0:T(8,128)(2,1)S(1)}, bf16[384,1024]{1,0:T(8,128)(2,1)S(1)}, u32[]{:S(2)}, u32[]{:S(2)}) collective-permute-start(bf16[384,1024]{1,0:T(8,128)(2,1)S(1)} %shard_map.184.refs_0_), channel_id=1, source_target_pairs={{8,0},{4,12},{9,1},{5,13},{10,2},{6,14},{11,3},{7,15},{24,16},{20,... | collective-permute-start | bytes 2359304 | tf_op jit(solution)/shard_map/ppermute | solution.py:453
  97.7 2.0 %collective-permute-start.23 = (f32[264,512]{1,0:T(8,128)S(1)}, f32[264,512]{1,0:T(8,128)S(1)}, u32[]{:S(2)}, u32[]{:S(2)}) collective-permute-start(f32[264,512]{1,0:T(8,128)S(1)} %get-tuple-element.71), channel_id=1, source_target_pairs={{0,1},{1,0},{2,3},{3,2},{4,5},{5,4},{6,7},{7,6},{8,9},{9,8},{10,11... | collective-permute-start | bytes 1622024 | tf_op jit(solution)/shard_map/ppermute | solution.py:457
  97.8 18.2 %collective-permute-start.24 = (f32[256,512]{1,0:T(8,128)S(1)}, f32[256,512]{1,0:T(8,128)S(1)}, u32[]{:S(2)}, u32[]{:S(2)}) collective-permute-start(f32[256,512]{1,0:T(8,128)S(1)} %get-tuple-element.73), channel_id=1, source_target_pairs={{0,1},{1,0},{2,3},{3,2},{4,5},{5,4},{6,7},{7,6},{8,9},{9,8},{10,11... | collective-permute-start | bytes 1572872 | tf_op jit(solution)/shard_map/ppermute | solution.py:457
  100.4 16.8 %collective-permute-start.25 = (f16[272,512]{1,0:T(8,128)(2,1)S(1)}, f16[272,512]{1,0:T(8,128)(2,1)S(1)}, u32[]{:S(2)}, u32[]{:S(2)}) collective-permute-start(f16[272,512]{1,0:T(8,128)(2,1)S(1)} %convert_element_type.25), channel_id=1, source_target_pairs={{0,2},{1,3},{2,0},{3,1},{4,6},{5,7},{6,4},{7,5},{8,10},{9,11},{10,... | collective-permute-start | bytes 835592 | tf_op jit(solution)/shard_map/ppermute | solution.py:457
  117.2 2.5 %collective-permute-start.26 = (f32[256,512]{1,0:T(8,128)S(1)}, f32[256,512]{1,0:T(8,128)S(1)}, u32[]{:S(2)}, u32[]{:S(2)}) collective-permute-start(f32[256,512]{1,0:T(8,128)S(1)} %get-tuple-element.82), channel_id=1, source_target_pairs={{0,1},{1,0},{2,3},{3,2},{4,5},{5,4},{6,7},{7,6},{8,9},{9,8},{10,11... | collective-permute-start | bytes 1572872 | tf_op jit(solution)/shard_map/ppermute | solution.py:457
  119.0 5.2 %collective-permute-start.27 = (f32[256,512]{1,0:T(8,128)S(1)}, f32[256,512]{1,0:T(8,128)S(1)}, u32[]{:S(2)}, u32[]{:S(2)}) collective-permute-start(f32[256,512]{1,0:T(8,128)S(1)} %get-tuple-element.85), channel_id=1, source_target_pairs={{0,1},{1,0},{2,3},{3,2},{4,5},{5,4},{6,7},{7,6},{8,9},{9,8},{10,11... | collective-permute-start | bytes 1572872 | tf_op jit(solution)/shard_map/ppermute | solution.py:457
  119.6 4.6 %collective-permute-start.28 = (f32[256,512]{1,0:T(8,128)S(1)}, f32[256,512]{1,0:T(8,128)S(1)}, u32[]{:S(2)}, u32[]{:S(2)}) collective-permute-start(f32[256,512]{1,0:T(8,128)S(1)} %get-tuple-element.86), channel_id=1, source_target_pairs={{0,1},{1,0},{2,3},{3,2},{4,5},{5,4},{6,7},{7,6},{8,9},{9,8},{10,11... | collective-permute-start | bytes 1572872 | tf_op jit(solution)/shard_map/ppermute | solution.py:457
  120.4 9.5 %collective-permute-start.31 = (f16[272,512]{1,0:T(8,128)(2,1)S(1)}, f16[272,512]{1,0:T(8,128)(2,1)S(1)}, u32[]{:S(2)}, u32[]{:S(2)}) collective-permute-start(f16[272,512]{1,0:T(8,128)(2,1)S(1)} %convert_element_type.28), channel_id=1, source_target_pairs={{0,2},{1,3},{2,0},{3,1},{4,6},{5,7},{6,4},{7,5},{8,10},{9,11},{10,... | collective-permute-start | bytes 835592 | tf_op jit(solution)/shard_map/ppermute | solution.py:457
  123.5 6.5 %collective-permute-start.33 = (f32[256,512]{1,0:T(8,128)S(1)}, f32[256,512]{1,0:T(8,128)S(1)}, u32[]{:S(2)}, u32[]{:S(2)}) collective-permute-start(f32[256,512]{1,0:T(8,128)S(1)} %get-tuple-element.97), channel_id=1, source_target_pairs={{0,1},{1,0},{2,3},{3,2},{4,5},{5,4},{6,7},{7,6},{8,9},{9,8},{10,11... | collective-permute-start | bytes 1572872 | tf_op jit(solution)/shard_map/ppermute | solution.py:457
  123.7 17.4 %collective-permute-start.29 = (f32[512,512]{1,0:T(8,128)S(1)}, f32[512,512]{1,0:T(8,128)S(1)}, u32[]{:S(2)}, u32[]{:S(2)}) collective-permute-start(f32[512,512]{1,0:T(8,128)S(1)} %get-tuple-element.90), channel_id=1, source_target_pairs={{0,1},{1,0},{2,3},{3,2},{4,5},{5,4},{6,7},{7,6},{8,9},{9,8},{10,11... | collective-permute-start | bytes 3145736 | tf_op jit(solution)/shard_map/ppermute | solution.py:457
  125.0 5.2 %copy-start.3 = (f32[512,512]{1,0:T(8,128)S(1)}, f32[512,512]{1,0:T(8,128)}, u32[]{:S(2)}) copy-start(f32[512,512]{1,0:T(8,128)} %moment) | copy-start | bytes 3145732
  125.0 5.2 %copy-start.4 = (f32[512,512]{1,0:T(8,128)S(1)}, f32[512,512]{1,0:T(8,128)}, u32[]{:S(2)}) copy-start(f32[512,512]{1,0:T(8,128)} %square) | copy-start | bytes 3145732
  125.2 15.9 %collective-permute-start.30 = (f16[528,512]{1,0:T(8,128)(2,1)S(1)}, f16[528,512]{1,0:T(8,128)(2,1)S(1)}, u32[]{:S(2)}, u32[]{:S(2)}) collective-permute-start(f16[528,512]{1,0:T(8,128)(2,1)S(1)} %convert_element_type.26), channel_id=1, source_target_pairs={{0,2},{1,3},{2,0},{3,1},{4,6},{5,7},{6,4},{7,5},{8,10},{9,11},{10,... | collective-permute-start | bytes 1622024 | tf_op jit(solution)/shard_map/ppermute | solution.py:457
  130.0 3.2 %collective-permute-start.32 = (f32[1,512]{1,0:T(1,128)S(1)}, f32[1,512]{1,0:T(1,128)S(1)}, u32[]{:S(2)}, u32[]{:S(2)}) collective-permute-start(f32[1,512]{1,0:T(1,128)S(1)} %get-tuple-element.112.refs_3_), channel_id=1, source_target_pairs={{0,1},{1,0},{2,3},{3,2},{4,5},{5,4},{6,7},{7,6},{8,9},{9,8},{10,11... | collective-permute-start | bytes 6152 | tf_op jit(solution)/shard_map/ppermute | solution.py:457
  130.2 3.0 %copy-start.8 = (f32[128]{0:T(128)S(1)}, f32[128]{0:T(128)}, u32[]{:S(2)}) copy-start(f32[128]{0:T(128)} %param.16) | copy-start | bytes 1540
  130.2 3.0 %copy-start.9 = (f32[128]{0:T(128)S(1)}, f32[128]{0:T(128)}, u32[]{:S(2)}) copy-start(f32[128]{0:T(128)} %param.17) | copy-start | bytes 1540
  130.2 10.9 %copy-start.10 = (f32[512,512]{1,0:T(8,128)S(1)}, f32[512,512]{1,0:T(8,128)}, u32[]{:S(2)}) copy-start(f32[512,512]{1,0:T(8,128)} %param.14) | copy-start | bytes 3145732
  130.2 10.9 %copy-start.11 = (f32[512,512]{1,0:T(8,128)S(1)}, f32[512,512]{1,0:T(8,128)}, u32[]{:S(2)}) copy-start(f32[512,512]{1,0:T(8,128)} %param.15) | copy-start | bytes 3145732
  133.2 7.9 %copy-start.1 = (f32[512,512]{1,0:T(8,128)S(1)}, f32[512,512]{1,0:T(8,128)}, u32[]{:S(2)}) copy-start(f32[512,512]{1,0:T(8,128)} %refs_0_.3) | copy-start | bytes 3145732
  133.2 1.3 copy-start.5

commit v21 on v20

--- a/solution.py
+++ b/solution.py
@@ -620,7 +620,7 @@
     decoder, dec_moment, dec_square, encoder, enc_moment, enc_square = lax.optimization_barrier(
         (decoder, dec_moment, dec_square, encoder, enc_moment, enc_square, enc_packed)
     )[:6]
-    near_block, active_there = unpack(near_received)
+    near_block, active_there = unpack(behind(near_received, enc_packed))
     far_block, bias_there = unpack(far_received)
     enc_block, _ = unpack(enc_received)
     near_grad = near_kept[0] + near_kept[1] + near_block

time: 144 us -> 156 us (1.083)
  waiting for transfers between devices: 67.1 us -> 85.1 us
  starting transfers between devices: 47.9 us -> 40.3 us
    ppermute x14, waiting for transfers between devices: 55.5 us -> 70.7 us  [along(): return lax.ppermute(value, 'latent', pairs)]
    ppermute x14, starting transfers between devices: 38 us -> 30.3 us  [along(): return lax.ppermute(value, 'latent', pairs)]
    ppermute x20, waiting for transfers between devices: 11.6 us -> 14.4 us  [flip(): return lax.ppermute(value, ('latent', 'dp'), pairs)]
  transfers between devices with their start and end apart: 34 -> 34, of which waited for: 12 -> 11; matrix products, arithmetic and copies ran while one was open for 0% -> 0% of each run, Pallas kernels for 13% -> 12%
where the time goes in v21:
time: 156 us; the launch traced here: 155 us
  waiting for transfers between devices  85.1 us (55%)
  starting transfers between devices  40.3 us (26%)
  Pallas kernels  21.6 us (14%)
  local copies, waits for them, and re-layouts  3.85 us (2%)
  other arithmetic  2.9 us (2%)
    ppermute x14, waiting for transfers between devices, along(): return lax.ppermute(value, 'latent', pairs)  70.7 us
    ppermute x14, starting transfers between devices, along(): return lax.ppermute(value, 'latent', pairs)  30.3 us
    pallas_call x16, Pallas kernels, local_kernel(): pl.pallas_call(run, out_shape=outs, in_specs=[SMEM] + [VMEM] * len(args)...  18.7 us
    ppermute x20, waiting for transfers between devices, flip(): return lax.ppermute(value, ('latent', 'dp'), pairs)  14.4 us
    ppermute x20, starting transfers between devices, flip(): return lax.ppermute(value, ('latent', 'dp'), pairs)  9.98 us
    unnamed x26, local copies, waits for them, and re-layouts  3.84 us
  transfers between devices with their start and end apart: 34, of which 11 were waited for; matrix products, arithmetic and copies ran while one was open for 0% of the time, Pallas kernels for 12%

profile of v21, /device:TPU:0, one launch (start us, length us, event | category | flops | bytes accessed | tf_op | source)
XLA Modules:
  0.0 155.0 jit_solution(14206820295529921352)
XLA Ops:
  0.7 1.2 copy-done
  3.1 5.8 %collective-permute-start.2 = (bf16[384,512]{1,0:T(8,128)(2,1)S(1)}, bf16[384,512]{1,0:T(8,128)(2,1)S(1)}, u32[]{:S(2)}, u32[]{:S(2)}) collective-permute-start(bf16[384,512]{1,0:T(8,128)(2,1)S(1)} %copy-done.6), channel_id=1, source_target_pairs={{0,8},{12,4},{1,9},{13,5},{2,10},{14,6},{3,11},{15,7},{16,24},{28,... | collective-permute-start | bytes 1179656 | tf_op jit(solution)/shard_map/ppermute | solution.py:453
  8.9 1.3 collective-permute-start
  10.2 1.3 collective-permute-start.1
  11.5 1.6 %collective-permute-start.6 = (bf16[544,512]{1,0:T(8,128)(2,1)S(1)}, bf16[544,512]{1,0:T(8,128)(2,1)S(1)}, u32[]{:S(2)}, u32[]{:S(2)}) collective-permute-start(bf16[544,512]{1,0:T(8,128)(2,1)S(1)} %shard_map.178.refs_6_), channel_id=1, source_target_pairs={{0,2},{1,3},{2,0},{3,1},{4,6},{5,7},{6,4},{7,5},{8,10},{9,11},{10,... | collective-permute-start | bytes 1671176 | tf_op jit(solution)/shard_map/ppermute | solution.py:457
  13.1 0.6 shard_map.179.refs_0_.refs_10_.refs_4_.refs_3_
  13.8 0.6 collective-permute-start.9
  14.4 4.0 %collective-permute-done.2.refs_3_ = bf16[384,512]{1,0:T(8,128)(2,1)S(1)} collective-permute-done((bf16[384,512]{1,0:T(8,128)(2,1)S(1)}, bf16[384,512]{1,0:T(8,128)(2,1)S(1)}, u32[]{:S(2)}, u32[]{:S(2)}) %collective-permute-start.2) | collective-permute-done | bytes 393248 | tf_op jit(solution)/shard_map/ppermute | solution.py:453
  18.4 1.3 collective-permute-start.4
  19.7 0.6 shard_map.180
  20.3 5.8 %collective-permute-done.refs_0_.refs_1_ = bf16[384,512]{1,0:T(8,128)(2,1)S(1)} collective-permute-done((bf16[384,512]{1,0:T(8,128)(2,1)S(1)}, bf16[384,512]{1,0:T(8,128)(2,1)S(1)}, u32[]{:S(2)}, u32[]{:S(2)}) %collective-permute-start) | collective-permute-done | bytes 393248 | tf_op jit(solution)/shard_map/ppermute | solution.py:453
  26.1 4.4 %collective-permute-start.11 = (bf16[256,512]{1,0:T(8,128)(2,1)S(1)}, bf16[256,512]{1,0:T(8,128)(2,1)S(1)}, u32[]{:S(2)}, u32[]{:S(2)}) collective-permute-start(bf16[256,512]{1,0:T(8,128)(2,1)S(1)} %get-tuple-element.60), channel_id=1, source_target_pairs={{0,4},{4,8},{1,5},{5,9},{2,6},{6,10},{3,7},{7,11},{16,20},{20,24},... | collective-permute-start | bytes 786440 | tf_op jit(solution)/shard_map/ppermute | solution.py:453
  30.5 0.7 collective-permute-start.12
  31.2 6.0 %collective-permute-start.13 = (bf16[256,512]{1,0:T(8,128)(2,1)S(1)}, bf16[256,512]{1,0:T(8,128)(2,1)S(1)}, u32[]{:S(2)}, u32[]{:S(2)}) collective-permute-start(bf16[256,512]{1,0:T(8,128)(2,1)S(1)} %get-tuple-element.64), channel_id=1, source_target_pairs={{0,8},{12,4},{1,9},{13,5},{2,10},{14,6},{3,11},{15,7},{16,24},{28,... | collective-permute-start | bytes 786440 | tf_op jit(solution)/shard_map/ppermute | solution.py:453
  37.8 1.3 collective-permute-start.3
  39.8 2.5 %collective-permute-done.13 = bf16[256,512]{1,0:T(8,128)(2,1)S(1)} collective-permute-done((bf16[256,512]{1,0:T(8,128)(2,1)S(1)}, bf16[256,512]{1,0:T(8,128)(2,1)S(1)}, u32[]{:S(2)}, u32[]{:S(2)}) %collective-permute-start.13) | collective-permute-done | bytes 262176 | tf_op jit(solution)/shard_map/ppermute | solution.py:453
  42.4 0.7 collective-permute-start.18
  43.1 6.8 %collective-permute-done.3.refs_4_ = bf16[384,512]{1,0:T(8,128)(2,1)S(1)} collective-permute-done((bf16[384,512]{1,0:T(8,128)(2,1)S(1)}, bf16[384,512]{1,0:T(8,128)(2,1)S(1)}, u32[]{:S(2)}, u32[]{:S(2)}) %collective-permute-start.3) | collective-permute-done | bytes 393248 | tf_op jit(solution)/shard_map/ppermute | solution.py:453
  49.9 1.8 %shard_map.181 = (bf16[384,512]{1,0:T(8,128)(2,1)S(1)}, bf16[384,512]{1,0:T(8,128)(2,1)S(1)}, bf16[384,2048]{1,0:T(8,128)(2,1)S(1)}, f32[1,512]{1,0:T(1,128)S(1)}) custom-call(s32[2]{0:T(128)S(1)} %pad_add_fusion.place, bf16[384,512]{1,0:T(8,128)(2,1)S(1)} %copy-done.6, bf16[384,512]{1,0:T(8,128)(2,1)S(1)} %collective-permute-done.refs_0_.refs_1_, ...), custom_call_target="tpu_custom_call" | custom-call | flops 1 | bytes 1 | tf_op jit(solution)/shard_map/pallas_call | solution.py:121
  51.7 1.9 %collective-permute-start.14 = (bf16[384,512]{1,0:T(8,128)(2,1)S(1)}, bf16[384,512]{1,0:T(8,128)(2,1)S(1)}, u32[]{:S(2)}, u32[]{:S(2)}) collective-permute-start(bf16[384,512]{1,0:T(8,128)(2,1)S(1)} %get-tuple-element.67.refs_0_.refs_2_.refs_4_), channel_id=1, source_target_pairs={{0,8},{12,4},{1,9},{13,5},{2,10},{14,6},{3,11},{15,7},{16,24},{28,... | collective-permute-start | bytes 1179656 | tf_op jit(solution)/shard_map/ppermute | solution.py:453
  53.6 2.3 %collective-permute-start.15 = (bf16[384,512]{1,0:T(8,128)(2,1)S(1)}, bf16[384,512]{1,0:T(8,128)(2,1)S(1)}, u32[]{:S(2)}, u32[]{:S(2)}) collective-permute-start(bf16[384,512]{1,0:T(8,128)(2,1)S(1)} %get-tuple-element.67.refs_0_.refs_2_.refs_4_), channel_id=1, source_target_pairs={{0,4},{12,8},{1,5},{13,9},{2,6},{14,10},{3,7},{15,11},{16,20},{28,... | collective-permute-start | bytes 1179656 | tf_op jit(solution)/shard_map/ppermute | solution.py:453
  55.9 0.7 collective-permute-start.16
  56.6 0.7 collective-permute-start.17
  57.4 5.7 %collective-permute-done.14.refs_1_.refs_2_ = bf16[384,512]{1,0:T(8,128)(2,1)S(1)} collective-permute-done((bf16[384,512]{1,0:T(8,128)(2,1)S(1)}, bf16[384,512]{1,0:T(8,128)(2,1)S(1)}, u32[]{:S(2)}, u32[]{:S(2)}) %collective-permute-start.14) | collective-permute-done | bytes 393248 | tf_op jit(solution)/shard_map/ppermute | solution.py:453
  63.1 0.7 collective-permute-start.19
  63.8 7.0 %collective-permute-done.15.refs_1_ = bf16[384,512]{1,0:T(8,128)(2,1)S(1)} collective-permute-done((bf16[384,512]{1,0:T(8,128)(2,1)S(1)}, bf16[384,512]{1,0:T(8,128)(2,1)S(1)}, u32[]{:S(2)}, u32[]{:S(2)}) %collective-permute-start.15) | collective-permute-done | bytes 393248 | tf_op jit(solution)/shard_map/ppermute | solution.py:453
  71.4 2.4 %shard_map.184.refs_0_ = bf16[384,1024]{1,0:T(8,128)(2,1)S(1)} custom-call(s32[2]{0:T(128)S(1)} %pad_add_fusion.place, bf16[384,512]{1,0:T(8,128)(2,1)S(1)} %get-tuple-element.67.refs_0_.refs_2_.refs_4_, bf16[384,512]{1,0:T(8,128)(2,1)S(1)} %collective-permute-done.15.refs_1_, bf16[384,512]{1,0:T(8,128)(2,1)S(1)} %collective-permute-done.14.refs_1_.refs_2_, ...), custom_call_target="tpu_custom_call" | custom-call | flops 1 | bytes 1 | tf_op jit(solution)/shard_map/pallas_call | solution.py:121
  73.8 0.7 collective-permute-start.20
  74.5 1.3 collective-permute-start.22
  75.8 1.3 collective-permute-start.21
  77.2 38.8 %collective-permute-done.22.refs_1_ = bf16[384,1024]{1,0:T(8,128)(2,1)S(1)} collective-permute-done((bf16[384,1024]{1,0:T(8,128)(2,1)S(1)}, bf16[384,1024]{1,0:T(8,128)(2,1)S(1)}, u32[]{:S(2)}, u32[]{:S(2)}) %collective-permute-start.22) | collective-permute-done | bytes 786464 | tf_op jit(solution)/shard_map/ppermute | solution.py:453
  116.0 1.8 %shard_map.185 = (f32[384,512]{1,0:T(8,128)S(1)}, bf16[384,1024]{1,0:T(8,128)(2,1)S(1)}, f32[264,512]{1,0:T(8,128)S(1)}, f32[256,512]{1,0:T(8,128)S(1)}, f32[256,512]{1,0:T(8,128)S(1)}, /*index=5*/f32[256,512]{1,0:T(8,128)S(1)}) custom-call(s32[2]{0:T(128)S(1)} %pad_add_fusion.place, bf16[384,1024]{1,0:T(8,128)(2,1)S(1)} %shard_map.184.refs_0_, ...), custom_call_target="tpu_custom_call" | custom-call | flops 1 | bytes 1 | tf_op jit(solution)/shard_map/pallas_call | solution.py:121
  118.3 1.0 shard_map.182.refs_7_.refs_0_
  119.7 0.7 shard_map.186
  121.1 1.3 shard_map.187
  122.4 6.8 %collective-permute-done.25 = f16[272,512]{1,0:T(8,128)(2,1)S(1)} collective-permute-done((f16[272,512]{1,0:T(8,128)(2,1)S(1)}, f16[272,512]{1,0:T(8,128)(2,1)S(1)}, u32[]{:S(2)}, u32[]{:S(2)}) %collective-permute-start.25) | collective-permute-done | bytes 278560 | tf_op jit(solution)/shard_map/ppermute | solution.py:457
  129.2 1.7 %shard_map.188 = (bf16[384,512]{1,0:T(8,128)(2,1)S(1)}, f32[1,512]{1,0:T(1,128)S(1)}, f32[1,512]{1,0:T(1,128)S(1)}, f32[256,512]{1,0:T(8,128)S(1)}, f32[256,512]{1,0:T(8,128)S(1)}) custom-call(s32[2]{0:T(128)S(1)} %pad_add_fusion.place, bf16[384,1024]{1,0:T(8,128)(2,1)S(1)} %get-tuple-element.75.refs_0_.refs_3_, f32[384,512]{1,0:T(8,128)S(1)} %get-tuple-element.77.refs_1_, ...), custom_call_target="tpu_custom_call" | custom-call | flops 10000000000 | bytes 1 | tf_op jit(solution)/shard_map/pallas_call | solution.py:121
  131.5 0.7 shard_map.189.refs_5_
  132.9 2.5 %shard_map.190 = (bf16[384,512]{1,0:T(8,128)(2,1)}, f32[512,512]{1,0:T(8,128)S(1)}, f32[512,512]{1,0:T(8,128)S(1)}, f32[512,512]{1,0:T(8,128)S(1)}, f32[256,512]{1,0:T(8,128)S(1)}, /*index=5*/f32[256,512]{1,0:T(8,128)S(1)}) custom-call(s32[2]{0:T(128)S(1)} %pad_add_fusion.place, bf16[2048,384]{1,0:T(8,128)(2,1)S(1)} %shard_map.182.refs_7_.refs_0_, ...), custom_call_target="tpu_custom_call" | custom-call | flops 1 | bytes 1 | tf_op jit(solution)/shard_map/pallas_call | solution.py:121
  135.9 0.8 shard_map.191
  136.8 1.6 %collective-permute-start.30 = (f16[528,512]{1,0:T(8,128)(2,1)S(1)}, f16[528,512]{1,0:T(8,128)(2,1)S(1)}, u32[]{:S(2)}, u32[]{:S(2)}) collective-permute-start(f16[528,512]{1,0:T(8,128)(2,1)S(1)} %convert_element_type.26), channel_id=1, source_target_pairs={{0,2},{1,3},{2,0},{3,1},{4,6},{5,7},{6,4},{7,5},{8,10},{9,11},{10,... | collective-permute-start | bytes 1622024 | tf_op jit(solution)/shard_map/ppermute | solution.py:457
  138.4 3.5 %collective-permute-done.31 = f16[272,512]{1,0:T(8,128)(2,1)S(1)} collective-permute-done((f16[272,512]{1,0:T(8,128)(2,1)S(1)}, f16[272,512]{1,0:T(8,128)(2,1)S(1)}, u32[]{:S(2)}, u32[]{:S(2)}) %collective-permute-start.31) | collective-permute-done | bytes 278560 | tf_op jit(solution)/shard_map/ppermute | solution.py:457
  142.4 0.9 copy-done.3
  143.6 3.0 %shard_map.192 = (f32[512,512]{1,0:T(8,128)}, f32[512,512]{1,0:T(8,128)}, f32[512,512]{1,0:T(8,128)}) custom-call(s32[2]{0:T(128)S(1)} %pad_add_fusion.place, f32[512,512]{1,0:T(8,128)S(1)} %copy-done.2, f32[512,512]{1,0:T(8,128)S(1)} %copy-done.3, f32[512,512]{1,0:T(8,128)S(1)} %copy-done.4, f32[256,512]{1,0:T(8,128)S(1)} %multiply_add_fusion.3.near, ...), custom_call_target="tpu_custom_call" | custom-call | flops 1 | bytes 1 | tf_op jit(solution)/shard_map/pallas_call | solution.py:637
  146.6 1.3 copy-done.5
  147.9 1.1 shard_map.193
  149.0 3.6 %collective-permute-done.30 = f16[528,512]{1,0:T(8,128)(2,1)S(1)} collective-permute-done((f16[528,512]{1,0:T(8,128)(2,1)S(1)}, f16[528,512]{1,0:T(8,128)(2,1)S(1)}, u32[]{:S(2)}, u32[]{:S(2)}) %collective-permute-start.30) | collective-permute-done | bytes 540704 | tf_op jit(solution)/shard_map/ppermute | solution.py:457
  152.7 2.3 %divide_subtract_fusion = (f32[512,512]{1,0:T(8,128)}, f32[512,512]{1,0:T(8,128)}, f32[512,512]{1,0:T(8,128)}) fusion(f32[512,512]{1,0:T(8,128)S(1)} %copy-done.1, f32[512]{0:T(512)S(1)} %bitcast.15, f16[528,512]{1,0:T(8,128)(2,1)S(1)} %collective-permute-done.30, f32[512,512]{1,0:T(8,128)S(1)} %get-tuple-element.90, ...), kind=kLoop, calls=%fused_computation.2 | loop fusion | flops 4194304 | bytes 8914944 | tf_op jit(solution)/shard_map/sub | solution.py:28
  (76 shorter events, 7.3 us)
Async XLA Ops:
  0.6 12.5 %copy-start.7 = (f32[128]{0:T(128)S(1)}, f32[128]{0:T(128)}, u32[]{:S(2)}) copy-start(f32[128]{0:T(128)} %param.12) | copy-start | bytes 1540
  0.7 1.2 copy-start
  2.0 1.1 copy-start.6
  2.0 11.1 %copy-start.2 = (f32[512,512]{1,0:T(8,128)S(1)}, f32[512,512]{1,0:T(8,128)}, u32[]{:S(2)}) copy-start(f32[512,512]{1,0:T(8,128)} %param.20) | copy-start | bytes 3145732
  2.6 10.5 %collective-permute-start.5 = (bf16[544,512]{1,0:T(8,128)(2,1)S(1)}, bf16[544,512]{1,0:T(8,128)(2,1)S(1)}, u32[]{:S(2)}, u32[]{:S(2)}) collective-permute-start(bf16[544,512]{1,0:T(8,128)(2,1)S(1)} %shard_map.178.refs_6_), channel_id=1, source_target_pairs={{0,1},{1,0},{2,3},{3,2},{4,5},{5,4},{6,7},{7,6},{8,9},{9,8},{10,11... | collective-permute-start | bytes 1671176 | tf_op jit(solution)/shard_map/ppermute | solution.py:457
  3.1 15.3 %collective-permute-start.2 = (bf16[384,512]{1,0:T(8,128)(2,1)S(1)}, bf16[384,512]{1,0:T(8,128)(2,1)S(1)}, u32[]{:S(2)}, u32[]{:S(2)}) collective-permute-start(bf16[384,512]{1,0:T(8,128)(2,1)S(1)} %copy-done.6), channel_id=1, source_target_pairs={{0,8},{12,4},{1,9},{13,5},{2,10},{14,6},{3,11},{15,7},{16,24},{28,... | collective-permute-start | bytes 1179656 | tf_op jit(solution)/shard_map/ppermute | solution.py:453
  8.9 17.2 %collective-permute-start = (bf16[384,512]{1,0:T(8,128)(2,1)S(1)}, bf16[384,512]{1,0:T(8,128)(2,1)S(1)}, u32[]{:S(2)}, u32[]{:S(2)}) collective-permute-start(bf16[384,512]{1,0:T(8,128)(2,1)S(1)} %copy-done.6), channel_id=1, source_target_pairs={{0,4},{4,8},{8,12},{1,5},{5,9},{9,13},{2,6},{6,10},{10,14},{3,7},{... | collective-permute-start | bytes 1179656 | tf_op jit(solution)/shard_map/ppermute | solution.py:453
  10.2 20.2 %collective-permute-start.1 = (bf16[384,512]{1,0:T(8,128)(2,1)S(1)}, bf16[384,512]{1,0:T(8,128)(2,1)S(1)}, u32[]{:S(2)}, u32[]{:S(2)}) collective-permute-start(bf16[384,512]{1,0:T(8,128)(2,1)S(1)} %copy-done.6), channel_id=1, source_target_pairs={{4,0},{8,4},{12,8},{5,1},{9,5},{13,9},{6,2},{10,6},{14,10},{7,3},{... | collective-permute-start | bytes 1179656 | tf_op jit(solution)/shard_map/ppermute | solution.py:453
  11.5 19.6 %collective-permute-start.6 = (bf16[544,512]{1,0:T(8,128)(2,1)S(1)}, bf16[544,512]{1,0:T(8,128)(2,1)S(1)}, u32[]{:S(2)}, u32[]{:S(2)}) collective-permute-start(bf16[544,512]{1,0:T(8,128)(2,1)S(1)} %shard_map.178.refs_6_), channel_id=1, source_target_pairs={{0,2},{1,3},{2,0},{3,1},{4,6},{5,7},{6,4},{7,5},{8,10},{9,11},{10,... | collective-permute-start | bytes 1671176 | tf_op jit(solution)/shard_map/ppermute | solution.py:457
  13.8 25.4 %collective-permute-start.9 = (bf16[544,512]{1,0:T(8,128)(2,1)S(1)}, bf16[544,512]{1,0:T(8,128)(2,1)S(1)}, u32[]{:S(2)}, u32[]{:S(2)}) collective-permute-start(bf16[544,512]{1,0:T(8,128)(2,1)S(1)} %shard_map.179.refs_0_.refs_10_.refs_4_.refs_3_), channel_id=1, source_target_pairs={{0,2},{1,3},{2,0},{3,1},{4,6},{5,7},{6,4},{7,5},{8,10},{9,11},{10,... | collective-permute-start | bytes 1671176 | tf_op jit(solution)/shard_map/ppermute | solution.py:457
  18.4 19.4 %collective-permute-start.4 = (bf16[384,512]{1,0:T(8,128)(2,1)S(1)}, bf16[384,512]{1,0:T(8,128)(2,1)S(1)}, u32[]{:S(2)}, u32[]{:S(2)}) collective-permute-start(bf16[384,512]{1,0:T(8,128)(2,1)S(1)} %collective-permute-done.2.refs_3_), channel_id=1, source_target_pairs={{4,0},{8,12},{5,1},{9,13},{6,2},{10,14},{7,3},{11,15},{20,16},{24,... | collective-permute-start | bytes 1179656 | tf_op jit(solution)/shard_map/ppermute | solution.py:453
  26.1 13.0 %collective-permute-start.11 = (bf16[256,512]{1,0:T(8,128)(2,1)S(1)}, bf16[256,512]{1,0:T(8,128)(2,1)S(1)}, u32[]{:S(2)}, u32[]{:S(2)}) collective-permute-start(bf16[256,512]{1,0:T(8,128)(2,1)S(1)} %get-tuple-element.60), channel_id=1, source_target_pairs={{0,4},{4,8},{1,5},{5,9},{2,6},{6,10},{3,7},{7,11},{16,20},{20,24},... | collective-permute-start | bytes 786440 | tf_op jit(solution)/shard_map/ppermute | solution.py:453
  30.5 9.2 %collective-permute-start.12 = (bf16[256,512]{1,0:T(8,128)(2,1)S(1)}, bf16[256,512]{1,0:T(8,128)(2,1)S(1)}, u32[]{:S(2)}, u32[]{:S(2)}) collective-permute-start(bf16[256,512]{1,0:T(8,128)(2,1)S(1)} %get-tuple-element.62), channel_id=1, source_target_pairs={{8,4},{12,8},{9,5},{13,9},{10,6},{14,10},{11,7},{15,11},{24,20},{2... | collective-permute-start | bytes 786440 | tf_op jit(solution)/shard_map/ppermute | solution.py:453
  31.2 11.2 %collective-permute-start.13 = (bf16[256,512]{1,0:T(8,128)(2,1)S(1)}, bf16[256,512]{1,0:T(8,128)(2,1)S(1)}, u32[]{:S(2)}, u32[]{:S(2)}) collective-permute-start(bf16[256,512]{1,0:T(8,128)(2,1)S(1)} %get-tuple-element.64), channel_id=1, source_target_pairs={{0,8},{12,4},{1,9},{13,5},{2,10},{14,6},{3,11},{15,7},{16,24},{28,... | collective-permute-start | bytes 786440 | tf_op jit(solution)/shard_map/ppermute | solution.py:453
  37.8 12.1 %collective-permute-start.3 = (bf16[384,512]{1,0:T(8,128)(2,1)S(1)}, bf16[384,512]{1,0:T(8,128)(2,1)S(1)}, u32[]{:S(2)}, u32[]{:S(2)}) collective-permute-start(bf16[384,512]{1,0:T(8,128)(2,1)S(1)} %shard_map.177), channel_id=1, source_target_pairs={{4,0},{8,12},{5,1},{9,13},{6,2},{10,14},{7,3},{11,15},{20,16},{24,... | collective-permute-start | bytes 1179656 | tf_op jit(solution)/shard_map/ppermute | solution.py:453
  39.1 10.8 %collective-permute-start.8 = (bf16[544,512]{1,0:T(8,128)(2,1)S(1)}, bf16[544,512]{1,0:T(8,128)(2,1)S(1)}, u32[]{:S(2)}, u32[]{:S(2)}) collective-permute-start(bf16[544,512]{1,0:T(8,128)(2,1)S(1)} %shard_map.179.refs_0_.refs_10_.refs_4_.refs_3_), channel_id=1, source_target_pairs={{0,1},{1,0},{2,3},{3,2},{4,5},{5,4},{6,7},{7,6},{8,9},{9,8},{10,11... | collective-permute-start | bytes 1671176 | tf_op jit(solution)/shard_map/ppermute | solution.py:457
  39.2 10.7 %collective-permute-start.7 = (bf16[544,512]{1,0:T(8,128)(2,1)S(1)}, bf16[544,512]{1,0:T(8,128)(2,1)S(1)}, u32[]{:S(2)}, u32[]{:S(2)}) collective-permute-start(bf16[544,512]{1,0:T(8,128)(2,1)S(1)} %collective-permute-done.6.refs_8_), channel_id=1, source_target_pairs={{0,1},{1,0},{2,3},{3,2},{4,5},{5,4},{6,7},{7,6},{8,9},{9,8},{10,11... | collective-permute-start | bytes 1671176 | tf_op jit(solution)/shard_map/ppermute | solution.py:457
  39.7 10.2 %collective-permute-start.10 = (bf16[544,512]{1,0:T(8,128)(2,1)S(1)}, bf16[544,512]{1,0:T(8,128)(2,1)S(1)}, u32[]{:S(2)}, u32[]{:S(2)}) collective-permute-start(bf16[544,512]{1,0:T(8,128)(2,1)S(1)} %collective-permute-done.9.refs_12_.refs_6_.refs_5_), channel_id=1, source_target_pairs={{0,1},{1,0},{2,3},{3,2},{4,5},{5,4},{6,7},{7,6},{8,9},{9,8},{10,11... | collective-permute-start | bytes 1671176 | tf_op jit(solution)/shard_map/ppermute | solution.py:457
  42.4 15.0 %collective-permute-start.18 = (bf16[768,512]{1,0:T(8,128)(2,1)S(1)}, bf16[768,512]{1,0:T(8,128)(2,1)S(1)}, u32[]{:S(2)}, u32[]{:S(2)}) collective-permute-start(bf16[768,512]{1,0:T(8,128)(2,1)S(1)} %constant_dynamic-update-slice_fusion.refs_14_.refs_8_), channel_id=1, source_target_pairs={{4,6},{5,7},{6,4},{7,5},{8,10},{9,11},{10,8},{11,9},{20,22},{21,23... | collective-permute-start | bytes 2359304 | tf_op jit(solution)/shard_map/ppermute | solution.py:457
  51.7 11.4 %collective-permute-start.14 = (bf16[384,512]{1,0:T(8,128)(2,1)S(1)}, bf16[384,512]{1,0:T(8,128)(2,1)S(1)}, u32[]{:S(2)}, u32[]{:S(2)}) collective-permute-start(bf16[384,512]{1,0:T(8,128)(2,1)S(1)} %get-tuple-element.67.refs_0_.refs_2_.refs_4_), channel_id=1, source_target_pairs={{0,8},{12,4},{1,9},{13,5},{2,10},{14,6},{3,11},{15,7},{16,24},{28,... | collective-permute-start | bytes 1179656 | tf_op jit(solution)/shard_map/ppermute | solution.py:453
  53.6 17.2 %collective-permute-start.15 = (bf16[384,512]{1,0:T(8,128)(2,1)S(1)}, bf16[384,512]{1,0:T(8,128)(2,1)S(1)}, u32[]{:S(2)}, u32[]{:S(2)}) collective-permute-start(bf16[384,512]{1,0:T(8,128)(2,1)S(1)} %get-tuple-element.67.refs_0_.refs_2_.refs_4_), channel_id=1, source_target_pairs={{0,4},{12,8},{1,5},{13,9},{2,6},{14,10},{3,7},{15,11},{16,20},{28,... | collective-permute-start | bytes 1179656 | tf_op jit(solution)/shard_map/ppermute | solution.py:453
  55.9 14.9 %collective-permute-start.16 = (bf16[384,512]{1,0:T(8,128)(2,1)S(1)}, bf16[384,512]{1,0:T(8,128)(2,1)S(1)}, u32[]{:S(2)}, u32[]{:S(2)}) collective-permute-start(bf16[384,512]{1,0:T(8,128)(2,1)S(1)} %get-tuple-element.67.refs_0_.refs_2_.refs_4_), channel_id=1, source_target_pairs={{4,8},{8,4},{5,9},{9,5},{6,10},{10,6},{7,11},{11,7},{20,24},{24,20... | collective-permute-start | bytes 1179656 | tf_op jit(solution)/shard_map/ppermute | solution.py:453
  56.6 14.7 %collective-permute-start.17 = (bf16[768,512]{1,0:T(8,128)(2,1)S(1)}, bf16[768,512]{1,0:T(8,128)(2,1)S(1)}, u32[]{:S(2)}, u32[]{:S(2)}) collective-permute-start(bf16[768,512]{1,0:T(8,128)(2,1)S(1)} %constant_dynamic-update-slice_fusion.refs_14_.refs_8_), channel_id=1, source_target_pairs={{4,5},{5,4},{6,7},{7,6},{8,9},{9,8},{10,11},{11,10},{20,21},{21,20... | collective-permute-start | bytes 2359304 | tf_op jit(solution)/shard_map/ppermute | solution.py:457
  63.1 8.3 %collective-permute-start.19 = (bf16[768,512]{1,0:T(8,128)(2,1)S(1)}, bf16[768,512]{1,0:T(8,128)(2,1)S(1)}, u32[]{:S(2)}, u32[]{:S(2)}) collective-permute-start(bf16[768,512]{1,0:T(8,128)(2,1)S(1)} %collective-permute-done.18.refs_4_.refs_10_), channel_id=1, source_target_pairs={{4,5},{5,4},{6,7},{7,6},{8,9},{9,8},{10,11},{11,10},{20,21},{21,20... | collective-permute-start | bytes 2359304 | tf_op jit(solution)/shard_map/ppermute | solution.py:457
  73.8 3.3 %collective-permute-start.20 = (bf16[384,1024]{1,0:T(8,128)(2,1)S(1)}, bf16[384,1024]{1,0:T(8,128)(2,1)S(1)}, u32[]{:S(2)}, u32[]{:S(2)}) collective-permute-start(bf16[384,1024]{1,0:T(8,128)(2,1)S(1)} %shard_map.184.refs_0_), channel_id=1, source_target_pairs={{4,8},{8,4},{5,9},{9,5},{6,10},{10,6},{7,11},{11,7},{20,24},{24,20... | collective-permute-start | bytes 2359304 | tf_op jit(solution)/shard_map/ppermute | solution.py:453
  74.5 41.4 %collective-permute-start.22 = (bf16[384,1024]{1,0:T(8,128)(2,1)S(1)}, bf16[384,1024]{1,0:T(8,128)(2,1)S(1)}, u32[]{:S(2)}, u32[]{:S(2)}) collective-permute-start(bf16[384,1024]{1,0:T(8,128)(2,1)S(1)} %shard_map.184.refs_0_), channel_id=1, source_target_pairs={{4,0},{8,12},{5,1},{9,13},{6,2},{10,14},{7,3},{11,15},{20,16},{24,... | collective-permute-start | bytes 2359304 | tf_op jit(solution)/shard_map/ppermute | solution.py:453
  75.8 45.2 %collective-permute-start.21 = (bf16[384,1024]{1,0:T(8,128)(2,1)S(1)}, bf16[384,1024]{1,0:T(8,128)(2,1)S(1)}, u32[]{:S(2)}, u32[]{:S(2)}) collective-permute-start(bf16[384,1024]{1,0:T(8,128)(2,1)S(1)} %shard_map.184.refs_0_), channel_id=1, source_target_pairs={{8,0},{4,12},{9,1},{5,13},{10,2},{6,14},{11,3},{7,15},{24,16},{20,... | collective-permute-start | bytes 2359304 | tf_op jit(solution)/shard_map/ppermute | solution.py:453
  117.7 2.0 %collective-permute-start.23 = (f32[264,512]{1,0:T(8,128)S(1)}, f32[264,512]{1,0:T(8,128)S(1)}, u32[]{:S(2)}, u32[]{:S(2)}) collective-permute-start(f32[264,512]{1,0:T(8,128)S(1)} %get-tuple-element.72), channel_id=1, source_target_pairs={{0,1},{1,0},{2,3},{3,2},{4,5},{5,4},{6,7},{7,6},{8,9},{9,8},{10,11... | collective-permute-start | bytes 1622024 | tf_op jit(solution)/shard_map/ppermute | solution.py:457
  117.8 3.3 %collective-permute-start.24 = (f32[256,512]{1,0:T(8,128)S(1)}, f32[256,512]{1,0:T(8,128)S(1)}, u32[]{:S(2)}, u32[]{:S(2)}) collective-permute-start(f32[256,512]{1,0:T(8,128)S(1)} %get-tuple-element.74), channel_id=1, source_target_pairs={{0,1},{1,0},{2,3},{3,2},{4,5},{5,4},{6,7},{7,6},{8,9},{9,8},{10,11... | collective-permute-start | bytes 1572872 | tf_op jit(solution)/shard_map/ppermute | solution.py:457
  120.5 8.8 %collective-permute-start.25 = (f16[272,512]{1,0:T(8,128)(2,1)S(1)}, f16[272,512]{1,0:T(8,128)(2,1)S(1)}, u32[]{:S(2)}, u32[]{:S(2)}) collective-permute-start(f16[272,512]{1,0:T(8,128)(2,1)S(1)} %convert_element_type.25), channel_id=1, source_target_pairs={{0,2},{1,3},{2,0},{3,1},{4,6},{5,7},{6,4},{7,5},{8,10},{9,11},{10,... | collective-permute-start | bytes 835592 | tf_op jit(solution)/shard_map/ppermute | solution.py:457
  122.4 9.2 %collective-permute-start.26 = (f32[256,512]{1,0:T(8,128)S(1)}, f32[256,512]{1,0:T(8,128)S(1)}, u32[]{:S(2)}, u32[]{:S(2)}) collective-permute-start(f32[256,512]{1,0:T(8,128)S(1)} %get-tuple-element.83), channel_id=1, source_target_pairs={{0,1},{1,0},{2,3},{3,2},{4,5},{5,4},{6,7},{7,6},{8,9},{9,8},{10,11... | collective-permute-start | bytes 1572872 | tf_op jit(solution)/shard_map/ppermute | solution.py:457
  131.0 5.0 %collective-permute-start.27 = (f32[256,512]{1,0:T(8,128)S(1)}, f32[256,512]{1,0:T(8,128)S(1)}, u32[]{:S(2)}, u32[]{:S(2)}) collective-permute-start(f32[256,512]{1,0:T(8,128)S(1)} %get-tuple-element.86), channel_id=1, source_target_pairs={{0,1},{1,0},{2,3},{3,2},{4,5},{5,4},{6,7},{7,6},{8,9},{9,8},{10,11... | collective-permute-start | bytes 1572872 | tf_op jit(solution)/shard_map/ppermute | solution.py:457
  131.0 4.9 %collective-permute-start.28 = (f32[256,512]{1,0:T(8,128)S(1)}, f32[256,512]{1,0:T(8,128)S(1)}, u32[]{:S(2)}, u32[]{:S(2)}) collective-permute-start(f32[256,512]{1,0:T(8,128)S(1)} %get-tuple-element.87), channel_id=1, source_target_pairs={{0,1},{1,0},{2,3},{3,2},{4,5},{5,4},{6,7},{7,6},{8,9},{9,8},{10,11... | collective-permute-start | bytes 1572872 | tf_op jit(solution)/shard_map/ppermute | solution.py:457
  132.3 9.6 %collective-permute-start.31 = (f16[272,512]{1,0:T(8,128)(2,1)S(1)}, f16[272,512]{1,0:T(8,128)(2,1)S(1)}, u32[]{:S(2)}, u32[]{:S(2)}) collective-permute-start(f16[272,512]{1,0:T(8,128)(2,1)S(1)} %convert_element_type.28), channel_id=1, source_target_pairs={{0,2},{1,3},{2,0},{3,1},{4,6},{5,7},{6,4},{7,5},{8,10},{9,11},{10,... | collective-permute-start | bytes 835592 | tf_op jit(solution)/shard_map/ppermute | solution.py:457
  135.4 17.2 %collective-permute-start.29 = (f32[512,512]{1,0:T(8,128)S(1)}, f32[512,512]{1,0:T(8,128)S(1)}, u32[]{:S(2)}, u32[]{:S(2)}) collective-permute-start(f32[512,512]{1,0:T(8,128)S(1)} %get-tuple-element.91), channel_id=1, source_target_pairs={{0,1},{1,0},{2,3},{3,2},{4,5},{5,4},{6,7},{7,6},{8,9},{9,8},{10,11... | collective-permute-start | bytes 3145736 | tf_op jit(solution)/shard_map/ppermute | solution.py:457
  135.4 6.8 %collective-permute-start.33 = (f32[256,512]{1,0:T(8,128)S(1)}, f32[256,512]{1,0:T(8,128)S(1)}, u32[]{:S(2)}, u32[]{:S(2)}) collective-permute-start(f32[256,512]{1,0:T(8,128)S(1)} %get-tuple-element.99), channel_id=1, source_target_pairs={{0,1},{1,0},{2,3},{3,2},{4,5},{5,4},{6,7},{7,6},{8,9},{9,8},{10,11... | collective-permute-start | bytes 1572872 | tf_op jit(solution)/shard_map/ppermute | solution.py:457
  136.8 15.8 %collective-permute-start.30 = (f16[528,512]{1,0:T(8,128)(2,1)S(1)}, f16[528,512]{1,0:T(8,128)(2,1)S(1)}, u32[]{:S(2)}, u32[]{:S(2)}) collective-permute-start(f16[528,512]{1,0:T(8,128)(2,1)S(1)} %convert_element_type.26), channel_id=1, source_target_pairs={{0,2},{1,3},{2,0},{3,1},{4,6},{5,7},{6,4},{7,5},{8,10},{9,11},{10,... | collective-permute-start | bytes 1622024 | tf_op jit(solution)/shard_map/ppermute | solution.py:457
  141.9 4.6 %collective-permute-start.32 = (f32[1,512]{1,0:T(1,128)S(1)}, f32[1,512]{1,0:T(1,128)S(1)}, u32[]{:S(2)}, u32[]{:S(2)}) collective-permute-start(f32[1,512]{1,0:T(1,128)S(1)} %get-tuple-element.114.refs_3_), channel_id=1, source_target_pairs={{0,1},{1,0},{2,3},{3,2},{4,5},{5,4},{6,7},{7,6},{8,9},{9,8},{10,11... | collective-permute-start | bytes 6152 | tf_op jit(solution)/shard_map/ppermute | solution.py:457
  142.0 1.2 copy-start.3
  142.0 1.5 copy-start.4
  143.6 3.0 %copy-start.8 = (f32[128]{0:T(128)S(1)}, f32[128]{0:T(128)}, u32[]{:S(2)}) copy-start(f32[128]{0:T(128)} %param.16) | copy-start | bytes 1540
  143.6 3.0 %copy-start.9 = (f32[128]{0:T(128)S(1)}, f32[128]{0:T(128)}, u32[]{:S(2)}) copy-start(f32[128]{0:T(128)} %param.17) | copy-start | bytes 1540
  143.6 9.0 %copy-start.10 = (f32[512,512]{1,0:T(8,128)S(1)}, f32[512,512]{1,0:T(8,128)}, u32[]{:S(2)}) copy-start(f32[512,512]{1,0:T(8,128)} %param.14) | copy-start | bytes 3145732
  143.6 9.1 %copy-start.11 = (f32[512,512]{1,0:T(8,128)S(1)}, f32[512,512]{1,0:T(8,128)}, u32[]{:S(2)}) copy-start(f32[512,512]{1,0:T(8,128)} %param.15) | copy-start | bytes 3145732
  146.6 6.1 %copy-start.1 = (f32[512,512]{1,0:T(8,128)S(1)}, f32[512,512]{1,0:T(8,128)}, u32[]{:S(2)}) copy-start(f32[512,512]{1,0:T(8,128)} %refs_0_.3) | copy-start | bytes 3145732
  146.6 1.3 copy-start.5
